TPU v7x, 32 devices: a whole 2x2x4 slice. The times are simulated.
32 devices in a mesh: parts: 2 (over y), mesh: 4 (over z), sub: 2 (over x), lat: 2 (over core).
Axes of the slice: x: 2, y: 2, z: 4, core: 2. Of those that a mesh axis runs over, the one named last changes fastest.
Arguments:
- node_state: bfloat16 [2048, 512], P(('parts', 'mesh', 'sub')), parts along dimension 0, may hold values from -6 to 6
- send_rows: int32 [16, 4, 32], P(('parts', 'mesh', 'sub')), parts along dimension 0, may hold values from 0 to 127
- edge_src: int32 [8192], P(('parts', 'mesh', 'sub')), parts along dimension 0, may hold values from 0 to 255, as said below
- edge_dst: int32 [8192], P(('parts', 'mesh', 'sub')), parts along dimension 0, may hold values from 0 to 127, as said below
- block_count: int32 [64], P(('parts', 'mesh', 'sub')), parts along dimension 0, may hold values from 1 to 128
- w_src: bfloat16 [512, 512], P(None, 'lat'), may hold values from -0.25 to 0.25
- w_dst: bfloat16 [512, 512], P(None, 'lat'), may hold values from -0.25 to 0.25
- hidden_bias: float32 [512], P('lat'), may hold values from -3 to 3
- w_out: bfloat16 [512, 512], P('lat'), may hold values from -0.25 to 0.25
- norm_gain: float32 [512], replicated, may hold values from 0.5 to 1.5
- cotangent: bfloat16 [2048, 512], P(('parts', 'mesh', 'sub')), parts along dimension 0, may hold values from -6 to 6
Outputs:
- updated: bfloat16 [2048, 512], P(('parts', 'mesh', 'sub')), parts along dimension 0
- node_grad: float32 [2048, 512], P(('parts', 'mesh', 'sub')), parts along dimension 0
- src_grad: float32 [1024, 512], P('parts', 'lat'), parts along dimension 0
- dst_grad: float32 [1024, 512], P('parts', 'lat'), parts along dimension 0
- out_grad: float32 [1024, 512], P(('parts', 'lat')), parts along dimension 0
- bias_grad: float32 [1024], P(('parts', 'lat')), parts along dimension 0
- gain_grad: float32 [1024], P('parts'), parts along dimension 0
There are 2 independent parts, one for each index of `parts`. A program takes and returns all parts, laid end to end along the dimension named above; an argument that names none is the same for every part. Nothing has to cross between parts.
Inputs may be any that keep to these rules, and one draw needn't show every extreme that they name: `send_rows`: local row of the sending device. `edge_src`: below 128: a node of the edge's own device; 128 + d * 32 + c: the row that the neighbour of direction d sends in slot c. `edge_dst`: slot j of a device's 512 edge slots points to a node of rows (j // 256) * 64 to (j // 256 + 1) * 64 - 1 of that device.
All inputs are finite; a program needn't handle non-finite values.
Results may differ from a plain program's by a relative error of at most 0.008.
Values may be sent and summed in bfloat16 or wider, within the bound.
No kernel may reach another device: no remote copies, remote signals or barrier semaphores. Data moves between devices by JAX's collectives and lax.ppermute only.
A program may use at most 64 MiB of HBM per device.

v0:
```python
import jax
import jax.numpy as jnp
from jax import lax
from jax.sharding import PartitionSpec as P

BLOCK = 128


epsilon = 1e-05


def shifted(x, axis, by):
    count = lax.axis_size(axis)
    return lax.ppermute(x, axis, [(i, (i + by) % count) for i in range(count)])


def layer_norm(aggregate):
    center = aggregate - jnp.mean(aggregate, axis=1, keepdims=True)
    variance = jnp.mean(center * center, axis=1, keepdims=True)
    inverse = lax.rsqrt(variance + epsilon)
    return (center * inverse, inverse)


def norm_backward(upstream, norm_gain, normed, inverse):
    scaled = upstream * norm_gain
    return inverse * (
        scaled
        - jnp.mean(scaled, axis=1, keepdims=True)
        - normed * jnp.mean(scaled * normed, axis=1, keepdims=True)
    )


def edge_usable(counts):
    return (
        (jnp.arange(BLOCK, dtype=jnp.int32)[None, :] < counts[:, None])
        .astype(jnp.float32)
        .reshape(-1)
    )


def edge_forward(source_rows, target_rows, first_weight, second_weight, bias, out_weight, usable):
    pre_act = (
        jnp.dot(source_rows, first_weight, preferred_element_type=jnp.float32)
        + jnp.dot(target_rows, second_weight, preferred_element_type=jnp.float32)
        + bias
    )
    activated = jax.nn.silu(pre_act).astype(jnp.bfloat16)
    messages = jnp.dot(activated, out_weight, preferred_element_type=jnp.float32) * usable[:, None]
    return (pre_act, activated, messages)


def edge_backward(
    source_rows,
    target_rows,
    pre_act,
    activated,
    message_grad,
    first_weight,
    second_weight,
    out_weight,
):
    contract = (((0,), (0,)), ((), ()))
    out_part = lax.dot_general(
        activated, message_grad, contract, preferred_element_type=jnp.float32
    )
    act_grad = lax.dot_general(
        message_grad, out_weight, (((1,), (1,)), ((), ())), preferred_element_type=jnp.float32
    )
    sigmoid_pre = jax.nn.sigmoid(pre_act)
    pre_grad = (act_grad * sigmoid_pre * (1.0 + pre_act * (1.0 - sigmoid_pre))).astype(jnp.bfloat16)
    src_part = lax.dot_general(source_rows, pre_grad, contract, preferred_element_type=jnp.float32)
    dst_part = lax.dot_general(target_rows, pre_grad, contract, preferred_element_type=jnp.float32)
    bias_part = jnp.sum(pre_grad.astype(jnp.float32), axis=0)
    back_src = lax.dot_general(
        pre_grad, first_weight, (((1,), (1,)), ((), ())), preferred_element_type=jnp.float32
    )
    back_dst = lax.dot_general(
        pre_grad, second_weight, (((1,), (1,)), ((), ())), preferred_element_type=jnp.float32
    )
    return (src_part, dst_part, out_part, bias_part, back_src, back_dst)


def shards(
    node_state,
    send_rows,
    edge_src,
    edge_dst,
    block_count,
    w_src,
    w_dst,
    hidden_bias,
    w_out,
    norm_gain,
    cotangent,
):
    local_rows = node_state.shape[0]
    width = node_state.shape[1]
    halo_rows = send_rows.shape[2]
    sent_index = send_rows[0]
    outgoing = node_state[sent_index.reshape(-1)].reshape(4, halo_rows, width)
    pieces = []
    for slot, step in ((0, 1), (1, -1)):
        pieces.append(shifted(outgoing[slot], "mesh", step))
    for slot, step in ((2, 1), (3, -1)):
        pieces.append(shifted(outgoing[slot], "sub", step))
    arrived = jnp.stack(pieces, axis=0)
    table = jnp.concatenate([node_state, arrived.reshape(4 * halo_rows, width)], axis=0)
    table_size = table.shape[0]
    upstream = cotangent.astype(jnp.float32)
    usable = edge_usable(block_count)
    source_rows = table[edge_src]
    target_rows = node_state[edge_dst]
    pre_act, activated, messages = edge_forward(
        source_rows, target_rows, w_src, w_dst, hidden_bias, w_out, usable
    )
    partial_sum = jax.ops.segment_sum(messages, edge_dst, num_segments=local_rows)
    aggregate = lax.psum(partial_sum.astype(jnp.bfloat16), "lat").astype(jnp.float32)
    normed, inverse = layer_norm(aggregate)
    agg_grad = norm_backward(upstream, norm_gain, normed, inverse)
    updated = (node_state.astype(jnp.float32) + norm_gain * normed).astype(jnp.bfloat16)
    gain_part = jnp.sum(upstream * normed, axis=0)
    message_grad = (usable[:, None] * agg_grad[edge_dst]).astype(jnp.bfloat16)
    src_part, dst_part, out_part, bias_part, back_src, back_dst = edge_backward(
        source_rows, target_rows, pre_act, activated, message_grad, w_src, w_dst, w_out
    )
    table_part = jax.ops.segment_sum(
        jnp.concatenate([back_src, back_dst], axis=0),
        jnp.concatenate([edge_src, edge_dst], axis=0),
        num_segments=table_size,
    )
    table_grad = lax.psum(table_part.astype(jnp.bfloat16), "lat").astype(jnp.float32)
    slot_grad = table_grad[local_rows:].reshape(4, halo_rows, width)
    backs = []
    for slot, step in ((0, -1), (1, 1)):
        backs.append(
            shifted(slot_grad[slot].astype(jnp.bfloat16), "mesh", step).astype(jnp.float32)
        )
    for slot, step in ((2, -1), (3, 1)):
        backs.append(shifted(slot_grad[slot].astype(jnp.bfloat16), "sub", step).astype(jnp.float32))
    returned = jnp.stack(backs, axis=0)
    node_grad = (
        upstream
        + table_grad[:local_rows]
        + jax.ops.segment_sum(
            returned.reshape(4 * halo_rows, width), sent_index.reshape(-1), num_segments=local_rows
        )
    )
    src_grad, dst_grad, out_grad, bias_grad, gain_grad = lax.psum(
        (src_part, dst_part, out_part, bias_part, gain_part), ("mesh", "sub")
    )
    return (updated, node_grad, src_grad, dst_grad, out_grad, bias_grad, gain_grad)


def solution(mesh):
    in_specs = (
        P(("parts", "mesh", "sub"), None),
        P(("parts", "mesh", "sub"), None, None),
        P(("parts", "mesh", "sub")),
        P(("parts", "mesh", "sub")),
        P(("parts", "mesh", "sub")),
        P(None, "lat"),
        P(None, "lat"),
        P("lat"),
        P("lat", None),
        P(),
        P(("parts", "mesh", "sub"), None),
    )
    out_specs = (
        P(("parts", "mesh", "sub"), None),
        P(("parts", "mesh", "sub"), None),
        P("parts", "lat"),
        P("parts", "lat"),
        P(("parts", "lat"), None),
        P(("parts", "lat")),
        P("parts"),
    )
    return jax.shard_map(shards, mesh=mesh, in_specs=in_specs, out_specs=out_specs, check_vma=False)
```

profile of v0, /device:TPU:0, one launch (start us, length us, event | category | flops | bytes accessed | tf_op | source)
XLA Modules:
  0.0 191.7 jit_solution(8451614240443880985)
XLA Ops:
  7.2 0.0 copy-start
  7.2 0.0 copy-start.1
  7.2 0.0 all-reduce.6.cloned.1.call-start
  7.3 0.8 reshape_squeeze.3
  8.1 1.8 gather_fusion
  9.9 3.1 %collective-permute-start = (bf16[32,512]{1,0:T(8,128)(2,1)S(1)}, bf16[32,512]{1,0:T(8,128)(2,1)S(1)}, u32[]{:S(2)}, u32[]{:S(2)}) collective-permute-start(bf16[32,512]{1,0:T(8,128)(2,1)S(1)} %get-tuple-element.21), channel_id=1, source_target_pairs={{0,4},{4,8},{8,12},{12,0},{1,5},{5,9},{9,13},{13,1},{2,6},{6,10},{... | collective-permute-start | bytes 98312 | tf_op jit(solution)/shard_map/ppermute | solution.py:14
  13.0 2.1 %collective-permute-start.1 = (bf16[32,512]{1,0:T(8,128)(2,1)S(1)}, bf16[32,512]{1,0:T(8,128)(2,1)S(1)}, u32[]{:S(2)}, u32[]{:S(2)}) collective-permute-start(bf16[32,512]{1,0:T(8,128)(2,1)S(1)} %get-tuple-element.23), channel_id=1, source_target_pairs={{0,12},{4,0},{8,4},{12,8},{1,13},{5,1},{9,5},{13,9},{2,14},{6,2},{... | collective-permute-start | bytes 98312 | tf_op jit(solution)/shard_map/ppermute | solution.py:14
  15.1 1.6 collective-permute-start.2
  16.7 0.4 collective-permute-start.3
  17.1 0.1 convert_bitcast_fusion
  17.2 2.0 %gather_fusion.2 = bf16[512,512]{1,0:T(8,128)(2,1)S(1)} fusion(bf16[128,512]{1,0:T(8,128)(2,1)S(1)} %copy-done.1, s32[1024]{0:T(1024)S(1)} %pad_clamp_fusion), kind=kCustom, calls=%fused_computation.2 | custom fusion | bytes 1050624 | tf_op jit(solution)/shard_map/gather | solution.py:112
  19.2 0.0 collective-permute-done
  19.2 0.0 collective-permute-done.2
  19.2 1.4 collective-permute-done.3
  20.7 0.0 copy-start.6
  20.7 2.0 %gather_fusion.1 = bf16[512,512]{1,0:T(8,128)(2,1)S(1)} fusion(bf16[256,512]{1,0:T(8,128)(2,1)S(1)} %pad_maximum_fusion, s32[1024]{0:T(1024)S(1)} %pad_clamp_fusion.1), kind=kCustom, calls=%fused_computation.1 | custom fusion | bytes 1050624 | tf_op jit(solution)/shard_map/gather | solution.py:111
  22.7 0.0 copy-start.7
  22.7 0.0 copy-start.16
  22.7 0.3 fusion.30
  23.0 0.6 copy-done.7
  23.6 0.3 fusion.5
  24.0 1.3 convolution_multiply_fusion
  25.3 4.3 %scatter_custom_fusion = f32[128,512]{1,0:T(8,128)S(1)} fusion(s32[512]{0:T(512)S(1)} %copy-done.14, f32[512,512]{1,0:T(8,128)} %convolution_multiply_fusion, f32[]{:T(128)} %constant.7.clone.1), kind=kCustom, calls=%fused_computation.46 | custom fusion | flops 262144 | bytes 262656 | tf_op jit(solution)/shard_map/scatter-add | solution.py:116
  29.6 0.7 convert_element_type.53
  30.3 0.0 all-reduce.6.cloned.1.call-update
  30.3 0.0 all-reduce.8.cloned.1.call-start
  30.4 16.5 %all-reduce.6.cloned.1.call-done = bf16[128,512]{1,0:T(8,128)(2,1)} async-done(((bf16[128,512]{1,0:T(8,128)(2,1)}), bf16[128,512]{1,0:T(8,128)(2,1)}) %all-reduce.6.cloned.1.call-update) | async-done | bytes 131088 | tf_op jit(solution)/shard_map/psum | solution.py:117
  46.9 1.0 convert_reduce_fusion.1
  47.9 1.1 fusion.18
  49.1 1.1 fusion.20
  50.2 1.7 fusion.17
  51.9 1.6 gather_fusion.3
  53.5 1.2 fusion.27
  54.7 0.4 convert_reduce_fusion
  55.2 0.0 copy-start.2
  55.2 0.0 copy-start.8
  55.2 0.3 fusion.31
  55.5 0.3 copy-done.2
  55.9 0.4 copy-done.8
  56.2 0.3 fusion.32
  56.6 7.7 %scatter_custom_fusion.1 = f32[256,512]{1,0:T(8,128)} fusion(s32[1024]{0:T(1024)S(1)} %pad_add_fusion, f32[512,512]{1,0:T(8,128)S(1)} %fusion.32, f32[]{:T(128)} %constant.27, f32[512,512]{1,0:T(8,128)S(1)} %fusion.31, f32[]{:T(128)} %constant.7.clone.1), kind=kCustom, calls=%fused_computation.7 | custom fusion | flops 1048576 | bytes 2621448 | tf_op jit(solution)/shard_map/scatter-add | solution.py:126
  64.2 1.8 convert_element_type.59
  66.1 0.0 all-reduce.8.cloned.1.call-update
  66.1 0.0 all-reduce.10.cloned.1.call-start
  66.1 1.1 fusion.33
  67.3 1.1 fusion.34
  68.4 0.0 all-reduce.10.cloned.1.call-update
  68.4 0.7 copy-done.13
  69.1 0.1 reshape.165
  69.2 22.2 %all-reduce = (f32[256]{0:T(256)}, f32[512]{0:T(512)}) all-reduce(f32[256]{0:T(256)S(1)} %get-tuple-element.25, f32[512]{0:T(512)S(1)} %get-tuple-element.7), channel_id=1, replica_groups=mesh['parts'=2,'mesh'=4,'sub'=2,'lat'=2] {'mesh','sub'}, use_global_device_ids=true, to_apply=%region_13.14 | all-reduce | flops 768 | bytes 6144 | tf_op jit(solution)/shard_map/psum | solution.py:148
  91.3 0.8 fusion.28
  92.2 0.1 collective-permute-start.7
  92.2 0.3 collective-permute-start.4
  92.5 1.8 collective-permute-start.5
  94.3 2.0 %collective-permute-start.6 = (bf16[32,512]{1,0:T(8,128)(2,1)S(1)}, bf16[32,512]{1,0:T(8,128)(2,1)S(1)}, u32[]{:S(2)}, u32[]{:S(2)}) collective-permute-start(bf16[32,512]{1,0:T(8,128)(2,1)S(1)} %get-tuple-element.17), channel_id=1, source_target_pairs={{0,2},{2,0},{1,3},{3,1},{4,6},{6,4},{5,7},{7,5},{8,10},{10,8},{9,1... | collective-permute-start | bytes 98312 | tf_op jit(solution)/shard_map/ppermute | solution.py:14
  96.3 0.9 convert_add_fusion
  97.3 0.0 collective-permute-done.4
  97.3 1.0 collective-permute-done.5
  98.3 1.5 scatter_custom_fusion.2
  99.8 0.0 copy-start.11
  99.8 81.8 %all-reduce.10.cloned.1.call-done = (f32[512,256]{1,0:T(8,128)}, f32[512,256]{1,0:T(8,128)}, f32[256,512]{1,0:T(8,128)}) async-done(((f32[512,256]{1,0:T(8,128)}, f32[512,256]{1,0:T(8,128)}, f32[256,512]{1,0:T(8,128)}), (f32[512,256]{1,0:T(8,128)}, f32[512,256]{1,0:T(8,128)}, f32[256,512]{1,0:T(8,128)})) %all-reduce.10.cloned.1.call-update) | async-done | bytes 1572880 | tf_op jit(solution)/shard_map/psum | solution.py:148
  181.6 2.0 %copy.24 = f32[512,256]{1,0:T(8,128)} copy(f32[512,256]{1,0:T(8,128)} %get-tuple-element.31) | data formatting | bytes 1048576
  183.6 0.8 copy.25
  184.4 0.8 copy.26
  (42 shorter events, 0.2 us)
Async XLA Ops:
  7.2 16.8 %copy-start = (bf16[256,512]{1,0:T(8,128)(2,1)S(1)}, bf16[256,512]{1,0:T(8,128)(2,1)}, u32[]{:S(2)}) copy-start(bf16[256,512]{1,0:T(8,128)(2,1)} %param.19) | copy-start | bytes 786436
  7.2 10.0 %copy-start.1 = (bf16[128,512]{1,0:T(8,128)(2,1)S(1)}, bf16[128,512]{1,0:T(8,128)(2,1)}, u32[]{:S(2)}) copy-start(bf16[128,512]{1,0:T(8,128)(2,1)} %param.11) | copy-start | bytes 393220
  7.2 9.9 %copy-start.15 = (s32[512]{0:T(512)S(1)}, s32[512]{0:T(512)}, u32[]{:S(2)}) copy-start(s32[512]{0:T(512)} %param.13) | copy-start | bytes 6148
  7.2 9.9 %copy-start.14 = (s32[512]{0:T(512)S(1)}, s32[512]{0:T(512)}, u32[]{:S(2)}) copy-start(s32[512]{0:T(512)} %param.14) | copy-start | bytes 6148
  7.2 9.9 %copy-start.17 = (s32[4]{0:T(128)S(1)}, s32[4]{0:T(128)}, u32[]{:S(2)}) copy-start(s32[4]{0:T(128)} %param.15) | copy-start | bytes 52
  7.2 39.7 %all-reduce.6.cloned.1.call-start = ((), (), s32[]{:S(2)}) async-start(), calls=%async_computation | async-start | bytes 262144 | tf_op jit(solution)/shard_map/psum | solution.py:117
  9.9 9.3 %collective-permute-start = (bf16[32,512]{1,0:T(8,128)(2,1)S(1)}, bf16[32,512]{1,0:T(8,128)(2,1)S(1)}, u32[]{:S(2)}, u32[]{:S(2)}) collective-permute-start(bf16[32,512]{1,0:T(8,128)(2,1)S(1)} %get-tuple-element.21), channel_id=1, source_target_pairs={{0,4},{4,8},{8,12},{12,0},{1,5},{5,9},{9,13},{13,1},{2,6},{6,10},{... | collective-permute-start | bytes 98312 | tf_op jit(solution)/shard_map/ppermute | solution.py:14
  13.0 6.2 %collective-permute-start.1 = (bf16[32,512]{1,0:T(8,128)(2,1)S(1)}, bf16[32,512]{1,0:T(8,128)(2,1)S(1)}, u32[]{:S(2)}, u32[]{:S(2)}) collective-permute-start(bf16[32,512]{1,0:T(8,128)(2,1)S(1)} %get-tuple-element.23), channel_id=1, source_target_pairs={{0,12},{4,0},{8,4},{12,8},{1,13},{5,1},{9,5},{13,9},{2,14},{6,2},{... | collective-permute-start | bytes 98312 | tf_op jit(solution)/shard_map/ppermute | solution.py:14
  15.1 4.2 %collective-permute-start.2 = (bf16[32,512]{1,0:T(8,128)(2,1)S(1)}, bf16[32,512]{1,0:T(8,128)(2,1)S(1)}, u32[]{:S(2)}, u32[]{:S(2)}) collective-permute-start(bf16[32,512]{1,0:T(8,128)(2,1)S(1)} %get-tuple-element.22), channel_id=1, source_target_pairs={{0,2},{2,0},{1,3},{3,1},{4,6},{6,4},{5,7},{7,5},{8,10},{10,8},{9,1... | collective-permute-start | bytes 98312 | tf_op jit(solution)/shard_map/ppermute | solution.py:14
  16.7 3.9 %collective-permute-start.3 = (bf16[32,512]{1,0:T(8,128)(2,1)S(1)}, bf16[32,512]{1,0:T(8,128)(2,1)S(1)}, u32[]{:S(2)}, u32[]{:S(2)}) collective-permute-start(bf16[32,512]{1,0:T(8,128)(2,1)S(1)} %get-tuple-element.24), channel_id=1, source_target_pairs={{0,2},{2,0},{1,3},{3,1},{4,6},{6,4},{5,7},{7,5},{8,10},{10,8},{9,1... | collective-permute-start | bytes 98312 | tf_op jit(solution)/shard_map/ppermute | solution.py:14
  20.7 2.0 %copy-start.6 = (bf16[512,256]{1,0:T(8,128)(2,1)S(1)}, bf16[512,256]{1,0:T(8,128)(2,1)}, u32[]{:S(2)}) copy-start(bf16[512,256]{1,0:T(8,128)(2,1)} %param.16) | copy-start | bytes 786436
  22.7 1.0 copy-start.7
  22.7 0.9 copy-start.16
  25.3 23.8 %copy-start.4 = (bf16[128,512]{1,0:T(8,128)(2,1)S(1)}, bf16[128,512]{1,0:T(8,128)(2,1)}, u32[]{:S(2)}) copy-start(bf16[128,512]{1,0:T(8,128)(2,1)} %param.21) | copy-start | bytes 393220
  25.3 23.8 %copy-start.12 = (f32[512]{0:T(512)S(1)}, f32[512]{0:T(512)}, u32[]{:S(2)}) copy-start(f32[512]{0:T(512)} %param.20) | copy-start | bytes 6148
  30.3 61.0 %all-reduce.8.cloned.1.call-start = ((), (), s32[]{:S(2)}) async-start(), calls=%async_computation.1 | async-start | bytes 524288 | tf_op jit(solution)/shard_map/psum | solution.py:131
  55.2 0.7 copy-start.2
  55.2 1.0 copy-start.8
  64.2 1.9 copy-start.3
  66.1 115.5 %all-reduce.10.cloned.1.call-start = ((), (), s32[]{:S(2)}) async-start(), calls=%async_computation.2 | async-start | bytes 3145728 | tf_op jit(solution)/shard_map/psum | solution.py:148
  68.4 0.7 copy-start.13
  68.4 27.9 %copy-start.5 = (bf16[128,512]{1,0:T(8,128)(2,1)S(1)}, bf16[128,512]{1,0:T(8,128)(2,1)}, u32[]{:S(2)}) copy-start(bf16[128,512]{1,0:T(8,128)(2,1)} %param.21) | copy-start | bytes 393220
  92.2 5.1 %collective-permute-start.7 = (bf16[32,512]{1,0:T(8,128)(2,1)S(1)}, bf16[32,512]{1,0:T(8,128)(2,1)S(1)}, u32[]{:S(2)}, u32[]{:S(2)}) collective-permute-start(bf16[32,512]{1,0:T(8,128)(2,1)S(1)} %get-tuple-element.16), channel_id=1, source_target_pairs={{0,2},{2,0},{1,3},{3,1},{4,6},{6,4},{5,7},{7,5},{8,10},{10,8},{9,1... | collective-permute-start | bytes 98312 | tf_op jit(solution)/shard_map/ppermute | solution.py:14
  92.2 5.0 %collective-permute-start.4 = (bf16[32,512]{1,0:T(8,128)(2,1)S(1)}, bf16[32,512]{1,0:T(8,128)(2,1)S(1)}, u32[]{:S(2)}, u32[]{:S(2)}) collective-permute-start(bf16[32,512]{1,0:T(8,128)(2,1)S(1)} %get-tuple-element.15), channel_id=1, source_target_pairs={{0,12},{4,0},{8,4},{12,8},{1,13},{5,1},{9,5},{13,9},{2,14},{6,2},{... | collective-permute-start | bytes 98312 | tf_op jit(solution)/shard_map/ppermute | solution.py:14
  92.5 5.7 %collective-permute-start.5 = (bf16[32,512]{1,0:T(8,128)(2,1)S(1)}, bf16[32,512]{1,0:T(8,128)(2,1)S(1)}, u32[]{:S(2)}, u32[]{:S(2)}) collective-permute-start(bf16[32,512]{1,0:T(8,128)(2,1)S(1)} %get-tuple-element.18), channel_id=1, source_target_pairs={{0,4},{4,8},{8,12},{12,0},{1,5},{5,9},{9,13},{13,1},{2,6},{6,10},{... | collective-permute-start | bytes 98312 | tf_op jit(solution)/shard_map/ppermute | solution.py:14
  94.3 3.9 %collective-permute-start.6 = (bf16[32,512]{1,0:T(8,128)(2,1)S(1)}, bf16[32,512]{1,0:T(8,128)(2,1)S(1)}, u32[]{:S(2)}, u32[]{:S(2)}) collective-permute-start(bf16[32,512]{1,0:T(8,128)(2,1)S(1)} %get-tuple-element.17), channel_id=1, source_target_pairs={{0,2},{2,0},{1,3},{3,1},{4,6},{6,4},{5,7},{7,5},{8,10},{10,8},{9,1... | collective-permute-start | bytes 98312 | tf_op jit(solution)/shard_map/ppermute | solution.py:14
  99.8 84.6 %copy-start.11 = (f32[128,512]{1,0:T(8,128)}, f32[128,512]{1,0:T(8,128)S(1)}, u32[]{:S(2)}) copy-start(f32[128,512]{1,0:T(8,128)S(1)} %scatter_custom_fusion.2) | copy-start | bytes 786436
  181.6 2.0 %copy-start.10 = (f32[512,256]{1,0:T(8,128)S(1)}, f32[512,256]{1,0:T(8,128)}, u32[]{:S(2)}) copy-start(f32[512,256]{1,0:T(8,128)} %get-tuple-element.32) | copy-start | bytes 1572868
  181.6 2.8 %copy-start.9 = (f32[256,512]{1,0:T(8,128)S(1)}, f32[256,512]{1,0:T(8,128)}, u32[]{:S(2)}) copy-start(f32[256,512]{1,0:T(8,128)} %get-tuple-element.33) | copy-start | bytes 1572868
Sparse Core Ops, SparseCore 0:
  30.4 16.4 all-reduce.5
  66.2 19.3 all-reduce.7
  90.6 90.9 all-reduce.9
where the time goes:
time: 192 us
  waiting for transfers between devices  101 us (53%)
  blocking collectives  22.2 us (12%)
  other arithmetic  22.1 us (12%)
  local copies, waits for them, and re-layouts  14.7 us (8%)
  between operations  14.1 us (7%)
  starting transfers between devices  11.4 us (6%)
  matrix products  6.43 us (3%)
    psum x1, waiting for transfers between devices, shards(): lax.psum((src_part, dst_part, out_part, bias_part, gain_part), ('mesh', '...  81.8 us
    psum x1, blocking collectives, shards(): lax.psum((src_part, dst_part, out_part, bias_part, gain_part), ('mesh', '...  22.2 us
    psum x1, waiting for transfers between devices, shards(): lax.psum(partial_sum.astype(jnp.bfloat16), 'lat').astype(jnp.float32)  16.5 us
    ppermute x8, starting transfers between devices, shifted(): return lax.ppermute(x, axis, [(i, (i + by) % count) for i in range(count)])  11.3 us
    scatter-add x1, other arithmetic, shards(): jax.ops.segment_sum(jnp.concatenate([back_src, back_dst], axis=0), jnp.co...  7.69 us
    unnamed x39, local copies, waits for them, and re-layouts  5.61 us
    scatter-add x1, other arithmetic, shards(): jax.ops.segment_sum(messages, edge_dst, num_segments=local_rows)  4.35 us
  transfers between devices with their start and end apart: 11, of which 4 were waited for; matrix products, arithmetic and copies ran while one was open for 4% of the time, Pallas kernels for 0%

commit v1 on v0

v1 whole, which is shorter than its diff:
```python
import functools

import jax
import jax.numpy as jnp
from jax import lax
from jax.experimental import pallas as pl
from jax.experimental.pallas import tpu as pltpu
from jax.sharding import PartitionSpec as P

BLOCK = 128
EPSILON = 1e-05
TAIL = 16
VMEM_LIMIT = 24 * 1024 * 1024

f32 = jnp.float32
bf16 = jnp.bfloat16

NN = (((1,), (0,)), ((), ()))
NT = (((1,), (1,)), ((), ()))
TN = (((0,), (0,)), ((), ()))


def dot(a, b, dims=NN):
    return lax.dot_general(a, b, dims, preferred_element_type=f32)


def iota(shape, dim):
    return lax.broadcasted_iota(jnp.int32, shape, dim)


def one_hot(condition):
    return jnp.where(condition, 1.0, 0.0).astype(bf16)


def split(x):
    high = x.astype(bf16)
    return high, (x - high.astype(f32)).astype(bf16)


def columns_of(row, lanes):
    return jnp.transpose(jnp.broadcast_to(row, (lanes, row.shape[1])))


def usable_row(count_ref, edges):
    lane = iota((1, BLOCK), 1)
    parts = [lane < count_ref[b] for b in range(edges // BLOCK)]
    return jnp.concatenate([jnp.where(p, 1, 0) for p in parts], axis=1)


def usable_columns(count_ref, edges, lanes):
    sub = iota((BLOCK, lanes), 0)
    return jnp.concatenate(
        [jnp.where(sub < count_ref[b], 1, 0) for b in range(edges // BLOCK)], axis=0
    )


def table_columns(row, rows):
    columns = columns_of(row, 128)
    lane = iota(columns.shape, 1)
    return [one_hot(columns == lane + 128 * b) for b in range(rows // 128)]


def send_kernel(node_ref, send_ref, *out_refs):
    node = node_ref[...]
    rows = node.shape[0]
    halo = send_ref.shape[1]
    pieces = []
    for d in range(4):
        pick = one_hot(iota((rows, halo), 0) == send_ref[d : d + 1, :])
        pieces.append(dot(pick, node, TN).astype(bf16))
    out_refs[0][...] = pieces[0]
    out_refs[1][...] = pieces[1]
    if len(out_refs) == 3:
        out_refs[2][0:halo, :] = pieces[2]
        out_refs[2][halo:, :] = pieces[3]
    else:
        out_refs[2][...] = pieces[2]
        out_refs[3][...] = pieces[3]


def forward_kernel(
    count_ref, node_ref, src_ref, dst_ref, w_src_ref, w_dst_ref, bias_ref, w_out_ref, *rest
):
    *halo_refs, factor_ref, hidden_ref, partial_ref = rest
    node = node_ref[...]
    rows = node.shape[0]
    edges = src_ref.shape[1]
    table = jnp.concatenate([node] + [r[...] for r in halo_refs], axis=0)
    picks = table_columns(src_ref[...], table.shape[0])
    source = dot(jnp.concatenate(picks, axis=1), table).astype(bf16)
    (target_pick,) = table_columns(dst_ref[...], rows)
    target = dot(target_pick, node).astype(bf16)
    pre = dot(source, w_src_ref[...]) + dot(target, w_dst_ref[...]) + bias_ref[...]
    sig = 0.5 + 0.5 * jnp.tanh(0.5 * pre)
    factor_ref[...] = sig * (1.0 + pre * (1.0 - sig))
    activated = (pre * sig).astype(bf16)
    used = usable_row(count_ref, edges)
    collect = one_hot((iota((rows, edges), 0) == dst_ref[...]) & (used > 0))
    hidden = dot(collect, activated)
    high, low = split(hidden)
    hidden_ref[...] = high
    partial_ref[...] = (dot(high, w_out_ref[...]) + dot(low, w_out_ref[...])).astype(bf16)


def backward_kernel(
    geometry,
    count_ref,
    node_ref,
    src_ref,
    dst_ref,
    w_out_ref,
    gain_ref,
    cot_ref,
    factor_ref,
    hidden_ref,
    own_ref,
    other_ref,
    *rest,
):
    peers, chunk, merged = geometry
    n_halo = 3 if merged else 4
    halo_refs = rest[:n_halo]
    updated_ref, message_ref, local_ref, target_ref = rest[n_halo : n_halo + 4]
    back_refs = rest[n_halo + 4 :]
    node = node_ref[...]
    rows, width = node.shape
    edges = src_ref.shape[1]
    aggregate = own_ref[...].astype(f32) + other_ref[...].astype(f32)
    center = aggregate - jnp.mean(aggregate, axis=1, keepdims=True)
    variance = jnp.mean(center * center, axis=1, keepdims=True)
    inverse = lax.rsqrt(variance + EPSILON)
    normed = center * inverse
    gain = gain_ref[...]
    updated_ref[...] = (node.astype(f32) + gain * normed).astype(bf16)
    upstream = cot_ref[...].astype(f32)
    gain_part = jnp.sum(upstream * normed, axis=0, keepdims=True)
    scaled = upstream * gain
    agg_grad = inverse * (
        scaled
        - jnp.mean(scaled, axis=1, keepdims=True)
        - normed * jnp.mean(scaled * normed, axis=1, keepdims=True)
    )
    agg_grad = agg_grad.astype(bf16)

    columns = columns_of(dst_ref[...], 128)
    used = usable_columns(count_ref, edges, 128)
    spread = one_hot((columns == iota(columns.shape, 1)) & (used > 0))
    message_grad = dot(spread, agg_grad).astype(bf16)
    act_grad = dot(message_grad, w_out_ref[...], NT)
    pre_grad = (act_grad * factor_ref[...]).astype(bf16)

    table = jnp.concatenate([node] + [r[...] for r in halo_refs], axis=0)
    size = table.shape[0]
    by_source = dot(one_hot(iota((size, edges), 0) == src_ref[...]), pre_grad)
    by_target = dot(one_hot(iota((rows, edges), 0) == dst_ref[...]), pre_grad)
    local_ref[...] = by_source[:rows]
    by_target_low = by_target.astype(bf16)
    target_ref[...] = by_target_low
    at = rows
    for ref in back_refs:
        ref[...] = by_source[at : at + ref.shape[0]].astype(bf16)
        at += ref.shape[0]

    hid = by_source.shape[1]
    bias_part = jnp.sum(by_target, axis=0, keepdims=True)
    src_part = dot(table, by_source.astype(bf16), TN).astype(bf16)
    dst_part = dot(node, by_target_low, TN).astype(bf16)
    out_part = dot(hidden_ref[...], agg_grad, TN).astype(bf16)
    blocks = [src_part, dst_part]
    for at in range(0, width, hid):
        blocks.append(out_part[:, at : at + hid])
    vectors = [bias_part] + [gain_part[:, at : at + hid] for at in range(0, width, hid)]
    tail = []
    for v in vectors:
        high = v.astype(bf16)
        tail += [high.astype(f32), (v - high.astype(f32))]
    tail.append(jnp.zeros((TAIL - len(tail), hid), f32))
    tail = jnp.concatenate(tail, axis=0).astype(bf16)
    done = 0
    for block in blocks:
        at = 0
        while at < block.shape[0]:
            peer, offset = divmod(done, chunk)
            take = min(chunk - offset, block.shape[0] - at)
            message_ref[peer, offset : offset + take, :] = block[at : at + take]
            at += take
            done += take
    while done < peers * chunk:
        peer, offset = divmod(done, chunk)
        take = chunk - offset
        message_ref[peer, offset : offset + take, :] = jnp.zeros((take, hid), bf16)
        done += take
    for peer in range(peers):
        message_ref[peer, chunk:, :] = tail


def sum_kernel(chunk, arrived_ref, out_ref, bias_ref, gain_ref):
    peers = arrived_ref.shape[0]
    total = arrived_ref[0].astype(f32)
    for peer in range(1, peers):
        total += arrived_ref[peer].astype(f32)
    low = total[:chunk].astype(bf16)
    for peer in range(peers):
        out_ref[peer] = low
    tail = total[chunk:]
    bias_ref[...] = tail[0:1] + tail[1:2]
    hid = tail.shape[1]
    for k in range(gain_ref.shape[1] // hid):
        gain_ref[:, k * hid : (k + 1) * hid] = tail[2 + 2 * k : 3 + 2 * k] + tail[3 + 2 * k : 4 + 2 * k]


def unpack_kernel(arrived_ref, src_ref, dst_ref, out_ref):
    hid = src_ref.shape[1]
    rows = src_ref.shape[0]
    src_ref[...] = arrived_ref[0:rows, :].astype(f32)
    dst_ref[...] = arrived_ref[rows : 2 * rows, :].astype(f32)
    at = 2 * rows
    for k in range(out_ref.shape[1] // hid):
        out_ref[:, k * hid : (k + 1) * hid] = arrived_ref[at : at + out_ref.shape[0], :].astype(f32)
        at += out_ref.shape[0]


def node_kernel(send_ref, local_ref, target_ref, w_src_ref, w_dst_ref, *rest):
    *back_refs, out_ref = rest
    rows = local_ref.shape[0]
    halo = send_ref.shape[1]
    returned = jnp.concatenate([r[...] for r in back_refs], axis=0)
    total = local_ref[...]
    for d in range(4):
        pick = one_hot(iota((rows, halo), 0) == send_ref[d : d + 1, :])
        total += dot(pick, returned[d * halo : (d + 1) * halo])
    out_ref[...] = (
        dot(total.astype(bf16), w_src_ref[...], NT) + dot(target_ref[...], w_dst_ref[...], NT)
    ).astype(bf16)


def finish_kernel(cot_ref, own_ref, other_ref, out_ref):
    out_ref[...] = cot_ref[...].astype(f32) + (
        own_ref[...].astype(f32) + other_ref[...].astype(f32)
    )


VMEM = pl.BlockSpec(memory_space=pltpu.VMEM)
SMEM = pl.BlockSpec(memory_space=pltpu.SMEM)


def shape(dims, dtype):
    return jax.ShapeDtypeStruct(dims, dtype)


def call(kernel, outs, *args, smem=0, flops=10**8):
    return pl.pallas_call(
        kernel,
        out_shape=outs,
        in_specs=[SMEM] * smem + [VMEM] * (len(args) - smem),
        out_specs=jax.tree.map(lambda _: VMEM, outs),
        compiler_params=pltpu.CompilerParams(vmem_limit_bytes=VMEM_LIMIT),
        cost_estimate=pl.CostEstimate(flops=flops, bytes_accessed=10**6, transcendentals=0),
    )(*args)


def shifted(x, axis, by):
    count = lax.axis_size(axis)
    return lax.ppermute(x, axis, [(i, (i + by) % count) for i in range(count)])


def shards(
    node_state,
    send_rows,
    edge_src,
    edge_dst,
    block_count,
    w_src,
    w_dst,
    hidden_bias,
    w_out,
    norm_gain,
    cotangent,
):
    rows, width = node_state.shape
    hid = w_src.shape[1]
    halo = send_rows.shape[2]
    edges = edge_src.shape[0]
    peers = lax.axis_size("mesh") * lax.axis_size("sub")
    merged = lax.axis_size("sub") == 2
    total_rows = 2 * width + (width // hid) * hid
    chunk = -(-total_rows // (peers * 16)) * 16

    send = send_rows[0]
    src = edge_src.reshape(1, edges)
    dst = edge_dst.reshape(1, edges)
    bias = hidden_bias.reshape(1, hid)
    gain = norm_gain.reshape(1, width)

    piece = [halo, halo, 2 * halo] if merged else [halo] * 4
    routes = [("mesh", 1), ("mesh", -1), ("sub", 1)] + ([] if merged else [("sub", -1)])

    outgoing = call(send_kernel, [shape((n, width), bf16) for n in piece], node_state, send)
    arrived = [shifted(x, axis, by) for x, (axis, by) in zip(outgoing, routes)]

    factor, hidden, partial = call(
        forward_kernel,
        [shape((edges, hid), f32), shape((rows, hid), bf16), shape((rows, width), bf16)],
        block_count, node_state, src, dst, w_src, w_dst, bias, w_out, *arrived,
        smem=1,
    )
    other = shifted(partial, "lat", 1)

    updated, message, local, target, *backs = call(
        functools.partial(backward_kernel, (peers, chunk, merged)),
        [
            shape((rows, width), bf16),
            shape((peers, chunk + TAIL, hid), bf16),
            shape((rows, hid), f32),
            shape((rows, hid), bf16),
        ]
        + [shape((n, hid), bf16) for n in piece],
        block_count, node_state, src, dst, w_out, gain, cotangent, factor, hidden, partial, other,
        *arrived,
        smem=1,
    )
    returned = [shifted(x, axis, -by) for x, (axis, by) in zip(backs, routes)]

    exchanged = lax.all_to_all(message, ("mesh", "sub"), 0, 0)

    node_part = call(
        node_kernel, shape((rows, width), bf16), send, local, target, w_src, w_dst, *returned
    )
    node_grad = call(
        finish_kernel, shape((rows, width), f32),
        cotangent, node_part, shifted(node_part, "lat", 1),
    )

    reduced, bias_grad, gain_grad = call(
        functools.partial(sum_kernel, chunk),
        [shape((peers, chunk, hid), bf16), shape((1, hid), f32), shape((1, width), f32)],
        exchanged,
    )
    gathered = lax.all_to_all(reduced, ("mesh", "sub"), 0, 0)
    src_grad, dst_grad, out_grad = call(
        unpack_kernel,
        [shape((width, hid), f32), shape((width, hid), f32), shape((hid, width), f32)],
        gathered.reshape(peers * chunk, hid),
    )
    return (
        updated, node_grad, src_grad, dst_grad, out_grad,
        bias_grad.reshape(hid), gain_grad.reshape(width),
    )


def solution(mesh):
    nodes = P(("parts", "mesh", "sub"), None)
    slots = P(("parts", "mesh", "sub"))
    in_specs = (
        nodes,
        P(("parts", "mesh", "sub"), None, None),
        slots,
        slots,
        slots,
        P(None, "lat"),
        P(None, "lat"),
        P("lat"),
        P("lat", None),
        P(),
        nodes,
    )
    out_specs = (
        nodes,
        nodes,
        P("parts", "lat"),
        P("parts", "lat"),
        P(("parts", "lat"), None),
        P(("parts", "lat")),
        P("parts"),
    )
    return jax.shard_map(shards, mesh=mesh, in_specs=in_specs, out_specs=out_specs, check_vma=False)
```

time: 192 us -> 74.6 us (0.39)
  waiting for transfers between devices: 101 us -> 17.1 us
  other arithmetic: 22.1 us -> 0 us
  between operations: 14.1 us -> 0.75 us
  local copies, waits for them, and re-layouts: 14.7 us -> 4.91 us
  Pallas kernels: 0 us -> 7.86 us
  matrix products: 6.43 us -> 0 us
  blocking collectives: 22.2 us -> 27.1 us
  starting transfers between devices: 11.4 us -> 15.9 us
    psum x3 -> x0, waiting for transfers between devices: 98.3 us -> none  [the longest x1 81.8 us: shards(): lax.psum((src_part, dst_part, out_part, bias_part, gain_part), ('mesh', '...]
    all_to_all x0 -> x1, blocking collectives: none -> 27.1 us  [shards(): exchanged = lax.all_to_all(message, ('mesh', 'sub'), 0, 0)]
    psum x1 -> x0, blocking collectives: 22.2 us -> none  [shards(): lax.psum((src_part, dst_part, out_part, bias_part, gain_part), ('mesh', '...]
    ppermute x8, waiting for transfers between devices: 2.4 us -> 16.6 us  [shifted(): return lax.ppermute(x, axis, [(i, (i + by) % count) for i in range(count)])]
    scatter-add x3 -> x0, other arithmetic: 13.5 us -> none  [the longest x1 7.69 us: shards(): jax.ops.segment_sum(jnp.concatenate([back_src, back_dst], axis=0), jnp.co...]
    pallas_call x0 -> x7, Pallas kernels: none -> 7.86 us  [call(): pl.pallas_call(kernel, out_shape=outs, in_specs=[SMEM] * smem + [VMEM] *...]
    gather x4 -> x0, local copies, waits for them, and re-layouts: 7.35 us -> none  [the longest x1 1.97 us: shards(): target_rows = node_state[edge_dst]]
    dot_general x9 -> x0, matrix products: 6.43 us -> none  [the longest x1 1.3 us: edge_forward(): jnp.dot(activated, out_weight, preferred_element_type=jnp.float32)]
  transfers between devices with their start and end apart: 11 -> 9, of which waited for: 4 -> 6; matrix products, arithmetic and copies ran while one was open for 4% -> 0% of each run, Pallas kernels for 0% -> 2%
where the time goes in v1:
time: 74.6 us; the launch traced here: 73.6 us
  blocking collectives  27.1 us (36%)
  waiting for transfers between devices  17.1 us (23%)
  starting transfers between devices  15.9 us (21%)
  Pallas kernels  7.86 us (11%)
  local copies, waits for them, and re-layouts  4.91 us (7%)
  between operations  0.75 us (1%)
    all_to_all x1, blocking collectives, shards(): exchanged = lax.all_to_all(message, ('mesh', 'sub'), 0, 0)  27.1 us
    ppermute x8, waiting for transfers between devices, shifted(): return lax.ppermute(x, axis, [(i, (i + by) % count) for i in range(count)])  16.6 us
    ppermute x8, starting transfers between devices, shifted(): return lax.ppermute(x, axis, [(i, (i + by) % count) for i in range(count)])  12.2 us
    pallas_call x7, Pallas kernels, call(): pl.pallas_call(kernel, out_shape=outs, in_specs=[SMEM] * smem + [VMEM] *...  7.86 us
    unnamed x28, local copies, waits for them, and re-layouts  4.91 us
    all_to_all x1, starting transfers between devices, shards(): gathered = lax.all_to_all(reduced, ('mesh', 'sub'), 0, 0)  3.68 us
  transfers between devices with their start and end apart: 9, of which 6 were waited for; matrix products, arithmetic and copies ran while one was open for 0% of the time, Pallas kernels for 2%

profile of v1, /device:TPU:0, one launch (start us, length us, event | category | flops | bytes accessed | tf_op | source)
XLA Modules:
  0.0 73.6 jit_solution(2519804398731339860)
XLA Ops:
  0.6 0.0 copy-start
  0.6 0.0 copy-start.5
  0.7 0.9 %copy-done.5 = bf16[128,512]{1,0:T(8,128)(2,1)S(1)} copy-done((bf16[128,512]{1,0:T(8,128)(2,1)S(1)}, bf16[128,512]{1,0:T(8,128)(2,1)}, u32[]{:S(2)}) %copy-start.5) | copy-done | bytes 131096
  1.6 0.0 copy-start.10
  1.6 0.7 copy-done.10
  2.3 0.2 shard_map.162
  2.5 3.0 %collective-permute-start.2 = (bf16[64,512]{1,0:T(8,128)(2,1)S(1)}, bf16[64,512]{1,0:T(8,128)(2,1)S(1)}, u32[]{:S(2)}, u32[]{:S(2)}) collective-permute-start(bf16[64,512]{1,0:T(8,128)(2,1)S(1)} %get-tuple-element.28), channel_id=1, source_target_pairs={{0,2},{2,0},{1,3},{3,1},{4,6},{6,4},{5,7},{7,5},{8,10},{10,8},{9,1... | collective-permute-start | bytes 196616 | tf_op jit(solution)/shard_map/ppermute | solution.py:264
  5.5 1.6 %collective-permute-start = (bf16[32,512]{1,0:T(8,128)(2,1)S(1)}, bf16[32,512]{1,0:T(8,128)(2,1)S(1)}, u32[]{:S(2)}, u32[]{:S(2)}) collective-permute-start(bf16[32,512]{1,0:T(8,128)(2,1)S(1)} %get-tuple-element.26), channel_id=1, source_target_pairs={{0,4},{4,8},{8,12},{12,0},{1,5},{5,9},{9,13},{13,1},{2,6},{6,10},{... | collective-permute-start | bytes 98312 | tf_op jit(solution)/shard_map/ppermute | solution.py:264
  7.1 2.2 %collective-permute-start.1 = (bf16[32,512]{1,0:T(8,128)(2,1)S(1)}, bf16[32,512]{1,0:T(8,128)(2,1)S(1)}, u32[]{:S(2)}, u32[]{:S(2)}) collective-permute-start(bf16[32,512]{1,0:T(8,128)(2,1)S(1)} %get-tuple-element.27), channel_id=1, source_target_pairs={{0,12},{4,0},{8,4},{12,8},{1,13},{5,1},{9,5},{13,9},{2,14},{6,2},{... | collective-permute-start | bytes 98312 | tf_op jit(solution)/shard_map/ppermute | solution.py:264
  9.3 2.1 %collective-permute-done.rest_0_ = bf16[32,512]{1,0:T(8,128)(2,1)S(1)} collective-permute-done((bf16[32,512]{1,0:T(8,128)(2,1)S(1)}, bf16[32,512]{1,0:T(8,128)(2,1)S(1)}, u32[]{:S(2)}, u32[]{:S(2)}) %collective-permute-start) | collective-permute-done | bytes 32800 | tf_op jit(solution)/shard_map/ppermute | solution.py:264
  11.5 0.0 collective-permute-done.1.rest_1_
  11.5 0.0 collective-permute-done.2.rest_2_
  11.5 0.0 copy-start.8
  11.5 0.0 copy-start.7
  11.5 0.0 copy-start.12
  11.5 0.0 copy-start.13
  11.5 0.0 copy-done
  11.5 0.6 copy-done.8
  12.1 0.0 copy-done.7
  12.2 0.0 copy-done.12
  12.2 0.0 copy-done.13
  12.2 0.0 copy-start.1
  12.2 0.9 %copy-done.1 = bf16[512,256]{1,0:T(8,128)(2,1)S(1)} copy-done((bf16[512,256]{1,0:T(8,128)(2,1)S(1)}, bf16[512,256]{1,0:T(8,128)(2,1)}, u32[]{:S(2)}) %copy-start.1) | copy-done | bytes 262168
  13.1 0.0 copy-start.3
  13.1 0.9 %copy-done.3 = bf16[256,512]{1,0:T(8,128)(2,1)S(1)} copy-done((bf16[256,512]{1,0:T(8,128)(2,1)S(1)}, bf16[256,512]{1,0:T(8,128)(2,1)}, u32[]{:S(2)}) %copy-start.3) | copy-done | bytes 262168
  14.1 0.0 copy-start.4
  14.1 0.0 copy-start.6
  14.1 2.0 %shard_map.163 = (f32[512,256]{1,0:T(8,128)S(1)}, bf16[128,256]{1,0:T(8,128)(2,1)S(1)}, bf16[128,512]{1,0:T(8,128)(2,1)S(1)}) custom-call(s32[4]{0:T(128)S(1)} %copy-done.12, bf16[128,512]{1,0:T(8,128)(2,1)S(1)} %copy-done.5, s32[1,512]{1,0:T(1,128)S(1)} %bitcast.9, s32[1,512]{1,0:T(1,128)S(1)} %bitcast.11, bf16[512,256]{1,0:T(8,128)(2,1)S(1)} %copy-done, ...), custom_call_target="tpu_custom_call" | custom-call | flops 100000000 | bytes 1000000 | tf_op jit(solution)/shard_map/pallas_call | solution.py:252
  16.1 0.1 collective-permute-start.3
  16.2 1.3 %collective-permute-done.3.other_ref = bf16[128,512]{1,0:T(8,128)(2,1)S(1)} collective-permute-done((bf16[128,512]{1,0:T(8,128)(2,1)S(1)}, bf16[128,512]{1,0:T(8,128)(2,1)S(1)}, u32[]{:S(2)}, u32[]{:S(2)}) %collective-permute-start.3) | collective-permute-done | bytes 131104 | tf_op jit(solution)/shard_map/ppermute | solution.py:264
  17.5 0.0 copy-start.9
  17.5 0.0 copy-done.4
  17.5 0.0 copy-done.6
  17.5 0.7 copy-done.9
  18.2 2.2 %shard_map.164 = (bf16[128,512]{1,0:T(8,128)(2,1)}, bf16[8,208,256]{2,1,0:T(8,128)(2,1)S(1)}, f32[128,256]{1,0:T(8,128)S(1)}, bf16[128,256]{1,0:T(8,128)(2,1)S(1...) custom-call(s32[4]{0:T(128)S(1)} %copy-done.12, ...), custom_call_target="tpu_custom_call" | custom-call | flops 100000000 | bytes 1000000 | tf_op jit(solution)/shard_map/pallas_call | solution.py:252
  20.4 27.1 %all_to_all.10.arrived_ref = bf16[8,208,256]{2,1,0:T(8,128)(2,1)S(1)} all-to-all(bf16[8,208,256]{2,1,0:T(8,128)(2,1)S(1)} %get-tuple-element.38), channel_id=1, replica_groups=mesh['parts'=2,'mesh'=4,'sub'=2,'lat'=2] {'mesh','sub'}, dimensions={0} | all-to-all | bytes 1703936 | tf_op jit(solution)/shard_map/all_to_all | solution.py:324
  47.5 1.0 %shard_map.167 = (bf16[8,192,256]{2,1,0:T(8,128)(2,1)}, f32[1,256]{1,0:T(1,128)}, f32[1,512]{1,0:T(1,128)}) custom-call(bf16[8,208,256]{2,1,0:T(8,128)(2,1)S(1)} %all_to_all.10.arrived_ref), custom_call_target="tpu_custom_call" | custom-call | flops 100000000 | bytes 1000000 | tf_op jit(solution)/shard_map/pallas_call | solution.py:252
  48.5 0.0 copy-start.2
  48.6 3.7 %all-to-all-start.1 = ((bf16[8,192,256]{2,1,0:T(8,128)(2,1)}), bf16[8,192,256]{2,1,0:T(8,128)(2,1)S(1)}, u32[]{:S(2)}, u32[]{:S(2)}) async-start(bf16[8,192,256]{2,1,0:T(8,128)(2,1)} %get-tuple-element.39), calls=%async_computation.1 | async-start | bytes 1572864 | tf_op jit(solution)/shard_map/all_to_all | solution.py:339
  52.2 1.9 %collective-permute-start.6 = (bf16[64,256]{1,0:T(8,128)(2,1)S(1)}, bf16[64,256]{1,0:T(8,128)(2,1)S(1)}, u32[]{:S(2)}, u32[]{:S(2)}) collective-permute-start(bf16[64,256]{1,0:T(8,128)(2,1)S(1)} %get-tuple-element.37), channel_id=1, source_target_pairs={{0,2},{2,0},{1,3},{3,1},{4,6},{6,4},{5,7},{7,5},{8,10},{10,8},{9,1... | collective-permute-start | bytes 98312 | tf_op jit(solution)/shard_map/ppermute | solution.py:264
  54.2 3.3 %collective-permute-start.4 = (bf16[32,256]{1,0:T(8,128)(2,1)S(1)}, bf16[32,256]{1,0:T(8,128)(2,1)S(1)}, u32[]{:S(2)}, u32[]{:S(2)}) collective-permute-start(bf16[32,256]{1,0:T(8,128)(2,1)S(1)} %get-tuple-element.35), channel_id=1, source_target_pairs={{0,12},{4,0},{8,4},{12,8},{1,13},{5,1},{9,5},{13,9},{2,14},{6,2},{... | collective-permute-start | bytes 49160 | tf_op jit(solution)/shard_map/ppermute | solution.py:264
  57.5 0.0 copy-start.11
  57.5 0.0 collective-permute-start.5
  57.5 7.5 %collective-permute-done.4.rest_0_ = bf16[32,256]{1,0:T(8,128)(2,1)S(1)} collective-permute-done((bf16[32,256]{1,0:T(8,128)(2,1)S(1)}, bf16[32,256]{1,0:T(8,128)(2,1)S(1)}, u32[]{:S(2)}, u32[]{:S(2)}) %collective-permute-start.4) | collective-permute-done | bytes 16416 | tf_op jit(solution)/shard_map/ppermute | solution.py:264
  65.0 4.3 %collective-permute-done.5.rest_1_ = bf16[32,256]{1,0:T(8,128)(2,1)S(1)} collective-permute-done((bf16[32,256]{1,0:T(8,128)(2,1)S(1)}, bf16[32,256]{1,0:T(8,128)(2,1)S(1)}, u32[]{:S(2)}, u32[]{:S(2)}) %collective-permute-start.5) | collective-permute-done | bytes 16416 | tf_op jit(solution)/shard_map/ppermute | solution.py:264
  69.3 0.0 collective-permute-done.6.rest_2_
  69.3 0.0 copy-done.2
  69.3 0.0 copy-done.11
  69.3 0.4 shard_map.165.own_ref
  69.7 0.1 collective-permute-start.7
  69.8 1.3 %collective-permute-done.7.other_ref = bf16[128,512]{1,0:T(8,128)(2,1)S(1)} collective-permute-done((bf16[128,512]{1,0:T(8,128)(2,1)S(1)}, bf16[128,512]{1,0:T(8,128)(2,1)S(1)}, u32[]{:S(2)}, u32[]{:S(2)}) %collective-permute-start.7) | collective-permute-done | bytes 131104 | tf_op jit(solution)/shard_map/ppermute | solution.py:264
  71.2 0.7 %shard_map.166 = f32[128,512]{1,0:T(8,128)} custom-call(bf16[128,512]{1,0:T(8,128)(2,1)S(1)} %copy-done.6, bf16[128,512]{1,0:T(8,128)(2,1)S(1)} %shard_map.165.own_ref, bf16[128,512]{1,0:T(8,128)(2,1)S(1)} %collective-permute-done.7.other_ref), custom_call_target="tpu_custom_call" | custom-call | flops 100000000 | bytes 1000000 | tf_op jit(solution)/shard_map/pallas_call | solution.py:252
  71.9 0.5 all-to-all-done.1
  72.4 1.2 %shard_map.168 = (f32[512,256]{1,0:T(8,128)}, f32[512,256]{1,0:T(8,128)}, f32[256,512]{1,0:T(8,128)}) custom-call(bf16[1536,256]{1,0:T(8,128)(2,1)S(1)} %bitcast.8), custom_call_target="tpu_custom_call" | custom-call | flops 100000000 | bytes 1000000 | tf_op jit(solution)/shard_map/pallas_call | solution.py:252
Async XLA Ops:
  0.6 10.9 %copy-start = (bf16[512,256]{1,0:T(8,128)(2,1)S(1)}, bf16[512,256]{1,0:T(8,128)(2,1)}, u32[]{:S(2)}) copy-start(bf16[512,256]{1,0:T(8,128)(2,1)} %w_src_ref.3) | copy-start | bytes 786436
  0.6 0.9 %copy-start.5 = (bf16[128,512]{1,0:T(8,128)(2,1)S(1)}, bf16[128,512]{1,0:T(8,128)(2,1)}, u32[]{:S(2)}) copy-start(bf16[128,512]{1,0:T(8,128)(2,1)} %node_ref.5) | copy-start | bytes 393220
  1.6 0.7 copy-start.10
  2.5 9.0 %collective-permute-start.2 = (bf16[64,512]{1,0:T(8,128)(2,1)S(1)}, bf16[64,512]{1,0:T(8,128)(2,1)S(1)}, u32[]{:S(2)}, u32[]{:S(2)}) collective-permute-start(bf16[64,512]{1,0:T(8,128)(2,1)S(1)} %get-tuple-element.28), channel_id=1, source_target_pairs={{0,2},{2,0},{1,3},{3,1},{4,6},{6,4},{5,7},{7,5},{8,10},{10,8},{9,1... | collective-permute-start | bytes 196616 | tf_op jit(solution)/shard_map/ppermute | solution.py:264
  5.5 5.9 %collective-permute-start = (bf16[32,512]{1,0:T(8,128)(2,1)S(1)}, bf16[32,512]{1,0:T(8,128)(2,1)S(1)}, u32[]{:S(2)}, u32[]{:S(2)}) collective-permute-start(bf16[32,512]{1,0:T(8,128)(2,1)S(1)} %get-tuple-element.26), channel_id=1, source_target_pairs={{0,4},{4,8},{8,12},{12,0},{1,5},{5,9},{9,13},{13,1},{2,6},{6,10},{... | collective-permute-start | bytes 98312 | tf_op jit(solution)/shard_map/ppermute | solution.py:264
  7.1 4.4 %collective-permute-start.1 = (bf16[32,512]{1,0:T(8,128)(2,1)S(1)}, bf16[32,512]{1,0:T(8,128)(2,1)S(1)}, u32[]{:S(2)}, u32[]{:S(2)}) collective-permute-start(bf16[32,512]{1,0:T(8,128)(2,1)S(1)} %get-tuple-element.27), channel_id=1, source_target_pairs={{0,12},{4,0},{8,4},{12,8},{1,13},{5,1},{9,5},{13,9},{2,14},{6,2},{... | collective-permute-start | bytes 98312 | tf_op jit(solution)/shard_map/ppermute | solution.py:264
  11.5 0.7 copy-start.8
  11.5 0.7 copy-start.7
  11.5 0.7 copy-start.12
  11.5 0.7 copy-start.13
  12.2 0.9 %copy-start.1 = (bf16[512,256]{1,0:T(8,128)(2,1)S(1)}, bf16[512,256]{1,0:T(8,128)(2,1)}, u32[]{:S(2)}) copy-start(bf16[512,256]{1,0:T(8,128)(2,1)} %w_dst_ref.3) | copy-start | bytes 786436
  13.1 0.9 %copy-start.3 = (bf16[256,512]{1,0:T(8,128)(2,1)S(1)}, bf16[256,512]{1,0:T(8,128)(2,1)}, u32[]{:S(2)}) copy-start(bf16[256,512]{1,0:T(8,128)(2,1)} %w_out_ref.3) | copy-start | bytes 786436
  14.1 3.4 %copy-start.4 = (bf16[256,512]{1,0:T(8,128)(2,1)S(1)}, bf16[256,512]{1,0:T(8,128)(2,1)}, u32[]{:S(2)}) copy-start(bf16[256,512]{1,0:T(8,128)(2,1)} %w_out_ref.3) | copy-start | bytes 786436
  14.1 3.4 %copy-start.6 = (bf16[128,512]{1,0:T(8,128)(2,1)S(1)}, bf16[128,512]{1,0:T(8,128)(2,1)}, u32[]{:S(2)}) copy-start(bf16[128,512]{1,0:T(8,128)(2,1)} %cot_ref.3) | copy-start | bytes 393220
  16.1 1.4 %collective-permute-start.3 = (bf16[128,512]{1,0:T(8,128)(2,1)S(1)}, bf16[128,512]{1,0:T(8,128)(2,1)S(1)}, u32[]{:S(2)}, u32[]{:S(2)}) collective-permute-start(bf16[128,512]{1,0:T(8,128)(2,1)S(1)} %get-tuple-element.31.own_ref), channel_id=1, source_target_pairs={{0,1},{1,0},{2,3},{3,2},{4,5},{5,4},{6,7},{7,6},{8,9},{9,8},{10,11... | collective-permute-start | bytes 393224 | tf_op jit(solution)/shard_map/ppermute | solution.py:264
  17.5 0.7 copy-start.9
  48.5 20.7 %copy-start.2 = (bf16[512,256]{1,0:T(8,128)(2,1)S(1)}, bf16[512,256]{1,0:T(8,128)(2,1)}, u32[]{:S(2)}) copy-start(bf16[512,256]{1,0:T(8,128)(2,1)} %w_dst_ref.3) | copy-start | bytes 786436
  48.6 23.8 %all-to-all-start.1 = ((bf16[8,192,256]{2,1,0:T(8,128)(2,1)}), bf16[8,192,256]{2,1,0:T(8,128)(2,1)S(1)}, u32[]{:S(2)}, u32[]{:S(2)}) async-start(bf16[8,192,256]{2,1,0:T(8,128)(2,1)} %get-tuple-element.39), calls=%async_computation.1 | async-start | bytes 1572864 | tf_op jit(solution)/shard_map/all_to_all | solution.py:339
  52.2 17.0 %collective-permute-start.6 = (bf16[64,256]{1,0:T(8,128)(2,1)S(1)}, bf16[64,256]{1,0:T(8,128)(2,1)S(1)}, u32[]{:S(2)}, u32[]{:S(2)}) collective-permute-start(bf16[64,256]{1,0:T(8,128)(2,1)S(1)} %get-tuple-element.37), channel_id=1, source_target_pairs={{0,2},{2,0},{1,3},{3,1},{4,6},{6,4},{5,7},{7,5},{8,10},{10,8},{9,1... | collective-permute-start | bytes 98312 | tf_op jit(solution)/shard_map/ppermute | solution.py:264
  54.2 10.8 %collective-permute-start.4 = (bf16[32,256]{1,0:T(8,128)(2,1)S(1)}, bf16[32,256]{1,0:T(8,128)(2,1)S(1)}, u32[]{:S(2)}, u32[]{:S(2)}) collective-permute-start(bf16[32,256]{1,0:T(8,128)(2,1)S(1)} %get-tuple-element.35), channel_id=1, source_target_pairs={{0,12},{4,0},{8,4},{12,8},{1,13},{5,1},{9,5},{13,9},{2,14},{6,2},{... | collective-permute-start | bytes 49160 | tf_op jit(solution)/shard_map/ppermute | solution.py:264
  57.5 11.8 %copy-start.11 = (s32[1,4,32]{2,1,0:T(4,128)S(1)}, s32[1,4,32]{2,1,0:T(4,128)}, u32[]{:S(2)}) copy-start(s32[1,4,32]{2,1,0:T(4,128)} %param.12) | copy-start | bytes 1540
  57.5 11.8 %collective-permute-start.5 = (bf16[32,256]{1,0:T(8,128)(2,1)S(1)}, bf16[32,256]{1,0:T(8,128)(2,1)S(1)}, u32[]{:S(2)}, u32[]{:S(2)}) collective-permute-start(bf16[32,256]{1,0:T(8,128)(2,1)S(1)} %get-tuple-element.36), channel_id=1, source_target_pairs={{0,4},{4,8},{8,12},{12,0},{1,5},{5,9},{9,13},{13,1},{2,6},{6,10},{... | collective-permute-start | bytes 49160 | tf_op jit(solution)/shard_map/ppermute | solution.py:264
  69.7 1.4 %collective-permute-start.7 = (bf16[128,512]{1,0:T(8,128)(2,1)S(1)}, bf16[128,512]{1,0:T(8,128)(2,1)S(1)}, u32[]{:S(2)}, u32[]{:S(2)}) collective-permute-start(bf16[128,512]{1,0:T(8,128)(2,1)S(1)} %shard_map.165.own_ref), channel_id=1, source_target_pairs={{0,1},{1,0},{2,3},{3,2},{4,5},{5,4},{6,7},{7,6},{8,9},{9,8},{10,11... | collective-permute-start | bytes 393224 | tf_op jit(solution)/shard_map/ppermute | solution.py:264

commit v2 on v1

--- a/solution.py
+++ b/solution.py
@@ -117,11 +117,12 @@
     other_ref,
     *rest,
 ):
-    peers, chunk, merged = geometry
-    n_halo = 3 if merged else 4
+    peers, chunk, n_halo, n_message, paired = geometry
+    *rest, out_scratch = rest
     halo_refs = rest[:n_halo]
-    updated_ref, message_ref, local_ref, target_ref = rest[n_halo : n_halo + 4]
-    back_refs = rest[n_halo + 4 :]
+    updated_ref, local_ref, target_ref = rest[n_halo : n_halo + 3]
+    back_refs = rest[n_halo + 3 : 2 * n_halo + 3]
+    message_refs = rest[2 * n_halo + 3 :]
     node = node_ref[...]
     rows, width = node.shape
     edges = src_ref.shape[1]
@@ -166,9 +167,6 @@
     src_part = dot(table, by_source.astype(bf16), TN).astype(bf16)
     dst_part = dot(node, by_target_low, TN).astype(bf16)
     out_part = dot(hidden_ref[...], agg_grad, TN).astype(bf16)
-    blocks = [src_part, dst_part]
-    for at in range(0, width, hid):
-        blocks.append(out_part[:, at : at + hid])
     vectors = [bias_part] + [gain_part[:, at : at + hid] for at in range(0, width, hid)]
     tail = []
     for v in vectors:
@@ -176,6 +174,35 @@
         tail += [high.astype(f32), (v - high.astype(f32))]
     tail.append(jnp.zeros((TAIL - len(tail), hid), f32))
     tail = jnp.concatenate(tail, axis=0).astype(bf16)
+
+    if paired:
+        send_ref, keep_ref, *out_refs = message_refs
+        sub = lax.axis_index("sub")
+        mesh = lax.axis_index("mesh")
+
+        @pl.when(sub == 0)
+        def _():
+            send_ref[0:width, :] = dst_part
+            keep_ref[0:width, :] = src_part
+
+        @pl.when(sub == 1)
+        def _():
+            send_ref[0:width, :] = src_part
+            keep_ref[0:width, :] = dst_part
+
+        send_ref[width:, :] = tail
+        keep_ref[width:, :] = tail
+        out_scratch[...] = out_part
+        strip = hid // len(out_refs)
+        for k, ref in enumerate(out_refs):
+            start = pl.multiple_of((mesh ^ k) * strip, strip)
+            ref[...] = out_scratch[pl.ds(start, strip), :]
+        return
+
+    (message_ref,) = message_refs
+    blocks = [src_part, dst_part]
+    for at in range(0, width, hid):
+        blocks.append(out_part[:, at : at + hid])
     done = 0
     for block in blocks:
         at = 0
@@ -194,6 +221,77 @@
         message_ref[peer, chunk:, :] = tail
 
 
+def tree(terms):
+    while len(terms) > 1:
+        terms = [terms[i] + terms[i + 1] for i in range(0, len(terms), 2)]
+    return terms[0]
+
+
+def turn_kernel(count, keep_ref, arrived_ref, *refs):
+    out_terms = refs[:count]
+    line_refs = refs[count : 2 * count]
+    out_send_ref, out_keep_ref, scratch = refs[2 * count :]
+    sub = lax.axis_index("sub")
+    mesh = lax.axis_index("mesh")
+    hid = keep_ref.shape[1]
+    total = keep_ref[...].astype(f32) + arrived_ref[...].astype(f32)
+    rows = total.shape[0] - TAIL
+    strip = rows // count
+    vectors = total[rows:]
+    high = vectors.astype(bf16)
+    low = (vectors - high.astype(f32)).astype(bf16)
+    scratch[...] = total[:rows].astype(bf16)
+    for k, ref in enumerate(line_refs):
+        start = pl.multiple_of((mesh ^ k) * strip, strip)
+        ref[0:strip, :] = scratch[pl.ds(start, strip), :]
+        ref[strip : strip + TAIL, :] = high
+        ref[strip + TAIL :, :] = low
+    out = tree([r[...].astype(f32) for r in out_terms])
+    left, right = out[:, :hid], out[:, hid:]
+    out_send_ref[...] = jnp.where(sub == 0, right, left).astype(bf16)
+    out_keep_ref[...] = jnp.where(sub == 0, left, right).astype(bf16)
+
+
+def own_kernel(count, *refs):
+    line_refs = refs[:count]
+    out_keep_ref, out_arrived_ref, own_ref, bias_ref, gain_ref = refs[count:]
+    total = tree([r[...].astype(f32) for r in line_refs])
+    strip = own_ref.shape[0] - out_keep_ref.shape[0]
+    own_ref[0:strip, :] = total[:strip].astype(bf16)
+    own_ref[strip:, :] = (
+        out_keep_ref[...].astype(f32) + out_arrived_ref[...].astype(f32)
+    ).astype(bf16)
+    tail = total[strip : strip + TAIL] + total[strip + TAIL :]
+    write_vectors(tail, bias_ref, gain_ref)
+
+
+def write_vectors(tail, bias_ref, gain_ref):
+    bias_ref[...] = tail[0:1] + tail[1:2]
+    hid = tail.shape[1]
+    for k in range(gain_ref.shape[1] // hid):
+        gain_ref[:, k * hid : (k + 1) * hid] = tail[2 + 2 * k : 3 + 2 * k] + tail[3 + 2 * k : 4 + 2 * k]
+
+
+def place_kernel(count, *refs):
+    mine, theirs = refs[:count], refs[count : 2 * count]
+    src_ref, dst_ref, out_ref = refs[2 * count :]
+    first = lax.axis_index("sub") == 0
+    mesh = lax.axis_index("mesh")
+    width, hid = src_ref.shape
+    strip = width // count
+    narrow = hid // count
+    for k in range(count):
+        a, b = mine[k][...], theirs[k][...]
+        low = jnp.where(first, a, b).astype(f32)
+        high = jnp.where(first, b, a).astype(f32)
+        start = pl.multiple_of((mesh ^ k) * strip, strip)
+        src_ref[pl.ds(start, strip), :] = low[:strip]
+        dst_ref[pl.ds(start, strip), :] = high[:strip]
+        start = pl.multiple_of((mesh ^ k) * narrow, narrow)
+        out_ref[pl.ds(start, narrow), 0:hid] = low[strip:]
+        out_ref[pl.ds(start, narrow), hid:] = high[strip:]
+
+
 def sum_kernel(chunk, arrived_ref, out_ref, bias_ref, gain_ref):
     peers = arrived_ref.shape[0]
     total = arrived_ref[0].astype(f32)
@@ -203,10 +301,7 @@
     for peer in range(peers):
         out_ref[peer] = low
     tail = total[chunk:]
-    bias_ref[...] = tail[0:1] + tail[1:2]
-    hid = tail.shape[1]
-    for k in range(gain_ref.shape[1] // hid):
-        gain_ref[:, k * hid : (k + 1) * hid] = tail[2 + 2 * k : 3 + 2 * k] + tail[3 + 2 * k : 4 + 2 * k]
+    write_vectors(tail, bias_ref, gain_ref)
 
 
 def unpack_kernel(arrived_ref, src_ref, dst_ref, out_ref):
@@ -248,12 +343,13 @@
     return jax.ShapeDtypeStruct(dims, dtype)
 
 
-def call(kernel, outs, *args, smem=0, flops=10**8):
+def call(kernel, outs, *args, smem=0, flops=10**8, scratch=()):
     return pl.pallas_call(
         kernel,
         out_shape=outs,
         in_specs=[SMEM] * smem + [VMEM] * (len(args) - smem),
         out_specs=jax.tree.map(lambda _: VMEM, outs),
+        scratch_shapes=scratch,
         compiler_params=pltpu.CompilerParams(vmem_limit_bytes=VMEM_LIMIT),
         cost_estimate=pl.CostEstimate(flops=flops, bytes_accessed=10**6, transcendentals=0),
     )(*args)
@@ -262,6 +358,37 @@
 def shifted(x, axis, by):
     count = lax.axis_size(axis)
     return lax.ppermute(x, axis, [(i, (i + by) % count) for i in range(count)])
+
+
+def across(x, axis, k):
+    count = lax.axis_size(axis)
+    return lax.ppermute(x, axis, [(i, i ^ k) for i in range(count)])
+
+
+def paired_sums(messages, lines, strip, narrow, width, hid):
+    send, keep, *outs = messages
+    out_terms = [outs[0]] + [across(outs[k], "mesh", k) for k in range(1, lines)]
+    arrived = across(send, "sub", 1)
+    *line, out_send, out_keep = call(
+        functools.partial(turn_kernel, lines),
+        [shape((strip + 2 * TAIL, hid), bf16)] * lines + [shape((narrow, hid), bf16)] * 2,
+        keep, arrived, *out_terms,
+        scratch=[pltpu.VMEM((width, hid), bf16)],
+    )
+    line_terms = [line[0]] + [across(line[k], "mesh", k) for k in range(1, lines)]
+    own, bias_grad, gain_grad = call(
+        functools.partial(own_kernel, lines),
+        [shape((strip + narrow, hid), bf16), shape((1, hid), f32), shape((1, width), f32)],
+        *line_terms, out_keep, across(out_send, "sub", 1),
+    )
+    mine = [own] + [across(own, "mesh", k) for k in range(1, lines)]
+    theirs = [across(x, "sub", 1) for x in mine]
+    grads = call(
+        functools.partial(place_kernel, lines),
+        [shape((width, hid), f32), shape((width, hid), f32), shape((hid, width), f32)],
+        *mine, *theirs,
+    )
+    return (*grads, bias_grad, gain_grad)
 
 
 def shards(
@@ -306,22 +433,29 @@
     )
     other = shifted(partial, "lat", 1)
 
-    updated, message, local, target, *backs = call(
-        functools.partial(backward_kernel, (peers, chunk, merged)),
-        [
-            shape((rows, width), bf16),
-            shape((peers, chunk + TAIL, hid), bf16),
-            shape((rows, hid), f32),
-            shape((rows, hid), bf16),
-        ]
-        + [shape((n, hid), bf16) for n in piece],
+    lines = lax.axis_size("mesh")
+    paired = merged and lines == 4
+    if paired:
+        strip = width // lines
+        narrow = hid // lines
+        message_shapes = [shape((width + TAIL, hid), bf16)] * 2 + [shape((narrow, width), bf16)] * lines
+    else:
+        message_shapes = [shape((peers, chunk + TAIL, hid), bf16)]
+    n_halo = len(piece)
+    updated, local, target, *rest = call(
+        functools.partial(
+            backward_kernel, (peers, chunk, n_halo, len(message_shapes), paired)
+        ),
+        [shape((rows, width), bf16), shape((rows, hid), f32), shape((rows, hid), bf16)]
+        + [shape((n, hid), bf16) for n in piece]
+        + message_shapes,
         block_count, node_state, src, dst, w_out, gain, cotangent, factor, hidden, partial, other,
         *arrived,
         smem=1,
-    )
+        scratch=[pltpu.VMEM((hid, width), bf16)],
+    )
+    backs, messages = rest[:n_halo], rest[n_halo:]
     returned = [shifted(x, axis, -by) for x, (axis, by) in zip(backs, routes)]
-
-    exchanged = lax.all_to_all(message, ("mesh", "sub"), 0, 0)
 
     node_part = call(
         node_kernel, shape((rows, width), bf16), send, local, target, w_src, w_dst, *returned
@@ -331,17 +465,23 @@
         cotangent, node_part, shifted(node_part, "lat", 1),
     )
 
-    reduced, bias_grad, gain_grad = call(
-        functools.partial(sum_kernel, chunk),
-        [shape((peers, chunk, hid), bf16), shape((1, hid), f32), shape((1, width), f32)],
-        exchanged,
-    )
-    gathered = lax.all_to_all(reduced, ("mesh", "sub"), 0, 0)
-    src_grad, dst_grad, out_grad = call(
-        unpack_kernel,
-        [shape((width, hid), f32), shape((width, hid), f32), shape((hid, width), f32)],
-        gathered.reshape(peers * chunk, hid),
-    )
+    if paired:
+        src_grad, dst_grad, out_grad, bias_grad, gain_grad = paired_sums(
+            messages, lines, strip, narrow, width, hid
+        )
+    else:
+        exchanged = lax.all_to_all(messages[0], ("mesh", "sub"), 0, 0)
+        reduced, bias_grad, gain_grad = call(
+            functools.partial(sum_kernel, chunk),
+            [shape((peers, chunk, hid), bf16), shape((1, hid), f32), shape((1, width), f32)],
+            exchanged,
+        )
+        gathered = lax.all_to_all(reduced, ("mesh", "sub"), 0, 0)
+        src_grad, dst_grad, out_grad = call(
+            unpack_kernel,
+            [shape((width, hid), f32), shape((width, hid), f32), shape((hid, width), f32)],
+            gathered.reshape(peers * chunk, hid),
+        )
     return (
         updated, node_grad, src_grad, dst_grad, out_grad,
         bias_grad.reshape(hid), gain_grad.reshape(width),

time: 74.6 us -> 68.6 us (0.920)
  blocking collectives: 27.1 us -> 0 us
  starting transfers between devices: 15.9 us -> 32.7 us
  waiting for transfers between devices: 17.1 us -> 21.9 us
    all_to_all x1 -> x0, blocking collectives: 27.1 us -> none  [shards(): exchanged = lax.all_to_all(message, ('mesh', 'sub'), 0, 0)]
    ppermute x0 -> x15, starting transfers between devices: none -> 19.5 us  [across(): return lax.ppermute(x, axis, [(i, i ^ k) for i in range(count)])]
    ppermute x0 -> x15, waiting for transfers between devices: none -> 14.9 us  [across(): return lax.ppermute(x, axis, [(i, i ^ k) for i in range(count)])]
    ppermute x8, waiting for transfers between devices: 16.6 us -> 6.96 us  [shifted(): return lax.ppermute(x, axis, [(i, (i + by) % count) for i in range(count)])]
    all_to_all x1 -> x0, starting transfers between devices: 3.68 us -> none  [shards(): gathered = lax.all_to_all(reduced, ('mesh', 'sub'), 0, 0)]
    ppermute x8, starting transfers between devices: 12.2 us -> 13.2 us  [shifted(): return lax.ppermute(x, axis, [(i, (i + by) % count) for i in range(count)])]
    pallas_call x7 -> x8, Pallas kernels: 7.86 us -> 8.06 us  [call(): pl.pallas_call(kernel, out_shape=outs, in_specs=[SMEM] * smem + [VMEM] *...]
  transfers between devices with their start and end apart: 9 -> 23, of which waited for: 6 -> 12; matrix products, arithmetic and copies ran while one was open for 0% -> 0% of each run, Pallas kernels for 2% -> 2%
where the time goes in v2:
time: 68.6 us; the launch traced here: 68.3 us
  starting transfers between devices  32.7 us (48%)
  waiting for transfers between devices  21.9 us (32%)
  Pallas kernels  8.06 us (12%)
  local copies, waits for them, and re-layouts  4.91 us (7%)
  between operations  0.78 us (1%)
    ppermute x15, starting transfers between devices, across(): return lax.ppermute(x, axis, [(i, i ^ k) for i in range(count)])  19.5 us
    ppermute x15, waiting for transfers between devices, across(): return lax.ppermute(x, axis, [(i, i ^ k) for i in range(count)])  14.9 us
    ppermute x8, starting transfers between devices, shifted(): return lax.ppermute(x, axis, [(i, (i + by) % count) for i in range(count)])  13.2 us
    pallas_call x8, Pallas kernels, call(): pl.pallas_call(kernel, out_shape=outs, in_specs=[SMEM] * smem + [VMEM] *...  8.06 us
    ppermute x8, waiting for transfers between devices, shifted(): return lax.ppermute(x, axis, [(i, (i + by) % count) for i in range(count)])  6.96 us
    unnamed x28, local copies, waits for them, and re-layouts  4.91 us
  transfers between devices with their start and end apart: 23, of which 12 were waited for; matrix products, arithmetic and copies ran while one was open for 0% of the time, Pallas kernels for 2%

profile of v2, /device:TPU:0, one launch (start us, length us, event | category | flops | bytes accessed | tf_op | source)
XLA Modules:
  0.0 68.3 jit_solution(5893006925465322256)
XLA Ops:
  0.7 0.9 %copy-done.5 = bf16[128,512]{1,0:T(8,128)(2,1)S(1)} copy-done((bf16[128,512]{1,0:T(8,128)(2,1)S(1)}, bf16[128,512]{1,0:T(8,128)(2,1)}, u32[]{:S(2)}) %copy-start.5) | copy-done | bytes 131096
  1.6 0.7 copy-done.10
  2.3 0.2 shard_map.162
  2.5 3.0 %collective-permute-start.2 = (bf16[64,512]{1,0:T(8,128)(2,1)S(1)}, bf16[64,512]{1,0:T(8,128)(2,1)S(1)}, u32[]{:S(2)}, u32[]{:S(2)}) collective-permute-start(bf16[64,512]{1,0:T(8,128)(2,1)S(1)} %get-tuple-element.39), channel_id=1, source_target_pairs={{0,2},{2,0},{1,3},{3,1},{4,6},{6,4},{5,7},{7,5},{8,10},{10,8},{9,1... | collective-permute-start | bytes 196616 | tf_op jit(solution)/shard_map/ppermute | solution.py:360
  5.5 1.6 %collective-permute-start = (bf16[32,512]{1,0:T(8,128)(2,1)S(1)}, bf16[32,512]{1,0:T(8,128)(2,1)S(1)}, u32[]{:S(2)}, u32[]{:S(2)}) collective-permute-start(bf16[32,512]{1,0:T(8,128)(2,1)S(1)} %get-tuple-element.37), channel_id=1, source_target_pairs={{0,4},{4,8},{8,12},{12,0},{1,5},{5,9},{9,13},{13,1},{2,6},{6,10},{... | collective-permute-start | bytes 98312 | tf_op jit(solution)/shard_map/ppermute | solution.py:360
  7.1 2.2 %collective-permute-start.1 = (bf16[32,512]{1,0:T(8,128)(2,1)S(1)}, bf16[32,512]{1,0:T(8,128)(2,1)S(1)}, u32[]{:S(2)}, u32[]{:S(2)}) collective-permute-start(bf16[32,512]{1,0:T(8,128)(2,1)S(1)} %get-tuple-element.38), channel_id=1, source_target_pairs={{0,12},{4,0},{8,4},{12,8},{1,13},{5,1},{9,5},{13,9},{2,14},{6,2},{... | collective-permute-start | bytes 98312 | tf_op jit(solution)/shard_map/ppermute | solution.py:360
  9.3 2.1 %collective-permute-done.rest_0_ = bf16[32,512]{1,0:T(8,128)(2,1)S(1)} collective-permute-done((bf16[32,512]{1,0:T(8,128)(2,1)S(1)}, bf16[32,512]{1,0:T(8,128)(2,1)S(1)}, u32[]{:S(2)}, u32[]{:S(2)}) %collective-permute-start) | collective-permute-done | bytes 32800 | tf_op jit(solution)/shard_map/ppermute | solution.py:360
  11.5 0.0 collective-permute-done.1.rest_1_
  11.5 0.0 collective-permute-done.2.rest_2_
  11.5 0.0 copy-start.7
  11.5 0.0 copy-start.12
  11.5 0.0 copy-start.13
  11.5 0.6 copy-done.8
  12.1 0.0 copy-done.7
  12.2 0.0 copy-done.13
  12.2 0.9 %copy-done.1 = bf16[512,256]{1,0:T(8,128)(2,1)S(1)} copy-done((bf16[512,256]{1,0:T(8,128)(2,1)S(1)}, bf16[512,256]{1,0:T(8,128)(2,1)}, u32[]{:S(2)}) %copy-start.1) | copy-done | bytes 262168
  13.1 0.9 %copy-done.3 = bf16[256,512]{1,0:T(8,128)(2,1)S(1)} copy-done((bf16[256,512]{1,0:T(8,128)(2,1)S(1)}, bf16[256,512]{1,0:T(8,128)(2,1)}, u32[]{:S(2)}) %copy-start.3) | copy-done | bytes 262168
  14.1 2.0 %shard_map.163 = (f32[512,256]{1,0:T(8,128)S(1)}, bf16[128,256]{1,0:T(8,128)(2,1)S(1)}, bf16[128,512]{1,0:T(8,128)(2,1)S(1)}) custom-call(s32[4]{0:T(128)S(1)} %copy-done.12, bf16[128,512]{1,0:T(8,128)(2,1)S(1)} %copy-done.5, s32[1,512]{1,0:T(1,128)S(1)} %bitcast.7, s32[1,512]{1,0:T(1,128)S(1)} %bitcast.9, bf16[512,256]{1,0:T(8,128)(2,1)S(1)} %copy-done, ...), custom_call_target="tpu_custom_call" | custom-call | flops 100000000 | bytes 1000000 | tf_op jit(solution)/shard_map/pallas_call | solution.py:347
  16.1 0.1 collective-permute-start.3
  16.2 1.3 %collective-permute-done.3.other_ref = bf16[128,512]{1,0:T(8,128)(2,1)S(1)} collective-permute-done((bf16[128,512]{1,0:T(8,128)(2,1)S(1)}, bf16[128,512]{1,0:T(8,128)(2,1)S(1)}, u32[]{:S(2)}, u32[]{:S(2)}) %collective-permute-start.3) | collective-permute-done | bytes 131104 | tf_op jit(solution)/shard_map/ppermute | solution.py:360
  17.5 0.7 copy-done.9
  18.2 2.6 %shard_map.164 = (bf16[128,512]{1,0:T(8,128)(2,1)}, f32[128,256]{1,0:T(8,128)S(1)}, bf16[128,256]{1,0:T(8,128)(2,1)S(1)}, bf16[32,256]{1,0:T(8,128)(2,1)S(1)}, b...) custom-call(s32[4]{0:T(128)S(1)} %copy-done.12, ...), custom_call_target="tpu_custom_call" | custom-call | flops 100000000 | bytes 1000000 | tf_op jit(solution)/shard_map/pallas_call | solution.py:347
  20.8 0.4 collective-permute-start.8
  21.3 1.2 %collective-permute-start.9 = (bf16[64,512]{1,0:T(8,128)(2,1)S(1)}, bf16[64,512]{1,0:T(8,128)(2,1)S(1)}, u32[]{:S(2)}, u32[]{:S(2)}) collective-permute-start(bf16[64,512]{1,0:T(8,128)(2,1)S(1)} %get-tuple-element.52), channel_id=1, source_target_pairs={{0,4},{4,0},{8,12},{12,8},{1,5},{5,1},{9,13},{13,9},{2,6},{6,2},{1... | collective-permute-start | bytes 196616 | tf_op jit(solution)/shard_map/ppermute | solution.py:365
  22.5 2.8 %collective-permute-start.10 = (bf16[64,512]{1,0:T(8,128)(2,1)S(1)}, bf16[64,512]{1,0:T(8,128)(2,1)S(1)}, u32[]{:S(2)}, u32[]{:S(2)}) collective-permute-start(bf16[64,512]{1,0:T(8,128)(2,1)S(1)} %get-tuple-element.53), channel_id=1, source_target_pairs={{0,8},{4,12},{8,0},{12,4},{1,9},{5,13},{9,1},{13,5},{2,10},{6,14},... | collective-permute-start | bytes 196616 | tf_op jit(solution)/shard_map/ppermute | solution.py:365
  25.3 0.3 collective-permute-start.11
  25.7 0.0 collective-permute-done.9.refs_1_
  25.7 4.3 %collective-permute-done.10.refs_2_ = bf16[64,512]{1,0:T(8,128)(2,1)S(1)} collective-permute-done((bf16[64,512]{1,0:T(8,128)(2,1)S(1)}, bf16[64,512]{1,0:T(8,128)(2,1)S(1)}, u32[]{:S(2)}, u32[]{:S(2)}) %collective-permute-start.10) | collective-permute-done | bytes 65568 | tf_op jit(solution)/shard_map/ppermute | solution.py:365
  29.9 1.5 %collective-permute-done.11.refs_3_ = bf16[64,512]{1,0:T(8,128)(2,1)S(1)} collective-permute-done((bf16[64,512]{1,0:T(8,128)(2,1)S(1)}, bf16[64,512]{1,0:T(8,128)(2,1)S(1)}, u32[]{:S(2)}, u32[]{:S(2)}) %collective-permute-start.11) | collective-permute-done | bytes 65568 | tf_op jit(solution)/shard_map/ppermute | solution.py:365
  31.4 0.0 collective-permute-done.8.arrived_ref
  31.4 0.2 shard_map.167
  31.6 0.0 copy-start.2
  31.6 0.1 collective-permute-start.12
  31.7 2.2 %collective-permute-start.13 = (bf16[160,256]{1,0:T(8,128)(2,1)S(1)}, bf16[160,256]{1,0:T(8,128)(2,1)S(1)}, u32[]{:S(2)}, u32[]{:S(2)}) collective-permute-start(bf16[160,256]{1,0:T(8,128)(2,1)S(1)} %get-tuple-element.57), channel_id=1, source_target_pairs={{0,8},{4,12},{8,0},{12,4},{1,9},{5,13},{9,1},{13,5},{2,10},{6,14},... | collective-permute-start | bytes 245768 | tf_op jit(solution)/shard_map/ppermute | solution.py:365
  33.9 2.2 %collective-permute-start.14 = (bf16[160,256]{1,0:T(8,128)(2,1)S(1)}, bf16[160,256]{1,0:T(8,128)(2,1)S(1)}, u32[]{:S(2)}, u32[]{:S(2)}) collective-permute-start(bf16[160,256]{1,0:T(8,128)(2,1)S(1)} %get-tuple-element.58), channel_id=1, source_target_pairs={{0,12},{4,8},{8,4},{12,0},{1,13},{5,9},{9,5},{13,1},{2,14},{6,10},... | collective-permute-start | bytes 245768 | tf_op jit(solution)/shard_map/ppermute | solution.py:365
  36.0 1.7 %collective-permute-start.15 = (bf16[64,256]{1,0:T(8,128)(2,1)S(1)}, bf16[64,256]{1,0:T(8,128)(2,1)S(1)}, u32[]{:S(2)}, u32[]{:S(2)}) collective-permute-start(bf16[64,256]{1,0:T(8,128)(2,1)S(1)} %get-tuple-element.60), channel_id=1, source_target_pairs={{0,2},{2,0},{1,3},{3,1},{4,6},{6,4},{5,7},{7,5},{8,10},{10,8},{9,1... | collective-permute-start | bytes 98312 | tf_op jit(solution)/shard_map/ppermute | solution.py:365
  37.7 2.2 %collective-permute-done.15.refs_5_ = bf16[64,256]{1,0:T(8,128)(2,1)S(1)} collective-permute-done((bf16[64,256]{1,0:T(8,128)(2,1)S(1)}, bf16[64,256]{1,0:T(8,128)(2,1)S(1)}, u32[]{:S(2)}, u32[]{:S(2)}) %collective-permute-start.15) | collective-permute-done | bytes 32800 | tf_op jit(solution)/shard_map/ppermute | solution.py:365
  40.0 0.0 collective-permute-done.12.refs_1_
  40.0 0.3 collective-permute-done.13.refs_2_
  40.3 0.0 collective-permute-done.14.refs_3_
  40.3 0.6 shard_map.168
  40.9 2.4 %collective-permute-start.18 = (bf16[192,256]{1,0:T(8,128)(2,1)S(1)}, bf16[192,256]{1,0:T(8,128)(2,1)S(1)}, u32[]{:S(2)}, u32[]{:S(2)}) collective-permute-start(bf16[192,256]{1,0:T(8,128)(2,1)S(1)} %get-tuple-element.61.refs_0_), channel_id=1, source_target_pairs={{0,12},{4,8},{8,4},{12,0},{1,13},{5,9},{9,5},{13,1},{2,14},{6,10},... | collective-permute-start | bytes 294920 | tf_op jit(solution)/shard_map/ppermute | solution.py:365
  43.3 0.5 collective-permute-start.17
  43.8 1.5 %collective-permute-start.16 = (bf16[192,256]{1,0:T(8,128)(2,1)S(1)}, bf16[192,256]{1,0:T(8,128)(2,1)S(1)}, u32[]{:S(2)}, u32[]{:S(2)}) collective-permute-start(bf16[192,256]{1,0:T(8,128)(2,1)S(1)} %get-tuple-element.61.refs_0_), channel_id=1, source_target_pairs={{0,4},{4,0},{8,12},{12,8},{1,5},{5,1},{9,13},{13,9},{2,6},{6,2},{1... | collective-permute-start | bytes 294920 | tf_op jit(solution)/shard_map/ppermute | solution.py:365
  45.3 2.4 %collective-permute-start.4 = (bf16[32,256]{1,0:T(8,128)(2,1)S(1)}, bf16[32,256]{1,0:T(8,128)(2,1)S(1)}, u32[]{:S(2)}, u32[]{:S(2)}) collective-permute-start(bf16[32,256]{1,0:T(8,128)(2,1)S(1)} %get-tuple-element.46), channel_id=1, source_target_pairs={{0,12},{4,0},{8,4},{12,8},{1,13},{5,1},{9,5},{13,9},{2,14},{6,2},{... | collective-permute-start | bytes 49160 | tf_op jit(solution)/shard_map/ppermute | solution.py:360
  47.7 1.4 %collective-permute-start.6 = (bf16[64,256]{1,0:T(8,128)(2,1)S(1)}, bf16[64,256]{1,0:T(8,128)(2,1)S(1)}, u32[]{:S(2)}, u32[]{:S(2)}) collective-permute-start(bf16[64,256]{1,0:T(8,128)(2,1)S(1)} %get-tuple-element.48), channel_id=1, source_target_pairs={{0,2},{2,0},{1,3},{3,1},{4,6},{6,4},{5,7},{7,5},{8,10},{10,8},{9,1... | collective-permute-start | bytes 98312 | tf_op jit(solution)/shard_map/ppermute | solution.py:360
  49.1 0.1 collective-permute-done.4.rest_0_
  49.2 2.4 %collective-permute-start.5 = (bf16[32,256]{1,0:T(8,128)(2,1)S(1)}, bf16[32,256]{1,0:T(8,128)(2,1)S(1)}, u32[]{:S(2)}, u32[]{:S(2)}) collective-permute-start(bf16[32,256]{1,0:T(8,128)(2,1)S(1)} %get-tuple-element.47), channel_id=1, source_target_pairs={{0,4},{4,8},{8,12},{12,0},{1,5},{5,9},{9,13},{13,1},{2,6},{6,10},{... | collective-permute-start | bytes 49160 | tf_op jit(solution)/shard_map/ppermute | solution.py:360
  51.6 3.4 %collective-permute-done.5.rest_1_ = bf16[32,256]{1,0:T(8,128)(2,1)S(1)} collective-permute-done((bf16[32,256]{1,0:T(8,128)(2,1)S(1)}, bf16[32,256]{1,0:T(8,128)(2,1)S(1)}, u32[]{:S(2)}, u32[]{:S(2)}) %collective-permute-start.5) | collective-permute-done | bytes 16416 | tf_op jit(solution)/shard_map/ppermute | solution.py:360
  55.0 0.4 shard_map.165.own_ref
  55.5 0.1 collective-permute-start.7
  55.6 1.5 %collective-permute-start.19 = (bf16[192,256]{1,0:T(8,128)(2,1)S(1)}, bf16[192,256]{1,0:T(8,128)(2,1)S(1)}, u32[]{:S(2)}, u32[]{:S(2)}) collective-permute-start(bf16[192,256]{1,0:T(8,128)(2,1)S(1)} %get-tuple-element.61.refs_0_), channel_id=1, source_target_pairs={{0,2},{2,0},{1,3},{3,1},{4,6},{6,4},{5,7},{7,5},{8,10},{10,8},{9,1... | collective-permute-start | bytes 294920 | tf_op jit(solution)/shard_map/ppermute | solution.py:365
  57.1 0.0 collective-permute-done.18.refs_3_
  57.1 0.6 collective-permute-start.22
  57.6 0.0 collective-permute-done.17.refs_2_
  57.7 1.4 %collective-permute-start.21 = (bf16[192,256]{1,0:T(8,128)(2,1)S(1)}, bf16[192,256]{1,0:T(8,128)(2,1)S(1)}, u32[]{:S(2)}, u32[]{:S(2)}) collective-permute-start(bf16[192,256]{1,0:T(8,128)(2,1)S(1)} %collective-permute-done.17.refs_2_), channel_id=1, source_target_pairs={{0,2},{2,0},{1,3},{3,1},{4,6},{6,4},{5,7},{7,5},{8,10},{10,8},{9,1... | collective-permute-start | bytes 294920 | tf_op jit(solution)/shard_map/ppermute | solution.py:365
  59.1 0.6 collective-permute-start.20
  59.7 0.0 collective-permute-done.7.other_ref
  59.7 0.7 %shard_map.166 = f32[128,512]{1,0:T(8,128)} custom-call(bf16[128,512]{1,0:T(8,128)(2,1)S(1)} %copy-done.6, bf16[128,512]{1,0:T(8,128)(2,1)S(1)} %shard_map.165.own_ref, bf16[128,512]{1,0:T(8,128)(2,1)S(1)} %collective-permute-done.7.other_ref), custom_call_target="tpu_custom_call" | custom-call | flops 100000000 | bytes 1000000 | tf_op jit(solution)/shard_map/pallas_call | solution.py:347
  60.4 0.8 %collective-permute-done.19.refs_4_ = bf16[192,256]{1,0:T(8,128)(2,1)S(1)} collective-permute-done((bf16[192,256]{1,0:T(8,128)(2,1)S(1)}, bf16[192,256]{1,0:T(8,128)(2,1)S(1)}, u32[]{:S(2)}, u32[]{:S(2)}) %collective-permute-start.19) | collective-permute-done | bytes 98336 | tf_op jit(solution)/shard_map/ppermute | solution.py:365
  61.2 2.1 %collective-permute-done.22.refs_7_ = bf16[192,256]{1,0:T(8,128)(2,1)S(1)} collective-permute-done((bf16[192,256]{1,0:T(8,128)(2,1)S(1)}, bf16[192,256]{1,0:T(8,128)(2,1)S(1)}, u32[]{:S(2)}, u32[]{:S(2)}) %collective-permute-start.22) | collective-permute-done | bytes 98336 | tf_op jit(solution)/shard_map/ppermute | solution.py:365
  63.3 2.1 %collective-permute-done.21.refs_6_ = bf16[192,256]{1,0:T(8,128)(2,1)S(1)} collective-permute-done((bf16[192,256]{1,0:T(8,128)(2,1)S(1)}, bf16[192,256]{1,0:T(8,128)(2,1)S(1)}, u32[]{:S(2)}, u32[]{:S(2)}) %collective-permute-start.21) | collective-permute-done | bytes 98336 | tf_op jit(solution)/shard_map/ppermute | solution.py:365
  65.4 1.7 %collective-permute-done.20.refs_5_ = bf16[192,256]{1,0:T(8,128)(2,1)S(1)} collective-permute-done((bf16[192,256]{1,0:T(8,128)(2,1)S(1)}, bf16[192,256]{1,0:T(8,128)(2,1)S(1)}, u32[]{:S(2)}, u32[]{:S(2)}) %collective-permute-start.20) | collective-permute-done | bytes 98336 | tf_op jit(solution)/shard_map/ppermute | solution.py:365
  67.1 1.2 %shard_map.169 = (f32[512,256]{1,0:T(8,128)}, f32[512,256]{1,0:T(8,128)}, f32[256,512]{1,0:T(8,128)}) custom-call(bf16[192,256]{1,0:T(8,128)(2,1)S(1)} %get-tuple-element.61.refs_0_, bf16[192,256]{1,0:T(8,128)(2,1)S(1)} %collective-permute-done.16.refs_1_, bf16[192,256]{1,0:T(8,128)(2,1)S(1)} %collective-permute-done.17.refs_2_, ...), custom_call_target="tpu_custom_call" | custom-call | flops 100000000 | bytes 1000000 | tf_op jit(solution)/shard_map/pallas_call | solution.py:347
  (18 shorter events, 0.0 us)
Async XLA Ops:
  0.6 10.9 %copy-start = (bf16[512,256]{1,0:T(8,128)(2,1)S(1)}, bf16[512,256]{1,0:T(8,128)(2,1)}, u32[]{:S(2)}) copy-start(bf16[512,256]{1,0:T(8,128)(2,1)} %w_src_ref.3) | copy-start | bytes 786436
  0.6 0.9 %copy-start.5 = (bf16[128,512]{1,0:T(8,128)(2,1)S(1)}, bf16[128,512]{1,0:T(8,128)(2,1)}, u32[]{:S(2)}) copy-start(bf16[128,512]{1,0:T(8,128)(2,1)} %node_ref.5) | copy-start | bytes 393220
  1.6 0.7 copy-start.10
  2.5 9.0 %collective-permute-start.2 = (bf16[64,512]{1,0:T(8,128)(2,1)S(1)}, bf16[64,512]{1,0:T(8,128)(2,1)S(1)}, u32[]{:S(2)}, u32[]{:S(2)}) collective-permute-start(bf16[64,512]{1,0:T(8,128)(2,1)S(1)} %get-tuple-element.39), channel_id=1, source_target_pairs={{0,2},{2,0},{1,3},{3,1},{4,6},{6,4},{5,7},{7,5},{8,10},{10,8},{9,1... | collective-permute-start | bytes 196616 | tf_op jit(solution)/shard_map/ppermute | solution.py:360
  5.5 5.9 %collective-permute-start = (bf16[32,512]{1,0:T(8,128)(2,1)S(1)}, bf16[32,512]{1,0:T(8,128)(2,1)S(1)}, u32[]{:S(2)}, u32[]{:S(2)}) collective-permute-start(bf16[32,512]{1,0:T(8,128)(2,1)S(1)} %get-tuple-element.37), channel_id=1, source_target_pairs={{0,4},{4,8},{8,12},{12,0},{1,5},{5,9},{9,13},{13,1},{2,6},{6,10},{... | collective-permute-start | bytes 98312 | tf_op jit(solution)/shard_map/ppermute | solution.py:360
  7.1 4.4 %collective-permute-start.1 = (bf16[32,512]{1,0:T(8,128)(2,1)S(1)}, bf16[32,512]{1,0:T(8,128)(2,1)S(1)}, u32[]{:S(2)}, u32[]{:S(2)}) collective-permute-start(bf16[32,512]{1,0:T(8,128)(2,1)S(1)} %get-tuple-element.38), channel_id=1, source_target_pairs={{0,12},{4,0},{8,4},{12,8},{1,13},{5,1},{9,5},{13,9},{2,14},{6,2},{... | collective-permute-start | bytes 98312 | tf_op jit(solution)/shard_map/ppermute | solution.py:360
  11.5 0.7 %copy-start.8 = (s32[512]{0:T(512)S(1)}, s32[512]{0:T(512)}, u32[]{:S(2)}) copy-start(s32[512]{0:T(512)} %param.14) | copy-start | bytes 6148
  11.5 0.7 %copy-start.7 = (s32[512]{0:T(512)S(1)}, s32[512]{0:T(512)}, u32[]{:S(2)}) copy-start(s32[512]{0:T(512)} %param.13) | copy-start | bytes 6148
  11.5 0.7 %copy-start.12 = (s32[4]{0:T(128)S(1)}, s32[4]{0:T(128)}, u32[]{:S(2)}) copy-start(s32[4]{0:T(128)} %count_ref.3) | copy-start | bytes 52
  11.5 0.7 %copy-start.13 = (f32[256]{0:T(256)S(1)}, f32[256]{0:T(256)}, u32[]{:S(2)}) copy-start(f32[256]{0:T(256)} %param.18) | copy-start | bytes 3076
  12.2 0.9 %copy-start.1 = (bf16[512,256]{1,0:T(8,128)(2,1)S(1)}, bf16[512,256]{1,0:T(8,128)(2,1)}, u32[]{:S(2)}) copy-start(bf16[512,256]{1,0:T(8,128)(2,1)} %w_dst_ref.3) | copy-start | bytes 786436
  13.1 0.9 %copy-start.3 = (bf16[256,512]{1,0:T(8,128)(2,1)S(1)}, bf16[256,512]{1,0:T(8,128)(2,1)}, u32[]{:S(2)}) copy-start(bf16[256,512]{1,0:T(8,128)(2,1)} %w_out_ref.3) | copy-start | bytes 786436
  14.1 3.4 %copy-start.4 = (bf16[256,512]{1,0:T(8,128)(2,1)S(1)}, bf16[256,512]{1,0:T(8,128)(2,1)}, u32[]{:S(2)}) copy-start(bf16[256,512]{1,0:T(8,128)(2,1)} %w_out_ref.3) | copy-start | bytes 786436
  14.1 3.4 %copy-start.6 = (bf16[128,512]{1,0:T(8,128)(2,1)S(1)}, bf16[128,512]{1,0:T(8,128)(2,1)}, u32[]{:S(2)}) copy-start(bf16[128,512]{1,0:T(8,128)(2,1)} %cot_ref.3) | copy-start | bytes 393220
  16.1 1.4 %collective-permute-start.3 = (bf16[128,512]{1,0:T(8,128)(2,1)S(1)}, bf16[128,512]{1,0:T(8,128)(2,1)S(1)}, u32[]{:S(2)}, u32[]{:S(2)}) collective-permute-start(bf16[128,512]{1,0:T(8,128)(2,1)S(1)} %get-tuple-element.42.own_ref), channel_id=1, source_target_pairs={{0,1},{1,0},{2,3},{3,2},{4,5},{5,4},{6,7},{7,6},{8,9},{9,8},{10,11... | collective-permute-start | bytes 393224 | tf_op jit(solution)/shard_map/ppermute | solution.py:360
  17.5 0.7 copy-start.9
  20.8 10.5 %collective-permute-start.8 = (bf16[528,256]{1,0:T(8,128)(2,1)S(1)}, bf16[528,256]{1,0:T(8,128)(2,1)S(1)}, u32[]{:S(2)}, u32[]{:S(2)}) collective-permute-start(bf16[528,256]{1,0:T(8,128)(2,1)S(1)} %get-tuple-element.50), channel_id=1, source_target_pairs={{0,2},{2,0},{1,3},{3,1},{4,6},{6,4},{5,7},{7,5},{8,10},{10,8},{9,1... | collective-permute-start | bytes 811016 | tf_op jit(solution)/shard_map/ppermute | solution.py:365
  21.3 4.4 %collective-permute-start.9 = (bf16[64,512]{1,0:T(8,128)(2,1)S(1)}, bf16[64,512]{1,0:T(8,128)(2,1)S(1)}, u32[]{:S(2)}, u32[]{:S(2)}) collective-permute-start(bf16[64,512]{1,0:T(8,128)(2,1)S(1)} %get-tuple-element.52), channel_id=1, source_target_pairs={{0,4},{4,0},{8,12},{12,8},{1,5},{5,1},{9,13},{13,9},{2,6},{6,2},{1... | collective-permute-start | bytes 196616 | tf_op jit(solution)/shard_map/ppermute | solution.py:365
  22.5 7.4 %collective-permute-start.10 = (bf16[64,512]{1,0:T(8,128)(2,1)S(1)}, bf16[64,512]{1,0:T(8,128)(2,1)S(1)}, u32[]{:S(2)}, u32[]{:S(2)}) collective-permute-start(bf16[64,512]{1,0:T(8,128)(2,1)S(1)} %get-tuple-element.53), channel_id=1, source_target_pairs={{0,8},{4,12},{8,0},{12,4},{1,9},{5,13},{9,1},{13,5},{2,10},{6,14},... | collective-permute-start | bytes 196616 | tf_op jit(solution)/shard_map/ppermute | solution.py:365
  25.3 6.1 %collective-permute-start.11 = (bf16[64,512]{1,0:T(8,128)(2,1)S(1)}, bf16[64,512]{1,0:T(8,128)(2,1)S(1)}, u32[]{:S(2)}, u32[]{:S(2)}) collective-permute-start(bf16[64,512]{1,0:T(8,128)(2,1)S(1)} %get-tuple-element.54), channel_id=1, source_target_pairs={{0,12},{4,8},{8,4},{12,0},{1,13},{5,9},{9,5},{13,1},{2,14},{6,10},... | collective-permute-start | bytes 196616 | tf_op jit(solution)/shard_map/ppermute | solution.py:365
  31.6 23.4 %copy-start.2 = (bf16[512,256]{1,0:T(8,128)(2,1)S(1)}, bf16[512,256]{1,0:T(8,128)(2,1)}, u32[]{:S(2)}) copy-start(bf16[512,256]{1,0:T(8,128)(2,1)} %w_dst_ref.3) | copy-start | bytes 786436
  31.6 8.4 %collective-permute-start.12 = (bf16[160,256]{1,0:T(8,128)(2,1)S(1)}, bf16[160,256]{1,0:T(8,128)(2,1)S(1)}, u32[]{:S(2)}, u32[]{:S(2)}) collective-permute-start(bf16[160,256]{1,0:T(8,128)(2,1)S(1)} %get-tuple-element.56), channel_id=1, source_target_pairs={{0,4},{4,0},{8,12},{12,8},{1,5},{5,1},{9,13},{13,9},{2,6},{6,2},{1... | collective-permute-start | bytes 245768 | tf_op jit(solution)/shard_map/ppermute | solution.py:365
  31.7 8.6 %collective-permute-start.13 = (bf16[160,256]{1,0:T(8,128)(2,1)S(1)}, bf16[160,256]{1,0:T(8,128)(2,1)S(1)}, u32[]{:S(2)}, u32[]{:S(2)}) collective-permute-start(bf16[160,256]{1,0:T(8,128)(2,1)S(1)} %get-tuple-element.57), channel_id=1, source_target_pairs={{0,8},{4,12},{8,0},{12,4},{1,9},{5,13},{9,1},{13,5},{2,10},{6,14},... | collective-permute-start | bytes 245768 | tf_op jit(solution)/shard_map/ppermute | solution.py:365
  33.9 6.4 %collective-permute-start.14 = (bf16[160,256]{1,0:T(8,128)(2,1)S(1)}, bf16[160,256]{1,0:T(8,128)(2,1)S(1)}, u32[]{:S(2)}, u32[]{:S(2)}) collective-permute-start(bf16[160,256]{1,0:T(8,128)(2,1)S(1)} %get-tuple-element.58), channel_id=1, source_target_pairs={{0,12},{4,8},{8,4},{12,0},{1,13},{5,9},{9,5},{13,1},{2,14},{6,10},... | collective-permute-start | bytes 245768 | tf_op jit(solution)/shard_map/ppermute | solution.py:365
  36.0 3.9 %collective-permute-start.15 = (bf16[64,256]{1,0:T(8,128)(2,1)S(1)}, bf16[64,256]{1,0:T(8,128)(2,1)S(1)}, u32[]{:S(2)}, u32[]{:S(2)}) collective-permute-start(bf16[64,256]{1,0:T(8,128)(2,1)S(1)} %get-tuple-element.60), channel_id=1, source_target_pairs={{0,2},{2,0},{1,3},{3,1},{4,6},{6,4},{5,7},{7,5},{8,10},{10,8},{9,1... | collective-permute-start | bytes 98312 | tf_op jit(solution)/shard_map/ppermute | solution.py:365
  40.9 16.2 %collective-permute-start.18 = (bf16[192,256]{1,0:T(8,128)(2,1)S(1)}, bf16[192,256]{1,0:T(8,128)(2,1)S(1)}, u32[]{:S(2)}, u32[]{:S(2)}) collective-permute-start(bf16[192,256]{1,0:T(8,128)(2,1)S(1)} %get-tuple-element.61.refs_0_), channel_id=1, source_target_pairs={{0,12},{4,8},{8,4},{12,0},{1,13},{5,9},{9,5},{13,1},{2,14},{6,10},... | collective-permute-start | bytes 294920 | tf_op jit(solution)/shard_map/ppermute | solution.py:365
  43.3 14.3 %collective-permute-start.17 = (bf16[192,256]{1,0:T(8,128)(2,1)S(1)}, bf16[192,256]{1,0:T(8,128)(2,1)S(1)}, u32[]{:S(2)}, u32[]{:S(2)}) collective-permute-start(bf16[192,256]{1,0:T(8,128)(2,1)S(1)} %get-tuple-element.61.refs_0_), channel_id=1, source_target_pairs={{0,8},{4,12},{8,0},{12,4},{1,9},{5,13},{9,1},{13,5},{2,10},{6,14},... | collective-permute-start | bytes 294920 | tf_op jit(solution)/shard_map/ppermute | solution.py:365
  43.8 15.3 %collective-permute-start.16 = (bf16[192,256]{1,0:T(8,128)(2,1)S(1)}, bf16[192,256]{1,0:T(8,128)(2,1)S(1)}, u32[]{:S(2)}, u32[]{:S(2)}) collective-permute-start(bf16[192,256]{1,0:T(8,128)(2,1)S(1)} %get-tuple-element.61.refs_0_), channel_id=1, source_target_pairs={{0,4},{4,0},{8,12},{12,8},{1,5},{5,1},{9,13},{13,9},{2,6},{6,2},{1... | collective-permute-start | bytes 294920 | tf_op jit(solution)/shard_map/ppermute | solution.py:365
  45.3 3.9 %collective-permute-start.4 = (bf16[32,256]{1,0:T(8,128)(2,1)S(1)}, bf16[32,256]{1,0:T(8,128)(2,1)S(1)}, u32[]{:S(2)}, u32[]{:S(2)}) collective-permute-start(bf16[32,256]{1,0:T(8,128)(2,1)S(1)} %get-tuple-element.46), channel_id=1, source_target_pairs={{0,12},{4,0},{8,4},{12,8},{1,13},{5,1},{9,5},{13,9},{2,14},{6,2},{... | collective-permute-start | bytes 49160 | tf_op jit(solution)/shard_map/ppermute | solution.py:360
  47.7 7.3 %collective-permute-start.6 = (bf16[64,256]{1,0:T(8,128)(2,1)S(1)}, bf16[64,256]{1,0:T(8,128)(2,1)S(1)}, u32[]{:S(2)}, u32[]{:S(2)}) collective-permute-start(bf16[64,256]{1,0:T(8,128)(2,1)S(1)} %get-tuple-element.48), channel_id=1, source_target_pairs={{0,2},{2,0},{1,3},{3,1},{4,6},{6,4},{5,7},{7,5},{8,10},{10,8},{9,1... | collective-permute-start | bytes 98312 | tf_op jit(solution)/shard_map/ppermute | solution.py:360
  49.2 5.8 %copy-start.11 = (s32[1,4,32]{2,1,0:T(4,128)S(1)}, s32[1,4,32]{2,1,0:T(4,128)}, u32[]{:S(2)}) copy-start(s32[1,4,32]{2,1,0:T(4,128)} %param.12) | copy-start | bytes 1540
  49.2 5.8 %collective-permute-start.5 = (bf16[32,256]{1,0:T(8,128)(2,1)S(1)}, bf16[32,256]{1,0:T(8,128)(2,1)S(1)}, u32[]{:S(2)}, u32[]{:S(2)}) collective-permute-start(bf16[32,256]{1,0:T(8,128)(2,1)S(1)} %get-tuple-element.47), channel_id=1, source_target_pairs={{0,4},{4,8},{8,12},{12,0},{1,5},{5,9},{9,13},{13,1},{2,6},{6,10},{... | collective-permute-start | bytes 49160 | tf_op jit(solution)/shard_map/ppermute | solution.py:360
  55.5 4.2 %collective-permute-start.7 = (bf16[128,512]{1,0:T(8,128)(2,1)S(1)}, bf16[128,512]{1,0:T(8,128)(2,1)S(1)}, u32[]{:S(2)}, u32[]{:S(2)}) collective-permute-start(bf16[128,512]{1,0:T(8,128)(2,1)S(1)} %shard_map.165.own_ref), channel_id=1, source_target_pairs={{0,1},{1,0},{2,3},{3,2},{4,5},{5,4},{6,7},{7,6},{8,9},{9,8},{10,11... | collective-permute-start | bytes 393224 | tf_op jit(solution)/shard_map/ppermute | solution.py:360
  55.6 5.7 %collective-permute-start.19 = (bf16[192,256]{1,0:T(8,128)(2,1)S(1)}, bf16[192,256]{1,0:T(8,128)(2,1)S(1)}, u32[]{:S(2)}, u32[]{:S(2)}) collective-permute-start(bf16[192,256]{1,0:T(8,128)(2,1)S(1)} %get-tuple-element.61.refs_0_), channel_id=1, source_target_pairs={{0,2},{2,0},{1,3},{3,1},{4,6},{6,4},{5,7},{7,5},{8,10},{10,8},{9,1... | collective-permute-start | bytes 294920 | tf_op jit(solution)/shard_map/ppermute | solution.py:365
  57.1 6.3 %collective-permute-start.22 = (bf16[192,256]{1,0:T(8,128)(2,1)S(1)}, bf16[192,256]{1,0:T(8,128)(2,1)S(1)}, u32[]{:S(2)}, u32[]{:S(2)}) collective-permute-start(bf16[192,256]{1,0:T(8,128)(2,1)S(1)} %collective-permute-done.18.refs_3_), channel_id=1, source_target_pairs={{0,2},{2,0},{1,3},{3,1},{4,6},{6,4},{5,7},{7,5},{8,10},{10,8},{9,1... | collective-permute-start | bytes 294920 | tf_op jit(solution)/shard_map/ppermute | solution.py:365
  57.7 7.8 %collective-permute-start.21 = (bf16[192,256]{1,0:T(8,128)(2,1)S(1)}, bf16[192,256]{1,0:T(8,128)(2,1)S(1)}, u32[]{:S(2)}, u32[]{:S(2)}) collective-permute-start(bf16[192,256]{1,0:T(8,128)(2,1)S(1)} %collective-permute-done.17.refs_2_), channel_id=1, source_target_pairs={{0,2},{2,0},{1,3},{3,1},{4,6},{6,4},{5,7},{7,5},{8,10},{10,8},{9,1... | collective-permute-start | bytes 294920 | tf_op jit(solution)/shard_map/ppermute | solution.py:365
  59.1 8.0 %collective-permute-start.20 = (bf16[192,256]{1,0:T(8,128)(2,1)S(1)}, bf16[192,256]{1,0:T(8,128)(2,1)S(1)}, u32[]{:S(2)}, u32[]{:S(2)}) collective-permute-start(bf16[192,256]{1,0:T(8,128)(2,1)S(1)} %collective-permute-done.16.refs_1_), channel_id=1, source_target_pairs={{0,2},{2,0},{1,3},{3,1},{4,6},{6,4},{5,7},{7,5},{8,10},{10,8},{9,1... | collective-permute-start | bytes 294920 | tf_op jit(solution)/shard_map/ppermute | solution.py:365

commit v3 on v2

v3 whole, which is shorter than its diff:
```python
import functools

import jax
import jax.numpy as jnp
from jax import lax
from jax.experimental import pallas as pl
from jax.experimental.pallas import tpu as pltpu
from jax.sharding import PartitionSpec as P

BLOCK = 128
EPSILON = 1e-05
TAIL = 16
VMEM_LIMIT = 24 * 1024 * 1024

f32 = jnp.float32
bf16 = jnp.bfloat16

NN = (((1,), (0,)), ((), ()))
NT = (((1,), (1,)), ((), ()))
TN = (((0,), (0,)), ((), ()))


def dot(a, b, dims=NN):
    return lax.dot_general(a, b, dims, preferred_element_type=f32)


def iota(shape, dim):
    return lax.broadcasted_iota(jnp.int32, shape, dim)


def one_hot(condition):
    return jnp.where(condition, 1.0, 0.0).astype(bf16)


def split(x):
    high = x.astype(bf16)
    return high, (x - high.astype(f32)).astype(bf16)


def columns_of(row, lanes):
    return jnp.transpose(jnp.broadcast_to(row, (lanes, row.shape[1])))


def usable_row(count_ref, edges):
    lane = iota((1, BLOCK), 1)
    parts = [lane < count_ref[b] for b in range(edges // BLOCK)]
    return jnp.concatenate([jnp.where(p, 1, 0) for p in parts], axis=1)


def usable_columns(count_ref, edges, lanes):
    sub = iota((BLOCK, lanes), 0)
    return jnp.concatenate(
        [jnp.where(sub < count_ref[b], 1, 0) for b in range(edges // BLOCK)], axis=0
    )


def fetch(sems, *pairs):
    copies = [pltpu.make_async_copy(a, b, sems.at[i]) for i, (a, b) in enumerate(pairs)]
    for copy in copies:
        copy.start()
    return copies


def send_kernel(node_hbm, send_hbm, node_ref, send_ref, *rest):
    *out_refs, sems = rest
    for copy in fetch(sems, (node_hbm, node_ref), (send_hbm, send_ref)):
        copy.wait()
    node = node_ref[...]
    rows = node.shape[0]
    halo = send_ref.shape[2]
    pieces = []
    for d in range(4):
        pick = one_hot(iota((rows, halo), 0) == send_ref[0, d : d + 1, :])
        pieces.append(dot(pick, node, TN).astype(bf16))
    out_refs[0][...] = pieces[0]
    out_refs[1][...] = pieces[1]
    if len(out_refs) == 3:
        out_refs[2][0:halo, :] = pieces[2]
        out_refs[2][halo:, :] = pieces[3]
    else:
        out_refs[2][...] = pieces[2]
        out_refs[3][...] = pieces[3]


def local_kernel(
    count_ref, node_ref, src_hbm, dst_hbm, bias_hbm, w_src_hbm, w_dst_hbm, w_out_hbm, gain_hbm, cot_hbm,
    pre_ref, pick_ref, collect_ref, spread_ref, scatter_ref,
    w_src_ref, w_dst_ref, w_out_ref, gain_ref, cot_ref,
    src_ref, dst_ref, bias_ref, sems,
):
    copies = fetch(
        sems, (src_hbm, src_ref), (dst_hbm, dst_ref), (bias_hbm, bias_ref), (w_src_hbm, w_src_ref),
        (w_dst_hbm, w_dst_ref), (w_out_hbm, w_out_ref), (gain_hbm, gain_ref), (cot_hbm, cot_ref),
    )
    node = node_ref[...]
    rows = node.shape[0]
    edges = src_ref.shape[1]
    copies[0].wait()
    copies[1].wait()
    scatter_ref[...] = one_hot(iota(scatter_ref.shape, 0) == src_ref[...])
    used = usable_row(count_ref, edges) > 0
    collect_ref[...] = one_hot((iota((rows, edges), 0) == dst_ref[...]) & used)
    source = columns_of(src_ref[...], 128)
    target = columns_of(dst_ref[...], 128)
    lane = iota(source.shape, 1)
    used = usable_columns(count_ref, edges, 128) > 0
    near = one_hot(source == lane)
    pick_ref[...] = one_hot(source == lane + rows)
    spread_ref[...] = one_hot((target == lane) & used)
    both = jnp.concatenate([dot(near, node), dot(one_hot(target == lane), node)], axis=1).astype(bf16)
    copies[2].wait()
    copies[3].wait()
    copies[4].wait()
    weights = jnp.concatenate([w_src_ref[...], w_dst_ref[...]], axis=0)
    pre_ref[...] = dot(both, weights) + bias_ref[...]
    for copy in copies[5:]:
        copy.wait()


def twice(x):
    return jnp.concatenate([x, x], axis=1)


def stacked(x):
    return jnp.concatenate(split(x), axis=0)


def forward_kernel(pre_ref, pick_ref, collect_ref, w_src_ref, w_out_ref, *rest):
    *halo_refs, factor_ref, hidden_ref, partial_ref = rest
    halo = jnp.concatenate([r[...] for r in halo_refs], axis=0)
    far = stacked(dot(halo, w_src_ref[...]))
    pre = pre_ref[...] + dot(twice(pick_ref[...]), far)
    sig = 0.5 + 0.5 * jnp.tanh(0.5 * pre)
    factor_ref[...] = sig * (1.0 + pre * (1.0 - sig))
    hidden = dot(collect_ref[...], (pre * sig).astype(bf16))
    high, low = split(hidden)
    hidden_ref[...] = high
    w_out = w_out_ref[...]
    partial_ref[...] = (dot(high, w_out) + dot(low, w_out)).astype(bf16)


def backward_kernel(
    geometry,
    node_ref, collect_ref, spread_ref, scatter_ref, w_out_ref, gain_ref, cot_ref,
    factor_ref, hidden_ref, own_ref, other_ref,
    *rest,
):
    peers, chunk, n_halo, paired = geometry
    *rest, out_scratch, back_scratch = rest
    halo_refs = rest[:n_halo]
    updated_ref, local_ref, target_ref, *message_refs = rest[n_halo:]
    node = node_ref[...]
    rows, width = node.shape
    aggregate = own_ref[...].astype(f32) + other_ref[...].astype(f32)
    center = aggregate - jnp.mean(aggregate, axis=1, keepdims=True)
    variance = jnp.mean(center * center, axis=1, keepdims=True)
    inverse = lax.rsqrt(variance + EPSILON)
    normed = center * inverse
    gain = gain_ref[...]
    upstream = cot_ref[...].astype(f32)
    scaled = upstream * gain
    agg_grad = inverse * (
        scaled
        - jnp.mean(scaled, axis=1, keepdims=True)
        - normed * jnp.mean(scaled * normed, axis=1, keepdims=True)
    )
    agg_grad = agg_grad.astype(bf16)
    updated_ref[...] = (node.astype(f32) + gain * normed).astype(bf16)
    gain_part = jnp.sum(upstream * normed, axis=0, keepdims=True)

    act_grad = dot(twice(spread_ref[...]), stacked(dot(agg_grad, w_out_ref[...], NT)))
    pre_grad = (act_grad * factor_ref[...]).astype(bf16)

    table = jnp.concatenate([node] + [r[...] for r in halo_refs], axis=0)
    by_source = dot(scatter_ref[...], pre_grad)
    by_target = dot(collect_ref[...], pre_grad)
    local_ref[...] = by_source[:rows]
    by_target_low = by_target.astype(bf16)
    by_source_low = by_source.astype(bf16)
    target_ref[...] = by_target_low

    hid = by_source.shape[1]
    bias_part = jnp.sum(by_target, axis=0, keepdims=True)
    src_part = dot(table, by_source_low, TN).astype(bf16)
    dst_part = dot(node, by_target_low, TN).astype(bf16)
    out_part = dot(hidden_ref[...], agg_grad, TN).astype(bf16)
    vectors = [bias_part] + [gain_part[:, at : at + hid] for at in range(0, width, hid)]
    tail = tail_of(vectors)
    back = by_source_low[rows:]

    if paired:
        send_ref, keep_ref, *out_refs = message_refs
        sub = lax.axis_index("sub")
        mesh = lax.axis_index("mesh")

        @pl.when(sub == 0)
        def _():
            send_ref[0:width, :] = dst_part
            keep_ref[0:width, :] = src_part

        @pl.when(sub == 1)
        def _():
            send_ref[0:width, :] = src_part
            keep_ref[0:width, :] = dst_part

        halo = back.shape[0] // 4
        send_ref[width : width + TAIL, :] = tail
        keep_ref[width:, :] = tail
        send_ref[width + TAIL :, :] = back[2 * halo :]
        back_scratch[...] = back[: 2 * halo]
        out_scratch[...] = out_part
        strip = hid // len(out_refs)
        for k, ref in enumerate(out_refs):
            start = pl.multiple_of((mesh ^ k) * strip, strip)
            ref[0:strip, :] = out_scratch[pl.ds(start, strip), :]
            if k % 2 == 1:
                slot = (mesh + (k // 2) + 1) % 2
                start = pl.multiple_of(slot * halo, halo)
                rows_back = back_scratch[pl.ds(start, halo), :]
                ref[strip:, 0:hid] = rows_back[: halo // 2]
                ref[strip:, hid:] = rows_back[halo // 2 :]
        return

    message_ref, *back_refs = message_refs
    at = 0
    for ref in back_refs:
        ref[...] = back[at : at + ref.shape[0]]
        at += ref.shape[0]
    blocks = [src_part, dst_part]
    for at in range(0, width, hid):
        blocks.append(out_part[:, at : at + hid])
    done = 0
    for block in blocks:
        at = 0
        while at < block.shape[0]:
            peer, offset = divmod(done, chunk)
            take = min(chunk - offset, block.shape[0] - at)
            message_ref[peer, offset : offset + take, :] = block[at : at + take]
            at += take
            done += take
    while done < peers * chunk:
        peer, offset = divmod(done, chunk)
        take = chunk - offset
        message_ref[peer, offset : offset + take, :] = jnp.zeros((take, hid), bf16)
        done += take
    for peer in range(peers):
        message_ref[peer, chunk:, :] = tail


def tail_of(vectors):
    tail = []
    for v in vectors:
        high = v.astype(bf16).astype(f32)
        tail += [high, v - high]
    tail.append(jnp.zeros((TAIL - len(tail), vectors[0].shape[1]), f32))
    return jnp.concatenate(tail, axis=0).astype(bf16)


def tree(terms):
    while len(terms) > 1:
        terms = [terms[i] + terms[i + 1] for i in range(0, len(terms), 2)]
    return terms[0]


def turn_kernel(count, *refs):
    out_terms = refs[count - 1 :: -1]
    arrived_ref, keep_ref, *refs = refs[count:]
    refs = [None] * count + refs
    line_refs = refs[count : 2 * count]
    out_send_ref, out_keep_ref, scratch = refs[2 * count :]
    sub = lax.axis_index("sub")
    mesh = lax.axis_index("mesh")
    full, hid = keep_ref.shape
    total = keep_ref[...].astype(f32) + arrived_ref[0:full, :].astype(f32)
    rows = full - TAIL
    strip = rows // count
    tail = total[rows:]
    tail = tail_of([tail[at : at + 1] + tail[at + 1 : at + 2] for at in range(0, 6, 2)])
    scratch[...] = total[:rows].astype(bf16)
    for k, ref in enumerate(line_refs):
        start = pl.multiple_of((mesh ^ k) * strip, strip)
        ref[0:strip, :] = scratch[pl.ds(start, strip), :]
        ref[strip:, :] = tail
    out_strip = out_keep_ref.shape[0]
    out = tree([r[0:out_strip, :].astype(f32) for r in out_terms])
    left, right = out[:, :hid], out[:, hid:]
    out_send_ref[...] = jnp.where(sub == 0, right, left).astype(bf16)
    out_keep_ref[...] = jnp.where(sub == 0, left, right).astype(bf16)


def own_kernel(count, *refs):
    line_refs = refs[count - 1 :: -1]
    out_keep_ref, out_arrived_ref, own_ref, bias_ref, gain_ref = refs[count:]
    total = tree([r[...].astype(f32) for r in line_refs])
    strip = own_ref.shape[0] - out_keep_ref.shape[0]
    own_ref[0:strip, :] = total[:strip].astype(bf16)
    own_ref[strip:, :] = (
        out_keep_ref[...].astype(f32) + out_arrived_ref[...].astype(f32)
    ).astype(bf16)
    write_vectors(total[strip:], bias_ref, gain_ref)


def write_vectors(tail, bias_ref, gain_ref):
    bias_ref[...] = tail[0:1] + tail[1:2]
    hid = tail.shape[1]
    for k in range(gain_ref.shape[1] // hid):
        gain_ref[:, k * hid : (k + 1) * hid] = tail[2 + 2 * k : 3 + 2 * k] + tail[3 + 2 * k : 4 + 2 * k]


def place_kernel(count, *refs):
    mine, theirs = refs[:count], refs[count : 2 * count]
    src_ref, dst_ref, out_ref = refs[2 * count :]
    first = lax.axis_index("sub") == 0
    mesh = lax.axis_index("mesh")
    width, hid = src_ref.shape
    strip = width // count
    narrow = hid // count
    for k in range(count):
        a, b = mine[k][...], theirs[k][...]
        low = jnp.where(first, a, b).astype(f32)
        high = jnp.where(first, b, a).astype(f32)
        start = pl.multiple_of((mesh ^ k) * strip, strip)
        src_ref[pl.ds(start, strip), :] = low[:strip]
        dst_ref[pl.ds(start, strip), :] = high[:strip]
        start = pl.multiple_of((mesh ^ k) * narrow, narrow)
        out_ref[pl.ds(start, narrow), 0:hid] = low[strip:]
        out_ref[pl.ds(start, narrow), hid:] = high[strip:]


def sum_kernel(chunk, arrived_ref, out_ref, bias_ref, gain_ref):
    peers = arrived_ref.shape[0]
    total = arrived_ref[0].astype(f32)
    for peer in range(1, peers):
        total += arrived_ref[peer].astype(f32)
    low = total[:chunk].astype(bf16)
    for peer in range(peers):
        out_ref[peer] = low
    tail = total[chunk:]
    write_vectors(tail, bias_ref, gain_ref)


def unpack_kernel(arrived_ref, src_ref, dst_ref, out_ref):
    hid = src_ref.shape[1]
    rows = src_ref.shape[0]
    src_ref[...] = arrived_ref[0:rows, :].astype(f32)
    dst_ref[...] = arrived_ref[rows : 2 * rows, :].astype(f32)
    at = 2 * rows
    for k in range(out_ref.shape[1] // hid):
        out_ref[:, k * hid : (k + 1) * hid] = arrived_ref[at : at + out_ref.shape[0], :].astype(f32)
        at += out_ref.shape[0]


def node_part(send_ref, local_ref, target_ref, w_src_ref, w_dst_ref, returned, out_ref):
    rows = local_ref.shape[0]
    halo = send_ref.shape[2]
    picks = [one_hot(iota((rows, halo), 0) == send_ref[0, d : d + 1, :]) for d in range(4)]
    total = local_ref[...] + dot(jnp.concatenate(picks, axis=1), jnp.concatenate(returned, axis=0))
    out_ref[...] = (
        dot(total.astype(bf16), w_src_ref[...], NT) + dot(target_ref[...], w_dst_ref[...], NT)
    ).astype(bf16)


def node_kernel(send_ref, local_ref, target_ref, w_src_ref, w_dst_ref, *rest):
    *back_refs, out_ref = rest
    returned = [r[...] for r in back_refs]
    node_part(send_ref, local_ref, target_ref, w_src_ref, w_dst_ref, returned, out_ref)


def paired_node_kernel(
    send_ref, local_ref, target_ref, w_src_ref, w_dst_ref, three_ref, one_ref, pair_ref, out_ref
):
    even = lax.axis_index("mesh") % 2 == 0
    halo = send_ref.shape[2]
    hid = local_ref.shape[1]
    at = one_ref.shape[0] - halo // 2
    one, three = [
        jnp.concatenate([r[at:, :hid], r[at:, hid:]], axis=0) for r in (one_ref, three_ref)
    ]
    returned = [
        jnp.where(even, one, three), jnp.where(even, three, one), pair_ref[pair_ref.shape[0] - 2 * halo :, :]
    ]
    node_part(send_ref, local_ref, target_ref, w_src_ref, w_dst_ref, returned, out_ref)


def finish_kernel(cot_ref, own_ref, other_ref, out_ref):
    out_ref[...] = cot_ref[...].astype(f32) + (
        own_ref[...].astype(f32) + other_ref[...].astype(f32)
    )


VMEM = pl.BlockSpec(memory_space=pltpu.VMEM)
SMEM = pl.BlockSpec(memory_space=pltpu.SMEM)
HBM = pl.BlockSpec(memory_space=pltpu.HBM)


def shape(dims, dtype):
    return jax.ShapeDtypeStruct(dims, dtype)


def call(kernel, outs, *args, specs=None, flops=10**8, scratch=()):
    return pl.pallas_call(
        kernel,
        out_shape=outs,
        in_specs=specs or [VMEM] * len(args),
        out_specs=jax.tree.map(lambda _: VMEM, outs),
        scratch_shapes=scratch,
        compiler_params=pltpu.CompilerParams(vmem_limit_bytes=VMEM_LIMIT),
        cost_estimate=pl.CostEstimate(flops=flops, bytes_accessed=10**6, transcendentals=0),
    )(*args)


def shifted(x, axis, by):
    count = lax.axis_size(axis)
    return lax.ppermute(x, axis, [(i, (i + by) % count) for i in range(count)])


def across(x, axis, k):
    count = lax.axis_size(axis)
    return lax.ppermute(x, axis, [(i, i ^ k) for i in range(count)])


def paired_sums(messages, lines, strip, narrow, width, hid):
    send, keep, *outs = messages
    order = range(lines - 1, 0, -1)
    out_terms = {k: across(outs[k], "mesh", k) for k in order}
    arrived = across(send, "sub", 1)
    *line, out_send, out_keep = call(
        functools.partial(turn_kernel, lines),
        [shape((strip + TAIL, hid), bf16)] * lines + [shape((narrow, hid), bf16)] * 2,
        *[out_terms[k] for k in order], outs[0], arrived, keep,
        scratch=[pltpu.VMEM((width, hid), bf16)],
    )
    line_terms = {k: across(line[k], "mesh", k) for k in order}
    own, bias_grad, gain_grad = call(
        functools.partial(own_kernel, lines),
        [shape((strip + narrow, hid), bf16), shape((1, hid), f32), shape((1, width), f32)],
        *[line_terms[k] for k in order], line[0], out_keep, across(out_send, "sub", 1),
    )
    mine = {k: across(own, "mesh", k) for k in order}
    mine[0] = own
    theirs = {k: across(mine[k], "sub", 1) for k in mine}
    grads = call(
        functools.partial(place_kernel, lines),
        [shape((width, hid), f32), shape((width, hid), f32), shape((hid, width), f32)],
        *[mine[k] for k in range(lines)], *[theirs[k] for k in range(lines)],
    )
    return (*grads, bias_grad, gain_grad), (out_terms[3], out_terms[1], arrived)


def shards(
    node_state,
    send_rows,
    edge_src,
    edge_dst,
    block_count,
    w_src,
    w_dst,
    hidden_bias,
    w_out,
    norm_gain,
    cotangent,
):
    rows, width = node_state.shape
    hid = w_src.shape[1]
    halo = send_rows.shape[2]
    edges = edge_src.shape[0]
    peers = lax.axis_size("mesh") * lax.axis_size("sub")
    merged = lax.axis_size("sub") == 2
    total_rows = 2 * width + (width // hid) * hid
    chunk = -(-total_rows // (peers * 16)) * 16

    piece = [halo, halo, 2 * halo] if merged else [halo] * 4
    routes = [("mesh", 1), ("mesh", -1), ("sub", 1)] + ([] if merged else [("sub", -1)])
    n_halo = len(piece)

    node, send, *outgoing = call(
        send_kernel,
        [shape((rows, width), bf16), shape(send_rows.shape, jnp.int32)]
        + [shape((n, width), bf16) for n in piece],
        node_state, send_rows,
        specs=[HBM, HBM],
        scratch=[pltpu.SemaphoreType.DMA((2,))],
    )
    arrived = [shifted(x, axis, by) for x, (axis, by) in zip(outgoing, routes)]

    pre, pick, collect, spread, scatter, w_src, w_dst, w_out, gain, cot = call(
        local_kernel,
        [
            shape((edges, hid), f32),
            shape((edges, 4 * halo), bf16),
            shape((rows, edges), bf16),
            shape((edges, rows), bf16),
            shape((rows + 4 * halo, edges), bf16),
            shape(w_src.shape, bf16),
            shape(w_dst.shape, bf16),
            shape(w_out.shape, bf16),
            shape((1, width), f32),
            shape((rows, width), bf16),
        ],
        block_count, node, edge_src.reshape(1, edges), edge_dst.reshape(1, edges),
        hidden_bias.reshape(1, hid), w_src, w_dst, w_out, norm_gain.reshape(1, width), cotangent,
        specs=[SMEM, VMEM] + [HBM] * 8,
        scratch=[
            pltpu.VMEM((1, edges), jnp.int32),
            pltpu.VMEM((1, edges), jnp.int32),
            pltpu.VMEM((1, hid), f32),
            pltpu.SemaphoreType.DMA((8,)),
        ],
    )

    factor, hidden, partial = call(
        forward_kernel,
        [shape((edges, hid), f32), shape((rows, hid), bf16), shape((rows, width), bf16)],
        pre, pick, collect, w_src, w_out, *arrived,
    )
    other = shifted(partial, "lat", 1)

    lines = lax.axis_size("mesh")
    paired = merged and lines == 4
    if paired:
        strip = width // lines
        narrow = hid // lines
        message_shapes = [shape((width + TAIL + 2 * halo, hid), bf16), shape((width + TAIL, hid), bf16)]
        message_shapes += [shape((narrow + k % 2 * (halo // 2), width), bf16) for k in range(lines)]
    else:
        message_shapes = [shape((peers, chunk + TAIL, hid), bf16)]
        message_shapes += [shape((n, hid), bf16) for n in piece]
    updated, local, target, *messages = call(
        functools.partial(backward_kernel, (peers, chunk, n_halo, paired)),
        [shape((rows, width), bf16), shape((rows, hid), f32), shape((rows, hid), bf16)]
        + message_shapes,
        node, collect, spread, scatter, w_out, gain, cot, factor, hidden, partial, other, *arrived,
        scratch=[pltpu.VMEM((hid, width), bf16), pltpu.VMEM((2 * halo, hid), bf16)],
    )

    if paired:
        (src_grad, dst_grad, out_grad, bias_grad, gain_grad), returned = paired_sums(
            messages, lines, strip, narrow, width, hid
        )
    else:
        returned = [shifted(x, axis, -by) for x, (axis, by) in zip(messages[1:], routes)]
        exchanged = lax.all_to_all(messages[0], ("mesh", "sub"), 0, 0)
        reduced, bias_grad, gain_grad = call(
            functools.partial(sum_kernel, chunk),
            [shape((peers, chunk, hid), bf16), shape((1, hid), f32), shape((1, width), f32)],
            exchanged,
        )
        gathered = lax.all_to_all(reduced, ("mesh", "sub"), 0, 0)
        src_grad, dst_grad, out_grad = call(
            unpack_kernel,
            [shape((width, hid), f32), shape((width, hid), f32), shape((hid, width), f32)],
            gathered.reshape(peers * chunk, hid),
        )
    node_part = call(
        paired_node_kernel if paired else node_kernel,
        shape((rows, width), bf16),
        send, local, target, w_src, w_dst, *returned,
    )
    node_grad = call(
        finish_kernel, shape((rows, width), f32), cot, node_part, shifted(node_part, "lat", 1)
    )
    return (
        updated, node_grad, src_grad, dst_grad, out_grad,
        bias_grad.reshape(hid), gain_grad.reshape(width),
    )


def solution(mesh):
    nodes = P(("parts", "mesh", "sub"), None)
    slots = P(("parts", "mesh", "sub"))
    in_specs = (
        nodes,
        P(("parts", "mesh", "sub"), None, None),
        slots,
        slots,
        slots,
        P(None, "lat"),
        P(None, "lat"),
        P("lat"),
        P("lat", None),
        P(),
        nodes,
    )
    out_specs = (
        nodes,
        nodes,
        P("parts", "lat"),
        P("parts", "lat"),
        P(("parts", "lat"), None),
        P(("parts", "lat")),
        P("parts"),
    )
    return jax.shard_map(shards, mesh=mesh, in_specs=in_specs, out_specs=out_specs, check_vma=False)
```

time: 68.6 us -> 58 us (0.85)
  waiting for transfers between devices: 21.9 us -> 15.8 us
  starting transfers between devices: 32.7 us -> 27.6 us
    ppermute x8 -> x5, starting transfers between devices: 13.2 us -> 6.97 us  [shifted(): return lax.ppermute(x, axis, [(i, (i + by) % count) for i in range(count)])]
    ppermute x8 -> x5, waiting for transfers between devices: 6.96 us -> 1.35 us  [shifted(): return lax.ppermute(x, axis, [(i, (i + by) % count) for i in range(count)])]
    ppermute x15, starting transfers between devices: 19.5 us -> 20.6 us  [across(): return lax.ppermute(x, axis, [(i, i ^ k) for i in range(count)])]
    pallas_call x8 -> x9, Pallas kernels: 8.06 us -> 8.51 us  [call(): pl.pallas_call(kernel, out_shape=outs, in_specs=specs or [VMEM] * len(arg...]
    unnamed x28 -> x22, local copies, waits for them, and re-layouts: 4.91 us -> 5.13 us
  transfers between devices with their start and end apart: 23 -> 20, of which waited for: 12 -> 9; matrix products, arithmetic and copies ran while one was open for 0% -> 0% of each run, Pallas kernels for 2% -> 6%
where the time goes in v3:
time: 58 us; the launch traced here: 57.8 us
  starting transfers between devices  27.6 us (48%)
  waiting for transfers between devices  15.8 us (27%)
  Pallas kernels  8.51 us (15%)
  local copies, waits for them, and re-layouts  5.13 us (9%)
  between operations  0.77 us (1%)
    ppermute x15, starting transfers between devices, across(): return lax.ppermute(x, axis, [(i, i ^ k) for i in range(count)])  20.6 us
    ppermute x15, waiting for transfers between devices, across(): return lax.ppermute(x, axis, [(i, i ^ k) for i in range(count)])  14.5 us
    pallas_call x9, Pallas kernels, call(): pl.pallas_call(kernel, out_shape=outs, in_specs=specs or [VMEM] * len(arg...  8.51 us
    ppermute x5, starting transfers between devices, shifted(): return lax.ppermute(x, axis, [(i, (i + by) % count) for i in range(count)])  6.97 us
    unnamed x22, local copies, waits for them, and re-layouts  5.13 us
    ppermute x5, waiting for transfers between devices, shifted(): return lax.ppermute(x, axis, [(i, (i + by) % count) for i in range(count)])  1.35 us
  transfers between devices with their start and end apart: 20, of which 9 were waited for; matrix products, arithmetic and copies ran while one was open for 0% of the time, Pallas kernels for 6%

profile of v3, /device:TPU:0, one launch (start us, length us, event | category | flops | bytes accessed | tf_op | source)
XLA Modules:
  0.0 57.8 jit_solution(3307109302048825485)
XLA Ops:
  0.6 0.0 copy-start
  0.6 0.0 copy-start.9
  0.7 0.9 %copy-done.9 = bf16[128,512]{1,0:T(8,128)(2,1)S(1)} copy-done((bf16[128,512]{1,0:T(8,128)(2,1)S(1)}, bf16[128,512]{1,0:T(8,128)(2,1)}, u32[]{:S(2)}) %copy-start.9) | copy-done | bytes 131096
  1.6 0.0 copy-start.10
  1.6 0.7 %copy-done.10 = s32[1,4,32]{2,1,0:T(4,128)S(1)} copy-done((s32[1,4,32]{2,1,0:T(4,128)S(1)}, s32[1,4,32]{2,1,0:T(4,128)}, u32[]{:S(2)}) %copy-start.10) | copy-done | bytes 536
  2.3 0.4 shard_map.162
  2.7 3.0 %collective-permute-start.2 = (bf16[64,512]{1,0:T(8,128)(2,1)S(1)}, bf16[64,512]{1,0:T(8,128)(2,1)S(1)}, u32[]{:S(2)}, u32[]{:S(2)}) collective-permute-start(bf16[64,512]{1,0:T(8,128)(2,1)S(1)} %get-tuple-element.58), channel_id=1, source_target_pairs={{0,2},{2,0},{1,3},{3,1},{4,6},{6,4},{5,7},{7,5},{8,10},{10,8},{9,1... | collective-permute-start | bytes 196616 | tf_op jit(solution)/shard_map/ppermute | solution.py:414
  5.7 1.6 %collective-permute-start = (bf16[32,512]{1,0:T(8,128)(2,1)S(1)}, bf16[32,512]{1,0:T(8,128)(2,1)S(1)}, u32[]{:S(2)}, u32[]{:S(2)}) collective-permute-start(bf16[32,512]{1,0:T(8,128)(2,1)S(1)} %get-tuple-element.56), channel_id=1, source_target_pairs={{0,4},{4,8},{8,12},{12,0},{1,5},{5,9},{9,13},{13,1},{2,6},{6,10},{... | collective-permute-start | bytes 98312 | tf_op jit(solution)/shard_map/ppermute | solution.py:414
  7.3 2.2 %collective-permute-start.1 = (bf16[32,512]{1,0:T(8,128)(2,1)S(1)}, bf16[32,512]{1,0:T(8,128)(2,1)S(1)}, u32[]{:S(2)}, u32[]{:S(2)}) collective-permute-start(bf16[32,512]{1,0:T(8,128)(2,1)S(1)} %get-tuple-element.57), channel_id=1, source_target_pairs={{0,12},{4,0},{8,4},{12,8},{1,13},{5,1},{9,5},{13,9},{2,14},{6,2},{... | collective-permute-start | bytes 98312 | tf_op jit(solution)/shard_map/ppermute | solution.py:414
  9.5 0.0 copy-start.8
  9.5 0.0 copy-done
  9.5 0.6 %copy-done.6 = f32[512]{0:T(512)S(1)} copy-done((f32[512]{0:T(512)S(1)}, f32[512]{0:T(512)}, u32[]{:S(2)}) %copy-start.6) | copy-done | bytes 2072
  10.2 0.0 copy-done.5
  10.2 0.0 copy-done.4
  10.2 0.0 copy-done.7
  10.2 0.0 copy-done.8
  10.2 0.9 %copy-done.1 = bf16[512,256]{1,0:T(8,128)(2,1)S(1)} copy-done((bf16[512,256]{1,0:T(8,128)(2,1)S(1)}, bf16[512,256]{1,0:T(8,128)(2,1)}, u32[]{:S(2)}) %copy-start.1) | copy-done | bytes 262168
  11.2 0.9 %copy-done.2 = bf16[256,512]{1,0:T(8,128)(2,1)S(1)} copy-done((bf16[256,512]{1,0:T(8,128)(2,1)S(1)}, bf16[256,512]{1,0:T(8,128)(2,1)}, u32[]{:S(2)}) %copy-start.2) | copy-done | bytes 262168
  12.1 0.9 %copy-done.3 = bf16[128,512]{1,0:T(8,128)(2,1)S(1)} copy-done((bf16[128,512]{1,0:T(8,128)(2,1)S(1)}, bf16[128,512]{1,0:T(8,128)(2,1)}, u32[]{:S(2)}) %copy-start.3) | copy-done | bytes 131096
  13.0 2.1 %shard_map.163 = (f32[512,256]{1,0:T(8,128)S(1)}, bf16[512,128]{1,0:T(8,128)(2,1)S(1)}, bf16[128,512]{1,0:T(8,128)(2,1)S(1)}, bf16[512,128]{1,0:T(8,128)(2,1)S(1...) custom-call(s32[4]{0:T(128)S(1)} %copy-done.8, ...), custom_call_target="tpu_custom_call" | custom-call | flops 100000000 | bytes 1000000 | tf_op jit(solution)/shard_map/pallas_call | solution.py:401
  15.1 0.0 collective-permute-done.rest_0_
  15.1 0.0 collective-permute-done.1.rest_1_
  15.1 0.0 collective-permute-done.2.rest_2_
  15.1 0.9 %shard_map.164 = (f32[512,256]{1,0:T(8,128)S(1)}, bf16[128,256]{1,0:T(8,128)(2,1)S(1)}, bf16[128,512]{1,0:T(8,128)(2,1)S(1)}) custom-call(f32[512,256]{1,0:T(8,128)S(1)} %get-tuple-element.53.pre_ref, bf16[512,128]{1,0:T(8,128)(2,1)S(1)} %get-tuple-element.54.pick_ref, bf16[128,512]{1,0:T(8,128)(2,1)S(1)} %get-tuple-element.47.collect_ref, ...), custom_call_target="tpu_custom_call" | custom-call | flops 100000000 | bytes 1000000 | tf_op jit(solution)/shard_map/pallas_call | solution.py:401
  16.0 0.1 collective-permute-start.3
  16.1 1.3 %collective-permute-done.3.other_ref = bf16[128,512]{1,0:T(8,128)(2,1)S(1)} collective-permute-done((bf16[128,512]{1,0:T(8,128)(2,1)S(1)}, bf16[128,512]{1,0:T(8,128)(2,1)S(1)}, u32[]{:S(2)}, u32[]{:S(2)}) %collective-permute-start.3) | collective-permute-done | bytes 131104 | tf_op jit(solution)/shard_map/ppermute | solution.py:414
  17.4 2.0 %shard_map.165 = (bf16[128,512]{1,0:T(8,128)(2,1)}, f32[128,256]{1,0:T(8,128)S(1)}, bf16[128,256]{1,0:T(8,128)(2,1)S(1)}, bf16[592,256]{1,0:T(8,128)(2,1)S(1)}, ...) custom-call(bf16[128,512]{1,0:T(8,128)(2,1)S(1)} %get-tuple-element., ...), custom_call_target="tpu_custom_call" | custom-call | flops 100000000 | bytes 1000000 | tf_op jit(solution)/shard_map/pallas_call | solution.py:401
  19.5 0.3 collective-permute-start.6
  19.8 2.0 %collective-permute-start.4 = (bf16[80,512]{1,0:T(8,128)(2,1)S(1)}, bf16[80,512]{1,0:T(8,128)(2,1)S(1)}, u32[]{:S(2)}, u32[]{:S(2)}) collective-permute-start(bf16[80,512]{1,0:T(8,128)(2,1)S(1)} %get-tuple-element.67), channel_id=1, source_target_pairs={{0,12},{4,8},{8,4},{12,0},{1,13},{5,9},{9,5},{13,1},{2,14},{6,10},... | collective-permute-start | bytes 245768 | tf_op jit(solution)/shard_map/ppermute | solution.py:419
  21.8 0.0 collective-permute-start.5
  21.8 2.4 %collective-permute-start.8 = (bf16[64,512]{1,0:T(8,128)(2,1)S(1)}, bf16[64,512]{1,0:T(8,128)(2,1)S(1)}, u32[]{:S(2)}, u32[]{:S(2)}) collective-permute-start(bf16[64,512]{1,0:T(8,128)(2,1)S(1)} %get-tuple-element.70), channel_id=1, source_target_pairs={{0,8},{4,12},{8,0},{12,4},{1,9},{5,13},{9,1},{13,5},{2,10},{6,14},... | collective-permute-start | bytes 196616 | tf_op jit(solution)/shard_map/ppermute | solution.py:419
  24.2 3.8 %collective-permute-done.8.refs_1_ = bf16[64,512]{1,0:T(8,128)(2,1)S(1)} collective-permute-done((bf16[64,512]{1,0:T(8,128)(2,1)S(1)}, bf16[64,512]{1,0:T(8,128)(2,1)S(1)}, u32[]{:S(2)}, u32[]{:S(2)}) %collective-permute-start.8) | collective-permute-done | bytes 65568 | tf_op jit(solution)/shard_map/ppermute | solution.py:419
  28.0 0.0 collective-permute-done.4.three_ref.refs_0_
  28.0 0.9 %collective-permute-done.5.one_ref.refs_2_ = bf16[80,512]{1,0:T(8,128)(2,1)S(1)} collective-permute-done((bf16[80,512]{1,0:T(8,128)(2,1)S(1)}, bf16[80,512]{1,0:T(8,128)(2,1)S(1)}, u32[]{:S(2)}, u32[]{:S(2)}) %collective-permute-start.5) | collective-permute-done | bytes 81952 | tf_op jit(solution)/shard_map/ppermute | solution.py:419
  28.9 0.0 collective-permute-done.6.pair_ref.refs_4_
  28.9 0.2 shard_map.168
  29.1 1.9 %collective-permute-start.9 = (bf16[144,256]{1,0:T(8,128)(2,1)S(1)}, bf16[144,256]{1,0:T(8,128)(2,1)S(1)}, u32[]{:S(2)}, u32[]{:S(2)}) collective-permute-start(bf16[144,256]{1,0:T(8,128)(2,1)S(1)} %get-tuple-element.73), channel_id=1, source_target_pairs={{0,12},{4,8},{8,4},{12,0},{1,13},{5,9},{9,5},{13,1},{2,14},{6,10},... | collective-permute-start | bytes 221192 | tf_op jit(solution)/shard_map/ppermute | solution.py:419
  31.0 0.3 collective-permute-start.10
  31.3 2.3 %collective-permute-start.11 = (bf16[144,256]{1,0:T(8,128)(2,1)S(1)}, bf16[144,256]{1,0:T(8,128)(2,1)S(1)}, u32[]{:S(2)}, u32[]{:S(2)}) collective-permute-start(bf16[144,256]{1,0:T(8,128)(2,1)S(1)} %get-tuple-element.75), channel_id=1, source_target_pairs={{0,4},{4,0},{8,12},{12,8},{1,5},{5,1},{9,13},{13,9},{2,6},{6,2},{1... | collective-permute-start | bytes 221192 | tf_op jit(solution)/shard_map/ppermute | solution.py:419
  33.6 1.5 %collective-permute-start.12 = (bf16[64,256]{1,0:T(8,128)(2,1)S(1)}, bf16[64,256]{1,0:T(8,128)(2,1)S(1)}, u32[]{:S(2)}, u32[]{:S(2)}) collective-permute-start(bf16[64,256]{1,0:T(8,128)(2,1)S(1)} %get-tuple-element.78), channel_id=1, source_target_pairs={{0,2},{2,0},{1,3},{3,1},{4,6},{6,4},{5,7},{7,5},{8,10},{10,8},{9,1... | collective-permute-start | bytes 98312 | tf_op jit(solution)/shard_map/ppermute | solution.py:419
  35.0 2.4 %collective-permute-done.12.refs_5_ = bf16[64,256]{1,0:T(8,128)(2,1)S(1)} collective-permute-done((bf16[64,256]{1,0:T(8,128)(2,1)S(1)}, bf16[64,256]{1,0:T(8,128)(2,1)S(1)}, u32[]{:S(2)}, u32[]{:S(2)}) %collective-permute-start.12) | collective-permute-done | bytes 32800 | tf_op jit(solution)/shard_map/ppermute | solution.py:419
  37.5 0.0 collective-permute-done.9.refs_0_
  37.5 0.9 %collective-permute-done.10.refs_1_ = bf16[144,256]{1,0:T(8,128)(2,1)S(1)} collective-permute-done((bf16[144,256]{1,0:T(8,128)(2,1)S(1)}, bf16[144,256]{1,0:T(8,128)(2,1)S(1)}, u32[]{:S(2)}, u32[]{:S(2)}) %collective-permute-start.10) | collective-permute-done | bytes 73760 | tf_op jit(solution)/shard_map/ppermute | solution.py:419
  38.3 0.0 collective-permute-done.11.refs_2_
  38.3 0.6 %shard_map.169 = (bf16[192,256]{1,0:T(8,128)(2,1)S(1)}, f32[1,256]{1,0:T(1,128)}, f32[1,512]{1,0:T(1,128)}) custom-call(bf16[144,256]{1,0:T(8,128)(2,1)S(1)} %collective-permute-done.9.refs_0_, bf16[144,256]{1,0:T(8,128)(2,1)S(1)} %collective-permute-done.10.refs_1_, bf16[144,256]{1,0:T(8,128)(2,1)S(1)} %collective-permute-done.11.refs_2_, ...), custom_call_target="tpu_custom_call" | custom-call | flops 100000000 | bytes 1000000 | tf_op jit(solution)/shard_map/pallas_call | solution.py:401
  38.9 2.0 %collective-permute-start.15 = (bf16[192,256]{1,0:T(8,128)(2,1)S(1)}, bf16[192,256]{1,0:T(8,128)(2,1)S(1)}, u32[]{:S(2)}, u32[]{:S(2)}) collective-permute-start(bf16[192,256]{1,0:T(8,128)(2,1)S(1)} %get-tuple-element.79.refs_0_), channel_id=1, source_target_pairs={{0,12},{4,8},{8,4},{12,0},{1,13},{5,9},{9,5},{13,1},{2,14},{6,10},... | collective-permute-start | bytes 294920 | tf_op jit(solution)/shard_map/ppermute | solution.py:419
  40.9 0.0 collective-permute-start.14
  40.9 2.4 %collective-permute-start.13 = (bf16[192,256]{1,0:T(8,128)(2,1)S(1)}, bf16[192,256]{1,0:T(8,128)(2,1)S(1)}, u32[]{:S(2)}, u32[]{:S(2)}) collective-permute-start(bf16[192,256]{1,0:T(8,128)(2,1)S(1)} %get-tuple-element.79.refs_0_), channel_id=1, source_target_pairs={{0,4},{4,0},{8,12},{12,8},{1,5},{5,1},{9,13},{13,9},{2,6},{6,2},{1... | collective-permute-start | bytes 294920 | tf_op jit(solution)/shard_map/ppermute | solution.py:419
  43.3 0.4 shard_map.166.own_ref
  43.7 0.1 collective-permute-start.7
  43.8 1.8 %collective-permute-start.16 = (bf16[192,256]{1,0:T(8,128)(2,1)S(1)}, bf16[192,256]{1,0:T(8,128)(2,1)S(1)}, u32[]{:S(2)}, u32[]{:S(2)}) collective-permute-start(bf16[192,256]{1,0:T(8,128)(2,1)S(1)} %get-tuple-element.79.refs_0_), channel_id=1, source_target_pairs={{0,2},{2,0},{1,3},{3,1},{4,6},{6,4},{5,7},{7,5},{8,10},{10,8},{9,1... | collective-permute-start | bytes 294920 | tf_op jit(solution)/shard_map/ppermute | solution.py:419
  45.6 0.9 %collective-permute-done.15.refs_3_ = bf16[192,256]{1,0:T(8,128)(2,1)S(1)} collective-permute-done((bf16[192,256]{1,0:T(8,128)(2,1)S(1)}, bf16[192,256]{1,0:T(8,128)(2,1)S(1)}, u32[]{:S(2)}, u32[]{:S(2)}) %collective-permute-start.15) | collective-permute-done | bytes 98336 | tf_op jit(solution)/shard_map/ppermute | solution.py:419
  46.5 1.8 %collective-permute-start.19 = (bf16[192,256]{1,0:T(8,128)(2,1)S(1)}, bf16[192,256]{1,0:T(8,128)(2,1)S(1)}, u32[]{:S(2)}, u32[]{:S(2)}) collective-permute-start(bf16[192,256]{1,0:T(8,128)(2,1)S(1)} %collective-permute-done.15.refs_3_), channel_id=1, source_target_pairs={{0,2},{2,0},{1,3},{3,1},{4,6},{6,4},{5,7},{7,5},{8,10},{10,8},{9,1... | collective-permute-start | bytes 294920 | tf_op jit(solution)/shard_map/ppermute | solution.py:419
  48.2 1.5 %collective-permute-done.14.refs_2_ = bf16[192,256]{1,0:T(8,128)(2,1)S(1)} collective-permute-done((bf16[192,256]{1,0:T(8,128)(2,1)S(1)}, bf16[192,256]{1,0:T(8,128)(2,1)S(1)}, u32[]{:S(2)}, u32[]{:S(2)}) %collective-permute-start.14) | collective-permute-done | bytes 98336 | tf_op jit(solution)/shard_map/ppermute | solution.py:419
  49.7 1.3 %collective-permute-start.18 = (bf16[192,256]{1,0:T(8,128)(2,1)S(1)}, bf16[192,256]{1,0:T(8,128)(2,1)S(1)}, u32[]{:S(2)}, u32[]{:S(2)}) collective-permute-start(bf16[192,256]{1,0:T(8,128)(2,1)S(1)} %collective-permute-done.14.refs_2_), channel_id=1, source_target_pairs={{0,2},{2,0},{1,3},{3,1},{4,6},{6,4},{5,7},{7,5},{8,10},{10,8},{9,1... | collective-permute-start | bytes 294920 | tf_op jit(solution)/shard_map/ppermute | solution.py:419
  51.0 0.0 collective-permute-done.13.refs_1_
  51.0 0.7 %collective-permute-start.17 = (bf16[192,256]{1,0:T(8,128)(2,1)S(1)}, bf16[192,256]{1,0:T(8,128)(2,1)S(1)}, u32[]{:S(2)}, u32[]{:S(2)}) collective-permute-start(bf16[192,256]{1,0:T(8,128)(2,1)S(1)} %collective-permute-done.13.refs_1_), channel_id=1, source_target_pairs={{0,2},{2,0},{1,3},{3,1},{4,6},{6,4},{5,7},{7,5},{8,10},{10,8},{9,1... | collective-permute-start | bytes 294920 | tf_op jit(solution)/shard_map/ppermute | solution.py:419
  51.8 0.0 collective-permute-done.7.other_ref
  51.8 0.8 %shard_map.167 = f32[128,512]{1,0:T(8,128)} custom-call(bf16[128,512]{1,0:T(8,128)(2,1)S(1)} %get-tuple-element.52.cot_ref, bf16[128,512]{1,0:T(8,128)(2,1)S(1)} %shard_map.166.own_ref, bf16[128,512]{1,0:T(8,128)(2,1)S(1)} %collective-permute-done.7.other_ref), custom_call_target="tpu_custom_call" | custom-call | flops 100000000 | bytes 1000000 | tf_op jit(solution)/shard_map/pallas_call | solution.py:401
  52.5 0.0 collective-permute-done.16.refs_4_
  52.5 0.0 collective-permute-done.19.refs_7_
  52.5 2.9 %collective-permute-done.18.refs_6_ = bf16[192,256]{1,0:T(8,128)(2,1)S(1)} collective-permute-done((bf16[192,256]{1,0:T(8,128)(2,1)S(1)}, bf16[192,256]{1,0:T(8,128)(2,1)S(1)}, u32[]{:S(2)}, u32[]{:S(2)}) %collective-permute-start.18) | collective-permute-done | bytes 98336 | tf_op jit(solution)/shard_map/ppermute | solution.py:419
  55.4 1.2 %collective-permute-done.17.refs_5_ = bf16[192,256]{1,0:T(8,128)(2,1)S(1)} collective-permute-done((bf16[192,256]{1,0:T(8,128)(2,1)S(1)}, bf16[192,256]{1,0:T(8,128)(2,1)S(1)}, u32[]{:S(2)}, u32[]{:S(2)}) %collective-permute-start.17) | collective-permute-done | bytes 98336 | tf_op jit(solution)/shard_map/ppermute | solution.py:419
  56.5 1.2 %shard_map.170 = (f32[512,256]{1,0:T(8,128)}, f32[512,256]{1,0:T(8,128)}, f32[256,512]{1,0:T(8,128)}) custom-call(bf16[192,256]{1,0:T(8,128)(2,1)S(1)} %get-tuple-element.79.refs_0_, bf16[192,256]{1,0:T(8,128)(2,1)S(1)} %collective-permute-done.13.refs_1_, bf16[192,256]{1,0:T(8,128)(2,1)S(1)} %collective-permute-done.14.refs_2_, ...), custom_call_target="tpu_custom_call" | custom-call | flops 100000000 | bytes 1000000 | tf_op jit(solution)/shard_map/pallas_call | solution.py:401
  (7 shorter events, 0.0 us)
Async XLA Ops:
  0.6 8.9 %copy-start = (bf16[512,256]{1,0:T(8,128)(2,1)S(1)}, bf16[512,256]{1,0:T(8,128)(2,1)}, u32[]{:S(2)}) copy-start(bf16[512,256]{1,0:T(8,128)(2,1)} %w_src_hbm.1) | copy-start | bytes 786436
  0.6 0.9 %copy-start.9 = (bf16[128,512]{1,0:T(8,128)(2,1)S(1)}, bf16[128,512]{1,0:T(8,128)(2,1)}, u32[]{:S(2)}) copy-start(bf16[128,512]{1,0:T(8,128)(2,1)} %node_hbm.1) | copy-start | bytes 393220
  1.6 0.7 %copy-start.10 = (s32[1,4,32]{2,1,0:T(4,128)S(1)}, s32[1,4,32]{2,1,0:T(4,128)}, u32[]{:S(2)}) copy-start(s32[1,4,32]{2,1,0:T(4,128)} %send_hbm.1) | copy-start | bytes 1540
  2.7 12.4 %collective-permute-start.2 = (bf16[64,512]{1,0:T(8,128)(2,1)S(1)}, bf16[64,512]{1,0:T(8,128)(2,1)S(1)}, u32[]{:S(2)}, u32[]{:S(2)}) collective-permute-start(bf16[64,512]{1,0:T(8,128)(2,1)S(1)} %get-tuple-element.58), channel_id=1, source_target_pairs={{0,2},{2,0},{1,3},{3,1},{4,6},{6,4},{5,7},{7,5},{8,10},{10,8},{9,1... | collective-permute-start | bytes 196616 | tf_op jit(solution)/shard_map/ppermute | solution.py:414
  5.7 9.4 %collective-permute-start = (bf16[32,512]{1,0:T(8,128)(2,1)S(1)}, bf16[32,512]{1,0:T(8,128)(2,1)S(1)}, u32[]{:S(2)}, u32[]{:S(2)}) collective-permute-start(bf16[32,512]{1,0:T(8,128)(2,1)S(1)} %get-tuple-element.56), channel_id=1, source_target_pairs={{0,4},{4,8},{8,12},{12,0},{1,5},{5,9},{9,13},{13,1},{2,6},{6,10},{... | collective-permute-start | bytes 98312 | tf_op jit(solution)/shard_map/ppermute | solution.py:414
  7.3 7.9 %collective-permute-start.1 = (bf16[32,512]{1,0:T(8,128)(2,1)S(1)}, bf16[32,512]{1,0:T(8,128)(2,1)S(1)}, u32[]{:S(2)}, u32[]{:S(2)}) collective-permute-start(bf16[32,512]{1,0:T(8,128)(2,1)S(1)} %get-tuple-element.57), channel_id=1, source_target_pairs={{0,12},{4,0},{8,4},{12,8},{1,13},{5,1},{9,5},{13,9},{2,14},{6,2},{... | collective-permute-start | bytes 98312 | tf_op jit(solution)/shard_map/ppermute | solution.py:414
  9.5 0.7 %copy-start.6 = (f32[512]{0:T(512)S(1)}, f32[512]{0:T(512)}, u32[]{:S(2)}) copy-start(f32[512]{0:T(512)} %param.20) | copy-start | bytes 6148
  9.5 0.7 %copy-start.5 = (s32[512]{0:T(512)S(1)}, s32[512]{0:T(512)}, u32[]{:S(2)}) copy-start(s32[512]{0:T(512)} %param.14) | copy-start | bytes 6148
  9.5 0.7 %copy-start.4 = (s32[512]{0:T(512)S(1)}, s32[512]{0:T(512)}, u32[]{:S(2)}) copy-start(s32[512]{0:T(512)} %param.13) | copy-start | bytes 6148
  9.5 0.7 %copy-start.7 = (f32[256]{0:T(256)S(1)}, f32[256]{0:T(256)}, u32[]{:S(2)}) copy-start(f32[256]{0:T(256)} %param.18) | copy-start | bytes 3076
  9.5 0.7 %copy-start.8 = (s32[4]{0:T(128)S(1)}, s32[4]{0:T(128)}, u32[]{:S(2)}) copy-start(s32[4]{0:T(128)} %count_ref.1) | copy-start | bytes 52
  10.2 1.0 %copy-start.1 = (bf16[512,256]{1,0:T(8,128)(2,1)S(1)}, bf16[512,256]{1,0:T(8,128)(2,1)}, u32[]{:S(2)}) copy-start(bf16[512,256]{1,0:T(8,128)(2,1)} %w_dst_hbm.1) | copy-start | bytes 786436
  11.2 0.9 %copy-start.2 = (bf16[256,512]{1,0:T(8,128)(2,1)S(1)}, bf16[256,512]{1,0:T(8,128)(2,1)}, u32[]{:S(2)}) copy-start(bf16[256,512]{1,0:T(8,128)(2,1)} %w_out_hbm.1) | copy-start | bytes 786436
  12.1 0.9 %copy-start.3 = (bf16[128,512]{1,0:T(8,128)(2,1)S(1)}, bf16[128,512]{1,0:T(8,128)(2,1)}, u32[]{:S(2)}) copy-start(bf16[128,512]{1,0:T(8,128)(2,1)} %cot_hbm.1) | copy-start | bytes 393220
  16.0 1.4 %collective-permute-start.3 = (bf16[128,512]{1,0:T(8,128)(2,1)S(1)}, bf16[128,512]{1,0:T(8,128)(2,1)S(1)}, u32[]{:S(2)}, u32[]{:S(2)}) collective-permute-start(bf16[128,512]{1,0:T(8,128)(2,1)S(1)} %get-tuple-element.61.own_ref), channel_id=1, source_target_pairs={{0,1},{1,0},{2,3},{3,2},{4,5},{5,4},{6,7},{7,6},{8,9},{9,8},{10,11... | collective-permute-start | bytes 393224 | tf_op jit(solution)/shard_map/ppermute | solution.py:414
  19.5 9.4 %collective-permute-start.6 = (bf16[592,256]{1,0:T(8,128)(2,1)S(1)}, bf16[592,256]{1,0:T(8,128)(2,1)S(1)}, u32[]{:S(2)}, u32[]{:S(2)}) collective-permute-start(bf16[592,256]{1,0:T(8,128)(2,1)S(1)} %get-tuple-element.69), channel_id=1, source_target_pairs={{0,2},{2,0},{1,3},{3,1},{4,6},{6,4},{5,7},{7,5},{8,10},{10,8},{9,1... | collective-permute-start | bytes 909320 | tf_op jit(solution)/shard_map/ppermute | solution.py:419
  19.8 8.2 %collective-permute-start.4 = (bf16[80,512]{1,0:T(8,128)(2,1)S(1)}, bf16[80,512]{1,0:T(8,128)(2,1)S(1)}, u32[]{:S(2)}, u32[]{:S(2)}) collective-permute-start(bf16[80,512]{1,0:T(8,128)(2,1)S(1)} %get-tuple-element.67), channel_id=1, source_target_pairs={{0,12},{4,8},{8,4},{12,0},{1,13},{5,9},{9,5},{13,1},{2,14},{6,10},... | collective-permute-start | bytes 245768 | tf_op jit(solution)/shard_map/ppermute | solution.py:419
  21.8 7.1 %collective-permute-start.5 = (bf16[80,512]{1,0:T(8,128)(2,1)S(1)}, bf16[80,512]{1,0:T(8,128)(2,1)S(1)}, u32[]{:S(2)}, u32[]{:S(2)}) collective-permute-start(bf16[80,512]{1,0:T(8,128)(2,1)S(1)} %get-tuple-element.68), channel_id=1, source_target_pairs={{0,4},{4,0},{8,12},{12,8},{1,5},{5,1},{9,13},{13,9},{2,6},{6,2},{1... | collective-permute-start | bytes 245768 | tf_op jit(solution)/shard_map/ppermute | solution.py:419
  21.8 6.2 %collective-permute-start.8 = (bf16[64,512]{1,0:T(8,128)(2,1)S(1)}, bf16[64,512]{1,0:T(8,128)(2,1)S(1)}, u32[]{:S(2)}, u32[]{:S(2)}) collective-permute-start(bf16[64,512]{1,0:T(8,128)(2,1)S(1)} %get-tuple-element.70), channel_id=1, source_target_pairs={{0,8},{4,12},{8,0},{12,4},{1,9},{5,13},{9,1},{13,5},{2,10},{6,14},... | collective-permute-start | bytes 196616 | tf_op jit(solution)/shard_map/ppermute | solution.py:419
  29.1 8.4 %collective-permute-start.9 = (bf16[144,256]{1,0:T(8,128)(2,1)S(1)}, bf16[144,256]{1,0:T(8,128)(2,1)S(1)}, u32[]{:S(2)}, u32[]{:S(2)}) collective-permute-start(bf16[144,256]{1,0:T(8,128)(2,1)S(1)} %get-tuple-element.73), channel_id=1, source_target_pairs={{0,12},{4,8},{8,4},{12,0},{1,13},{5,9},{9,5},{13,1},{2,14},{6,10},... | collective-permute-start | bytes 221192 | tf_op jit(solution)/shard_map/ppermute | solution.py:419
  31.0 7.4 %collective-permute-start.10 = (bf16[144,256]{1,0:T(8,128)(2,1)S(1)}, bf16[144,256]{1,0:T(8,128)(2,1)S(1)}, u32[]{:S(2)}, u32[]{:S(2)}) collective-permute-start(bf16[144,256]{1,0:T(8,128)(2,1)S(1)} %get-tuple-element.74), channel_id=1, source_target_pairs={{0,8},{4,12},{8,0},{12,4},{1,9},{5,13},{9,1},{13,5},{2,10},{6,14},... | collective-permute-start | bytes 221192 | tf_op jit(solution)/shard_map/ppermute | solution.py:419
  31.3 7.1 %collective-permute-start.11 = (bf16[144,256]{1,0:T(8,128)(2,1)S(1)}, bf16[144,256]{1,0:T(8,128)(2,1)S(1)}, u32[]{:S(2)}, u32[]{:S(2)}) collective-permute-start(bf16[144,256]{1,0:T(8,128)(2,1)S(1)} %get-tuple-element.75), channel_id=1, source_target_pairs={{0,4},{4,0},{8,12},{12,8},{1,5},{5,1},{9,13},{13,9},{2,6},{6,2},{1... | collective-permute-start | bytes 221192 | tf_op jit(solution)/shard_map/ppermute | solution.py:419
  33.6 3.9 %collective-permute-start.12 = (bf16[64,256]{1,0:T(8,128)(2,1)S(1)}, bf16[64,256]{1,0:T(8,128)(2,1)S(1)}, u32[]{:S(2)}, u32[]{:S(2)}) collective-permute-start(bf16[64,256]{1,0:T(8,128)(2,1)S(1)} %get-tuple-element.78), channel_id=1, source_target_pairs={{0,2},{2,0},{1,3},{3,1},{4,6},{6,4},{5,7},{7,5},{8,10},{10,8},{9,1... | collective-permute-start | bytes 98312 | tf_op jit(solution)/shard_map/ppermute | solution.py:419
  38.9 7.5 %collective-permute-start.15 = (bf16[192,256]{1,0:T(8,128)(2,1)S(1)}, bf16[192,256]{1,0:T(8,128)(2,1)S(1)}, u32[]{:S(2)}, u32[]{:S(2)}) collective-permute-start(bf16[192,256]{1,0:T(8,128)(2,1)S(1)} %get-tuple-element.79.refs_0_), channel_id=1, source_target_pairs={{0,12},{4,8},{8,4},{12,0},{1,13},{5,9},{9,5},{13,1},{2,14},{6,10},... | collective-permute-start | bytes 294920 | tf_op jit(solution)/shard_map/ppermute | solution.py:419
  40.9 8.8 %collective-permute-start.14 = (bf16[192,256]{1,0:T(8,128)(2,1)S(1)}, bf16[192,256]{1,0:T(8,128)(2,1)S(1)}, u32[]{:S(2)}, u32[]{:S(2)}) collective-permute-start(bf16[192,256]{1,0:T(8,128)(2,1)S(1)} %get-tuple-element.79.refs_0_), channel_id=1, source_target_pairs={{0,8},{4,12},{8,0},{12,4},{1,9},{5,13},{9,1},{13,5},{2,10},{6,14},... | collective-permute-start | bytes 294920 | tf_op jit(solution)/shard_map/ppermute | solution.py:419
  40.9 10.1 %collective-permute-start.13 = (bf16[192,256]{1,0:T(8,128)(2,1)S(1)}, bf16[192,256]{1,0:T(8,128)(2,1)S(1)}, u32[]{:S(2)}, u32[]{:S(2)}) collective-permute-start(bf16[192,256]{1,0:T(8,128)(2,1)S(1)} %get-tuple-element.79.refs_0_), channel_id=1, source_target_pairs={{0,4},{4,0},{8,12},{12,8},{1,5},{5,1},{9,13},{13,9},{2,6},{6,2},{1... | collective-permute-start | bytes 294920 | tf_op jit(solution)/shard_map/ppermute | solution.py:419
  43.7 8.1 %collective-permute-start.7 = (bf16[128,512]{1,0:T(8,128)(2,1)S(1)}, bf16[128,512]{1,0:T(8,128)(2,1)S(1)}, u32[]{:S(2)}, u32[]{:S(2)}) collective-permute-start(bf16[128,512]{1,0:T(8,128)(2,1)S(1)} %shard_map.166.own_ref), channel_id=1, source_target_pairs={{0,1},{1,0},{2,3},{3,2},{4,5},{5,4},{6,7},{7,6},{8,9},{9,8},{10,11... | collective-permute-start | bytes 393224 | tf_op jit(solution)/shard_map/ppermute | solution.py:414
  43.8 8.7 %collective-permute-start.16 = (bf16[192,256]{1,0:T(8,128)(2,1)S(1)}, bf16[192,256]{1,0:T(8,128)(2,1)S(1)}, u32[]{:S(2)}, u32[]{:S(2)}) collective-permute-start(bf16[192,256]{1,0:T(8,128)(2,1)S(1)} %get-tuple-element.79.refs_0_), channel_id=1, source_target_pairs={{0,2},{2,0},{1,3},{3,1},{4,6},{6,4},{5,7},{7,5},{8,10},{10,8},{9,1... | collective-permute-start | bytes 294920 | tf_op jit(solution)/shard_map/ppermute | solution.py:419
  46.5 6.0 %collective-permute-start.19 = (bf16[192,256]{1,0:T(8,128)(2,1)S(1)}, bf16[192,256]{1,0:T(8,128)(2,1)S(1)}, u32[]{:S(2)}, u32[]{:S(2)}) collective-permute-start(bf16[192,256]{1,0:T(8,128)(2,1)S(1)} %collective-permute-done.15.refs_3_), channel_id=1, source_target_pairs={{0,2},{2,0},{1,3},{3,1},{4,6},{6,4},{5,7},{7,5},{8,10},{10,8},{9,1... | collective-permute-start | bytes 294920 | tf_op jit(solution)/shard_map/ppermute | solution.py:419
  49.7 5.7 %collective-permute-start.18 = (bf16[192,256]{1,0:T(8,128)(2,1)S(1)}, bf16[192,256]{1,0:T(8,128)(2,1)S(1)}, u32[]{:S(2)}, u32[]{:S(2)}) collective-permute-start(bf16[192,256]{1,0:T(8,128)(2,1)S(1)} %collective-permute-done.14.refs_2_), channel_id=1, source_target_pairs={{0,2},{2,0},{1,3},{3,1},{4,6},{6,4},{5,7},{7,5},{8,10},{10,8},{9,1... | collective-permute-start | bytes 294920 | tf_op jit(solution)/shard_map/ppermute | solution.py:419
  51.0 5.5 %collective-permute-start.17 = (bf16[192,256]{1,0:T(8,128)(2,1)S(1)}, bf16[192,256]{1,0:T(8,128)(2,1)S(1)}, u32[]{:S(2)}, u32[]{:S(2)}) collective-permute-start(bf16[192,256]{1,0:T(8,128)(2,1)S(1)} %collective-permute-done.13.refs_1_), channel_id=1, source_target_pairs={{0,2},{2,0},{1,3},{3,1},{4,6},{6,4},{5,7},{7,5},{8,10},{10,8},{9,1... | collective-permute-start | bytes 294920 | tf_op jit(solution)/shard_map/ppermute | solution.py:419

commit v4 on v3

--- a/solution.py
+++ b/solution.py
@@ -10,6 +10,7 @@
 BLOCK = 128
 EPSILON = 1e-05
 TAIL = 16
+N_OPERANDS = 10
 VMEM_LIMIT = 24 * 1024 * 1024
 
 f32 = jnp.float32
@@ -61,10 +62,13 @@
     return copies
 
 
-def send_kernel(node_hbm, send_hbm, node_ref, send_ref, *rest):
-    *out_refs, sems = rest
-    for copy in fetch(sems, (node_hbm, node_ref), (send_hbm, send_ref)):
-        copy.wait()
+def send_kernel(*refs):
+    count = N_OPERANDS
+    ins, outs, out_refs, sems = refs[:count], refs[count : 2 * count], refs[2 * count : -1], refs[-1]
+    copies = fetch(sems, *zip(ins, outs))
+    node_ref, send_ref = outs[:2]
+    copies[0].wait()
+    copies[1].wait()
     node = node_ref[...]
     rows = node.shape[0]
     halo = send_ref.shape[2]
@@ -80,23 +84,17 @@
     else:
         out_refs[2][...] = pieces[2]
         out_refs[3][...] = pieces[3]
+    for copy in copies[2:]:
+        copy.wait()
 
 
 def local_kernel(
-    count_ref, node_ref, src_hbm, dst_hbm, bias_hbm, w_src_hbm, w_dst_hbm, w_out_hbm, gain_hbm, cot_hbm,
+    count_ref, node_ref, src_ref, dst_ref, bias_ref, w_src_ref, w_dst_ref,
     pre_ref, pick_ref, collect_ref, spread_ref, scatter_ref,
-    w_src_ref, w_dst_ref, w_out_ref, gain_ref, cot_ref,
-    src_ref, dst_ref, bias_ref, sems,
 ):
-    copies = fetch(
-        sems, (src_hbm, src_ref), (dst_hbm, dst_ref), (bias_hbm, bias_ref), (w_src_hbm, w_src_ref),
-        (w_dst_hbm, w_dst_ref), (w_out_hbm, w_out_ref), (gain_hbm, gain_ref), (cot_hbm, cot_ref),
-    )
     node = node_ref[...]
     rows = node.shape[0]
     edges = src_ref.shape[1]
-    copies[0].wait()
-    copies[1].wait()
     scatter_ref[...] = one_hot(iota(scatter_ref.shape, 0) == src_ref[...])
     used = usable_row(count_ref, edges) > 0
     collect_ref[...] = one_hot((iota((rows, edges), 0) == dst_ref[...]) & used)
@@ -108,13 +106,8 @@
     pick_ref[...] = one_hot(source == lane + rows)
     spread_ref[...] = one_hot((target == lane) & used)
     both = jnp.concatenate([dot(near, node), dot(one_hot(target == lane), node)], axis=1).astype(bf16)
-    copies[2].wait()
-    copies[3].wait()
-    copies[4].wait()
     weights = jnp.concatenate([w_src_ref[...], w_dst_ref[...]], axis=0)
     pre_ref[...] = dot(both, weights) + bias_ref[...]
-    for copy in copies[5:]:
-        copy.wait()
 
 
 def twice(x):
@@ -262,15 +255,10 @@
     return terms[0]
 
 
-def turn_kernel(count, *refs):
-    out_terms = refs[count - 1 :: -1]
-    arrived_ref, keep_ref, *refs = refs[count:]
-    refs = [None] * count + refs
-    line_refs = refs[count : 2 * count]
-    out_send_ref, out_keep_ref, scratch = refs[2 * count :]
-    sub = lax.axis_index("sub")
+def turn_kernel(count, arrived_ref, keep_ref, *refs):
+    *line_refs, scratch = refs
     mesh = lax.axis_index("mesh")
-    full, hid = keep_ref.shape
+    full = keep_ref.shape[0]
     total = keep_ref[...].astype(f32) + arrived_ref[0:full, :].astype(f32)
     rows = full - TAIL
     strip = rows // count
@@ -281,22 +269,23 @@
         start = pl.multiple_of((mesh ^ k) * strip, strip)
         ref[0:strip, :] = scratch[pl.ds(start, strip), :]
         ref[strip:, :] = tail
-    out_strip = out_keep_ref.shape[0]
-    out = tree([r[0:out_strip, :].astype(f32) for r in out_terms])
-    left, right = out[:, :hid], out[:, hid:]
-    out_send_ref[...] = jnp.where(sub == 0, right, left).astype(bf16)
-    out_keep_ref[...] = jnp.where(sub == 0, left, right).astype(bf16)
-
-
-def own_kernel(count, *refs):
-    line_refs = refs[count - 1 :: -1]
-    out_keep_ref, out_arrived_ref, own_ref, bias_ref, gain_ref = refs[count:]
-    total = tree([r[...].astype(f32) for r in line_refs])
-    strip = own_ref.shape[0] - out_keep_ref.shape[0]
-    own_ref[0:strip, :] = total[:strip].astype(bf16)
-    own_ref[strip:, :] = (
-        out_keep_ref[...].astype(f32) + out_arrived_ref[...].astype(f32)
-    ).astype(bf16)
+
+
+def line_kernel(*refs):
+    *terms, out_ref = refs
+    rows = out_ref.shape[0]
+    out_ref[...] = tree([r[0:rows, :].astype(f32) for r in terms]).astype(bf16)
+
+
+def pair_kernel(a_ref, b_ref, out_ref):
+    out_ref[...] = (a_ref[...].astype(f32) + b_ref[...].astype(f32)).astype(bf16)
+
+
+def own_kernel(*refs):
+    *terms, own_ref, bias_ref, gain_ref = refs
+    total = tree([r[...].astype(f32) for r in terms])
+    strip = own_ref.shape[0]
+    own_ref[...] = total[:strip].astype(bf16)
     write_vectors(total[strip:], bias_ref, gain_ref)
 
 
@@ -308,23 +297,19 @@
 
 
 def place_kernel(count, *refs):
-    mine, theirs = refs[:count], refs[count : 2 * count]
-    src_ref, dst_ref, out_ref = refs[2 * count :]
+    mine, theirs, outs = refs[:count], refs[count : 2 * count], refs[2 * count : 3 * count]
+    src_ref, dst_ref, out_ref = refs[3 * count :]
     first = lax.axis_index("sub") == 0
     mesh = lax.axis_index("mesh")
-    width, hid = src_ref.shape
-    strip = width // count
-    narrow = hid // count
+    strip = mine[0].shape[0]
+    narrow = outs[0].shape[0]
     for k in range(count):
         a, b = mine[k][...], theirs[k][...]
-        low = jnp.where(first, a, b).astype(f32)
-        high = jnp.where(first, b, a).astype(f32)
         start = pl.multiple_of((mesh ^ k) * strip, strip)
-        src_ref[pl.ds(start, strip), :] = low[:strip]
-        dst_ref[pl.ds(start, strip), :] = high[:strip]
+        src_ref[pl.ds(start, strip), :] = jnp.where(first, a, b).astype(f32)
+        dst_ref[pl.ds(start, strip), :] = jnp.where(first, b, a).astype(f32)
         start = pl.multiple_of((mesh ^ k) * narrow, narrow)
-        out_ref[pl.ds(start, narrow), 0:hid] = low[strip:]
-        out_ref[pl.ds(start, narrow), hid:] = high[strip:]
+        out_ref[pl.ds(start, narrow), :] = outs[k][...].astype(f32)
 
 
 def sum_kernel(chunk, arrived_ref, out_ref, bias_ref, gain_ref):
@@ -419,30 +404,40 @@
     return lax.ppermute(x, axis, [(i, i ^ k) for i in range(count)])
 
 
+def gather_line(x, lines):
+    three = across(x, "mesh", 3)
+    one = across(x, "mesh", 1)
+    return [x, one, across(three, "mesh", 1), three]
+
+
 def paired_sums(messages, lines, strip, narrow, width, hid):
     send, keep, *outs = messages
     order = range(lines - 1, 0, -1)
     out_terms = {k: across(outs[k], "mesh", k) for k in order}
     arrived = across(send, "sub", 1)
-    *line, out_send, out_keep = call(
+    line = call(
         functools.partial(turn_kernel, lines),
-        [shape((strip + TAIL, hid), bf16)] * lines + [shape((narrow, hid), bf16)] * 2,
-        *[out_terms[k] for k in order], outs[0], arrived, keep,
+        [shape((strip + TAIL, hid), bf16)] * lines,
+        arrived, keep,
         scratch=[pltpu.VMEM((width, hid), bf16)],
     )
     line_terms = {k: across(line[k], "mesh", k) for k in order}
+    quarter = call(
+        line_kernel, shape((narrow, width), bf16), *[out_terms[k] for k in order], outs[0]
+    )
+    quarter = call(pair_kernel, shape((narrow, width), bf16), quarter, across(quarter, "sub", 1))
     own, bias_grad, gain_grad = call(
-        functools.partial(own_kernel, lines),
-        [shape((strip + narrow, hid), bf16), shape((1, hid), f32), shape((1, width), f32)],
-        *[line_terms[k] for k in order], line[0], out_keep, across(out_send, "sub", 1),
-    )
-    mine = {k: across(own, "mesh", k) for k in order}
-    mine[0] = own
-    theirs = {k: across(mine[k], "sub", 1) for k in mine}
+        own_kernel,
+        [shape((strip, hid), bf16), shape((1, hid), f32), shape((1, width), f32)],
+        *[line_terms[k] for k in order], line[0],
+    )
+    out = gather_line(quarter, lines)
+    mine = gather_line(own, lines)
+    theirs = [across(x, "sub", 1) for x in mine]
     grads = call(
         functools.partial(place_kernel, lines),
         [shape((width, hid), f32), shape((width, hid), f32), shape((hid, width), f32)],
-        *[mine[k] for k in range(lines)], *[theirs[k] for k in range(lines)],
+        *mine, *theirs, *out,
     )
     return (*grads, bias_grad, gain_grad), (out_terms[3], out_terms[1], arrived)
 
@@ -473,17 +468,20 @@
     routes = [("mesh", 1), ("mesh", -1), ("sub", 1)] + ([] if merged else [("sub", -1)])
     n_halo = len(piece)
 
-    node, send, *outgoing = call(
+    operands = [
+        node_state, send_rows, edge_src.reshape(1, edges), edge_dst.reshape(1, edges),
+        hidden_bias.reshape(1, hid), w_src, w_dst, w_out, norm_gain.reshape(1, width), cotangent,
+    ]
+    node, send, src, dst, bias, w_src, w_dst, w_out, gain, cot, *outgoing = call(
         send_kernel,
-        [shape((rows, width), bf16), shape(send_rows.shape, jnp.int32)]
-        + [shape((n, width), bf16) for n in piece],
-        node_state, send_rows,
-        specs=[HBM, HBM],
-        scratch=[pltpu.SemaphoreType.DMA((2,))],
+        [shape(x.shape, x.dtype) for x in operands] + [shape((n, width), bf16) for n in piece],
+        *[pltpu.with_memory_space_constraint(x, pltpu.HBM) for x in operands],
+        specs=[HBM] * len(operands),
+        scratch=[pltpu.SemaphoreType.DMA((N_OPERANDS,))],
     )
     arrived = [shifted(x, axis, by) for x, (axis, by) in zip(outgoing, routes)]
 
-    pre, pick, collect, spread, scatter, w_src, w_dst, w_out, gain, cot = call(
+    pre, pick, collect, spread, scatter = call(
         local_kernel,
         [
             shape((edges, hid), f32),
@@ -491,21 +489,9 @@
             shape((rows, edges), bf16),
             shape((edges, rows), bf16),
             shape((rows + 4 * halo, edges), bf16),
-            shape(w_src.shape, bf16),
-            shape(w_dst.shape, bf16),
-            shape(w_out.shape, bf16),
-            shape((1, width), f32),
-            shape((rows, width), bf16),
         ],
-        block_count, node, edge_src.reshape(1, edges), edge_dst.reshape(1, edges),
-        hidden_bias.reshape(1, hid), w_src, w_dst, w_out, norm_gain.reshape(1, width), cotangent,
-        specs=[SMEM, VMEM] + [HBM] * 8,
-        scratch=[
-            pltpu.VMEM((1, edges), jnp.int32),
-            pltpu.VMEM((1, edges), jnp.int32),
-            pltpu.VMEM((1, hid), f32),
-            pltpu.SemaphoreType.DMA((8,)),
-        ],
+        block_count, node, src, dst, bias, w_src, w_dst,
+        specs=[SMEM] + [VMEM] * 6,
     )
 
     factor, hidden, partial = call(

time: 58 us -> 52.8 us (0.910)
  local copies, waits for them, and re-layouts: 5.13 us -> 0.65 us
  starting transfers between devices: 27.6 us -> 26.7 us
    unnamed x22 -> x2, local copies, waits for them, and re-layouts: 5.13 us -> 0.65 us
    ppermute x15 -> x18, starting transfers between devices: 20.6 us -> 19.8 us  [across(): return lax.ppermute(x, axis, [(i, i ^ k) for i in range(count)])]
    pallas_call x9 -> x11, Pallas kernels: 8.51 us -> 8.89 us  [call(): pl.pallas_call(kernel, out_shape=outs, in_specs=specs or [VMEM] * len(arg...]
    ppermute x15 -> x18, waiting for transfers between devices: 14.5 us -> 14.3 us  [across(): return lax.ppermute(x, axis, [(i, i ^ k) for i in range(count)])]
  transfers between devices with their start and end apart: 20 -> 23, of which waited for: 9 -> 10; matrix products, arithmetic and copies ran while one was open for 0% -> 0% of each run, Pallas kernels for 6% -> 6%
where the time goes in v4:
time: 52.8 us; the launch traced here: 52.6 us
  starting transfers between devices  26.7 us (51%)
  waiting for transfers between devices  15.6 us (30%)
  Pallas kernels  8.89 us (17%)
  between operations  0.72 us (1%)
  local copies, waits for them, and re-layouts  0.65 us (1%)
    ppermute x18, starting transfers between devices, across(): return lax.ppermute(x, axis, [(i, i ^ k) for i in range(count)])  19.8 us
    ppermute x18, waiting for transfers between devices, across(): return lax.ppermute(x, axis, [(i, i ^ k) for i in range(count)])  14.3 us
    pallas_call x11, Pallas kernels, call(): pl.pallas_call(kernel, out_shape=outs, in_specs=specs or [VMEM] * len(arg...  8.89 us
    ppermute x5, starting transfers between devices, shifted(): return lax.ppermute(x, axis, [(i, (i + by) % count) for i in range(count)])  6.97 us
    ppermute x5, waiting for transfers between devices, shifted(): return lax.ppermute(x, axis, [(i, (i + by) % count) for i in range(count)])  1.37 us
  transfers between devices with their start and end apart: 23, of which 10 were waited for; matrix products, arithmetic and copies ran while one was open for 0% of the time, Pallas kernels for 6%

profile of v4, /device:TPU:0, one launch (start us, length us, event | category | flops | bytes accessed | tf_op | source)
XLA Modules:
  0.0 52.6 jit_solution(4707648524718091312)
XLA Ops:
  0.6 1.4 %shard_map.162 = (bf16[128,512]{1,0:T(8,128)(2,1)S(1)}, s32[1,4,32]{2,1,0:T(4,128)S(1)}, s32[1,512]{1,0:T(1,128)S(1)}, s32[1,512]{1,0:T(1,128)S(1)}, f32[1,256]{...) custom-call(bf16[128,512]{1,0:T(8,128)(2,1)} %refs_0_.1, ...), custom_call_target="tpu_custom_call" | custom-call | flops 100000000 | bytes 1000000 | tf_op jit(solution)/shard_map/pallas_call | solution.py:386
  2.0 3.0 %collective-permute-start.2 = (bf16[64,512]{1,0:T(8,128)(2,1)S(1)}, bf16[64,512]{1,0:T(8,128)(2,1)S(1)}, u32[]{:S(2)}, u32[]{:S(2)}) collective-permute-start(bf16[64,512]{1,0:T(8,128)(2,1)S(1)} %get-tuple-element.63), channel_id=1, source_target_pairs={{0,2},{2,0},{1,3},{3,1},{4,6},{6,4},{5,7},{7,5},{8,10},{10,8},{9,1... | collective-permute-start | bytes 196616 | tf_op jit(solution)/shard_map/ppermute | solution.py:399
  5.0 1.6 %collective-permute-start = (bf16[32,512]{1,0:T(8,128)(2,1)S(1)}, bf16[32,512]{1,0:T(8,128)(2,1)S(1)}, u32[]{:S(2)}, u32[]{:S(2)}) collective-permute-start(bf16[32,512]{1,0:T(8,128)(2,1)S(1)} %get-tuple-element.61), channel_id=1, source_target_pairs={{0,4},{4,8},{8,12},{12,0},{1,5},{5,9},{9,13},{13,1},{2,6},{6,10},{... | collective-permute-start | bytes 98312 | tf_op jit(solution)/shard_map/ppermute | solution.py:399
  6.6 2.2 %collective-permute-start.1 = (bf16[32,512]{1,0:T(8,128)(2,1)S(1)}, bf16[32,512]{1,0:T(8,128)(2,1)S(1)}, u32[]{:S(2)}, u32[]{:S(2)}) collective-permute-start(bf16[32,512]{1,0:T(8,128)(2,1)S(1)} %get-tuple-element.62), channel_id=1, source_target_pairs={{0,12},{4,0},{8,4},{12,8},{1,13},{5,1},{9,5},{13,9},{2,14},{6,2},{... | collective-permute-start | bytes 98312 | tf_op jit(solution)/shard_map/ppermute | solution.py:399
  8.8 0.0 copy-start
  8.9 0.7 %copy-done = s32[4]{0:T(128)S(1)} copy-done((s32[4]{0:T(128)S(1)}, s32[4]{0:T(128)}, u32[]{:S(2)}) %copy-start) | copy-done | bytes 40
  9.5 1.4 %shard_map.163 = (f32[512,256]{1,0:T(8,128)S(1)}, bf16[512,128]{1,0:T(8,128)(2,1)S(1)}, bf16[128,512]{1,0:T(8,128)(2,1)S(1)}, bf16[512,128]{1,0:T(8,128)(2,1)S(1)}, bf16[256,512]{1,0:T(8,128)(2,1)S(1)}) custom-call(s32[4]{0:T(128)S(1)} %copy-done, bf16[128,512]{1,0:T(8,128)(2,1)S(1)} %get-tuple-element.47.node_ref, s32[1,512]{1,0:T(1,128)S(1)} %get-tuple-element.48.src_ref, ...), custom_call_target="tpu_custom_call" | custom-call | flops 100000000 | bytes 1000000 | tf_op jit(solution)/shard_map/pallas_call | solution.py:386
  11.0 0.0 collective-permute-done.rest_0_
  11.0 0.0 collective-permute-done.1.rest_1_
  11.0 0.0 collective-permute-done.2.rest_2_
  11.0 0.9 %shard_map.164 = (f32[512,256]{1,0:T(8,128)S(1)}, bf16[128,256]{1,0:T(8,128)(2,1)S(1)}, bf16[128,512]{1,0:T(8,128)(2,1)S(1)}) custom-call(f32[512,256]{1,0:T(8,128)S(1)} %get-tuple-element.59.pre_ref, bf16[512,128]{1,0:T(8,128)(2,1)S(1)} %get-tuple-element.60.pick_ref, bf16[128,512]{1,0:T(8,128)(2,1)S(1)} %get-tuple-element.53.collect_ref, ...), custom_call_target="tpu_custom_call" | custom-call | flops 100000000 | bytes 1000000 | tf_op jit(solution)/shard_map/pallas_call | solution.py:386
  11.9 0.1 collective-permute-start.3
  11.9 1.3 %collective-permute-done.3.other_ref = bf16[128,512]{1,0:T(8,128)(2,1)S(1)} collective-permute-done((bf16[128,512]{1,0:T(8,128)(2,1)S(1)}, bf16[128,512]{1,0:T(8,128)(2,1)S(1)}, u32[]{:S(2)}, u32[]{:S(2)}) %collective-permute-start.3) | collective-permute-done | bytes 131104 | tf_op jit(solution)/shard_map/ppermute | solution.py:399
  13.3 2.1 %shard_map.165 = (bf16[128,512]{1,0:T(8,128)(2,1)}, f32[128,256]{1,0:T(8,128)S(1)}, bf16[128,256]{1,0:T(8,128)(2,1)S(1)}, bf16[592,256]{1,0:T(8,128)(2,1)S(1)}, ...) custom-call(bf16[128,512]{1,0:T(8,128)(2,1)S(1)} %get-tuple-element., ...), custom_call_target="tpu_custom_call" | custom-call | flops 100000000 | bytes 1000000 | tf_op jit(solution)/shard_map/pallas_call | solution.py:386
  15.3 0.4 collective-permute-start.6
  15.8 2.2 %collective-permute-start.18 = (bf16[64,512]{1,0:T(8,128)(2,1)S(1)}, bf16[64,512]{1,0:T(8,128)(2,1)S(1)}, u32[]{:S(2)}, u32[]{:S(2)}) collective-permute-start(bf16[64,512]{1,0:T(8,128)(2,1)S(1)} %get-tuple-element.80), channel_id=1, source_target_pairs={{0,8},{4,12},{8,0},{12,4},{1,9},{5,13},{9,1},{13,5},{2,10},{6,14},... | collective-permute-start | bytes 196616 | tf_op jit(solution)/shard_map/ppermute | solution.py:404
  18.0 1.3 %collective-permute-start.4 = (bf16[80,512]{1,0:T(8,128)(2,1)S(1)}, bf16[80,512]{1,0:T(8,128)(2,1)S(1)}, u32[]{:S(2)}, u32[]{:S(2)}) collective-permute-start(bf16[80,512]{1,0:T(8,128)(2,1)S(1)} %get-tuple-element.71), channel_id=1, source_target_pairs={{0,12},{4,8},{8,4},{12,0},{1,13},{5,9},{9,5},{13,1},{2,14},{6,10},... | collective-permute-start | bytes 245768 | tf_op jit(solution)/shard_map/ppermute | solution.py:404
  19.3 0.5 collective-permute-start.5
  19.8 4.8 %collective-permute-done.6.pair_ref.arrived_ref = bf16[592,256]{1,0:T(8,128)(2,1)S(1)} collective-permute-done((bf16[592,256]{1,0:T(8,128)(2,1)S(1)}, bf16[592,256]{1,0:T(8,128)(2,1)S(1)}, u32[]{:S(2)}, u32[]{:S(2)}) %collective-permute-start.6) | collective-permute-done | bytes 303136 | tf_op jit(solution)/shard_map/ppermute | solution.py:404
  24.6 0.1 shard_map.168
  24.7 3.6 %collective-permute-start.8 = (bf16[144,256]{1,0:T(8,128)(2,1)S(1)}, bf16[144,256]{1,0:T(8,128)(2,1)S(1)}, u32[]{:S(2)}, u32[]{:S(2)}) collective-permute-start(bf16[144,256]{1,0:T(8,128)(2,1)S(1)} %get-tuple-element.75), channel_id=1, source_target_pairs={{0,12},{4,8},{8,4},{12,0},{1,13},{5,9},{9,5},{13,1},{2,14},{6,10},... | collective-permute-start | bytes 221192 | tf_op jit(solution)/shard_map/ppermute | solution.py:404
  28.4 0.0 collective-permute-start.9
  28.4 0.0 collective-permute-done.18.refs_1_
  28.4 0.8 %collective-permute-start.10 = (bf16[144,256]{1,0:T(8,128)(2,1)S(1)}, bf16[144,256]{1,0:T(8,128)(2,1)S(1)}, u32[]{:S(2)}, u32[]{:S(2)}) collective-permute-start(bf16[144,256]{1,0:T(8,128)(2,1)S(1)} %get-tuple-element.77), channel_id=1, source_target_pairs={{0,4},{4,0},{8,12},{12,8},{1,5},{5,1},{9,13},{13,9},{2,6},{6,2},{1... | collective-permute-start | bytes 221192 | tf_op jit(solution)/shard_map/ppermute | solution.py:404
  29.2 0.0 collective-permute-done.4.three_ref.refs_0_
  29.2 0.0 collective-permute-done.5.one_ref.refs_2_
  29.2 0.5 collective-permute-start.19
  29.7 0.4 shard_map.166.own_ref
  30.1 0.1 collective-permute-start.7
  30.2 0.9 %collective-permute-done.8.refs_0_ = bf16[144,256]{1,0:T(8,128)(2,1)S(1)} collective-permute-done((bf16[144,256]{1,0:T(8,128)(2,1)S(1)}, bf16[144,256]{1,0:T(8,128)(2,1)S(1)}, u32[]{:S(2)}, u32[]{:S(2)}) %collective-permute-start.8) | collective-permute-done | bytes 73760 | tf_op jit(solution)/shard_map/ppermute | solution.py:404
  31.1 3.0 %collective-permute-done.9.refs_1_ = bf16[144,256]{1,0:T(8,128)(2,1)S(1)} collective-permute-done((bf16[144,256]{1,0:T(8,128)(2,1)S(1)}, bf16[144,256]{1,0:T(8,128)(2,1)S(1)}, u32[]{:S(2)}, u32[]{:S(2)}) %collective-permute-start.9) | collective-permute-done | bytes 73760 | tf_op jit(solution)/shard_map/ppermute | solution.py:404
  34.1 0.0 collective-permute-done.10.refs_2_
  34.1 0.6 %shard_map.169 = (bf16[128,256]{1,0:T(8,128)(2,1)S(1)}, f32[1,256]{1,0:T(1,128)}, f32[1,512]{1,0:T(1,128)}) custom-call(bf16[144,256]{1,0:T(8,128)(2,1)S(1)} %collective-permute-done.8.refs_0_, bf16[144,256]{1,0:T(8,128)(2,1)S(1)} %collective-permute-done.9.refs_1_, bf16[144,256]{1,0:T(8,128)(2,1)S(1)} %collective-permute-done.10.refs_2_, ...), custom_call_target="tpu_custom_call" | custom-call | flops 100000000 | bytes 1000000 | tf_op jit(solution)/shard_map/pallas_call | solution.py:386
  34.7 2.6 %collective-permute-start.12 = (bf16[128,256]{1,0:T(8,128)(2,1)S(1)}, bf16[128,256]{1,0:T(8,128)(2,1)S(1)}, u32[]{:S(2)}, u32[]{:S(2)}) collective-permute-start(bf16[128,256]{1,0:T(8,128)(2,1)S(1)} %get-tuple-element.79.refs_0_), channel_id=1, source_target_pairs={{0,12},{4,8},{8,4},{12,0},{1,13},{5,9},{9,5},{13,1},{2,14},{6,10},... | collective-permute-start | bytes 196616 | tf_op jit(solution)/shard_map/ppermute | solution.py:404
  37.4 0.0 collective-permute-done.19.b_ref
  37.4 1.3 %collective-permute-start.21 = (bf16[64,512]{1,0:T(8,128)(2,1)S(1)}, bf16[64,512]{1,0:T(8,128)(2,1)S(1)}, u32[]{:S(2)}, u32[]{:S(2)}) collective-permute-start(bf16[64,512]{1,0:T(8,128)(2,1)S(1)} %shard_map.171.refs_8_), channel_id=1, source_target_pairs={{0,12},{4,8},{8,4},{12,0},{1,13},{5,9},{9,5},{13,1},{2,14},{6,10},... | collective-permute-start | bytes 196616 | tf_op jit(solution)/shard_map/ppermute | solution.py:404
  38.7 0.0 collective-permute-start.20
  38.7 2.0 %collective-permute-start.11 = (bf16[128,256]{1,0:T(8,128)(2,1)S(1)}, bf16[128,256]{1,0:T(8,128)(2,1)S(1)}, u32[]{:S(2)}, u32[]{:S(2)}) collective-permute-start(bf16[128,256]{1,0:T(8,128)(2,1)S(1)} %get-tuple-element.79.refs_0_), channel_id=1, source_target_pairs={{0,4},{4,0},{8,12},{12,8},{1,5},{5,1},{9,13},{13,9},{2,6},{6,2},{1... | collective-permute-start | bytes 196616 | tf_op jit(solution)/shard_map/ppermute | solution.py:404
  40.7 0.7 %collective-permute-done.12.refs_3_ = bf16[128,256]{1,0:T(8,128)(2,1)S(1)} collective-permute-done((bf16[128,256]{1,0:T(8,128)(2,1)S(1)}, bf16[128,256]{1,0:T(8,128)(2,1)S(1)}, u32[]{:S(2)}, u32[]{:S(2)}) %collective-permute-start.12) | collective-permute-done | bytes 65568 | tf_op jit(solution)/shard_map/ppermute | solution.py:404
  41.4 0.4 collective-permute-start.13
  41.8 2.2 %collective-permute-done.21.refs_11_ = bf16[64,512]{1,0:T(8,128)(2,1)S(1)} collective-permute-done((bf16[64,512]{1,0:T(8,128)(2,1)S(1)}, bf16[64,512]{1,0:T(8,128)(2,1)S(1)}, u32[]{:S(2)}, u32[]{:S(2)}) %collective-permute-start.21) | collective-permute-done | bytes 65568 | tf_op jit(solution)/shard_map/ppermute | solution.py:404
  44.0 0.0 collective-permute-start.22
  44.0 0.4 collective-permute-done.20.refs_9_
  44.4 0.3 collective-permute-start.14
  44.7 0.0 collective-permute-done.7.other_ref
  44.7 1.7 %collective-permute-start.17 = (bf16[128,256]{1,0:T(8,128)(2,1)S(1)}, bf16[128,256]{1,0:T(8,128)(2,1)S(1)}, u32[]{:S(2)}, u32[]{:S(2)}) collective-permute-start(bf16[128,256]{1,0:T(8,128)(2,1)S(1)} %collective-permute-done.12.refs_3_), channel_id=1, source_target_pairs={{0,2},{2,0},{1,3},{3,1},{4,6},{6,4},{5,7},{7,5},{8,10},{10,8},{9,1... | collective-permute-start | bytes 196616 | tf_op jit(solution)/shard_map/ppermute | solution.py:404
  46.4 0.0 collective-permute-done.11.refs_1_
  46.4 0.3 collective-permute-start.15
  46.7 0.0 collective-permute-done.13.refs_2_
  46.8 1.7 %collective-permute-start.16 = (bf16[128,256]{1,0:T(8,128)(2,1)S(1)}, bf16[128,256]{1,0:T(8,128)(2,1)S(1)}, u32[]{:S(2)}, u32[]{:S(2)}) collective-permute-start(bf16[128,256]{1,0:T(8,128)(2,1)S(1)} %collective-permute-done.13.refs_2_), channel_id=1, source_target_pairs={{0,2},{2,0},{1,3},{3,1},{4,6},{6,4},{5,7},{7,5},{8,10},{10,8},{9,1... | collective-permute-start | bytes 196616 | tf_op jit(solution)/shard_map/ppermute | solution.py:404
  48.5 0.8 %shard_map.167 = f32[128,512]{1,0:T(8,128)} custom-call(bf16[128,512]{1,0:T(8,128)(2,1)S(1)} %get-tuple-element.58.cot_ref, bf16[128,512]{1,0:T(8,128)(2,1)S(1)} %shard_map.166.own_ref, bf16[128,512]{1,0:T(8,128)(2,1)S(1)} %collective-permute-done.7.other_ref), custom_call_target="tpu_custom_call" | custom-call | flops 100000000 | bytes 1000000 | tf_op jit(solution)/shard_map/pallas_call | solution.py:386
  49.2 0.0 collective-permute-done.22.refs_10_
  49.2 0.0 collective-permute-done.14.refs_4_
  49.2 0.5 collective-permute-done.17.refs_7_
  49.7 1.0 %collective-permute-done.15.refs_5_ = bf16[128,256]{1,0:T(8,128)(2,1)S(1)} collective-permute-done((bf16[128,256]{1,0:T(8,128)(2,1)S(1)}, bf16[128,256]{1,0:T(8,128)(2,1)S(1)}, u32[]{:S(2)}, u32[]{:S(2)}) %collective-permute-start.15) | collective-permute-done | bytes 65568 | tf_op jit(solution)/shard_map/ppermute | solution.py:404
  50.7 0.7 %collective-permute-done.16.refs_6_ = bf16[128,256]{1,0:T(8,128)(2,1)S(1)} collective-permute-done((bf16[128,256]{1,0:T(8,128)(2,1)S(1)}, bf16[128,256]{1,0:T(8,128)(2,1)S(1)}, u32[]{:S(2)}, u32[]{:S(2)}) %collective-permute-start.16) | collective-permute-done | bytes 65568 | tf_op jit(solution)/shard_map/ppermute | solution.py:404
  51.4 1.2 %shard_map.172 = (f32[512,256]{1,0:T(8,128)}, f32[512,256]{1,0:T(8,128)}, f32[256,512]{1,0:T(8,128)}) custom-call(bf16[128,256]{1,0:T(8,128)(2,1)S(1)} %get-tuple-element.79.refs_0_, bf16[128,256]{1,0:T(8,128)(2,1)S(1)} %collective-permute-done.11.refs_1_, bf16[128,256]{1,0:T(8,128)(2,1)S(1)} %collective-permute-done.13.refs_2_, ...), custom_call_target="tpu_custom_call" | custom-call | flops 100000000 | bytes 1000000 | tf_op jit(solution)/shard_map/pallas_call | solution.py:386
  (2 shorter events, 0.1 us)
Async XLA Ops:
  2.0 9.0 %collective-permute-start.2 = (bf16[64,512]{1,0:T(8,128)(2,1)S(1)}, bf16[64,512]{1,0:T(8,128)(2,1)S(1)}, u32[]{:S(2)}, u32[]{:S(2)}) collective-permute-start(bf16[64,512]{1,0:T(8,128)(2,1)S(1)} %get-tuple-element.63), channel_id=1, source_target_pairs={{0,2},{2,0},{1,3},{3,1},{4,6},{6,4},{5,7},{7,5},{8,10},{10,8},{9,1... | collective-permute-start | bytes 196616 | tf_op jit(solution)/shard_map/ppermute | solution.py:399
  5.0 6.0 %collective-permute-start = (bf16[32,512]{1,0:T(8,128)(2,1)S(1)}, bf16[32,512]{1,0:T(8,128)(2,1)S(1)}, u32[]{:S(2)}, u32[]{:S(2)}) collective-permute-start(bf16[32,512]{1,0:T(8,128)(2,1)S(1)} %get-tuple-element.61), channel_id=1, source_target_pairs={{0,4},{4,8},{8,12},{12,0},{1,5},{5,9},{9,13},{13,1},{2,6},{6,10},{... | collective-permute-start | bytes 98312 | tf_op jit(solution)/shard_map/ppermute | solution.py:399
  6.6 4.4 %collective-permute-start.1 = (bf16[32,512]{1,0:T(8,128)(2,1)S(1)}, bf16[32,512]{1,0:T(8,128)(2,1)S(1)}, u32[]{:S(2)}, u32[]{:S(2)}) collective-permute-start(bf16[32,512]{1,0:T(8,128)(2,1)S(1)} %get-tuple-element.62), channel_id=1, source_target_pairs={{0,12},{4,0},{8,4},{12,8},{1,13},{5,1},{9,5},{13,9},{2,14},{6,2},{... | collective-permute-start | bytes 98312 | tf_op jit(solution)/shard_map/ppermute | solution.py:399
  8.8 0.7 %copy-start = (s32[4]{0:T(128)S(1)}, s32[4]{0:T(128)}, u32[]{:S(2)}) copy-start(s32[4]{0:T(128)} %count_ref.1) | copy-start | bytes 52
  11.9 1.4 %collective-permute-start.3 = (bf16[128,512]{1,0:T(8,128)(2,1)S(1)}, bf16[128,512]{1,0:T(8,128)(2,1)S(1)}, u32[]{:S(2)}, u32[]{:S(2)}) collective-permute-start(bf16[128,512]{1,0:T(8,128)(2,1)S(1)} %get-tuple-element.66.own_ref), channel_id=1, source_target_pairs={{0,1},{1,0},{2,3},{3,2},{4,5},{5,4},{6,7},{7,6},{8,9},{9,8},{10,11... | collective-permute-start | bytes 393224 | tf_op jit(solution)/shard_map/ppermute | solution.py:399
  15.3 9.2 %collective-permute-start.6 = (bf16[592,256]{1,0:T(8,128)(2,1)S(1)}, bf16[592,256]{1,0:T(8,128)(2,1)S(1)}, u32[]{:S(2)}, u32[]{:S(2)}) collective-permute-start(bf16[592,256]{1,0:T(8,128)(2,1)S(1)} %get-tuple-element.73), channel_id=1, source_target_pairs={{0,2},{2,0},{1,3},{3,1},{4,6},{6,4},{5,7},{7,5},{8,10},{10,8},{9,1... | collective-permute-start | bytes 909320 | tf_op jit(solution)/shard_map/ppermute | solution.py:404
  15.8 12.6 %collective-permute-start.18 = (bf16[64,512]{1,0:T(8,128)(2,1)S(1)}, bf16[64,512]{1,0:T(8,128)(2,1)S(1)}, u32[]{:S(2)}, u32[]{:S(2)}) collective-permute-start(bf16[64,512]{1,0:T(8,128)(2,1)S(1)} %get-tuple-element.80), channel_id=1, source_target_pairs={{0,8},{4,12},{8,0},{12,4},{1,9},{5,13},{9,1},{13,5},{2,10},{6,14},... | collective-permute-start | bytes 196616 | tf_op jit(solution)/shard_map/ppermute | solution.py:404
  18.0 11.2 %collective-permute-start.4 = (bf16[80,512]{1,0:T(8,128)(2,1)S(1)}, bf16[80,512]{1,0:T(8,128)(2,1)S(1)}, u32[]{:S(2)}, u32[]{:S(2)}) collective-permute-start(bf16[80,512]{1,0:T(8,128)(2,1)S(1)} %get-tuple-element.71), channel_id=1, source_target_pairs={{0,12},{4,8},{8,4},{12,0},{1,13},{5,9},{9,5},{13,1},{2,14},{6,10},... | collective-permute-start | bytes 245768 | tf_op jit(solution)/shard_map/ppermute | solution.py:404
  19.3 9.8 %collective-permute-start.5 = (bf16[80,512]{1,0:T(8,128)(2,1)S(1)}, bf16[80,512]{1,0:T(8,128)(2,1)S(1)}, u32[]{:S(2)}, u32[]{:S(2)}) collective-permute-start(bf16[80,512]{1,0:T(8,128)(2,1)S(1)} %get-tuple-element.72), channel_id=1, source_target_pairs={{0,4},{4,0},{8,12},{12,8},{1,5},{5,1},{9,13},{13,9},{2,6},{6,2},{1... | collective-permute-start | bytes 245768 | tf_op jit(solution)/shard_map/ppermute | solution.py:404
  24.7 6.4 %collective-permute-start.8 = (bf16[144,256]{1,0:T(8,128)(2,1)S(1)}, bf16[144,256]{1,0:T(8,128)(2,1)S(1)}, u32[]{:S(2)}, u32[]{:S(2)}) collective-permute-start(bf16[144,256]{1,0:T(8,128)(2,1)S(1)} %get-tuple-element.75), channel_id=1, source_target_pairs={{0,12},{4,8},{8,4},{12,0},{1,13},{5,9},{9,5},{13,1},{2,14},{6,10},... | collective-permute-start | bytes 221192 | tf_op jit(solution)/shard_map/ppermute | solution.py:404
  28.4 5.8 %collective-permute-start.9 = (bf16[144,256]{1,0:T(8,128)(2,1)S(1)}, bf16[144,256]{1,0:T(8,128)(2,1)S(1)}, u32[]{:S(2)}, u32[]{:S(2)}) collective-permute-start(bf16[144,256]{1,0:T(8,128)(2,1)S(1)} %get-tuple-element.76), channel_id=1, source_target_pairs={{0,8},{4,12},{8,0},{12,4},{1,9},{5,13},{9,1},{13,5},{2,10},{6,14},... | collective-permute-start | bytes 221192 | tf_op jit(solution)/shard_map/ppermute | solution.py:404
  28.4 5.8 %collective-permute-start.10 = (bf16[144,256]{1,0:T(8,128)(2,1)S(1)}, bf16[144,256]{1,0:T(8,128)(2,1)S(1)}, u32[]{:S(2)}, u32[]{:S(2)}) collective-permute-start(bf16[144,256]{1,0:T(8,128)(2,1)S(1)} %get-tuple-element.77), channel_id=1, source_target_pairs={{0,4},{4,0},{8,12},{12,8},{1,5},{5,1},{9,13},{13,9},{2,6},{6,2},{1... | collective-permute-start | bytes 221192 | tf_op jit(solution)/shard_map/ppermute | solution.py:404
  29.2 8.2 %collective-permute-start.19 = (bf16[64,512]{1,0:T(8,128)(2,1)S(1)}, bf16[64,512]{1,0:T(8,128)(2,1)S(1)}, u32[]{:S(2)}, u32[]{:S(2)}) collective-permute-start(bf16[64,512]{1,0:T(8,128)(2,1)S(1)} %shard_map.170.a_ref), channel_id=1, source_target_pairs={{0,2},{2,0},{1,3},{3,1},{4,6},{6,4},{5,7},{7,5},{8,10},{10,8},{9,1... | collective-permute-start | bytes 196616 | tf_op jit(solution)/shard_map/ppermute | solution.py:404
  30.1 14.6 %collective-permute-start.7 = (bf16[128,512]{1,0:T(8,128)(2,1)S(1)}, bf16[128,512]{1,0:T(8,128)(2,1)S(1)}, u32[]{:S(2)}, u32[]{:S(2)}) collective-permute-start(bf16[128,512]{1,0:T(8,128)(2,1)S(1)} %shard_map.166.own_ref), channel_id=1, source_target_pairs={{0,1},{1,0},{2,3},{3,2},{4,5},{5,4},{6,7},{7,6},{8,9},{9,8},{10,11... | collective-permute-start | bytes 393224 | tf_op jit(solution)/shard_map/ppermute | solution.py:399
  34.7 6.7 %collective-permute-start.12 = (bf16[128,256]{1,0:T(8,128)(2,1)S(1)}, bf16[128,256]{1,0:T(8,128)(2,1)S(1)}, u32[]{:S(2)}, u32[]{:S(2)}) collective-permute-start(bf16[128,256]{1,0:T(8,128)(2,1)S(1)} %get-tuple-element.79.refs_0_), channel_id=1, source_target_pairs={{0,12},{4,8},{8,4},{12,0},{1,13},{5,9},{9,5},{13,1},{2,14},{6,10},... | collective-permute-start | bytes 196616 | tf_op jit(solution)/shard_map/ppermute | solution.py:404
  37.4 6.6 %collective-permute-start.21 = (bf16[64,512]{1,0:T(8,128)(2,1)S(1)}, bf16[64,512]{1,0:T(8,128)(2,1)S(1)}, u32[]{:S(2)}, u32[]{:S(2)}) collective-permute-start(bf16[64,512]{1,0:T(8,128)(2,1)S(1)} %shard_map.171.refs_8_), channel_id=1, source_target_pairs={{0,12},{4,8},{8,4},{12,0},{1,13},{5,9},{9,5},{13,1},{2,14},{6,10},... | collective-permute-start | bytes 196616 | tf_op jit(solution)/shard_map/ppermute | solution.py:404
  38.7 5.7 %collective-permute-start.20 = (bf16[64,512]{1,0:T(8,128)(2,1)S(1)}, bf16[64,512]{1,0:T(8,128)(2,1)S(1)}, u32[]{:S(2)}, u32[]{:S(2)}) collective-permute-start(bf16[64,512]{1,0:T(8,128)(2,1)S(1)} %shard_map.171.refs_8_), channel_id=1, source_target_pairs={{0,4},{4,0},{8,12},{12,8},{1,5},{5,1},{9,13},{13,9},{2,6},{6,2},{1... | collective-permute-start | bytes 196616 | tf_op jit(solution)/shard_map/ppermute | solution.py:404
  38.7 7.8 %collective-permute-start.11 = (bf16[128,256]{1,0:T(8,128)(2,1)S(1)}, bf16[128,256]{1,0:T(8,128)(2,1)S(1)}, u32[]{:S(2)}, u32[]{:S(2)}) collective-permute-start(bf16[128,256]{1,0:T(8,128)(2,1)S(1)} %get-tuple-element.79.refs_0_), channel_id=1, source_target_pairs={{0,4},{4,0},{8,12},{12,8},{1,5},{5,1},{9,13},{13,9},{2,6},{6,2},{1... | collective-permute-start | bytes 196616 | tf_op jit(solution)/shard_map/ppermute | solution.py:404
  41.4 5.3 %collective-permute-start.13 = (bf16[128,256]{1,0:T(8,128)(2,1)S(1)}, bf16[128,256]{1,0:T(8,128)(2,1)S(1)}, u32[]{:S(2)}, u32[]{:S(2)}) collective-permute-start(bf16[128,256]{1,0:T(8,128)(2,1)S(1)} %collective-permute-done.12.refs_3_), channel_id=1, source_target_pairs={{0,4},{4,0},{8,12},{12,8},{1,5},{5,1},{9,13},{13,9},{2,6},{6,2},{1... | collective-permute-start | bytes 196616 | tf_op jit(solution)/shard_map/ppermute | solution.py:404
  44.0 5.2 %collective-permute-start.22 = (bf16[64,512]{1,0:T(8,128)(2,1)S(1)}, bf16[64,512]{1,0:T(8,128)(2,1)S(1)}, u32[]{:S(2)}, u32[]{:S(2)}) collective-permute-start(bf16[64,512]{1,0:T(8,128)(2,1)S(1)} %collective-permute-done.21.refs_11_), channel_id=1, source_target_pairs={{0,4},{4,0},{8,12},{12,8},{1,5},{5,1},{9,13},{13,9},{2,6},{6,2},{1... | collective-permute-start | bytes 196616 | tf_op jit(solution)/shard_map/ppermute | solution.py:404
  44.4 4.8 %collective-permute-start.14 = (bf16[128,256]{1,0:T(8,128)(2,1)S(1)}, bf16[128,256]{1,0:T(8,128)(2,1)S(1)}, u32[]{:S(2)}, u32[]{:S(2)}) collective-permute-start(bf16[128,256]{1,0:T(8,128)(2,1)S(1)} %get-tuple-element.79.refs_0_), channel_id=1, source_target_pairs={{0,2},{2,0},{1,3},{3,1},{4,6},{6,4},{5,7},{7,5},{8,10},{10,8},{9,1... | collective-permute-start | bytes 196616 | tf_op jit(solution)/shard_map/ppermute | solution.py:404
  44.7 5.0 %collective-permute-start.17 = (bf16[128,256]{1,0:T(8,128)(2,1)S(1)}, bf16[128,256]{1,0:T(8,128)(2,1)S(1)}, u32[]{:S(2)}, u32[]{:S(2)}) collective-permute-start(bf16[128,256]{1,0:T(8,128)(2,1)S(1)} %collective-permute-done.12.refs_3_), channel_id=1, source_target_pairs={{0,2},{2,0},{1,3},{3,1},{4,6},{6,4},{5,7},{7,5},{8,10},{10,8},{9,1... | collective-permute-start | bytes 196616 | tf_op jit(solution)/shard_map/ppermute | solution.py:404
  46.4 4.3 %collective-permute-start.15 = (bf16[128,256]{1,0:T(8,128)(2,1)S(1)}, bf16[128,256]{1,0:T(8,128)(2,1)S(1)}, u32[]{:S(2)}, u32[]{:S(2)}) collective-permute-start(bf16[128,256]{1,0:T(8,128)(2,1)S(1)} %collective-permute-done.11.refs_1_), channel_id=1, source_target_pairs={{0,2},{2,0},{1,3},{3,1},{4,6},{6,4},{5,7},{7,5},{8,10},{10,8},{9,1... | collective-permute-start | bytes 196616 | tf_op jit(solution)/shard_map/ppermute | solution.py:404
  46.8 4.6 %collective-permute-start.16 = (bf16[128,256]{1,0:T(8,128)(2,1)S(1)}, bf16[128,256]{1,0:T(8,128)(2,1)S(1)}, u32[]{:S(2)}, u32[]{:S(2)}) collective-permute-start(bf16[128,256]{1,0:T(8,128)(2,1)S(1)} %collective-permute-done.13.refs_2_), channel_id=1, source_target_pairs={{0,2},{2,0},{1,3},{3,1},{4,6},{6,4},{5,7},{7,5},{8,10},{10,8},{9,1... | collective-permute-start | bytes 196616 | tf_op jit(solution)/shard_map/ppermute | solution.py:404

commit v5 on v3

--- a/solution.py
+++ b/solution.py
@@ -10,6 +10,7 @@
 BLOCK = 128
 EPSILON = 1e-05
 TAIL = 16
+N_FETCHED = 9
 VMEM_LIMIT = 24 * 1024 * 1024
 
 f32 = jnp.float32
@@ -82,21 +83,17 @@
         out_refs[3][...] = pieces[3]
 
 
-def local_kernel(
-    count_ref, node_ref, src_hbm, dst_hbm, bias_hbm, w_src_hbm, w_dst_hbm, w_out_hbm, gain_hbm, cot_hbm,
-    pre_ref, pick_ref, collect_ref, spread_ref, scatter_ref,
-    w_src_ref, w_dst_ref, w_out_ref, gain_ref, cot_ref,
-    src_ref, dst_ref, bias_ref, sems,
-):
-    copies = fetch(
-        sems, (src_hbm, src_ref), (dst_hbm, dst_ref), (bias_hbm, bias_ref), (w_src_hbm, w_src_ref),
-        (w_dst_hbm, w_dst_ref), (w_out_hbm, w_out_ref), (gain_hbm, gain_ref), (cot_hbm, cot_ref),
-    )
+def local_kernel(*refs):
+    node_ref, ins, refs = refs[0], refs[1 : 1 + N_FETCHED], refs[1 + N_FETCHED :]
+    pre_ref, pick_ref, collect_ref, spread_ref, scatter_ref, *refs = refs
+    w_src_ref, w_dst_ref, w_out_ref, gain_ref, cot_ref, count_ref, src_ref, dst_ref, bias_ref, sems = refs
+    outs = (src_ref, dst_ref, count_ref, bias_ref, w_src_ref, w_dst_ref, w_out_ref, gain_ref, cot_ref)
+    copies = fetch(sems, *zip(ins, outs))
     node = node_ref[...]
     rows = node.shape[0]
     edges = src_ref.shape[1]
-    copies[0].wait()
-    copies[1].wait()
+    for copy in copies[:3]:
+        copy.wait()
     scatter_ref[...] = one_hot(iota(scatter_ref.shape, 0) == src_ref[...])
     used = usable_row(count_ref, edges) > 0
     collect_ref[...] = one_hot((iota((rows, edges), 0) == dst_ref[...]) & used)
@@ -108,13 +105,10 @@
     pick_ref[...] = one_hot(source == lane + rows)
     spread_ref[...] = one_hot((target == lane) & used)
     both = jnp.concatenate([dot(near, node), dot(one_hot(target == lane), node)], axis=1).astype(bf16)
-    copies[2].wait()
-    copies[3].wait()
-    copies[4].wait()
+    for copy in copies[3:]:
+        copy.wait()
     weights = jnp.concatenate([w_src_ref[...], w_dst_ref[...]], axis=0)
     pre_ref[...] = dot(both, weights) + bias_ref[...]
-    for copy in copies[5:]:
-        copy.wait()
 
 
 def twice(x):
@@ -146,9 +140,9 @@
     *rest,
 ):
     peers, chunk, n_halo, paired = geometry
-    *rest, out_scratch, back_scratch = rest
+    *rest, out_scratch, back_scratch, pair_scratch = rest
     halo_refs = rest[:n_halo]
-    updated_ref, local_ref, target_ref, *message_refs = rest[n_halo:]
+    normed_ref, local_ref, target_ref, *message_refs = rest[n_halo:]
     node = node_ref[...]
     rows, width = node.shape
     aggregate = own_ref[...].astype(f32) + other_ref[...].astype(f32)
@@ -165,7 +159,7 @@
         - normed * jnp.mean(scaled * normed, axis=1, keepdims=True)
     )
     agg_grad = agg_grad.astype(bf16)
-    updated_ref[...] = (node.astype(f32) + gain * normed).astype(bf16)
+    normed_ref[...] = normed
     gain_part = jnp.sum(upstream * normed, axis=0, keepdims=True)
 
     act_grad = dot(twice(spread_ref[...]), stacked(dot(agg_grad, w_out_ref[...], NT)))
@@ -189,24 +183,22 @@
     back = by_source_low[rows:]
 
     if paired:
-        send_ref, keep_ref, *out_refs = message_refs
+        far_send_ref, far_keep_ref, near_send_ref, near_keep_ref, *out_refs = message_refs
         sub = lax.axis_index("sub")
         mesh = lax.axis_index("mesh")
-
-        @pl.when(sub == 0)
-        def _():
-            send_ref[0:width, :] = dst_part
-            keep_ref[0:width, :] = src_part
-
-        @pl.when(sub == 1)
-        def _():
-            send_ref[0:width, :] = src_part
-            keep_ref[0:width, :] = dst_part
-
+        lines = len(out_refs)
         halo = back.shape[0] // 4
-        send_ref[width : width + TAIL, :] = tail
-        keep_ref[width:, :] = tail
-        send_ref[width + TAIL :, :] = back[2 * halo :]
+        first = sub == 0
+        pair_scratch[0] = jnp.where(first, dst_part, src_part)
+        pair_scratch[1] = jnp.where(first, src_part, dst_part)
+        strip = width // lines
+        for slot, far_ref, near_ref in ((0, far_send_ref, near_send_ref), (1, far_keep_ref, near_keep_ref)):
+            for at, k in enumerate((3, 2, 1, 0)):
+                start = pl.multiple_of((mesh ^ k) * strip, strip)
+                ref = far_ref if at < 2 else near_ref
+                ref[at % 2 * strip : (at % 2 + 1) * strip, :] = pair_scratch[slot, pl.ds(start, strip), :]
+            far_ref[2 * strip : 2 * strip + TAIL, :] = tail
+        far_send_ref[2 * strip + TAIL :, :] = back[2 * halo :]
         back_scratch[...] = back[: 2 * halo]
         out_scratch[...] = out_part
         strip = hid // len(out_refs)
@@ -262,42 +254,46 @@
     return terms[0]
 
 
-def turn_kernel(count, *refs):
-    out_terms = refs[count - 1 :: -1]
-    arrived_ref, keep_ref, *refs = refs[count:]
-    refs = [None] * count + refs
-    line_refs = refs[count : 2 * count]
-    out_send_ref, out_keep_ref, scratch = refs[2 * count :]
-    sub = lax.axis_index("sub")
-    mesh = lax.axis_index("mesh")
-    full, hid = keep_ref.shape
+def far_kernel(arrived_ref, keep_ref, three_ref, two_ref, tail_ref):
+    full = keep_ref.shape[0]
     total = keep_ref[...].astype(f32) + arrived_ref[0:full, :].astype(f32)
-    rows = full - TAIL
-    strip = rows // count
-    tail = total[rows:]
+    strip = three_ref.shape[0] - TAIL
+    tail = total[2 * strip :]
     tail = tail_of([tail[at : at + 1] + tail[at + 1 : at + 2] for at in range(0, 6, 2)])
-    scratch[...] = total[:rows].astype(bf16)
-    for k, ref in enumerate(line_refs):
-        start = pl.multiple_of((mesh ^ k) * strip, strip)
-        ref[0:strip, :] = scratch[pl.ds(start, strip), :]
+    for k, ref in enumerate((three_ref, two_ref)):
+        ref[0:strip, :] = total[k * strip : (k + 1) * strip].astype(bf16)
         ref[strip:, :] = tail
-    out_strip = out_keep_ref.shape[0]
-    out = tree([r[0:out_strip, :].astype(f32) for r in out_terms])
-    left, right = out[:, :hid], out[:, hid:]
-    out_send_ref[...] = jnp.where(sub == 0, right, left).astype(bf16)
-    out_keep_ref[...] = jnp.where(sub == 0, left, right).astype(bf16)
-
-
-def own_kernel(count, *refs):
-    line_refs = refs[count - 1 :: -1]
-    out_keep_ref, out_arrived_ref, own_ref, bias_ref, gain_ref = refs[count:]
-    total = tree([r[...].astype(f32) for r in line_refs])
+    tail_ref[...] = tail
+
+
+def near_kernel(arrived_ref, keep_ref, tail_ref, one_ref, zero_ref):
+    full = keep_ref.shape[0]
+    total = (keep_ref[...].astype(f32) + arrived_ref[...].astype(f32)).astype(bf16)
+    strip = full // 2
+    for k, ref in enumerate((one_ref, zero_ref)):
+        ref[0:strip, :] = total[k * strip : (k + 1) * strip]
+        ref[strip:, :] = tail_ref[...]
+
+
+def line_kernel(*refs):
+    *terms, _, send_ref, keep_ref = refs
+    rows, hid = send_ref.shape
+    total = tree([r[0:rows, :].astype(f32) for r in terms])
+    first = lax.axis_index("sub") == 0
+    left, right = total[:, :hid], total[:, hid:]
+    send_ref[...] = jnp.where(first, right, left).astype(bf16)
+    keep_ref[...] = jnp.where(first, left, right).astype(bf16)
+
+
+def own_kernel(*refs):
+    *terms, out_keep_ref, out_arrived_ref, _, own_ref, tail_ref = refs
+    total = tree([r[...].astype(f32) for r in terms])
     strip = own_ref.shape[0] - out_keep_ref.shape[0]
     own_ref[0:strip, :] = total[:strip].astype(bf16)
     own_ref[strip:, :] = (
         out_keep_ref[...].astype(f32) + out_arrived_ref[...].astype(f32)
     ).astype(bf16)
-    write_vectors(total[strip:], bias_ref, gain_ref)
+    tail_ref[...] = total[strip:]
 
 
 def write_vectors(tail, bias_ref, gain_ref):
@@ -307,24 +303,34 @@
         gain_ref[:, k * hid : (k + 1) * hid] = tail[2 + 2 * k : 3 + 2 * k] + tail[3 + 2 * k : 4 + 2 * k]
 
 
-def place_kernel(count, *refs):
+def place_kernel(count, tail_ref, *refs):
     mine, theirs = refs[:count], refs[count : 2 * count]
-    src_ref, dst_ref, out_ref = refs[2 * count :]
+    src_hbm, dst_hbm, out_hbm, bias_ref, gain_ref, src_ref, dst_ref, out_ref, sems = refs[2 * count :]
     first = lax.axis_index("sub") == 0
     mesh = lax.axis_index("mesh")
-    width, hid = src_ref.shape
-    strip = width // count
-    narrow = hid // count
+    strip, hid = src_ref.shape[1:]
+    narrow = out_ref.shape[1]
+    copies = []
+
+    def put(ref, hbm, k, rows):
+        start = pl.multiple_of((mesh ^ k) * rows, rows)
+        copies.append(pltpu.make_async_copy(ref.at[k], hbm.at[pl.ds(start, rows)], sems.at[len(copies)]))
+        copies[-1].start()
+
     for k in range(count):
         a, b = mine[k][...], theirs[k][...]
         low = jnp.where(first, a, b).astype(f32)
         high = jnp.where(first, b, a).astype(f32)
-        start = pl.multiple_of((mesh ^ k) * strip, strip)
-        src_ref[pl.ds(start, strip), :] = low[:strip]
-        dst_ref[pl.ds(start, strip), :] = high[:strip]
-        start = pl.multiple_of((mesh ^ k) * narrow, narrow)
-        out_ref[pl.ds(start, narrow), 0:hid] = low[strip:]
-        out_ref[pl.ds(start, narrow), hid:] = high[strip:]
+        src_ref[k] = low[:strip]
+        put(src_ref, src_hbm, k, strip)
+        dst_ref[k] = high[:strip]
+        put(dst_ref, dst_hbm, k, strip)
+        out_ref[k, :, 0:hid] = low[strip:]
+        out_ref[k, :, hid:] = high[strip:]
+        put(out_ref, out_hbm, k, narrow)
+    write_vectors(tail_ref[...], bias_ref, gain_ref)
+    for copy in copies:
+        copy.wait()
 
 
 def sum_kernel(chunk, arrived_ref, out_ref, bias_ref, gain_ref):
@@ -382,10 +388,11 @@
     node_part(send_ref, local_ref, target_ref, w_src_ref, w_dst_ref, returned, out_ref)
 
 
-def finish_kernel(cot_ref, own_ref, other_ref, out_ref):
-    out_ref[...] = cot_ref[...].astype(f32) + (
+def finish_kernel(cot_ref, node_ref, gain_ref, normed_ref, own_ref, other_ref, grad_ref, updated_ref):
+    grad_ref[...] = cot_ref[...].astype(f32) + (
         own_ref[...].astype(f32) + other_ref[...].astype(f32)
     )
+    updated_ref[...] = (node_ref[...].astype(f32) + gain_ref[...] * normed_ref[...]).astype(bf16)
 
 
 VMEM = pl.BlockSpec(memory_space=pltpu.VMEM)
@@ -397,12 +404,12 @@
     return jax.ShapeDtypeStruct(dims, dtype)
 
 
-def call(kernel, outs, *args, specs=None, flops=10**8, scratch=()):
+def call(kernel, outs, *args, specs=None, out_specs=None, flops=10**8, scratch=()):
     return pl.pallas_call(
         kernel,
         out_shape=outs,
         in_specs=specs or [VMEM] * len(args),
-        out_specs=jax.tree.map(lambda _: VMEM, outs),
+        out_specs=out_specs or jax.tree.map(lambda _: VMEM, outs),
         scratch_shapes=scratch,
         compiler_params=pltpu.CompilerParams(vmem_limit_bytes=VMEM_LIMIT),
         cost_estimate=pl.CostEstimate(flops=flops, bytes_accessed=10**6, transcendentals=0),
@@ -419,32 +426,48 @@
     return lax.ppermute(x, axis, [(i, i ^ k) for i in range(count)])
 
 
-def paired_sums(messages, lines, strip, narrow, width, hid):
-    send, keep, *outs = messages
+def paired_sums(messages, lines, strip, narrow, width, hid, node_terms):
+    far_send, far_keep, near_send, near_keep, *outs = messages
     order = range(lines - 1, 0, -1)
+    block = shape((strip + TAIL, hid), bf16)
+    far = across(far_send, "sub", 1)
     out_terms = {k: across(outs[k], "mesh", k) for k in order}
-    arrived = across(send, "sub", 1)
-    *line, out_send, out_keep = call(
-        functools.partial(turn_kernel, lines),
-        [shape((strip + TAIL, hid), bf16)] * lines + [shape((narrow, hid), bf16)] * 2,
-        *[out_terms[k] for k in order], outs[0], arrived, keep,
-        scratch=[pltpu.VMEM((width, hid), bf16)],
-    )
+    near = across(near_send, "sub", 1)
+    line = {}
+    line[3], line[2], tail = call(far_kernel, [block, block, shape((TAIL, hid), bf16)], far, far_keep)
+    line[1], line[0] = call(near_kernel, [block, block], near, near_keep, tail)
     line_terms = {k: across(line[k], "mesh", k) for k in order}
-    own, bias_grad, gain_grad = call(
-        functools.partial(own_kernel, lines),
-        [shape((strip + narrow, hid), bf16), shape((1, hid), f32), shape((1, width), f32)],
+    out_send, out_keep = call(
+        line_kernel,
+        [shape((narrow, hid), bf16)] * 2,
+        *[out_terms[k] for k in order], outs[0], line_terms[3],
+    )
+    node_part = node_terms(out_terms[3], out_terms[1], far)
+    own, tail = call(
+        own_kernel,
+        [shape((strip + narrow, hid), bf16), shape((TAIL, hid), f32)],
         *[line_terms[k] for k in order], line[0], out_keep, across(out_send, "sub", 1),
+        node_part,
     )
     mine = {k: across(own, "mesh", k) for k in order}
     mine[0] = own
-    theirs = {k: across(mine[k], "sub", 1) for k in mine}
+    theirs = {k: across(mine[k], "sub", 1) for k in (0, 1, 3, 2)}
     grads = call(
         functools.partial(place_kernel, lines),
-        [shape((width, hid), f32), shape((width, hid), f32), shape((hid, width), f32)],
-        *[mine[k] for k in range(lines)], *[theirs[k] for k in range(lines)],
-    )
-    return (*grads, bias_grad, gain_grad), (out_terms[3], out_terms[1], arrived)
+        [
+            shape((width, hid), f32), shape((width, hid), f32), shape((hid, width), f32),
+            shape((1, hid), f32), shape((1, width), f32),
+        ],
+        tail, *[mine[k] for k in range(lines)], *[theirs[k] for k in range(lines)],
+        out_specs=[HBM] * 3 + [VMEM] * 2,
+        scratch=[
+            pltpu.VMEM((lines, strip, hid), f32),
+            pltpu.VMEM((lines, strip, hid), f32),
+            pltpu.VMEM((lines, narrow, width), f32),
+            pltpu.SemaphoreType.DMA((3 * lines,)),
+        ],
+    )
+    return grads, node_part
 
 
 def shards(
@@ -473,16 +496,23 @@
     routes = [("mesh", 1), ("mesh", -1), ("sub", 1)] + ([] if merged else [("sub", -1)])
     n_halo = len(piece)
 
+    def in_hbm(x):
+        return pltpu.with_memory_space_constraint(x, pltpu.HBM)
+
     node, send, *outgoing = call(
         send_kernel,
         [shape((rows, width), bf16), shape(send_rows.shape, jnp.int32)]
         + [shape((n, width), bf16) for n in piece],
-        node_state, send_rows,
+        in_hbm(node_state), in_hbm(send_rows),
         specs=[HBM, HBM],
         scratch=[pltpu.SemaphoreType.DMA((2,))],
     )
     arrived = [shifted(x, axis, by) for x, (axis, by) in zip(outgoing, routes)]
 
+    fetched = [
+        edge_src.reshape(1, edges), edge_dst.reshape(1, edges), block_count,
+        hidden_bias.reshape(1, hid), w_src, w_dst, w_out, norm_gain.reshape(1, width), cotangent,
+    ]
     pre, pick, collect, spread, scatter, w_src, w_dst, w_out, gain, cot = call(
         local_kernel,
         [
@@ -491,20 +521,16 @@
             shape((rows, edges), bf16),
             shape((edges, rows), bf16),
             shape((rows + 4 * halo, edges), bf16),
-            shape(w_src.shape, bf16),
-            shape(w_dst.shape, bf16),
-            shape(w_out.shape, bf16),
-            shape((1, width), f32),
-            shape((rows, width), bf16),
-        ],
-        block_count, node, edge_src.reshape(1, edges), edge_dst.reshape(1, edges),
-        hidden_bias.reshape(1, hid), w_src, w_dst, w_out, norm_gain.reshape(1, width), cotangent,
-        specs=[SMEM, VMEM] + [HBM] * 8,
+        ]
+        + [shape(x.shape, x.dtype) for x in fetched[4:]],
+        node, *[in_hbm(x) for x in fetched],
+        specs=[VMEM] + [HBM] * len(fetched),
         scratch=[
+            pltpu.SMEM(block_count.shape, jnp.int32),
             pltpu.VMEM((1, edges), jnp.int32),
             pltpu.VMEM((1, edges), jnp.int32),
             pltpu.VMEM((1, hid), f32),
-            pltpu.SemaphoreType.DMA((8,)),
+            pltpu.SemaphoreType.DMA((N_FETCHED,)),
         ],
     )
 
@@ -520,25 +546,39 @@
     if paired:
         strip = width // lines
         narrow = hid // lines
-        message_shapes = [shape((width + TAIL + 2 * halo, hid), bf16), shape((width + TAIL, hid), bf16)]
+        message_shapes = [shape((2 * strip + TAIL + 2 * halo, hid), bf16), shape((2 * strip + TAIL, hid), bf16)]
+        message_shapes += [shape((2 * strip, hid), bf16)] * 2
         message_shapes += [shape((narrow + k % 2 * (halo // 2), width), bf16) for k in range(lines)]
     else:
         message_shapes = [shape((peers, chunk + TAIL, hid), bf16)]
         message_shapes += [shape((n, hid), bf16) for n in piece]
-    updated, local, target, *messages = call(
+    normed, local, target, *messages = call(
         functools.partial(backward_kernel, (peers, chunk, n_halo, paired)),
-        [shape((rows, width), bf16), shape((rows, hid), f32), shape((rows, hid), bf16)]
+        [shape((rows, width), f32), shape((rows, hid), f32), shape((rows, hid), bf16)]
         + message_shapes,
         node, collect, spread, scatter, w_out, gain, cot, factor, hidden, partial, other, *arrived,
-        scratch=[pltpu.VMEM((hid, width), bf16), pltpu.VMEM((2 * halo, hid), bf16)],
-    )
+        scratch=[
+            pltpu.VMEM((hid, width), bf16),
+            pltpu.VMEM((2 * halo, hid), bf16),
+            pltpu.VMEM((2, width, hid), bf16),
+        ],
+    )
+
+    def node_terms(*returned):
+        return call(
+            paired_node_kernel if paired else node_kernel,
+            shape((rows, width), bf16),
+            send, local, target, w_src, w_dst, *returned,
+        )
 
     if paired:
-        (src_grad, dst_grad, out_grad, bias_grad, gain_grad), returned = paired_sums(
-            messages, lines, strip, narrow, width, hid
+        (src_grad, dst_grad, out_grad, bias_grad, gain_grad), node_part = paired_sums(
+            messages, lines, strip, narrow, width, hid, node_terms
         )
     else:
-        returned = [shifted(x, axis, -by) for x, (axis, by) in zip(messages[1:], routes)]
+        node_part = node_terms(
+            *[shifted(x, axis, -by) for x, (axis, by) in zip(messages[1:], routes)]
+        )
         exchanged = lax.all_to_all(messages[0], ("mesh", "sub"), 0, 0)
         reduced, bias_grad, gain_grad = call(
             functools.partial(sum_kernel, chunk),
@@ -551,13 +591,10 @@
             [shape((width, hid), f32), shape((width, hid), f32), shape((hid, width), f32)],
             gathered.reshape(peers * chunk, hid),
         )
-    node_part = call(
-        paired_node_kernel if paired else node_kernel,
-        shape((rows, width), bf16),
-        send, local, target, w_src, w_dst, *returned,
-    )
-    node_grad = call(
-        finish_kernel, shape((rows, width), f32), cot, node_part, shifted(node_part, "lat", 1)
+    node_grad, updated = call(
+        finish_kernel,
+        [shape((rows, width), f32), shape((rows, width), bf16)],
+        cot, node, gain, normed, node_part, shifted(node_part, "lat", 1),
     )
     return (
         updated, node_grad, src_grad, dst_grad, out_grad,

time: 58 us -> 53 us (0.914)
  local copies, waits for them, and re-layouts: 5.13 us -> 0 us
  starting transfers between devices: 27.6 us -> 28.4 us
  waiting for transfers between devices: 15.8 us -> 15.1 us
    unnamed x22 -> x0, local copies, waits for them, and re-layouts: 5.13 us -> none
    ppermute x15 -> x16, starting transfers between devices: 20.6 us -> 21.5 us  [across(): return lax.ppermute(x, axis, [(i, i ^ k) for i in range(count)])]
    ppermute x15 -> x16, waiting for transfers between devices: 14.5 us -> 13.7 us  [across(): return lax.ppermute(x, axis, [(i, i ^ k) for i in range(count)])]
    pallas_call x9 -> x11, Pallas kernels: 8.51 us -> 8.65 us  [call(): pl.pallas_call(kernel, out_shape=outs, in_specs=specs or [VMEM] * len(arg...]
  transfers between devices with their start and end apart: 20 -> 21, of which waited for: 9 -> 9; matrix products, arithmetic and copies ran while one was open for 0% -> 0% of each run, Pallas kernels for 6% -> 6%
where the time goes in v5:
time: 53 us; the launch traced here: 52.8 us
  starting transfers between devices  28.4 us (54%)
  waiting for transfers between devices  15.1 us (28%)
  Pallas kernels  8.65 us (16%)
  between operations  0.72 us (1%)
    ppermute x16, starting transfers between devices, across(): return lax.ppermute(x, axis, [(i, i ^ k) for i in range(count)])  21.5 us
    ppermute x16, waiting for transfers between devices, across(): return lax.ppermute(x, axis, [(i, i ^ k) for i in range(count)])  13.7 us
    pallas_call x11, Pallas kernels, call(): pl.pallas_call(kernel, out_shape=outs, in_specs=specs or [VMEM] * len(arg...  8.65 us
    ppermute x5, starting transfers between devices, shifted(): return lax.ppermute(x, axis, [(i, (i + by) % count) for i in range(count)])  6.9 us
    ppermute x5, waiting for transfers between devices, shifted(): return lax.ppermute(x, axis, [(i, (i + by) % count) for i in range(count)])  1.38 us
  transfers between devices with their start and end apart: 21, of which 9 were waited for; matrix products, arithmetic and copies ran while one was open for 0% of the time, Pallas kernels for 6%

profile of v5, /device:TPU:0, one launch (start us, length us, event | category | flops | bytes accessed | tf_op | source)
XLA Modules:
  0.0 52.8 jit_solution(15097757873244895820)
XLA Ops:
  0.6 1.2 %shard_map.162 = (bf16[128,512]{1,0:T(8,128)(2,1)S(1)}, s32[1,4,32]{2,1,0:T(4,128)S(1)}, bf16[32,512]{1,0:T(8,128)(2,1)S(1)}, bf16[32,512]{1,0:T(8,128)(2,1)S(1)}, bf16[64,512]{1,0:T(8,128)(2,1)S(1)}) custom-call(bf16[128,512]{1,0:T(8,128)(2,1)} %node_hbm.1, s32[1,4,32]{2,1,0:T(4,128)} %send_hbm.1), custom_call_target="tpu_custom_call" | custom-call | flops 100000000 | bytes 1000000 | tf_op jit(solution)/shard_map/pallas_call | solution.py:408
  1.8 3.0 %collective-permute-start.2 = (bf16[64,512]{1,0:T(8,128)(2,1)S(1)}, bf16[64,512]{1,0:T(8,128)(2,1)S(1)}, u32[]{:S(2)}, u32[]{:S(2)}) collective-permute-start(bf16[64,512]{1,0:T(8,128)(2,1)S(1)} %get-tuple-element.64), channel_id=1, source_target_pairs={{0,2},{2,0},{1,3},{3,1},{4,6},{6,4},{5,7},{7,5},{8,10},{10,8},{9,1... | collective-permute-start | bytes 196616 | tf_op jit(solution)/shard_map/ppermute | solution.py:421
  4.8 1.6 %collective-permute-start = (bf16[32,512]{1,0:T(8,128)(2,1)S(1)}, bf16[32,512]{1,0:T(8,128)(2,1)S(1)}, u32[]{:S(2)}, u32[]{:S(2)}) collective-permute-start(bf16[32,512]{1,0:T(8,128)(2,1)S(1)} %get-tuple-element.62), channel_id=1, source_target_pairs={{0,4},{4,8},{8,12},{12,0},{1,5},{5,9},{9,13},{13,1},{2,6},{6,10},{... | collective-permute-start | bytes 98312 | tf_op jit(solution)/shard_map/ppermute | solution.py:421
  6.4 2.2 %collective-permute-start.1 = (bf16[32,512]{1,0:T(8,128)(2,1)S(1)}, bf16[32,512]{1,0:T(8,128)(2,1)S(1)}, u32[]{:S(2)}, u32[]{:S(2)}) collective-permute-start(bf16[32,512]{1,0:T(8,128)(2,1)S(1)} %get-tuple-element.63), channel_id=1, source_target_pairs={{0,12},{4,0},{8,4},{12,8},{1,13},{5,1},{9,5},{13,9},{2,14},{6,2},{... | collective-permute-start | bytes 98312 | tf_op jit(solution)/shard_map/ppermute | solution.py:421
  8.6 2.1 %shard_map.163 = (f32[512,256]{1,0:T(8,128)S(1)}, bf16[512,128]{1,0:T(8,128)(2,1)S(1)}, bf16[128,512]{1,0:T(8,128)(2,1)S(1)}, bf16[512,128]{1,0:T(8,128)(2,1)S(1...) custom-call(bf16[128,512]{1,0:T(8,128)(2,1)S(1)} %get-tuple-element., ...), custom_call_target="tpu_custom_call" | custom-call | flops 100000000 | bytes 1000000 | tf_op jit(solution)/shard_map/pallas_call | solution.py:408
  10.7 0.0 collective-permute-done.rest_0_
  10.8 0.0 collective-permute-done.1.rest_1_
  10.8 0.0 collective-permute-done.2.rest_2_
  10.8 0.9 %shard_map.164 = (f32[512,256]{1,0:T(8,128)S(1)}, bf16[128,256]{1,0:T(8,128)(2,1)S(1)}, bf16[128,512]{1,0:T(8,128)(2,1)S(1)}) custom-call(f32[512,256]{1,0:T(8,128)S(1)} %get-tuple-element.59.pre_ref, bf16[512,128]{1,0:T(8,128)(2,1)S(1)} %get-tuple-element.60.pick_ref, bf16[128,512]{1,0:T(8,128)(2,1)S(1)} %get-tuple-element.55.collect_ref, ...), custom_call_target="tpu_custom_call" | custom-call | flops 100000000 | bytes 1000000 | tf_op jit(solution)/shard_map/pallas_call | solution.py:408
  11.6 0.1 collective-permute-start.3
  11.7 1.3 %collective-permute-done.3.other_ref = bf16[128,512]{1,0:T(8,128)(2,1)S(1)} collective-permute-done((bf16[128,512]{1,0:T(8,128)(2,1)S(1)}, bf16[128,512]{1,0:T(8,128)(2,1)S(1)}, u32[]{:S(2)}, u32[]{:S(2)}) %collective-permute-start.3) | collective-permute-done | bytes 131104 | tf_op jit(solution)/shard_map/ppermute | solution.py:421
  13.1 1.4 %shard_map.165 = (f32[128,512]{1,0:T(8,128)S(1)}, f32[128,256]{1,0:T(8,128)S(1)}, bf16[128,256]{1,0:T(8,128)(2,1)S(1)}, bf16[336,256]{1,0:T(8,128)(2,1)S(1)}, bf...) custom-call(bf16[128,512]{1,0:T(8,128)(2,1)S(1)} %get-tuple-element., ...), custom_call_target="tpu_custom_call" | custom-call | flops 100000000 | bytes 1000000 | tf_op jit(solution)/shard_map/pallas_call | solution.py:408
  14.4 0.5 collective-permute-start.6
  14.9 1.6 %collective-permute-start.10 = (bf16[256,256]{1,0:T(8,128)(2,1)S(1)}, bf16[256,256]{1,0:T(8,128)(2,1)S(1)}, u32[]{:S(2)}, u32[]{:S(2)}) collective-permute-start(bf16[256,256]{1,0:T(8,128)(2,1)S(1)} %get-tuple-element.81), channel_id=1, source_target_pairs={{0,2},{2,0},{1,3},{3,1},{4,6},{6,4},{5,7},{7,5},{8,10},{10,8},{9,1... | collective-permute-start | bytes 393224 | tf_op jit(solution)/shard_map/ppermute | solution.py:426
  16.5 2.1 %collective-permute-start.12 = (bf16[64,512]{1,0:T(8,128)(2,1)S(1)}, bf16[64,512]{1,0:T(8,128)(2,1)S(1)}, u32[]{:S(2)}, u32[]{:S(2)}) collective-permute-start(bf16[64,512]{1,0:T(8,128)(2,1)S(1)} %get-tuple-element.86), channel_id=1, source_target_pairs={{0,8},{4,12},{8,0},{12,4},{1,9},{5,13},{9,1},{13,5},{2,10},{6,14},... | collective-permute-start | bytes 196616 | tf_op jit(solution)/shard_map/ppermute | solution.py:426
  18.7 1.5 %collective-permute-start.4 = (bf16[80,512]{1,0:T(8,128)(2,1)S(1)}, bf16[80,512]{1,0:T(8,128)(2,1)S(1)}, u32[]{:S(2)}, u32[]{:S(2)}) collective-permute-start(bf16[80,512]{1,0:T(8,128)(2,1)S(1)} %get-tuple-element.73), channel_id=1, source_target_pairs={{0,12},{4,8},{8,4},{12,0},{1,13},{5,9},{9,5},{13,1},{2,14},{6,10},... | collective-permute-start | bytes 245768 | tf_op jit(solution)/shard_map/ppermute | solution.py:426
  20.1 0.6 %collective-permute-start.5 = (bf16[80,512]{1,0:T(8,128)(2,1)S(1)}, bf16[80,512]{1,0:T(8,128)(2,1)S(1)}, u32[]{:S(2)}, u32[]{:S(2)}) collective-permute-start(bf16[80,512]{1,0:T(8,128)(2,1)S(1)} %get-tuple-element.74), channel_id=1, source_target_pairs={{0,4},{4,0},{8,12},{12,8},{1,5},{5,1},{9,13},{13,9},{2,6},{6,2},{1... | collective-permute-start | bytes 245768 | tf_op jit(solution)/shard_map/ppermute | solution.py:426
  20.7 1.0 %collective-permute-done.6.pair_ref.arrived_ref = bf16[336,256]{1,0:T(8,128)(2,1)S(1)} collective-permute-done((bf16[336,256]{1,0:T(8,128)(2,1)S(1)}, bf16[336,256]{1,0:T(8,128)(2,1)S(1)}, u32[]{:S(2)}, u32[]{:S(2)}) %collective-permute-start.6) | collective-permute-done | bytes 172064 | tf_op jit(solution)/shard_map/ppermute | solution.py:426
  21.8 3.7 %collective-permute-start.8 = (bf16[144,256]{1,0:T(8,128)(2,1)S(1)}, bf16[144,256]{1,0:T(8,128)(2,1)S(1)}, u32[]{:S(2)}, u32[]{:S(2)}) collective-permute-start(bf16[144,256]{1,0:T(8,128)(2,1)S(1)} %get-tuple-element.79), channel_id=1, source_target_pairs={{0,12},{4,8},{8,4},{12,0},{1,13},{5,9},{9,5},{13,1},{2,14},{6,10},... | collective-permute-start | bytes 221192 | tf_op jit(solution)/shard_map/ppermute | solution.py:426
  25.4 0.0 collective-permute-done.10.arrived_ref
  25.4 0.4 collective-permute-start.9
  25.9 0.0 collective-permute-done.12.refs_1_
  25.9 2.1 %collective-permute-start.11 = (bf16[144,256]{1,0:T(8,128)(2,1)S(1)}, bf16[144,256]{1,0:T(8,128)(2,1)S(1)}, u32[]{:S(2)}, u32[]{:S(2)}) collective-permute-start(bf16[144,256]{1,0:T(8,128)(2,1)S(1)} %get-tuple-element.84), channel_id=1, source_target_pairs={{0,4},{4,0},{8,12},{12,8},{1,5},{5,1},{9,13},{13,9},{2,6},{6,2},{1... | collective-permute-start | bytes 221192 | tf_op jit(solution)/shard_map/ppermute | solution.py:426
  28.0 0.0 collective-permute-done.4.three_ref.refs_0_
  28.0 0.0 collective-permute-done.5.one_ref.refs_2_
  28.0 0.5 collective-permute-done.8.refs_4_.refs_0_
  28.6 0.6 %collective-permute-start.13 = (bf16[64,256]{1,0:T(8,128)(2,1)S(1)}, bf16[64,256]{1,0:T(8,128)(2,1)S(1)}, u32[]{:S(2)}, u32[]{:S(2)}) collective-permute-start(bf16[64,256]{1,0:T(8,128)(2,1)S(1)} %get-tuple-element.89), channel_id=1, source_target_pairs={{0,2},{2,0},{1,3},{3,1},{4,6},{6,4},{5,7},{7,5},{8,10},{10,8},{9,1... | collective-permute-start | bytes 98312 | tf_op jit(solution)/shard_map/ppermute | solution.py:426
  29.2 0.4 shard_map.166.own_ref.refs_6_
  29.6 2.9 %collective-permute-done.9.refs_1_ = bf16[144,256]{1,0:T(8,128)(2,1)S(1)} collective-permute-done((bf16[144,256]{1,0:T(8,128)(2,1)S(1)}, bf16[144,256]{1,0:T(8,128)(2,1)S(1)}, u32[]{:S(2)}, u32[]{:S(2)}) %collective-permute-start.9) | collective-permute-done | bytes 73760 | tf_op jit(solution)/shard_map/ppermute | solution.py:426
  32.5 0.0 collective-permute-done.11.refs_2_
  32.5 0.1 collective-permute-done.13.refs_5_
  32.6 3.3 %collective-permute-start.16 = (bf16[192,256]{1,0:T(8,128)(2,1)S(1)}, bf16[192,256]{1,0:T(8,128)(2,1)S(1)}, u32[]{:S(2)}, u32[]{:S(2)}) collective-permute-start(bf16[192,256]{1,0:T(8,128)(2,1)S(1)} %get-tuple-element.91.refs_0_), channel_id=1, source_target_pairs={{0,12},{4,8},{8,4},{12,0},{1,13},{5,9},{9,5},{13,1},{2,14},{6,10},... | collective-permute-start | bytes 294920 | tf_op jit(solution)/shard_map/ppermute | solution.py:426
  35.9 1.9 %collective-permute-start.15 = (bf16[192,256]{1,0:T(8,128)(2,1)S(1)}, bf16[192,256]{1,0:T(8,128)(2,1)S(1)}, u32[]{:S(2)}, u32[]{:S(2)}) collective-permute-start(bf16[192,256]{1,0:T(8,128)(2,1)S(1)} %get-tuple-element.91.refs_0_), channel_id=1, source_target_pairs={{0,8},{4,12},{8,0},{12,4},{1,9},{5,13},{9,1},{13,5},{2,10},{6,14},... | collective-permute-start | bytes 294920 | tf_op jit(solution)/shard_map/ppermute | solution.py:426
  37.8 0.5 collective-permute-start.14
  38.3 0.0 collective-permute-start.7
  38.3 0.5 collective-permute-start.17
  38.8 1.4 %collective-permute-done.16.refs_3_ = bf16[192,256]{1,0:T(8,128)(2,1)S(1)} collective-permute-done((bf16[192,256]{1,0:T(8,128)(2,1)S(1)}, bf16[192,256]{1,0:T(8,128)(2,1)S(1)}, u32[]{:S(2)}, u32[]{:S(2)}) %collective-permute-start.16) | collective-permute-done | bytes 98336 | tf_op jit(solution)/shard_map/ppermute | solution.py:426
  40.2 0.3 collective-permute-start.20
  40.4 4.3 %collective-permute-done.15.refs_2_ = bf16[192,256]{1,0:T(8,128)(2,1)S(1)} collective-permute-done((bf16[192,256]{1,0:T(8,128)(2,1)S(1)}, bf16[192,256]{1,0:T(8,128)(2,1)S(1)}, u32[]{:S(2)}, u32[]{:S(2)}) %collective-permute-start.15) | collective-permute-done | bytes 98336 | tf_op jit(solution)/shard_map/ppermute | solution.py:426
  44.8 0.4 collective-permute-start.19
  45.2 0.0 collective-permute-done.14.refs_1_
  45.2 1.6 %collective-permute-start.18 = (bf16[192,256]{1,0:T(8,128)(2,1)S(1)}, bf16[192,256]{1,0:T(8,128)(2,1)S(1)}, u32[]{:S(2)}, u32[]{:S(2)}) collective-permute-start(bf16[192,256]{1,0:T(8,128)(2,1)S(1)} %collective-permute-done.14.refs_1_), channel_id=1, source_target_pairs={{0,2},{2,0},{1,3},{3,1},{4,6},{6,4},{5,7},{7,5},{8,10},{10,8},{9,1... | collective-permute-start | bytes 294920 | tf_op jit(solution)/shard_map/ppermute | solution.py:426
  46.8 0.0 collective-permute-done.7.other_ref
  46.8 0.8 %shard_map.167 = (f32[128,512]{1,0:T(8,128)}, bf16[128,512]{1,0:T(8,128)(2,1)}) custom-call(bf16[128,512]{1,0:T(8,128)(2,1)S(1)} %get-tuple-element.53.cot_ref, bf16[128,512]{1,0:T(8,128)(2,1)S(1)} %get-tuple-element.52.refs_0_.node_ref, f32[1,512]{1,0:T(1,128)S(1)} %get-tuple-element.54.gain_ref, f32[128,512]{1,0:T(8,128)S(1)} %get-tuple-element.68.normed_ref, ...), custom_call_target="tpu_custom_call" | custom-call | flops 100000000 | bytes 1000000 | tf_op jit(solution)/shard_map/pallas_call | solution.py:408
  47.6 0.0 collective-permute-done.17.refs_4_
  47.6 0.0 collective-permute-done.20.refs_7_
  47.6 2.4 %collective-permute-done.19.refs_6_ = bf16[192,256]{1,0:T(8,128)(2,1)S(1)} collective-permute-done((bf16[192,256]{1,0:T(8,128)(2,1)S(1)}, bf16[192,256]{1,0:T(8,128)(2,1)S(1)}, u32[]{:S(2)}, u32[]{:S(2)}) %collective-permute-start.19) | collective-permute-done | bytes 98336 | tf_op jit(solution)/shard_map/ppermute | solution.py:426
  50.0 1.1 %collective-permute-done.18.refs_5_ = bf16[192,256]{1,0:T(8,128)(2,1)S(1)} collective-permute-done((bf16[192,256]{1,0:T(8,128)(2,1)S(1)}, bf16[192,256]{1,0:T(8,128)(2,1)S(1)}, u32[]{:S(2)}, u32[]{:S(2)}) %collective-permute-start.18) | collective-permute-done | bytes 98336 | tf_op jit(solution)/shard_map/ppermute | solution.py:426
  51.0 1.8 %shard_map.172 = (f32[512,256]{1,0:T(8,128)}, f32[512,256]{1,0:T(8,128)}, f32[256,512]{1,0:T(8,128)}, f32[1,256]{1,0:T(1,128)}, f32[1,512]{1,0:T(1,128)}) custom-call(f32[16,256]{1,0:T(8,128)S(1)} %get-tuple-element.90.tail_ref, bf16[192,256]{1,0:T(8,128)(2,1)S(1)} %get-tuple-element.91.refs_0_, bf16[192,256]{1,0:T(8,128)(2,1)S(1)} %collective-permute-done.14.refs_1_, ...), custom_call_target="tpu_custom_call" | custom-call | flops 100000000 | bytes 1000000 | tf_op jit(solution)/shard_map/pallas_call | solution.py:408
  (4 shorter events, 0.2 us)
Async XLA Ops:
  1.8 9.0 %collective-permute-start.2 = (bf16[64,512]{1,0:T(8,128)(2,1)S(1)}, bf16[64,512]{1,0:T(8,128)(2,1)S(1)}, u32[]{:S(2)}, u32[]{:S(2)}) collective-permute-start(bf16[64,512]{1,0:T(8,128)(2,1)S(1)} %get-tuple-element.64), channel_id=1, source_target_pairs={{0,2},{2,0},{1,3},{3,1},{4,6},{6,4},{5,7},{7,5},{8,10},{10,8},{9,1... | collective-permute-start | bytes 196616 | tf_op jit(solution)/shard_map/ppermute | solution.py:421
  4.8 5.9 %collective-permute-start = (bf16[32,512]{1,0:T(8,128)(2,1)S(1)}, bf16[32,512]{1,0:T(8,128)(2,1)S(1)}, u32[]{:S(2)}, u32[]{:S(2)}) collective-permute-start(bf16[32,512]{1,0:T(8,128)(2,1)S(1)} %get-tuple-element.62), channel_id=1, source_target_pairs={{0,4},{4,8},{8,12},{12,0},{1,5},{5,9},{9,13},{13,1},{2,6},{6,10},{... | collective-permute-start | bytes 98312 | tf_op jit(solution)/shard_map/ppermute | solution.py:421
  6.4 4.4 %collective-permute-start.1 = (bf16[32,512]{1,0:T(8,128)(2,1)S(1)}, bf16[32,512]{1,0:T(8,128)(2,1)S(1)}, u32[]{:S(2)}, u32[]{:S(2)}) collective-permute-start(bf16[32,512]{1,0:T(8,128)(2,1)S(1)} %get-tuple-element.63), channel_id=1, source_target_pairs={{0,12},{4,0},{8,4},{12,8},{1,13},{5,1},{9,5},{13,9},{2,14},{6,2},{... | collective-permute-start | bytes 98312 | tf_op jit(solution)/shard_map/ppermute | solution.py:421
  11.6 1.4 %collective-permute-start.3 = (bf16[128,512]{1,0:T(8,128)(2,1)S(1)}, bf16[128,512]{1,0:T(8,128)(2,1)S(1)}, u32[]{:S(2)}, u32[]{:S(2)}) collective-permute-start(bf16[128,512]{1,0:T(8,128)(2,1)S(1)} %get-tuple-element.67.own_ref), channel_id=1, source_target_pairs={{0,1},{1,0},{2,3},{3,2},{4,5},{5,4},{6,7},{7,6},{8,9},{9,8},{10,11... | collective-permute-start | bytes 393224 | tf_op jit(solution)/shard_map/ppermute | solution.py:421
  14.4 7.3 %collective-permute-start.6 = (bf16[336,256]{1,0:T(8,128)(2,1)S(1)}, bf16[336,256]{1,0:T(8,128)(2,1)S(1)}, u32[]{:S(2)}, u32[]{:S(2)}) collective-permute-start(bf16[336,256]{1,0:T(8,128)(2,1)S(1)} %get-tuple-element.75), channel_id=1, source_target_pairs={{0,2},{2,0},{1,3},{3,1},{4,6},{6,4},{5,7},{7,5},{8,10},{10,8},{9,1... | collective-permute-start | bytes 516104 | tf_op jit(solution)/shard_map/ppermute | solution.py:426
  14.9 10.5 %collective-permute-start.10 = (bf16[256,256]{1,0:T(8,128)(2,1)S(1)}, bf16[256,256]{1,0:T(8,128)(2,1)S(1)}, u32[]{:S(2)}, u32[]{:S(2)}) collective-permute-start(bf16[256,256]{1,0:T(8,128)(2,1)S(1)} %get-tuple-element.81), channel_id=1, source_target_pairs={{0,2},{2,0},{1,3},{3,1},{4,6},{6,4},{5,7},{7,5},{8,10},{10,8},{9,1... | collective-permute-start | bytes 393224 | tf_op jit(solution)/shard_map/ppermute | solution.py:426
  16.5 9.4 %collective-permute-start.12 = (bf16[64,512]{1,0:T(8,128)(2,1)S(1)}, bf16[64,512]{1,0:T(8,128)(2,1)S(1)}, u32[]{:S(2)}, u32[]{:S(2)}) collective-permute-start(bf16[64,512]{1,0:T(8,128)(2,1)S(1)} %get-tuple-element.86), channel_id=1, source_target_pairs={{0,8},{4,12},{8,0},{12,4},{1,9},{5,13},{9,1},{13,5},{2,10},{6,14},... | collective-permute-start | bytes 196616 | tf_op jit(solution)/shard_map/ppermute | solution.py:426
  18.7 9.4 %collective-permute-start.4 = (bf16[80,512]{1,0:T(8,128)(2,1)S(1)}, bf16[80,512]{1,0:T(8,128)(2,1)S(1)}, u32[]{:S(2)}, u32[]{:S(2)}) collective-permute-start(bf16[80,512]{1,0:T(8,128)(2,1)S(1)} %get-tuple-element.73), channel_id=1, source_target_pairs={{0,12},{4,8},{8,4},{12,0},{1,13},{5,9},{9,5},{13,1},{2,14},{6,10},... | collective-permute-start | bytes 245768 | tf_op jit(solution)/shard_map/ppermute | solution.py:426
  20.1 7.9 %collective-permute-start.5 = (bf16[80,512]{1,0:T(8,128)(2,1)S(1)}, bf16[80,512]{1,0:T(8,128)(2,1)S(1)}, u32[]{:S(2)}, u32[]{:S(2)}) collective-permute-start(bf16[80,512]{1,0:T(8,128)(2,1)S(1)} %get-tuple-element.74), channel_id=1, source_target_pairs={{0,4},{4,0},{8,12},{12,8},{1,5},{5,1},{9,13},{13,9},{2,6},{6,2},{1... | collective-permute-start | bytes 245768 | tf_op jit(solution)/shard_map/ppermute | solution.py:426
  21.8 6.8 %collective-permute-start.8 = (bf16[144,256]{1,0:T(8,128)(2,1)S(1)}, bf16[144,256]{1,0:T(8,128)(2,1)S(1)}, u32[]{:S(2)}, u32[]{:S(2)}) collective-permute-start(bf16[144,256]{1,0:T(8,128)(2,1)S(1)} %get-tuple-element.79), channel_id=1, source_target_pairs={{0,12},{4,8},{8,4},{12,0},{1,13},{5,9},{9,5},{13,1},{2,14},{6,10},... | collective-permute-start | bytes 221192 | tf_op jit(solution)/shard_map/ppermute | solution.py:426
  25.4 7.1 %collective-permute-start.9 = (bf16[144,256]{1,0:T(8,128)(2,1)S(1)}, bf16[144,256]{1,0:T(8,128)(2,1)S(1)}, u32[]{:S(2)}, u32[]{:S(2)}) collective-permute-start(bf16[144,256]{1,0:T(8,128)(2,1)S(1)} %get-tuple-element.80), channel_id=1, source_target_pairs={{0,8},{4,12},{8,0},{12,4},{1,9},{5,13},{9,1},{13,5},{2,10},{6,14},... | collective-permute-start | bytes 221192 | tf_op jit(solution)/shard_map/ppermute | solution.py:426
  25.9 6.6 %collective-permute-start.11 = (bf16[144,256]{1,0:T(8,128)(2,1)S(1)}, bf16[144,256]{1,0:T(8,128)(2,1)S(1)}, u32[]{:S(2)}, u32[]{:S(2)}) collective-permute-start(bf16[144,256]{1,0:T(8,128)(2,1)S(1)} %get-tuple-element.84), channel_id=1, source_target_pairs={{0,4},{4,0},{8,12},{12,8},{1,5},{5,1},{9,13},{13,9},{2,6},{6,2},{1... | collective-permute-start | bytes 221192 | tf_op jit(solution)/shard_map/ppermute | solution.py:426
  28.6 4.0 %collective-permute-start.13 = (bf16[64,256]{1,0:T(8,128)(2,1)S(1)}, bf16[64,256]{1,0:T(8,128)(2,1)S(1)}, u32[]{:S(2)}, u32[]{:S(2)}) collective-permute-start(bf16[64,256]{1,0:T(8,128)(2,1)S(1)} %get-tuple-element.89), channel_id=1, source_target_pairs={{0,2},{2,0},{1,3},{3,1},{4,6},{6,4},{5,7},{7,5},{8,10},{10,8},{9,1... | collective-permute-start | bytes 98312 | tf_op jit(solution)/shard_map/ppermute | solution.py:426
  32.6 7.6 %collective-permute-start.16 = (bf16[192,256]{1,0:T(8,128)(2,1)S(1)}, bf16[192,256]{1,0:T(8,128)(2,1)S(1)}, u32[]{:S(2)}, u32[]{:S(2)}) collective-permute-start(bf16[192,256]{1,0:T(8,128)(2,1)S(1)} %get-tuple-element.91.refs_0_), channel_id=1, source_target_pairs={{0,12},{4,8},{8,4},{12,0},{1,13},{5,9},{9,5},{13,1},{2,14},{6,10},... | collective-permute-start | bytes 294920 | tf_op jit(solution)/shard_map/ppermute | solution.py:426
  35.9 8.8 %collective-permute-start.15 = (bf16[192,256]{1,0:T(8,128)(2,1)S(1)}, bf16[192,256]{1,0:T(8,128)(2,1)S(1)}, u32[]{:S(2)}, u32[]{:S(2)}) collective-permute-start(bf16[192,256]{1,0:T(8,128)(2,1)S(1)} %get-tuple-element.91.refs_0_), channel_id=1, source_target_pairs={{0,8},{4,12},{8,0},{12,4},{1,9},{5,13},{9,1},{13,5},{2,10},{6,14},... | collective-permute-start | bytes 294920 | tf_op jit(solution)/shard_map/ppermute | solution.py:426
  37.8 7.3 %collective-permute-start.14 = (bf16[192,256]{1,0:T(8,128)(2,1)S(1)}, bf16[192,256]{1,0:T(8,128)(2,1)S(1)}, u32[]{:S(2)}, u32[]{:S(2)}) collective-permute-start(bf16[192,256]{1,0:T(8,128)(2,1)S(1)} %get-tuple-element.91.refs_0_), channel_id=1, source_target_pairs={{0,4},{4,0},{8,12},{12,8},{1,5},{5,1},{9,13},{13,9},{2,6},{6,2},{1... | collective-permute-start | bytes 294920 | tf_op jit(solution)/shard_map/ppermute | solution.py:426
  38.3 8.5 %collective-permute-start.7 = (bf16[128,512]{1,0:T(8,128)(2,1)S(1)}, bf16[128,512]{1,0:T(8,128)(2,1)S(1)}, u32[]{:S(2)}, u32[]{:S(2)}) collective-permute-start(bf16[128,512]{1,0:T(8,128)(2,1)S(1)} %shard_map.166.own_ref.refs_6_), channel_id=1, source_target_pairs={{0,1},{1,0},{2,3},{3,2},{4,5},{5,4},{6,7},{7,6},{8,9},{9,8},{10,11... | collective-permute-start | bytes 393224 | tf_op jit(solution)/shard_map/ppermute | solution.py:421
  38.3 9.3 %collective-permute-start.17 = (bf16[192,256]{1,0:T(8,128)(2,1)S(1)}, bf16[192,256]{1,0:T(8,128)(2,1)S(1)}, u32[]{:S(2)}, u32[]{:S(2)}) collective-permute-start(bf16[192,256]{1,0:T(8,128)(2,1)S(1)} %get-tuple-element.91.refs_0_), channel_id=1, source_target_pairs={{0,2},{2,0},{1,3},{3,1},{4,6},{6,4},{5,7},{7,5},{8,10},{10,8},{9,1... | collective-permute-start | bytes 294920 | tf_op jit(solution)/shard_map/ppermute | solution.py:426
  40.2 7.4 %collective-permute-start.20 = (bf16[192,256]{1,0:T(8,128)(2,1)S(1)}, bf16[192,256]{1,0:T(8,128)(2,1)S(1)}, u32[]{:S(2)}, u32[]{:S(2)}) collective-permute-start(bf16[192,256]{1,0:T(8,128)(2,1)S(1)} %collective-permute-done.16.refs_3_), channel_id=1, source_target_pairs={{0,2},{2,0},{1,3},{3,1},{4,6},{6,4},{5,7},{7,5},{8,10},{10,8},{9,1... | collective-permute-start | bytes 294920 | tf_op jit(solution)/shard_map/ppermute | solution.py:426
  44.8 5.2 %collective-permute-start.19 = (bf16[192,256]{1,0:T(8,128)(2,1)S(1)}, bf16[192,256]{1,0:T(8,128)(2,1)S(1)}, u32[]{:S(2)}, u32[]{:S(2)}) collective-permute-start(bf16[192,256]{1,0:T(8,128)(2,1)S(1)} %collective-permute-done.15.refs_2_), channel_id=1, source_target_pairs={{0,2},{2,0},{1,3},{3,1},{4,6},{6,4},{5,7},{7,5},{8,10},{10,8},{9,1... | collective-permute-start | bytes 294920 | tf_op jit(solution)/shard_map/ppermute | solution.py:426
  45.2 5.8 %collective-permute-start.18 = (bf16[192,256]{1,0:T(8,128)(2,1)S(1)}, bf16[192,256]{1,0:T(8,128)(2,1)S(1)}, u32[]{:S(2)}, u32[]{:S(2)}) collective-permute-start(bf16[192,256]{1,0:T(8,128)(2,1)S(1)} %collective-permute-done.14.refs_1_), channel_id=1, source_target_pairs={{0,2},{2,0},{1,3},{3,1},{4,6},{6,4},{5,7},{7,5},{8,10},{10,8},{9,1... | collective-permute-start | bytes 294920 | tf_op jit(solution)/shard_map/ppermute | solution.py:426

commit v6 on v5

--- a/solution.py
+++ b/solution.py
@@ -62,16 +62,20 @@
     return copies
 
 
-def send_kernel(node_hbm, send_hbm, node_ref, send_ref, *rest):
+def send_kernel(paired, node_hbm, send_hbm, node_ref, send_ref, *rest):
     *out_refs, sems = rest
     for copy in fetch(sems, (node_hbm, node_ref), (send_hbm, send_ref)):
         copy.wait()
     node = node_ref[...]
     rows = node.shape[0]
     halo = send_ref.shape[2]
+    chosen = [send_ref[0, d : d + 1, :] for d in range(4)]
+    if paired:
+        even = lax.axis_index("mesh") % 2 == 0
+        chosen[:2] = jnp.where(even, chosen[1], chosen[0]), jnp.where(even, chosen[0], chosen[1])
     pieces = []
-    for d in range(4):
-        pick = one_hot(iota((rows, halo), 0) == send_ref[0, d : d + 1, :])
+    for row in chosen:
+        pick = one_hot(iota((rows, halo), 0) == row)
         pieces.append(dot(pick, node, TN).astype(bf16))
     out_refs[0][...] = pieces[0]
     out_refs[1][...] = pieces[1]
@@ -83,7 +87,7 @@
         out_refs[3][...] = pieces[3]
 
 
-def local_kernel(*refs):
+def local_kernel(paired, *refs):
     node_ref, ins, refs = refs[0], refs[1 : 1 + N_FETCHED], refs[1 + N_FETCHED :]
     pre_ref, pick_ref, collect_ref, spread_ref, scatter_ref, *refs = refs
     w_src_ref, w_dst_ref, w_out_ref, gain_ref, cot_ref, count_ref, src_ref, dst_ref, bias_ref, sems = refs
@@ -94,10 +98,17 @@
     edges = src_ref.shape[1]
     for copy in copies[:3]:
         copy.wait()
-    scatter_ref[...] = one_hot(iota(scatter_ref.shape, 0) == src_ref[...])
+    src_row = src_ref[...]
+    if paired:
+        halo = (scatter_ref.shape[0] - rows) // 4
+        odd = lax.axis_index("mesh") % 2 == 1
+        step = jnp.where(src_row < rows + halo, halo, -halo)
+        ring = (src_row >= rows) & (src_row < rows + 2 * halo)
+        src_row = src_row + jnp.where(ring & odd, step, 0)
+    scatter_ref[...] = one_hot(iota(scatter_ref.shape, 0) == src_row)
     used = usable_row(count_ref, edges) > 0
     collect_ref[...] = one_hot((iota((rows, edges), 0) == dst_ref[...]) & used)
-    source = columns_of(src_ref[...], 128)
+    source = columns_of(src_row, 128)
     target = columns_of(dst_ref[...], 128)
     lane = iota(source.shape, 1)
     used = usable_columns(count_ref, edges, 128) > 0
@@ -140,7 +151,7 @@
     *rest,
 ):
     peers, chunk, n_halo, paired = geometry
-    *rest, out_scratch, back_scratch, pair_scratch = rest
+    *rest, out_scratch, pair_scratch = rest
     halo_refs = rest[:n_halo]
     normed_ref, local_ref, target_ref, *message_refs = rest[n_halo:]
     node = node_ref[...]
@@ -199,16 +210,13 @@
                 ref[at % 2 * strip : (at % 2 + 1) * strip, :] = pair_scratch[slot, pl.ds(start, strip), :]
             far_ref[2 * strip : 2 * strip + TAIL, :] = tail
         far_send_ref[2 * strip + TAIL :, :] = back[2 * halo :]
-        back_scratch[...] = back[: 2 * halo]
         out_scratch[...] = out_part
-        strip = hid // len(out_refs)
+        strip = hid // lines
         for k, ref in enumerate(out_refs):
             start = pl.multiple_of((mesh ^ k) * strip, strip)
             ref[0:strip, :] = out_scratch[pl.ds(start, strip), :]
             if k % 2 == 1:
-                slot = (mesh + (k // 2) + 1) % 2
-                start = pl.multiple_of(slot * halo, halo)
-                rows_back = back_scratch[pl.ds(start, halo), :]
+                rows_back = back[(1 - k // 2) * halo : (2 - k // 2) * halo]
                 ref[strip:, 0:hid] = rows_back[: halo // 2]
                 ref[strip:, hid:] = rows_back[halo // 2 :]
         return
@@ -303,34 +311,25 @@
         gain_ref[:, k * hid : (k + 1) * hid] = tail[2 + 2 * k : 3 + 2 * k] + tail[3 + 2 * k : 4 + 2 * k]
 
 
-def place_kernel(count, tail_ref, *refs):
+def place_kernel(order, *refs):
+    count = len(order)
     mine, theirs = refs[:count], refs[count : 2 * count]
-    src_hbm, dst_hbm, out_hbm, bias_ref, gain_ref, src_ref, dst_ref, out_ref, sems = refs[2 * count :]
+    src_ref, dst_ref, out_ref = refs[2 * count :]
     first = lax.axis_index("sub") == 0
     mesh = lax.axis_index("mesh")
-    strip, hid = src_ref.shape[1:]
-    narrow = out_ref.shape[1]
-    copies = []
-
-    def put(ref, hbm, k, rows):
-        start = pl.multiple_of((mesh ^ k) * rows, rows)
-        copies.append(pltpu.make_async_copy(ref.at[k], hbm.at[pl.ds(start, rows)], sems.at[len(copies)]))
-        copies[-1].start()
-
-    for k in range(count):
-        a, b = mine[k][...], theirs[k][...]
+    width, hid = src_ref.shape
+    strip = width // count
+    narrow = hid // count
+    for at, k in enumerate(order):
+        a, b = mine[at][...], theirs[at][...]
         low = jnp.where(first, a, b).astype(f32)
         high = jnp.where(first, b, a).astype(f32)
-        src_ref[k] = low[:strip]
-        put(src_ref, src_hbm, k, strip)
-        dst_ref[k] = high[:strip]
-        put(dst_ref, dst_hbm, k, strip)
-        out_ref[k, :, 0:hid] = low[strip:]
-        out_ref[k, :, hid:] = high[strip:]
-        put(out_ref, out_hbm, k, narrow)
-    write_vectors(tail_ref[...], bias_ref, gain_ref)
-    for copy in copies:
-        copy.wait()
+        start = pl.multiple_of((mesh ^ k) * strip, strip)
+        src_ref[pl.ds(start, strip), :] = low[:strip]
+        dst_ref[pl.ds(start, strip), :] = high[:strip]
+        start = pl.multiple_of((mesh ^ k) * narrow, narrow)
+        out_ref[pl.ds(start, narrow), 0:hid] = low[strip:]
+        out_ref[pl.ds(start, narrow), hid:] = high[strip:]
 
 
 def sum_kernel(chunk, arrived_ref, out_ref, bias_ref, gain_ref):
@@ -388,7 +387,11 @@
     node_part(send_ref, local_ref, target_ref, w_src_ref, w_dst_ref, returned, out_ref)
 
 
-def finish_kernel(cot_ref, node_ref, gain_ref, normed_ref, own_ref, other_ref, grad_ref, updated_ref):
+def finish_kernel(cot_ref, node_ref, gain_ref, normed_ref, own_ref, other_ref, *rest):
+    if len(rest) == 5:
+        tail_ref, *rest, bias_out_ref, gain_out_ref = rest
+        write_vectors(tail_ref[...], bias_out_ref, gain_out_ref)
+    grad_ref, updated_ref = rest
     grad_ref[...] = cot_ref[...].astype(f32) + (
         own_ref[...].astype(f32) + other_ref[...].astype(f32)
     )
@@ -440,34 +443,25 @@
     out_send, out_keep = call(
         line_kernel,
         [shape((narrow, hid), bf16)] * 2,
-        *[out_terms[k] for k in order], outs[0], line_terms[3],
+        *[out_terms[k] for k in order], outs[0], line_terms[2],
     )
     node_part = node_terms(out_terms[3], out_terms[1], far)
     own, tail = call(
         own_kernel,
         [shape((strip + narrow, hid), bf16), shape((TAIL, hid), f32)],
-        *[line_terms[k] for k in order], line[0], out_keep, across(out_send, "sub", 1),
+        *[line_terms[k] for k in (2, 3, 1)], line[0], out_keep, across(out_send, "sub", 1),
         node_part,
     )
     mine = {k: across(own, "mesh", k) for k in order}
     mine[0] = own
-    theirs = {k: across(mine[k], "sub", 1) for k in (0, 1, 3, 2)}
+    theirs = {k: across(mine[k], "sub", 1) for k in mine}
+    placed = (0, 3, 1, 2)
     grads = call(
-        functools.partial(place_kernel, lines),
-        [
-            shape((width, hid), f32), shape((width, hid), f32), shape((hid, width), f32),
-            shape((1, hid), f32), shape((1, width), f32),
-        ],
-        tail, *[mine[k] for k in range(lines)], *[theirs[k] for k in range(lines)],
-        out_specs=[HBM] * 3 + [VMEM] * 2,
-        scratch=[
-            pltpu.VMEM((lines, strip, hid), f32),
-            pltpu.VMEM((lines, strip, hid), f32),
-            pltpu.VMEM((lines, narrow, width), f32),
-            pltpu.SemaphoreType.DMA((3 * lines,)),
-        ],
-    )
-    return grads, node_part
+        functools.partial(place_kernel, placed),
+        [shape((width, hid), f32), shape((width, hid), f32), shape((hid, width), f32)],
+        *[mine[k] for k in placed], *[theirs[k] for k in placed],
+    )
+    return (*grads, tail), node_part
 
 
 def shards(
@@ -495,26 +489,33 @@
     piece = [halo, halo, 2 * halo] if merged else [halo] * 4
     routes = [("mesh", 1), ("mesh", -1), ("sub", 1)] + ([] if merged else [("sub", -1)])
     n_halo = len(piece)
+    lines = lax.axis_size("mesh")
+    paired = merged and lines == 4
 
     def in_hbm(x):
         return pltpu.with_memory_space_constraint(x, pltpu.HBM)
 
     node, send, *outgoing = call(
-        send_kernel,
+        functools.partial(send_kernel, paired),
         [shape((rows, width), bf16), shape(send_rows.shape, jnp.int32)]
         + [shape((n, width), bf16) for n in piece],
         in_hbm(node_state), in_hbm(send_rows),
         specs=[HBM, HBM],
         scratch=[pltpu.SemaphoreType.DMA((2,))],
     )
-    arrived = [shifted(x, axis, by) for x, (axis, by) in zip(outgoing, routes)]
+    if paired:
+        pair = across(outgoing[2], "sub", 1)
+        one = across(outgoing[1], "mesh", 1)
+        arrived = [across(outgoing[0], "mesh", 3), one, pair]
+    else:
+        arrived = [shifted(x, axis, by) for x, (axis, by) in zip(outgoing, routes)]
 
     fetched = [
         edge_src.reshape(1, edges), edge_dst.reshape(1, edges), block_count,
         hidden_bias.reshape(1, hid), w_src, w_dst, w_out, norm_gain.reshape(1, width), cotangent,
     ]
     pre, pick, collect, spread, scatter, w_src, w_dst, w_out, gain, cot = call(
-        local_kernel,
+        functools.partial(local_kernel, paired),
         [
             shape((edges, hid), f32),
             shape((edges, 4 * halo), bf16),
@@ -541,8 +542,6 @@
     )
     other = shifted(partial, "lat", 1)
 
-    lines = lax.axis_size("mesh")
-    paired = merged and lines == 4
     if paired:
         strip = width // lines
         narrow = hid // lines
@@ -559,7 +558,6 @@
         node, collect, spread, scatter, w_out, gain, cot, factor, hidden, partial, other, *arrived,
         scratch=[
             pltpu.VMEM((hid, width), bf16),
-            pltpu.VMEM((2 * halo, hid), bf16),
             pltpu.VMEM((2, width, hid), bf16),
         ],
     )
@@ -572,7 +570,7 @@
         )
 
     if paired:
-        (src_grad, dst_grad, out_grad, bias_grad, gain_grad), node_part = paired_sums(
+        (src_grad, dst_grad, out_grad, tail), node_part = paired_sums(
             messages, lines, strip, narrow, width, hid, node_terms
         )
     else:
@@ -591,11 +589,14 @@
             [shape((width, hid), f32), shape((width, hid), f32), shape((hid, width), f32)],
             gathered.reshape(peers * chunk, hid),
         )
-    node_grad, updated = call(
-        finish_kernel,
-        [shape((rows, width), f32), shape((rows, width), bf16)],
-        cot, node, gain, normed, node_part, shifted(node_part, "lat", 1),
-    )
+    finished = [shape((rows, width), f32), shape((rows, width), bf16)]
+    ends = [cot, node, gain, normed, node_part, shifted(node_part, "lat", 1)]
+    if paired:
+        node_grad, updated, bias_grad, gain_grad = call(
+            finish_kernel, finished + [shape((1, hid), f32), shape((1, width), f32)], *ends, tail
+        )
+    else:
+        node_grad, updated = call(finish_kernel, finished, *ends)
     return (
         updated, node_grad, src_grad, dst_grad, out_grad,
         bias_grad.reshape(hid), gain_grad.reshape(width),

time: 53 us -> 54 us (1.019)
  waiting for transfers between devices: 15.1 us -> 22.5 us
  starting transfers between devices: 28.4 us -> 22.5 us
  Pallas kernels: 8.65 us -> 8.07 us
    ppermute x16 -> x19, waiting for transfers between devices: 13.7 us -> 21.2 us  [across(): return lax.ppermute(x, axis, [(i, i ^ k) for i in range(count)])]
    ppermute x5 -> x2, starting transfers between devices: 6.9 us -> 0.07 us  [shifted(): return lax.ppermute(x, axis, [(i, (i + by) % count) for i in range(count)])]
    ppermute x16 -> x19, starting transfers between devices: 21.5 us -> 22.4 us  [across(): return lax.ppermute(x, axis, [(i, i ^ k) for i in range(count)])]
    pallas_call x11, Pallas kernels: 8.65 us -> 8.07 us  [call(): pl.pallas_call(kernel, out_shape=outs, in_specs=specs or [VMEM] * len(arg...]
    ppermute x5 -> x2, waiting for transfers between devices: 1.38 us -> 1.34 us  [shifted(): return lax.ppermute(x, axis, [(i, (i + by) % count) for i in range(count)])]
  transfers between devices with their start and end apart: 21 -> 21, of which waited for: 9 -> 10; matrix products, arithmetic and copies ran while one was open for 0% -> 0% of each run, Pallas kernels for 6% -> 6%
where the time goes in v6:
time: 54 us; the launch traced here: 53.8 us
  starting transfers between devices  22.5 us (42%)
  waiting for transfers between devices  22.5 us (42%)
  Pallas kernels  8.07 us (15%)
  between operations  0.77 us (1%)
    ppermute x19, starting transfers between devices, across(): return lax.ppermute(x, axis, [(i, i ^ k) for i in range(count)])  22.4 us
    ppermute x19, waiting for transfers between devices, across(): return lax.ppermute(x, axis, [(i, i ^ k) for i in range(count)])  21.2 us
    pallas_call x11, Pallas kernels, call(): pl.pallas_call(kernel, out_shape=outs, in_specs=specs or [VMEM] * len(arg...  8.07 us
    ppermute x2, waiting for transfers between devices, shifted(): return lax.ppermute(x, axis, [(i, (i + by) % count) for i in range(count)])  1.34 us
  transfers between devices with their start and end apart: 21, of which 10 were waited for; matrix products, arithmetic and copies ran while one was open for 0% of the time, Pallas kernels for 6%

profile of v6, /device:TPU:0, one launch (start us, length us, event | category | flops | bytes accessed | tf_op | source)
XLA Modules:
  0.0 53.8 jit_solution(5583795404855694823)
XLA Ops:
  0.6 1.2 %shard_map.162 = (bf16[128,512]{1,0:T(8,128)(2,1)S(1)}, s32[1,4,32]{2,1,0:T(4,128)S(1)}, bf16[32,512]{1,0:T(8,128)(2,1)S(1)}, bf16[32,512]{1,0:T(8,128)(2,1)S(1)}, bf16[64,512]{1,0:T(8,128)(2,1)S(1)}) custom-call(bf16[128,512]{1,0:T(8,128)(2,1)} %node_hbm.1, s32[1,4,32]{2,1,0:T(4,128)} %send_hbm.1), custom_call_target="tpu_custom_call" | custom-call | flops 100000000 | bytes 1000000 | tf_op jit(solution)/shard_map/pallas_call | solution.py:411
  1.8 3.0 %collective-permute-start.2 = (bf16[64,512]{1,0:T(8,128)(2,1)S(1)}, bf16[64,512]{1,0:T(8,128)(2,1)S(1)}, u32[]{:S(2)}, u32[]{:S(2)}) collective-permute-start(bf16[64,512]{1,0:T(8,128)(2,1)S(1)} %get-tuple-element.64), channel_id=1, source_target_pairs={{0,2},{2,0},{1,3},{3,1},{4,6},{6,4},{5,7},{7,5},{8,10},{10,8},{9,1... | collective-permute-start | bytes 196616 | tf_op jit(solution)/shard_map/ppermute | solution.py:429
  4.8 3.6 %collective-permute-start = (bf16[32,512]{1,0:T(8,128)(2,1)S(1)}, bf16[32,512]{1,0:T(8,128)(2,1)S(1)}, u32[]{:S(2)}, u32[]{:S(2)}) collective-permute-start(bf16[32,512]{1,0:T(8,128)(2,1)S(1)} %get-tuple-element.62), channel_id=1, source_target_pairs={{0,12},{4,8},{8,4},{12,0},{1,13},{5,9},{9,5},{13,1},{2,14},{6,10},... | collective-permute-start | bytes 98312 | tf_op jit(solution)/shard_map/ppermute | solution.py:429
  8.4 0.0 collective-permute-start.1
  8.4 2.1 %shard_map.163 = (f32[512,256]{1,0:T(8,128)S(1)}, bf16[512,128]{1,0:T(8,128)(2,1)S(1)}, bf16[128,512]{1,0:T(8,128)(2,1)S(1)}, bf16[512,128]{1,0:T(8,128)(2,1)S(1...) custom-call(bf16[128,512]{1,0:T(8,128)(2,1)S(1)} %get-tuple-element., ...), custom_call_target="tpu_custom_call" | custom-call | flops 100000000 | bytes 1000000 | tf_op jit(solution)/shard_map/pallas_call | solution.py:411
  10.5 0.0 collective-permute-done.rest_0_
  10.6 1.8 %collective-permute-done.1.rest_1_ = bf16[32,512]{1,0:T(8,128)(2,1)S(1)} collective-permute-done((bf16[32,512]{1,0:T(8,128)(2,1)S(1)}, bf16[32,512]{1,0:T(8,128)(2,1)S(1)}, u32[]{:S(2)}, u32[]{:S(2)}) %collective-permute-start.1) | collective-permute-done | bytes 32800 | tf_op jit(solution)/shard_map/ppermute | solution.py:429
  12.3 0.0 collective-permute-done.2.rest_2_
  12.4 0.9 %shard_map.164 = (f32[512,256]{1,0:T(8,128)S(1)}, bf16[128,256]{1,0:T(8,128)(2,1)S(1)}, bf16[128,512]{1,0:T(8,128)(2,1)S(1)}) custom-call(f32[512,256]{1,0:T(8,128)S(1)} %get-tuple-element.59.pre_ref, bf16[512,128]{1,0:T(8,128)(2,1)S(1)} %get-tuple-element.60.pick_ref, bf16[128,512]{1,0:T(8,128)(2,1)S(1)} %get-tuple-element.55.collect_ref, ...), custom_call_target="tpu_custom_call" | custom-call | flops 100000000 | bytes 1000000 | tf_op jit(solution)/shard_map/pallas_call | solution.py:411
  13.2 0.1 collective-permute-start.3
  13.3 1.3 %collective-permute-done.3.other_ref = bf16[128,512]{1,0:T(8,128)(2,1)S(1)} collective-permute-done((bf16[128,512]{1,0:T(8,128)(2,1)S(1)}, bf16[128,512]{1,0:T(8,128)(2,1)S(1)}, u32[]{:S(2)}, u32[]{:S(2)}) %collective-permute-start.3) | collective-permute-done | bytes 131104 | tf_op jit(solution)/shard_map/ppermute | solution.py:424
  14.6 1.4 %shard_map.165 = (f32[128,512]{1,0:T(8,128)S(1)}, f32[128,256]{1,0:T(8,128)S(1)}, bf16[128,256]{1,0:T(8,128)(2,1)S(1)}, bf16[336,256]{1,0:T(8,128)(2,1)S(1)}, bf...) custom-call(bf16[128,512]{1,0:T(8,128)(2,1)S(1)} %get-tuple-element., ...), custom_call_target="tpu_custom_call" | custom-call | flops 100000000 | bytes 1000000 | tf_op jit(solution)/shard_map/pallas_call | solution.py:411
  16.0 0.6 %collective-permute-start.6 = (bf16[336,256]{1,0:T(8,128)(2,1)S(1)}, bf16[336,256]{1,0:T(8,128)(2,1)S(1)}, u32[]{:S(2)}, u32[]{:S(2)}) collective-permute-start(bf16[336,256]{1,0:T(8,128)(2,1)S(1)} %get-tuple-element.75), channel_id=1, source_target_pairs={{0,2},{2,0},{1,3},{3,1},{4,6},{6,4},{5,7},{7,5},{8,10},{10,8},{9,1... | collective-permute-start | bytes 516104 | tf_op jit(solution)/shard_map/ppermute | solution.py:429
  16.6 1.5 %collective-permute-start.10 = (bf16[256,256]{1,0:T(8,128)(2,1)S(1)}, bf16[256,256]{1,0:T(8,128)(2,1)S(1)}, u32[]{:S(2)}, u32[]{:S(2)}) collective-permute-start(bf16[256,256]{1,0:T(8,128)(2,1)S(1)} %get-tuple-element.79), channel_id=1, source_target_pairs={{0,2},{2,0},{1,3},{3,1},{4,6},{6,4},{5,7},{7,5},{8,10},{10,8},{9,1... | collective-permute-start | bytes 393224 | tf_op jit(solution)/shard_map/ppermute | solution.py:429
  18.1 0.0 collective-permute-start.12
  18.1 2.7 %collective-permute-start.4 = (bf16[80,512]{1,0:T(8,128)(2,1)S(1)}, bf16[80,512]{1,0:T(8,128)(2,1)S(1)}, u32[]{:S(2)}, u32[]{:S(2)}) collective-permute-start(bf16[80,512]{1,0:T(8,128)(2,1)S(1)} %get-tuple-element.73), channel_id=1, source_target_pairs={{0,12},{4,8},{8,4},{12,0},{1,13},{5,9},{9,5},{13,1},{2,14},{6,10},... | collective-permute-start | bytes 245768 | tf_op jit(solution)/shard_map/ppermute | solution.py:429
  20.8 0.8 %collective-permute-start.5 = (bf16[80,512]{1,0:T(8,128)(2,1)S(1)}, bf16[80,512]{1,0:T(8,128)(2,1)S(1)}, u32[]{:S(2)}, u32[]{:S(2)}) collective-permute-start(bf16[80,512]{1,0:T(8,128)(2,1)S(1)} %get-tuple-element.74), channel_id=1, source_target_pairs={{0,4},{4,0},{8,12},{12,8},{1,5},{5,1},{9,13},{13,9},{2,6},{6,2},{1... | collective-permute-start | bytes 245768 | tf_op jit(solution)/shard_map/ppermute | solution.py:429
  21.6 1.7 %collective-permute-done.6.pair_ref.arrived_ref = bf16[336,256]{1,0:T(8,128)(2,1)S(1)} collective-permute-done((bf16[336,256]{1,0:T(8,128)(2,1)S(1)}, bf16[336,256]{1,0:T(8,128)(2,1)S(1)}, u32[]{:S(2)}, u32[]{:S(2)}) %collective-permute-start.6) | collective-permute-done | bytes 172064 | tf_op jit(solution)/shard_map/ppermute | solution.py:429
  23.3 0.1 collective-permute-start.8
  23.4 1.9 %collective-permute-done.10.arrived_ref = bf16[256,256]{1,0:T(8,128)(2,1)S(1)} collective-permute-done((bf16[256,256]{1,0:T(8,128)(2,1)S(1)}, bf16[256,256]{1,0:T(8,128)(2,1)S(1)}, u32[]{:S(2)}, u32[]{:S(2)}) %collective-permute-start.10) | collective-permute-done | bytes 131104 | tf_op jit(solution)/shard_map/ppermute | solution.py:429
  25.3 1.8 %collective-permute-start.9 = (bf16[144,256]{1,0:T(8,128)(2,1)S(1)}, bf16[144,256]{1,0:T(8,128)(2,1)S(1)}, u32[]{:S(2)}, u32[]{:S(2)}) collective-permute-start(bf16[144,256]{1,0:T(8,128)(2,1)S(1)} %get-tuple-element.78), channel_id=1, source_target_pairs={{0,12},{4,8},{8,4},{12,0},{1,13},{5,9},{9,5},{13,1},{2,14},{6,10},... | collective-permute-start | bytes 221192 | tf_op jit(solution)/shard_map/ppermute | solution.py:429
  27.2 0.0 collective-permute-done.12.refs_1_
  27.2 0.1 collective-permute-start.11
  27.3 0.0 collective-permute-done.4.three_ref.refs_0_
  27.3 0.0 collective-permute-done.5.one_ref.refs_2_
  27.3 5.2 %collective-permute-done.8.refs_4_.refs_0_ = bf16[144,256]{1,0:T(8,128)(2,1)S(1)} collective-permute-done((bf16[144,256]{1,0:T(8,128)(2,1)S(1)}, bf16[144,256]{1,0:T(8,128)(2,1)S(1)}, u32[]{:S(2)}, u32[]{:S(2)}) %collective-permute-start.8) | collective-permute-done | bytes 73760 | tf_op jit(solution)/shard_map/ppermute | solution.py:429
  32.6 0.6 %collective-permute-start.13 = (bf16[64,256]{1,0:T(8,128)(2,1)S(1)}, bf16[64,256]{1,0:T(8,128)(2,1)S(1)}, u32[]{:S(2)}, u32[]{:S(2)}) collective-permute-start(bf16[64,256]{1,0:T(8,128)(2,1)S(1)} %get-tuple-element.87), channel_id=1, source_target_pairs={{0,2},{2,0},{1,3},{3,1},{4,6},{6,4},{5,7},{7,5},{8,10},{10,8},{9,1... | collective-permute-start | bytes 98312 | tf_op jit(solution)/shard_map/ppermute | solution.py:429
  33.2 0.4 shard_map.166.refs_6_.own_ref
  33.6 0.0 collective-permute-done.9.refs_1_
  33.6 0.0 collective-permute-done.11.refs_2_
  33.6 2.9 %collective-permute-done.13.refs_5_ = bf16[64,256]{1,0:T(8,128)(2,1)S(1)} collective-permute-done((bf16[64,256]{1,0:T(8,128)(2,1)S(1)}, bf16[64,256]{1,0:T(8,128)(2,1)S(1)}, u32[]{:S(2)}, u32[]{:S(2)}) %collective-permute-start.13) | collective-permute-done | bytes 32800 | tf_op jit(solution)/shard_map/ppermute | solution.py:429
  36.6 0.1 collective-permute-start.16
  36.7 2.2 %collective-permute-start.15 = (bf16[192,256]{1,0:T(8,128)(2,1)S(1)}, bf16[192,256]{1,0:T(8,128)(2,1)S(1)}, u32[]{:S(2)}, u32[]{:S(2)}) collective-permute-start(bf16[192,256]{1,0:T(8,128)(2,1)S(1)} %get-tuple-element.91.refs_0_), channel_id=1, source_target_pairs={{0,4},{4,0},{8,12},{12,8},{1,5},{5,1},{9,13},{13,9},{2,6},{6,2},{1... | collective-permute-start | bytes 294920 | tf_op jit(solution)/shard_map/ppermute | solution.py:429
  38.9 2.2 %collective-permute-start.14 = (bf16[192,256]{1,0:T(8,128)(2,1)S(1)}, bf16[192,256]{1,0:T(8,128)(2,1)S(1)}, u32[]{:S(2)}, u32[]{:S(2)}) collective-permute-start(bf16[192,256]{1,0:T(8,128)(2,1)S(1)} %get-tuple-element.91.refs_0_), channel_id=1, source_target_pairs={{0,12},{4,8},{8,4},{12,0},{1,13},{5,9},{9,5},{13,1},{2,14},{6,10},... | collective-permute-start | bytes 294920 | tf_op jit(solution)/shard_map/ppermute | solution.py:429
  41.0 0.0 collective-permute-start.7
  41.0 0.6 %collective-permute-start.17 = (bf16[192,256]{1,0:T(8,128)(2,1)S(1)}, bf16[192,256]{1,0:T(8,128)(2,1)S(1)}, u32[]{:S(2)}, u32[]{:S(2)}) collective-permute-start(bf16[192,256]{1,0:T(8,128)(2,1)S(1)} %get-tuple-element.91.refs_0_), channel_id=1, source_target_pairs={{0,2},{2,0},{1,3},{3,1},{4,6},{6,4},{5,7},{7,5},{8,10},{10,8},{9,1... | collective-permute-start | bytes 294920 | tf_op jit(solution)/shard_map/ppermute | solution.py:429
  41.6 2.0 %collective-permute-done.16.refs_3_ = bf16[192,256]{1,0:T(8,128)(2,1)S(1)} collective-permute-done((bf16[192,256]{1,0:T(8,128)(2,1)S(1)}, bf16[192,256]{1,0:T(8,128)(2,1)S(1)}, u32[]{:S(2)}, u32[]{:S(2)}) %collective-permute-start.16) | collective-permute-done | bytes 98336 | tf_op jit(solution)/shard_map/ppermute | solution.py:429
  43.6 0.6 %collective-permute-start.20 = (bf16[192,256]{1,0:T(8,128)(2,1)S(1)}, bf16[192,256]{1,0:T(8,128)(2,1)S(1)}, u32[]{:S(2)}, u32[]{:S(2)}) collective-permute-start(bf16[192,256]{1,0:T(8,128)(2,1)S(1)} %collective-permute-done.16.refs_3_), channel_id=1, source_target_pairs={{0,2},{2,0},{1,3},{3,1},{4,6},{6,4},{5,7},{7,5},{8,10},{10,8},{9,1... | collective-permute-start | bytes 294920 | tf_op jit(solution)/shard_map/ppermute | solution.py:429
  44.1 0.0 collective-permute-done.15.refs_2_
  44.2 1.5 %collective-permute-start.19 = (bf16[192,256]{1,0:T(8,128)(2,1)S(1)}, bf16[192,256]{1,0:T(8,128)(2,1)S(1)}, u32[]{:S(2)}, u32[]{:S(2)}) collective-permute-start(bf16[192,256]{1,0:T(8,128)(2,1)S(1)} %collective-permute-done.15.refs_2_), channel_id=1, source_target_pairs={{0,2},{2,0},{1,3},{3,1},{4,6},{6,4},{5,7},{7,5},{8,10},{10,8},{9,1... | collective-permute-start | bytes 294920 | tf_op jit(solution)/shard_map/ppermute | solution.py:429
  45.6 0.0 collective-permute-done.14.refs_1_
  45.6 0.6 %collective-permute-start.18 = (bf16[192,256]{1,0:T(8,128)(2,1)S(1)}, bf16[192,256]{1,0:T(8,128)(2,1)S(1)}, u32[]{:S(2)}, u32[]{:S(2)}) collective-permute-start(bf16[192,256]{1,0:T(8,128)(2,1)S(1)} %collective-permute-done.14.refs_1_), channel_id=1, source_target_pairs={{0,2},{2,0},{1,3},{3,1},{4,6},{6,4},{5,7},{7,5},{8,10},{10,8},{9,1... | collective-permute-start | bytes 294920 | tf_op jit(solution)/shard_map/ppermute | solution.py:429
  46.2 0.0 collective-permute-done.7.other_ref
  46.2 0.8 %shard_map.171 = (f32[128,512]{1,0:T(8,128)}, bf16[128,512]{1,0:T(8,128)(2,1)}, f32[1,256]{1,0:T(1,128)}, f32[1,512]{1,0:T(1,128)}) custom-call(bf16[128,512]{1,0:T(8,128)(2,1)S(1)} %get-tuple-element.53.cot_ref, bf16[128,512]{1,0:T(8,128)(2,1)S(1)} %get-tuple-element.52.refs_0_.node_ref, f32[1,512]{1,0:T(1,128)S(1)} %get-tuple-element.54.gain_ref, ...), custom_call_target="tpu_custom_call" | custom-call | flops 100000000 | bytes 1000000 | tf_op jit(solution)/shard_map/pallas_call | solution.py:411
  47.0 0.0 collective-permute-done.17.refs_4_
  47.0 2.3 %collective-permute-done.20.refs_7_ = bf16[192,256]{1,0:T(8,128)(2,1)S(1)} collective-permute-done((bf16[192,256]{1,0:T(8,128)(2,1)S(1)}, bf16[192,256]{1,0:T(8,128)(2,1)S(1)}, u32[]{:S(2)}, u32[]{:S(2)}) %collective-permute-start.20) | collective-permute-done | bytes 98336 | tf_op jit(solution)/shard_map/ppermute | solution.py:429
  49.3 2.1 %collective-permute-done.19.refs_6_ = bf16[192,256]{1,0:T(8,128)(2,1)S(1)} collective-permute-done((bf16[192,256]{1,0:T(8,128)(2,1)S(1)}, bf16[192,256]{1,0:T(8,128)(2,1)S(1)}, u32[]{:S(2)}, u32[]{:S(2)}) %collective-permute-start.19) | collective-permute-done | bytes 98336 | tf_op jit(solution)/shard_map/ppermute | solution.py:429
  51.4 1.2 %collective-permute-done.18.refs_5_ = bf16[192,256]{1,0:T(8,128)(2,1)S(1)} collective-permute-done((bf16[192,256]{1,0:T(8,128)(2,1)S(1)}, bf16[192,256]{1,0:T(8,128)(2,1)S(1)}, u32[]{:S(2)}, u32[]{:S(2)}) %collective-permute-start.18) | collective-permute-done | bytes 98336 | tf_op jit(solution)/shard_map/ppermute | solution.py:429
  52.6 1.2 %shard_map.172 = (f32[512,256]{1,0:T(8,128)}, f32[512,256]{1,0:T(8,128)}, f32[256,512]{1,0:T(8,128)}) custom-call(bf16[192,256]{1,0:T(8,128)(2,1)S(1)} %get-tuple-element.91.refs_0_, bf16[192,256]{1,0:T(8,128)(2,1)S(1)} %collective-permute-done.14.refs_1_, bf16[192,256]{1,0:T(8,128)(2,1)S(1)} %collective-permute-done.15.refs_2_, ...), custom_call_target="tpu_custom_call" | custom-call | flops 100000000 | bytes 1000000 | tf_op jit(solution)/shard_map/pallas_call | solution.py:411
  (4 shorter events, 0.2 us)
Async XLA Ops:
  1.8 10.5 %collective-permute-start.2 = (bf16[64,512]{1,0:T(8,128)(2,1)S(1)}, bf16[64,512]{1,0:T(8,128)(2,1)S(1)}, u32[]{:S(2)}, u32[]{:S(2)}) collective-permute-start(bf16[64,512]{1,0:T(8,128)(2,1)S(1)} %get-tuple-element.64), channel_id=1, source_target_pairs={{0,2},{2,0},{1,3},{3,1},{4,6},{6,4},{5,7},{7,5},{8,10},{10,8},{9,1... | collective-permute-start | bytes 196616 | tf_op jit(solution)/shard_map/ppermute | solution.py:429
  4.8 5.7 %collective-permute-start = (bf16[32,512]{1,0:T(8,128)(2,1)S(1)}, bf16[32,512]{1,0:T(8,128)(2,1)S(1)}, u32[]{:S(2)}, u32[]{:S(2)}) collective-permute-start(bf16[32,512]{1,0:T(8,128)(2,1)S(1)} %get-tuple-element.62), channel_id=1, source_target_pairs={{0,12},{4,8},{8,4},{12,0},{1,13},{5,9},{9,5},{13,1},{2,14},{6,10},... | collective-permute-start | bytes 98312 | tf_op jit(solution)/shard_map/ppermute | solution.py:429
  8.4 3.9 %collective-permute-start.1 = (bf16[32,512]{1,0:T(8,128)(2,1)S(1)}, bf16[32,512]{1,0:T(8,128)(2,1)S(1)}, u32[]{:S(2)}, u32[]{:S(2)}) collective-permute-start(bf16[32,512]{1,0:T(8,128)(2,1)S(1)} %get-tuple-element.63), channel_id=1, source_target_pairs={{0,4},{4,0},{8,12},{12,8},{1,5},{5,1},{9,13},{13,9},{2,6},{6,2},{1... | collective-permute-start | bytes 98312 | tf_op jit(solution)/shard_map/ppermute | solution.py:429
  13.2 1.4 %collective-permute-start.3 = (bf16[128,512]{1,0:T(8,128)(2,1)S(1)}, bf16[128,512]{1,0:T(8,128)(2,1)S(1)}, u32[]{:S(2)}, u32[]{:S(2)}) collective-permute-start(bf16[128,512]{1,0:T(8,128)(2,1)S(1)} %get-tuple-element.67.own_ref), channel_id=1, source_target_pairs={{0,1},{1,0},{2,3},{3,2},{4,5},{5,4},{6,7},{7,6},{8,9},{9,8},{10,11... | collective-permute-start | bytes 393224 | tf_op jit(solution)/shard_map/ppermute | solution.py:424
  16.0 7.3 %collective-permute-start.6 = (bf16[336,256]{1,0:T(8,128)(2,1)S(1)}, bf16[336,256]{1,0:T(8,128)(2,1)S(1)}, u32[]{:S(2)}, u32[]{:S(2)}) collective-permute-start(bf16[336,256]{1,0:T(8,128)(2,1)S(1)} %get-tuple-element.75), channel_id=1, source_target_pairs={{0,2},{2,0},{1,3},{3,1},{4,6},{6,4},{5,7},{7,5},{8,10},{10,8},{9,1... | collective-permute-start | bytes 516104 | tf_op jit(solution)/shard_map/ppermute | solution.py:429
  16.6 8.7 %collective-permute-start.10 = (bf16[256,256]{1,0:T(8,128)(2,1)S(1)}, bf16[256,256]{1,0:T(8,128)(2,1)S(1)}, u32[]{:S(2)}, u32[]{:S(2)}) collective-permute-start(bf16[256,256]{1,0:T(8,128)(2,1)S(1)} %get-tuple-element.79), channel_id=1, source_target_pairs={{0,2},{2,0},{1,3},{3,1},{4,6},{6,4},{5,7},{7,5},{8,10},{10,8},{9,1... | collective-permute-start | bytes 393224 | tf_op jit(solution)/shard_map/ppermute | solution.py:429
  18.1 9.1 %collective-permute-start.12 = (bf16[64,512]{1,0:T(8,128)(2,1)S(1)}, bf16[64,512]{1,0:T(8,128)(2,1)S(1)}, u32[]{:S(2)}, u32[]{:S(2)}) collective-permute-start(bf16[64,512]{1,0:T(8,128)(2,1)S(1)} %get-tuple-element.84), channel_id=1, source_target_pairs={{0,8},{4,12},{8,0},{12,4},{1,9},{5,13},{9,1},{13,5},{2,10},{6,14},... | collective-permute-start | bytes 196616 | tf_op jit(solution)/shard_map/ppermute | solution.py:429
  18.1 9.2 %collective-permute-start.4 = (bf16[80,512]{1,0:T(8,128)(2,1)S(1)}, bf16[80,512]{1,0:T(8,128)(2,1)S(1)}, u32[]{:S(2)}, u32[]{:S(2)}) collective-permute-start(bf16[80,512]{1,0:T(8,128)(2,1)S(1)} %get-tuple-element.73), channel_id=1, source_target_pairs={{0,12},{4,8},{8,4},{12,0},{1,13},{5,9},{9,5},{13,1},{2,14},{6,10},... | collective-permute-start | bytes 245768 | tf_op jit(solution)/shard_map/ppermute | solution.py:429
  20.8 6.5 %collective-permute-start.5 = (bf16[80,512]{1,0:T(8,128)(2,1)S(1)}, bf16[80,512]{1,0:T(8,128)(2,1)S(1)}, u32[]{:S(2)}, u32[]{:S(2)}) collective-permute-start(bf16[80,512]{1,0:T(8,128)(2,1)S(1)} %get-tuple-element.74), channel_id=1, source_target_pairs={{0,4},{4,0},{8,12},{12,8},{1,5},{5,1},{9,13},{13,9},{2,6},{6,2},{1... | collective-permute-start | bytes 245768 | tf_op jit(solution)/shard_map/ppermute | solution.py:429
  23.3 9.2 %collective-permute-start.8 = (bf16[144,256]{1,0:T(8,128)(2,1)S(1)}, bf16[144,256]{1,0:T(8,128)(2,1)S(1)}, u32[]{:S(2)}, u32[]{:S(2)}) collective-permute-start(bf16[144,256]{1,0:T(8,128)(2,1)S(1)} %get-tuple-element.77), channel_id=1, source_target_pairs={{0,8},{4,12},{8,0},{12,4},{1,9},{5,13},{9,1},{13,5},{2,10},{6,14},... | collective-permute-start | bytes 221192 | tf_op jit(solution)/shard_map/ppermute | solution.py:429
  25.3 8.3 %collective-permute-start.9 = (bf16[144,256]{1,0:T(8,128)(2,1)S(1)}, bf16[144,256]{1,0:T(8,128)(2,1)S(1)}, u32[]{:S(2)}, u32[]{:S(2)}) collective-permute-start(bf16[144,256]{1,0:T(8,128)(2,1)S(1)} %get-tuple-element.78), channel_id=1, source_target_pairs={{0,12},{4,8},{8,4},{12,0},{1,13},{5,9},{9,5},{13,1},{2,14},{6,10},... | collective-permute-start | bytes 221192 | tf_op jit(solution)/shard_map/ppermute | solution.py:429
  27.2 6.4 %collective-permute-start.11 = (bf16[144,256]{1,0:T(8,128)(2,1)S(1)}, bf16[144,256]{1,0:T(8,128)(2,1)S(1)}, u32[]{:S(2)}, u32[]{:S(2)}) collective-permute-start(bf16[144,256]{1,0:T(8,128)(2,1)S(1)} %get-tuple-element.82), channel_id=1, source_target_pairs={{0,4},{4,0},{8,12},{12,8},{1,5},{5,1},{9,13},{13,9},{2,6},{6,2},{1... | collective-permute-start | bytes 221192 | tf_op jit(solution)/shard_map/ppermute | solution.py:429
  32.6 4.0 %collective-permute-start.13 = (bf16[64,256]{1,0:T(8,128)(2,1)S(1)}, bf16[64,256]{1,0:T(8,128)(2,1)S(1)}, u32[]{:S(2)}, u32[]{:S(2)}) collective-permute-start(bf16[64,256]{1,0:T(8,128)(2,1)S(1)} %get-tuple-element.87), channel_id=1, source_target_pairs={{0,2},{2,0},{1,3},{3,1},{4,6},{6,4},{5,7},{7,5},{8,10},{10,8},{9,1... | collective-permute-start | bytes 98312 | tf_op jit(solution)/shard_map/ppermute | solution.py:429
  36.6 7.0 %collective-permute-start.16 = (bf16[192,256]{1,0:T(8,128)(2,1)S(1)}, bf16[192,256]{1,0:T(8,128)(2,1)S(1)}, u32[]{:S(2)}, u32[]{:S(2)}) collective-permute-start(bf16[192,256]{1,0:T(8,128)(2,1)S(1)} %get-tuple-element.91.refs_0_), channel_id=1, source_target_pairs={{0,8},{4,12},{8,0},{12,4},{1,9},{5,13},{9,1},{13,5},{2,10},{6,14},... | collective-permute-start | bytes 294920 | tf_op jit(solution)/shard_map/ppermute | solution.py:429
  36.7 7.5 %collective-permute-start.15 = (bf16[192,256]{1,0:T(8,128)(2,1)S(1)}, bf16[192,256]{1,0:T(8,128)(2,1)S(1)}, u32[]{:S(2)}, u32[]{:S(2)}) collective-permute-start(bf16[192,256]{1,0:T(8,128)(2,1)S(1)} %get-tuple-element.91.refs_0_), channel_id=1, source_target_pairs={{0,4},{4,0},{8,12},{12,8},{1,5},{5,1},{9,13},{13,9},{2,6},{6,2},{1... | collective-permute-start | bytes 294920 | tf_op jit(solution)/shard_map/ppermute | solution.py:429
  38.9 6.7 %collective-permute-start.14 = (bf16[192,256]{1,0:T(8,128)(2,1)S(1)}, bf16[192,256]{1,0:T(8,128)(2,1)S(1)}, u32[]{:S(2)}, u32[]{:S(2)}) collective-permute-start(bf16[192,256]{1,0:T(8,128)(2,1)S(1)} %get-tuple-element.91.refs_0_), channel_id=1, source_target_pairs={{0,12},{4,8},{8,4},{12,0},{1,13},{5,9},{9,5},{13,1},{2,14},{6,10},... | collective-permute-start | bytes 294920 | tf_op jit(solution)/shard_map/ppermute | solution.py:429
  41.0 5.1 %collective-permute-start.7 = (bf16[128,512]{1,0:T(8,128)(2,1)S(1)}, bf16[128,512]{1,0:T(8,128)(2,1)S(1)}, u32[]{:S(2)}, u32[]{:S(2)}) collective-permute-start(bf16[128,512]{1,0:T(8,128)(2,1)S(1)} %shard_map.166.refs_6_.own_ref), channel_id=1, source_target_pairs={{0,1},{1,0},{2,3},{3,2},{4,5},{5,4},{6,7},{7,6},{8,9},{9,8},{10,11... | collective-permute-start | bytes 393224 | tf_op jit(solution)/shard_map/ppermute | solution.py:424
  41.0 5.9 %collective-permute-start.17 = (bf16[192,256]{1,0:T(8,128)(2,1)S(1)}, bf16[192,256]{1,0:T(8,128)(2,1)S(1)}, u32[]{:S(2)}, u32[]{:S(2)}) collective-permute-start(bf16[192,256]{1,0:T(8,128)(2,1)S(1)} %get-tuple-element.91.refs_0_), channel_id=1, source_target_pairs={{0,2},{2,0},{1,3},{3,1},{4,6},{6,4},{5,7},{7,5},{8,10},{10,8},{9,1... | collective-permute-start | bytes 294920 | tf_op jit(solution)/shard_map/ppermute | solution.py:429
  43.6 5.7 %collective-permute-start.20 = (bf16[192,256]{1,0:T(8,128)(2,1)S(1)}, bf16[192,256]{1,0:T(8,128)(2,1)S(1)}, u32[]{:S(2)}, u32[]{:S(2)}) collective-permute-start(bf16[192,256]{1,0:T(8,128)(2,1)S(1)} %collective-permute-done.16.refs_3_), channel_id=1, source_target_pairs={{0,2},{2,0},{1,3},{3,1},{4,6},{6,4},{5,7},{7,5},{8,10},{10,8},{9,1... | collective-permute-start | bytes 294920 | tf_op jit(solution)/shard_map/ppermute | solution.py:429
  44.2 7.3 %collective-permute-start.19 = (bf16[192,256]{1,0:T(8,128)(2,1)S(1)}, bf16[192,256]{1,0:T(8,128)(2,1)S(1)}, u32[]{:S(2)}, u32[]{:S(2)}) collective-permute-start(bf16[192,256]{1,0:T(8,128)(2,1)S(1)} %collective-permute-done.15.refs_2_), channel_id=1, source_target_pairs={{0,2},{2,0},{1,3},{3,1},{4,6},{6,4},{5,7},{7,5},{8,10},{10,8},{9,1... | collective-permute-start | bytes 294920 | tf_op jit(solution)/shard_map/ppermute | solution.py:429
  45.6 7.0 %collective-permute-start.18 = (bf16[192,256]{1,0:T(8,128)(2,1)S(1)}, bf16[192,256]{1,0:T(8,128)(2,1)S(1)}, u32[]{:S(2)}, u32[]{:S(2)}) collective-permute-start(bf16[192,256]{1,0:T(8,128)(2,1)S(1)} %collective-permute-done.14.refs_1_), channel_id=1, source_target_pairs={{0,2},{2,0},{1,3},{3,1},{4,6},{6,4},{5,7},{7,5},{8,10},{10,8},{9,1... | collective-permute-start | bytes 294920 | tf_op jit(solution)/shard_map/ppermute | solution.py:429

commit v7 on v6

--- a/solution.py
+++ b/solution.py
@@ -62,20 +62,16 @@
     return copies
 
 
-def send_kernel(paired, node_hbm, send_hbm, node_ref, send_ref, *rest):
+def send_kernel(node_hbm, send_hbm, node_ref, send_ref, *rest):
     *out_refs, sems = rest
     for copy in fetch(sems, (node_hbm, node_ref), (send_hbm, send_ref)):
         copy.wait()
     node = node_ref[...]
     rows = node.shape[0]
     halo = send_ref.shape[2]
-    chosen = [send_ref[0, d : d + 1, :] for d in range(4)]
-    if paired:
-        even = lax.axis_index("mesh") % 2 == 0
-        chosen[:2] = jnp.where(even, chosen[1], chosen[0]), jnp.where(even, chosen[0], chosen[1])
     pieces = []
-    for row in chosen:
-        pick = one_hot(iota((rows, halo), 0) == row)
+    for d in range(4):
+        pick = one_hot(iota((rows, halo), 0) == send_ref[0, d : d + 1, :])
         pieces.append(dot(pick, node, TN).astype(bf16))
     out_refs[0][...] = pieces[0]
     out_refs[1][...] = pieces[1]
@@ -87,7 +83,7 @@
         out_refs[3][...] = pieces[3]
 
 
-def local_kernel(paired, *refs):
+def local_kernel(*refs):
     node_ref, ins, refs = refs[0], refs[1 : 1 + N_FETCHED], refs[1 + N_FETCHED :]
     pre_ref, pick_ref, collect_ref, spread_ref, scatter_ref, *refs = refs
     w_src_ref, w_dst_ref, w_out_ref, gain_ref, cot_ref, count_ref, src_ref, dst_ref, bias_ref, sems = refs
@@ -98,17 +94,10 @@
     edges = src_ref.shape[1]
     for copy in copies[:3]:
         copy.wait()
-    src_row = src_ref[...]
-    if paired:
-        halo = (scatter_ref.shape[0] - rows) // 4
-        odd = lax.axis_index("mesh") % 2 == 1
-        step = jnp.where(src_row < rows + halo, halo, -halo)
-        ring = (src_row >= rows) & (src_row < rows + 2 * halo)
-        src_row = src_row + jnp.where(ring & odd, step, 0)
-    scatter_ref[...] = one_hot(iota(scatter_ref.shape, 0) == src_row)
+    scatter_ref[...] = one_hot(iota(scatter_ref.shape, 0) == src_ref[...])
     used = usable_row(count_ref, edges) > 0
     collect_ref[...] = one_hot((iota((rows, edges), 0) == dst_ref[...]) & used)
-    source = columns_of(src_row, 128)
+    source = columns_of(src_ref[...], 128)
     target = columns_of(dst_ref[...], 128)
     lane = iota(source.shape, 1)
     used = usable_columns(count_ref, edges, 128) > 0
@@ -151,7 +140,7 @@
     *rest,
 ):
     peers, chunk, n_halo, paired = geometry
-    *rest, out_scratch, pair_scratch = rest
+    *rest, out_scratch, back_scratch, pair_scratch = rest
     halo_refs = rest[:n_halo]
     normed_ref, local_ref, target_ref, *message_refs = rest[n_halo:]
     node = node_ref[...]
@@ -210,13 +199,16 @@
                 ref[at % 2 * strip : (at % 2 + 1) * strip, :] = pair_scratch[slot, pl.ds(start, strip), :]
             far_ref[2 * strip : 2 * strip + TAIL, :] = tail
         far_send_ref[2 * strip + TAIL :, :] = back[2 * halo :]
+        back_scratch[...] = back[: 2 * halo]
         out_scratch[...] = out_part
-        strip = hid // lines
+        strip = hid // len(out_refs)
         for k, ref in enumerate(out_refs):
             start = pl.multiple_of((mesh ^ k) * strip, strip)
             ref[0:strip, :] = out_scratch[pl.ds(start, strip), :]
             if k % 2 == 1:
-                rows_back = back[(1 - k // 2) * halo : (2 - k // 2) * halo]
+                slot = (mesh + (k // 2) + 1) % 2
+                start = pl.multiple_of(slot * halo, halo)
+                rows_back = back_scratch[pl.ds(start, halo), :]
                 ref[strip:, 0:hid] = rows_back[: halo // 2]
                 ref[strip:, hid:] = rows_back[halo // 2 :]
         return
@@ -311,6 +303,10 @@
         gain_ref[:, k * hid : (k + 1) * hid] = tail[2 + 2 * k : 3 + 2 * k] + tail[3 + 2 * k : 4 + 2 * k]
 
 
+def relay_kernel(strip_ref, _, out_ref):
+    out_ref[...] = strip_ref[...]
+
+
 def place_kernel(order, *refs):
     count = len(order)
     mine, theirs = refs[:count], refs[count : 2 * count]
@@ -443,18 +439,20 @@
     out_send, out_keep = call(
         line_kernel,
         [shape((narrow, hid), bf16)] * 2,
-        *[out_terms[k] for k in order], outs[0], line_terms[2],
+        *[out_terms[k] for k in order], outs[0], line_terms[3],
     )
     node_part = node_terms(out_terms[3], out_terms[1], far)
     own, tail = call(
         own_kernel,
         [shape((strip + narrow, hid), bf16), shape((TAIL, hid), f32)],
-        *[line_terms[k] for k in (2, 3, 1)], line[0], out_keep, across(out_send, "sub", 1),
+        *[line_terms[k] for k in (3, 2, 1)], line[0], out_keep, across(out_send, "sub", 1),
         node_part,
     )
     mine = {k: across(own, "mesh", k) for k in order}
     mine[0] = own
-    theirs = {k: across(mine[k], "sub", 1) for k in mine}
+    theirs = {0: across(own, "sub", 1)}
+    first = call(relay_kernel, shape(own.shape, bf16), mine[2], theirs[0])
+    theirs |= {k: across(first if k == 2 else mine[k], "sub", 1) for k in order}
     placed = (0, 3, 1, 2)
     grads = call(
         functools.partial(place_kernel, placed),
@@ -489,33 +487,26 @@
     piece = [halo, halo, 2 * halo] if merged else [halo] * 4
     routes = [("mesh", 1), ("mesh", -1), ("sub", 1)] + ([] if merged else [("sub", -1)])
     n_halo = len(piece)
-    lines = lax.axis_size("mesh")
-    paired = merged and lines == 4
 
     def in_hbm(x):
         return pltpu.with_memory_space_constraint(x, pltpu.HBM)
 
     node, send, *outgoing = call(
-        functools.partial(send_kernel, paired),
+        send_kernel,
         [shape((rows, width), bf16), shape(send_rows.shape, jnp.int32)]
         + [shape((n, width), bf16) for n in piece],
         in_hbm(node_state), in_hbm(send_rows),
         specs=[HBM, HBM],
         scratch=[pltpu.SemaphoreType.DMA((2,))],
     )
-    if paired:
-        pair = across(outgoing[2], "sub", 1)
-        one = across(outgoing[1], "mesh", 1)
-        arrived = [across(outgoing[0], "mesh", 3), one, pair]
-    else:
-        arrived = [shifted(x, axis, by) for x, (axis, by) in zip(outgoing, routes)]
+    arrived = [shifted(x, axis, by) for x, (axis, by) in zip(outgoing, routes)]
 
     fetched = [
         edge_src.reshape(1, edges), edge_dst.reshape(1, edges), block_count,
         hidden_bias.reshape(1, hid), w_src, w_dst, w_out, norm_gain.reshape(1, width), cotangent,
     ]
     pre, pick, collect, spread, scatter, w_src, w_dst, w_out, gain, cot = call(
-        functools.partial(local_kernel, paired),
+        local_kernel,
         [
             shape((edges, hid), f32),
             shape((edges, 4 * halo), bf16),
@@ -542,6 +533,8 @@
     )
     other = shifted(partial, "lat", 1)
 
+    lines = lax.axis_size("mesh")
+    paired = merged and lines == 4
     if paired:
         strip = width // lines
         narrow = hid // lines
@@ -558,6 +551,7 @@
         node, collect, spread, scatter, w_out, gain, cot, factor, hidden, partial, other, *arrived,
         scratch=[
             pltpu.VMEM((hid, width), bf16),
+            pltpu.VMEM((2 * halo, hid), bf16),
             pltpu.VMEM((2, width, hid), bf16),
         ],
     )

time: 54 us -> 52 us (0.963)
  waiting for transfers between devices: 22.5 us -> 12.9 us
  starting transfers between devices: 22.5 us -> 30.2 us
    ppermute x19 -> x16, waiting for transfers between devices: 21.2 us -> 11.5 us  [across(): return lax.ppermute(x, axis, [(i, i ^ k) for i in range(count)])]
    ppermute x2 -> x5, starting transfers between devices: 0.07 us -> 6.9 us  [shifted(): return lax.ppermute(x, axis, [(i, (i + by) % count) for i in range(count)])]
    ppermute x19 -> x16, starting transfers between devices: 22.4 us -> 23.3 us  [across(): return lax.ppermute(x, axis, [(i, i ^ k) for i in range(count)])]
    ppermute x2 -> x5, waiting for transfers between devices: 1.34 us -> 1.38 us  [shifted(): return lax.ppermute(x, axis, [(i, (i + by) % count) for i in range(count)])]
    pallas_call x11 -> x12, Pallas kernels: 8.07 us -> 8.08 us  [call(): pl.pallas_call(kernel, out_shape=outs, in_specs=specs or [VMEM] * len(arg...]
  transfers between devices with their start and end apart: 21 -> 21, of which waited for: 10 -> 10; matrix products, arithmetic and copies ran while one was open for 0% -> 0% of each run, Pallas kernels for 6% -> 7%
where the time goes in v7:
time: 52 us; the launch traced here: 51.9 us
  starting transfers between devices  30.2 us (58%)
  waiting for transfers between devices  12.9 us (25%)
  Pallas kernels  8.08 us (16%)
  between operations  0.72 us (1%)
    ppermute x16, starting transfers between devices, across(): return lax.ppermute(x, axis, [(i, i ^ k) for i in range(count)])  23.3 us
    ppermute x16, waiting for transfers between devices, across(): return lax.ppermute(x, axis, [(i, i ^ k) for i in range(count)])  11.5 us
    pallas_call x12, Pallas kernels, call(): pl.pallas_call(kernel, out_shape=outs, in_specs=specs or [VMEM] * len(arg...  8.08 us
    ppermute x5, starting transfers between devices, shifted(): return lax.ppermute(x, axis, [(i, (i + by) % count) for i in range(count)])  6.9 us
    ppermute x5, waiting for transfers between devices, shifted(): return lax.ppermute(x, axis, [(i, (i + by) % count) for i in range(count)])  1.38 us
  transfers between devices with their start and end apart: 21, of which 10 were waited for; matrix products, arithmetic and copies ran while one was open for 0% of the time, Pallas kernels for 7%

profile of v7, /device:TPU:0, one launch (start us, length us, event | category | flops | bytes accessed | tf_op | source)
XLA Modules:
  0.0 51.9 jit_solution(7739036298765546825)
XLA Ops:
  0.6 1.2 %shard_map.162 = (bf16[128,512]{1,0:T(8,128)(2,1)S(1)}, s32[1,4,32]{2,1,0:T(4,128)S(1)}, bf16[32,512]{1,0:T(8,128)(2,1)S(1)}, bf16[32,512]{1,0:T(8,128)(2,1)S(1)}, bf16[64,512]{1,0:T(8,128)(2,1)S(1)}) custom-call(bf16[128,512]{1,0:T(8,128)(2,1)} %node_hbm.1, s32[1,4,32]{2,1,0:T(4,128)} %send_hbm.1), custom_call_target="tpu_custom_call" | custom-call | flops 100000000 | bytes 1000000 | tf_op jit(solution)/shard_map/pallas_call | solution.py:407
  1.8 3.0 %collective-permute-start.2 = (bf16[64,512]{1,0:T(8,128)(2,1)S(1)}, bf16[64,512]{1,0:T(8,128)(2,1)S(1)}, u32[]{:S(2)}, u32[]{:S(2)}) collective-permute-start(bf16[64,512]{1,0:T(8,128)(2,1)S(1)} %get-tuple-element.64), channel_id=1, source_target_pairs={{0,2},{2,0},{1,3},{3,1},{4,6},{6,4},{5,7},{7,5},{8,10},{10,8},{9,1... | collective-permute-start | bytes 196616 | tf_op jit(solution)/shard_map/ppermute | solution.py:420
  4.8 1.6 %collective-permute-start = (bf16[32,512]{1,0:T(8,128)(2,1)S(1)}, bf16[32,512]{1,0:T(8,128)(2,1)S(1)}, u32[]{:S(2)}, u32[]{:S(2)}) collective-permute-start(bf16[32,512]{1,0:T(8,128)(2,1)S(1)} %get-tuple-element.62), channel_id=1, source_target_pairs={{0,4},{4,8},{8,12},{12,0},{1,5},{5,9},{9,13},{13,1},{2,6},{6,10},{... | collective-permute-start | bytes 98312 | tf_op jit(solution)/shard_map/ppermute | solution.py:420
  6.4 2.2 %collective-permute-start.1 = (bf16[32,512]{1,0:T(8,128)(2,1)S(1)}, bf16[32,512]{1,0:T(8,128)(2,1)S(1)}, u32[]{:S(2)}, u32[]{:S(2)}) collective-permute-start(bf16[32,512]{1,0:T(8,128)(2,1)S(1)} %get-tuple-element.63), channel_id=1, source_target_pairs={{0,12},{4,0},{8,4},{12,8},{1,13},{5,1},{9,5},{13,9},{2,14},{6,2},{... | collective-permute-start | bytes 98312 | tf_op jit(solution)/shard_map/ppermute | solution.py:420
  8.6 2.1 %shard_map.163 = (f32[512,256]{1,0:T(8,128)S(1)}, bf16[512,128]{1,0:T(8,128)(2,1)S(1)}, bf16[128,512]{1,0:T(8,128)(2,1)S(1)}, bf16[512,128]{1,0:T(8,128)(2,1)S(1...) custom-call(bf16[128,512]{1,0:T(8,128)(2,1)S(1)} %get-tuple-element., ...), custom_call_target="tpu_custom_call" | custom-call | flops 100000000 | bytes 1000000 | tf_op jit(solution)/shard_map/pallas_call | solution.py:407
  10.7 0.0 collective-permute-done.rest_0_
  10.8 0.0 collective-permute-done.1.rest_1_
  10.8 0.0 collective-permute-done.2.rest_2_
  10.8 0.9 %shard_map.164 = (f32[512,256]{1,0:T(8,128)S(1)}, bf16[128,256]{1,0:T(8,128)(2,1)S(1)}, bf16[128,512]{1,0:T(8,128)(2,1)S(1)}) custom-call(f32[512,256]{1,0:T(8,128)S(1)} %get-tuple-element.59.pre_ref, bf16[512,128]{1,0:T(8,128)(2,1)S(1)} %get-tuple-element.60.pick_ref, bf16[128,512]{1,0:T(8,128)(2,1)S(1)} %get-tuple-element.55.collect_ref, ...), custom_call_target="tpu_custom_call" | custom-call | flops 100000000 | bytes 1000000 | tf_op jit(solution)/shard_map/pallas_call | solution.py:407
  11.6 0.1 collective-permute-start.3
  11.7 1.3 %collective-permute-done.3.other_ref = bf16[128,512]{1,0:T(8,128)(2,1)S(1)} collective-permute-done((bf16[128,512]{1,0:T(8,128)(2,1)S(1)}, bf16[128,512]{1,0:T(8,128)(2,1)S(1)}, u32[]{:S(2)}, u32[]{:S(2)}) %collective-permute-start.3) | collective-permute-done | bytes 131104 | tf_op jit(solution)/shard_map/ppermute | solution.py:420
  13.1 1.4 %shard_map.165 = (f32[128,512]{1,0:T(8,128)S(1)}, f32[128,256]{1,0:T(8,128)S(1)}, bf16[128,256]{1,0:T(8,128)(2,1)S(1)}, bf16[336,256]{1,0:T(8,128)(2,1)S(1)}, bf...) custom-call(bf16[128,512]{1,0:T(8,128)(2,1)S(1)} %get-tuple-element., ...), custom_call_target="tpu_custom_call" | custom-call | flops 100000000 | bytes 1000000 | tf_op jit(solution)/shard_map/pallas_call | solution.py:407
  14.4 0.5 collective-permute-start.6
  14.9 1.6 %collective-permute-start.10 = (bf16[256,256]{1,0:T(8,128)(2,1)S(1)}, bf16[256,256]{1,0:T(8,128)(2,1)S(1)}, u32[]{:S(2)}, u32[]{:S(2)}) collective-permute-start(bf16[256,256]{1,0:T(8,128)(2,1)S(1)} %get-tuple-element.79), channel_id=1, source_target_pairs={{0,2},{2,0},{1,3},{3,1},{4,6},{6,4},{5,7},{7,5},{8,10},{10,8},{9,1... | collective-permute-start | bytes 393224 | tf_op jit(solution)/shard_map/ppermute | solution.py:425
  16.5 2.1 %collective-permute-start.12 = (bf16[64,512]{1,0:T(8,128)(2,1)S(1)}, bf16[64,512]{1,0:T(8,128)(2,1)S(1)}, u32[]{:S(2)}, u32[]{:S(2)}) collective-permute-start(bf16[64,512]{1,0:T(8,128)(2,1)S(1)} %get-tuple-element.84), channel_id=1, source_target_pairs={{0,8},{4,12},{8,0},{12,4},{1,9},{5,13},{9,1},{13,5},{2,10},{6,14},... | collective-permute-start | bytes 196616 | tf_op jit(solution)/shard_map/ppermute | solution.py:425
  18.7 1.5 %collective-permute-start.4 = (bf16[80,512]{1,0:T(8,128)(2,1)S(1)}, bf16[80,512]{1,0:T(8,128)(2,1)S(1)}, u32[]{:S(2)}, u32[]{:S(2)}) collective-permute-start(bf16[80,512]{1,0:T(8,128)(2,1)S(1)} %get-tuple-element.73), channel_id=1, source_target_pairs={{0,12},{4,8},{8,4},{12,0},{1,13},{5,9},{9,5},{13,1},{2,14},{6,10},... | collective-permute-start | bytes 245768 | tf_op jit(solution)/shard_map/ppermute | solution.py:425
  20.1 0.6 %collective-permute-start.5 = (bf16[80,512]{1,0:T(8,128)(2,1)S(1)}, bf16[80,512]{1,0:T(8,128)(2,1)S(1)}, u32[]{:S(2)}, u32[]{:S(2)}) collective-permute-start(bf16[80,512]{1,0:T(8,128)(2,1)S(1)} %get-tuple-element.74), channel_id=1, source_target_pairs={{0,4},{4,0},{8,12},{12,8},{1,5},{5,1},{9,13},{13,9},{2,6},{6,2},{1... | collective-permute-start | bytes 245768 | tf_op jit(solution)/shard_map/ppermute | solution.py:425
  20.7 1.0 %collective-permute-done.6.pair_ref.arrived_ref = bf16[336,256]{1,0:T(8,128)(2,1)S(1)} collective-permute-done((bf16[336,256]{1,0:T(8,128)(2,1)S(1)}, bf16[336,256]{1,0:T(8,128)(2,1)S(1)}, u32[]{:S(2)}, u32[]{:S(2)}) %collective-permute-start.6) | collective-permute-done | bytes 172064 | tf_op jit(solution)/shard_map/ppermute | solution.py:425
  21.8 3.7 %collective-permute-start.8 = (bf16[144,256]{1,0:T(8,128)(2,1)S(1)}, bf16[144,256]{1,0:T(8,128)(2,1)S(1)}, u32[]{:S(2)}, u32[]{:S(2)}) collective-permute-start(bf16[144,256]{1,0:T(8,128)(2,1)S(1)} %get-tuple-element.77), channel_id=1, source_target_pairs={{0,12},{4,8},{8,4},{12,0},{1,13},{5,9},{9,5},{13,1},{2,14},{6,10},... | collective-permute-start | bytes 221192 | tf_op jit(solution)/shard_map/ppermute | solution.py:425
  25.4 0.0 collective-permute-done.10.arrived_ref
  25.4 0.4 collective-permute-start.9
  25.9 0.0 collective-permute-done.12.refs_1_
  25.9 2.1 %collective-permute-start.11 = (bf16[144,256]{1,0:T(8,128)(2,1)S(1)}, bf16[144,256]{1,0:T(8,128)(2,1)S(1)}, u32[]{:S(2)}, u32[]{:S(2)}) collective-permute-start(bf16[144,256]{1,0:T(8,128)(2,1)S(1)} %get-tuple-element.82), channel_id=1, source_target_pairs={{0,4},{4,0},{8,12},{12,8},{1,5},{5,1},{9,13},{13,9},{2,6},{6,2},{1... | collective-permute-start | bytes 221192 | tf_op jit(solution)/shard_map/ppermute | solution.py:425
  28.0 0.0 collective-permute-done.4.three_ref.refs_0_
  28.0 0.0 collective-permute-done.5.one_ref.refs_2_
  28.0 0.5 collective-permute-done.8.refs_4_.refs_0_
  28.6 0.6 %collective-permute-start.13 = (bf16[64,256]{1,0:T(8,128)(2,1)S(1)}, bf16[64,256]{1,0:T(8,128)(2,1)S(1)}, u32[]{:S(2)}, u32[]{:S(2)}) collective-permute-start(bf16[64,256]{1,0:T(8,128)(2,1)S(1)} %get-tuple-element.87), channel_id=1, source_target_pairs={{0,2},{2,0},{1,3},{3,1},{4,6},{6,4},{5,7},{7,5},{8,10},{10,8},{9,1... | collective-permute-start | bytes 98312 | tf_op jit(solution)/shard_map/ppermute | solution.py:425
  29.2 0.4 shard_map.166.refs_6_.own_ref
  29.6 2.9 %collective-permute-done.9.refs_1_ = bf16[144,256]{1,0:T(8,128)(2,1)S(1)} collective-permute-done((bf16[144,256]{1,0:T(8,128)(2,1)S(1)}, bf16[144,256]{1,0:T(8,128)(2,1)S(1)}, u32[]{:S(2)}, u32[]{:S(2)}) %collective-permute-start.9) | collective-permute-done | bytes 73760 | tf_op jit(solution)/shard_map/ppermute | solution.py:425
  32.5 0.0 collective-permute-done.11.refs_2_
  32.5 0.1 collective-permute-done.13.refs_5_
  32.6 0.6 %collective-permute-start.17 = (bf16[192,256]{1,0:T(8,128)(2,1)S(1)}, bf16[192,256]{1,0:T(8,128)(2,1)S(1)}, u32[]{:S(2)}, u32[]{:S(2)}) collective-permute-start(bf16[192,256]{1,0:T(8,128)(2,1)S(1)} %get-tuple-element.91.refs_0_), channel_id=1, source_target_pairs={{0,2},{2,0},{1,3},{3,1},{4,6},{6,4},{5,7},{7,5},{8,10},{10,8},{9,1... | collective-permute-start | bytes 294920 | tf_op jit(solution)/shard_map/ppermute | solution.py:425
  33.2 5.0 %collective-permute-start.16 = (bf16[192,256]{1,0:T(8,128)(2,1)S(1)}, bf16[192,256]{1,0:T(8,128)(2,1)S(1)}, u32[]{:S(2)}, u32[]{:S(2)}) collective-permute-start(bf16[192,256]{1,0:T(8,128)(2,1)S(1)} %get-tuple-element.91.refs_0_), channel_id=1, source_target_pairs={{0,8},{4,12},{8,0},{12,4},{1,9},{5,13},{9,1},{13,5},{2,10},{6,14},... | collective-permute-start | bytes 294920 | tf_op jit(solution)/shard_map/ppermute | solution.py:425
  38.2 0.0 collective-permute-start.15
  38.2 1.5 %collective-permute-start.14 = (bf16[192,256]{1,0:T(8,128)(2,1)S(1)}, bf16[192,256]{1,0:T(8,128)(2,1)S(1)}, u32[]{:S(2)}, u32[]{:S(2)}) collective-permute-start(bf16[192,256]{1,0:T(8,128)(2,1)S(1)} %get-tuple-element.91.refs_0_), channel_id=1, source_target_pairs={{0,12},{4,8},{8,4},{12,0},{1,13},{5,9},{9,5},{13,1},{2,14},{6,10},... | collective-permute-start | bytes 294920 | tf_op jit(solution)/shard_map/ppermute | solution.py:425
  39.7 0.0 collective-permute-start.7
  39.7 0.0 collective-permute-done.17._.refs_4_
  39.7 3.5 %collective-permute-done.16.strip_ref.refs_3_ = bf16[192,256]{1,0:T(8,128)(2,1)S(1)} collective-permute-done((bf16[192,256]{1,0:T(8,128)(2,1)S(1)}, bf16[192,256]{1,0:T(8,128)(2,1)S(1)}, u32[]{:S(2)}, u32[]{:S(2)}) %collective-permute-start.16) | collective-permute-done | bytes 98336 | tf_op jit(solution)/shard_map/ppermute | solution.py:425
  43.3 1.1 %collective-permute-start.20 = (bf16[192,256]{1,0:T(8,128)(2,1)S(1)}, bf16[192,256]{1,0:T(8,128)(2,1)S(1)}, u32[]{:S(2)}, u32[]{:S(2)}) collective-permute-start(bf16[192,256]{1,0:T(8,128)(2,1)S(1)} %shard_map.172), channel_id=1, source_target_pairs={{0,2},{2,0},{1,3},{3,1},{4,6},{6,4},{5,7},{7,5},{8,10},{10,8},{9,1... | collective-permute-start | bytes 294920 | tf_op jit(solution)/shard_map/ppermute | solution.py:425
  44.4 0.6 %collective-permute-done.15.refs_2_ = bf16[192,256]{1,0:T(8,128)(2,1)S(1)} collective-permute-done((bf16[192,256]{1,0:T(8,128)(2,1)S(1)}, bf16[192,256]{1,0:T(8,128)(2,1)S(1)}, u32[]{:S(2)}, u32[]{:S(2)}) %collective-permute-start.15) | collective-permute-done | bytes 98336 | tf_op jit(solution)/shard_map/ppermute | solution.py:425
  44.9 0.4 collective-permute-start.19
  45.4 0.0 collective-permute-done.14.refs_1_
  45.4 1.6 %collective-permute-start.18 = (bf16[192,256]{1,0:T(8,128)(2,1)S(1)}, bf16[192,256]{1,0:T(8,128)(2,1)S(1)}, u32[]{:S(2)}, u32[]{:S(2)}) collective-permute-start(bf16[192,256]{1,0:T(8,128)(2,1)S(1)} %collective-permute-done.14.refs_1_), channel_id=1, source_target_pairs={{0,2},{2,0},{1,3},{3,1},{4,6},{6,4},{5,7},{7,5},{8,10},{10,8},{9,1... | collective-permute-start | bytes 294920 | tf_op jit(solution)/shard_map/ppermute | solution.py:425
  47.0 0.0 collective-permute-done.7.other_ref
  47.0 0.8 %shard_map.171 = (f32[128,512]{1,0:T(8,128)}, bf16[128,512]{1,0:T(8,128)(2,1)}, f32[1,256]{1,0:T(1,128)}, f32[1,512]{1,0:T(1,128)}) custom-call(bf16[128,512]{1,0:T(8,128)(2,1)S(1)} %get-tuple-element.53.cot_ref, bf16[128,512]{1,0:T(8,128)(2,1)S(1)} %get-tuple-element.52.refs_0_.node_ref, f32[1,512]{1,0:T(1,128)S(1)} %get-tuple-element.54.gain_ref, ...), custom_call_target="tpu_custom_call" | custom-call | flops 100000000 | bytes 1000000 | tf_op jit(solution)/shard_map/pallas_call | solution.py:407
  47.8 0.2 collective-permute-done.20.refs_7_
  47.9 1.6 %collective-permute-done.19.refs_6_ = bf16[192,256]{1,0:T(8,128)(2,1)S(1)} collective-permute-done((bf16[192,256]{1,0:T(8,128)(2,1)S(1)}, bf16[192,256]{1,0:T(8,128)(2,1)S(1)}, u32[]{:S(2)}, u32[]{:S(2)}) %collective-permute-start.19) | collective-permute-done | bytes 98336 | tf_op jit(solution)/shard_map/ppermute | solution.py:425
  49.6 1.1 %collective-permute-done.18.refs_5_ = bf16[192,256]{1,0:T(8,128)(2,1)S(1)} collective-permute-done((bf16[192,256]{1,0:T(8,128)(2,1)S(1)}, bf16[192,256]{1,0:T(8,128)(2,1)S(1)}, u32[]{:S(2)}, u32[]{:S(2)}) %collective-permute-start.18) | collective-permute-done | bytes 98336 | tf_op jit(solution)/shard_map/ppermute | solution.py:425
  50.6 1.2 %shard_map.173 = (f32[512,256]{1,0:T(8,128)}, f32[512,256]{1,0:T(8,128)}, f32[256,512]{1,0:T(8,128)}) custom-call(bf16[192,256]{1,0:T(8,128)(2,1)S(1)} %get-tuple-element.91.refs_0_, bf16[192,256]{1,0:T(8,128)(2,1)S(1)} %collective-permute-done.14.refs_1_, bf16[192,256]{1,0:T(8,128)(2,1)S(1)} %collective-permute-done.15.refs_2_, ...), custom_call_target="tpu_custom_call" | custom-call | flops 100000000 | bytes 1000000 | tf_op jit(solution)/shard_map/pallas_call | solution.py:407
  (5 shorter events, 0.2 us)
Async XLA Ops:
  1.8 9.0 %collective-permute-start.2 = (bf16[64,512]{1,0:T(8,128)(2,1)S(1)}, bf16[64,512]{1,0:T(8,128)(2,1)S(1)}, u32[]{:S(2)}, u32[]{:S(2)}) collective-permute-start(bf16[64,512]{1,0:T(8,128)(2,1)S(1)} %get-tuple-element.64), channel_id=1, source_target_pairs={{0,2},{2,0},{1,3},{3,1},{4,6},{6,4},{5,7},{7,5},{8,10},{10,8},{9,1... | collective-permute-start | bytes 196616 | tf_op jit(solution)/shard_map/ppermute | solution.py:420
  4.8 5.9 %collective-permute-start = (bf16[32,512]{1,0:T(8,128)(2,1)S(1)}, bf16[32,512]{1,0:T(8,128)(2,1)S(1)}, u32[]{:S(2)}, u32[]{:S(2)}) collective-permute-start(bf16[32,512]{1,0:T(8,128)(2,1)S(1)} %get-tuple-element.62), channel_id=1, source_target_pairs={{0,4},{4,8},{8,12},{12,0},{1,5},{5,9},{9,13},{13,1},{2,6},{6,10},{... | collective-permute-start | bytes 98312 | tf_op jit(solution)/shard_map/ppermute | solution.py:420
  6.4 4.4 %collective-permute-start.1 = (bf16[32,512]{1,0:T(8,128)(2,1)S(1)}, bf16[32,512]{1,0:T(8,128)(2,1)S(1)}, u32[]{:S(2)}, u32[]{:S(2)}) collective-permute-start(bf16[32,512]{1,0:T(8,128)(2,1)S(1)} %get-tuple-element.63), channel_id=1, source_target_pairs={{0,12},{4,0},{8,4},{12,8},{1,13},{5,1},{9,5},{13,9},{2,14},{6,2},{... | collective-permute-start | bytes 98312 | tf_op jit(solution)/shard_map/ppermute | solution.py:420
  11.6 1.4 %collective-permute-start.3 = (bf16[128,512]{1,0:T(8,128)(2,1)S(1)}, bf16[128,512]{1,0:T(8,128)(2,1)S(1)}, u32[]{:S(2)}, u32[]{:S(2)}) collective-permute-start(bf16[128,512]{1,0:T(8,128)(2,1)S(1)} %get-tuple-element.67.own_ref), channel_id=1, source_target_pairs={{0,1},{1,0},{2,3},{3,2},{4,5},{5,4},{6,7},{7,6},{8,9},{9,8},{10,11... | collective-permute-start | bytes 393224 | tf_op jit(solution)/shard_map/ppermute | solution.py:420
  14.4 7.3 %collective-permute-start.6 = (bf16[336,256]{1,0:T(8,128)(2,1)S(1)}, bf16[336,256]{1,0:T(8,128)(2,1)S(1)}, u32[]{:S(2)}, u32[]{:S(2)}) collective-permute-start(bf16[336,256]{1,0:T(8,128)(2,1)S(1)} %get-tuple-element.75), channel_id=1, source_target_pairs={{0,2},{2,0},{1,3},{3,1},{4,6},{6,4},{5,7},{7,5},{8,10},{10,8},{9,1... | collective-permute-start | bytes 516104 | tf_op jit(solution)/shard_map/ppermute | solution.py:425
  14.9 10.5 %collective-permute-start.10 = (bf16[256,256]{1,0:T(8,128)(2,1)S(1)}, bf16[256,256]{1,0:T(8,128)(2,1)S(1)}, u32[]{:S(2)}, u32[]{:S(2)}) collective-permute-start(bf16[256,256]{1,0:T(8,128)(2,1)S(1)} %get-tuple-element.79), channel_id=1, source_target_pairs={{0,2},{2,0},{1,3},{3,1},{4,6},{6,4},{5,7},{7,5},{8,10},{10,8},{9,1... | collective-permute-start | bytes 393224 | tf_op jit(solution)/shard_map/ppermute | solution.py:425
  16.5 9.4 %collective-permute-start.12 = (bf16[64,512]{1,0:T(8,128)(2,1)S(1)}, bf16[64,512]{1,0:T(8,128)(2,1)S(1)}, u32[]{:S(2)}, u32[]{:S(2)}) collective-permute-start(bf16[64,512]{1,0:T(8,128)(2,1)S(1)} %get-tuple-element.84), channel_id=1, source_target_pairs={{0,8},{4,12},{8,0},{12,4},{1,9},{5,13},{9,1},{13,5},{2,10},{6,14},... | collective-permute-start | bytes 196616 | tf_op jit(solution)/shard_map/ppermute | solution.py:425
  18.7 9.4 %collective-permute-start.4 = (bf16[80,512]{1,0:T(8,128)(2,1)S(1)}, bf16[80,512]{1,0:T(8,128)(2,1)S(1)}, u32[]{:S(2)}, u32[]{:S(2)}) collective-permute-start(bf16[80,512]{1,0:T(8,128)(2,1)S(1)} %get-tuple-element.73), channel_id=1, source_target_pairs={{0,12},{4,8},{8,4},{12,0},{1,13},{5,9},{9,5},{13,1},{2,14},{6,10},... | collective-permute-start | bytes 245768 | tf_op jit(solution)/shard_map/ppermute | solution.py:425
  20.1 7.9 %collective-permute-start.5 = (bf16[80,512]{1,0:T(8,128)(2,1)S(1)}, bf16[80,512]{1,0:T(8,128)(2,1)S(1)}, u32[]{:S(2)}, u32[]{:S(2)}) collective-permute-start(bf16[80,512]{1,0:T(8,128)(2,1)S(1)} %get-tuple-element.74), channel_id=1, source_target_pairs={{0,4},{4,0},{8,12},{12,8},{1,5},{5,1},{9,13},{13,9},{2,6},{6,2},{1... | collective-permute-start | bytes 245768 | tf_op jit(solution)/shard_map/ppermute | solution.py:425
  21.8 6.8 %collective-permute-start.8 = (bf16[144,256]{1,0:T(8,128)(2,1)S(1)}, bf16[144,256]{1,0:T(8,128)(2,1)S(1)}, u32[]{:S(2)}, u32[]{:S(2)}) collective-permute-start(bf16[144,256]{1,0:T(8,128)(2,1)S(1)} %get-tuple-element.77), channel_id=1, source_target_pairs={{0,12},{4,8},{8,4},{12,0},{1,13},{5,9},{9,5},{13,1},{2,14},{6,10},... | collective-permute-start | bytes 221192 | tf_op jit(solution)/shard_map/ppermute | solution.py:425
  25.4 7.1 %collective-permute-start.9 = (bf16[144,256]{1,0:T(8,128)(2,1)S(1)}, bf16[144,256]{1,0:T(8,128)(2,1)S(1)}, u32[]{:S(2)}, u32[]{:S(2)}) collective-permute-start(bf16[144,256]{1,0:T(8,128)(2,1)S(1)} %get-tuple-element.78), channel_id=1, source_target_pairs={{0,8},{4,12},{8,0},{12,4},{1,9},{5,13},{9,1},{13,5},{2,10},{6,14},... | collective-permute-start | bytes 221192 | tf_op jit(solution)/shard_map/ppermute | solution.py:425
  25.9 6.6 %collective-permute-start.11 = (bf16[144,256]{1,0:T(8,128)(2,1)S(1)}, bf16[144,256]{1,0:T(8,128)(2,1)S(1)}, u32[]{:S(2)}, u32[]{:S(2)}) collective-permute-start(bf16[144,256]{1,0:T(8,128)(2,1)S(1)} %get-tuple-element.82), channel_id=1, source_target_pairs={{0,4},{4,0},{8,12},{12,8},{1,5},{5,1},{9,13},{13,9},{2,6},{6,2},{1... | collective-permute-start | bytes 221192 | tf_op jit(solution)/shard_map/ppermute | solution.py:425
  28.6 4.0 %collective-permute-start.13 = (bf16[64,256]{1,0:T(8,128)(2,1)S(1)}, bf16[64,256]{1,0:T(8,128)(2,1)S(1)}, u32[]{:S(2)}, u32[]{:S(2)}) collective-permute-start(bf16[64,256]{1,0:T(8,128)(2,1)S(1)} %get-tuple-element.87), channel_id=1, source_target_pairs={{0,2},{2,0},{1,3},{3,1},{4,6},{6,4},{5,7},{7,5},{8,10},{10,8},{9,1... | collective-permute-start | bytes 98312 | tf_op jit(solution)/shard_map/ppermute | solution.py:425
  32.6 7.1 %collective-permute-start.17 = (bf16[192,256]{1,0:T(8,128)(2,1)S(1)}, bf16[192,256]{1,0:T(8,128)(2,1)S(1)}, u32[]{:S(2)}, u32[]{:S(2)}) collective-permute-start(bf16[192,256]{1,0:T(8,128)(2,1)S(1)} %get-tuple-element.91.refs_0_), channel_id=1, source_target_pairs={{0,2},{2,0},{1,3},{3,1},{4,6},{6,4},{5,7},{7,5},{8,10},{10,8},{9,1... | collective-permute-start | bytes 294920 | tf_op jit(solution)/shard_map/ppermute | solution.py:425
  33.2 10.0 %collective-permute-start.16 = (bf16[192,256]{1,0:T(8,128)(2,1)S(1)}, bf16[192,256]{1,0:T(8,128)(2,1)S(1)}, u32[]{:S(2)}, u32[]{:S(2)}) collective-permute-start(bf16[192,256]{1,0:T(8,128)(2,1)S(1)} %get-tuple-element.91.refs_0_), channel_id=1, source_target_pairs={{0,8},{4,12},{8,0},{12,4},{1,9},{5,13},{9,1},{13,5},{2,10},{6,14},... | collective-permute-start | bytes 294920 | tf_op jit(solution)/shard_map/ppermute | solution.py:425
  38.2 6.7 %collective-permute-start.15 = (bf16[192,256]{1,0:T(8,128)(2,1)S(1)}, bf16[192,256]{1,0:T(8,128)(2,1)S(1)}, u32[]{:S(2)}, u32[]{:S(2)}) collective-permute-start(bf16[192,256]{1,0:T(8,128)(2,1)S(1)} %get-tuple-element.91.refs_0_), channel_id=1, source_target_pairs={{0,4},{4,0},{8,12},{12,8},{1,5},{5,1},{9,13},{13,9},{2,6},{6,2},{1... | collective-permute-start | bytes 294920 | tf_op jit(solution)/shard_map/ppermute | solution.py:425
  38.2 7.1 %collective-permute-start.14 = (bf16[192,256]{1,0:T(8,128)(2,1)S(1)}, bf16[192,256]{1,0:T(8,128)(2,1)S(1)}, u32[]{:S(2)}, u32[]{:S(2)}) collective-permute-start(bf16[192,256]{1,0:T(8,128)(2,1)S(1)} %get-tuple-element.91.refs_0_), channel_id=1, source_target_pairs={{0,12},{4,8},{8,4},{12,0},{1,13},{5,9},{9,5},{13,1},{2,14},{6,10},... | collective-permute-start | bytes 294920 | tf_op jit(solution)/shard_map/ppermute | solution.py:425
  39.7 7.3 %collective-permute-start.7 = (bf16[128,512]{1,0:T(8,128)(2,1)S(1)}, bf16[128,512]{1,0:T(8,128)(2,1)S(1)}, u32[]{:S(2)}, u32[]{:S(2)}) collective-permute-start(bf16[128,512]{1,0:T(8,128)(2,1)S(1)} %shard_map.166.refs_6_.own_ref), channel_id=1, source_target_pairs={{0,1},{1,0},{2,3},{3,2},{4,5},{5,4},{6,7},{7,6},{8,9},{9,8},{10,11... | collective-permute-start | bytes 393224 | tf_op jit(solution)/shard_map/ppermute | solution.py:420
  43.3 4.7 %collective-permute-start.20 = (bf16[192,256]{1,0:T(8,128)(2,1)S(1)}, bf16[192,256]{1,0:T(8,128)(2,1)S(1)}, u32[]{:S(2)}, u32[]{:S(2)}) collective-permute-start(bf16[192,256]{1,0:T(8,128)(2,1)S(1)} %shard_map.172), channel_id=1, source_target_pairs={{0,2},{2,0},{1,3},{3,1},{4,6},{6,4},{5,7},{7,5},{8,10},{10,8},{9,1... | collective-permute-start | bytes 294920 | tf_op jit(solution)/shard_map/ppermute | solution.py:425
  44.9 4.6 %collective-permute-start.19 = (bf16[192,256]{1,0:T(8,128)(2,1)S(1)}, bf16[192,256]{1,0:T(8,128)(2,1)S(1)}, u32[]{:S(2)}, u32[]{:S(2)}) collective-permute-start(bf16[192,256]{1,0:T(8,128)(2,1)S(1)} %collective-permute-done.15.refs_2_), channel_id=1, source_target_pairs={{0,2},{2,0},{1,3},{3,1},{4,6},{6,4},{5,7},{7,5},{8,10},{10,8},{9,1... | collective-permute-start | bytes 294920 | tf_op jit(solution)/shard_map/ppermute | solution.py:425
  45.4 5.2 %collective-permute-start.18 = (bf16[192,256]{1,0:T(8,128)(2,1)S(1)}, bf16[192,256]{1,0:T(8,128)(2,1)S(1)}, u32[]{:S(2)}, u32[]{:S(2)}) collective-permute-start(bf16[192,256]{1,0:T(8,128)(2,1)S(1)} %collective-permute-done.14.refs_1_), channel_id=1, source_target_pairs={{0,2},{2,0},{1,3},{3,1},{4,6},{6,4},{5,7},{7,5},{8,10},{10,8},{9,1... | collective-permute-start | bytes 294920 | tf_op jit(solution)/shard_map/ppermute | solution.py:425

commit v8 on v7

--- a/solution.py
+++ b/solution.py
@@ -183,7 +183,7 @@
     back = by_source_low[rows:]
 
     if paired:
-        far_send_ref, far_keep_ref, near_send_ref, near_keep_ref, *out_refs = message_refs
+        sends, keeps, out_refs = message_refs[:3], message_refs[3:6], message_refs[6:]
         sub = lax.axis_index("sub")
         mesh = lax.axis_index("mesh")
         lines = len(out_refs)
@@ -192,13 +192,13 @@
         pair_scratch[0] = jnp.where(first, dst_part, src_part)
         pair_scratch[1] = jnp.where(first, src_part, dst_part)
         strip = width // lines
-        for slot, far_ref, near_ref in ((0, far_send_ref, near_send_ref), (1, far_keep_ref, near_keep_ref)):
-            for at, k in enumerate((3, 2, 1, 0)):
+        for slot, (far_ref, one_ref, zero_ref) in enumerate((sends, keeps)):
+            places = ((far_ref, 0, 3), (far_ref, strip, 2), (one_ref, 0, 1), (zero_ref, 0, 0))
+            for ref, at, k in places:
                 start = pl.multiple_of((mesh ^ k) * strip, strip)
-                ref = far_ref if at < 2 else near_ref
-                ref[at % 2 * strip : (at % 2 + 1) * strip, :] = pair_scratch[slot, pl.ds(start, strip), :]
-            far_ref[2 * strip : 2 * strip + TAIL, :] = tail
-        far_send_ref[2 * strip + TAIL :, :] = back[2 * halo :]
+                ref[at : at + strip, :] = pair_scratch[slot, pl.ds(start, strip), :]
+            far_ref[2 * strip :, :] = tail
+        sends[2][strip:, :] = back[2 * halo :]
         back_scratch[...] = back[: 2 * halo]
         out_scratch[...] = out_part
         strip = hid // len(out_refs)
@@ -255,8 +255,7 @@
 
 
 def far_kernel(arrived_ref, keep_ref, three_ref, two_ref, tail_ref):
-    full = keep_ref.shape[0]
-    total = keep_ref[...].astype(f32) + arrived_ref[0:full, :].astype(f32)
+    total = keep_ref[...].astype(f32) + arrived_ref[...].astype(f32)
     strip = three_ref.shape[0] - TAIL
     tail = total[2 * strip :]
     tail = tail_of([tail[at : at + 1] + tail[at + 1 : at + 2] for at in range(0, 6, 2)])
@@ -266,13 +265,10 @@
     tail_ref[...] = tail
 
 
-def near_kernel(arrived_ref, keep_ref, tail_ref, one_ref, zero_ref):
-    full = keep_ref.shape[0]
-    total = (keep_ref[...].astype(f32) + arrived_ref[...].astype(f32)).astype(bf16)
-    strip = full // 2
-    for k, ref in enumerate((one_ref, zero_ref)):
-        ref[0:strip, :] = total[k * strip : (k + 1) * strip]
-        ref[strip:, :] = tail_ref[...]
+def near_kernel(arrived_ref, keep_ref, tail_ref, one_ref):
+    strip = keep_ref.shape[0]
+    one_ref[0:strip, :] = (keep_ref[...].astype(f32) + arrived_ref[...].astype(f32)).astype(bf16)
+    one_ref[strip:, :] = tail_ref[...]
 
 
 def line_kernel(*refs):
@@ -286,14 +282,15 @@
 
 
 def own_kernel(*refs):
-    *terms, out_keep_ref, out_arrived_ref, _, own_ref, tail_ref = refs
-    total = tree([r[...].astype(f32) for r in terms])
-    strip = own_ref.shape[0] - out_keep_ref.shape[0]
-    own_ref[0:strip, :] = total[:strip].astype(bf16)
+    *terms, keep_ref, arrived_ref, vectors_ref, out_keep_ref, out_arrived_ref, _, own_ref, tail_ref = refs
+    strip = keep_ref.shape[0]
+    zero = (keep_ref[...].astype(f32) + arrived_ref[0:strip, :].astype(f32)).astype(bf16)
+    total = tree([r[0:strip, :].astype(f32) for r in terms] + [zero.astype(f32)])
+    own_ref[0:strip, :] = total.astype(bf16)
     own_ref[strip:, :] = (
         out_keep_ref[...].astype(f32) + out_arrived_ref[...].astype(f32)
     ).astype(bf16)
-    tail_ref[...] = total[strip:]
+    tail_ref[...] = tree([r[strip:, :].astype(f32) for r in terms] + [vectors_ref[...].astype(f32)])
 
 
 def write_vectors(tail, bias_ref, gain_ref):
@@ -426,26 +423,27 @@
 
 
 def paired_sums(messages, lines, strip, narrow, width, hid, node_terms):
-    far_send, far_keep, near_send, near_keep, *outs = messages
+    sends, keeps, outs = messages[:3], messages[3:6], messages[6:]
     order = range(lines - 1, 0, -1)
     block = shape((strip + TAIL, hid), bf16)
-    far = across(far_send, "sub", 1)
+    far = across(sends[0], "sub", 1)
     out_terms = {k: across(outs[k], "mesh", k) for k in order}
-    near = across(near_send, "sub", 1)
+    one = across(sends[1], "sub", 1)
+    zero = across(sends[2], "sub", 1)
     line = {}
-    line[3], line[2], tail = call(far_kernel, [block, block, shape((TAIL, hid), bf16)], far, far_keep)
-    line[1], line[0] = call(near_kernel, [block, block], near, near_keep, tail)
+    line[3], line[2], tail = call(far_kernel, [block, block, shape((TAIL, hid), bf16)], far, keeps[0])
+    line[1] = call(near_kernel, block, one, keeps[1], tail)
     line_terms = {k: across(line[k], "mesh", k) for k in order}
     out_send, out_keep = call(
         line_kernel,
         [shape((narrow, hid), bf16)] * 2,
-        *[out_terms[k] for k in order], outs[0], line_terms[3],
-    )
-    node_part = node_terms(out_terms[3], out_terms[1], far)
+        *[out_terms[k] for k in order], outs[0], line[1],
+    )
+    node_part = node_terms(out_terms[3], out_terms[1], zero)
     own, tail = call(
         own_kernel,
         [shape((strip + narrow, hid), bf16), shape((TAIL, hid), f32)],
-        *[line_terms[k] for k in (3, 2, 1)], line[0], out_keep, across(out_send, "sub", 1),
+        *[line_terms[k] for k in order], keeps[2], zero, tail, out_keep, across(out_send, "sub", 1),
         node_part,
     )
     mine = {k: across(own, "mesh", k) for k in order}
@@ -538,8 +536,8 @@
     if paired:
         strip = width // lines
         narrow = hid // lines
-        message_shapes = [shape((2 * strip + TAIL + 2 * halo, hid), bf16), shape((2 * strip + TAIL, hid), bf16)]
-        message_shapes += [shape((2 * strip, hid), bf16)] * 2
+        rows_of = (2 * strip + TAIL, strip, strip + 2 * halo, 2 * strip + TAIL, strip, strip)
+        message_shapes = [shape((n, hid), bf16) for n in rows_of]
         message_shapes += [shape((narrow + k % 2 * (halo // 2), width), bf16) for k in range(lines)]
     else:
         message_shapes = [shape((peers, chunk + TAIL, hid), bf16)]

time: 52 us -> 49.5 us (0.952)
  starting transfers between devices: 30.2 us -> 28.7 us
  waiting for transfers between devices: 12.9 us -> 11.8 us
    ppermute x16 -> x17, starting transfers between devices: 23.3 us -> 21.8 us  [across(): return lax.ppermute(x, axis, [(i, i ^ k) for i in range(count)])]
    ppermute x16 -> x17, waiting for transfers between devices: 11.5 us -> 10.4 us  [across(): return lax.ppermute(x, axis, [(i, i ^ k) for i in range(count)])]
  transfers between devices with their start and end apart: 21 -> 22, of which waited for: 10 -> 8; matrix products, arithmetic and copies ran while one was open for 0% -> 0% of each run, Pallas kernels for 7% -> 7%
where the time goes in v8:
time: 49.5 us; the launch traced here: 49.4 us
  starting transfers between devices  28.7 us (58%)
  waiting for transfers between devices  11.8 us (24%)
  Pallas kernels  8.08 us (16%)
  between operations  0.72 us (1%)
    ppermute x17, starting transfers between devices, across(): return lax.ppermute(x, axis, [(i, i ^ k) for i in range(count)])  21.8 us
    ppermute x17, waiting for transfers between devices, across(): return lax.ppermute(x, axis, [(i, i ^ k) for i in range(count)])  10.4 us
    pallas_call x12, Pallas kernels, call(): pl.pallas_call(kernel, out_shape=outs, in_specs=specs or [VMEM] * len(arg...  8.08 us
    ppermute x5, starting transfers between devices, shifted(): return lax.ppermute(x, axis, [(i, (i + by) % count) for i in range(count)])  6.9 us
    ppermute x5, waiting for transfers between devices, shifted(): return lax.ppermute(x, axis, [(i, (i + by) % count) for i in range(count)])  1.38 us
  transfers between devices with their start and end apart: 22, of which 8 were waited for; matrix products, arithmetic and copies ran while one was open for 0% of the time, Pallas kernels for 7%

profile of v8, /device:TPU:0, one launch (start us, length us, event | category | flops | bytes accessed | tf_op | source)
XLA Modules:
  0.0 49.4 jit_solution(7145166322602066844)
XLA Ops:
  0.6 1.2 %shard_map.162 = (bf16[128,512]{1,0:T(8,128)(2,1)S(1)}, s32[1,4,32]{2,1,0:T(4,128)S(1)}, bf16[32,512]{1,0:T(8,128)(2,1)S(1)}, bf16[32,512]{1,0:T(8,128)(2,1)S(1)}, bf16[64,512]{1,0:T(8,128)(2,1)S(1)}) custom-call(bf16[128,512]{1,0:T(8,128)(2,1)} %node_hbm.1, s32[1,4,32]{2,1,0:T(4,128)} %send_hbm.1), custom_call_target="tpu_custom_call" | custom-call | flops 100000000 | bytes 1000000 | tf_op jit(solution)/shard_map/pallas_call | solution.py:404
  1.8 3.0 %collective-permute-start.2 = (bf16[64,512]{1,0:T(8,128)(2,1)S(1)}, bf16[64,512]{1,0:T(8,128)(2,1)S(1)}, u32[]{:S(2)}, u32[]{:S(2)}) collective-permute-start(bf16[64,512]{1,0:T(8,128)(2,1)S(1)} %get-tuple-element.64), channel_id=1, source_target_pairs={{0,2},{2,0},{1,3},{3,1},{4,6},{6,4},{5,7},{7,5},{8,10},{10,8},{9,1... | collective-permute-start | bytes 196616 | tf_op jit(solution)/shard_map/ppermute | solution.py:417
  4.8 1.6 %collective-permute-start = (bf16[32,512]{1,0:T(8,128)(2,1)S(1)}, bf16[32,512]{1,0:T(8,128)(2,1)S(1)}, u32[]{:S(2)}, u32[]{:S(2)}) collective-permute-start(bf16[32,512]{1,0:T(8,128)(2,1)S(1)} %get-tuple-element.62), channel_id=1, source_target_pairs={{0,4},{4,8},{8,12},{12,0},{1,5},{5,9},{9,13},{13,1},{2,6},{6,10},{... | collective-permute-start | bytes 98312 | tf_op jit(solution)/shard_map/ppermute | solution.py:417
  6.4 2.2 %collective-permute-start.1 = (bf16[32,512]{1,0:T(8,128)(2,1)S(1)}, bf16[32,512]{1,0:T(8,128)(2,1)S(1)}, u32[]{:S(2)}, u32[]{:S(2)}) collective-permute-start(bf16[32,512]{1,0:T(8,128)(2,1)S(1)} %get-tuple-element.63), channel_id=1, source_target_pairs={{0,12},{4,0},{8,4},{12,8},{1,13},{5,1},{9,5},{13,9},{2,14},{6,2},{... | collective-permute-start | bytes 98312 | tf_op jit(solution)/shard_map/ppermute | solution.py:417
  8.6 2.1 %shard_map.163 = (f32[512,256]{1,0:T(8,128)S(1)}, bf16[512,128]{1,0:T(8,128)(2,1)S(1)}, bf16[128,512]{1,0:T(8,128)(2,1)S(1)}, bf16[512,128]{1,0:T(8,128)(2,1)S(1...) custom-call(bf16[128,512]{1,0:T(8,128)(2,1)S(1)} %get-tuple-element., ...), custom_call_target="tpu_custom_call" | custom-call | flops 100000000 | bytes 1000000 | tf_op jit(solution)/shard_map/pallas_call | solution.py:404
  10.7 0.0 collective-permute-done.rest_0_
  10.8 0.0 collective-permute-done.1.rest_1_
  10.8 0.0 collective-permute-done.2.rest_2_
  10.8 0.9 %shard_map.164 = (f32[512,256]{1,0:T(8,128)S(1)}, bf16[128,256]{1,0:T(8,128)(2,1)S(1)}, bf16[128,512]{1,0:T(8,128)(2,1)S(1)}) custom-call(f32[512,256]{1,0:T(8,128)S(1)} %get-tuple-element.59.pre_ref, bf16[512,128]{1,0:T(8,128)(2,1)S(1)} %get-tuple-element.60.pick_ref, bf16[128,512]{1,0:T(8,128)(2,1)S(1)} %get-tuple-element.55.collect_ref, ...), custom_call_target="tpu_custom_call" | custom-call | flops 100000000 | bytes 1000000 | tf_op jit(solution)/shard_map/pallas_call | solution.py:404
  11.6 0.1 collective-permute-start.3
  11.7 1.3 %collective-permute-done.3.other_ref = bf16[128,512]{1,0:T(8,128)(2,1)S(1)} collective-permute-done((bf16[128,512]{1,0:T(8,128)(2,1)S(1)}, bf16[128,512]{1,0:T(8,128)(2,1)S(1)}, u32[]{:S(2)}, u32[]{:S(2)}) %collective-permute-start.3) | collective-permute-done | bytes 131104 | tf_op jit(solution)/shard_map/ppermute | solution.py:417
  13.1 1.4 %shard_map.165 = (f32[128,512]{1,0:T(8,128)S(1)}, f32[128,256]{1,0:T(8,128)S(1)}, bf16[128,256]{1,0:T(8,128)(2,1)S(1)}, bf16[272,256]{1,0:T(8,128)(2,1)S(1)}, bf...) custom-call(bf16[128,512]{1,0:T(8,128)(2,1)S(1)} %get-tuple-element., ...), custom_call_target="tpu_custom_call" | custom-call | flops 100000000 | bytes 1000000 | tf_op jit(solution)/shard_map/pallas_call | solution.py:404
  14.4 0.5 collective-permute-start.8
  14.9 3.5 %collective-permute-start.4 = (bf16[80,512]{1,0:T(8,128)(2,1)S(1)}, bf16[80,512]{1,0:T(8,128)(2,1)S(1)}, u32[]{:S(2)}, u32[]{:S(2)}) collective-permute-start(bf16[80,512]{1,0:T(8,128)(2,1)S(1)} %get-tuple-element.73), channel_id=1, source_target_pairs={{0,12},{4,8},{8,4},{12,0},{1,13},{5,9},{9,5},{13,1},{2,14},{6,10},... | collective-permute-start | bytes 245768 | tf_op jit(solution)/shard_map/ppermute | solution.py:422
  18.4 1.7 %collective-permute-start.11 = (bf16[128,256]{1,0:T(8,128)(2,1)S(1)}, bf16[128,256]{1,0:T(8,128)(2,1)S(1)}, u32[]{:S(2)}, u32[]{:S(2)}) collective-permute-start(bf16[128,256]{1,0:T(8,128)(2,1)S(1)} %get-tuple-element.80), channel_id=1, source_target_pairs={{0,2},{2,0},{1,3},{3,1},{4,6},{6,4},{5,7},{7,5},{8,10},{10,8},{9,1... | collective-permute-start | bytes 196616 | tf_op jit(solution)/shard_map/ppermute | solution.py:422
  20.1 0.0 collective-permute-start.13
  20.1 0.8 %collective-permute-start.5 = (bf16[80,512]{1,0:T(8,128)(2,1)S(1)}, bf16[80,512]{1,0:T(8,128)(2,1)S(1)}, u32[]{:S(2)}, u32[]{:S(2)}) collective-permute-start(bf16[80,512]{1,0:T(8,128)(2,1)S(1)} %get-tuple-element.74), channel_id=1, source_target_pairs={{0,4},{4,0},{8,12},{12,8},{1,5},{5,1},{9,13},{13,9},{2,6},{6,2},{1... | collective-permute-start | bytes 245768 | tf_op jit(solution)/shard_map/ppermute | solution.py:422
  20.9 0.0 collective-permute-done.8.arrived_ref
  20.9 0.4 collective-permute-start.6
  21.4 1.7 %collective-permute-done.11.arrived_ref = bf16[128,256]{1,0:T(8,128)(2,1)S(1)} collective-permute-done((bf16[128,256]{1,0:T(8,128)(2,1)S(1)}, bf16[128,256]{1,0:T(8,128)(2,1)S(1)}, u32[]{:S(2)}, u32[]{:S(2)}) %collective-permute-start.11) | collective-permute-done | bytes 65568 | tf_op jit(solution)/shard_map/ppermute | solution.py:422
  23.1 2.2 %collective-permute-start.9 = (bf16[144,256]{1,0:T(8,128)(2,1)S(1)}, bf16[144,256]{1,0:T(8,128)(2,1)S(1)}, u32[]{:S(2)}, u32[]{:S(2)}) collective-permute-start(bf16[144,256]{1,0:T(8,128)(2,1)S(1)} %get-tuple-element.78), channel_id=1, source_target_pairs={{0,12},{4,8},{8,4},{12,0},{1,13},{5,9},{9,5},{13,1},{2,14},{6,10},... | collective-permute-start | bytes 221192 | tf_op jit(solution)/shard_map/ppermute | solution.py:422
  25.3 1.0 %collective-permute-done.13.refs_1_ = bf16[64,512]{1,0:T(8,128)(2,1)S(1)} collective-permute-done((bf16[64,512]{1,0:T(8,128)(2,1)S(1)}, bf16[64,512]{1,0:T(8,128)(2,1)S(1)}, u32[]{:S(2)}, u32[]{:S(2)}) %collective-permute-start.13) | collective-permute-done | bytes 65568 | tf_op jit(solution)/shard_map/ppermute | solution.py:422
  26.3 0.0 collective-permute-start.10
  26.3 0.0 collective-permute-done.4.three_ref.refs_0_
  26.3 1.8 %collective-permute-start.12 = (bf16[144,256]{1,0:T(8,128)(2,1)S(1)}, bf16[144,256]{1,0:T(8,128)(2,1)S(1)}, u32[]{:S(2)}, u32[]{:S(2)}) collective-permute-start(bf16[144,256]{1,0:T(8,128)(2,1)S(1)} %shard_map.168.refs_4_), channel_id=1, source_target_pairs={{0,4},{4,0},{8,12},{12,8},{1,5},{5,1},{9,13},{13,9},{2,6},{6,2},{1... | collective-permute-start | bytes 221192 | tf_op jit(solution)/shard_map/ppermute | solution.py:422
  28.0 0.0 collective-permute-done.5.one_ref.refs_2_
  28.1 1.7 %collective-permute-start.14 = (bf16[64,256]{1,0:T(8,128)(2,1)S(1)}, bf16[64,256]{1,0:T(8,128)(2,1)S(1)}, u32[]{:S(2)}, u32[]{:S(2)}) collective-permute-start(bf16[64,256]{1,0:T(8,128)(2,1)S(1)} %get-tuple-element.87), channel_id=1, source_target_pairs={{0,2},{2,0},{1,3},{3,1},{4,6},{6,4},{5,7},{7,5},{8,10},{10,8},{9,1... | collective-permute-start | bytes 98312 | tf_op jit(solution)/shard_map/ppermute | solution.py:422
  29.8 0.0 collective-permute-done.6.pair_ref.refs_4_
  29.8 0.4 shard_map.166.refs_8_.own_ref
  30.2 1.9 %collective-permute-done.14.refs_7_ = bf16[64,256]{1,0:T(8,128)(2,1)S(1)} collective-permute-done((bf16[64,256]{1,0:T(8,128)(2,1)S(1)}, bf16[64,256]{1,0:T(8,128)(2,1)S(1)}, u32[]{:S(2)}, u32[]{:S(2)}) %collective-permute-start.14) | collective-permute-done | bytes 32800 | tf_op jit(solution)/shard_map/ppermute | solution.py:422
  32.1 0.0 collective-permute-done.9.refs_0_
  32.1 0.0 collective-permute-done.10.refs_1_
  32.1 0.0 collective-permute-done.12.refs_2_
  32.1 0.1 shard_map.170
  32.2 1.7 %collective-permute-start.18 = (bf16[192,256]{1,0:T(8,128)(2,1)S(1)}, bf16[192,256]{1,0:T(8,128)(2,1)S(1)}, u32[]{:S(2)}, u32[]{:S(2)}) collective-permute-start(bf16[192,256]{1,0:T(8,128)(2,1)S(1)} %get-tuple-element.91.refs_0_), channel_id=1, source_target_pairs={{0,2},{2,0},{1,3},{3,1},{4,6},{6,4},{5,7},{7,5},{8,10},{10,8},{9,1... | collective-permute-start | bytes 294920 | tf_op jit(solution)/shard_map/ppermute | solution.py:422
  33.8 0.4 collective-permute-start.17
  34.2 1.7 %collective-permute-start.16 = (bf16[192,256]{1,0:T(8,128)(2,1)S(1)}, bf16[192,256]{1,0:T(8,128)(2,1)S(1)}, u32[]{:S(2)}, u32[]{:S(2)}) collective-permute-start(bf16[192,256]{1,0:T(8,128)(2,1)S(1)} %get-tuple-element.91.refs_0_), channel_id=1, source_target_pairs={{0,4},{4,0},{8,12},{12,8},{1,5},{5,1},{9,13},{13,9},{2,6},{6,2},{1... | collective-permute-start | bytes 294920 | tf_op jit(solution)/shard_map/ppermute | solution.py:422
  35.9 2.3 %collective-permute-start.15 = (bf16[192,256]{1,0:T(8,128)(2,1)S(1)}, bf16[192,256]{1,0:T(8,128)(2,1)S(1)}, u32[]{:S(2)}, u32[]{:S(2)}) collective-permute-start(bf16[192,256]{1,0:T(8,128)(2,1)S(1)} %get-tuple-element.91.refs_0_), channel_id=1, source_target_pairs={{0,12},{4,8},{8,4},{12,0},{1,13},{5,9},{9,5},{13,1},{2,14},{6,10},... | collective-permute-start | bytes 294920 | tf_op jit(solution)/shard_map/ppermute | solution.py:422
  38.2 0.0 collective-permute-start.7
  38.2 0.0 collective-permute-done.18._.refs_4_
  38.2 3.0 %collective-permute-done.17.strip_ref.refs_3_ = bf16[192,256]{1,0:T(8,128)(2,1)S(1)} collective-permute-done((bf16[192,256]{1,0:T(8,128)(2,1)S(1)}, bf16[192,256]{1,0:T(8,128)(2,1)S(1)}, u32[]{:S(2)}, u32[]{:S(2)}) %collective-permute-start.17) | collective-permute-done | bytes 98336 | tf_op jit(solution)/shard_map/ppermute | solution.py:422
  41.2 1.2 %collective-permute-start.21 = (bf16[192,256]{1,0:T(8,128)(2,1)S(1)}, bf16[192,256]{1,0:T(8,128)(2,1)S(1)}, u32[]{:S(2)}, u32[]{:S(2)}) collective-permute-start(bf16[192,256]{1,0:T(8,128)(2,1)S(1)} %shard_map.172), channel_id=1, source_target_pairs={{0,2},{2,0},{1,3},{3,1},{4,6},{6,4},{5,7},{7,5},{8,10},{10,8},{9,1... | collective-permute-start | bytes 294920 | tf_op jit(solution)/shard_map/ppermute | solution.py:422
  42.4 0.0 collective-permute-done.16.refs_2_
  42.4 0.9 %collective-permute-start.20 = (bf16[192,256]{1,0:T(8,128)(2,1)S(1)}, bf16[192,256]{1,0:T(8,128)(2,1)S(1)}, u32[]{:S(2)}, u32[]{:S(2)}) collective-permute-start(bf16[192,256]{1,0:T(8,128)(2,1)S(1)} %collective-permute-done.16.refs_2_), channel_id=1, source_target_pairs={{0,2},{2,0},{1,3},{3,1},{4,6},{6,4},{5,7},{7,5},{8,10},{10,8},{9,1... | collective-permute-start | bytes 294920 | tf_op jit(solution)/shard_map/ppermute | solution.py:422
  43.3 0.0 collective-permute-done.15.refs_1_
  43.3 1.2 %collective-permute-start.19 = (bf16[192,256]{1,0:T(8,128)(2,1)S(1)}, bf16[192,256]{1,0:T(8,128)(2,1)S(1)}, u32[]{:S(2)}, u32[]{:S(2)}) collective-permute-start(bf16[192,256]{1,0:T(8,128)(2,1)S(1)} %collective-permute-done.15.refs_1_), channel_id=1, source_target_pairs={{0,2},{2,0},{1,3},{3,1},{4,6},{6,4},{5,7},{7,5},{8,10},{10,8},{9,1... | collective-permute-start | bytes 294920 | tf_op jit(solution)/shard_map/ppermute | solution.py:422
  44.5 0.0 collective-permute-done.7.other_ref
  44.5 0.8 %shard_map.171 = (f32[128,512]{1,0:T(8,128)}, bf16[128,512]{1,0:T(8,128)(2,1)}, f32[1,256]{1,0:T(1,128)}, f32[1,512]{1,0:T(1,128)}) custom-call(bf16[128,512]{1,0:T(8,128)(2,1)S(1)} %get-tuple-element.53.cot_ref, bf16[128,512]{1,0:T(8,128)(2,1)S(1)} %get-tuple-element.52.refs_0_.node_ref, f32[1,512]{1,0:T(1,128)S(1)} %get-tuple-element.54.gain_ref, ...), custom_call_target="tpu_custom_call" | custom-call | flops 100000000 | bytes 1000000 | tf_op jit(solution)/shard_map/pallas_call | solution.py:404
  45.3 0.6 %collective-permute-done.21.refs_7_ = bf16[192,256]{1,0:T(8,128)(2,1)S(1)} collective-permute-done((bf16[192,256]{1,0:T(8,128)(2,1)S(1)}, bf16[192,256]{1,0:T(8,128)(2,1)S(1)}, u32[]{:S(2)}, u32[]{:S(2)}) %collective-permute-start.21) | collective-permute-done | bytes 98336 | tf_op jit(solution)/shard_map/ppermute | solution.py:422
  45.9 1.2 %collective-permute-done.20.refs_6_ = bf16[192,256]{1,0:T(8,128)(2,1)S(1)} collective-permute-done((bf16[192,256]{1,0:T(8,128)(2,1)S(1)}, bf16[192,256]{1,0:T(8,128)(2,1)S(1)}, u32[]{:S(2)}, u32[]{:S(2)}) %collective-permute-start.20) | collective-permute-done | bytes 98336 | tf_op jit(solution)/shard_map/ppermute | solution.py:422
  47.1 1.1 %collective-permute-done.19.refs_5_ = bf16[192,256]{1,0:T(8,128)(2,1)S(1)} collective-permute-done((bf16[192,256]{1,0:T(8,128)(2,1)S(1)}, bf16[192,256]{1,0:T(8,128)(2,1)S(1)}, u32[]{:S(2)}, u32[]{:S(2)}) %collective-permute-start.19) | collective-permute-done | bytes 98336 | tf_op jit(solution)/shard_map/ppermute | solution.py:422
  48.1 1.2 %shard_map.173 = (f32[512,256]{1,0:T(8,128)}, f32[512,256]{1,0:T(8,128)}, f32[256,512]{1,0:T(8,128)}) custom-call(bf16[192,256]{1,0:T(8,128)(2,1)S(1)} %get-tuple-element.91.refs_0_, bf16[192,256]{1,0:T(8,128)(2,1)S(1)} %collective-permute-done.15.refs_1_, bf16[192,256]{1,0:T(8,128)(2,1)S(1)} %collective-permute-done.16.refs_2_, ...), custom_call_target="tpu_custom_call" | custom-call | flops 100000000 | bytes 1000000 | tf_op jit(solution)/shard_map/pallas_call | solution.py:404
  (4 shorter events, 0.1 us)
Async XLA Ops:
  1.8 9.0 %collective-permute-start.2 = (bf16[64,512]{1,0:T(8,128)(2,1)S(1)}, bf16[64,512]{1,0:T(8,128)(2,1)S(1)}, u32[]{:S(2)}, u32[]{:S(2)}) collective-permute-start(bf16[64,512]{1,0:T(8,128)(2,1)S(1)} %get-tuple-element.64), channel_id=1, source_target_pairs={{0,2},{2,0},{1,3},{3,1},{4,6},{6,4},{5,7},{7,5},{8,10},{10,8},{9,1... | collective-permute-start | bytes 196616 | tf_op jit(solution)/shard_map/ppermute | solution.py:417
  4.8 5.9 %collective-permute-start = (bf16[32,512]{1,0:T(8,128)(2,1)S(1)}, bf16[32,512]{1,0:T(8,128)(2,1)S(1)}, u32[]{:S(2)}, u32[]{:S(2)}) collective-permute-start(bf16[32,512]{1,0:T(8,128)(2,1)S(1)} %get-tuple-element.62), channel_id=1, source_target_pairs={{0,4},{4,8},{8,12},{12,0},{1,5},{5,9},{9,13},{13,1},{2,6},{6,10},{... | collective-permute-start | bytes 98312 | tf_op jit(solution)/shard_map/ppermute | solution.py:417
  6.4 4.4 %collective-permute-start.1 = (bf16[32,512]{1,0:T(8,128)(2,1)S(1)}, bf16[32,512]{1,0:T(8,128)(2,1)S(1)}, u32[]{:S(2)}, u32[]{:S(2)}) collective-permute-start(bf16[32,512]{1,0:T(8,128)(2,1)S(1)} %get-tuple-element.63), channel_id=1, source_target_pairs={{0,12},{4,0},{8,4},{12,8},{1,13},{5,1},{9,5},{13,9},{2,14},{6,2},{... | collective-permute-start | bytes 98312 | tf_op jit(solution)/shard_map/ppermute | solution.py:417
  11.6 1.4 %collective-permute-start.3 = (bf16[128,512]{1,0:T(8,128)(2,1)S(1)}, bf16[128,512]{1,0:T(8,128)(2,1)S(1)}, u32[]{:S(2)}, u32[]{:S(2)}) collective-permute-start(bf16[128,512]{1,0:T(8,128)(2,1)S(1)} %get-tuple-element.67.own_ref), channel_id=1, source_target_pairs={{0,1},{1,0},{2,3},{3,2},{4,5},{5,4},{6,7},{7,6},{8,9},{9,8},{10,11... | collective-permute-start | bytes 393224 | tf_op jit(solution)/shard_map/ppermute | solution.py:417
  14.4 6.5 %collective-permute-start.8 = (bf16[272,256]{1,0:T(8,128)(2,1)S(1)}, bf16[272,256]{1,0:T(8,128)(2,1)S(1)}, u32[]{:S(2)}, u32[]{:S(2)}) collective-permute-start(bf16[272,256]{1,0:T(8,128)(2,1)S(1)} %get-tuple-element.76), channel_id=1, source_target_pairs={{0,2},{2,0},{1,3},{3,1},{4,6},{6,4},{5,7},{7,5},{8,10},{10,8},{9,1... | collective-permute-start | bytes 417800 | tf_op jit(solution)/shard_map/ppermute | solution.py:422
  14.9 11.4 %collective-permute-start.4 = (bf16[80,512]{1,0:T(8,128)(2,1)S(1)}, bf16[80,512]{1,0:T(8,128)(2,1)S(1)}, u32[]{:S(2)}, u32[]{:S(2)}) collective-permute-start(bf16[80,512]{1,0:T(8,128)(2,1)S(1)} %get-tuple-element.73), channel_id=1, source_target_pairs={{0,12},{4,8},{8,4},{12,0},{1,13},{5,9},{9,5},{13,1},{2,14},{6,10},... | collective-permute-start | bytes 245768 | tf_op jit(solution)/shard_map/ppermute | solution.py:422
  18.4 4.6 %collective-permute-start.11 = (bf16[128,256]{1,0:T(8,128)(2,1)S(1)}, bf16[128,256]{1,0:T(8,128)(2,1)S(1)}, u32[]{:S(2)}, u32[]{:S(2)}) collective-permute-start(bf16[128,256]{1,0:T(8,128)(2,1)S(1)} %get-tuple-element.80), channel_id=1, source_target_pairs={{0,2},{2,0},{1,3},{3,1},{4,6},{6,4},{5,7},{7,5},{8,10},{10,8},{9,1... | collective-permute-start | bytes 196616 | tf_op jit(solution)/shard_map/ppermute | solution.py:422
  20.1 6.1 %collective-permute-start.13 = (bf16[64,512]{1,0:T(8,128)(2,1)S(1)}, bf16[64,512]{1,0:T(8,128)(2,1)S(1)}, u32[]{:S(2)}, u32[]{:S(2)}) collective-permute-start(bf16[64,512]{1,0:T(8,128)(2,1)S(1)} %get-tuple-element.84), channel_id=1, source_target_pairs={{0,8},{4,12},{8,0},{12,4},{1,9},{5,13},{9,1},{13,5},{2,10},{6,14},... | collective-permute-start | bytes 196616 | tf_op jit(solution)/shard_map/ppermute | solution.py:422
  20.1 7.9 %collective-permute-start.5 = (bf16[80,512]{1,0:T(8,128)(2,1)S(1)}, bf16[80,512]{1,0:T(8,128)(2,1)S(1)}, u32[]{:S(2)}, u32[]{:S(2)}) collective-permute-start(bf16[80,512]{1,0:T(8,128)(2,1)S(1)} %get-tuple-element.74), channel_id=1, source_target_pairs={{0,4},{4,0},{8,12},{12,8},{1,5},{5,1},{9,13},{13,9},{2,6},{6,2},{1... | collective-permute-start | bytes 245768 | tf_op jit(solution)/shard_map/ppermute | solution.py:422
  20.9 8.8 %collective-permute-start.6 = (bf16[192,256]{1,0:T(8,128)(2,1)S(1)}, bf16[192,256]{1,0:T(8,128)(2,1)S(1)}, u32[]{:S(2)}, u32[]{:S(2)}) collective-permute-start(bf16[192,256]{1,0:T(8,128)(2,1)S(1)} %get-tuple-element.75), channel_id=1, source_target_pairs={{0,2},{2,0},{1,3},{3,1},{4,6},{6,4},{5,7},{7,5},{8,10},{10,8},{9,1... | collective-permute-start | bytes 294920 | tf_op jit(solution)/shard_map/ppermute | solution.py:422
  23.1 9.0 %collective-permute-start.9 = (bf16[144,256]{1,0:T(8,128)(2,1)S(1)}, bf16[144,256]{1,0:T(8,128)(2,1)S(1)}, u32[]{:S(2)}, u32[]{:S(2)}) collective-permute-start(bf16[144,256]{1,0:T(8,128)(2,1)S(1)} %get-tuple-element.78), channel_id=1, source_target_pairs={{0,12},{4,8},{8,4},{12,0},{1,13},{5,9},{9,5},{13,1},{2,14},{6,10},... | collective-permute-start | bytes 221192 | tf_op jit(solution)/shard_map/ppermute | solution.py:422
  26.3 5.8 %collective-permute-start.10 = (bf16[144,256]{1,0:T(8,128)(2,1)S(1)}, bf16[144,256]{1,0:T(8,128)(2,1)S(1)}, u32[]{:S(2)}, u32[]{:S(2)}) collective-permute-start(bf16[144,256]{1,0:T(8,128)(2,1)S(1)} %get-tuple-element.79), channel_id=1, source_target_pairs={{0,8},{4,12},{8,0},{12,4},{1,9},{5,13},{9,1},{13,5},{2,10},{6,14},... | collective-permute-start | bytes 221192 | tf_op jit(solution)/shard_map/ppermute | solution.py:422
  26.3 5.8 %collective-permute-start.12 = (bf16[144,256]{1,0:T(8,128)(2,1)S(1)}, bf16[144,256]{1,0:T(8,128)(2,1)S(1)}, u32[]{:S(2)}, u32[]{:S(2)}) collective-permute-start(bf16[144,256]{1,0:T(8,128)(2,1)S(1)} %shard_map.168.refs_4_), channel_id=1, source_target_pairs={{0,4},{4,0},{8,12},{12,8},{1,5},{5,1},{9,13},{13,9},{2,6},{6,2},{1... | collective-permute-start | bytes 221192 | tf_op jit(solution)/shard_map/ppermute | solution.py:422
  28.1 4.0 %collective-permute-start.14 = (bf16[64,256]{1,0:T(8,128)(2,1)S(1)}, bf16[64,256]{1,0:T(8,128)(2,1)S(1)}, u32[]{:S(2)}, u32[]{:S(2)}) collective-permute-start(bf16[64,256]{1,0:T(8,128)(2,1)S(1)} %get-tuple-element.87), channel_id=1, source_target_pairs={{0,2},{2,0},{1,3},{3,1},{4,6},{6,4},{5,7},{7,5},{8,10},{10,8},{9,1... | collective-permute-start | bytes 98312 | tf_op jit(solution)/shard_map/ppermute | solution.py:422
  32.2 6.1 %collective-permute-start.18 = (bf16[192,256]{1,0:T(8,128)(2,1)S(1)}, bf16[192,256]{1,0:T(8,128)(2,1)S(1)}, u32[]{:S(2)}, u32[]{:S(2)}) collective-permute-start(bf16[192,256]{1,0:T(8,128)(2,1)S(1)} %get-tuple-element.91.refs_0_), channel_id=1, source_target_pairs={{0,2},{2,0},{1,3},{3,1},{4,6},{6,4},{5,7},{7,5},{8,10},{10,8},{9,1... | collective-permute-start | bytes 294920 | tf_op jit(solution)/shard_map/ppermute | solution.py:422
  33.8 7.4 %collective-permute-start.17 = (bf16[192,256]{1,0:T(8,128)(2,1)S(1)}, bf16[192,256]{1,0:T(8,128)(2,1)S(1)}, u32[]{:S(2)}, u32[]{:S(2)}) collective-permute-start(bf16[192,256]{1,0:T(8,128)(2,1)S(1)} %get-tuple-element.91.refs_0_), channel_id=1, source_target_pairs={{0,8},{4,12},{8,0},{12,4},{1,9},{5,13},{9,1},{13,5},{2,10},{6,14},... | collective-permute-start | bytes 294920 | tf_op jit(solution)/shard_map/ppermute | solution.py:422
  34.2 8.2 %collective-permute-start.16 = (bf16[192,256]{1,0:T(8,128)(2,1)S(1)}, bf16[192,256]{1,0:T(8,128)(2,1)S(1)}, u32[]{:S(2)}, u32[]{:S(2)}) collective-permute-start(bf16[192,256]{1,0:T(8,128)(2,1)S(1)} %get-tuple-element.91.refs_0_), channel_id=1, source_target_pairs={{0,4},{4,0},{8,12},{12,8},{1,5},{5,1},{9,13},{13,9},{2,6},{6,2},{1... | collective-permute-start | bytes 294920 | tf_op jit(solution)/shard_map/ppermute | solution.py:422
  35.9 7.4 %collective-permute-start.15 = (bf16[192,256]{1,0:T(8,128)(2,1)S(1)}, bf16[192,256]{1,0:T(8,128)(2,1)S(1)}, u32[]{:S(2)}, u32[]{:S(2)}) collective-permute-start(bf16[192,256]{1,0:T(8,128)(2,1)S(1)} %get-tuple-element.91.refs_0_), channel_id=1, source_target_pairs={{0,12},{4,8},{8,4},{12,0},{1,13},{5,9},{9,5},{13,1},{2,14},{6,10},... | collective-permute-start | bytes 294920 | tf_op jit(solution)/shard_map/ppermute | solution.py:422
  38.2 6.3 %collective-permute-start.7 = (bf16[128,512]{1,0:T(8,128)(2,1)S(1)}, bf16[128,512]{1,0:T(8,128)(2,1)S(1)}, u32[]{:S(2)}, u32[]{:S(2)}) collective-permute-start(bf16[128,512]{1,0:T(8,128)(2,1)S(1)} %shard_map.166.refs_8_.own_ref), channel_id=1, source_target_pairs={{0,1},{1,0},{2,3},{3,2},{4,5},{5,4},{6,7},{7,6},{8,9},{9,8},{10,11... | collective-permute-start | bytes 393224 | tf_op jit(solution)/shard_map/ppermute | solution.py:417
  41.2 4.7 %collective-permute-start.21 = (bf16[192,256]{1,0:T(8,128)(2,1)S(1)}, bf16[192,256]{1,0:T(8,128)(2,1)S(1)}, u32[]{:S(2)}, u32[]{:S(2)}) collective-permute-start(bf16[192,256]{1,0:T(8,128)(2,1)S(1)} %shard_map.172), channel_id=1, source_target_pairs={{0,2},{2,0},{1,3},{3,1},{4,6},{6,4},{5,7},{7,5},{8,10},{10,8},{9,1... | collective-permute-start | bytes 294920 | tf_op jit(solution)/shard_map/ppermute | solution.py:422
  42.4 4.6 %collective-permute-start.20 = (bf16[192,256]{1,0:T(8,128)(2,1)S(1)}, bf16[192,256]{1,0:T(8,128)(2,1)S(1)}, u32[]{:S(2)}, u32[]{:S(2)}) collective-permute-start(bf16[192,256]{1,0:T(8,128)(2,1)S(1)} %collective-permute-done.16.refs_2_), channel_id=1, source_target_pairs={{0,2},{2,0},{1,3},{3,1},{4,6},{6,4},{5,7},{7,5},{8,10},{10,8},{9,1... | collective-permute-start | bytes 294920 | tf_op jit(solution)/shard_map/ppermute | solution.py:422
  43.3 4.8 %collective-permute-start.19 = (bf16[192,256]{1,0:T(8,128)(2,1)S(1)}, bf16[192,256]{1,0:T(8,128)(2,1)S(1)}, u32[]{:S(2)}, u32[]{:S(2)}) collective-permute-start(bf16[192,256]{1,0:T(8,128)(2,1)S(1)} %collective-permute-done.15.refs_1_), channel_id=1, source_target_pairs={{0,2},{2,0},{1,3},{3,1},{4,6},{6,4},{5,7},{7,5},{8,10},{10,8},{9,1... | collective-permute-start | bytes 294920 | tf_op jit(solution)/shard_map/ppermute | solution.py:422

commit v9 on v8

--- a/solution.py
+++ b/solution.py
@@ -300,10 +300,6 @@
         gain_ref[:, k * hid : (k + 1) * hid] = tail[2 + 2 * k : 3 + 2 * k] + tail[3 + 2 * k : 4 + 2 * k]
 
 
-def relay_kernel(strip_ref, _, out_ref):
-    out_ref[...] = strip_ref[...]
-
-
 def place_kernel(order, *refs):
     count = len(order)
     mine, theirs = refs[:count], refs[count : 2 * count]
@@ -449,8 +445,8 @@
     mine = {k: across(own, "mesh", k) for k in order}
     mine[0] = own
     theirs = {0: across(own, "sub", 1)}
-    first = call(relay_kernel, shape(own.shape, bf16), mine[2], theirs[0])
-    theirs |= {k: across(first if k == 2 else mine[k], "sub", 1) for k in order}
+    theirs[1] = across(theirs[0], "mesh", 1)
+    theirs |= {k: across(mine[k], "sub", 1) for k in (3, 2)}
     placed = (0, 3, 1, 2)
     grads = call(
         functools.partial(place_kernel, placed),

time: 49.5 us -> 49 us (0.990)
  starting transfers between devices: 28.7 us -> 27.8 us
  waiting for transfers between devices: 11.8 us -> 12.3 us
    ppermute x17, starting transfers between devices: 21.8 us -> 20.9 us  [across(): return lax.ppermute(x, axis, [(i, i ^ k) for i in range(count)])]
    pallas_call x12 -> x11, Pallas kernels: 8.08 us -> 8.07 us  [call(): pl.pallas_call(kernel, out_shape=outs, in_specs=specs or [VMEM] * len(arg...]
where the time goes in v9:
time: 49 us; the launch traced here: 48.9 us
  starting transfers between devices  27.8 us (57%)
  waiting for transfers between devices  12.3 us (25%)
  Pallas kernels  8.07 us (16%)
  between operations  0.72 us (1%)
    ppermute x17, starting transfers between devices, across(): return lax.ppermute(x, axis, [(i, i ^ k) for i in range(count)])  20.9 us
    ppermute x17, waiting for transfers between devices, across(): return lax.ppermute(x, axis, [(i, i ^ k) for i in range(count)])  10.9 us
    pallas_call x11, Pallas kernels, call(): pl.pallas_call(kernel, out_shape=outs, in_specs=specs or [VMEM] * len(arg...  8.07 us
    ppermute x5, starting transfers between devices, shifted(): return lax.ppermute(x, axis, [(i, (i + by) % count) for i in range(count)])  6.9 us
    ppermute x5, waiting for transfers between devices, shifted(): return lax.ppermute(x, axis, [(i, (i + by) % count) for i in range(count)])  1.38 us
  transfers between devices with their start and end apart: 22, of which 8 were waited for; matrix products, arithmetic and copies ran while one was open for 0% of the time, Pallas kernels for 7%

profile of v9, /device:TPU:0, one launch (start us, length us, event | category | flops | bytes accessed | tf_op | source)
XLA Modules:
  0.0 48.9 jit_solution(15054931183555942997)
XLA Ops:
  0.6 1.2 %shard_map.162 = (bf16[128,512]{1,0:T(8,128)(2,1)S(1)}, s32[1,4,32]{2,1,0:T(4,128)S(1)}, bf16[32,512]{1,0:T(8,128)(2,1)S(1)}, bf16[32,512]{1,0:T(8,128)(2,1)S(1)}, bf16[64,512]{1,0:T(8,128)(2,1)S(1)}) custom-call(bf16[128,512]{1,0:T(8,128)(2,1)} %node_hbm.1, s32[1,4,32]{2,1,0:T(4,128)} %send_hbm.1), custom_call_target="tpu_custom_call" | custom-call | flops 100000000 | bytes 1000000 | tf_op jit(solution)/shard_map/pallas_call | solution.py:400
  1.8 3.0 %collective-permute-start.2 = (bf16[64,512]{1,0:T(8,128)(2,1)S(1)}, bf16[64,512]{1,0:T(8,128)(2,1)S(1)}, u32[]{:S(2)}, u32[]{:S(2)}) collective-permute-start(bf16[64,512]{1,0:T(8,128)(2,1)S(1)} %get-tuple-element.64), channel_id=1, source_target_pairs={{0,2},{2,0},{1,3},{3,1},{4,6},{6,4},{5,7},{7,5},{8,10},{10,8},{9,1... | collective-permute-start | bytes 196616 | tf_op jit(solution)/shard_map/ppermute | solution.py:413
  4.8 1.6 %collective-permute-start = (bf16[32,512]{1,0:T(8,128)(2,1)S(1)}, bf16[32,512]{1,0:T(8,128)(2,1)S(1)}, u32[]{:S(2)}, u32[]{:S(2)}) collective-permute-start(bf16[32,512]{1,0:T(8,128)(2,1)S(1)} %get-tuple-element.62), channel_id=1, source_target_pairs={{0,4},{4,8},{8,12},{12,0},{1,5},{5,9},{9,13},{13,1},{2,6},{6,10},{... | collective-permute-start | bytes 98312 | tf_op jit(solution)/shard_map/ppermute | solution.py:413
  6.4 2.2 %collective-permute-start.1 = (bf16[32,512]{1,0:T(8,128)(2,1)S(1)}, bf16[32,512]{1,0:T(8,128)(2,1)S(1)}, u32[]{:S(2)}, u32[]{:S(2)}) collective-permute-start(bf16[32,512]{1,0:T(8,128)(2,1)S(1)} %get-tuple-element.63), channel_id=1, source_target_pairs={{0,12},{4,0},{8,4},{12,8},{1,13},{5,1},{9,5},{13,9},{2,14},{6,2},{... | collective-permute-start | bytes 98312 | tf_op jit(solution)/shard_map/ppermute | solution.py:413
  8.6 2.1 %shard_map.163 = (f32[512,256]{1,0:T(8,128)S(1)}, bf16[512,128]{1,0:T(8,128)(2,1)S(1)}, bf16[128,512]{1,0:T(8,128)(2,1)S(1)}, bf16[512,128]{1,0:T(8,128)(2,1)S(1...) custom-call(bf16[128,512]{1,0:T(8,128)(2,1)S(1)} %get-tuple-element., ...), custom_call_target="tpu_custom_call" | custom-call | flops 100000000 | bytes 1000000 | tf_op jit(solution)/shard_map/pallas_call | solution.py:400
  10.7 0.0 collective-permute-done.rest_0_
  10.8 0.0 collective-permute-done.1.rest_1_
  10.8 0.0 collective-permute-done.2.rest_2_
  10.8 0.9 %shard_map.164 = (f32[512,256]{1,0:T(8,128)S(1)}, bf16[128,256]{1,0:T(8,128)(2,1)S(1)}, bf16[128,512]{1,0:T(8,128)(2,1)S(1)}) custom-call(f32[512,256]{1,0:T(8,128)S(1)} %get-tuple-element.59.pre_ref, bf16[512,128]{1,0:T(8,128)(2,1)S(1)} %get-tuple-element.60.pick_ref, bf16[128,512]{1,0:T(8,128)(2,1)S(1)} %get-tuple-element.55.collect_ref, ...), custom_call_target="tpu_custom_call" | custom-call | flops 100000000 | bytes 1000000 | tf_op jit(solution)/shard_map/pallas_call | solution.py:400
  11.6 0.1 collective-permute-start.3
  11.7 1.3 %collective-permute-done.3.other_ref = bf16[128,512]{1,0:T(8,128)(2,1)S(1)} collective-permute-done((bf16[128,512]{1,0:T(8,128)(2,1)S(1)}, bf16[128,512]{1,0:T(8,128)(2,1)S(1)}, u32[]{:S(2)}, u32[]{:S(2)}) %collective-permute-start.3) | collective-permute-done | bytes 131104 | tf_op jit(solution)/shard_map/ppermute | solution.py:413
  13.1 1.4 %shard_map.165 = (f32[128,512]{1,0:T(8,128)S(1)}, f32[128,256]{1,0:T(8,128)S(1)}, bf16[128,256]{1,0:T(8,128)(2,1)S(1)}, bf16[272,256]{1,0:T(8,128)(2,1)S(1)}, bf...) custom-call(bf16[128,512]{1,0:T(8,128)(2,1)S(1)} %get-tuple-element., ...), custom_call_target="tpu_custom_call" | custom-call | flops 100000000 | bytes 1000000 | tf_op jit(solution)/shard_map/pallas_call | solution.py:400
  14.4 0.5 %collective-permute-start.8 = (bf16[272,256]{1,0:T(8,128)(2,1)S(1)}, bf16[272,256]{1,0:T(8,128)(2,1)S(1)}, u32[]{:S(2)}, u32[]{:S(2)}) collective-permute-start(bf16[272,256]{1,0:T(8,128)(2,1)S(1)} %get-tuple-element.76), channel_id=1, source_target_pairs={{0,2},{2,0},{1,3},{3,1},{4,6},{6,4},{5,7},{7,5},{8,10},{10,8},{9,1... | collective-permute-start | bytes 417800 | tf_op jit(solution)/shard_map/ppermute | solution.py:418
  14.9 3.5 %collective-permute-start.4 = (bf16[80,512]{1,0:T(8,128)(2,1)S(1)}, bf16[80,512]{1,0:T(8,128)(2,1)S(1)}, u32[]{:S(2)}, u32[]{:S(2)}) collective-permute-start(bf16[80,512]{1,0:T(8,128)(2,1)S(1)} %get-tuple-element.73), channel_id=1, source_target_pairs={{0,12},{4,8},{8,4},{12,0},{1,13},{5,9},{9,5},{13,1},{2,14},{6,10},... | collective-permute-start | bytes 245768 | tf_op jit(solution)/shard_map/ppermute | solution.py:418
  18.4 1.7 %collective-permute-start.11 = (bf16[128,256]{1,0:T(8,128)(2,1)S(1)}, bf16[128,256]{1,0:T(8,128)(2,1)S(1)}, u32[]{:S(2)}, u32[]{:S(2)}) collective-permute-start(bf16[128,256]{1,0:T(8,128)(2,1)S(1)} %get-tuple-element.80), channel_id=1, source_target_pairs={{0,2},{2,0},{1,3},{3,1},{4,6},{6,4},{5,7},{7,5},{8,10},{10,8},{9,1... | collective-permute-start | bytes 196616 | tf_op jit(solution)/shard_map/ppermute | solution.py:418
  20.1 0.0 collective-permute-start.13
  20.1 0.8 %collective-permute-start.5 = (bf16[80,512]{1,0:T(8,128)(2,1)S(1)}, bf16[80,512]{1,0:T(8,128)(2,1)S(1)}, u32[]{:S(2)}, u32[]{:S(2)}) collective-permute-start(bf16[80,512]{1,0:T(8,128)(2,1)S(1)} %get-tuple-element.74), channel_id=1, source_target_pairs={{0,4},{4,0},{8,12},{12,8},{1,5},{5,1},{9,13},{13,9},{2,6},{6,2},{1... | collective-permute-start | bytes 245768 | tf_op jit(solution)/shard_map/ppermute | solution.py:418
  20.9 0.0 collective-permute-done.8.arrived_ref
  20.9 0.4 collective-permute-start.6
  21.4 1.7 %collective-permute-done.11.arrived_ref = bf16[128,256]{1,0:T(8,128)(2,1)S(1)} collective-permute-done((bf16[128,256]{1,0:T(8,128)(2,1)S(1)}, bf16[128,256]{1,0:T(8,128)(2,1)S(1)}, u32[]{:S(2)}, u32[]{:S(2)}) %collective-permute-start.11) | collective-permute-done | bytes 65568 | tf_op jit(solution)/shard_map/ppermute | solution.py:418
  23.1 2.2 %collective-permute-start.9 = (bf16[144,256]{1,0:T(8,128)(2,1)S(1)}, bf16[144,256]{1,0:T(8,128)(2,1)S(1)}, u32[]{:S(2)}, u32[]{:S(2)}) collective-permute-start(bf16[144,256]{1,0:T(8,128)(2,1)S(1)} %get-tuple-element.78), channel_id=1, source_target_pairs={{0,12},{4,8},{8,4},{12,0},{1,13},{5,9},{9,5},{13,1},{2,14},{6,10},... | collective-permute-start | bytes 221192 | tf_op jit(solution)/shard_map/ppermute | solution.py:418
  25.3 1.0 %collective-permute-done.13.refs_1_ = bf16[64,512]{1,0:T(8,128)(2,1)S(1)} collective-permute-done((bf16[64,512]{1,0:T(8,128)(2,1)S(1)}, bf16[64,512]{1,0:T(8,128)(2,1)S(1)}, u32[]{:S(2)}, u32[]{:S(2)}) %collective-permute-start.13) | collective-permute-done | bytes 65568 | tf_op jit(solution)/shard_map/ppermute | solution.py:418
  26.3 0.0 collective-permute-start.10
  26.3 0.0 collective-permute-done.4.three_ref.refs_0_
  26.3 1.8 %collective-permute-start.12 = (bf16[144,256]{1,0:T(8,128)(2,1)S(1)}, bf16[144,256]{1,0:T(8,128)(2,1)S(1)}, u32[]{:S(2)}, u32[]{:S(2)}) collective-permute-start(bf16[144,256]{1,0:T(8,128)(2,1)S(1)} %shard_map.168.refs_4_), channel_id=1, source_target_pairs={{0,4},{4,0},{8,12},{12,8},{1,5},{5,1},{9,13},{13,9},{2,6},{6,2},{1... | collective-permute-start | bytes 221192 | tf_op jit(solution)/shard_map/ppermute | solution.py:418
  28.0 0.0 collective-permute-done.5.one_ref.refs_2_
  28.1 1.7 %collective-permute-start.14 = (bf16[64,256]{1,0:T(8,128)(2,1)S(1)}, bf16[64,256]{1,0:T(8,128)(2,1)S(1)}, u32[]{:S(2)}, u32[]{:S(2)}) collective-permute-start(bf16[64,256]{1,0:T(8,128)(2,1)S(1)} %get-tuple-element.87), channel_id=1, source_target_pairs={{0,2},{2,0},{1,3},{3,1},{4,6},{6,4},{5,7},{7,5},{8,10},{10,8},{9,1... | collective-permute-start | bytes 98312 | tf_op jit(solution)/shard_map/ppermute | solution.py:418
  29.8 0.0 collective-permute-done.6.pair_ref.refs_4_
  29.8 0.4 shard_map.166.refs_8_.own_ref
  30.2 1.9 %collective-permute-done.14.refs_7_ = bf16[64,256]{1,0:T(8,128)(2,1)S(1)} collective-permute-done((bf16[64,256]{1,0:T(8,128)(2,1)S(1)}, bf16[64,256]{1,0:T(8,128)(2,1)S(1)}, u32[]{:S(2)}, u32[]{:S(2)}) %collective-permute-start.14) | collective-permute-done | bytes 32800 | tf_op jit(solution)/shard_map/ppermute | solution.py:418
  32.1 0.0 collective-permute-done.9.refs_0_
  32.1 0.0 collective-permute-done.10.refs_1_
  32.1 0.0 collective-permute-done.12.refs_2_
  32.1 0.1 shard_map.170
  32.2 1.7 %collective-permute-start.18 = (bf16[192,256]{1,0:T(8,128)(2,1)S(1)}, bf16[192,256]{1,0:T(8,128)(2,1)S(1)}, u32[]{:S(2)}, u32[]{:S(2)}) collective-permute-start(bf16[192,256]{1,0:T(8,128)(2,1)S(1)} %get-tuple-element.91.refs_0_), channel_id=1, source_target_pairs={{0,2},{2,0},{1,3},{3,1},{4,6},{6,4},{5,7},{7,5},{8,10},{10,8},{9,1... | collective-permute-start | bytes 294920 | tf_op jit(solution)/shard_map/ppermute | solution.py:418
  33.8 0.4 collective-permute-start.17
  34.2 2.3 %collective-permute-start.15 = (bf16[192,256]{1,0:T(8,128)(2,1)S(1)}, bf16[192,256]{1,0:T(8,128)(2,1)S(1)}, u32[]{:S(2)}, u32[]{:S(2)}) collective-permute-start(bf16[192,256]{1,0:T(8,128)(2,1)S(1)} %get-tuple-element.91.refs_0_), channel_id=1, source_target_pairs={{0,12},{4,8},{8,4},{12,0},{1,13},{5,9},{9,5},{13,1},{2,14},{6,10},... | collective-permute-start | bytes 294920 | tf_op jit(solution)/shard_map/ppermute | solution.py:418
  36.5 0.0 collective-permute-start.7
  36.5 0.8 %collective-permute-start.16 = (bf16[192,256]{1,0:T(8,128)(2,1)S(1)}, bf16[192,256]{1,0:T(8,128)(2,1)S(1)}, u32[]{:S(2)}, u32[]{:S(2)}) collective-permute-start(bf16[192,256]{1,0:T(8,128)(2,1)S(1)} %get-tuple-element.91.refs_0_), channel_id=1, source_target_pairs={{0,4},{4,0},{8,12},{12,8},{1,5},{5,1},{9,13},{13,9},{2,6},{6,2},{1... | collective-permute-start | bytes 294920 | tf_op jit(solution)/shard_map/ppermute | solution.py:418
  37.3 0.0 collective-permute-done.18.refs_4_
  37.3 1.2 %collective-permute-start.20 = (bf16[192,256]{1,0:T(8,128)(2,1)S(1)}, bf16[192,256]{1,0:T(8,128)(2,1)S(1)}, u32[]{:S(2)}, u32[]{:S(2)}) collective-permute-start(bf16[192,256]{1,0:T(8,128)(2,1)S(1)} %collective-permute-done.18.refs_4_), channel_id=1, source_target_pairs={{0,4},{4,0},{8,12},{12,8},{1,5},{5,1},{9,13},{13,9},{2,6},{6,2},{1... | collective-permute-start | bytes 294920 | tf_op jit(solution)/shard_map/ppermute | solution.py:418
  38.5 3.4 %collective-permute-done.17.refs_3_ = bf16[192,256]{1,0:T(8,128)(2,1)S(1)} collective-permute-done((bf16[192,256]{1,0:T(8,128)(2,1)S(1)}, bf16[192,256]{1,0:T(8,128)(2,1)S(1)}, u32[]{:S(2)}, u32[]{:S(2)}) %collective-permute-start.17) | collective-permute-done | bytes 98336 | tf_op jit(solution)/shard_map/ppermute | solution.py:418
  42.0 1.1 %collective-permute-start.21 = (bf16[192,256]{1,0:T(8,128)(2,1)S(1)}, bf16[192,256]{1,0:T(8,128)(2,1)S(1)}, u32[]{:S(2)}, u32[]{:S(2)}) collective-permute-start(bf16[192,256]{1,0:T(8,128)(2,1)S(1)} %collective-permute-done.17.refs_3_), channel_id=1, source_target_pairs={{0,2},{2,0},{1,3},{3,1},{4,6},{6,4},{5,7},{7,5},{8,10},{10,8},{9,1... | collective-permute-start | bytes 294920 | tf_op jit(solution)/shard_map/ppermute | solution.py:418
  43.0 0.0 collective-permute-done.15.refs_1_
  43.0 1.0 %collective-permute-start.19 = (bf16[192,256]{1,0:T(8,128)(2,1)S(1)}, bf16[192,256]{1,0:T(8,128)(2,1)S(1)}, u32[]{:S(2)}, u32[]{:S(2)}) collective-permute-start(bf16[192,256]{1,0:T(8,128)(2,1)S(1)} %collective-permute-done.15.refs_1_), channel_id=1, source_target_pairs={{0,2},{2,0},{1,3},{3,1},{4,6},{6,4},{5,7},{7,5},{8,10},{10,8},{9,1... | collective-permute-start | bytes 294920 | tf_op jit(solution)/shard_map/ppermute | solution.py:418
  44.0 0.0 collective-permute-done.7.other_ref
  44.0 0.8 %shard_map.171 = (f32[128,512]{1,0:T(8,128)}, bf16[128,512]{1,0:T(8,128)(2,1)}, f32[1,256]{1,0:T(1,128)}, f32[1,512]{1,0:T(1,128)}) custom-call(bf16[128,512]{1,0:T(8,128)(2,1)S(1)} %get-tuple-element.53.cot_ref, bf16[128,512]{1,0:T(8,128)(2,1)S(1)} %get-tuple-element.52.refs_0_.node_ref, f32[1,512]{1,0:T(1,128)S(1)} %get-tuple-element.54.gain_ref, ...), custom_call_target="tpu_custom_call" | custom-call | flops 100000000 | bytes 1000000 | tf_op jit(solution)/shard_map/pallas_call | solution.py:400
  44.8 0.0 collective-permute-done.16.refs_2_
  44.8 0.9 %collective-permute-done.20.refs_6_ = bf16[192,256]{1,0:T(8,128)(2,1)S(1)} collective-permute-done((bf16[192,256]{1,0:T(8,128)(2,1)S(1)}, bf16[192,256]{1,0:T(8,128)(2,1)S(1)}, u32[]{:S(2)}, u32[]{:S(2)}) %collective-permute-start.20) | collective-permute-done | bytes 98336 | tf_op jit(solution)/shard_map/ppermute | solution.py:418
  45.7 0.8 %collective-permute-done.21.refs_7_ = bf16[192,256]{1,0:T(8,128)(2,1)S(1)} collective-permute-done((bf16[192,256]{1,0:T(8,128)(2,1)S(1)}, bf16[192,256]{1,0:T(8,128)(2,1)S(1)}, u32[]{:S(2)}, u32[]{:S(2)}) %collective-permute-start.21) | collective-permute-done | bytes 98336 | tf_op jit(solution)/shard_map/ppermute | solution.py:418
  46.6 1.1 %collective-permute-done.19.refs_5_ = bf16[192,256]{1,0:T(8,128)(2,1)S(1)} collective-permute-done((bf16[192,256]{1,0:T(8,128)(2,1)S(1)}, bf16[192,256]{1,0:T(8,128)(2,1)S(1)}, u32[]{:S(2)}, u32[]{:S(2)}) %collective-permute-start.19) | collective-permute-done | bytes 98336 | tf_op jit(solution)/shard_map/ppermute | solution.py:418
  47.6 1.2 %shard_map.172 = (f32[512,256]{1,0:T(8,128)}, f32[512,256]{1,0:T(8,128)}, f32[256,512]{1,0:T(8,128)}) custom-call(bf16[192,256]{1,0:T(8,128)(2,1)S(1)} %get-tuple-element.91.refs_0_, bf16[192,256]{1,0:T(8,128)(2,1)S(1)} %collective-permute-done.15.refs_1_, bf16[192,256]{1,0:T(8,128)(2,1)S(1)} %collective-permute-done.16.refs_2_, ...), custom_call_target="tpu_custom_call" | custom-call | flops 100000000 | bytes 1000000 | tf_op jit(solution)/shard_map/pallas_call | solution.py:400
  (3 shorter events, 0.1 us)
Async XLA Ops:
  1.8 9.0 %collective-permute-start.2 = (bf16[64,512]{1,0:T(8,128)(2,1)S(1)}, bf16[64,512]{1,0:T(8,128)(2,1)S(1)}, u32[]{:S(2)}, u32[]{:S(2)}) collective-permute-start(bf16[64,512]{1,0:T(8,128)(2,1)S(1)} %get-tuple-element.64), channel_id=1, source_target_pairs={{0,2},{2,0},{1,3},{3,1},{4,6},{6,4},{5,7},{7,5},{8,10},{10,8},{9,1... | collective-permute-start | bytes 196616 | tf_op jit(solution)/shard_map/ppermute | solution.py:413
  4.8 5.9 %collective-permute-start = (bf16[32,512]{1,0:T(8,128)(2,1)S(1)}, bf16[32,512]{1,0:T(8,128)(2,1)S(1)}, u32[]{:S(2)}, u32[]{:S(2)}) collective-permute-start(bf16[32,512]{1,0:T(8,128)(2,1)S(1)} %get-tuple-element.62), channel_id=1, source_target_pairs={{0,4},{4,8},{8,12},{12,0},{1,5},{5,9},{9,13},{13,1},{2,6},{6,10},{... | collective-permute-start | bytes 98312 | tf_op jit(solution)/shard_map/ppermute | solution.py:413
  6.4 4.4 %collective-permute-start.1 = (bf16[32,512]{1,0:T(8,128)(2,1)S(1)}, bf16[32,512]{1,0:T(8,128)(2,1)S(1)}, u32[]{:S(2)}, u32[]{:S(2)}) collective-permute-start(bf16[32,512]{1,0:T(8,128)(2,1)S(1)} %get-tuple-element.63), channel_id=1, source_target_pairs={{0,12},{4,0},{8,4},{12,8},{1,13},{5,1},{9,5},{13,9},{2,14},{6,2},{... | collective-permute-start | bytes 98312 | tf_op jit(solution)/shard_map/ppermute | solution.py:413
  11.6 1.4 %collective-permute-start.3 = (bf16[128,512]{1,0:T(8,128)(2,1)S(1)}, bf16[128,512]{1,0:T(8,128)(2,1)S(1)}, u32[]{:S(2)}, u32[]{:S(2)}) collective-permute-start(bf16[128,512]{1,0:T(8,128)(2,1)S(1)} %get-tuple-element.67.own_ref), channel_id=1, source_target_pairs={{0,1},{1,0},{2,3},{3,2},{4,5},{5,4},{6,7},{7,6},{8,9},{9,8},{10,11... | collective-permute-start | bytes 393224 | tf_op jit(solution)/shard_map/ppermute | solution.py:413
  14.4 6.5 %collective-permute-start.8 = (bf16[272,256]{1,0:T(8,128)(2,1)S(1)}, bf16[272,256]{1,0:T(8,128)(2,1)S(1)}, u32[]{:S(2)}, u32[]{:S(2)}) collective-permute-start(bf16[272,256]{1,0:T(8,128)(2,1)S(1)} %get-tuple-element.76), channel_id=1, source_target_pairs={{0,2},{2,0},{1,3},{3,1},{4,6},{6,4},{5,7},{7,5},{8,10},{10,8},{9,1... | collective-permute-start | bytes 417800 | tf_op jit(solution)/shard_map/ppermute | solution.py:418
  14.9 11.4 %collective-permute-start.4 = (bf16[80,512]{1,0:T(8,128)(2,1)S(1)}, bf16[80,512]{1,0:T(8,128)(2,1)S(1)}, u32[]{:S(2)}, u32[]{:S(2)}) collective-permute-start(bf16[80,512]{1,0:T(8,128)(2,1)S(1)} %get-tuple-element.73), channel_id=1, source_target_pairs={{0,12},{4,8},{8,4},{12,0},{1,13},{5,9},{9,5},{13,1},{2,14},{6,10},... | collective-permute-start | bytes 245768 | tf_op jit(solution)/shard_map/ppermute | solution.py:418
  18.4 4.6 %collective-permute-start.11 = (bf16[128,256]{1,0:T(8,128)(2,1)S(1)}, bf16[128,256]{1,0:T(8,128)(2,1)S(1)}, u32[]{:S(2)}, u32[]{:S(2)}) collective-permute-start(bf16[128,256]{1,0:T(8,128)(2,1)S(1)} %get-tuple-element.80), channel_id=1, source_target_pairs={{0,2},{2,0},{1,3},{3,1},{4,6},{6,4},{5,7},{7,5},{8,10},{10,8},{9,1... | collective-permute-start | bytes 196616 | tf_op jit(solution)/shard_map/ppermute | solution.py:418
  20.1 6.1 %collective-permute-start.13 = (bf16[64,512]{1,0:T(8,128)(2,1)S(1)}, bf16[64,512]{1,0:T(8,128)(2,1)S(1)}, u32[]{:S(2)}, u32[]{:S(2)}) collective-permute-start(bf16[64,512]{1,0:T(8,128)(2,1)S(1)} %get-tuple-element.84), channel_id=1, source_target_pairs={{0,8},{4,12},{8,0},{12,4},{1,9},{5,13},{9,1},{13,5},{2,10},{6,14},... | collective-permute-start | bytes 196616 | tf_op jit(solution)/shard_map/ppermute | solution.py:418
  20.1 7.9 %collective-permute-start.5 = (bf16[80,512]{1,0:T(8,128)(2,1)S(1)}, bf16[80,512]{1,0:T(8,128)(2,1)S(1)}, u32[]{:S(2)}, u32[]{:S(2)}) collective-permute-start(bf16[80,512]{1,0:T(8,128)(2,1)S(1)} %get-tuple-element.74), channel_id=1, source_target_pairs={{0,4},{4,0},{8,12},{12,8},{1,5},{5,1},{9,13},{13,9},{2,6},{6,2},{1... | collective-permute-start | bytes 245768 | tf_op jit(solution)/shard_map/ppermute | solution.py:418
  20.9 8.8 %collective-permute-start.6 = (bf16[192,256]{1,0:T(8,128)(2,1)S(1)}, bf16[192,256]{1,0:T(8,128)(2,1)S(1)}, u32[]{:S(2)}, u32[]{:S(2)}) collective-permute-start(bf16[192,256]{1,0:T(8,128)(2,1)S(1)} %get-tuple-element.75), channel_id=1, source_target_pairs={{0,2},{2,0},{1,3},{3,1},{4,6},{6,4},{5,7},{7,5},{8,10},{10,8},{9,1... | collective-permute-start | bytes 294920 | tf_op jit(solution)/shard_map/ppermute | solution.py:418
  23.1 9.0 %collective-permute-start.9 = (bf16[144,256]{1,0:T(8,128)(2,1)S(1)}, bf16[144,256]{1,0:T(8,128)(2,1)S(1)}, u32[]{:S(2)}, u32[]{:S(2)}) collective-permute-start(bf16[144,256]{1,0:T(8,128)(2,1)S(1)} %get-tuple-element.78), channel_id=1, source_target_pairs={{0,12},{4,8},{8,4},{12,0},{1,13},{5,9},{9,5},{13,1},{2,14},{6,10},... | collective-permute-start | bytes 221192 | tf_op jit(solution)/shard_map/ppermute | solution.py:418
  26.3 5.8 %collective-permute-start.10 = (bf16[144,256]{1,0:T(8,128)(2,1)S(1)}, bf16[144,256]{1,0:T(8,128)(2,1)S(1)}, u32[]{:S(2)}, u32[]{:S(2)}) collective-permute-start(bf16[144,256]{1,0:T(8,128)(2,1)S(1)} %get-tuple-element.79), channel_id=1, source_target_pairs={{0,8},{4,12},{8,0},{12,4},{1,9},{5,13},{9,1},{13,5},{2,10},{6,14},... | collective-permute-start | bytes 221192 | tf_op jit(solution)/shard_map/ppermute | solution.py:418
  26.3 5.8 %collective-permute-start.12 = (bf16[144,256]{1,0:T(8,128)(2,1)S(1)}, bf16[144,256]{1,0:T(8,128)(2,1)S(1)}, u32[]{:S(2)}, u32[]{:S(2)}) collective-permute-start(bf16[144,256]{1,0:T(8,128)(2,1)S(1)} %shard_map.168.refs_4_), channel_id=1, source_target_pairs={{0,4},{4,0},{8,12},{12,8},{1,5},{5,1},{9,13},{13,9},{2,6},{6,2},{1... | collective-permute-start | bytes 221192 | tf_op jit(solution)/shard_map/ppermute | solution.py:418
  28.1 4.0 %collective-permute-start.14 = (bf16[64,256]{1,0:T(8,128)(2,1)S(1)}, bf16[64,256]{1,0:T(8,128)(2,1)S(1)}, u32[]{:S(2)}, u32[]{:S(2)}) collective-permute-start(bf16[64,256]{1,0:T(8,128)(2,1)S(1)} %get-tuple-element.87), channel_id=1, source_target_pairs={{0,2},{2,0},{1,3},{3,1},{4,6},{6,4},{5,7},{7,5},{8,10},{10,8},{9,1... | collective-permute-start | bytes 98312 | tf_op jit(solution)/shard_map/ppermute | solution.py:418
  32.2 5.2 %collective-permute-start.18 = (bf16[192,256]{1,0:T(8,128)(2,1)S(1)}, bf16[192,256]{1,0:T(8,128)(2,1)S(1)}, u32[]{:S(2)}, u32[]{:S(2)}) collective-permute-start(bf16[192,256]{1,0:T(8,128)(2,1)S(1)} %get-tuple-element.91.refs_0_), channel_id=1, source_target_pairs={{0,2},{2,0},{1,3},{3,1},{4,6},{6,4},{5,7},{7,5},{8,10},{10,8},{9,1... | collective-permute-start | bytes 294920 | tf_op jit(solution)/shard_map/ppermute | solution.py:418
  33.8 8.1 %collective-permute-start.17 = (bf16[192,256]{1,0:T(8,128)(2,1)S(1)}, bf16[192,256]{1,0:T(8,128)(2,1)S(1)}, u32[]{:S(2)}, u32[]{:S(2)}) collective-permute-start(bf16[192,256]{1,0:T(8,128)(2,1)S(1)} %get-tuple-element.91.refs_0_), channel_id=1, source_target_pairs={{0,8},{4,12},{8,0},{12,4},{1,9},{5,13},{9,1},{13,5},{2,10},{6,14},... | collective-permute-start | bytes 294920 | tf_op jit(solution)/shard_map/ppermute | solution.py:418
  34.2 8.8 %collective-permute-start.15 = (bf16[192,256]{1,0:T(8,128)(2,1)S(1)}, bf16[192,256]{1,0:T(8,128)(2,1)S(1)}, u32[]{:S(2)}, u32[]{:S(2)}) collective-permute-start(bf16[192,256]{1,0:T(8,128)(2,1)S(1)} %get-tuple-element.91.refs_0_), channel_id=1, source_target_pairs={{0,12},{4,8},{8,4},{12,0},{1,13},{5,9},{9,5},{13,1},{2,14},{6,10},... | collective-permute-start | bytes 294920 | tf_op jit(solution)/shard_map/ppermute | solution.py:418
  36.5 7.5 %collective-permute-start.7 = (bf16[128,512]{1,0:T(8,128)(2,1)S(1)}, bf16[128,512]{1,0:T(8,128)(2,1)S(1)}, u32[]{:S(2)}, u32[]{:S(2)}) collective-permute-start(bf16[128,512]{1,0:T(8,128)(2,1)S(1)} %shard_map.166.refs_8_.own_ref), channel_id=1, source_target_pairs={{0,1},{1,0},{2,3},{3,2},{4,5},{5,4},{6,7},{7,6},{8,9},{9,8},{10,11... | collective-permute-start | bytes 393224 | tf_op jit(solution)/shard_map/ppermute | solution.py:413
  36.5 8.3 %collective-permute-start.16 = (bf16[192,256]{1,0:T(8,128)(2,1)S(1)}, bf16[192,256]{1,0:T(8,128)(2,1)S(1)}, u32[]{:S(2)}, u32[]{:S(2)}) collective-permute-start(bf16[192,256]{1,0:T(8,128)(2,1)S(1)} %get-tuple-element.91.refs_0_), channel_id=1, source_target_pairs={{0,4},{4,0},{8,12},{12,8},{1,5},{5,1},{9,13},{13,9},{2,6},{6,2},{1... | collective-permute-start | bytes 294920 | tf_op jit(solution)/shard_map/ppermute | solution.py:418
  37.3 8.4 %collective-permute-start.20 = (bf16[192,256]{1,0:T(8,128)(2,1)S(1)}, bf16[192,256]{1,0:T(8,128)(2,1)S(1)}, u32[]{:S(2)}, u32[]{:S(2)}) collective-permute-start(bf16[192,256]{1,0:T(8,128)(2,1)S(1)} %collective-permute-done.18.refs_4_), channel_id=1, source_target_pairs={{0,4},{4,0},{8,12},{12,8},{1,5},{5,1},{9,13},{13,9},{2,6},{6,2},{1... | collective-permute-start | bytes 294920 | tf_op jit(solution)/shard_map/ppermute | solution.py:418
  42.0 4.6 %collective-permute-start.21 = (bf16[192,256]{1,0:T(8,128)(2,1)S(1)}, bf16[192,256]{1,0:T(8,128)(2,1)S(1)}, u32[]{:S(2)}, u32[]{:S(2)}) collective-permute-start(bf16[192,256]{1,0:T(8,128)(2,1)S(1)} %collective-permute-done.17.refs_3_), channel_id=1, source_target_pairs={{0,2},{2,0},{1,3},{3,1},{4,6},{6,4},{5,7},{7,5},{8,10},{10,8},{9,1... | collective-permute-start | bytes 294920 | tf_op jit(solution)/shard_map/ppermute | solution.py:418
  43.0 4.6 %collective-permute-start.19 = (bf16[192,256]{1,0:T(8,128)(2,1)S(1)}, bf16[192,256]{1,0:T(8,128)(2,1)S(1)}, u32[]{:S(2)}, u32[]{:S(2)}) collective-permute-start(bf16[192,256]{1,0:T(8,128)(2,1)S(1)} %collective-permute-done.15.refs_1_), channel_id=1, source_target_pairs={{0,2},{2,0},{1,3},{3,1},{4,6},{6,4},{5,7},{7,5},{8,10},{10,8},{9,1... | collective-permute-start | bytes 294920 | tf_op jit(solution)/shard_map/ppermute | solution.py:418

commit v10 on v9

--- a/solution.py
+++ b/solution.py
@@ -10,6 +10,7 @@
 BLOCK = 128
 EPSILON = 1e-05
 TAIL = 16
+CUT = 32
 N_FETCHED = 9
 VMEM_LIMIT = 24 * 1024 * 1024
 
@@ -193,11 +194,15 @@
         pair_scratch[1] = jnp.where(first, src_part, dst_part)
         strip = width // lines
         for slot, (far_ref, one_ref, zero_ref) in enumerate((sends, keeps)):
-            places = ((far_ref, 0, 3), (far_ref, strip, 2), (one_ref, 0, 1), (zero_ref, 0, 0))
-            for ref, at, k in places:
-                start = pl.multiple_of((mesh ^ k) * strip, strip)
-                ref[at : at + strip, :] = pair_scratch[slot, pl.ds(start, strip), :]
-            far_ref[2 * strip :, :] = tail
+            cut = strip - CUT
+            places = (
+                (far_ref, 0, 3, 0, strip), (far_ref, strip, 2, 0, strip), (far_ref, 2 * strip + TAIL, 1, cut, CUT),
+                (one_ref, 0, 1, 0, cut), (zero_ref, 0, 0, 0, strip),
+            )
+            for ref, at, k, begin, size in places:
+                start = pl.multiple_of((mesh ^ k) * strip + begin, 16)
+                ref[at : at + size, :] = pair_scratch[slot, pl.ds(start, size), :]
+            far_ref[2 * strip : 2 * strip + TAIL, :] = tail
         sends[2][strip:, :] = back[2 * halo :]
         back_scratch[...] = back[: 2 * halo]
         out_scratch[...] = out_part
@@ -257,18 +262,20 @@
 def far_kernel(arrived_ref, keep_ref, three_ref, two_ref, tail_ref):
     total = keep_ref[...].astype(f32) + arrived_ref[...].astype(f32)
     strip = three_ref.shape[0] - TAIL
-    tail = total[2 * strip :]
+    tail = total[2 * strip : 2 * strip + TAIL]
     tail = tail_of([tail[at : at + 1] + tail[at + 1 : at + 2] for at in range(0, 6, 2)])
     for k, ref in enumerate((three_ref, two_ref)):
         ref[0:strip, :] = total[k * strip : (k + 1) * strip].astype(bf16)
         ref[strip:, :] = tail
-    tail_ref[...] = tail
+    tail_ref[0:TAIL, :] = tail
+    tail_ref[TAIL:, :] = total[2 * strip + TAIL :].astype(bf16)
 
 
 def near_kernel(arrived_ref, keep_ref, tail_ref, one_ref):
-    strip = keep_ref.shape[0]
-    one_ref[0:strip, :] = (keep_ref[...].astype(f32) + arrived_ref[...].astype(f32)).astype(bf16)
-    one_ref[strip:, :] = tail_ref[...]
+    cut = keep_ref.shape[0]
+    one_ref[0:cut, :] = (keep_ref[...].astype(f32) + arrived_ref[...].astype(f32)).astype(bf16)
+    one_ref[cut : cut + CUT, :] = tail_ref[TAIL:, :]
+    one_ref[cut + CUT :, :] = tail_ref[0:TAIL, :]
 
 
 def line_kernel(*refs):
@@ -290,7 +297,7 @@
     own_ref[strip:, :] = (
         out_keep_ref[...].astype(f32) + out_arrived_ref[...].astype(f32)
     ).astype(bf16)
-    tail_ref[...] = tree([r[strip:, :].astype(f32) for r in terms] + [vectors_ref[...].astype(f32)])
+    tail_ref[...] = tree([r[strip:, :].astype(f32) for r in terms] + [vectors_ref[0:TAIL, :].astype(f32)])
 
 
 def write_vectors(tail, bias_ref, gain_ref):
@@ -418,6 +425,12 @@
     return lax.ppermute(x, axis, [(i, i ^ k) for i in range(count)])
 
 
+def diagonal(x):
+    lines, pairs = lax.axis_size("mesh"), lax.axis_size("sub")
+    moves = [(m * pairs + p, (m ^ 1) * pairs + (p ^ 1)) for m in range(lines) for p in range(pairs)]
+    return lax.ppermute(x, ("mesh", "sub"), moves)
+
+
 def paired_sums(messages, lines, strip, narrow, width, hid, node_terms):
     sends, keeps, outs = messages[:3], messages[3:6], messages[6:]
     order = range(lines - 1, 0, -1)
@@ -427,7 +440,7 @@
     one = across(sends[1], "sub", 1)
     zero = across(sends[2], "sub", 1)
     line = {}
-    line[3], line[2], tail = call(far_kernel, [block, block, shape((TAIL, hid), bf16)], far, keeps[0])
+    line[3], line[2], tail = call(far_kernel, [block, block, shape((TAIL + CUT, hid), bf16)], far, keeps[0])
     line[1] = call(near_kernel, block, one, keeps[1], tail)
     line_terms = {k: across(line[k], "mesh", k) for k in order}
     out_send, out_keep = call(
@@ -444,8 +457,7 @@
     )
     mine = {k: across(own, "mesh", k) for k in order}
     mine[0] = own
-    theirs = {0: across(own, "sub", 1)}
-    theirs[1] = across(theirs[0], "mesh", 1)
+    theirs = {0: across(own, "sub", 1), 1: diagonal(own)}
     theirs |= {k: across(mine[k], "sub", 1) for k in (3, 2)}
     placed = (0, 3, 1, 2)
     grads = call(
@@ -532,7 +544,8 @@
     if paired:
         strip = width // lines
         narrow = hid // lines
-        rows_of = (2 * strip + TAIL, strip, strip + 2 * halo, 2 * strip + TAIL, strip, strip)
+        far_rows, cut = 2 * strip + TAIL + CUT, strip - CUT
+        rows_of = (far_rows, cut, strip + 2 * halo, far_rows, cut, strip)
         message_shapes = [shape((n, hid), bf16) for n in rows_of]
         message_shapes += [shape((narrow + k % 2 * (halo // 2), width), bf16) for k in range(lines)]
     else:

time: 49 us -> 49.1 us (level)
  waiting for transfers between devices: 12.3 us -> 11.1 us
  starting transfers between devices: 27.8 us -> 29 us
    ppermute x0 -> x1, starting transfers between devices: none -> 1.38 us  [diagonal(): return lax.ppermute(x, ('mesh', 'sub'), moves)]
    ppermute x17 -> x16, waiting for transfers between devices: 10.9 us -> 9.72 us  [across(): return lax.ppermute(x, axis, [(i, i ^ k) for i in range(count)])]
    ppermute x17 -> x16, starting transfers between devices: 20.9 us -> 20.6 us  [across(): return lax.ppermute(x, axis, [(i, i ^ k) for i in range(count)])]
where the time goes in v10:
time: 49.1 us; the launch traced here: 48.9 us
  starting transfers between devices  29 us (59%)
  waiting for transfers between devices  11.1 us (23%)
  Pallas kernels  8.06 us (16%)
  between operations  0.75 us (2%)
    ppermute x16, starting transfers between devices, across(): return lax.ppermute(x, axis, [(i, i ^ k) for i in range(count)])  20.6 us
    ppermute x16, waiting for transfers between devices, across(): return lax.ppermute(x, axis, [(i, i ^ k) for i in range(count)])  9.72 us
    pallas_call x11, Pallas kernels, call(): pl.pallas_call(kernel, out_shape=outs, in_specs=specs or [VMEM] * len(arg...  8.06 us
    ppermute x5, starting transfers between devices, shifted(): return lax.ppermute(x, axis, [(i, (i + by) % count) for i in range(count)])  6.97 us
    ppermute x5, waiting for transfers between devices, shifted(): return lax.ppermute(x, axis, [(i, (i + by) % count) for i in range(count)])  1.38 us
    ppermute x1, starting transfers between devices, diagonal(): return lax.ppermute(x, ('mesh', 'sub'), moves)  1.38 us
  transfers between devices with their start and end apart: 22, of which 8 were waited for; matrix products, arithmetic and copies ran while one was open for 0% of the time, Pallas kernels for 7%

profile of v10, /device:TPU:0, one launch (start us, length us, event | category | flops | bytes accessed | tf_op | source)
XLA Modules:
  0.0 48.9 jit_solution(13857087385146009050)
XLA Ops:
  0.6 1.2 %shard_map.162 = (bf16[128,512]{1,0:T(8,128)(2,1)S(1)}, s32[1,4,32]{2,1,0:T(4,128)S(1)}, bf16[32,512]{1,0:T(8,128)(2,1)S(1)}, bf16[32,512]{1,0:T(8,128)(2,1)S(1)}, bf16[64,512]{1,0:T(8,128)(2,1)S(1)}) custom-call(bf16[128,512]{1,0:T(8,128)(2,1)} %node_hbm.1, s32[1,4,32]{2,1,0:T(4,128)} %send_hbm.1), custom_call_target="tpu_custom_call" | custom-call | flops 100000000 | bytes 1000000 | tf_op jit(solution)/shard_map/pallas_call | solution.py:407
  1.8 3.0 %collective-permute-start.2 = (bf16[64,512]{1,0:T(8,128)(2,1)S(1)}, bf16[64,512]{1,0:T(8,128)(2,1)S(1)}, u32[]{:S(2)}, u32[]{:S(2)}) collective-permute-start(bf16[64,512]{1,0:T(8,128)(2,1)S(1)} %get-tuple-element.64), channel_id=1, source_target_pairs={{0,2},{2,0},{1,3},{3,1},{4,6},{6,4},{5,7},{7,5},{8,10},{10,8},{9,1... | collective-permute-start | bytes 196616 | tf_op jit(solution)/shard_map/ppermute | solution.py:420
  4.8 1.6 %collective-permute-start = (bf16[32,512]{1,0:T(8,128)(2,1)S(1)}, bf16[32,512]{1,0:T(8,128)(2,1)S(1)}, u32[]{:S(2)}, u32[]{:S(2)}) collective-permute-start(bf16[32,512]{1,0:T(8,128)(2,1)S(1)} %get-tuple-element.62), channel_id=1, source_target_pairs={{0,4},{4,8},{8,12},{12,0},{1,5},{5,9},{9,13},{13,1},{2,6},{6,10},{... | collective-permute-start | bytes 98312 | tf_op jit(solution)/shard_map/ppermute | solution.py:420
  6.4 2.2 %collective-permute-start.1 = (bf16[32,512]{1,0:T(8,128)(2,1)S(1)}, bf16[32,512]{1,0:T(8,128)(2,1)S(1)}, u32[]{:S(2)}, u32[]{:S(2)}) collective-permute-start(bf16[32,512]{1,0:T(8,128)(2,1)S(1)} %get-tuple-element.63), channel_id=1, source_target_pairs={{0,12},{4,0},{8,4},{12,8},{1,13},{5,1},{9,5},{13,9},{2,14},{6,2},{... | collective-permute-start | bytes 98312 | tf_op jit(solution)/shard_map/ppermute | solution.py:420
  8.6 2.1 %shard_map.163 = (f32[512,256]{1,0:T(8,128)S(1)}, bf16[512,128]{1,0:T(8,128)(2,1)S(1)}, bf16[128,512]{1,0:T(8,128)(2,1)S(1)}, bf16[512,128]{1,0:T(8,128)(2,1)S(1...) custom-call(bf16[128,512]{1,0:T(8,128)(2,1)S(1)} %get-tuple-element., ...), custom_call_target="tpu_custom_call" | custom-call | flops 100000000 | bytes 1000000 | tf_op jit(solution)/shard_map/pallas_call | solution.py:407
  10.7 0.0 collective-permute-done.rest_0_
  10.8 0.0 collective-permute-done.1.rest_1_
  10.8 0.0 collective-permute-done.2.rest_2_
  10.8 0.9 %shard_map.164 = (f32[512,256]{1,0:T(8,128)S(1)}, bf16[128,256]{1,0:T(8,128)(2,1)S(1)}, bf16[128,512]{1,0:T(8,128)(2,1)S(1)}) custom-call(f32[512,256]{1,0:T(8,128)S(1)} %get-tuple-element.59.pre_ref, bf16[512,128]{1,0:T(8,128)(2,1)S(1)} %get-tuple-element.60.pick_ref, bf16[128,512]{1,0:T(8,128)(2,1)S(1)} %get-tuple-element.55.collect_ref, ...), custom_call_target="tpu_custom_call" | custom-call | flops 100000000 | bytes 1000000 | tf_op jit(solution)/shard_map/pallas_call | solution.py:407
  11.6 0.1 collective-permute-start.3
  11.7 1.3 %collective-permute-done.3.other_ref = bf16[128,512]{1,0:T(8,128)(2,1)S(1)} collective-permute-done((bf16[128,512]{1,0:T(8,128)(2,1)S(1)}, bf16[128,512]{1,0:T(8,128)(2,1)S(1)}, u32[]{:S(2)}, u32[]{:S(2)}) %collective-permute-start.3) | collective-permute-done | bytes 131104 | tf_op jit(solution)/shard_map/ppermute | solution.py:420
  13.1 1.4 %shard_map.165 = (f32[128,512]{1,0:T(8,128)S(1)}, f32[128,256]{1,0:T(8,128)S(1)}, bf16[128,256]{1,0:T(8,128)(2,1)S(1)}, bf16[304,256]{1,0:T(8,128)(2,1)S(1)}, bf...) custom-call(bf16[128,512]{1,0:T(8,128)(2,1)S(1)} %get-tuple-element., ...), custom_call_target="tpu_custom_call" | custom-call | flops 100000000 | bytes 1000000 | tf_op jit(solution)/shard_map/pallas_call | solution.py:407
  14.4 0.5 %collective-permute-start.8 = (bf16[304,256]{1,0:T(8,128)(2,1)S(1)}, bf16[304,256]{1,0:T(8,128)(2,1)S(1)}, u32[]{:S(2)}, u32[]{:S(2)}) collective-permute-start(bf16[304,256]{1,0:T(8,128)(2,1)S(1)} %get-tuple-element.76), channel_id=1, source_target_pairs={{0,2},{2,0},{1,3},{3,1},{4,6},{6,4},{5,7},{7,5},{8,10},{10,8},{9,1... | collective-permute-start | bytes 466952 | tf_op jit(solution)/shard_map/ppermute | solution.py:425
  14.9 3.5 %collective-permute-start.4 = (bf16[80,512]{1,0:T(8,128)(2,1)S(1)}, bf16[80,512]{1,0:T(8,128)(2,1)S(1)}, u32[]{:S(2)}, u32[]{:S(2)}) collective-permute-start(bf16[80,512]{1,0:T(8,128)(2,1)S(1)} %get-tuple-element.73), channel_id=1, source_target_pairs={{0,12},{4,8},{8,4},{12,0},{1,13},{5,9},{9,5},{13,1},{2,14},{6,10},... | collective-permute-start | bytes 245768 | tf_op jit(solution)/shard_map/ppermute | solution.py:425
  18.4 0.0 collective-permute-start.13
  18.4 1.7 %collective-permute-start.11 = (bf16[96,256]{1,0:T(8,128)(2,1)S(1)}, bf16[96,256]{1,0:T(8,128)(2,1)S(1)}, u32[]{:S(2)}, u32[]{:S(2)}) collective-permute-start(bf16[96,256]{1,0:T(8,128)(2,1)S(1)} %get-tuple-element.80), channel_id=1, source_target_pairs={{0,2},{2,0},{1,3},{3,1},{4,6},{6,4},{5,7},{7,5},{8,10},{10,8},{9,1... | collective-permute-start | bytes 147464 | tf_op jit(solution)/shard_map/ppermute | solution.py:425
  20.1 0.3 collective-permute-start.6
  20.5 0.1 collective-permute-done.8.arrived_ref
  20.6 1.4 %collective-permute-start.5 = (bf16[80,512]{1,0:T(8,128)(2,1)S(1)}, bf16[80,512]{1,0:T(8,128)(2,1)S(1)}, u32[]{:S(2)}, u32[]{:S(2)}) collective-permute-start(bf16[80,512]{1,0:T(8,128)(2,1)S(1)} %get-tuple-element.74), channel_id=1, source_target_pairs={{0,4},{4,0},{8,12},{12,8},{1,5},{5,1},{9,13},{13,9},{2,6},{6,2},{1... | collective-permute-start | bytes 245768 | tf_op jit(solution)/shard_map/ppermute | solution.py:425
  22.1 0.9 %collective-permute-done.11.arrived_ref = bf16[96,256]{1,0:T(8,128)(2,1)S(1)} collective-permute-done((bf16[96,256]{1,0:T(8,128)(2,1)S(1)}, bf16[96,256]{1,0:T(8,128)(2,1)S(1)}, u32[]{:S(2)}, u32[]{:S(2)}) %collective-permute-start.11) | collective-permute-done | bytes 49184 | tf_op jit(solution)/shard_map/ppermute | solution.py:425
  23.0 3.0 %collective-permute-start.9 = (bf16[144,256]{1,0:T(8,128)(2,1)S(1)}, bf16[144,256]{1,0:T(8,128)(2,1)S(1)}, u32[]{:S(2)}, u32[]{:S(2)}) collective-permute-start(bf16[144,256]{1,0:T(8,128)(2,1)S(1)} %get-tuple-element.78), channel_id=1, source_target_pairs={{0,12},{4,8},{8,4},{12,0},{1,13},{5,9},{9,5},{13,1},{2,14},{6,10},... | collective-permute-start | bytes 221192 | tf_op jit(solution)/shard_map/ppermute | solution.py:425
  26.1 0.0 collective-permute-done.13.refs_1_
  26.1 0.1 collective-permute-start.10
  26.1 0.0 collective-permute-done.4.three_ref.refs_0_
  26.2 1.6 %collective-permute-start.12 = (bf16[144,256]{1,0:T(8,128)(2,1)S(1)}, bf16[144,256]{1,0:T(8,128)(2,1)S(1)}, u32[]{:S(2)}, u32[]{:S(2)}) collective-permute-start(bf16[144,256]{1,0:T(8,128)(2,1)S(1)} %shard_map.168.refs_4_), channel_id=1, source_target_pairs={{0,4},{4,0},{8,12},{12,8},{1,5},{5,1},{9,13},{13,9},{2,6},{6,2},{1... | collective-permute-start | bytes 221192 | tf_op jit(solution)/shard_map/ppermute | solution.py:425
  27.8 0.0 collective-permute-done.5.one_ref.refs_2_
  27.8 1.5 %collective-permute-start.14 = (bf16[64,256]{1,0:T(8,128)(2,1)S(1)}, bf16[64,256]{1,0:T(8,128)(2,1)S(1)}, u32[]{:S(2)}, u32[]{:S(2)}) collective-permute-start(bf16[64,256]{1,0:T(8,128)(2,1)S(1)} %get-tuple-element.87), channel_id=1, source_target_pairs={{0,2},{2,0},{1,3},{3,1},{4,6},{6,4},{5,7},{7,5},{8,10},{10,8},{9,1... | collective-permute-start | bytes 98312 | tf_op jit(solution)/shard_map/ppermute | solution.py:425
  29.3 0.0 collective-permute-done.6.pair_ref.refs_4_
  29.3 0.4 shard_map.166.refs_8_.own_ref
  29.6 0.1 collective-permute-start.7
  29.7 2.1 %collective-permute-done.14.refs_7_ = bf16[64,256]{1,0:T(8,128)(2,1)S(1)} collective-permute-done((bf16[64,256]{1,0:T(8,128)(2,1)S(1)}, bf16[64,256]{1,0:T(8,128)(2,1)S(1)}, u32[]{:S(2)}, u32[]{:S(2)}) %collective-permute-start.14) | collective-permute-done | bytes 32800 | tf_op jit(solution)/shard_map/ppermute | solution.py:425
  31.8 0.0 collective-permute-done.9.refs_0_
  31.8 0.4 collective-permute-done.10.refs_1_
  32.2 0.0 collective-permute-done.12.refs_2_
  32.2 0.1 shard_map.170
  32.2 1.5 %collective-permute-start.17 = (bf16[192,256]{1,0:T(8,128)(2,1)S(1)}, bf16[192,256]{1,0:T(8,128)(2,1)S(1)}, u32[]{:S(2)}, u32[]{:S(2)}) collective-permute-start(bf16[192,256]{1,0:T(8,128)(2,1)S(1)} %get-tuple-element.91.refs_0_), channel_id=1, source_target_pairs={{0,8},{4,12},{8,0},{12,4},{1,9},{5,13},{9,1},{13,5},{2,10},{6,14},... | collective-permute-start | bytes 294920 | tf_op jit(solution)/shard_map/ppermute | solution.py:425
  33.7 1.4 %collective-permute-start.15 = (bf16[192,256]{1,0:T(8,128)(2,1)S(1)}, bf16[192,256]{1,0:T(8,128)(2,1)S(1)}, u32[]{:S(2)}, u32[]{:S(2)}) collective-permute-start(bf16[192,256]{1,0:T(8,128)(2,1)S(1)} %get-tuple-element.91.refs_0_), channel_id=1, source_target_pairs={{0,12},{4,8},{8,4},{12,0},{1,13},{5,9},{9,5},{13,1},{2,14},{6,10},... | collective-permute-start | bytes 294920 | tf_op jit(solution)/shard_map/ppermute | solution.py:425
  35.1 1.4 %collective-permute-start.20 = (bf16[192,256]{1,0:T(8,128)(2,1)S(1)}, bf16[192,256]{1,0:T(8,128)(2,1)S(1)}, u32[]{:S(2)}, u32[]{:S(2)}) collective-permute-start(bf16[192,256]{1,0:T(8,128)(2,1)S(1)} %get-tuple-element.91.refs_0_), channel_id=1, source_target_pairs={{0,6},{2,4},{4,2},{6,0},{8,14},{10,12},{12,10},{14,8},{1,7},{3,5},... | collective-permute-start | bytes 294920 | tf_op jit(solution)/shard_map/ppermute | solution.py:431
  36.5 0.8 %collective-permute-start.18 = (bf16[192,256]{1,0:T(8,128)(2,1)S(1)}, bf16[192,256]{1,0:T(8,128)(2,1)S(1)}, u32[]{:S(2)}, u32[]{:S(2)}) collective-permute-start(bf16[192,256]{1,0:T(8,128)(2,1)S(1)} %get-tuple-element.91.refs_0_), channel_id=1, source_target_pairs={{0,2},{2,0},{1,3},{3,1},{4,6},{6,4},{5,7},{7,5},{8,10},{10,8},{9,1... | collective-permute-start | bytes 294920 | tf_op jit(solution)/shard_map/ppermute | solution.py:425
  37.3 0.0 collective-permute-done.7.other_ref
  37.3 1.3 %collective-permute-start.16 = (bf16[192,256]{1,0:T(8,128)(2,1)S(1)}, bf16[192,256]{1,0:T(8,128)(2,1)S(1)}, u32[]{:S(2)}, u32[]{:S(2)}) collective-permute-start(bf16[192,256]{1,0:T(8,128)(2,1)S(1)} %get-tuple-element.91.refs_0_), channel_id=1, source_target_pairs={{0,4},{4,0},{8,12},{12,8},{1,5},{5,1},{9,13},{13,9},{2,6},{6,2},{1... | collective-permute-start | bytes 294920 | tf_op jit(solution)/shard_map/ppermute | solution.py:425
  38.6 2.8 %collective-permute-done.17.refs_3_ = bf16[192,256]{1,0:T(8,128)(2,1)S(1)} collective-permute-done((bf16[192,256]{1,0:T(8,128)(2,1)S(1)}, bf16[192,256]{1,0:T(8,128)(2,1)S(1)}, u32[]{:S(2)}, u32[]{:S(2)}) %collective-permute-start.17) | collective-permute-done | bytes 98336 | tf_op jit(solution)/shard_map/ppermute | solution.py:425
  41.4 1.6 %collective-permute-start.21 = (bf16[192,256]{1,0:T(8,128)(2,1)S(1)}, bf16[192,256]{1,0:T(8,128)(2,1)S(1)}, u32[]{:S(2)}, u32[]{:S(2)}) collective-permute-start(bf16[192,256]{1,0:T(8,128)(2,1)S(1)} %collective-permute-done.17.refs_3_), channel_id=1, source_target_pairs={{0,2},{2,0},{1,3},{3,1},{4,6},{6,4},{5,7},{7,5},{8,10},{10,8},{9,1... | collective-permute-start | bytes 294920 | tf_op jit(solution)/shard_map/ppermute | solution.py:425
  43.0 0.0 collective-permute-done.15.refs_1_
  43.0 0.4 collective-permute-start.19
  43.5 0.8 %shard_map.171 = (f32[128,512]{1,0:T(8,128)}, bf16[128,512]{1,0:T(8,128)(2,1)}, f32[1,256]{1,0:T(1,128)}, f32[1,512]{1,0:T(1,128)}) custom-call(bf16[128,512]{1,0:T(8,128)(2,1)S(1)} %get-tuple-element.53.cot_ref, bf16[128,512]{1,0:T(8,128)(2,1)S(1)} %get-tuple-element.52.refs_0_.node_ref, f32[1,512]{1,0:T(1,128)S(1)} %get-tuple-element.54.gain_ref, ...), custom_call_target="tpu_custom_call" | custom-call | flops 100000000 | bytes 1000000 | tf_op jit(solution)/shard_map/pallas_call | solution.py:407
  44.3 0.0 collective-permute-done.20.refs_6_
  44.3 0.0 collective-permute-done.18.refs_4_
  44.3 0.0 collective-permute-done.16.refs_2_
  44.3 1.8 %collective-permute-done.21.refs_7_ = bf16[192,256]{1,0:T(8,128)(2,1)S(1)} collective-permute-done((bf16[192,256]{1,0:T(8,128)(2,1)S(1)}, bf16[192,256]{1,0:T(8,128)(2,1)S(1)}, u32[]{:S(2)}, u32[]{:S(2)}) %collective-permute-start.21) | collective-permute-done | bytes 98336 | tf_op jit(solution)/shard_map/ppermute | solution.py:425
  46.0 1.6 %collective-permute-done.19.refs_5_ = bf16[192,256]{1,0:T(8,128)(2,1)S(1)} collective-permute-done((bf16[192,256]{1,0:T(8,128)(2,1)S(1)}, bf16[192,256]{1,0:T(8,128)(2,1)S(1)}, u32[]{:S(2)}, u32[]{:S(2)}) %collective-permute-start.19) | collective-permute-done | bytes 98336 | tf_op jit(solution)/shard_map/ppermute | solution.py:425
  47.7 1.2 %shard_map.172 = (f32[512,256]{1,0:T(8,128)}, f32[512,256]{1,0:T(8,128)}, f32[256,512]{1,0:T(8,128)}) custom-call(bf16[192,256]{1,0:T(8,128)(2,1)S(1)} %get-tuple-element.91.refs_0_, bf16[192,256]{1,0:T(8,128)(2,1)S(1)} %collective-permute-done.15.refs_1_, bf16[192,256]{1,0:T(8,128)(2,1)S(1)} %collective-permute-done.16.refs_2_, ...), custom_call_target="tpu_custom_call" | custom-call | flops 100000000 | bytes 1000000 | tf_op jit(solution)/shard_map/pallas_call | solution.py:407
  (3 shorter events, 0.1 us)
Async XLA Ops:
  1.8 9.0 %collective-permute-start.2 = (bf16[64,512]{1,0:T(8,128)(2,1)S(1)}, bf16[64,512]{1,0:T(8,128)(2,1)S(1)}, u32[]{:S(2)}, u32[]{:S(2)}) collective-permute-start(bf16[64,512]{1,0:T(8,128)(2,1)S(1)} %get-tuple-element.64), channel_id=1, source_target_pairs={{0,2},{2,0},{1,3},{3,1},{4,6},{6,4},{5,7},{7,5},{8,10},{10,8},{9,1... | collective-permute-start | bytes 196616 | tf_op jit(solution)/shard_map/ppermute | solution.py:420
  4.8 5.9 %collective-permute-start = (bf16[32,512]{1,0:T(8,128)(2,1)S(1)}, bf16[32,512]{1,0:T(8,128)(2,1)S(1)}, u32[]{:S(2)}, u32[]{:S(2)}) collective-permute-start(bf16[32,512]{1,0:T(8,128)(2,1)S(1)} %get-tuple-element.62), channel_id=1, source_target_pairs={{0,4},{4,8},{8,12},{12,0},{1,5},{5,9},{9,13},{13,1},{2,6},{6,10},{... | collective-permute-start | bytes 98312 | tf_op jit(solution)/shard_map/ppermute | solution.py:420
  6.4 4.4 %collective-permute-start.1 = (bf16[32,512]{1,0:T(8,128)(2,1)S(1)}, bf16[32,512]{1,0:T(8,128)(2,1)S(1)}, u32[]{:S(2)}, u32[]{:S(2)}) collective-permute-start(bf16[32,512]{1,0:T(8,128)(2,1)S(1)} %get-tuple-element.63), channel_id=1, source_target_pairs={{0,12},{4,0},{8,4},{12,8},{1,13},{5,1},{9,5},{13,9},{2,14},{6,2},{... | collective-permute-start | bytes 98312 | tf_op jit(solution)/shard_map/ppermute | solution.py:420
  11.6 1.4 %collective-permute-start.3 = (bf16[128,512]{1,0:T(8,128)(2,1)S(1)}, bf16[128,512]{1,0:T(8,128)(2,1)S(1)}, u32[]{:S(2)}, u32[]{:S(2)}) collective-permute-start(bf16[128,512]{1,0:T(8,128)(2,1)S(1)} %get-tuple-element.67.own_ref), channel_id=1, source_target_pairs={{0,1},{1,0},{2,3},{3,2},{4,5},{5,4},{6,7},{7,6},{8,9},{9,8},{10,11... | collective-permute-start | bytes 393224 | tf_op jit(solution)/shard_map/ppermute | solution.py:420
  14.4 6.1 %collective-permute-start.8 = (bf16[304,256]{1,0:T(8,128)(2,1)S(1)}, bf16[304,256]{1,0:T(8,128)(2,1)S(1)}, u32[]{:S(2)}, u32[]{:S(2)}) collective-permute-start(bf16[304,256]{1,0:T(8,128)(2,1)S(1)} %get-tuple-element.76), channel_id=1, source_target_pairs={{0,2},{2,0},{1,3},{3,1},{4,6},{6,4},{5,7},{7,5},{8,10},{10,8},{9,1... | collective-permute-start | bytes 466952 | tf_op jit(solution)/shard_map/ppermute | solution.py:425
  14.9 11.2 %collective-permute-start.4 = (bf16[80,512]{1,0:T(8,128)(2,1)S(1)}, bf16[80,512]{1,0:T(8,128)(2,1)S(1)}, u32[]{:S(2)}, u32[]{:S(2)}) collective-permute-start(bf16[80,512]{1,0:T(8,128)(2,1)S(1)} %get-tuple-element.73), channel_id=1, source_target_pairs={{0,12},{4,8},{8,4},{12,0},{1,13},{5,9},{9,5},{13,1},{2,14},{6,10},... | collective-permute-start | bytes 245768 | tf_op jit(solution)/shard_map/ppermute | solution.py:425
  18.4 7.6 %collective-permute-start.13 = (bf16[64,512]{1,0:T(8,128)(2,1)S(1)}, bf16[64,512]{1,0:T(8,128)(2,1)S(1)}, u32[]{:S(2)}, u32[]{:S(2)}) collective-permute-start(bf16[64,512]{1,0:T(8,128)(2,1)S(1)} %get-tuple-element.84), channel_id=1, source_target_pairs={{0,8},{4,12},{8,0},{12,4},{1,9},{5,13},{9,1},{13,5},{2,10},{6,14},... | collective-permute-start | bytes 196616 | tf_op jit(solution)/shard_map/ppermute | solution.py:425
  18.4 4.6 %collective-permute-start.11 = (bf16[96,256]{1,0:T(8,128)(2,1)S(1)}, bf16[96,256]{1,0:T(8,128)(2,1)S(1)}, u32[]{:S(2)}, u32[]{:S(2)}) collective-permute-start(bf16[96,256]{1,0:T(8,128)(2,1)S(1)} %get-tuple-element.80), channel_id=1, source_target_pairs={{0,2},{2,0},{1,3},{3,1},{4,6},{6,4},{5,7},{7,5},{8,10},{10,8},{9,1... | collective-permute-start | bytes 147464 | tf_op jit(solution)/shard_map/ppermute | solution.py:425
  20.1 9.1 %collective-permute-start.6 = (bf16[192,256]{1,0:T(8,128)(2,1)S(1)}, bf16[192,256]{1,0:T(8,128)(2,1)S(1)}, u32[]{:S(2)}, u32[]{:S(2)}) collective-permute-start(bf16[192,256]{1,0:T(8,128)(2,1)S(1)} %get-tuple-element.75), channel_id=1, source_target_pairs={{0,2},{2,0},{1,3},{3,1},{4,6},{6,4},{5,7},{7,5},{8,10},{10,8},{9,1... | collective-permute-start | bytes 294920 | tf_op jit(solution)/shard_map/ppermute | solution.py:425
  20.6 7.2 %collective-permute-start.5 = (bf16[80,512]{1,0:T(8,128)(2,1)S(1)}, bf16[80,512]{1,0:T(8,128)(2,1)S(1)}, u32[]{:S(2)}, u32[]{:S(2)}) collective-permute-start(bf16[80,512]{1,0:T(8,128)(2,1)S(1)} %get-tuple-element.74), channel_id=1, source_target_pairs={{0,4},{4,0},{8,12},{12,8},{1,5},{5,1},{9,13},{13,9},{2,6},{6,2},{1... | collective-permute-start | bytes 245768 | tf_op jit(solution)/shard_map/ppermute | solution.py:425
  23.0 8.8 %collective-permute-start.9 = (bf16[144,256]{1,0:T(8,128)(2,1)S(1)}, bf16[144,256]{1,0:T(8,128)(2,1)S(1)}, u32[]{:S(2)}, u32[]{:S(2)}) collective-permute-start(bf16[144,256]{1,0:T(8,128)(2,1)S(1)} %get-tuple-element.78), channel_id=1, source_target_pairs={{0,12},{4,8},{8,4},{12,0},{1,13},{5,9},{9,5},{13,1},{2,14},{6,10},... | collective-permute-start | bytes 221192 | tf_op jit(solution)/shard_map/ppermute | solution.py:425
  26.1 6.1 %collective-permute-start.10 = (bf16[144,256]{1,0:T(8,128)(2,1)S(1)}, bf16[144,256]{1,0:T(8,128)(2,1)S(1)}, u32[]{:S(2)}, u32[]{:S(2)}) collective-permute-start(bf16[144,256]{1,0:T(8,128)(2,1)S(1)} %get-tuple-element.79), channel_id=1, source_target_pairs={{0,8},{4,12},{8,0},{12,4},{1,9},{5,13},{9,1},{13,5},{2,10},{6,14},... | collective-permute-start | bytes 221192 | tf_op jit(solution)/shard_map/ppermute | solution.py:425
  26.2 6.0 %collective-permute-start.12 = (bf16[144,256]{1,0:T(8,128)(2,1)S(1)}, bf16[144,256]{1,0:T(8,128)(2,1)S(1)}, u32[]{:S(2)}, u32[]{:S(2)}) collective-permute-start(bf16[144,256]{1,0:T(8,128)(2,1)S(1)} %shard_map.168.refs_4_), channel_id=1, source_target_pairs={{0,4},{4,0},{8,12},{12,8},{1,5},{5,1},{9,13},{13,9},{2,6},{6,2},{1... | collective-permute-start | bytes 221192 | tf_op jit(solution)/shard_map/ppermute | solution.py:425
  27.8 4.0 %collective-permute-start.14 = (bf16[64,256]{1,0:T(8,128)(2,1)S(1)}, bf16[64,256]{1,0:T(8,128)(2,1)S(1)}, u32[]{:S(2)}, u32[]{:S(2)}) collective-permute-start(bf16[64,256]{1,0:T(8,128)(2,1)S(1)} %get-tuple-element.87), channel_id=1, source_target_pairs={{0,2},{2,0},{1,3},{3,1},{4,6},{6,4},{5,7},{7,5},{8,10},{10,8},{9,1... | collective-permute-start | bytes 98312 | tf_op jit(solution)/shard_map/ppermute | solution.py:425
  29.6 7.6 %collective-permute-start.7 = (bf16[128,512]{1,0:T(8,128)(2,1)S(1)}, bf16[128,512]{1,0:T(8,128)(2,1)S(1)}, u32[]{:S(2)}, u32[]{:S(2)}) collective-permute-start(bf16[128,512]{1,0:T(8,128)(2,1)S(1)} %shard_map.166.refs_8_.own_ref), channel_id=1, source_target_pairs={{0,1},{1,0},{2,3},{3,2},{4,5},{5,4},{6,7},{7,6},{8,9},{9,8},{10,11... | collective-permute-start | bytes 393224 | tf_op jit(solution)/shard_map/ppermute | solution.py:420
  32.2 9.2 %collective-permute-start.17 = (bf16[192,256]{1,0:T(8,128)(2,1)S(1)}, bf16[192,256]{1,0:T(8,128)(2,1)S(1)}, u32[]{:S(2)}, u32[]{:S(2)}) collective-permute-start(bf16[192,256]{1,0:T(8,128)(2,1)S(1)} %get-tuple-element.91.refs_0_), channel_id=1, source_target_pairs={{0,8},{4,12},{8,0},{12,4},{1,9},{5,13},{9,1},{13,5},{2,10},{6,14},... | collective-permute-start | bytes 294920 | tf_op jit(solution)/shard_map/ppermute | solution.py:425
  33.7 9.3 %collective-permute-start.15 = (bf16[192,256]{1,0:T(8,128)(2,1)S(1)}, bf16[192,256]{1,0:T(8,128)(2,1)S(1)}, u32[]{:S(2)}, u32[]{:S(2)}) collective-permute-start(bf16[192,256]{1,0:T(8,128)(2,1)S(1)} %get-tuple-element.91.refs_0_), channel_id=1, source_target_pairs={{0,12},{4,8},{8,4},{12,0},{1,13},{5,9},{9,5},{13,1},{2,14},{6,10},... | collective-permute-start | bytes 294920 | tf_op jit(solution)/shard_map/ppermute | solution.py:425
  35.1 9.1 %collective-permute-start.20 = (bf16[192,256]{1,0:T(8,128)(2,1)S(1)}, bf16[192,256]{1,0:T(8,128)(2,1)S(1)}, u32[]{:S(2)}, u32[]{:S(2)}) collective-permute-start(bf16[192,256]{1,0:T(8,128)(2,1)S(1)} %get-tuple-element.91.refs_0_), channel_id=1, source_target_pairs={{0,6},{2,4},{4,2},{6,0},{8,14},{10,12},{12,10},{14,8},{1,7},{3,5},... | collective-permute-start | bytes 294920 | tf_op jit(solution)/shard_map/ppermute | solution.py:431
  36.5 7.8 %collective-permute-start.18 = (bf16[192,256]{1,0:T(8,128)(2,1)S(1)}, bf16[192,256]{1,0:T(8,128)(2,1)S(1)}, u32[]{:S(2)}, u32[]{:S(2)}) collective-permute-start(bf16[192,256]{1,0:T(8,128)(2,1)S(1)} %get-tuple-element.91.refs_0_), channel_id=1, source_target_pairs={{0,2},{2,0},{1,3},{3,1},{4,6},{6,4},{5,7},{7,5},{8,10},{10,8},{9,1... | collective-permute-start | bytes 294920 | tf_op jit(solution)/shard_map/ppermute | solution.py:425
  37.3 7.0 %collective-permute-start.16 = (bf16[192,256]{1,0:T(8,128)(2,1)S(1)}, bf16[192,256]{1,0:T(8,128)(2,1)S(1)}, u32[]{:S(2)}, u32[]{:S(2)}) collective-permute-start(bf16[192,256]{1,0:T(8,128)(2,1)S(1)} %get-tuple-element.91.refs_0_), channel_id=1, source_target_pairs={{0,4},{4,0},{8,12},{12,8},{1,5},{5,1},{9,13},{13,9},{2,6},{6,2},{1... | collective-permute-start | bytes 294920 | tf_op jit(solution)/shard_map/ppermute | solution.py:425
  41.4 4.6 %collective-permute-start.21 = (bf16[192,256]{1,0:T(8,128)(2,1)S(1)}, bf16[192,256]{1,0:T(8,128)(2,1)S(1)}, u32[]{:S(2)}, u32[]{:S(2)}) collective-permute-start(bf16[192,256]{1,0:T(8,128)(2,1)S(1)} %collective-permute-done.17.refs_3_), channel_id=1, source_target_pairs={{0,2},{2,0},{1,3},{3,1},{4,6},{6,4},{5,7},{7,5},{8,10},{10,8},{9,1... | collective-permute-start | bytes 294920 | tf_op jit(solution)/shard_map/ppermute | solution.py:425
  43.0 4.6 %collective-permute-start.19 = (bf16[192,256]{1,0:T(8,128)(2,1)S(1)}, bf16[192,256]{1,0:T(8,128)(2,1)S(1)}, u32[]{:S(2)}, u32[]{:S(2)}) collective-permute-start(bf16[192,256]{1,0:T(8,128)(2,1)S(1)} %collective-permute-done.15.refs_1_), channel_id=1, source_target_pairs={{0,2},{2,0},{1,3},{3,1},{4,6},{6,4},{5,7},{7,5},{8,10},{10,8},{9,1... | collective-permute-start | bytes 294920 | tf_op jit(solution)/shard_map/ppermute | solution.py:425

commit v11 on v9

--- a/solution.py
+++ b/solution.py
@@ -84,7 +84,8 @@
 
 
 def local_kernel(*refs):
-    node_ref, ins, refs = refs[0], refs[1 : 1 + N_FETCHED], refs[1 + N_FETCHED :]
+    node_ref, w_src_other_ref, w_dst_other_ref, bias_other_ref, *refs = refs
+    ins, refs = refs[:N_FETCHED], refs[N_FETCHED:]
     pre_ref, pick_ref, collect_ref, spread_ref, scatter_ref, *refs = refs
     w_src_ref, w_dst_ref, w_out_ref, gain_ref, cot_ref, count_ref, src_ref, dst_ref, bias_ref, sems = refs
     outs = (src_ref, dst_ref, count_ref, bias_ref, w_src_ref, w_dst_ref, w_out_ref, gain_ref, cot_ref)
@@ -92,23 +93,27 @@
     node = node_ref[...]
     rows = node.shape[0]
     edges = src_ref.shape[1]
-    for copy in copies[:3]:
+    for copy in copies:
         copy.wait()
-    scatter_ref[...] = one_hot(iota(scatter_ref.shape, 0) == src_ref[...])
+    weights = [w_src_ref[...], w_src_other_ref[...], w_dst_ref[...], w_dst_other_ref[...]]
+    projected = dot(node, jnp.concatenate(weights, axis=1))
+    both = projected.shape[1] // 2
+    projected = jnp.concatenate([projected[:, :both], projected[:, both:]], axis=0)
+    high, low = split(projected)
+    src_row = src_ref[...]
+    scatter_ref[...] = one_hot(iota(scatter_ref.shape, 0) == src_row)
     used = usable_row(count_ref, edges) > 0
     collect_ref[...] = one_hot((iota((rows, edges), 0) == dst_ref[...]) & used)
-    source = columns_of(src_ref[...], 128)
+    source = columns_of(src_row, 128)
     target = columns_of(dst_ref[...], 128)
     lane = iota(source.shape, 1)
     used = usable_columns(count_ref, edges, 128) > 0
     near = one_hot(source == lane)
     pick_ref[...] = one_hot(source == lane + rows)
     spread_ref[...] = one_hot((target == lane) & used)
-    both = jnp.concatenate([dot(near, node), dot(one_hot(target == lane), node)], axis=1).astype(bf16)
-    for copy in copies[3:]:
-        copy.wait()
-    weights = jnp.concatenate([w_src_ref[...], w_dst_ref[...]], axis=0)
-    pre_ref[...] = dot(both, weights) + bias_ref[...]
+    ends = jnp.concatenate([near, one_hot(target == lane)], axis=1)
+    bias = jnp.concatenate([bias_ref[...], bias_other_ref[...]], axis=1)
+    pre_ref[...] = dot(ends, high) + dot(ends, low) + bias
 
 
 def twice(x):
@@ -119,24 +124,10 @@
     return jnp.concatenate(split(x), axis=0)
 
 
-def forward_kernel(pre_ref, pick_ref, collect_ref, w_src_ref, w_out_ref, *rest):
-    *halo_refs, factor_ref, hidden_ref, partial_ref = rest
-    halo = jnp.concatenate([r[...] for r in halo_refs], axis=0)
-    far = stacked(dot(halo, w_src_ref[...]))
-    pre = pre_ref[...] + dot(twice(pick_ref[...]), far)
-    sig = 0.5 + 0.5 * jnp.tanh(0.5 * pre)
-    factor_ref[...] = sig * (1.0 + pre * (1.0 - sig))
-    hidden = dot(collect_ref[...], (pre * sig).astype(bf16))
-    high, low = split(hidden)
-    hidden_ref[...] = high
-    w_out = w_out_ref[...]
-    partial_ref[...] = (dot(high, w_out) + dot(low, w_out)).astype(bf16)
-
-
-def backward_kernel(
+def edge_kernel(
     geometry,
-    node_ref, collect_ref, spread_ref, scatter_ref, w_out_ref, gain_ref, cot_ref,
-    factor_ref, hidden_ref, own_ref, other_ref,
+    node_ref, pre_ref, pick_ref, collect_ref, spread_ref, scatter_ref,
+    w_src_ref, w_src_other_ref, w_out_ref, w_out_other_ref, gain_ref, cot_ref,
     *rest,
 ):
     peers, chunk, n_halo, paired = geometry
@@ -145,7 +136,24 @@
     normed_ref, local_ref, target_ref, *message_refs = rest[n_halo:]
     node = node_ref[...]
     rows, width = node.shape
-    aggregate = own_ref[...].astype(f32) + other_ref[...].astype(f32)
+    hid = w_src_ref.shape[1]
+    halo_rows = jnp.concatenate([r[...] for r in halo_refs], axis=0)
+
+    weights = jnp.concatenate([w_src_ref[...], w_src_other_ref[...]], axis=1)
+    far = stacked(dot(halo_rows, weights))
+    pre = pre_ref[...] + dot(twice(pick_ref[...]), far)
+    sig = 0.5 + 0.5 * jnp.tanh(0.5 * pre)
+    hidden = dot(collect_ref[...], (pre * sig).astype(bf16))
+    pre, sig = pre[:, :hid], sig[:, :hid]
+    factor = sig * (1.0 + pre * (1.0 - sig))
+    hidden_low, parts = None, []
+    for at, w_ref in ((0, w_out_ref), (hid, w_out_other_ref)):
+        high, low = split(hidden[:, at : at + hid])
+        hidden_low = high if at == 0 else hidden_low
+        w_out = w_ref[...]
+        parts.append(dot(high, w_out) + dot(low, w_out))
+    aggregate = parts[0] + parts[1]
+
     center = aggregate - jnp.mean(aggregate, axis=1, keepdims=True)
     variance = jnp.mean(center * center, axis=1, keepdims=True)
     inverse = lax.rsqrt(variance + EPSILON)
@@ -163,9 +171,9 @@
     gain_part = jnp.sum(upstream * normed, axis=0, keepdims=True)
 
     act_grad = dot(twice(spread_ref[...]), stacked(dot(agg_grad, w_out_ref[...], NT)))
-    pre_grad = (act_grad * factor_ref[...]).astype(bf16)
-
-    table = jnp.concatenate([node] + [r[...] for r in halo_refs], axis=0)
+    pre_grad = (act_grad * factor).astype(bf16)
+
+    table = jnp.concatenate([node, halo_rows], axis=0)
     by_source = dot(scatter_ref[...], pre_grad)
     by_target = dot(collect_ref[...], pre_grad)
     local_ref[...] = by_source[:rows]
@@ -173,11 +181,10 @@
     by_source_low = by_source.astype(bf16)
     target_ref[...] = by_target_low
 
-    hid = by_source.shape[1]
     bias_part = jnp.sum(by_target, axis=0, keepdims=True)
     src_part = dot(table, by_source_low, TN).astype(bf16)
     dst_part = dot(node, by_target_low, TN).astype(bf16)
-    out_part = dot(hidden_ref[...], agg_grad, TN).astype(bf16)
+    out_part = dot(hidden_low, agg_grad, TN).astype(bf16)
     vectors = [bias_part] + [gain_part[:, at : at + hid] for at in range(0, width, hid)]
     tail = tail_of(vectors)
     back = by_source_low[rows:]
@@ -300,25 +307,37 @@
         gain_ref[:, k * hid : (k + 1) * hid] = tail[2 + 2 * k : 3 + 2 * k] + tail[3 + 2 * k : 4 + 2 * k]
 
 
-def place_kernel(order, *refs):
-    count = len(order)
-    mine, theirs = refs[:count], refs[count : 2 * count]
-    src_ref, dst_ref, out_ref = refs[2 * count :]
+def relay_kernel(*refs):
+    *_, strip_ref, out_ref = refs
+    out_ref[...] = strip_ref[...]
+
+
+def place_kernel(lines, which, a_ref, b_ref, c_ref, d_ref, *refs):
+    src_hbm, dst_hbm, out_hbm, src_ref, dst_ref, out_ref, sems = refs[-7:]
     first = lax.axis_index("sub") == 0
     mesh = lax.axis_index("mesh")
-    width, hid = src_ref.shape
-    strip = width // count
-    narrow = hid // count
-    for at, k in enumerate(order):
-        a, b = mine[at][...], theirs[at][...]
-        low = jnp.where(first, a, b).astype(f32)
-        high = jnp.where(first, b, a).astype(f32)
-        start = pl.multiple_of((mesh ^ k) * strip, strip)
-        src_ref[pl.ds(start, strip), :] = low[:strip]
-        dst_ref[pl.ds(start, strip), :] = high[:strip]
-        start = pl.multiple_of((mesh ^ k) * narrow, narrow)
-        out_ref[pl.ds(start, narrow), 0:hid] = low[strip:]
-        out_ref[pl.ds(start, narrow), hid:] = high[strip:]
+    strip, hid = src_ref.shape[1:]
+    narrow = out_ref.shape[1]
+    copies = []
+
+    def put(ref, hbm, at, rows):
+        start = pl.multiple_of((mesh ^ which[at]) * rows, rows)
+        copies.append(pltpu.make_async_copy(ref.at[at], hbm.at[pl.ds(start, rows)], sems.at[len(copies)]))
+        copies[-1].start()
+
+    for at, (mine_ref, theirs_ref) in enumerate(((a_ref, c_ref), (b_ref, d_ref))):
+        mine, theirs = mine_ref[...], theirs_ref[...]
+        low = jnp.where(first, mine, theirs).astype(f32)
+        high = jnp.where(first, theirs, mine).astype(f32)
+        src_ref[at] = low[:strip]
+        put(src_ref, src_hbm, at, strip)
+        dst_ref[at] = high[:strip]
+        put(dst_ref, dst_hbm, at, strip)
+        out_ref[at, :, 0:hid] = low[strip:]
+        out_ref[at, :, hid:] = high[strip:]
+        put(out_ref, out_hbm, at, narrow)
+    for copy in copies:
+        copy.wait()
 
 
 def sum_kernel(chunk, arrived_ref, out_ref, bias_ref, gain_ref):
@@ -396,13 +415,14 @@
     return jax.ShapeDtypeStruct(dims, dtype)
 
 
-def call(kernel, outs, *args, specs=None, out_specs=None, flops=10**8, scratch=()):
+def call(kernel, outs, *args, specs=None, out_specs=None, flops=10**8, scratch=(), **options):
     return pl.pallas_call(
         kernel,
         out_shape=outs,
         in_specs=specs or [VMEM] * len(args),
         out_specs=out_specs or jax.tree.map(lambda _: VMEM, outs),
         scratch_shapes=scratch,
+        **options,
         compiler_params=pltpu.CompilerParams(vmem_limit_bytes=VMEM_LIMIT),
         cost_estimate=pl.CostEstimate(flops=flops, bytes_accessed=10**6, transcendentals=0),
     )(*args)
@@ -416,6 +436,12 @@
 def across(x, axis, k):
     count = lax.axis_size(axis)
     return lax.ppermute(x, axis, [(i, i ^ k) for i in range(count)])
+
+
+def diagonal(x):
+    lines, pairs = lax.axis_size("mesh"), lax.axis_size("sub")
+    moves = [(m * pairs + p, (m ^ 1) * pairs + (p ^ 1)) for m in range(lines) for p in range(pairs)]
+    return lax.ppermute(x, ("mesh", "sub"), moves)
 
 
 def paired_sums(messages, lines, strip, narrow, width, hid, node_terms):
@@ -444,14 +470,25 @@
     )
     mine = {k: across(own, "mesh", k) for k in order}
     mine[0] = own
-    theirs = {0: across(own, "sub", 1)}
-    theirs[1] = across(theirs[0], "mesh", 1)
-    theirs |= {k: across(mine[k], "sub", 1) for k in (3, 2)}
-    placed = (0, 3, 1, 2)
+    theirs = {0: across(own, "sub", 1), 1: diagonal(own)}
+    early = (mine[0], mine[1], theirs[0], theirs[1])
+    theirs[2] = across(mine[2], "sub", 1)
+    last = call(relay_kernel, shape(own.shape, bf16), *early, mine[3])
+    theirs[3] = across(last, "sub", 1)
+    wholes = [shape((width, hid), f32), shape((width, hid), f32), shape((hid, width), f32)]
+    scratch = [
+        pltpu.VMEM((2, strip, hid), f32), pltpu.VMEM((2, strip, hid), f32), pltpu.VMEM((2, narrow, width), f32),
+        pltpu.SemaphoreType.DMA((6,)),
+    ]
     grads = call(
-        functools.partial(place_kernel, placed),
-        [shape((width, hid), f32), shape((width, hid), f32), shape((hid, width), f32)],
-        *[mine[k] for k in placed], *[theirs[k] for k in placed],
+        functools.partial(place_kernel, lines, (0, 1)), wholes, *early,
+        out_specs=[HBM] * 3, scratch=scratch, flops=10**8,
+    )
+    grads = call(
+        functools.partial(place_kernel, lines, (3, 2)), wholes,
+        mine[3], mine[2], theirs[3], theirs[2], *grads,
+        specs=[VMEM] * 4 + [HBM] * 3, out_specs=[HBM] * 3, scratch=scratch,
+        input_output_aliases={4: 0, 5: 1, 6: 2},
     )
     return (*grads, tail), node_part
 
@@ -499,18 +536,20 @@
         edge_src.reshape(1, edges), edge_dst.reshape(1, edges), block_count,
         hidden_bias.reshape(1, hid), w_src, w_dst, w_out, norm_gain.reshape(1, width), cotangent,
     ]
+    w_src_other, w_dst_other, w_out_other = [shifted(w, "lat", 1) for w in (w_src, w_dst, w_out)]
+    bias_other = shifted(fetched[3], "lat", 1)
     pre, pick, collect, spread, scatter, w_src, w_dst, w_out, gain, cot = call(
         local_kernel,
         [
-            shape((edges, hid), f32),
+            shape((edges, 2 * hid), f32),
             shape((edges, 4 * halo), bf16),
             shape((rows, edges), bf16),
             shape((edges, rows), bf16),
             shape((rows + 4 * halo, edges), bf16),
         ]
         + [shape(x.shape, x.dtype) for x in fetched[4:]],
-        node, *[in_hbm(x) for x in fetched],
-        specs=[VMEM] + [HBM] * len(fetched),
+        node, w_src_other, w_dst_other, bias_other, *[in_hbm(x) for x in fetched],
+        specs=[VMEM] * 4 + [HBM] * len(fetched),
         scratch=[
             pltpu.SMEM(block_count.shape, jnp.int32),
             pltpu.VMEM((1, edges), jnp.int32),
@@ -520,12 +559,6 @@
         ],
     )
 
-    factor, hidden, partial = call(
-        forward_kernel,
-        [shape((edges, hid), f32), shape((rows, hid), bf16), shape((rows, width), bf16)],
-        pre, pick, collect, w_src, w_out, *arrived,
-    )
-    other = shifted(partial, "lat", 1)
 
     lines = lax.axis_size("mesh")
     paired = merged and lines == 4
@@ -539,10 +572,10 @@
         message_shapes = [shape((peers, chunk + TAIL, hid), bf16)]
         message_shapes += [shape((n, hid), bf16) for n in piece]
     normed, local, target, *messages = call(
-        functools.partial(backward_kernel, (peers, chunk, n_halo, paired)),
+        functools.partial(edge_kernel, (peers, chunk, n_halo, paired)),
         [shape((rows, width), f32), shape((rows, hid), f32), shape((rows, hid), bf16)]
         + message_shapes,
-        node, collect, spread, scatter, w_out, gain, cot, factor, hidden, partial, other, *arrived,
+        node, pre, pick, collect, spread, scatter, w_src, w_src_other, w_out, w_out_other, gain, cot, *arrived,
         scratch=[
             pltpu.VMEM((hid, width), bf16),
             pltpu.VMEM((2 * halo, hid), bf16),

time: 49 us -> 51.3 us (1.047)
  starting transfers between devices: 27.8 us -> 29.5 us
  Pallas kernels: 8.07 us -> 8.75 us
    ppermute x0 -> x1, starting transfers between devices: none -> 1.29 us  [diagonal(): return lax.ppermute(x, ('mesh', 'sub'), moves)]
    ppermute x0 -> x1, waiting for transfers between devices: none -> 1.13 us  [diagonal(): return lax.ppermute(x, ('mesh', 'sub'), moves)]
    ppermute x17 -> x16, waiting for transfers between devices: 10.9 us -> 9.97 us  [across(): return lax.ppermute(x, axis, [(i, i ^ k) for i in range(count)])]
    ppermute x5 -> x8, starting transfers between devices: 6.9 us -> 7.65 us  [shifted(): return lax.ppermute(x, axis, [(i, (i + by) % count) for i in range(count)])]
    pallas_call x11 -> x12, Pallas kernels: 8.07 us -> 8.75 us  [call(): pl.pallas_call(kernel, out_shape=outs, in_specs=specs or [VMEM] * len(arg...]
    ppermute x5 -> x8, waiting for transfers between devices: 1.38 us -> 0.99 us  [shifted(): return lax.ppermute(x, axis, [(i, (i + by) % count) for i in range(count)])]
    ppermute x17 -> x16, starting transfers between devices: 20.9 us -> 20.6 us  [across(): return lax.ppermute(x, axis, [(i, i ^ k) for i in range(count)])]
  transfers between devices with their start and end apart: 22 -> 25, of which waited for: 8 -> 8; matrix products, arithmetic and copies ran while one was open for 0% -> 0% of each run, Pallas kernels for 7% -> 11%
where the time goes in v11:
time: 51.3 us; the launch traced here: 51.1 us
  starting transfers between devices  29.5 us (58%)
  waiting for transfers between devices  12.1 us (24%)
  Pallas kernels  8.75 us (17%)
  between operations  0.76 us (1%)
    ppermute x16, starting transfers between devices, across(): return lax.ppermute(x, axis, [(i, i ^ k) for i in range(count)])  20.6 us
    ppermute x16, waiting for transfers between devices, across(): return lax.ppermute(x, axis, [(i, i ^ k) for i in range(count)])  9.97 us
    pallas_call x12, Pallas kernels, call(): pl.pallas_call(kernel, out_shape=outs, in_specs=specs or [VMEM] * len(arg...  8.75 us
    ppermute x8, starting transfers between devices, shifted(): return lax.ppermute(x, axis, [(i, (i + by) % count) for i in range(count)])  7.65 us
    ppermute x1, starting transfers between devices, diagonal(): return lax.ppermute(x, ('mesh', 'sub'), moves)  1.29 us
    ppermute x1, waiting for transfers between devices, diagonal(): return lax.ppermute(x, ('mesh', 'sub'), moves)  1.13 us
  transfers between devices with their start and end apart: 25, of which 8 were waited for; matrix products, arithmetic and copies ran while one was open for 0% of the time, Pallas kernels for 11%

profile of v11, /device:TPU:0, one launch (start us, length us, event | category | flops | bytes accessed | tf_op | source)
XLA Modules:
  0.0 51.1 jit_solution(1988659380568179473)
XLA Ops:
  0.6 0.5 %collective-permute-start = (bf16[512,256]{1,0:T(8,128)(2,1)}, bf16[512,256]{1,0:T(8,128)(2,1)S(1)}, u32[]{:S(2)}, u32[]{:S(2)}) collective-permute-start(bf16[512,256]{1,0:T(8,128)(2,1)} %refs_8_.1), channel_id=1, source_target_pairs={{0,1},{1,0},{2,3},{3,2},{4,5},{5,4},{6,7},{7,6},{8,9},{9,8},{10,11... | collective-permute-start | bytes 786440 | tf_op jit(solution)/shard_map/ppermute | solution.py:433
  1.1 0.1 collective-permute-start.1
  1.2 0.4 collective-permute-start.3
  1.7 1.2 %shard_map.162 = (bf16[128,512]{1,0:T(8,128)(2,1)S(1)}, s32[1,4,32]{2,1,0:T(4,128)S(1)}, bf16[32,512]{1,0:T(8,128)(2,1)S(1)}, bf16[32,512]{1,0:T(8,128)(2,1)S(1)}, bf16[64,512]{1,0:T(8,128)(2,1)S(1)}) custom-call(bf16[128,512]{1,0:T(8,128)(2,1)} %node_hbm.1, s32[1,4,32]{2,1,0:T(4,128)} %send_hbm.1), custom_call_target="tpu_custom_call" | custom-call | flops 100000000 | bytes 1000000 | tf_op jit(solution)/shard_map/pallas_call | solution.py:419
  2.8 0.0 copy-start
  2.8 2.6 %collective-permute-start.6 = (bf16[64,512]{1,0:T(8,128)(2,1)S(1)}, bf16[64,512]{1,0:T(8,128)(2,1)S(1)}, u32[]{:S(2)}, u32[]{:S(2)}) collective-permute-start(bf16[64,512]{1,0:T(8,128)(2,1)S(1)} %get-tuple-element.64), channel_id=1, source_target_pairs={{0,2},{2,0},{1,3},{3,1},{4,6},{6,4},{5,7},{7,5},{8,10},{10,8},{9,1... | collective-permute-start | bytes 196616 | tf_op jit(solution)/shard_map/ppermute | solution.py:433
  5.5 0.0 copy-done
  5.5 0.2 collective-permute-start.2
  5.6 1.0 %collective-permute-done.2.refs_3_ = f32[1,256]{1,0:T(1,128)S(1)} collective-permute-done((f32[1,256]{1,0:T(1,128)S(1)}, f32[1,256]{1,0:T(1,128)S(1)}, u32[]{:S(2)}, u32[]{:S(2)}) %collective-permute-start.2) | collective-permute-done | bytes 1056 | tf_op jit(solution)/shard_map/ppermute | solution.py:433
  6.6 1.6 %collective-permute-start.4 = (bf16[32,512]{1,0:T(8,128)(2,1)S(1)}, bf16[32,512]{1,0:T(8,128)(2,1)S(1)}, u32[]{:S(2)}, u32[]{:S(2)}) collective-permute-start(bf16[32,512]{1,0:T(8,128)(2,1)S(1)} %get-tuple-element.62), channel_id=1, source_target_pairs={{0,4},{4,8},{8,12},{12,0},{1,5},{5,9},{9,13},{13,1},{2,6},{6,10},{... | collective-permute-start | bytes 98312 | tf_op jit(solution)/shard_map/ppermute | solution.py:433
  8.2 0.0 collective-permute-done.refs_1_.w_src_other_ref
  8.2 2.2 %collective-permute-start.5 = (bf16[32,512]{1,0:T(8,128)(2,1)S(1)}, bf16[32,512]{1,0:T(8,128)(2,1)S(1)}, u32[]{:S(2)}, u32[]{:S(2)}) collective-permute-start(bf16[32,512]{1,0:T(8,128)(2,1)S(1)} %get-tuple-element.63), channel_id=1, source_target_pairs={{0,12},{4,0},{8,4},{12,8},{1,13},{5,1},{9,5},{13,9},{2,14},{6,2},{... | collective-permute-start | bytes 98312 | tf_op jit(solution)/shard_map/ppermute | solution.py:433
  10.5 0.0 collective-permute-done.1.refs_2_
  10.5 2.1 %shard_map.163 = (f32[512,512]{1,0:T(8,128)S(1)}, bf16[512,128]{1,0:T(8,128)(2,1)S(1)}, bf16[128,512]{1,0:T(8,128)(2,1)S(1)}, bf16[512,128]{1,0:T(8,128)(2,1)S(1...) custom-call(bf16[128,512]{1,0:T(8,128)(2,1)S(1)} %get-tuple-element., ...), custom_call_target="tpu_custom_call" | custom-call | flops 100000000 | bytes 1000000 | tf_op jit(solution)/shard_map/pallas_call | solution.py:419
  12.5 0.0 collective-permute-done.4.rest_0_
  12.5 0.0 collective-permute-done.5.rest_1_
  12.6 0.0 collective-permute-done.6.rest_2_
  12.6 0.0 collective-permute-done.3.w_out_other_ref
  12.6 2.3 %shard_map.164 = (f32[128,512]{1,0:T(8,128)S(1)}, f32[128,256]{1,0:T(8,128)S(1)}, bf16[128,256]{1,0:T(8,128)(2,1)S(1)}, bf16[272,256]{1,0:T(8,128)(2,1)S(1)}, bf...) custom-call(bf16[128,512]{1,0:T(8,128)(2,1)S(1)} %get-tuple-element., ...), custom_call_target="tpu_custom_call" | custom-call | flops 100000000 | bytes 1000000 | tf_op jit(solution)/shard_map/pallas_call | solution.py:419
  14.9 0.8 %collective-permute-start.11 = (bf16[272,256]{1,0:T(8,128)(2,1)S(1)}, bf16[272,256]{1,0:T(8,128)(2,1)S(1)}, u32[]{:S(2)}, u32[]{:S(2)}) collective-permute-start(bf16[272,256]{1,0:T(8,128)(2,1)S(1)} %get-tuple-element.73), channel_id=1, source_target_pairs={{0,2},{2,0},{1,3},{3,1},{4,6},{6,4},{5,7},{7,5},{8,10},{10,8},{9,1... | collective-permute-start | bytes 417800 | tf_op jit(solution)/shard_map/ppermute | solution.py:438
  15.6 3.6 %collective-permute-start.7 = (bf16[80,512]{1,0:T(8,128)(2,1)S(1)}, bf16[80,512]{1,0:T(8,128)(2,1)S(1)}, u32[]{:S(2)}, u32[]{:S(2)}) collective-permute-start(bf16[80,512]{1,0:T(8,128)(2,1)S(1)} %get-tuple-element.70), channel_id=1, source_target_pairs={{0,12},{4,8},{8,4},{12,0},{1,13},{5,9},{9,5},{13,1},{2,14},{6,10},... | collective-permute-start | bytes 245768 | tf_op jit(solution)/shard_map/ppermute | solution.py:438
  19.2 1.3 %collective-permute-start.14 = (bf16[128,256]{1,0:T(8,128)(2,1)S(1)}, bf16[128,256]{1,0:T(8,128)(2,1)S(1)}, u32[]{:S(2)}, u32[]{:S(2)}) collective-permute-start(bf16[128,256]{1,0:T(8,128)(2,1)S(1)} %get-tuple-element.77), channel_id=1, source_target_pairs={{0,2},{2,0},{1,3},{3,1},{4,6},{6,4},{5,7},{7,5},{8,10},{10,8},{9,1... | collective-permute-start | bytes 196616 | tf_op jit(solution)/shard_map/ppermute | solution.py:438
  20.6 0.0 collective-permute-start.16
  20.6 0.8 %collective-permute-start.8 = (bf16[80,512]{1,0:T(8,128)(2,1)S(1)}, bf16[80,512]{1,0:T(8,128)(2,1)S(1)}, u32[]{:S(2)}, u32[]{:S(2)}) collective-permute-start(bf16[80,512]{1,0:T(8,128)(2,1)S(1)} %get-tuple-element.71), channel_id=1, source_target_pairs={{0,4},{4,0},{8,12},{12,8},{1,5},{5,1},{9,13},{13,9},{2,6},{6,2},{1... | collective-permute-start | bytes 245768 | tf_op jit(solution)/shard_map/ppermute | solution.py:438
  21.3 0.0 collective-permute-done.11.arrived_ref
  21.4 0.7 %collective-permute-start.9 = (bf16[192,256]{1,0:T(8,128)(2,1)S(1)}, bf16[192,256]{1,0:T(8,128)(2,1)S(1)}, u32[]{:S(2)}, u32[]{:S(2)}) collective-permute-start(bf16[192,256]{1,0:T(8,128)(2,1)S(1)} %get-tuple-element.72), channel_id=1, source_target_pairs={{0,2},{2,0},{1,3},{3,1},{4,6},{6,4},{5,7},{7,5},{8,10},{10,8},{9,1... | collective-permute-start | bytes 294920 | tf_op jit(solution)/shard_map/ppermute | solution.py:438
  22.1 1.9 %collective-permute-done.14.arrived_ref = bf16[128,256]{1,0:T(8,128)(2,1)S(1)} collective-permute-done((bf16[128,256]{1,0:T(8,128)(2,1)S(1)}, bf16[128,256]{1,0:T(8,128)(2,1)S(1)}, u32[]{:S(2)}, u32[]{:S(2)}) %collective-permute-start.14) | collective-permute-done | bytes 65568 | tf_op jit(solution)/shard_map/ppermute | solution.py:438
  24.0 1.8 %collective-permute-start.12 = (bf16[144,256]{1,0:T(8,128)(2,1)S(1)}, bf16[144,256]{1,0:T(8,128)(2,1)S(1)}, u32[]{:S(2)}, u32[]{:S(2)}) collective-permute-start(bf16[144,256]{1,0:T(8,128)(2,1)S(1)} %get-tuple-element.75), channel_id=1, source_target_pairs={{0,12},{4,8},{8,4},{12,0},{1,13},{5,9},{9,5},{13,1},{2,14},{6,10},... | collective-permute-start | bytes 221192 | tf_op jit(solution)/shard_map/ppermute | solution.py:438
  25.8 0.8 %collective-permute-done.16.refs_1_ = bf16[64,512]{1,0:T(8,128)(2,1)S(1)} collective-permute-done((bf16[64,512]{1,0:T(8,128)(2,1)S(1)}, bf16[64,512]{1,0:T(8,128)(2,1)S(1)}, u32[]{:S(2)}, u32[]{:S(2)}) %collective-permute-start.16) | collective-permute-done | bytes 65568 | tf_op jit(solution)/shard_map/ppermute | solution.py:438
  26.6 0.0 collective-permute-start.13
  26.6 0.0 collective-permute-done.7.three_ref.refs_0_
  26.6 3.9 %collective-permute-start.15 = (bf16[144,256]{1,0:T(8,128)(2,1)S(1)}, bf16[144,256]{1,0:T(8,128)(2,1)S(1)}, u32[]{:S(2)}, u32[]{:S(2)}) collective-permute-start(bf16[144,256]{1,0:T(8,128)(2,1)S(1)} %shard_map.167.refs_4_), channel_id=1, source_target_pairs={{0,4},{4,0},{8,12},{12,8},{1,5},{5,1},{9,13},{13,9},{2,6},{6,2},{1... | collective-permute-start | bytes 221192 | tf_op jit(solution)/shard_map/ppermute | solution.py:438
  30.5 0.0 collective-permute-done.8.one_ref.refs_2_
  30.6 1.5 %collective-permute-start.17 = (bf16[64,256]{1,0:T(8,128)(2,1)S(1)}, bf16[64,256]{1,0:T(8,128)(2,1)S(1)}, u32[]{:S(2)}, u32[]{:S(2)}) collective-permute-start(bf16[64,256]{1,0:T(8,128)(2,1)S(1)} %get-tuple-element.84), channel_id=1, source_target_pairs={{0,2},{2,0},{1,3},{3,1},{4,6},{6,4},{5,7},{7,5},{8,10},{10,8},{9,1... | collective-permute-start | bytes 98312 | tf_op jit(solution)/shard_map/ppermute | solution.py:438
  32.1 0.0 collective-permute-done.9.pair_ref.refs_4_
  32.1 0.4 shard_map.165.refs_8_.own_ref
  32.5 2.8 %collective-permute-done.17.refs_7_ = bf16[64,256]{1,0:T(8,128)(2,1)S(1)} collective-permute-done((bf16[64,256]{1,0:T(8,128)(2,1)S(1)}, bf16[64,256]{1,0:T(8,128)(2,1)S(1)}, u32[]{:S(2)}, u32[]{:S(2)}) %collective-permute-start.17) | collective-permute-done | bytes 32800 | tf_op jit(solution)/shard_map/ppermute | solution.py:438
  35.3 0.0 collective-permute-done.12.refs_0_
  35.3 0.0 collective-permute-done.13.refs_1_
  35.3 0.0 collective-permute-done.15.refs_2_
  35.3 0.1 shard_map.169
  35.4 1.3 %collective-permute-start.22 = (bf16[192,256]{1,0:T(8,128)(2,1)S(1)}, bf16[192,256]{1,0:T(8,128)(2,1)S(1)}, u32[]{:S(2)}, u32[]{:S(2)}) collective-permute-start(bf16[192,256]{1,0:T(8,128)(2,1)S(1)} %get-tuple-element.88.refs_0_.a_ref), channel_id=1, source_target_pairs={{0,6},{2,4},{4,2},{6,0},{8,14},{10,12},{12,10},{14,8},{1,7},{3,5},... | collective-permute-start | bytes 294920 | tf_op jit(solution)/shard_map/ppermute | solution.py:444
  36.7 0.1 collective-permute-start.19
  36.8 0.6 %collective-permute-start.21 = (bf16[192,256]{1,0:T(8,128)(2,1)S(1)}, bf16[192,256]{1,0:T(8,128)(2,1)S(1)}, u32[]{:S(2)}, u32[]{:S(2)}) collective-permute-start(bf16[192,256]{1,0:T(8,128)(2,1)S(1)} %get-tuple-element.88.refs_0_.a_ref), channel_id=1, source_target_pairs={{0,2},{2,0},{1,3},{3,1},{4,6},{6,4},{5,7},{7,5},{8,10},{10,8},{9,1... | collective-permute-start | bytes 294920 | tf_op jit(solution)/shard_map/ppermute | solution.py:438
  37.4 1.6 %collective-permute-start.20 = (bf16[192,256]{1,0:T(8,128)(2,1)S(1)}, bf16[192,256]{1,0:T(8,128)(2,1)S(1)}, u32[]{:S(2)}, u32[]{:S(2)}) collective-permute-start(bf16[192,256]{1,0:T(8,128)(2,1)S(1)} %get-tuple-element.88.refs_0_.a_ref), channel_id=1, source_target_pairs={{0,4},{4,0},{8,12},{12,8},{1,5},{5,1},{9,13},{13,9},{2,6},{6,2},{1... | collective-permute-start | bytes 294920 | tf_op jit(solution)/shard_map/ppermute | solution.py:438
  39.0 2.4 %collective-permute-start.18 = (bf16[192,256]{1,0:T(8,128)(2,1)S(1)}, bf16[192,256]{1,0:T(8,128)(2,1)S(1)}, u32[]{:S(2)}, u32[]{:S(2)}) collective-permute-start(bf16[192,256]{1,0:T(8,128)(2,1)S(1)} %get-tuple-element.88.refs_0_.a_ref), channel_id=1, source_target_pairs={{0,12},{4,8},{8,4},{12,0},{1,13},{5,9},{9,5},{13,1},{2,14},{6,10},... | collective-permute-start | bytes 294920 | tf_op jit(solution)/shard_map/ppermute | solution.py:438
  41.3 1.1 %collective-permute-done.22.refs_3_.d_ref = bf16[192,256]{1,0:T(8,128)(2,1)S(1)} collective-permute-done((bf16[192,256]{1,0:T(8,128)(2,1)S(1)}, bf16[192,256]{1,0:T(8,128)(2,1)S(1)}, u32[]{:S(2)}, u32[]{:S(2)}) %collective-permute-start.22) | collective-permute-done | bytes 98336 | tf_op jit(solution)/shard_map/ppermute | solution.py:444
  42.5 0.0 collective-permute-start.10
  42.5 0.8 %collective-permute-done.19.b_ref = bf16[192,256]{1,0:T(8,128)(2,1)S(1)} collective-permute-done((bf16[192,256]{1,0:T(8,128)(2,1)S(1)}, bf16[192,256]{1,0:T(8,128)(2,1)S(1)}, u32[]{:S(2)}, u32[]{:S(2)}) %collective-permute-start.19) | collective-permute-done | bytes 98336 | tf_op jit(solution)/shard_map/ppermute | solution.py:438
  43.3 0.0 collective-permute-start.24
  43.3 0.0 collective-permute-done.21.refs_2_.c_ref
  43.3 0.0 collective-permute-done.20.refs_1_.b_ref
  43.3 2.2 %collective-permute-done.18.refs_4_.a_ref = bf16[192,256]{1,0:T(8,128)(2,1)S(1)} collective-permute-done((bf16[192,256]{1,0:T(8,128)(2,1)S(1)}, bf16[192,256]{1,0:T(8,128)(2,1)S(1)}, u32[]{:S(2)}, u32[]{:S(2)}) %collective-permute-start.18) | collective-permute-done | bytes 98336 | tf_op jit(solution)/shard_map/ppermute | solution.py:438
  45.5 1.5 %collective-permute-start.23 = (bf16[192,256]{1,0:T(8,128)(2,1)S(1)}, bf16[192,256]{1,0:T(8,128)(2,1)S(1)}, u32[]{:S(2)}, u32[]{:S(2)}) collective-permute-start(bf16[192,256]{1,0:T(8,128)(2,1)S(1)} %shard_map.171), channel_id=1, source_target_pairs={{0,2},{2,0},{1,3},{3,1},{4,6},{6,4},{5,7},{7,5},{8,10},{10,8},{9,1... | collective-permute-start | bytes 294920 | tf_op jit(solution)/shard_map/ppermute | solution.py:438
  46.9 0.0 collective-permute-done.10.other_ref
  47.0 0.8 %shard_map.170 = (f32[128,512]{1,0:T(8,128)}, bf16[128,512]{1,0:T(8,128)(2,1)}, f32[1,256]{1,0:T(1,128)}, f32[1,512]{1,0:T(1,128)}) custom-call(bf16[128,512]{1,0:T(8,128)(2,1)S(1)} %get-tuple-element.53.cot_ref, bf16[128,512]{1,0:T(8,128)(2,1)S(1)} %get-tuple-element.52.refs_0_.node_ref, f32[1,512]{1,0:T(1,128)S(1)} %get-tuple-element.54.gain_ref, ...), custom_call_target="tpu_custom_call" | custom-call | flops 100000000 | bytes 1000000 | tf_op jit(solution)/shard_map/pallas_call | solution.py:419
  47.8 0.9 %shard_map.172 = (f32[512,256]{1,0:T(8,128)}, f32[512,256]{1,0:T(8,128)}, f32[256,512]{1,0:T(8,128)}) custom-call(bf16[192,256]{1,0:T(8,128)(2,1)S(1)} %get-tuple-element.88.refs_0_.a_ref, bf16[192,256]{1,0:T(8,128)(2,1)S(1)} %collective-permute-done.20.refs_1_.b_ref, bf16[192,256]{1,0:T(8,128)(2,1)S(1)} %collective-permute-done.21.refs_2_.c_ref, ...), custom_call_target="tpu_custom_call" | custom-call | flops 100000000 | bytes 1000000 | tf_op jit(solution)/shard_map/pallas_call | solution.py:419
  48.7 0.0 collective-permute-done.24.d_ref
  48.7 1.4 %collective-permute-done.23.c_ref = bf16[192,256]{1,0:T(8,128)(2,1)S(1)} collective-permute-done((bf16[192,256]{1,0:T(8,128)(2,1)S(1)}, bf16[192,256]{1,0:T(8,128)(2,1)S(1)}, u32[]{:S(2)}, u32[]{:S(2)}) %collective-permute-start.23) | collective-permute-done | bytes 98336 | tf_op jit(solution)/shard_map/ppermute | solution.py:438
  50.2 0.9 %shard_map.173 = (f32[512,256]{1,0:T(8,128)}, f32[512,256]{1,0:T(8,128)}, f32[256,512]{1,0:T(8,128)}) custom-call(bf16[192,256]{1,0:T(8,128)(2,1)S(1)} %collective-permute-done.18.refs_4_.a_ref, bf16[192,256]{1,0:T(8,128)(2,1)S(1)} %collective-permute-done.19.b_ref, ...), custom_call_target="tpu_custom_call", output_to_operand_aliasing={{0}: (4, {}), {1}: (5, {}), {2}: (6, {})} | custom-call | flops 100000000 | bytes 1000000 | tf_op jit(solution)/shard_map/pallas_call | solution.py:419
  (4 shorter events, 0.1 us)
Async XLA Ops:
  0.6 7.6 %collective-permute-start = (bf16[512,256]{1,0:T(8,128)(2,1)}, bf16[512,256]{1,0:T(8,128)(2,1)S(1)}, u32[]{:S(2)}, u32[]{:S(2)}) collective-permute-start(bf16[512,256]{1,0:T(8,128)(2,1)} %refs_8_.1), channel_id=1, source_target_pairs={{0,1},{1,0},{2,3},{3,2},{4,5},{5,4},{6,7},{7,6},{8,9},{9,8},{10,11... | collective-permute-start | bytes 786440 | tf_op jit(solution)/shard_map/ppermute | solution.py:433
  1.1 9.3 %collective-permute-start.1 = (bf16[512,256]{1,0:T(8,128)(2,1)}, bf16[512,256]{1,0:T(8,128)(2,1)S(1)}, u32[]{:S(2)}, u32[]{:S(2)}) collective-permute-start(bf16[512,256]{1,0:T(8,128)(2,1)} %refs_9_.1), channel_id=1, source_target_pairs={{0,1},{1,0},{2,3},{3,2},{4,5},{5,4},{6,7},{7,6},{8,9},{9,8},{10,11... | collective-permute-start | bytes 786440 | tf_op jit(solution)/shard_map/ppermute | solution.py:433
  1.2 11.3 %collective-permute-start.3 = (bf16[256,512]{1,0:T(8,128)(2,1)}, bf16[256,512]{1,0:T(8,128)(2,1)S(1)}, u32[]{:S(2)}, u32[]{:S(2)}) collective-permute-start(bf16[256,512]{1,0:T(8,128)(2,1)} %refs_10_.1), channel_id=1, source_target_pairs={{0,1},{1,0},{2,3},{3,2},{4,5},{5,4},{6,7},{7,6},{8,9},{9,8},{10,11... | collective-permute-start | bytes 786440 | tf_op jit(solution)/shard_map/ppermute | solution.py:433
  2.8 2.6 %copy-start = (f32[256]{0:T(256)S(1)}, f32[256]{0:T(256)}, u32[]{:S(2)}) copy-start(f32[256]{0:T(256)} %param.18) | copy-start | bytes 3076
  2.8 9.7 %collective-permute-start.6 = (bf16[64,512]{1,0:T(8,128)(2,1)S(1)}, bf16[64,512]{1,0:T(8,128)(2,1)S(1)}, u32[]{:S(2)}, u32[]{:S(2)}) collective-permute-start(bf16[64,512]{1,0:T(8,128)(2,1)S(1)} %get-tuple-element.64), channel_id=1, source_target_pairs={{0,2},{2,0},{1,3},{3,1},{4,6},{6,4},{5,7},{7,5},{8,10},{10,8},{9,1... | collective-permute-start | bytes 196616 | tf_op jit(solution)/shard_map/ppermute | solution.py:433
  5.5 1.1 %collective-permute-start.2 = (f32[1,256]{1,0:T(1,128)S(1)}, f32[1,256]{1,0:T(1,128)S(1)}, u32[]{:S(2)}, u32[]{:S(2)}) collective-permute-start(f32[1,256]{1,0:T(1,128)S(1)} %bitcast.10), channel_id=1, source_target_pairs={{0,1},{1,0},{2,3},{3,2},{4,5},{5,4},{6,7},{7,6},{8,9},{9,8},{10,11... | collective-permute-start | bytes 3080 | tf_op jit(solution)/shard_map/ppermute | solution.py:433
  6.6 5.9 %collective-permute-start.4 = (bf16[32,512]{1,0:T(8,128)(2,1)S(1)}, bf16[32,512]{1,0:T(8,128)(2,1)S(1)}, u32[]{:S(2)}, u32[]{:S(2)}) collective-permute-start(bf16[32,512]{1,0:T(8,128)(2,1)S(1)} %get-tuple-element.62), channel_id=1, source_target_pairs={{0,4},{4,8},{8,12},{12,0},{1,5},{5,9},{9,13},{13,1},{2,6},{6,10},{... | collective-permute-start | bytes 98312 | tf_op jit(solution)/shard_map/ppermute | solution.py:433
  8.2 4.3 %collective-permute-start.5 = (bf16[32,512]{1,0:T(8,128)(2,1)S(1)}, bf16[32,512]{1,0:T(8,128)(2,1)S(1)}, u32[]{:S(2)}, u32[]{:S(2)}) collective-permute-start(bf16[32,512]{1,0:T(8,128)(2,1)S(1)} %get-tuple-element.63), channel_id=1, source_target_pairs={{0,12},{4,0},{8,4},{12,8},{1,13},{5,1},{9,5},{13,9},{2,14},{6,2},{... | collective-permute-start | bytes 98312 | tf_op jit(solution)/shard_map/ppermute | solution.py:433
  14.9 6.5 %collective-permute-start.11 = (bf16[272,256]{1,0:T(8,128)(2,1)S(1)}, bf16[272,256]{1,0:T(8,128)(2,1)S(1)}, u32[]{:S(2)}, u32[]{:S(2)}) collective-permute-start(bf16[272,256]{1,0:T(8,128)(2,1)S(1)} %get-tuple-element.73), channel_id=1, source_target_pairs={{0,2},{2,0},{1,3},{3,1},{4,6},{6,4},{5,7},{7,5},{8,10},{10,8},{9,1... | collective-permute-start | bytes 417800 | tf_op jit(solution)/shard_map/ppermute | solution.py:438
  15.6 11.0 %collective-permute-start.7 = (bf16[80,512]{1,0:T(8,128)(2,1)S(1)}, bf16[80,512]{1,0:T(8,128)(2,1)S(1)}, u32[]{:S(2)}, u32[]{:S(2)}) collective-permute-start(bf16[80,512]{1,0:T(8,128)(2,1)S(1)} %get-tuple-element.70), channel_id=1, source_target_pairs={{0,12},{4,8},{8,4},{12,0},{1,13},{5,9},{9,5},{13,1},{2,14},{6,10},... | collective-permute-start | bytes 245768 | tf_op jit(solution)/shard_map/ppermute | solution.py:438
  19.2 4.7 %collective-permute-start.14 = (bf16[128,256]{1,0:T(8,128)(2,1)S(1)}, bf16[128,256]{1,0:T(8,128)(2,1)S(1)}, u32[]{:S(2)}, u32[]{:S(2)}) collective-permute-start(bf16[128,256]{1,0:T(8,128)(2,1)S(1)} %get-tuple-element.77), channel_id=1, source_target_pairs={{0,2},{2,0},{1,3},{3,1},{4,6},{6,4},{5,7},{7,5},{8,10},{10,8},{9,1... | collective-permute-start | bytes 196616 | tf_op jit(solution)/shard_map/ppermute | solution.py:438
  20.6 6.0 %collective-permute-start.16 = (bf16[64,512]{1,0:T(8,128)(2,1)S(1)}, bf16[64,512]{1,0:T(8,128)(2,1)S(1)}, u32[]{:S(2)}, u32[]{:S(2)}) collective-permute-start(bf16[64,512]{1,0:T(8,128)(2,1)S(1)} %get-tuple-element.81), channel_id=1, source_target_pairs={{0,8},{4,12},{8,0},{12,4},{1,9},{5,13},{9,1},{13,5},{2,10},{6,14},... | collective-permute-start | bytes 196616 | tf_op jit(solution)/shard_map/ppermute | solution.py:438
  20.6 10.0 %collective-permute-start.8 = (bf16[80,512]{1,0:T(8,128)(2,1)S(1)}, bf16[80,512]{1,0:T(8,128)(2,1)S(1)}, u32[]{:S(2)}, u32[]{:S(2)}) collective-permute-start(bf16[80,512]{1,0:T(8,128)(2,1)S(1)} %get-tuple-element.71), channel_id=1, source_target_pairs={{0,4},{4,0},{8,12},{12,8},{1,5},{5,1},{9,13},{13,9},{2,6},{6,2},{1... | collective-permute-start | bytes 245768 | tf_op jit(solution)/shard_map/ppermute | solution.py:438
  21.4 10.7 %collective-permute-start.9 = (bf16[192,256]{1,0:T(8,128)(2,1)S(1)}, bf16[192,256]{1,0:T(8,128)(2,1)S(1)}, u32[]{:S(2)}, u32[]{:S(2)}) collective-permute-start(bf16[192,256]{1,0:T(8,128)(2,1)S(1)} %get-tuple-element.72), channel_id=1, source_target_pairs={{0,2},{2,0},{1,3},{3,1},{4,6},{6,4},{5,7},{7,5},{8,10},{10,8},{9,1... | collective-permute-start | bytes 294920 | tf_op jit(solution)/shard_map/ppermute | solution.py:438
  24.0 11.3 %collective-permute-start.12 = (bf16[144,256]{1,0:T(8,128)(2,1)S(1)}, bf16[144,256]{1,0:T(8,128)(2,1)S(1)}, u32[]{:S(2)}, u32[]{:S(2)}) collective-permute-start(bf16[144,256]{1,0:T(8,128)(2,1)S(1)} %get-tuple-element.75), channel_id=1, source_target_pairs={{0,12},{4,8},{8,4},{12,0},{1,13},{5,9},{9,5},{13,1},{2,14},{6,10},... | collective-permute-start | bytes 221192 | tf_op jit(solution)/shard_map/ppermute | solution.py:438
  26.6 8.7 %collective-permute-start.13 = (bf16[144,256]{1,0:T(8,128)(2,1)S(1)}, bf16[144,256]{1,0:T(8,128)(2,1)S(1)}, u32[]{:S(2)}, u32[]{:S(2)}) collective-permute-start(bf16[144,256]{1,0:T(8,128)(2,1)S(1)} %get-tuple-element.76), channel_id=1, source_target_pairs={{0,8},{4,12},{8,0},{12,4},{1,9},{5,13},{9,1},{13,5},{2,10},{6,14},... | collective-permute-start | bytes 221192 | tf_op jit(solution)/shard_map/ppermute | solution.py:438
  26.6 8.7 %collective-permute-start.15 = (bf16[144,256]{1,0:T(8,128)(2,1)S(1)}, bf16[144,256]{1,0:T(8,128)(2,1)S(1)}, u32[]{:S(2)}, u32[]{:S(2)}) collective-permute-start(bf16[144,256]{1,0:T(8,128)(2,1)S(1)} %shard_map.167.refs_4_), channel_id=1, source_target_pairs={{0,4},{4,0},{8,12},{12,8},{1,5},{5,1},{9,13},{13,9},{2,6},{6,2},{1... | collective-permute-start | bytes 221192 | tf_op jit(solution)/shard_map/ppermute | solution.py:438
  30.6 4.8 %collective-permute-start.17 = (bf16[64,256]{1,0:T(8,128)(2,1)S(1)}, bf16[64,256]{1,0:T(8,128)(2,1)S(1)}, u32[]{:S(2)}, u32[]{:S(2)}) collective-permute-start(bf16[64,256]{1,0:T(8,128)(2,1)S(1)} %get-tuple-element.84), channel_id=1, source_target_pairs={{0,2},{2,0},{1,3},{3,1},{4,6},{6,4},{5,7},{7,5},{8,10},{10,8},{9,1... | collective-permute-start | bytes 98312 | tf_op jit(solution)/shard_map/ppermute | solution.py:438
  35.4 7.1 %collective-permute-start.22 = (bf16[192,256]{1,0:T(8,128)(2,1)S(1)}, bf16[192,256]{1,0:T(8,128)(2,1)S(1)}, u32[]{:S(2)}, u32[]{:S(2)}) collective-permute-start(bf16[192,256]{1,0:T(8,128)(2,1)S(1)} %get-tuple-element.88.refs_0_.a_ref), channel_id=1, source_target_pairs={{0,6},{2,4},{4,2},{6,0},{8,14},{10,12},{12,10},{14,8},{1,7},{3,5},... | collective-permute-start | bytes 294920 | tf_op jit(solution)/shard_map/ppermute | solution.py:444
  36.7 6.6 %collective-permute-start.19 = (bf16[192,256]{1,0:T(8,128)(2,1)S(1)}, bf16[192,256]{1,0:T(8,128)(2,1)S(1)}, u32[]{:S(2)}, u32[]{:S(2)}) collective-permute-start(bf16[192,256]{1,0:T(8,128)(2,1)S(1)} %get-tuple-element.88.refs_0_.a_ref), channel_id=1, source_target_pairs={{0,8},{4,12},{8,0},{12,4},{1,9},{5,13},{9,1},{13,5},{2,10},{6,14},... | collective-permute-start | bytes 294920 | tf_op jit(solution)/shard_map/ppermute | solution.py:438
  36.8 6.5 %collective-permute-start.21 = (bf16[192,256]{1,0:T(8,128)(2,1)S(1)}, bf16[192,256]{1,0:T(8,128)(2,1)S(1)}, u32[]{:S(2)}, u32[]{:S(2)}) collective-permute-start(bf16[192,256]{1,0:T(8,128)(2,1)S(1)} %get-tuple-element.88.refs_0_.a_ref), channel_id=1, source_target_pairs={{0,2},{2,0},{1,3},{3,1},{4,6},{6,4},{5,7},{7,5},{8,10},{10,8},{9,1... | collective-permute-start | bytes 294920 | tf_op jit(solution)/shard_map/ppermute | solution.py:438
  37.4 5.9 %collective-permute-start.20 = (bf16[192,256]{1,0:T(8,128)(2,1)S(1)}, bf16[192,256]{1,0:T(8,128)(2,1)S(1)}, u32[]{:S(2)}, u32[]{:S(2)}) collective-permute-start(bf16[192,256]{1,0:T(8,128)(2,1)S(1)} %get-tuple-element.88.refs_0_.a_ref), channel_id=1, source_target_pairs={{0,4},{4,0},{8,12},{12,8},{1,5},{5,1},{9,13},{13,9},{2,6},{6,2},{1... | collective-permute-start | bytes 294920 | tf_op jit(solution)/shard_map/ppermute | solution.py:438
  39.0 6.5 %collective-permute-start.18 = (bf16[192,256]{1,0:T(8,128)(2,1)S(1)}, bf16[192,256]{1,0:T(8,128)(2,1)S(1)}, u32[]{:S(2)}, u32[]{:S(2)}) collective-permute-start(bf16[192,256]{1,0:T(8,128)(2,1)S(1)} %get-tuple-element.88.refs_0_.a_ref), channel_id=1, source_target_pairs={{0,12},{4,8},{8,4},{12,0},{1,13},{5,9},{9,5},{13,1},{2,14},{6,10},... | collective-permute-start | bytes 294920 | tf_op jit(solution)/shard_map/ppermute | solution.py:438
  42.5 4.5 %collective-permute-start.10 = (bf16[128,512]{1,0:T(8,128)(2,1)S(1)}, bf16[128,512]{1,0:T(8,128)(2,1)S(1)}, u32[]{:S(2)}, u32[]{:S(2)}) collective-permute-start(bf16[128,512]{1,0:T(8,128)(2,1)S(1)} %shard_map.165.refs_8_.own_ref), channel_id=1, source_target_pairs={{0,1},{1,0},{2,3},{3,2},{4,5},{5,4},{6,7},{7,6},{8,9},{9,8},{10,11... | collective-permute-start | bytes 393224 | tf_op jit(solution)/shard_map/ppermute | solution.py:433
  43.3 5.5 %collective-permute-start.24 = (bf16[192,256]{1,0:T(8,128)(2,1)S(1)}, bf16[192,256]{1,0:T(8,128)(2,1)S(1)}, u32[]{:S(2)}, u32[]{:S(2)}) collective-permute-start(bf16[192,256]{1,0:T(8,128)(2,1)S(1)} %collective-permute-done.19.b_ref), channel_id=1, source_target_pairs={{0,2},{2,0},{1,3},{3,1},{4,6},{6,4},{5,7},{7,5},{8,10},{10,8},{9,1... | collective-permute-start | bytes 294920 | tf_op jit(solution)/shard_map/ppermute | solution.py:438
  45.5 4.7 %collective-permute-start.23 = (bf16[192,256]{1,0:T(8,128)(2,1)S(1)}, bf16[192,256]{1,0:T(8,128)(2,1)S(1)}, u32[]{:S(2)}, u32[]{:S(2)}) collective-permute-start(bf16[192,256]{1,0:T(8,128)(2,1)S(1)} %shard_map.171), channel_id=1, source_target_pairs={{0,2},{2,0},{1,3},{3,1},{4,6},{6,4},{5,7},{7,5},{8,10},{10,8},{9,1... | collective-permute-start | bytes 294920 | tf_op jit(solution)/shard_map/ppermute | solution.py:438

commit v12 on v9

--- a/solution.py
+++ b/solution.py
@@ -300,25 +300,37 @@
         gain_ref[:, k * hid : (k + 1) * hid] = tail[2 + 2 * k : 3 + 2 * k] + tail[3 + 2 * k : 4 + 2 * k]
 
 
-def place_kernel(order, *refs):
-    count = len(order)
-    mine, theirs = refs[:count], refs[count : 2 * count]
-    src_ref, dst_ref, out_ref = refs[2 * count :]
+def relay_kernel(*refs):
+    *_, strip_ref, out_ref = refs
+    out_ref[...] = strip_ref[...]
+
+
+def place_kernel(lines, which, a_ref, b_ref, c_ref, d_ref, *refs):
+    src_hbm, dst_hbm, out_hbm, src_ref, dst_ref, out_ref, sems = refs[-7:]
     first = lax.axis_index("sub") == 0
     mesh = lax.axis_index("mesh")
-    width, hid = src_ref.shape
-    strip = width // count
-    narrow = hid // count
-    for at, k in enumerate(order):
-        a, b = mine[at][...], theirs[at][...]
-        low = jnp.where(first, a, b).astype(f32)
-        high = jnp.where(first, b, a).astype(f32)
-        start = pl.multiple_of((mesh ^ k) * strip, strip)
-        src_ref[pl.ds(start, strip), :] = low[:strip]
-        dst_ref[pl.ds(start, strip), :] = high[:strip]
-        start = pl.multiple_of((mesh ^ k) * narrow, narrow)
-        out_ref[pl.ds(start, narrow), 0:hid] = low[strip:]
-        out_ref[pl.ds(start, narrow), hid:] = high[strip:]
+    strip, hid = src_ref.shape[1:]
+    narrow = out_ref.shape[1]
+    copies = []
+
+    def put(ref, hbm, at, rows):
+        start = pl.multiple_of((mesh ^ which[at]) * rows, rows)
+        copies.append(pltpu.make_async_copy(ref.at[at], hbm.at[pl.ds(start, rows)], sems.at[len(copies)]))
+        copies[-1].start()
+
+    for at, (mine_ref, theirs_ref) in enumerate(((a_ref, c_ref), (b_ref, d_ref))):
+        mine, theirs = mine_ref[...], theirs_ref[...]
+        low = jnp.where(first, mine, theirs).astype(f32)
+        high = jnp.where(first, theirs, mine).astype(f32)
+        src_ref[at] = low[:strip]
+        put(src_ref, src_hbm, at, strip)
+        dst_ref[at] = high[:strip]
+        put(dst_ref, dst_hbm, at, strip)
+        out_ref[at, :, 0:hid] = low[strip:]
+        out_ref[at, :, hid:] = high[strip:]
+        put(out_ref, out_hbm, at, narrow)
+    for copy in copies:
+        copy.wait()
 
 
 def sum_kernel(chunk, arrived_ref, out_ref, bias_ref, gain_ref):
@@ -396,13 +408,14 @@
     return jax.ShapeDtypeStruct(dims, dtype)
 
 
-def call(kernel, outs, *args, specs=None, out_specs=None, flops=10**8, scratch=()):
+def call(kernel, outs, *args, specs=None, out_specs=None, flops=10**8, scratch=(), **options):
     return pl.pallas_call(
         kernel,
         out_shape=outs,
         in_specs=specs or [VMEM] * len(args),
         out_specs=out_specs or jax.tree.map(lambda _: VMEM, outs),
         scratch_shapes=scratch,
+        **options,
         compiler_params=pltpu.CompilerParams(vmem_limit_bytes=VMEM_LIMIT),
         cost_estimate=pl.CostEstimate(flops=flops, bytes_accessed=10**6, transcendentals=0),
     )(*args)
@@ -416,6 +429,12 @@
 def across(x, axis, k):
     count = lax.axis_size(axis)
     return lax.ppermute(x, axis, [(i, i ^ k) for i in range(count)])
+
+
+def diagonal(x):
+    lines, pairs = lax.axis_size("mesh"), lax.axis_size("sub")
+    moves = [(m * pairs + p, (m ^ 1) * pairs + (p ^ 1)) for m in range(lines) for p in range(pairs)]
+    return lax.ppermute(x, ("mesh", "sub"), moves)
 
 
 def paired_sums(messages, lines, strip, narrow, width, hid, node_terms):
@@ -444,14 +463,25 @@
     )
     mine = {k: across(own, "mesh", k) for k in order}
     mine[0] = own
-    theirs = {0: across(own, "sub", 1)}
-    theirs[1] = across(theirs[0], "mesh", 1)
-    theirs |= {k: across(mine[k], "sub", 1) for k in (3, 2)}
-    placed = (0, 3, 1, 2)
+    theirs = {0: across(own, "sub", 1), 1: diagonal(own)}
+    early = (mine[0], mine[1], theirs[0], theirs[1])
+    theirs[2] = across(mine[2], "sub", 1)
+    last = call(relay_kernel, shape(own.shape, bf16), *early, mine[3])
+    theirs[3] = across(last, "sub", 1)
+    wholes = [shape((width, hid), f32), shape((width, hid), f32), shape((hid, width), f32)]
+    scratch = [
+        pltpu.VMEM((2, strip, hid), f32), pltpu.VMEM((2, strip, hid), f32), pltpu.VMEM((2, narrow, width), f32),
+        pltpu.SemaphoreType.DMA((6,)),
+    ]
     grads = call(
-        functools.partial(place_kernel, placed),
-        [shape((width, hid), f32), shape((width, hid), f32), shape((hid, width), f32)],
-        *[mine[k] for k in placed], *[theirs[k] for k in placed],
+        functools.partial(place_kernel, lines, (0, 1)), wholes, *early,
+        out_specs=[HBM] * 3, scratch=scratch, flops=10**8,
+    )
+    grads = call(
+        functools.partial(place_kernel, lines, (3, 2)), wholes,
+        mine[3], mine[2], theirs[3], theirs[2], *grads,
+        specs=[VMEM] * 4 + [HBM] * 3, out_specs=[HBM] * 3, scratch=scratch,
+        input_output_aliases={4: 0, 5: 1, 6: 2},
     )
     return (*grads, tail), node_part
 

time: 49 us -> 49.5 us (1.010)
  starting transfers between devices: 27.8 us -> 26.4 us
  waiting for transfers between devices: 12.3 us -> 13.5 us
  Pallas kernels: 8.07 us -> 8.71 us
    ppermute x17 -> x16, starting transfers between devices: 20.9 us -> 18.1 us  [across(): return lax.ppermute(x, axis, [(i, i ^ k) for i in range(count)])]
    ppermute x0 -> x1, waiting for transfers between devices: none -> 1.62 us  [diagonal(): return lax.ppermute(x, ('mesh', 'sub'), moves)]
    ppermute x0 -> x1, starting transfers between devices: none -> 1.41 us  [diagonal(): return lax.ppermute(x, ('mesh', 'sub'), moves)]
    pallas_call x11 -> x13, Pallas kernels: 8.07 us -> 8.71 us  [call(): pl.pallas_call(kernel, out_shape=outs, in_specs=specs or [VMEM] * len(arg...]
    ppermute x17 -> x16, waiting for transfers between devices: 10.9 us -> 10.5 us  [across(): return lax.ppermute(x, axis, [(i, i ^ k) for i in range(count)])]
  transfers between devices with their start and end apart: 22 -> 22, of which waited for: 8 -> 9; matrix products, arithmetic and copies ran while one was open for 0% -> 0% of each run, Pallas kernels for 7% -> 9%
where the time goes in v12:
time: 49.5 us; the launch traced here: 49.3 us
  starting transfers between devices  26.4 us (53%)
  waiting for transfers between devices  13.5 us (27%)
  Pallas kernels  8.71 us (18%)
  between operations  0.74 us (1%)
    ppermute x16, starting transfers between devices, across(): return lax.ppermute(x, axis, [(i, i ^ k) for i in range(count)])  18.1 us
    ppermute x16, waiting for transfers between devices, across(): return lax.ppermute(x, axis, [(i, i ^ k) for i in range(count)])  10.5 us
    pallas_call x13, Pallas kernels, call(): pl.pallas_call(kernel, out_shape=outs, in_specs=specs or [VMEM] * len(arg...  8.71 us
    ppermute x5, starting transfers between devices, shifted(): return lax.ppermute(x, axis, [(i, (i + by) % count) for i in range(count)])  6.9 us
    ppermute x1, waiting for transfers between devices, diagonal(): return lax.ppermute(x, ('mesh', 'sub'), moves)  1.62 us
    ppermute x1, starting transfers between devices, diagonal(): return lax.ppermute(x, ('mesh', 'sub'), moves)  1.41 us
    ppermute x5, waiting for transfers between devices, shifted(): return lax.ppermute(x, axis, [(i, (i + by) % count) for i in range(count)])  1.38 us
  transfers between devices with their start and end apart: 22, of which 9 were waited for; matrix products, arithmetic and copies ran while one was open for 0% of the time, Pallas kernels for 9%

profile of v12, /device:TPU:0, one launch (start us, length us, event | category | flops | bytes accessed | tf_op | source)
XLA Modules:
  0.0 49.3 jit_solution(8708661710738814065)
XLA Ops:
  0.6 1.2 %shard_map.162 = (bf16[128,512]{1,0:T(8,128)(2,1)S(1)}, s32[1,4,32]{2,1,0:T(4,128)S(1)}, bf16[32,512]{1,0:T(8,128)(2,1)S(1)}, bf16[32,512]{1,0:T(8,128)(2,1)S(1)}, bf16[64,512]{1,0:T(8,128)(2,1)S(1)}) custom-call(bf16[128,512]{1,0:T(8,128)(2,1)} %node_hbm.1, s32[1,4,32]{2,1,0:T(4,128)} %send_hbm.1), custom_call_target="tpu_custom_call" | custom-call | flops 100000000 | bytes 1000000 | tf_op jit(solution)/shard_map/pallas_call | solution.py:412
  1.8 3.0 %collective-permute-start.2 = (bf16[64,512]{1,0:T(8,128)(2,1)S(1)}, bf16[64,512]{1,0:T(8,128)(2,1)S(1)}, u32[]{:S(2)}, u32[]{:S(2)}) collective-permute-start(bf16[64,512]{1,0:T(8,128)(2,1)S(1)} %get-tuple-element.67), channel_id=1, source_target_pairs={{0,2},{2,0},{1,3},{3,1},{4,6},{6,4},{5,7},{7,5},{8,10},{10,8},{9,1... | collective-permute-start | bytes 196616 | tf_op jit(solution)/shard_map/ppermute | solution.py:426
  4.8 1.6 %collective-permute-start = (bf16[32,512]{1,0:T(8,128)(2,1)S(1)}, bf16[32,512]{1,0:T(8,128)(2,1)S(1)}, u32[]{:S(2)}, u32[]{:S(2)}) collective-permute-start(bf16[32,512]{1,0:T(8,128)(2,1)S(1)} %get-tuple-element.65), channel_id=1, source_target_pairs={{0,4},{4,8},{8,12},{12,0},{1,5},{5,9},{9,13},{13,1},{2,6},{6,10},{... | collective-permute-start | bytes 98312 | tf_op jit(solution)/shard_map/ppermute | solution.py:426
  6.4 2.2 %collective-permute-start.1 = (bf16[32,512]{1,0:T(8,128)(2,1)S(1)}, bf16[32,512]{1,0:T(8,128)(2,1)S(1)}, u32[]{:S(2)}, u32[]{:S(2)}) collective-permute-start(bf16[32,512]{1,0:T(8,128)(2,1)S(1)} %get-tuple-element.66), channel_id=1, source_target_pairs={{0,12},{4,0},{8,4},{12,8},{1,13},{5,1},{9,5},{13,9},{2,14},{6,2},{... | collective-permute-start | bytes 98312 | tf_op jit(solution)/shard_map/ppermute | solution.py:426
  8.6 2.1 %shard_map.163 = (f32[512,256]{1,0:T(8,128)S(1)}, bf16[512,128]{1,0:T(8,128)(2,1)S(1)}, bf16[128,512]{1,0:T(8,128)(2,1)S(1)}, bf16[512,128]{1,0:T(8,128)(2,1)S(1...) custom-call(bf16[128,512]{1,0:T(8,128)(2,1)S(1)} %get-tuple-element., ...), custom_call_target="tpu_custom_call" | custom-call | flops 100000000 | bytes 1000000 | tf_op jit(solution)/shard_map/pallas_call | solution.py:412
  10.7 0.0 collective-permute-done.rest_0_
  10.8 0.0 collective-permute-done.1.rest_1_
  10.8 0.0 collective-permute-done.2.rest_2_
  10.8 0.9 %shard_map.164 = (f32[512,256]{1,0:T(8,128)S(1)}, bf16[128,256]{1,0:T(8,128)(2,1)S(1)}, bf16[128,512]{1,0:T(8,128)(2,1)S(1)}) custom-call(f32[512,256]{1,0:T(8,128)S(1)} %get-tuple-element.62.pre_ref, bf16[512,128]{1,0:T(8,128)(2,1)S(1)} %get-tuple-element.63.pick_ref, bf16[128,512]{1,0:T(8,128)(2,1)S(1)} %get-tuple-element.58.collect_ref, ...), custom_call_target="tpu_custom_call" | custom-call | flops 100000000 | bytes 1000000 | tf_op jit(solution)/shard_map/pallas_call | solution.py:412
  11.6 0.1 collective-permute-start.3
  11.7 1.3 %collective-permute-done.3.other_ref = bf16[128,512]{1,0:T(8,128)(2,1)S(1)} collective-permute-done((bf16[128,512]{1,0:T(8,128)(2,1)S(1)}, bf16[128,512]{1,0:T(8,128)(2,1)S(1)}, u32[]{:S(2)}, u32[]{:S(2)}) %collective-permute-start.3) | collective-permute-done | bytes 131104 | tf_op jit(solution)/shard_map/ppermute | solution.py:426
  13.1 1.4 %shard_map.165 = (f32[128,512]{1,0:T(8,128)S(1)}, f32[128,256]{1,0:T(8,128)S(1)}, bf16[128,256]{1,0:T(8,128)(2,1)S(1)}, bf16[272,256]{1,0:T(8,128)(2,1)S(1)}, bf...) custom-call(bf16[128,512]{1,0:T(8,128)(2,1)S(1)} %get-tuple-element., ...), custom_call_target="tpu_custom_call" | custom-call | flops 100000000 | bytes 1000000 | tf_op jit(solution)/shard_map/pallas_call | solution.py:412
  14.4 0.5 collective-permute-start.8
  14.9 3.5 %collective-permute-start.4 = (bf16[80,512]{1,0:T(8,128)(2,1)S(1)}, bf16[80,512]{1,0:T(8,128)(2,1)S(1)}, u32[]{:S(2)}, u32[]{:S(2)}) collective-permute-start(bf16[80,512]{1,0:T(8,128)(2,1)S(1)} %get-tuple-element.76), channel_id=1, source_target_pairs={{0,12},{4,8},{8,4},{12,0},{1,13},{5,9},{9,5},{13,1},{2,14},{6,10},... | collective-permute-start | bytes 245768 | tf_op jit(solution)/shard_map/ppermute | solution.py:431
  18.4 1.7 %collective-permute-start.11 = (bf16[128,256]{1,0:T(8,128)(2,1)S(1)}, bf16[128,256]{1,0:T(8,128)(2,1)S(1)}, u32[]{:S(2)}, u32[]{:S(2)}) collective-permute-start(bf16[128,256]{1,0:T(8,128)(2,1)S(1)} %get-tuple-element.83), channel_id=1, source_target_pairs={{0,2},{2,0},{1,3},{3,1},{4,6},{6,4},{5,7},{7,5},{8,10},{10,8},{9,1... | collective-permute-start | bytes 196616 | tf_op jit(solution)/shard_map/ppermute | solution.py:431
  20.1 0.0 collective-permute-start.13
  20.1 0.8 %collective-permute-start.5 = (bf16[80,512]{1,0:T(8,128)(2,1)S(1)}, bf16[80,512]{1,0:T(8,128)(2,1)S(1)}, u32[]{:S(2)}, u32[]{:S(2)}) collective-permute-start(bf16[80,512]{1,0:T(8,128)(2,1)S(1)} %get-tuple-element.77), channel_id=1, source_target_pairs={{0,4},{4,0},{8,12},{12,8},{1,5},{5,1},{9,13},{13,9},{2,6},{6,2},{1... | collective-permute-start | bytes 245768 | tf_op jit(solution)/shard_map/ppermute | solution.py:431
  20.9 0.0 collective-permute-done.8.arrived_ref
  20.9 0.4 collective-permute-start.6
  21.4 1.7 %collective-permute-done.11.arrived_ref = bf16[128,256]{1,0:T(8,128)(2,1)S(1)} collective-permute-done((bf16[128,256]{1,0:T(8,128)(2,1)S(1)}, bf16[128,256]{1,0:T(8,128)(2,1)S(1)}, u32[]{:S(2)}, u32[]{:S(2)}) %collective-permute-start.11) | collective-permute-done | bytes 65568 | tf_op jit(solution)/shard_map/ppermute | solution.py:431
  23.1 2.2 %collective-permute-start.9 = (bf16[144,256]{1,0:T(8,128)(2,1)S(1)}, bf16[144,256]{1,0:T(8,128)(2,1)S(1)}, u32[]{:S(2)}, u32[]{:S(2)}) collective-permute-start(bf16[144,256]{1,0:T(8,128)(2,1)S(1)} %get-tuple-element.81), channel_id=1, source_target_pairs={{0,12},{4,8},{8,4},{12,0},{1,13},{5,9},{9,5},{13,1},{2,14},{6,10},... | collective-permute-start | bytes 221192 | tf_op jit(solution)/shard_map/ppermute | solution.py:431
  25.3 1.0 %collective-permute-done.13.refs_1_ = bf16[64,512]{1,0:T(8,128)(2,1)S(1)} collective-permute-done((bf16[64,512]{1,0:T(8,128)(2,1)S(1)}, bf16[64,512]{1,0:T(8,128)(2,1)S(1)}, u32[]{:S(2)}, u32[]{:S(2)}) %collective-permute-start.13) | collective-permute-done | bytes 65568 | tf_op jit(solution)/shard_map/ppermute | solution.py:431
  26.3 0.0 collective-permute-start.10
  26.3 0.0 collective-permute-done.4.three_ref.refs_0_
  26.3 1.8 %collective-permute-start.12 = (bf16[144,256]{1,0:T(8,128)(2,1)S(1)}, bf16[144,256]{1,0:T(8,128)(2,1)S(1)}, u32[]{:S(2)}, u32[]{:S(2)}) collective-permute-start(bf16[144,256]{1,0:T(8,128)(2,1)S(1)} %shard_map.168.refs_4_), channel_id=1, source_target_pairs={{0,4},{4,0},{8,12},{12,8},{1,5},{5,1},{9,13},{13,9},{2,6},{6,2},{1... | collective-permute-start | bytes 221192 | tf_op jit(solution)/shard_map/ppermute | solution.py:431
  28.0 0.0 collective-permute-done.5.one_ref.refs_2_
  28.1 1.7 %collective-permute-start.14 = (bf16[64,256]{1,0:T(8,128)(2,1)S(1)}, bf16[64,256]{1,0:T(8,128)(2,1)S(1)}, u32[]{:S(2)}, u32[]{:S(2)}) collective-permute-start(bf16[64,256]{1,0:T(8,128)(2,1)S(1)} %get-tuple-element.90), channel_id=1, source_target_pairs={{0,2},{2,0},{1,3},{3,1},{4,6},{6,4},{5,7},{7,5},{8,10},{10,8},{9,1... | collective-permute-start | bytes 98312 | tf_op jit(solution)/shard_map/ppermute | solution.py:431
  29.8 0.0 collective-permute-done.6.pair_ref.refs_4_
  29.8 0.4 shard_map.166.refs_8_.own_ref
  30.1 1.9 %collective-permute-done.14.refs_7_ = bf16[64,256]{1,0:T(8,128)(2,1)S(1)} collective-permute-done((bf16[64,256]{1,0:T(8,128)(2,1)S(1)}, bf16[64,256]{1,0:T(8,128)(2,1)S(1)}, u32[]{:S(2)}, u32[]{:S(2)}) %collective-permute-start.14) | collective-permute-done | bytes 32800 | tf_op jit(solution)/shard_map/ppermute | solution.py:431
  32.1 0.0 collective-permute-done.9.refs_0_
  32.1 0.0 collective-permute-done.10.refs_1_
  32.1 0.0 collective-permute-done.12.refs_2_
  32.1 0.1 shard_map.170
  32.2 1.4 %collective-permute-start.19 = (bf16[192,256]{1,0:T(8,128)(2,1)S(1)}, bf16[192,256]{1,0:T(8,128)(2,1)S(1)}, u32[]{:S(2)}, u32[]{:S(2)}) collective-permute-start(bf16[192,256]{1,0:T(8,128)(2,1)S(1)} %get-tuple-element.94.refs_0_.a_ref), channel_id=1, source_target_pairs={{0,6},{2,4},{4,2},{6,0},{8,14},{10,12},{12,10},{14,8},{1,7},{3,5},... | collective-permute-start | bytes 294920 | tf_op jit(solution)/shard_map/ppermute | solution.py:437
  33.6 1.8 %collective-permute-start.16 = (bf16[192,256]{1,0:T(8,128)(2,1)S(1)}, bf16[192,256]{1,0:T(8,128)(2,1)S(1)}, u32[]{:S(2)}, u32[]{:S(2)}) collective-permute-start(bf16[192,256]{1,0:T(8,128)(2,1)S(1)} %get-tuple-element.94.refs_0_.a_ref), channel_id=1, source_target_pairs={{0,8},{4,12},{8,0},{12,4},{1,9},{5,13},{9,1},{13,5},{2,10},{6,14},... | collective-permute-start | bytes 294920 | tf_op jit(solution)/shard_map/ppermute | solution.py:431
  35.4 1.5 %collective-permute-start.18 = (bf16[192,256]{1,0:T(8,128)(2,1)S(1)}, bf16[192,256]{1,0:T(8,128)(2,1)S(1)}, u32[]{:S(2)}, u32[]{:S(2)}) collective-permute-start(bf16[192,256]{1,0:T(8,128)(2,1)S(1)} %get-tuple-element.94.refs_0_.a_ref), channel_id=1, source_target_pairs={{0,2},{2,0},{1,3},{3,1},{4,6},{6,4},{5,7},{7,5},{8,10},{10,8},{9,1... | collective-permute-start | bytes 294920 | tf_op jit(solution)/shard_map/ppermute | solution.py:431
  36.9 0.3 collective-permute-start.17
  37.2 1.2 %collective-permute-start.15 = (bf16[192,256]{1,0:T(8,128)(2,1)S(1)}, bf16[192,256]{1,0:T(8,128)(2,1)S(1)}, u32[]{:S(2)}, u32[]{:S(2)}) collective-permute-start(bf16[192,256]{1,0:T(8,128)(2,1)S(1)} %get-tuple-element.94.refs_0_.a_ref), channel_id=1, source_target_pairs={{0,12},{4,8},{8,4},{12,0},{1,13},{5,9},{9,5},{13,1},{2,14},{6,10},... | collective-permute-start | bytes 294920 | tf_op jit(solution)/shard_map/ppermute | solution.py:431
  38.4 1.6 %collective-permute-done.19.refs_3_.d_ref = bf16[192,256]{1,0:T(8,128)(2,1)S(1)} collective-permute-done((bf16[192,256]{1,0:T(8,128)(2,1)S(1)}, bf16[192,256]{1,0:T(8,128)(2,1)S(1)}, u32[]{:S(2)}, u32[]{:S(2)}) %collective-permute-start.19) | collective-permute-done | bytes 98336 | tf_op jit(solution)/shard_map/ppermute | solution.py:437
  40.0 0.0 collective-permute-start.7
  40.0 1.6 %collective-permute-done.16.b_ref = bf16[192,256]{1,0:T(8,128)(2,1)S(1)} collective-permute-done((bf16[192,256]{1,0:T(8,128)(2,1)S(1)}, bf16[192,256]{1,0:T(8,128)(2,1)S(1)}, u32[]{:S(2)}, u32[]{:S(2)}) %collective-permute-start.16) | collective-permute-done | bytes 98336 | tf_op jit(solution)/shard_map/ppermute | solution.py:431
  41.6 0.0 collective-permute-start.21
  41.6 0.0 collective-permute-done.18.refs_2_.c_ref
  41.6 0.5 %collective-permute-done.17.refs_1_.b_ref = bf16[192,256]{1,0:T(8,128)(2,1)S(1)} collective-permute-done((bf16[192,256]{1,0:T(8,128)(2,1)S(1)}, bf16[192,256]{1,0:T(8,128)(2,1)S(1)}, u32[]{:S(2)}, u32[]{:S(2)}) %collective-permute-start.17) | collective-permute-done | bytes 98336 | tf_op jit(solution)/shard_map/ppermute | solution.py:431
  42.2 1.6 %collective-permute-done.15.refs_4_.a_ref = bf16[192,256]{1,0:T(8,128)(2,1)S(1)} collective-permute-done((bf16[192,256]{1,0:T(8,128)(2,1)S(1)}, bf16[192,256]{1,0:T(8,128)(2,1)S(1)}, u32[]{:S(2)}, u32[]{:S(2)}) %collective-permute-start.15) | collective-permute-done | bytes 98336 | tf_op jit(solution)/shard_map/ppermute | solution.py:431
  43.7 0.8 %collective-permute-start.20 = (bf16[192,256]{1,0:T(8,128)(2,1)S(1)}, bf16[192,256]{1,0:T(8,128)(2,1)S(1)}, u32[]{:S(2)}, u32[]{:S(2)}) collective-permute-start(bf16[192,256]{1,0:T(8,128)(2,1)S(1)} %shard_map.172), channel_id=1, source_target_pairs={{0,2},{2,0},{1,3},{3,1},{4,6},{6,4},{5,7},{7,5},{8,10},{10,8},{9,1... | collective-permute-start | bytes 294920 | tf_op jit(solution)/shard_map/ppermute | solution.py:431
  44.5 0.0 collective-permute-done.7.other_ref
  44.5 0.8 %shard_map.171 = (f32[128,512]{1,0:T(8,128)}, bf16[128,512]{1,0:T(8,128)(2,1)}, f32[1,256]{1,0:T(1,128)}, f32[1,512]{1,0:T(1,128)}) custom-call(bf16[128,512]{1,0:T(8,128)(2,1)S(1)} %get-tuple-element.56.cot_ref, bf16[128,512]{1,0:T(8,128)(2,1)S(1)} %get-tuple-element.55.refs_0_.node_ref, f32[1,512]{1,0:T(1,128)S(1)} %get-tuple-element.57.gain_ref, ...), custom_call_target="tpu_custom_call" | custom-call | flops 100000000 | bytes 1000000 | tf_op jit(solution)/shard_map/pallas_call | solution.py:412
  45.3 0.9 %shard_map.173 = (f32[512,256]{1,0:T(8,128)}, f32[512,256]{1,0:T(8,128)}, f32[256,512]{1,0:T(8,128)}) custom-call(bf16[192,256]{1,0:T(8,128)(2,1)S(1)} %get-tuple-element.94.refs_0_.a_ref, bf16[192,256]{1,0:T(8,128)(2,1)S(1)} %collective-permute-done.17.refs_1_.b_ref, bf16[192,256]{1,0:T(8,128)(2,1)S(1)} %collective-permute-done.18.refs_2_.c_ref, ...), custom_call_target="tpu_custom_call" | custom-call | flops 100000000 | bytes 1000000 | tf_op jit(solution)/shard_map/pallas_call | solution.py:412
  46.3 0.0 collective-permute-done.21.d_ref
  46.3 2.1 %collective-permute-done.20.c_ref = bf16[192,256]{1,0:T(8,128)(2,1)S(1)} collective-permute-done((bf16[192,256]{1,0:T(8,128)(2,1)S(1)}, bf16[192,256]{1,0:T(8,128)(2,1)S(1)}, u32[]{:S(2)}, u32[]{:S(2)}) %collective-permute-start.20) | collective-permute-done | bytes 98336 | tf_op jit(solution)/shard_map/ppermute | solution.py:431
  48.4 0.9 %shard_map.174 = (f32[512,256]{1,0:T(8,128)}, f32[512,256]{1,0:T(8,128)}, f32[256,512]{1,0:T(8,128)}) custom-call(bf16[192,256]{1,0:T(8,128)(2,1)S(1)} %collective-permute-done.15.refs_4_.a_ref, bf16[192,256]{1,0:T(8,128)(2,1)S(1)} %collective-permute-done.16.b_ref, ...), custom_call_target="tpu_custom_call", output_to_operand_aliasing={{0}: (4, {}), {1}: (5, {}), {2}: (6, {})} | custom-call | flops 100000000 | bytes 1000000 | tf_op jit(solution)/shard_map/pallas_call | solution.py:412
  (4 shorter events, 0.1 us)
Async XLA Ops:
  1.8 9.0 %collective-permute-start.2 = (bf16[64,512]{1,0:T(8,128)(2,1)S(1)}, bf16[64,512]{1,0:T(8,128)(2,1)S(1)}, u32[]{:S(2)}, u32[]{:S(2)}) collective-permute-start(bf16[64,512]{1,0:T(8,128)(2,1)S(1)} %get-tuple-element.67), channel_id=1, source_target_pairs={{0,2},{2,0},{1,3},{3,1},{4,6},{6,4},{5,7},{7,5},{8,10},{10,8},{9,1... | collective-permute-start | bytes 196616 | tf_op jit(solution)/shard_map/ppermute | solution.py:426
  4.8 5.9 %collective-permute-start = (bf16[32,512]{1,0:T(8,128)(2,1)S(1)}, bf16[32,512]{1,0:T(8,128)(2,1)S(1)}, u32[]{:S(2)}, u32[]{:S(2)}) collective-permute-start(bf16[32,512]{1,0:T(8,128)(2,1)S(1)} %get-tuple-element.65), channel_id=1, source_target_pairs={{0,4},{4,8},{8,12},{12,0},{1,5},{5,9},{9,13},{13,1},{2,6},{6,10},{... | collective-permute-start | bytes 98312 | tf_op jit(solution)/shard_map/ppermute | solution.py:426
  6.4 4.4 %collective-permute-start.1 = (bf16[32,512]{1,0:T(8,128)(2,1)S(1)}, bf16[32,512]{1,0:T(8,128)(2,1)S(1)}, u32[]{:S(2)}, u32[]{:S(2)}) collective-permute-start(bf16[32,512]{1,0:T(8,128)(2,1)S(1)} %get-tuple-element.66), channel_id=1, source_target_pairs={{0,12},{4,0},{8,4},{12,8},{1,13},{5,1},{9,5},{13,9},{2,14},{6,2},{... | collective-permute-start | bytes 98312 | tf_op jit(solution)/shard_map/ppermute | solution.py:426
  11.6 1.4 %collective-permute-start.3 = (bf16[128,512]{1,0:T(8,128)(2,1)S(1)}, bf16[128,512]{1,0:T(8,128)(2,1)S(1)}, u32[]{:S(2)}, u32[]{:S(2)}) collective-permute-start(bf16[128,512]{1,0:T(8,128)(2,1)S(1)} %get-tuple-element.70.own_ref), channel_id=1, source_target_pairs={{0,1},{1,0},{2,3},{3,2},{4,5},{5,4},{6,7},{7,6},{8,9},{9,8},{10,11... | collective-permute-start | bytes 393224 | tf_op jit(solution)/shard_map/ppermute | solution.py:426
  14.4 6.5 %collective-permute-start.8 = (bf16[272,256]{1,0:T(8,128)(2,1)S(1)}, bf16[272,256]{1,0:T(8,128)(2,1)S(1)}, u32[]{:S(2)}, u32[]{:S(2)}) collective-permute-start(bf16[272,256]{1,0:T(8,128)(2,1)S(1)} %get-tuple-element.79), channel_id=1, source_target_pairs={{0,2},{2,0},{1,3},{3,1},{4,6},{6,4},{5,7},{7,5},{8,10},{10,8},{9,1... | collective-permute-start | bytes 417800 | tf_op jit(solution)/shard_map/ppermute | solution.py:431
  14.9 11.4 %collective-permute-start.4 = (bf16[80,512]{1,0:T(8,128)(2,1)S(1)}, bf16[80,512]{1,0:T(8,128)(2,1)S(1)}, u32[]{:S(2)}, u32[]{:S(2)}) collective-permute-start(bf16[80,512]{1,0:T(8,128)(2,1)S(1)} %get-tuple-element.76), channel_id=1, source_target_pairs={{0,12},{4,8},{8,4},{12,0},{1,13},{5,9},{9,5},{13,1},{2,14},{6,10},... | collective-permute-start | bytes 245768 | tf_op jit(solution)/shard_map/ppermute | solution.py:431
  18.4 4.6 %collective-permute-start.11 = (bf16[128,256]{1,0:T(8,128)(2,1)S(1)}, bf16[128,256]{1,0:T(8,128)(2,1)S(1)}, u32[]{:S(2)}, u32[]{:S(2)}) collective-permute-start(bf16[128,256]{1,0:T(8,128)(2,1)S(1)} %get-tuple-element.83), channel_id=1, source_target_pairs={{0,2},{2,0},{1,3},{3,1},{4,6},{6,4},{5,7},{7,5},{8,10},{10,8},{9,1... | collective-permute-start | bytes 196616 | tf_op jit(solution)/shard_map/ppermute | solution.py:431
  20.1 6.1 %collective-permute-start.13 = (bf16[64,512]{1,0:T(8,128)(2,1)S(1)}, bf16[64,512]{1,0:T(8,128)(2,1)S(1)}, u32[]{:S(2)}, u32[]{:S(2)}) collective-permute-start(bf16[64,512]{1,0:T(8,128)(2,1)S(1)} %get-tuple-element.87), channel_id=1, source_target_pairs={{0,8},{4,12},{8,0},{12,4},{1,9},{5,13},{9,1},{13,5},{2,10},{6,14},... | collective-permute-start | bytes 196616 | tf_op jit(solution)/shard_map/ppermute | solution.py:431
  20.1 7.9 %collective-permute-start.5 = (bf16[80,512]{1,0:T(8,128)(2,1)S(1)}, bf16[80,512]{1,0:T(8,128)(2,1)S(1)}, u32[]{:S(2)}, u32[]{:S(2)}) collective-permute-start(bf16[80,512]{1,0:T(8,128)(2,1)S(1)} %get-tuple-element.77), channel_id=1, source_target_pairs={{0,4},{4,0},{8,12},{12,8},{1,5},{5,1},{9,13},{13,9},{2,6},{6,2},{1... | collective-permute-start | bytes 245768 | tf_op jit(solution)/shard_map/ppermute | solution.py:431
  20.9 8.8 %collective-permute-start.6 = (bf16[192,256]{1,0:T(8,128)(2,1)S(1)}, bf16[192,256]{1,0:T(8,128)(2,1)S(1)}, u32[]{:S(2)}, u32[]{:S(2)}) collective-permute-start(bf16[192,256]{1,0:T(8,128)(2,1)S(1)} %get-tuple-element.78), channel_id=1, source_target_pairs={{0,2},{2,0},{1,3},{3,1},{4,6},{6,4},{5,7},{7,5},{8,10},{10,8},{9,1... | collective-permute-start | bytes 294920 | tf_op jit(solution)/shard_map/ppermute | solution.py:431
  23.1 9.0 %collective-permute-start.9 = (bf16[144,256]{1,0:T(8,128)(2,1)S(1)}, bf16[144,256]{1,0:T(8,128)(2,1)S(1)}, u32[]{:S(2)}, u32[]{:S(2)}) collective-permute-start(bf16[144,256]{1,0:T(8,128)(2,1)S(1)} %get-tuple-element.81), channel_id=1, source_target_pairs={{0,12},{4,8},{8,4},{12,0},{1,13},{5,9},{9,5},{13,1},{2,14},{6,10},... | collective-permute-start | bytes 221192 | tf_op jit(solution)/shard_map/ppermute | solution.py:431
  26.3 5.8 %collective-permute-start.10 = (bf16[144,256]{1,0:T(8,128)(2,1)S(1)}, bf16[144,256]{1,0:T(8,128)(2,1)S(1)}, u32[]{:S(2)}, u32[]{:S(2)}) collective-permute-start(bf16[144,256]{1,0:T(8,128)(2,1)S(1)} %get-tuple-element.82), channel_id=1, source_target_pairs={{0,8},{4,12},{8,0},{12,4},{1,9},{5,13},{9,1},{13,5},{2,10},{6,14},... | collective-permute-start | bytes 221192 | tf_op jit(solution)/shard_map/ppermute | solution.py:431
  26.3 5.8 %collective-permute-start.12 = (bf16[144,256]{1,0:T(8,128)(2,1)S(1)}, bf16[144,256]{1,0:T(8,128)(2,1)S(1)}, u32[]{:S(2)}, u32[]{:S(2)}) collective-permute-start(bf16[144,256]{1,0:T(8,128)(2,1)S(1)} %shard_map.168.refs_4_), channel_id=1, source_target_pairs={{0,4},{4,0},{8,12},{12,8},{1,5},{5,1},{9,13},{13,9},{2,6},{6,2},{1... | collective-permute-start | bytes 221192 | tf_op jit(solution)/shard_map/ppermute | solution.py:431
  28.1 4.0 %collective-permute-start.14 = (bf16[64,256]{1,0:T(8,128)(2,1)S(1)}, bf16[64,256]{1,0:T(8,128)(2,1)S(1)}, u32[]{:S(2)}, u32[]{:S(2)}) collective-permute-start(bf16[64,256]{1,0:T(8,128)(2,1)S(1)} %get-tuple-element.90), channel_id=1, source_target_pairs={{0,2},{2,0},{1,3},{3,1},{4,6},{6,4},{5,7},{7,5},{8,10},{10,8},{9,1... | collective-permute-start | bytes 98312 | tf_op jit(solution)/shard_map/ppermute | solution.py:431
  32.2 7.8 %collective-permute-start.19 = (bf16[192,256]{1,0:T(8,128)(2,1)S(1)}, bf16[192,256]{1,0:T(8,128)(2,1)S(1)}, u32[]{:S(2)}, u32[]{:S(2)}) collective-permute-start(bf16[192,256]{1,0:T(8,128)(2,1)S(1)} %get-tuple-element.94.refs_0_.a_ref), channel_id=1, source_target_pairs={{0,6},{2,4},{4,2},{6,0},{8,14},{10,12},{12,10},{14,8},{1,7},{3,5},... | collective-permute-start | bytes 294920 | tf_op jit(solution)/shard_map/ppermute | solution.py:437
  33.6 8.1 %collective-permute-start.16 = (bf16[192,256]{1,0:T(8,128)(2,1)S(1)}, bf16[192,256]{1,0:T(8,128)(2,1)S(1)}, u32[]{:S(2)}, u32[]{:S(2)}) collective-permute-start(bf16[192,256]{1,0:T(8,128)(2,1)S(1)} %get-tuple-element.94.refs_0_.a_ref), channel_id=1, source_target_pairs={{0,8},{4,12},{8,0},{12,4},{1,9},{5,13},{9,1},{13,5},{2,10},{6,14},... | collective-permute-start | bytes 294920 | tf_op jit(solution)/shard_map/ppermute | solution.py:431
  35.4 6.3 %collective-permute-start.18 = (bf16[192,256]{1,0:T(8,128)(2,1)S(1)}, bf16[192,256]{1,0:T(8,128)(2,1)S(1)}, u32[]{:S(2)}, u32[]{:S(2)}) collective-permute-start(bf16[192,256]{1,0:T(8,128)(2,1)S(1)} %get-tuple-element.94.refs_0_.a_ref), channel_id=1, source_target_pairs={{0,2},{2,0},{1,3},{3,1},{4,6},{6,4},{5,7},{7,5},{8,10},{10,8},{9,1... | collective-permute-start | bytes 294920 | tf_op jit(solution)/shard_map/ppermute | solution.py:431
  36.9 5.3 %collective-permute-start.17 = (bf16[192,256]{1,0:T(8,128)(2,1)S(1)}, bf16[192,256]{1,0:T(8,128)(2,1)S(1)}, u32[]{:S(2)}, u32[]{:S(2)}) collective-permute-start(bf16[192,256]{1,0:T(8,128)(2,1)S(1)} %get-tuple-element.94.refs_0_.a_ref), channel_id=1, source_target_pairs={{0,4},{4,0},{8,12},{12,8},{1,5},{5,1},{9,13},{13,9},{2,6},{6,2},{1... | collective-permute-start | bytes 294920 | tf_op jit(solution)/shard_map/ppermute | solution.py:431
  37.2 6.5 %collective-permute-start.15 = (bf16[192,256]{1,0:T(8,128)(2,1)S(1)}, bf16[192,256]{1,0:T(8,128)(2,1)S(1)}, u32[]{:S(2)}, u32[]{:S(2)}) collective-permute-start(bf16[192,256]{1,0:T(8,128)(2,1)S(1)} %get-tuple-element.94.refs_0_.a_ref), channel_id=1, source_target_pairs={{0,12},{4,8},{8,4},{12,0},{1,13},{5,9},{9,5},{13,1},{2,14},{6,10},... | collective-permute-start | bytes 294920 | tf_op jit(solution)/shard_map/ppermute | solution.py:431
  40.0 4.5 %collective-permute-start.7 = (bf16[128,512]{1,0:T(8,128)(2,1)S(1)}, bf16[128,512]{1,0:T(8,128)(2,1)S(1)}, u32[]{:S(2)}, u32[]{:S(2)}) collective-permute-start(bf16[128,512]{1,0:T(8,128)(2,1)S(1)} %shard_map.166.refs_8_.own_ref), channel_id=1, source_target_pairs={{0,1},{1,0},{2,3},{3,2},{4,5},{5,4},{6,7},{7,6},{8,9},{9,8},{10,11... | collective-permute-start | bytes 393224 | tf_op jit(solution)/shard_map/ppermute | solution.py:426
  41.6 4.7 %collective-permute-start.21 = (bf16[192,256]{1,0:T(8,128)(2,1)S(1)}, bf16[192,256]{1,0:T(8,128)(2,1)S(1)}, u32[]{:S(2)}, u32[]{:S(2)}) collective-permute-start(bf16[192,256]{1,0:T(8,128)(2,1)S(1)} %collective-permute-done.16.b_ref), channel_id=1, source_target_pairs={{0,2},{2,0},{1,3},{3,1},{4,6},{6,4},{5,7},{7,5},{8,10},{10,8},{9,1... | collective-permute-start | bytes 294920 | tf_op jit(solution)/shard_map/ppermute | solution.py:431
  43.7 4.7 %collective-permute-start.20 = (bf16[192,256]{1,0:T(8,128)(2,1)S(1)}, bf16[192,256]{1,0:T(8,128)(2,1)S(1)}, u32[]{:S(2)}, u32[]{:S(2)}) collective-permute-start(bf16[192,256]{1,0:T(8,128)(2,1)S(1)} %shard_map.172), channel_id=1, source_target_pairs={{0,2},{2,0},{1,3},{3,1},{4,6},{6,4},{5,7},{7,5},{8,10},{10,8},{9,1... | collective-permute-start | bytes 294920 | tf_op jit(solution)/shard_map/ppermute | solution.py:431

commit v13 on v12

--- a/solution.py
+++ b/solution.py
@@ -183,7 +183,7 @@
     back = by_source_low[rows:]
 
     if paired:
-        sends, keeps, out_refs = message_refs[:3], message_refs[3:6], message_refs[6:]
+        sends, keeps, out_refs = message_refs[:2], message_refs[2:4], message_refs[4:]
         sub = lax.axis_index("sub")
         mesh = lax.axis_index("mesh")
         lines = len(out_refs)
@@ -192,13 +192,13 @@
         pair_scratch[0] = jnp.where(first, dst_part, src_part)
         pair_scratch[1] = jnp.where(first, src_part, dst_part)
         strip = width // lines
-        for slot, (far_ref, one_ref, zero_ref) in enumerate((sends, keeps)):
-            places = ((far_ref, 0, 3), (far_ref, strip, 2), (one_ref, 0, 1), (zero_ref, 0, 0))
+        for slot, (far_ref, zero_ref) in enumerate((sends, keeps)):
+            places = [(far_ref, at, k) for at, k in enumerate((3, 2, 1))] + [(zero_ref, 0, 0)]
             for ref, at, k in places:
                 start = pl.multiple_of((mesh ^ k) * strip, strip)
-                ref[at : at + strip, :] = pair_scratch[slot, pl.ds(start, strip), :]
-            far_ref[2 * strip :, :] = tail
-        sends[2][strip:, :] = back[2 * halo :]
+                ref[at * strip : (at + 1) * strip, :] = pair_scratch[slot, pl.ds(start, strip), :]
+            far_ref[3 * strip :, :] = tail
+        sends[1][strip:, :] = back[2 * halo :]
         back_scratch[...] = back[: 2 * halo]
         out_scratch[...] = out_part
         strip = hid // len(out_refs)
@@ -254,21 +254,16 @@
     return terms[0]
 
 
-def far_kernel(arrived_ref, keep_ref, three_ref, two_ref, tail_ref):
+def far_kernel(arrived_ref, keep_ref, *refs):
+    *line_refs, tail_ref = refs
     total = keep_ref[...].astype(f32) + arrived_ref[...].astype(f32)
-    strip = three_ref.shape[0] - TAIL
-    tail = total[2 * strip :]
+    strip = line_refs[0].shape[0] - TAIL
+    tail = total[len(line_refs) * strip :]
     tail = tail_of([tail[at : at + 1] + tail[at + 1 : at + 2] for at in range(0, 6, 2)])
-    for k, ref in enumerate((three_ref, two_ref)):
+    for k, ref in enumerate(line_refs):
         ref[0:strip, :] = total[k * strip : (k + 1) * strip].astype(bf16)
         ref[strip:, :] = tail
     tail_ref[...] = tail
-
-
-def near_kernel(arrived_ref, keep_ref, tail_ref, one_ref):
-    strip = keep_ref.shape[0]
-    one_ref[0:strip, :] = (keep_ref[...].astype(f32) + arrived_ref[...].astype(f32)).astype(bf16)
-    one_ref[strip:, :] = tail_ref[...]
 
 
 def line_kernel(*refs):
@@ -431,23 +426,17 @@
     return lax.ppermute(x, axis, [(i, i ^ k) for i in range(count)])
 
 
-def diagonal(x):
-    lines, pairs = lax.axis_size("mesh"), lax.axis_size("sub")
-    moves = [(m * pairs + p, (m ^ 1) * pairs + (p ^ 1)) for m in range(lines) for p in range(pairs)]
-    return lax.ppermute(x, ("mesh", "sub"), moves)
-
-
 def paired_sums(messages, lines, strip, narrow, width, hid, node_terms):
-    sends, keeps, outs = messages[:3], messages[3:6], messages[6:]
+    sends, keeps, outs = messages[:2], messages[2:4], messages[4:]
     order = range(lines - 1, 0, -1)
     block = shape((strip + TAIL, hid), bf16)
     far = across(sends[0], "sub", 1)
     out_terms = {k: across(outs[k], "mesh", k) for k in order}
-    one = across(sends[1], "sub", 1)
-    zero = across(sends[2], "sub", 1)
+    zero = across(sends[1], "sub", 1)
     line = {}
-    line[3], line[2], tail = call(far_kernel, [block, block, shape((TAIL, hid), bf16)], far, keeps[0])
-    line[1] = call(near_kernel, block, one, keeps[1], tail)
+    line[3], line[2], line[1], tail = call(
+        far_kernel, [block] * 3 + [shape((TAIL, hid), bf16)], far, keeps[0]
+    )
     line_terms = {k: across(line[k], "mesh", k) for k in order}
     out_send, out_keep = call(
         line_kernel,
@@ -458,16 +447,16 @@
     own, tail = call(
         own_kernel,
         [shape((strip + narrow, hid), bf16), shape((TAIL, hid), f32)],
-        *[line_terms[k] for k in order], keeps[2], zero, tail, out_keep, across(out_send, "sub", 1),
+        *[line_terms[k] for k in order], keeps[1], zero, tail, out_keep, across(out_send, "sub", 1),
         node_part,
     )
     mine = {k: across(own, "mesh", k) for k in order}
     mine[0] = own
-    theirs = {0: across(own, "sub", 1), 1: diagonal(own)}
+    theirs = {0: across(own, "sub", 1)}
+    theirs[1] = across(theirs[0], "mesh", 1)
     early = (mine[0], mine[1], theirs[0], theirs[1])
     theirs[2] = across(mine[2], "sub", 1)
-    last = call(relay_kernel, shape(own.shape, bf16), *early, mine[3])
-    theirs[3] = across(last, "sub", 1)
+    theirs[3] = across(mine[3], "sub", 1)
     wholes = [shape((width, hid), f32), shape((width, hid), f32), shape((hid, width), f32)]
     scratch = [
         pltpu.VMEM((2, strip, hid), f32), pltpu.VMEM((2, strip, hid), f32), pltpu.VMEM((2, narrow, width), f32),
@@ -562,7 +551,7 @@
     if paired:
         strip = width // lines
         narrow = hid // lines
-        rows_of = (2 * strip + TAIL, strip, strip + 2 * halo, 2 * strip + TAIL, strip, strip)
+        rows_of = (3 * strip + TAIL, strip + 2 * halo, 3 * strip + TAIL, strip)
         message_shapes = [shape((n, hid), bf16) for n in rows_of]
         message_shapes += [shape((narrow + k % 2 * (halo // 2), width), bf16) for k in range(lines)]
     else:

time: 49.5 us -> 48.7 us (0.984)
  waiting for transfers between devices: 13.5 us -> 9.51 us
  starting transfers between devices: 26.4 us -> 29.6 us
    ppermute x16, starting transfers between devices: 18.1 us -> 22.7 us  [across(): return lax.ppermute(x, axis, [(i, i ^ k) for i in range(count)])]
    ppermute x16, waiting for transfers between devices: 10.5 us -> 8.13 us  [across(): return lax.ppermute(x, axis, [(i, i ^ k) for i in range(count)])]
    ppermute x1 -> x0, waiting for transfers between devices: 1.62 us -> none  [diagonal(): return lax.ppermute(x, ('mesh', 'sub'), moves)]
    ppermute x1 -> x0, starting transfers between devices: 1.41 us -> none  [diagonal(): return lax.ppermute(x, ('mesh', 'sub'), moves)]
    pallas_call x13 -> x11, Pallas kernels: 8.71 us -> 8.7 us  [call(): pl.pallas_call(kernel, out_shape=outs, in_specs=specs or [VMEM] * len(arg...]
  transfers between devices with their start and end apart: 22 -> 21, of which waited for: 9 -> 6; matrix products, arithmetic and copies ran while one was open for 0% -> 0% of each run, Pallas kernels for 9% -> 9%
where the time goes in v13:
time: 48.7 us; the launch traced here: 48.5 us
  starting transfers between devices  29.6 us (61%)
  waiting for transfers between devices  9.51 us (20%)
  Pallas kernels  8.7 us (18%)
  between operations  0.73 us (1%)
    ppermute x16, starting transfers between devices, across(): return lax.ppermute(x, axis, [(i, i ^ k) for i in range(count)])  22.7 us
    pallas_call x11, Pallas kernels, call(): pl.pallas_call(kernel, out_shape=outs, in_specs=specs or [VMEM] * len(arg...  8.7 us
    ppermute x16, waiting for transfers between devices, across(): return lax.ppermute(x, axis, [(i, i ^ k) for i in range(count)])  8.13 us
    ppermute x5, starting transfers between devices, shifted(): return lax.ppermute(x, axis, [(i, (i + by) % count) for i in range(count)])  6.9 us
    ppermute x5, waiting for transfers between devices, shifted(): return lax.ppermute(x, axis, [(i, (i + by) % count) for i in range(count)])  1.38 us
  transfers between devices with their start and end apart: 21, of which 6 were waited for; matrix products, arithmetic and copies ran while one was open for 0% of the time, Pallas kernels for 9%

profile of v13, /device:TPU:0, one launch (start us, length us, event | category | flops | bytes accessed | tf_op | source)
XLA Modules:
  0.0 48.5 jit_solution(7364329903232009526)
XLA Ops:
  0.6 1.2 %shard_map.162 = (bf16[128,512]{1,0:T(8,128)(2,1)S(1)}, s32[1,4,32]{2,1,0:T(4,128)S(1)}, bf16[32,512]{1,0:T(8,128)(2,1)S(1)}, bf16[32,512]{1,0:T(8,128)(2,1)S(1)}, bf16[64,512]{1,0:T(8,128)(2,1)S(1)}) custom-call(bf16[128,512]{1,0:T(8,128)(2,1)} %node_hbm.1, s32[1,4,32]{2,1,0:T(4,128)} %send_hbm.1), custom_call_target="tpu_custom_call" | custom-call | flops 100000000 | bytes 1000000 | tf_op jit(solution)/shard_map/pallas_call | solution.py:407
  1.8 3.0 %collective-permute-start.2 = (bf16[64,512]{1,0:T(8,128)(2,1)S(1)}, bf16[64,512]{1,0:T(8,128)(2,1)S(1)}, u32[]{:S(2)}, u32[]{:S(2)}) collective-permute-start(bf16[64,512]{1,0:T(8,128)(2,1)S(1)} %get-tuple-element.66), channel_id=1, source_target_pairs={{0,2},{2,0},{1,3},{3,1},{4,6},{6,4},{5,7},{7,5},{8,10},{10,8},{9,1... | collective-permute-start | bytes 196616 | tf_op jit(solution)/shard_map/ppermute | solution.py:421
  4.8 1.6 %collective-permute-start = (bf16[32,512]{1,0:T(8,128)(2,1)S(1)}, bf16[32,512]{1,0:T(8,128)(2,1)S(1)}, u32[]{:S(2)}, u32[]{:S(2)}) collective-permute-start(bf16[32,512]{1,0:T(8,128)(2,1)S(1)} %get-tuple-element.64), channel_id=1, source_target_pairs={{0,4},{4,8},{8,12},{12,0},{1,5},{5,9},{9,13},{13,1},{2,6},{6,10},{... | collective-permute-start | bytes 98312 | tf_op jit(solution)/shard_map/ppermute | solution.py:421
  6.4 2.2 %collective-permute-start.1 = (bf16[32,512]{1,0:T(8,128)(2,1)S(1)}, bf16[32,512]{1,0:T(8,128)(2,1)S(1)}, u32[]{:S(2)}, u32[]{:S(2)}) collective-permute-start(bf16[32,512]{1,0:T(8,128)(2,1)S(1)} %get-tuple-element.65), channel_id=1, source_target_pairs={{0,12},{4,0},{8,4},{12,8},{1,13},{5,1},{9,5},{13,9},{2,14},{6,2},{... | collective-permute-start | bytes 98312 | tf_op jit(solution)/shard_map/ppermute | solution.py:421
  8.6 2.1 %shard_map.163 = (f32[512,256]{1,0:T(8,128)S(1)}, bf16[512,128]{1,0:T(8,128)(2,1)S(1)}, bf16[128,512]{1,0:T(8,128)(2,1)S(1)}, bf16[512,128]{1,0:T(8,128)(2,1)S(1...) custom-call(bf16[128,512]{1,0:T(8,128)(2,1)S(1)} %get-tuple-element., ...), custom_call_target="tpu_custom_call" | custom-call | flops 100000000 | bytes 1000000 | tf_op jit(solution)/shard_map/pallas_call | solution.py:407
  10.7 0.0 collective-permute-done.rest_0_
  10.8 0.0 collective-permute-done.1.rest_1_
  10.8 0.0 collective-permute-done.2.rest_2_
  10.8 0.9 %shard_map.164 = (f32[512,256]{1,0:T(8,128)S(1)}, bf16[128,256]{1,0:T(8,128)(2,1)S(1)}, bf16[128,512]{1,0:T(8,128)(2,1)S(1)}) custom-call(f32[512,256]{1,0:T(8,128)S(1)} %get-tuple-element.61.pre_ref, bf16[512,128]{1,0:T(8,128)(2,1)S(1)} %get-tuple-element.62.pick_ref, bf16[128,512]{1,0:T(8,128)(2,1)S(1)} %get-tuple-element.57.collect_ref, ...), custom_call_target="tpu_custom_call" | custom-call | flops 100000000 | bytes 1000000 | tf_op jit(solution)/shard_map/pallas_call | solution.py:407
  11.6 0.1 collective-permute-start.3
  11.7 1.3 %collective-permute-done.3.other_ref = bf16[128,512]{1,0:T(8,128)(2,1)S(1)} collective-permute-done((bf16[128,512]{1,0:T(8,128)(2,1)S(1)}, bf16[128,512]{1,0:T(8,128)(2,1)S(1)}, u32[]{:S(2)}, u32[]{:S(2)}) %collective-permute-start.3) | collective-permute-done | bytes 131104 | tf_op jit(solution)/shard_map/ppermute | solution.py:421
  13.1 1.4 %shard_map.165 = (f32[128,512]{1,0:T(8,128)S(1)}, f32[128,256]{1,0:T(8,128)S(1)}, bf16[128,256]{1,0:T(8,128)(2,1)S(1)}, bf16[400,256]{1,0:T(8,128)(2,1)S(1)}, bf...) custom-call(bf16[128,512]{1,0:T(8,128)(2,1)S(1)} %get-tuple-element., ...), custom_call_target="tpu_custom_call" | custom-call | flops 100000000 | bytes 1000000 | tf_op jit(solution)/shard_map/pallas_call | solution.py:407
  14.4 0.5 %collective-permute-start.8 = (bf16[400,256]{1,0:T(8,128)(2,1)S(1)}, bf16[400,256]{1,0:T(8,128)(2,1)S(1)}, u32[]{:S(2)}, u32[]{:S(2)}) collective-permute-start(bf16[400,256]{1,0:T(8,128)(2,1)S(1)} %get-tuple-element.78), channel_id=1, source_target_pairs={{0,2},{2,0},{1,3},{3,1},{4,6},{6,4},{5,7},{7,5},{8,10},{10,8},{9,1... | collective-permute-start | bytes 614408 | tf_op jit(solution)/shard_map/ppermute | solution.py:426
  14.9 3.5 %collective-permute-start.4 = (bf16[80,512]{1,0:T(8,128)(2,1)S(1)}, bf16[80,512]{1,0:T(8,128)(2,1)S(1)}, u32[]{:S(2)}, u32[]{:S(2)}) collective-permute-start(bf16[80,512]{1,0:T(8,128)(2,1)S(1)} %get-tuple-element.75), channel_id=1, source_target_pairs={{0,12},{4,8},{8,4},{12,0},{1,13},{5,9},{9,5},{13,1},{2,14},{6,10},... | collective-permute-start | bytes 245768 | tf_op jit(solution)/shard_map/ppermute | solution.py:426
  18.4 0.0 collective-permute-start.12
  18.4 0.9 %collective-permute-start.5 = (bf16[80,512]{1,0:T(8,128)(2,1)S(1)}, bf16[80,512]{1,0:T(8,128)(2,1)S(1)}, u32[]{:S(2)}, u32[]{:S(2)}) collective-permute-start(bf16[80,512]{1,0:T(8,128)(2,1)S(1)} %get-tuple-element.76), channel_id=1, source_target_pairs={{0,4},{4,0},{8,12},{12,8},{1,5},{5,1},{9,13},{13,9},{2,6},{6,2},{1... | collective-permute-start | bytes 245768 | tf_op jit(solution)/shard_map/ppermute | solution.py:426
  19.3 1.6 %collective-permute-start.6 = (bf16[192,256]{1,0:T(8,128)(2,1)S(1)}, bf16[192,256]{1,0:T(8,128)(2,1)S(1)}, u32[]{:S(2)}, u32[]{:S(2)}) collective-permute-start(bf16[192,256]{1,0:T(8,128)(2,1)S(1)} %get-tuple-element.77), channel_id=1, source_target_pairs={{0,2},{2,0},{1,3},{3,1},{4,6},{6,4},{5,7},{7,5},{8,10},{10,8},{9,1... | collective-permute-start | bytes 294920 | tf_op jit(solution)/shard_map/ppermute | solution.py:426
  20.9 1.3 %collective-permute-done.8.arrived_ref = bf16[400,256]{1,0:T(8,128)(2,1)S(1)} collective-permute-done((bf16[400,256]{1,0:T(8,128)(2,1)S(1)}, bf16[400,256]{1,0:T(8,128)(2,1)S(1)}, u32[]{:S(2)}, u32[]{:S(2)}) %collective-permute-start.8) | collective-permute-done | bytes 204832 | tf_op jit(solution)/shard_map/ppermute | solution.py:426
  22.2 0.1 shard_map.167
  22.2 3.8 %collective-permute-start.9 = (bf16[144,256]{1,0:T(8,128)(2,1)S(1)}, bf16[144,256]{1,0:T(8,128)(2,1)S(1)}, u32[]{:S(2)}, u32[]{:S(2)}) collective-permute-start(bf16[144,256]{1,0:T(8,128)(2,1)S(1)} %get-tuple-element.80), channel_id=1, source_target_pairs={{0,12},{4,8},{8,4},{12,0},{1,13},{5,9},{9,5},{13,1},{2,14},{6,10},... | collective-permute-start | bytes 221192 | tf_op jit(solution)/shard_map/ppermute | solution.py:426
  26.1 0.0 collective-permute-done.12.refs_1_
  26.1 0.0 collective-permute-start.10
  26.1 0.0 collective-permute-done.4.three_ref.refs_0_
  26.1 1.8 %collective-permute-start.11 = (bf16[144,256]{1,0:T(8,128)(2,1)S(1)}, bf16[144,256]{1,0:T(8,128)(2,1)S(1)}, u32[]{:S(2)}, u32[]{:S(2)}) collective-permute-start(bf16[144,256]{1,0:T(8,128)(2,1)S(1)} %get-tuple-element.82.refs_4_), channel_id=1, source_target_pairs={{0,4},{4,0},{8,12},{12,8},{1,5},{5,1},{9,13},{13,9},{2,6},{6,2},{1... | collective-permute-start | bytes 221192 | tf_op jit(solution)/shard_map/ppermute | solution.py:426
  27.8 0.0 collective-permute-done.5.one_ref.refs_2_
  27.9 2.0 %collective-permute-start.13 = (bf16[64,256]{1,0:T(8,128)(2,1)S(1)}, bf16[64,256]{1,0:T(8,128)(2,1)S(1)}, u32[]{:S(2)}, u32[]{:S(2)}) collective-permute-start(bf16[64,256]{1,0:T(8,128)(2,1)S(1)} %get-tuple-element.88), channel_id=1, source_target_pairs={{0,2},{2,0},{1,3},{3,1},{4,6},{6,4},{5,7},{7,5},{8,10},{10,8},{9,1... | collective-permute-start | bytes 98312 | tf_op jit(solution)/shard_map/ppermute | solution.py:426
  29.8 0.0 collective-permute-done.6.pair_ref.refs_4_
  29.9 0.4 shard_map.166.refs_8_.own_ref
  30.2 1.6 %collective-permute-done.13.refs_7_ = bf16[64,256]{1,0:T(8,128)(2,1)S(1)} collective-permute-done((bf16[64,256]{1,0:T(8,128)(2,1)S(1)}, bf16[64,256]{1,0:T(8,128)(2,1)S(1)}, u32[]{:S(2)}, u32[]{:S(2)}) %collective-permute-start.13) | collective-permute-done | bytes 32800 | tf_op jit(solution)/shard_map/ppermute | solution.py:426
  31.9 0.0 collective-permute-done.9.refs_0_
  31.9 0.0 collective-permute-done.10.refs_1_
  31.9 0.0 collective-permute-done.11.refs_2_
  31.9 0.1 shard_map.169
  32.0 2.1 %collective-permute-start.19 = (bf16[192,256]{1,0:T(8,128)(2,1)S(1)}, bf16[192,256]{1,0:T(8,128)(2,1)S(1)}, u32[]{:S(2)}, u32[]{:S(2)}) collective-permute-start(bf16[192,256]{1,0:T(8,128)(2,1)S(1)} %get-tuple-element.92.a_ref), channel_id=1, source_target_pairs={{0,2},{2,0},{1,3},{3,1},{4,6},{6,4},{5,7},{7,5},{8,10},{10,8},{9,1... | collective-permute-start | bytes 294920 | tf_op jit(solution)/shard_map/ppermute | solution.py:426
  34.1 0.8 %collective-permute-start.15 = (bf16[192,256]{1,0:T(8,128)(2,1)S(1)}, bf16[192,256]{1,0:T(8,128)(2,1)S(1)}, u32[]{:S(2)}, u32[]{:S(2)}) collective-permute-start(bf16[192,256]{1,0:T(8,128)(2,1)S(1)} %get-tuple-element.92.a_ref), channel_id=1, source_target_pairs={{0,8},{4,12},{8,0},{12,4},{1,9},{5,13},{9,1},{13,5},{2,10},{6,14},... | collective-permute-start | bytes 294920 | tf_op jit(solution)/shard_map/ppermute | solution.py:426
  34.9 1.7 %collective-permute-start.14 = (bf16[192,256]{1,0:T(8,128)(2,1)S(1)}, bf16[192,256]{1,0:T(8,128)(2,1)S(1)}, u32[]{:S(2)}, u32[]{:S(2)}) collective-permute-start(bf16[192,256]{1,0:T(8,128)(2,1)S(1)} %get-tuple-element.92.a_ref), channel_id=1, source_target_pairs={{0,12},{4,8},{8,4},{12,0},{1,13},{5,9},{9,5},{13,1},{2,14},{6,10},... | collective-permute-start | bytes 294920 | tf_op jit(solution)/shard_map/ppermute | solution.py:426
  36.6 0.0 collective-permute-start.7
  36.6 1.0 %collective-permute-start.18 = (bf16[192,256]{1,0:T(8,128)(2,1)S(1)}, bf16[192,256]{1,0:T(8,128)(2,1)S(1)}, u32[]{:S(2)}, u32[]{:S(2)}) collective-permute-start(bf16[192,256]{1,0:T(8,128)(2,1)S(1)} %get-tuple-element.92.a_ref), channel_id=1, source_target_pairs={{0,4},{4,0},{8,12},{12,8},{1,5},{5,1},{9,13},{13,9},{2,6},{6,2},{1... | collective-permute-start | bytes 294920 | tf_op jit(solution)/shard_map/ppermute | solution.py:426
  37.6 0.0 collective-permute-done.19.c_ref
  37.6 1.0 %collective-permute-start.20 = (bf16[192,256]{1,0:T(8,128)(2,1)S(1)}, bf16[192,256]{1,0:T(8,128)(2,1)S(1)}, u32[]{:S(2)}, u32[]{:S(2)}) collective-permute-start(bf16[192,256]{1,0:T(8,128)(2,1)S(1)} %collective-permute-done.19.c_ref), channel_id=1, source_target_pairs={{0,4},{4,0},{8,12},{12,8},{1,5},{5,1},{9,13},{13,9},{2,6},{6,2},{1... | collective-permute-start | bytes 294920 | tf_op jit(solution)/shard_map/ppermute | solution.py:426
  38.6 2.6 %collective-permute-done.15.b_ref = bf16[192,256]{1,0:T(8,128)(2,1)S(1)} collective-permute-done((bf16[192,256]{1,0:T(8,128)(2,1)S(1)}, bf16[192,256]{1,0:T(8,128)(2,1)S(1)}, u32[]{:S(2)}, u32[]{:S(2)}) %collective-permute-start.15) | collective-permute-done | bytes 98336 | tf_op jit(solution)/shard_map/ppermute | solution.py:426
  41.2 1.8 %collective-permute-start.17 = (bf16[192,256]{1,0:T(8,128)(2,1)S(1)}, bf16[192,256]{1,0:T(8,128)(2,1)S(1)}, u32[]{:S(2)}, u32[]{:S(2)}) collective-permute-start(bf16[192,256]{1,0:T(8,128)(2,1)S(1)} %collective-permute-done.15.b_ref), channel_id=1, source_target_pairs={{0,2},{2,0},{1,3},{3,1},{4,6},{6,4},{5,7},{7,5},{8,10},{10,8},{9,1... | collective-permute-start | bytes 294920 | tf_op jit(solution)/shard_map/ppermute | solution.py:426
  43.0 0.0 collective-permute-done.14.a_ref
  43.0 0.3 collective-permute-start.16
  43.2 0.0 collective-permute-done.7.other_ref
  43.2 0.8 %shard_map.170 = (f32[128,512]{1,0:T(8,128)}, bf16[128,512]{1,0:T(8,128)(2,1)}, f32[1,256]{1,0:T(1,128)}, f32[1,512]{1,0:T(1,128)}) custom-call(bf16[128,512]{1,0:T(8,128)(2,1)S(1)} %get-tuple-element.55.cot_ref, bf16[128,512]{1,0:T(8,128)(2,1)S(1)} %get-tuple-element.54.refs_0_.node_ref, f32[1,512]{1,0:T(1,128)S(1)} %get-tuple-element.56.gain_ref, ...), custom_call_target="tpu_custom_call" | custom-call | flops 100000000 | bytes 1000000 | tf_op jit(solution)/shard_map/pallas_call | solution.py:407
  44.0 0.0 collective-permute-done.18.b_ref
  44.0 1.8 %collective-permute-done.20.d_ref = bf16[192,256]{1,0:T(8,128)(2,1)S(1)} collective-permute-done((bf16[192,256]{1,0:T(8,128)(2,1)S(1)}, bf16[192,256]{1,0:T(8,128)(2,1)S(1)}, u32[]{:S(2)}, u32[]{:S(2)}) %collective-permute-start.20) | collective-permute-done | bytes 98336 | tf_op jit(solution)/shard_map/ppermute | solution.py:426
  45.8 0.9 %shard_map.171 = (f32[512,256]{1,0:T(8,128)}, f32[512,256]{1,0:T(8,128)}, f32[256,512]{1,0:T(8,128)}) custom-call(bf16[192,256]{1,0:T(8,128)(2,1)S(1)} %get-tuple-element.92.a_ref, bf16[192,256]{1,0:T(8,128)(2,1)S(1)} %collective-permute-done.18.b_ref, bf16[192,256]{1,0:T(8,128)(2,1)S(1)} %collective-permute-done.19.c_ref, ...), custom_call_target="tpu_custom_call" | custom-call | flops 100000000 | bytes 1000000 | tf_op jit(solution)/shard_map/pallas_call | solution.py:407
  46.7 0.0 collective-permute-done.17.d_ref
  46.7 0.8 %collective-permute-done.16.c_ref = bf16[192,256]{1,0:T(8,128)(2,1)S(1)} collective-permute-done((bf16[192,256]{1,0:T(8,128)(2,1)S(1)}, bf16[192,256]{1,0:T(8,128)(2,1)S(1)}, u32[]{:S(2)}, u32[]{:S(2)}) %collective-permute-start.16) | collective-permute-done | bytes 98336 | tf_op jit(solution)/shard_map/ppermute | solution.py:426
  47.6 0.9 %shard_map.172 = (f32[512,256]{1,0:T(8,128)}, f32[512,256]{1,0:T(8,128)}, f32[256,512]{1,0:T(8,128)}) custom-call(bf16[192,256]{1,0:T(8,128)(2,1)S(1)} %collective-permute-done.14.a_ref, bf16[192,256]{1,0:T(8,128)(2,1)S(1)} %collective-permute-done.15.b_ref, ...), custom_call_target="tpu_custom_call", output_to_operand_aliasing={{0}: (4, {}), {1}: (5, {}), {2}: (6, {})} | custom-call | flops 100000000 | bytes 1000000 | tf_op jit(solution)/shard_map/pallas_call | solution.py:407
  (1 shorter events, 0.0 us)
Async XLA Ops:
  1.8 9.0 %collective-permute-start.2 = (bf16[64,512]{1,0:T(8,128)(2,1)S(1)}, bf16[64,512]{1,0:T(8,128)(2,1)S(1)}, u32[]{:S(2)}, u32[]{:S(2)}) collective-permute-start(bf16[64,512]{1,0:T(8,128)(2,1)S(1)} %get-tuple-element.66), channel_id=1, source_target_pairs={{0,2},{2,0},{1,3},{3,1},{4,6},{6,4},{5,7},{7,5},{8,10},{10,8},{9,1... | collective-permute-start | bytes 196616 | tf_op jit(solution)/shard_map/ppermute | solution.py:421
  4.8 5.9 %collective-permute-start = (bf16[32,512]{1,0:T(8,128)(2,1)S(1)}, bf16[32,512]{1,0:T(8,128)(2,1)S(1)}, u32[]{:S(2)}, u32[]{:S(2)}) collective-permute-start(bf16[32,512]{1,0:T(8,128)(2,1)S(1)} %get-tuple-element.64), channel_id=1, source_target_pairs={{0,4},{4,8},{8,12},{12,0},{1,5},{5,9},{9,13},{13,1},{2,6},{6,10},{... | collective-permute-start | bytes 98312 | tf_op jit(solution)/shard_map/ppermute | solution.py:421
  6.4 4.4 %collective-permute-start.1 = (bf16[32,512]{1,0:T(8,128)(2,1)S(1)}, bf16[32,512]{1,0:T(8,128)(2,1)S(1)}, u32[]{:S(2)}, u32[]{:S(2)}) collective-permute-start(bf16[32,512]{1,0:T(8,128)(2,1)S(1)} %get-tuple-element.65), channel_id=1, source_target_pairs={{0,12},{4,0},{8,4},{12,8},{1,13},{5,1},{9,5},{13,9},{2,14},{6,2},{... | collective-permute-start | bytes 98312 | tf_op jit(solution)/shard_map/ppermute | solution.py:421
  11.6 1.4 %collective-permute-start.3 = (bf16[128,512]{1,0:T(8,128)(2,1)S(1)}, bf16[128,512]{1,0:T(8,128)(2,1)S(1)}, u32[]{:S(2)}, u32[]{:S(2)}) collective-permute-start(bf16[128,512]{1,0:T(8,128)(2,1)S(1)} %get-tuple-element.69.own_ref), channel_id=1, source_target_pairs={{0,1},{1,0},{2,3},{3,2},{4,5},{5,4},{6,7},{7,6},{8,9},{9,8},{10,11... | collective-permute-start | bytes 393224 | tf_op jit(solution)/shard_map/ppermute | solution.py:421
  14.4 7.7 %collective-permute-start.8 = (bf16[400,256]{1,0:T(8,128)(2,1)S(1)}, bf16[400,256]{1,0:T(8,128)(2,1)S(1)}, u32[]{:S(2)}, u32[]{:S(2)}) collective-permute-start(bf16[400,256]{1,0:T(8,128)(2,1)S(1)} %get-tuple-element.78), channel_id=1, source_target_pairs={{0,2},{2,0},{1,3},{3,1},{4,6},{6,4},{5,7},{7,5},{8,10},{10,8},{9,1... | collective-permute-start | bytes 614408 | tf_op jit(solution)/shard_map/ppermute | solution.py:426
  14.9 11.1 %collective-permute-start.4 = (bf16[80,512]{1,0:T(8,128)(2,1)S(1)}, bf16[80,512]{1,0:T(8,128)(2,1)S(1)}, u32[]{:S(2)}, u32[]{:S(2)}) collective-permute-start(bf16[80,512]{1,0:T(8,128)(2,1)S(1)} %get-tuple-element.75), channel_id=1, source_target_pairs={{0,12},{4,8},{8,4},{12,0},{1,13},{5,9},{9,5},{13,1},{2,14},{6,10},... | collective-permute-start | bytes 245768 | tf_op jit(solution)/shard_map/ppermute | solution.py:426
  18.4 7.6 %collective-permute-start.12 = (bf16[64,512]{1,0:T(8,128)(2,1)S(1)}, bf16[64,512]{1,0:T(8,128)(2,1)S(1)}, u32[]{:S(2)}, u32[]{:S(2)}) collective-permute-start(bf16[64,512]{1,0:T(8,128)(2,1)S(1)} %get-tuple-element.85), channel_id=1, source_target_pairs={{0,8},{4,12},{8,0},{12,4},{1,9},{5,13},{9,1},{13,5},{2,10},{6,14},... | collective-permute-start | bytes 196616 | tf_op jit(solution)/shard_map/ppermute | solution.py:426
  18.4 9.4 %collective-permute-start.5 = (bf16[80,512]{1,0:T(8,128)(2,1)S(1)}, bf16[80,512]{1,0:T(8,128)(2,1)S(1)}, u32[]{:S(2)}, u32[]{:S(2)}) collective-permute-start(bf16[80,512]{1,0:T(8,128)(2,1)S(1)} %get-tuple-element.76), channel_id=1, source_target_pairs={{0,4},{4,0},{8,12},{12,8},{1,5},{5,1},{9,13},{13,9},{2,6},{6,2},{1... | collective-permute-start | bytes 245768 | tf_op jit(solution)/shard_map/ppermute | solution.py:426
  19.3 10.5 %collective-permute-start.6 = (bf16[192,256]{1,0:T(8,128)(2,1)S(1)}, bf16[192,256]{1,0:T(8,128)(2,1)S(1)}, u32[]{:S(2)}, u32[]{:S(2)}) collective-permute-start(bf16[192,256]{1,0:T(8,128)(2,1)S(1)} %get-tuple-element.77), channel_id=1, source_target_pairs={{0,2},{2,0},{1,3},{3,1},{4,6},{6,4},{5,7},{7,5},{8,10},{10,8},{9,1... | collective-permute-start | bytes 294920 | tf_op jit(solution)/shard_map/ppermute | solution.py:426
  22.2 9.6 %collective-permute-start.9 = (bf16[144,256]{1,0:T(8,128)(2,1)S(1)}, bf16[144,256]{1,0:T(8,128)(2,1)S(1)}, u32[]{:S(2)}, u32[]{:S(2)}) collective-permute-start(bf16[144,256]{1,0:T(8,128)(2,1)S(1)} %get-tuple-element.80), channel_id=1, source_target_pairs={{0,12},{4,8},{8,4},{12,0},{1,13},{5,9},{9,5},{13,1},{2,14},{6,10},... | collective-permute-start | bytes 221192 | tf_op jit(solution)/shard_map/ppermute | solution.py:426
  26.1 5.8 %collective-permute-start.10 = (bf16[144,256]{1,0:T(8,128)(2,1)S(1)}, bf16[144,256]{1,0:T(8,128)(2,1)S(1)}, u32[]{:S(2)}, u32[]{:S(2)}) collective-permute-start(bf16[144,256]{1,0:T(8,128)(2,1)S(1)} %get-tuple-element.81), channel_id=1, source_target_pairs={{0,8},{4,12},{8,0},{12,4},{1,9},{5,13},{9,1},{13,5},{2,10},{6,14},... | collective-permute-start | bytes 221192 | tf_op jit(solution)/shard_map/ppermute | solution.py:426
  26.1 5.8 %collective-permute-start.11 = (bf16[144,256]{1,0:T(8,128)(2,1)S(1)}, bf16[144,256]{1,0:T(8,128)(2,1)S(1)}, u32[]{:S(2)}, u32[]{:S(2)}) collective-permute-start(bf16[144,256]{1,0:T(8,128)(2,1)S(1)} %get-tuple-element.82.refs_4_), channel_id=1, source_target_pairs={{0,4},{4,0},{8,12},{12,8},{1,5},{5,1},{9,13},{13,9},{2,6},{6,2},{1... | collective-permute-start | bytes 221192 | tf_op jit(solution)/shard_map/ppermute | solution.py:426
  27.9 4.0 %collective-permute-start.13 = (bf16[64,256]{1,0:T(8,128)(2,1)S(1)}, bf16[64,256]{1,0:T(8,128)(2,1)S(1)}, u32[]{:S(2)}, u32[]{:S(2)}) collective-permute-start(bf16[64,256]{1,0:T(8,128)(2,1)S(1)} %get-tuple-element.88), channel_id=1, source_target_pairs={{0,2},{2,0},{1,3},{3,1},{4,6},{6,4},{5,7},{7,5},{8,10},{10,8},{9,1... | collective-permute-start | bytes 98312 | tf_op jit(solution)/shard_map/ppermute | solution.py:426
  32.0 5.6 %collective-permute-start.19 = (bf16[192,256]{1,0:T(8,128)(2,1)S(1)}, bf16[192,256]{1,0:T(8,128)(2,1)S(1)}, u32[]{:S(2)}, u32[]{:S(2)}) collective-permute-start(bf16[192,256]{1,0:T(8,128)(2,1)S(1)} %get-tuple-element.92.a_ref), channel_id=1, source_target_pairs={{0,2},{2,0},{1,3},{3,1},{4,6},{6,4},{5,7},{7,5},{8,10},{10,8},{9,1... | collective-permute-start | bytes 294920 | tf_op jit(solution)/shard_map/ppermute | solution.py:426
  34.1 7.1 %collective-permute-start.15 = (bf16[192,256]{1,0:T(8,128)(2,1)S(1)}, bf16[192,256]{1,0:T(8,128)(2,1)S(1)}, u32[]{:S(2)}, u32[]{:S(2)}) collective-permute-start(bf16[192,256]{1,0:T(8,128)(2,1)S(1)} %get-tuple-element.92.a_ref), channel_id=1, source_target_pairs={{0,8},{4,12},{8,0},{12,4},{1,9},{5,13},{9,1},{13,5},{2,10},{6,14},... | collective-permute-start | bytes 294920 | tf_op jit(solution)/shard_map/ppermute | solution.py:426
  34.9 8.1 %collective-permute-start.14 = (bf16[192,256]{1,0:T(8,128)(2,1)S(1)}, bf16[192,256]{1,0:T(8,128)(2,1)S(1)}, u32[]{:S(2)}, u32[]{:S(2)}) collective-permute-start(bf16[192,256]{1,0:T(8,128)(2,1)S(1)} %get-tuple-element.92.a_ref), channel_id=1, source_target_pairs={{0,12},{4,8},{8,4},{12,0},{1,13},{5,9},{9,5},{13,1},{2,14},{6,10},... | collective-permute-start | bytes 294920 | tf_op jit(solution)/shard_map/ppermute | solution.py:426
  36.6 6.6 %collective-permute-start.7 = (bf16[128,512]{1,0:T(8,128)(2,1)S(1)}, bf16[128,512]{1,0:T(8,128)(2,1)S(1)}, u32[]{:S(2)}, u32[]{:S(2)}) collective-permute-start(bf16[128,512]{1,0:T(8,128)(2,1)S(1)} %shard_map.166.refs_8_.own_ref), channel_id=1, source_target_pairs={{0,1},{1,0},{2,3},{3,2},{4,5},{5,4},{6,7},{7,6},{8,9},{9,8},{10,11... | collective-permute-start | bytes 393224 | tf_op jit(solution)/shard_map/ppermute | solution.py:421
  36.6 7.4 %collective-permute-start.18 = (bf16[192,256]{1,0:T(8,128)(2,1)S(1)}, bf16[192,256]{1,0:T(8,128)(2,1)S(1)}, u32[]{:S(2)}, u32[]{:S(2)}) collective-permute-start(bf16[192,256]{1,0:T(8,128)(2,1)S(1)} %get-tuple-element.92.a_ref), channel_id=1, source_target_pairs={{0,4},{4,0},{8,12},{12,8},{1,5},{5,1},{9,13},{13,9},{2,6},{6,2},{1... | collective-permute-start | bytes 294920 | tf_op jit(solution)/shard_map/ppermute | solution.py:426
  37.6 8.2 %collective-permute-start.20 = (bf16[192,256]{1,0:T(8,128)(2,1)S(1)}, bf16[192,256]{1,0:T(8,128)(2,1)S(1)}, u32[]{:S(2)}, u32[]{:S(2)}) collective-permute-start(bf16[192,256]{1,0:T(8,128)(2,1)S(1)} %collective-permute-done.19.c_ref), channel_id=1, source_target_pairs={{0,4},{4,0},{8,12},{12,8},{1,5},{5,1},{9,13},{13,9},{2,6},{6,2},{1... | collective-permute-start | bytes 294920 | tf_op jit(solution)/shard_map/ppermute | solution.py:426
  41.2 5.5 %collective-permute-start.17 = (bf16[192,256]{1,0:T(8,128)(2,1)S(1)}, bf16[192,256]{1,0:T(8,128)(2,1)S(1)}, u32[]{:S(2)}, u32[]{:S(2)}) collective-permute-start(bf16[192,256]{1,0:T(8,128)(2,1)S(1)} %collective-permute-done.15.b_ref), channel_id=1, source_target_pairs={{0,2},{2,0},{1,3},{3,1},{4,6},{6,4},{5,7},{7,5},{8,10},{10,8},{9,1... | collective-permute-start | bytes 294920 | tf_op jit(solution)/shard_map/ppermute | solution.py:426
  43.0 4.6 %collective-permute-start.16 = (bf16[192,256]{1,0:T(8,128)(2,1)S(1)}, bf16[192,256]{1,0:T(8,128)(2,1)S(1)}, u32[]{:S(2)}, u32[]{:S(2)}) collective-permute-start(bf16[192,256]{1,0:T(8,128)(2,1)S(1)} %collective-permute-done.14.a_ref), channel_id=1, source_target_pairs={{0,2},{2,0},{1,3},{3,1},{4,6},{6,4},{5,7},{7,5},{8,10},{10,8},{9,1... | collective-permute-start | bytes 294920 | tf_op jit(solution)/shard_map/ppermute | solution.py:426

commit v14 on v13

--- a/solution.py
+++ b/solution.py
@@ -426,6 +426,12 @@
     return lax.ppermute(x, axis, [(i, i ^ k) for i in range(count)])
 
 
+def diagonal(x):
+    lines, pairs = lax.axis_size("mesh"), lax.axis_size("sub")
+    moves = [(m * pairs + p, (m ^ 1) * pairs + (p ^ 1)) for m in range(lines) for p in range(pairs)]
+    return lax.ppermute(x, ("mesh", "sub"), moves)
+
+
 def paired_sums(messages, lines, strip, narrow, width, hid, node_terms):
     sends, keeps, outs = messages[:2], messages[2:4], messages[4:]
     order = range(lines - 1, 0, -1)
@@ -452,8 +458,7 @@
     )
     mine = {k: across(own, "mesh", k) for k in order}
     mine[0] = own
-    theirs = {0: across(own, "sub", 1)}
-    theirs[1] = across(theirs[0], "mesh", 1)
+    theirs = {0: across(own, "sub", 1), 1: diagonal(own)}
     early = (mine[0], mine[1], theirs[0], theirs[1])
     theirs[2] = across(mine[2], "sub", 1)
     theirs[3] = across(mine[3], "sub", 1)
@@ -467,8 +472,8 @@
         out_specs=[HBM] * 3, scratch=scratch, flops=10**8,
     )
     grads = call(
-        functools.partial(place_kernel, lines, (3, 2)), wholes,
-        mine[3], mine[2], theirs[3], theirs[2], *grads,
+        functools.partial(place_kernel, lines, (2, 3)), wholes,
+        mine[2], mine[3], theirs[2], theirs[3], *grads,
         specs=[VMEM] * 4 + [HBM] * 3, out_specs=[HBM] * 3, scratch=scratch,
         input_output_aliases={4: 0, 5: 1, 6: 2},
     )

time: 48.7 us -> 48.6 us (level)
  starting transfers between devices: 29.6 us -> 27.9 us
  waiting for transfers between devices: 9.51 us -> 11.1 us
    ppermute x16 -> x15, starting transfers between devices: 22.7 us -> 18.4 us  [across(): return lax.ppermute(x, axis, [(i, i ^ k) for i in range(count)])]
    ppermute x0 -> x1, starting transfers between devices: none -> 2.55 us  [diagonal(): return lax.ppermute(x, ('mesh', 'sub'), moves)]
    ppermute x16 -> x15, waiting for transfers between devices: 8.13 us -> 9.76 us  [across(): return lax.ppermute(x, axis, [(i, i ^ k) for i in range(count)])]
  transfers between devices with their start and end apart: 21 -> 21, of which waited for: 6 -> 9; matrix products, arithmetic and copies ran while one was open for 0% -> 0% of each run, Pallas kernels for 9% -> 9%
where the time goes in v14:
time: 48.6 us; the launch traced here: 48.4 us
  starting transfers between devices  27.9 us (57%)
  waiting for transfers between devices  11.1 us (23%)
  Pallas kernels  8.69 us (18%)
  between operations  0.73 us (2%)
    ppermute x15, starting transfers between devices, across(): return lax.ppermute(x, axis, [(i, i ^ k) for i in range(count)])  18.4 us
    ppermute x15, waiting for transfers between devices, across(): return lax.ppermute(x, axis, [(i, i ^ k) for i in range(count)])  9.76 us
    pallas_call x11, Pallas kernels, call(): pl.pallas_call(kernel, out_shape=outs, in_specs=specs or [VMEM] * len(arg...  8.69 us
    ppermute x5, starting transfers between devices, shifted(): return lax.ppermute(x, axis, [(i, (i + by) % count) for i in range(count)])  6.97 us
    ppermute x1, starting transfers between devices, diagonal(): return lax.ppermute(x, ('mesh', 'sub'), moves)  2.55 us
    ppermute x5, waiting for transfers between devices, shifted(): return lax.ppermute(x, axis, [(i, (i + by) % count) for i in range(count)])  1.38 us
  transfers between devices with their start and end apart: 21, of which 9 were waited for; matrix products, arithmetic and copies ran while one was open for 0% of the time, Pallas kernels for 9%

profile of v14, /device:TPU:0, one launch (start us, length us, event | category | flops | bytes accessed | tf_op | source)
XLA Modules:
  0.0 48.4 jit_solution(14321284710374279653)
XLA Ops:
  0.6 1.2 %shard_map.162 = (bf16[128,512]{1,0:T(8,128)(2,1)S(1)}, s32[1,4,32]{2,1,0:T(4,128)S(1)}, bf16[32,512]{1,0:T(8,128)(2,1)S(1)}, bf16[32,512]{1,0:T(8,128)(2,1)S(1)}, bf16[64,512]{1,0:T(8,128)(2,1)S(1)}) custom-call(bf16[128,512]{1,0:T(8,128)(2,1)} %node_hbm.1, s32[1,4,32]{2,1,0:T(4,128)} %send_hbm.1), custom_call_target="tpu_custom_call" | custom-call | flops 100000000 | bytes 1000000 | tf_op jit(solution)/shard_map/pallas_call | solution.py:407
  1.8 3.0 %collective-permute-start.2 = (bf16[64,512]{1,0:T(8,128)(2,1)S(1)}, bf16[64,512]{1,0:T(8,128)(2,1)S(1)}, u32[]{:S(2)}, u32[]{:S(2)}) collective-permute-start(bf16[64,512]{1,0:T(8,128)(2,1)S(1)} %get-tuple-element.66), channel_id=1, source_target_pairs={{0,2},{2,0},{1,3},{3,1},{4,6},{6,4},{5,7},{7,5},{8,10},{10,8},{9,1... | collective-permute-start | bytes 196616 | tf_op jit(solution)/shard_map/ppermute | solution.py:421
  4.8 1.6 %collective-permute-start = (bf16[32,512]{1,0:T(8,128)(2,1)S(1)}, bf16[32,512]{1,0:T(8,128)(2,1)S(1)}, u32[]{:S(2)}, u32[]{:S(2)}) collective-permute-start(bf16[32,512]{1,0:T(8,128)(2,1)S(1)} %get-tuple-element.64), channel_id=1, source_target_pairs={{0,4},{4,8},{8,12},{12,0},{1,5},{5,9},{9,13},{13,1},{2,6},{6,10},{... | collective-permute-start | bytes 98312 | tf_op jit(solution)/shard_map/ppermute | solution.py:421
  6.4 2.2 %collective-permute-start.1 = (bf16[32,512]{1,0:T(8,128)(2,1)S(1)}, bf16[32,512]{1,0:T(8,128)(2,1)S(1)}, u32[]{:S(2)}, u32[]{:S(2)}) collective-permute-start(bf16[32,512]{1,0:T(8,128)(2,1)S(1)} %get-tuple-element.65), channel_id=1, source_target_pairs={{0,12},{4,0},{8,4},{12,8},{1,13},{5,1},{9,5},{13,9},{2,14},{6,2},{... | collective-permute-start | bytes 98312 | tf_op jit(solution)/shard_map/ppermute | solution.py:421
  8.6 2.1 %shard_map.163 = (f32[512,256]{1,0:T(8,128)S(1)}, bf16[512,128]{1,0:T(8,128)(2,1)S(1)}, bf16[128,512]{1,0:T(8,128)(2,1)S(1)}, bf16[512,128]{1,0:T(8,128)(2,1)S(1...) custom-call(bf16[128,512]{1,0:T(8,128)(2,1)S(1)} %get-tuple-element., ...), custom_call_target="tpu_custom_call" | custom-call | flops 100000000 | bytes 1000000 | tf_op jit(solution)/shard_map/pallas_call | solution.py:407
  10.7 0.0 collective-permute-done.rest_0_
  10.8 0.0 collective-permute-done.1.rest_1_
  10.8 0.0 collective-permute-done.2.rest_2_
  10.8 0.9 %shard_map.164 = (f32[512,256]{1,0:T(8,128)S(1)}, bf16[128,256]{1,0:T(8,128)(2,1)S(1)}, bf16[128,512]{1,0:T(8,128)(2,1)S(1)}) custom-call(f32[512,256]{1,0:T(8,128)S(1)} %get-tuple-element.61.pre_ref, bf16[512,128]{1,0:T(8,128)(2,1)S(1)} %get-tuple-element.62.pick_ref, bf16[128,512]{1,0:T(8,128)(2,1)S(1)} %get-tuple-element.57.collect_ref, ...), custom_call_target="tpu_custom_call" | custom-call | flops 100000000 | bytes 1000000 | tf_op jit(solution)/shard_map/pallas_call | solution.py:407
  11.6 0.1 collective-permute-start.3
  11.7 1.3 %collective-permute-done.3.other_ref = bf16[128,512]{1,0:T(8,128)(2,1)S(1)} collective-permute-done((bf16[128,512]{1,0:T(8,128)(2,1)S(1)}, bf16[128,512]{1,0:T(8,128)(2,1)S(1)}, u32[]{:S(2)}, u32[]{:S(2)}) %collective-permute-start.3) | collective-permute-done | bytes 131104 | tf_op jit(solution)/shard_map/ppermute | solution.py:421
  13.1 1.4 %shard_map.165 = (f32[128,512]{1,0:T(8,128)S(1)}, f32[128,256]{1,0:T(8,128)S(1)}, bf16[128,256]{1,0:T(8,128)(2,1)S(1)}, bf16[400,256]{1,0:T(8,128)(2,1)S(1)}, bf...) custom-call(bf16[128,512]{1,0:T(8,128)(2,1)S(1)} %get-tuple-element., ...), custom_call_target="tpu_custom_call" | custom-call | flops 100000000 | bytes 1000000 | tf_op jit(solution)/shard_map/pallas_call | solution.py:407
  14.4 0.5 %collective-permute-start.8 = (bf16[400,256]{1,0:T(8,128)(2,1)S(1)}, bf16[400,256]{1,0:T(8,128)(2,1)S(1)}, u32[]{:S(2)}, u32[]{:S(2)}) collective-permute-start(bf16[400,256]{1,0:T(8,128)(2,1)S(1)} %get-tuple-element.78), channel_id=1, source_target_pairs={{0,2},{2,0},{1,3},{3,1},{4,6},{6,4},{5,7},{7,5},{8,10},{10,8},{9,1... | collective-permute-start | bytes 614408 | tf_op jit(solution)/shard_map/ppermute | solution.py:426
  14.9 3.5 %collective-permute-start.4 = (bf16[80,512]{1,0:T(8,128)(2,1)S(1)}, bf16[80,512]{1,0:T(8,128)(2,1)S(1)}, u32[]{:S(2)}, u32[]{:S(2)}) collective-permute-start(bf16[80,512]{1,0:T(8,128)(2,1)S(1)} %get-tuple-element.75), channel_id=1, source_target_pairs={{0,12},{4,8},{8,4},{12,0},{1,13},{5,9},{9,5},{13,1},{2,14},{6,10},... | collective-permute-start | bytes 245768 | tf_op jit(solution)/shard_map/ppermute | solution.py:426
  18.4 1.7 %collective-permute-start.6 = (bf16[192,256]{1,0:T(8,128)(2,1)S(1)}, bf16[192,256]{1,0:T(8,128)(2,1)S(1)}, u32[]{:S(2)}, u32[]{:S(2)}) collective-permute-start(bf16[192,256]{1,0:T(8,128)(2,1)S(1)} %get-tuple-element.77), channel_id=1, source_target_pairs={{0,2},{2,0},{1,3},{3,1},{4,6},{6,4},{5,7},{7,5},{8,10},{10,8},{9,1... | collective-permute-start | bytes 294920 | tf_op jit(solution)/shard_map/ppermute | solution.py:426
  20.1 0.0 collective-permute-start.12
  20.1 0.8 %collective-permute-start.5 = (bf16[80,512]{1,0:T(8,128)(2,1)S(1)}, bf16[80,512]{1,0:T(8,128)(2,1)S(1)}, u32[]{:S(2)}, u32[]{:S(2)}) collective-permute-start(bf16[80,512]{1,0:T(8,128)(2,1)S(1)} %get-tuple-element.76), channel_id=1, source_target_pairs={{0,4},{4,0},{8,12},{12,8},{1,5},{5,1},{9,13},{13,9},{2,6},{6,2},{1... | collective-permute-start | bytes 245768 | tf_op jit(solution)/shard_map/ppermute | solution.py:426
  20.9 1.5 %collective-permute-done.8.arrived_ref = bf16[400,256]{1,0:T(8,128)(2,1)S(1)} collective-permute-done((bf16[400,256]{1,0:T(8,128)(2,1)S(1)}, bf16[400,256]{1,0:T(8,128)(2,1)S(1)}, u32[]{:S(2)}, u32[]{:S(2)}) %collective-permute-start.8) | collective-permute-done | bytes 204832 | tf_op jit(solution)/shard_map/ppermute | solution.py:426
  22.4 0.1 shard_map.167
  22.5 3.7 %collective-permute-start.9 = (bf16[144,256]{1,0:T(8,128)(2,1)S(1)}, bf16[144,256]{1,0:T(8,128)(2,1)S(1)}, u32[]{:S(2)}, u32[]{:S(2)}) collective-permute-start(bf16[144,256]{1,0:T(8,128)(2,1)S(1)} %get-tuple-element.80), channel_id=1, source_target_pairs={{0,12},{4,8},{8,4},{12,0},{1,13},{5,9},{9,5},{13,1},{2,14},{6,10},... | collective-permute-start | bytes 221192 | tf_op jit(solution)/shard_map/ppermute | solution.py:426
  26.2 0.4 collective-permute-done.12.refs_1_
  26.6 0.0 collective-permute-start.10
  26.6 0.0 collective-permute-done.4.three_ref.refs_0_
  26.6 1.5 %collective-permute-start.11 = (bf16[144,256]{1,0:T(8,128)(2,1)S(1)}, bf16[144,256]{1,0:T(8,128)(2,1)S(1)}, u32[]{:S(2)}, u32[]{:S(2)}) collective-permute-start(bf16[144,256]{1,0:T(8,128)(2,1)S(1)} %get-tuple-element.82.refs_4_), channel_id=1, source_target_pairs={{0,4},{4,0},{8,12},{12,8},{1,5},{5,1},{9,13},{13,9},{2,6},{6,2},{1... | collective-permute-start | bytes 221192 | tf_op jit(solution)/shard_map/ppermute | solution.py:426
  28.0 0.0 collective-permute-done.5.one_ref.refs_2_
  28.1 1.7 %collective-permute-start.13 = (bf16[64,256]{1,0:T(8,128)(2,1)S(1)}, bf16[64,256]{1,0:T(8,128)(2,1)S(1)}, u32[]{:S(2)}, u32[]{:S(2)}) collective-permute-start(bf16[64,256]{1,0:T(8,128)(2,1)S(1)} %get-tuple-element.88), channel_id=1, source_target_pairs={{0,2},{2,0},{1,3},{3,1},{4,6},{6,4},{5,7},{7,5},{8,10},{10,8},{9,1... | collective-permute-start | bytes 98312 | tf_op jit(solution)/shard_map/ppermute | solution.py:426
  29.8 0.0 collective-permute-done.6.pair_ref.refs_4_
  29.8 0.4 shard_map.166.refs_8_.own_ref
  30.2 0.1 collective-permute-start.7
  30.3 1.8 %collective-permute-done.13.refs_7_ = bf16[64,256]{1,0:T(8,128)(2,1)S(1)} collective-permute-done((bf16[64,256]{1,0:T(8,128)(2,1)S(1)}, bf16[64,256]{1,0:T(8,128)(2,1)S(1)}, u32[]{:S(2)}, u32[]{:S(2)}) %collective-permute-start.13) | collective-permute-done | bytes 32800 | tf_op jit(solution)/shard_map/ppermute | solution.py:426
  32.1 0.0 collective-permute-done.9.refs_0_
  32.1 0.0 collective-permute-done.10.refs_1_
  32.1 0.2 collective-permute-done.11.refs_2_
  32.2 0.1 shard_map.169
  32.3 2.8 %collective-permute-start.15 = (bf16[192,256]{1,0:T(8,128)(2,1)S(1)}, bf16[192,256]{1,0:T(8,128)(2,1)S(1)}, u32[]{:S(2)}, u32[]{:S(2)}) collective-permute-start(bf16[192,256]{1,0:T(8,128)(2,1)S(1)} %get-tuple-element.92.a_ref), channel_id=1, source_target_pairs={{0,12},{4,8},{8,4},{12,0},{1,13},{5,9},{9,5},{13,1},{2,14},{6,10},... | collective-permute-start | bytes 294920 | tf_op jit(solution)/shard_map/ppermute | solution.py:426
  35.1 0.0 collective-permute-start.14
  35.1 2.6 %collective-permute-start.20 = (bf16[192,256]{1,0:T(8,128)(2,1)S(1)}, bf16[192,256]{1,0:T(8,128)(2,1)S(1)}, u32[]{:S(2)}, u32[]{:S(2)}) collective-permute-start(bf16[192,256]{1,0:T(8,128)(2,1)S(1)} %get-tuple-element.92.a_ref), channel_id=1, source_target_pairs={{0,6},{2,4},{4,2},{6,0},{8,14},{10,12},{12,10},{14,8},{1,7},{3,5},... | collective-permute-start | bytes 294920 | tf_op jit(solution)/shard_map/ppermute | solution.py:432
  37.7 0.5 %collective-permute-start.19 = (bf16[192,256]{1,0:T(8,128)(2,1)S(1)}, bf16[192,256]{1,0:T(8,128)(2,1)S(1)}, u32[]{:S(2)}, u32[]{:S(2)}) collective-permute-start(bf16[192,256]{1,0:T(8,128)(2,1)S(1)} %get-tuple-element.92.a_ref), channel_id=1, source_target_pairs={{0,2},{2,0},{1,3},{3,1},{4,6},{6,4},{5,7},{7,5},{8,10},{10,8},{9,1... | collective-permute-start | bytes 294920 | tf_op jit(solution)/shard_map/ppermute | solution.py:426
  38.2 0.0 collective-permute-done.7.other_ref
  38.2 0.4 collective-permute-start.18
  38.6 0.9 %collective-permute-done.15.b_ref = bf16[192,256]{1,0:T(8,128)(2,1)S(1)} collective-permute-done((bf16[192,256]{1,0:T(8,128)(2,1)S(1)}, bf16[192,256]{1,0:T(8,128)(2,1)S(1)}, u32[]{:S(2)}, u32[]{:S(2)}) %collective-permute-start.15) | collective-permute-done | bytes 98336 | tf_op jit(solution)/shard_map/ppermute | solution.py:426
  39.5 1.1 %collective-permute-start.17 = (bf16[192,256]{1,0:T(8,128)(2,1)S(1)}, bf16[192,256]{1,0:T(8,128)(2,1)S(1)}, u32[]{:S(2)}, u32[]{:S(2)}) collective-permute-start(bf16[192,256]{1,0:T(8,128)(2,1)S(1)} %collective-permute-done.15.b_ref), channel_id=1, source_target_pairs={{0,2},{2,0},{1,3},{3,1},{4,6},{6,4},{5,7},{7,5},{8,10},{10,8},{9,1... | collective-permute-start | bytes 294920 | tf_op jit(solution)/shard_map/ppermute | solution.py:426
  40.6 2.3 %collective-permute-done.14.a_ref = bf16[192,256]{1,0:T(8,128)(2,1)S(1)} collective-permute-done((bf16[192,256]{1,0:T(8,128)(2,1)S(1)}, bf16[192,256]{1,0:T(8,128)(2,1)S(1)}, u32[]{:S(2)}, u32[]{:S(2)}) %collective-permute-start.14) | collective-permute-done | bytes 98336 | tf_op jit(solution)/shard_map/ppermute | solution.py:426
  42.9 0.2 collective-permute-start.16
  43.1 0.8 %shard_map.170 = (f32[128,512]{1,0:T(8,128)}, bf16[128,512]{1,0:T(8,128)(2,1)}, f32[1,256]{1,0:T(1,128)}, f32[1,512]{1,0:T(1,128)}) custom-call(bf16[128,512]{1,0:T(8,128)(2,1)S(1)} %get-tuple-element.55.cot_ref, bf16[128,512]{1,0:T(8,128)(2,1)S(1)} %get-tuple-element.54.refs_0_.node_ref, f32[1,512]{1,0:T(1,128)S(1)} %get-tuple-element.56.gain_ref, ...), custom_call_target="tpu_custom_call" | custom-call | flops 100000000 | bytes 1000000 | tf_op jit(solution)/shard_map/pallas_call | solution.py:407
  43.9 0.0 collective-permute-done.20.d_ref
  43.9 0.0 collective-permute-done.19.c_ref
  43.9 0.3 collective-permute-done.18.b_ref
  44.1 0.9 %shard_map.171 = (f32[512,256]{1,0:T(8,128)}, f32[512,256]{1,0:T(8,128)}, f32[256,512]{1,0:T(8,128)}) custom-call(bf16[192,256]{1,0:T(8,128)(2,1)S(1)} %get-tuple-element.92.a_ref, bf16[192,256]{1,0:T(8,128)(2,1)S(1)} %collective-permute-done.18.b_ref, bf16[192,256]{1,0:T(8,128)(2,1)S(1)} %collective-permute-done.19.c_ref, ...), custom_call_target="tpu_custom_call" | custom-call | flops 100000000 | bytes 1000000 | tf_op jit(solution)/shard_map/pallas_call | solution.py:407
  45.1 0.0 collective-permute-done.17.d_ref
  45.1 2.4 %collective-permute-done.16.c_ref = bf16[192,256]{1,0:T(8,128)(2,1)S(1)} collective-permute-done((bf16[192,256]{1,0:T(8,128)(2,1)S(1)}, bf16[192,256]{1,0:T(8,128)(2,1)S(1)}, u32[]{:S(2)}, u32[]{:S(2)}) %collective-permute-start.16) | collective-permute-done | bytes 98336 | tf_op jit(solution)/shard_map/ppermute | solution.py:426
  47.5 0.9 %shard_map.172 = (f32[512,256]{1,0:T(8,128)}, f32[512,256]{1,0:T(8,128)}, f32[256,512]{1,0:T(8,128)}) custom-call(bf16[192,256]{1,0:T(8,128)(2,1)S(1)} %collective-permute-done.14.a_ref, bf16[192,256]{1,0:T(8,128)(2,1)S(1)} %collective-permute-done.15.b_ref, ...), custom_call_target="tpu_custom_call", output_to_operand_aliasing={{0}: (4, {}), {1}: (5, {}), {2}: (6, {})} | custom-call | flops 100000000 | bytes 1000000 | tf_op jit(solution)/shard_map/pallas_call | solution.py:407
  (1 shorter events, 0.0 us)
Async XLA Ops:
  1.8 9.0 %collective-permute-start.2 = (bf16[64,512]{1,0:T(8,128)(2,1)S(1)}, bf16[64,512]{1,0:T(8,128)(2,1)S(1)}, u32[]{:S(2)}, u32[]{:S(2)}) collective-permute-start(bf16[64,512]{1,0:T(8,128)(2,1)S(1)} %get-tuple-element.66), channel_id=1, source_target_pairs={{0,2},{2,0},{1,3},{3,1},{4,6},{6,4},{5,7},{7,5},{8,10},{10,8},{9,1... | collective-permute-start | bytes 196616 | tf_op jit(solution)/shard_map/ppermute | solution.py:421
  4.8 5.9 %collective-permute-start = (bf16[32,512]{1,0:T(8,128)(2,1)S(1)}, bf16[32,512]{1,0:T(8,128)(2,1)S(1)}, u32[]{:S(2)}, u32[]{:S(2)}) collective-permute-start(bf16[32,512]{1,0:T(8,128)(2,1)S(1)} %get-tuple-element.64), channel_id=1, source_target_pairs={{0,4},{4,8},{8,12},{12,0},{1,5},{5,9},{9,13},{13,1},{2,6},{6,10},{... | collective-permute-start | bytes 98312 | tf_op jit(solution)/shard_map/ppermute | solution.py:421
  6.4 4.4 %collective-permute-start.1 = (bf16[32,512]{1,0:T(8,128)(2,1)S(1)}, bf16[32,512]{1,0:T(8,128)(2,1)S(1)}, u32[]{:S(2)}, u32[]{:S(2)}) collective-permute-start(bf16[32,512]{1,0:T(8,128)(2,1)S(1)} %get-tuple-element.65), channel_id=1, source_target_pairs={{0,12},{4,0},{8,4},{12,8},{1,13},{5,1},{9,5},{13,9},{2,14},{6,2},{... | collective-permute-start | bytes 98312 | tf_op jit(solution)/shard_map/ppermute | solution.py:421
  11.6 1.4 %collective-permute-start.3 = (bf16[128,512]{1,0:T(8,128)(2,1)S(1)}, bf16[128,512]{1,0:T(8,128)(2,1)S(1)}, u32[]{:S(2)}, u32[]{:S(2)}) collective-permute-start(bf16[128,512]{1,0:T(8,128)(2,1)S(1)} %get-tuple-element.69.own_ref), channel_id=1, source_target_pairs={{0,1},{1,0},{2,3},{3,2},{4,5},{5,4},{6,7},{7,6},{8,9},{9,8},{10,11... | collective-permute-start | bytes 393224 | tf_op jit(solution)/shard_map/ppermute | solution.py:421
  14.4 8.0 %collective-permute-start.8 = (bf16[400,256]{1,0:T(8,128)(2,1)S(1)}, bf16[400,256]{1,0:T(8,128)(2,1)S(1)}, u32[]{:S(2)}, u32[]{:S(2)}) collective-permute-start(bf16[400,256]{1,0:T(8,128)(2,1)S(1)} %get-tuple-element.78), channel_id=1, source_target_pairs={{0,2},{2,0},{1,3},{3,1},{4,6},{6,4},{5,7},{7,5},{8,10},{10,8},{9,1... | collective-permute-start | bytes 614408 | tf_op jit(solution)/shard_map/ppermute | solution.py:426
  14.9 11.6 %collective-permute-start.4 = (bf16[80,512]{1,0:T(8,128)(2,1)S(1)}, bf16[80,512]{1,0:T(8,128)(2,1)S(1)}, u32[]{:S(2)}, u32[]{:S(2)}) collective-permute-start(bf16[80,512]{1,0:T(8,128)(2,1)S(1)} %get-tuple-element.75), channel_id=1, source_target_pairs={{0,12},{4,8},{8,4},{12,0},{1,13},{5,9},{9,5},{13,1},{2,14},{6,10},... | collective-permute-start | bytes 245768 | tf_op jit(solution)/shard_map/ppermute | solution.py:426
  18.4 11.4 %collective-permute-start.6 = (bf16[192,256]{1,0:T(8,128)(2,1)S(1)}, bf16[192,256]{1,0:T(8,128)(2,1)S(1)}, u32[]{:S(2)}, u32[]{:S(2)}) collective-permute-start(bf16[192,256]{1,0:T(8,128)(2,1)S(1)} %get-tuple-element.77), channel_id=1, source_target_pairs={{0,2},{2,0},{1,3},{3,1},{4,6},{6,4},{5,7},{7,5},{8,10},{10,8},{9,1... | collective-permute-start | bytes 294920 | tf_op jit(solution)/shard_map/ppermute | solution.py:426
  20.1 6.4 %collective-permute-start.12 = (bf16[64,512]{1,0:T(8,128)(2,1)S(1)}, bf16[64,512]{1,0:T(8,128)(2,1)S(1)}, u32[]{:S(2)}, u32[]{:S(2)}) collective-permute-start(bf16[64,512]{1,0:T(8,128)(2,1)S(1)} %get-tuple-element.85), channel_id=1, source_target_pairs={{0,8},{4,12},{8,0},{12,4},{1,9},{5,13},{9,1},{13,5},{2,10},{6,14},... | collective-permute-start | bytes 196616 | tf_op jit(solution)/shard_map/ppermute | solution.py:426
  20.1 7.9 %collective-permute-start.5 = (bf16[80,512]{1,0:T(8,128)(2,1)S(1)}, bf16[80,512]{1,0:T(8,128)(2,1)S(1)}, u32[]{:S(2)}, u32[]{:S(2)}) collective-permute-start(bf16[80,512]{1,0:T(8,128)(2,1)S(1)} %get-tuple-element.76), channel_id=1, source_target_pairs={{0,4},{4,0},{8,12},{12,8},{1,5},{5,1},{9,13},{13,9},{2,6},{6,2},{1... | collective-permute-start | bytes 245768 | tf_op jit(solution)/shard_map/ppermute | solution.py:426
  22.5 9.6 %collective-permute-start.9 = (bf16[144,256]{1,0:T(8,128)(2,1)S(1)}, bf16[144,256]{1,0:T(8,128)(2,1)S(1)}, u32[]{:S(2)}, u32[]{:S(2)}) collective-permute-start(bf16[144,256]{1,0:T(8,128)(2,1)S(1)} %get-tuple-element.80), channel_id=1, source_target_pairs={{0,12},{4,8},{8,4},{12,0},{1,13},{5,9},{9,5},{13,1},{2,14},{6,10},... | collective-permute-start | bytes 221192 | tf_op jit(solution)/shard_map/ppermute | solution.py:426
  26.6 5.5 %collective-permute-start.10 = (bf16[144,256]{1,0:T(8,128)(2,1)S(1)}, bf16[144,256]{1,0:T(8,128)(2,1)S(1)}, u32[]{:S(2)}, u32[]{:S(2)}) collective-permute-start(bf16[144,256]{1,0:T(8,128)(2,1)S(1)} %get-tuple-element.81), channel_id=1, source_target_pairs={{0,8},{4,12},{8,0},{12,4},{1,9},{5,13},{9,1},{13,5},{2,10},{6,14},... | collective-permute-start | bytes 221192 | tf_op jit(solution)/shard_map/ppermute | solution.py:426
  26.6 5.7 %collective-permute-start.11 = (bf16[144,256]{1,0:T(8,128)(2,1)S(1)}, bf16[144,256]{1,0:T(8,128)(2,1)S(1)}, u32[]{:S(2)}, u32[]{:S(2)}) collective-permute-start(bf16[144,256]{1,0:T(8,128)(2,1)S(1)} %get-tuple-element.82.refs_4_), channel_id=1, source_target_pairs={{0,4},{4,0},{8,12},{12,8},{1,5},{5,1},{9,13},{13,9},{2,6},{6,2},{1... | collective-permute-start | bytes 221192 | tf_op jit(solution)/shard_map/ppermute | solution.py:426
  28.1 4.0 %collective-permute-start.13 = (bf16[64,256]{1,0:T(8,128)(2,1)S(1)}, bf16[64,256]{1,0:T(8,128)(2,1)S(1)}, u32[]{:S(2)}, u32[]{:S(2)}) collective-permute-start(bf16[64,256]{1,0:T(8,128)(2,1)S(1)} %get-tuple-element.88), channel_id=1, source_target_pairs={{0,2},{2,0},{1,3},{3,1},{4,6},{6,4},{5,7},{7,5},{8,10},{10,8},{9,1... | collective-permute-start | bytes 98312 | tf_op jit(solution)/shard_map/ppermute | solution.py:426
  30.2 8.0 %collective-permute-start.7 = (bf16[128,512]{1,0:T(8,128)(2,1)S(1)}, bf16[128,512]{1,0:T(8,128)(2,1)S(1)}, u32[]{:S(2)}, u32[]{:S(2)}) collective-permute-start(bf16[128,512]{1,0:T(8,128)(2,1)S(1)} %shard_map.166.refs_8_.own_ref), channel_id=1, source_target_pairs={{0,1},{1,0},{2,3},{3,2},{4,5},{5,4},{6,7},{7,6},{8,9},{9,8},{10,11... | collective-permute-start | bytes 393224 | tf_op jit(solution)/shard_map/ppermute | solution.py:421
  32.3 7.2 %collective-permute-start.15 = (bf16[192,256]{1,0:T(8,128)(2,1)S(1)}, bf16[192,256]{1,0:T(8,128)(2,1)S(1)}, u32[]{:S(2)}, u32[]{:S(2)}) collective-permute-start(bf16[192,256]{1,0:T(8,128)(2,1)S(1)} %get-tuple-element.92.a_ref), channel_id=1, source_target_pairs={{0,12},{4,8},{8,4},{12,0},{1,13},{5,9},{9,5},{13,1},{2,14},{6,10},... | collective-permute-start | bytes 294920 | tf_op jit(solution)/shard_map/ppermute | solution.py:426
  35.1 7.7 %collective-permute-start.14 = (bf16[192,256]{1,0:T(8,128)(2,1)S(1)}, bf16[192,256]{1,0:T(8,128)(2,1)S(1)}, u32[]{:S(2)}, u32[]{:S(2)}) collective-permute-start(bf16[192,256]{1,0:T(8,128)(2,1)S(1)} %get-tuple-element.92.a_ref), channel_id=1, source_target_pairs={{0,8},{4,12},{8,0},{12,4},{1,9},{5,13},{9,1},{13,5},{2,10},{6,14},... | collective-permute-start | bytes 294920 | tf_op jit(solution)/shard_map/ppermute | solution.py:426
  35.1 8.7 %collective-permute-start.20 = (bf16[192,256]{1,0:T(8,128)(2,1)S(1)}, bf16[192,256]{1,0:T(8,128)(2,1)S(1)}, u32[]{:S(2)}, u32[]{:S(2)}) collective-permute-start(bf16[192,256]{1,0:T(8,128)(2,1)S(1)} %get-tuple-element.92.a_ref), channel_id=1, source_target_pairs={{0,6},{2,4},{4,2},{6,0},{8,14},{10,12},{12,10},{14,8},{1,7},{3,5},... | collective-permute-start | bytes 294920 | tf_op jit(solution)/shard_map/ppermute | solution.py:432
  37.7 6.2 %collective-permute-start.19 = (bf16[192,256]{1,0:T(8,128)(2,1)S(1)}, bf16[192,256]{1,0:T(8,128)(2,1)S(1)}, u32[]{:S(2)}, u32[]{:S(2)}) collective-permute-start(bf16[192,256]{1,0:T(8,128)(2,1)S(1)} %get-tuple-element.92.a_ref), channel_id=1, source_target_pairs={{0,2},{2,0},{1,3},{3,1},{4,6},{6,4},{5,7},{7,5},{8,10},{10,8},{9,1... | collective-permute-start | bytes 294920 | tf_op jit(solution)/shard_map/ppermute | solution.py:426
  38.2 5.9 %collective-permute-start.18 = (bf16[192,256]{1,0:T(8,128)(2,1)S(1)}, bf16[192,256]{1,0:T(8,128)(2,1)S(1)}, u32[]{:S(2)}, u32[]{:S(2)}) collective-permute-start(bf16[192,256]{1,0:T(8,128)(2,1)S(1)} %get-tuple-element.92.a_ref), channel_id=1, source_target_pairs={{0,4},{4,0},{8,12},{12,8},{1,5},{5,1},{9,13},{13,9},{2,6},{6,2},{1... | collective-permute-start | bytes 294920 | tf_op jit(solution)/shard_map/ppermute | solution.py:426
  39.5 5.6 %collective-permute-start.17 = (bf16[192,256]{1,0:T(8,128)(2,1)S(1)}, bf16[192,256]{1,0:T(8,128)(2,1)S(1)}, u32[]{:S(2)}, u32[]{:S(2)}) collective-permute-start(bf16[192,256]{1,0:T(8,128)(2,1)S(1)} %collective-permute-done.15.b_ref), channel_id=1, source_target_pairs={{0,2},{2,0},{1,3},{3,1},{4,6},{6,4},{5,7},{7,5},{8,10},{10,8},{9,1... | collective-permute-start | bytes 294920 | tf_op jit(solution)/shard_map/ppermute | solution.py:426
  42.9 4.6 %collective-permute-start.16 = (bf16[192,256]{1,0:T(8,128)(2,1)S(1)}, bf16[192,256]{1,0:T(8,128)(2,1)S(1)}, u32[]{:S(2)}, u32[]{:S(2)}) collective-permute-start(bf16[192,256]{1,0:T(8,128)(2,1)S(1)} %collective-permute-done.14.a_ref), channel_id=1, source_target_pairs={{0,2},{2,0},{1,3},{3,1},{4,6},{6,4},{5,7},{7,5},{8,10},{10,8},{9,1... | collective-permute-start | bytes 294920 | tf_op jit(solution)/shard_map/ppermute | solution.py:426

commit v15 on v14

--- a/solution.py
+++ b/solution.py
@@ -10,7 +10,7 @@
 BLOCK = 128
 EPSILON = 1e-05
 TAIL = 16
-N_FETCHED = 9
+N_FETCHED = 5
 VMEM_LIMIT = 24 * 1024 * 1024
 
 f32 = jnp.float32
@@ -62,10 +62,21 @@
     return copies
 
 
-def send_kernel(node_hbm, send_hbm, node_ref, send_ref, *rest):
-    *out_refs, sems = rest
-    for copy in fetch(sems, (node_hbm, node_ref), (send_hbm, send_ref)):
-        copy.wait()
+def send_kernel(
+    node_hbm, send_hbm, w_src_hbm, w_dst_hbm, w_out_hbm, bias_hbm,
+    node_ref, send_ref, packed_ref, *rest,
+):
+    *out_refs, bias_ref, sems = rest
+    hid = packed_ref.shape[1]
+    width = w_src_hbm.shape[0]
+    pairs = [(node_hbm, node_ref), (send_hbm, send_ref), (bias_hbm, bias_ref)]
+    pairs += [(w_src_hbm, packed_ref.at[pl.ds(0, width)]), (w_dst_hbm, packed_ref.at[pl.ds(width, width)])]
+    for k in range(width // hid):
+        target = packed_ref.at[pl.ds(2 * width + k * hid, hid)]
+        pairs.append((w_out_hbm.at[:, pl.ds(k * hid, hid)], target))
+    copies = fetch(sems, *pairs)
+    copies[0].wait()
+    copies[1].wait()
     node = node_ref[...]
     rows = node.shape[0]
     halo = send_ref.shape[2]
@@ -81,19 +92,42 @@
     else:
         out_refs[2][...] = pieces[2]
         out_refs[3][...] = pieces[3]
-
-
-def local_kernel(*refs):
-    node_ref, ins, refs = refs[0], refs[1 : 1 + N_FETCHED], refs[1 + N_FETCHED :]
+    copies[2].wait()
+    bias = bias_ref[...]
+    parts = []
+    for _ in range(3):
+        parts.append(bias.astype(bf16).astype(f32))
+        bias = bias - parts[-1]
+    parts.append(jnp.zeros((TAIL - 3, hid), f32))
+    packed_ref[packed_ref.shape[0] - TAIL :, :] = jnp.concatenate(parts, axis=0).astype(bf16)
+    for copy in copies[3:]:
+        copy.wait()
+
+
+def unpacked(ref, width):
+    hid = ref.shape[1]
+    w_out = [ref[at : at + hid, :] for at in range(2 * width, 3 * width, hid)]
+    tail = ref[ref.shape[0] - TAIL :, :].astype(f32)
+    bias = tail[0:1] + tail[1:2] + tail[2:3]
+    return ref[0:width, :], ref[width : 2 * width, :], jnp.concatenate(w_out, axis=1), bias
+
+
+def local_kernel(node_ref, packed_ref, other_ref, *refs):
+    ins, refs = refs[:N_FETCHED], refs[N_FETCHED:]
     pre_ref, pick_ref, collect_ref, spread_ref, scatter_ref, *refs = refs
-    w_src_ref, w_dst_ref, w_out_ref, gain_ref, cot_ref, count_ref, src_ref, dst_ref, bias_ref, sems = refs
-    outs = (src_ref, dst_ref, count_ref, bias_ref, w_src_ref, w_dst_ref, w_out_ref, gain_ref, cot_ref)
-    copies = fetch(sems, *zip(ins, outs))
+    gain_ref, cot_ref, count_ref, src_ref, dst_ref, sems = refs
+    copies = fetch(sems, *zip(ins, (src_ref, dst_ref, count_ref, gain_ref, cot_ref)))
     node = node_ref[...]
-    rows = node.shape[0]
+    rows, width = node.shape
+    w_src, w_dst, _, bias = unpacked(packed_ref, width)
+    w_src_other, w_dst_other, _, bias_other = unpacked(other_ref, width)
+    projected = dot(node, jnp.concatenate([w_src, w_src_other, w_dst, w_dst_other], axis=1))
+    both = projected.shape[1] // 2
+    projected = jnp.concatenate([projected[:, :both], projected[:, both:]], axis=0)
+    high, low = split(projected)
+    for copy in copies:
+        copy.wait()
     edges = src_ref.shape[1]
-    for copy in copies[:3]:
-        copy.wait()
     scatter_ref[...] = one_hot(iota(scatter_ref.shape, 0) == src_ref[...])
     used = usable_row(count_ref, edges) > 0
     collect_ref[...] = one_hot((iota((rows, edges), 0) == dst_ref[...]) & used)
@@ -104,11 +138,8 @@
     near = one_hot(source == lane)
     pick_ref[...] = one_hot(source == lane + rows)
     spread_ref[...] = one_hot((target == lane) & used)
-    both = jnp.concatenate([dot(near, node), dot(one_hot(target == lane), node)], axis=1).astype(bf16)
-    for copy in copies[3:]:
-        copy.wait()
-    weights = jnp.concatenate([w_src_ref[...], w_dst_ref[...]], axis=0)
-    pre_ref[...] = dot(both, weights) + bias_ref[...]
+    ends = jnp.concatenate([near, one_hot(target == lane)], axis=1)
+    pre_ref[...] = dot(ends, high) + dot(ends, low) + jnp.concatenate([bias, bias_other], axis=1)
 
 
 def twice(x):
@@ -119,24 +150,9 @@
     return jnp.concatenate(split(x), axis=0)
 
 
-def forward_kernel(pre_ref, pick_ref, collect_ref, w_src_ref, w_out_ref, *rest):
-    *halo_refs, factor_ref, hidden_ref, partial_ref = rest
-    halo = jnp.concatenate([r[...] for r in halo_refs], axis=0)
-    far = stacked(dot(halo, w_src_ref[...]))
-    pre = pre_ref[...] + dot(twice(pick_ref[...]), far)
-    sig = 0.5 + 0.5 * jnp.tanh(0.5 * pre)
-    factor_ref[...] = sig * (1.0 + pre * (1.0 - sig))
-    hidden = dot(collect_ref[...], (pre * sig).astype(bf16))
-    high, low = split(hidden)
-    hidden_ref[...] = high
-    w_out = w_out_ref[...]
-    partial_ref[...] = (dot(high, w_out) + dot(low, w_out)).astype(bf16)
-
-
-def backward_kernel(
+def edge_kernel(
     geometry,
-    node_ref, collect_ref, spread_ref, scatter_ref, w_out_ref, gain_ref, cot_ref,
-    factor_ref, hidden_ref, own_ref, other_ref,
+    node_ref, pre_ref, pick_ref, collect_ref, spread_ref, scatter_ref, packed_ref, other_ref, gain_ref, cot_ref,
     *rest,
 ):
     peers, chunk, n_halo, paired = geometry
@@ -145,7 +161,24 @@
     normed_ref, local_ref, target_ref, *message_refs = rest[n_halo:]
     node = node_ref[...]
     rows, width = node.shape
-    aggregate = own_ref[...].astype(f32) + other_ref[...].astype(f32)
+    hid = packed_ref.shape[1]
+    halo_rows = jnp.concatenate([r[...] for r in halo_refs], axis=0)
+    w_src, _, w_out, _ = unpacked(packed_ref, width)
+    w_src_other, _, w_out_other, _ = unpacked(other_ref, width)
+
+    far = stacked(dot(halo_rows, jnp.concatenate([w_src, w_src_other], axis=1)))
+    pre = pre_ref[...] + dot(twice(pick_ref[...]), far)
+    sig = 0.5 + 0.5 * jnp.tanh(0.5 * pre)
+    hidden = dot(collect_ref[...], (pre * sig).astype(bf16))
+    pre, sig = pre[:, :hid], sig[:, :hid]
+    factor = sig * (1.0 + pre * (1.0 - sig))
+    parts = []
+    for at, w in ((0, w_out), (hid, w_out_other)):
+        high, low = split(hidden[:, at : at + hid])
+        parts.append(dot(high, w) + dot(low, w))
+    hidden_low = hidden[:, :hid].astype(bf16)
+    aggregate = parts[0] + parts[1]
+
     center = aggregate - jnp.mean(aggregate, axis=1, keepdims=True)
     variance = jnp.mean(center * center, axis=1, keepdims=True)
     inverse = lax.rsqrt(variance + EPSILON)
@@ -162,10 +195,10 @@
     normed_ref[...] = normed
     gain_part = jnp.sum(upstream * normed, axis=0, keepdims=True)
 
-    act_grad = dot(twice(spread_ref[...]), stacked(dot(agg_grad, w_out_ref[...], NT)))
-    pre_grad = (act_grad * factor_ref[...]).astype(bf16)
-
-    table = jnp.concatenate([node] + [r[...] for r in halo_refs], axis=0)
+    act_grad = dot(twice(spread_ref[...]), stacked(dot(agg_grad, w_out, NT)))
+    pre_grad = (act_grad * factor).astype(bf16)
+
+    table = jnp.concatenate([node, halo_rows], axis=0)
     by_source = dot(scatter_ref[...], pre_grad)
     by_target = dot(collect_ref[...], pre_grad)
     local_ref[...] = by_source[:rows]
@@ -173,11 +206,10 @@
     by_source_low = by_source.astype(bf16)
     target_ref[...] = by_target_low
 
-    hid = by_source.shape[1]
     bias_part = jnp.sum(by_target, axis=0, keepdims=True)
     src_part = dot(table, by_source_low, TN).astype(bf16)
     dst_part = dot(node, by_target_low, TN).astype(bf16)
-    out_part = dot(hidden_ref[...], agg_grad, TN).astype(bf16)
+    out_part = dot(hidden_low, agg_grad, TN).astype(bf16)
     vectors = [bias_part] + [gain_part[:, at : at + hid] for at in range(0, width, hid)]
     tail = tail_of(vectors)
     back = by_source_low[rows:]
@@ -351,24 +383,23 @@
         at += out_ref.shape[0]
 
 
-def node_part(send_ref, local_ref, target_ref, w_src_ref, w_dst_ref, returned, out_ref):
+def node_part(send_ref, local_ref, target_ref, packed_ref, returned, out_ref):
     rows = local_ref.shape[0]
     halo = send_ref.shape[2]
     picks = [one_hot(iota((rows, halo), 0) == send_ref[0, d : d + 1, :]) for d in range(4)]
     total = local_ref[...] + dot(jnp.concatenate(picks, axis=1), jnp.concatenate(returned, axis=0))
-    out_ref[...] = (
-        dot(total.astype(bf16), w_src_ref[...], NT) + dot(target_ref[...], w_dst_ref[...], NT)
-    ).astype(bf16)
-
-
-def node_kernel(send_ref, local_ref, target_ref, w_src_ref, w_dst_ref, *rest):
+    w_src, w_dst, _, _ = unpacked(packed_ref, out_ref.shape[1])
+    out_ref[...] = (dot(total.astype(bf16), w_src, NT) + dot(target_ref[...], w_dst, NT)).astype(bf16)
+
+
+def node_kernel(send_ref, local_ref, target_ref, packed_ref, *rest):
     *back_refs, out_ref = rest
     returned = [r[...] for r in back_refs]
-    node_part(send_ref, local_ref, target_ref, w_src_ref, w_dst_ref, returned, out_ref)
+    node_part(send_ref, local_ref, target_ref, packed_ref, returned, out_ref)
 
 
 def paired_node_kernel(
-    send_ref, local_ref, target_ref, w_src_ref, w_dst_ref, three_ref, one_ref, pair_ref, out_ref
+    send_ref, local_ref, target_ref, packed_ref, three_ref, one_ref, pair_ref, out_ref
 ):
     even = lax.axis_index("mesh") % 2 == 0
     halo = send_ref.shape[2]
@@ -380,7 +411,7 @@
     returned = [
         jnp.where(even, one, three), jnp.where(even, three, one), pair_ref[pair_ref.shape[0] - 2 * halo :, :]
     ]
-    node_part(send_ref, local_ref, target_ref, w_src_ref, w_dst_ref, returned, out_ref)
+    node_part(send_ref, local_ref, target_ref, packed_ref, returned, out_ref)
 
 
 def finish_kernel(cot_ref, node_ref, gain_ref, normed_ref, own_ref, other_ref, *rest):
@@ -509,47 +540,49 @@
     def in_hbm(x):
         return pltpu.with_memory_space_constraint(x, pltpu.HBM)
 
-    node, send, *outgoing = call(
+    bias = hidden_bias.reshape(1, hid)
+    operands = [node_state, send_rows, w_src, w_dst, w_out, bias]
+    node, send, packed, *outgoing = call(
         send_kernel,
-        [shape((rows, width), bf16), shape(send_rows.shape, jnp.int32)]
+        [
+            shape((rows, width), bf16),
+            shape(send_rows.shape, jnp.int32),
+            shape((3 * width + TAIL, hid), bf16),
+        ]
         + [shape((n, width), bf16) for n in piece],
-        in_hbm(node_state), in_hbm(send_rows),
-        specs=[HBM, HBM],
-        scratch=[pltpu.SemaphoreType.DMA((2,))],
+        *[in_hbm(x) for x in operands],
+        specs=[HBM] * len(operands),
+        scratch=[pltpu.VMEM((1, hid), f32), pltpu.SemaphoreType.DMA((5 + width // hid,))],
     )
     arrived = [shifted(x, axis, by) for x, (axis, by) in zip(outgoing, routes)]
+
+    other = shifted(packed, "lat", 1)
 
     fetched = [
         edge_src.reshape(1, edges), edge_dst.reshape(1, edges), block_count,
-        hidden_bias.reshape(1, hid), w_src, w_dst, w_out, norm_gain.reshape(1, width), cotangent,
+        norm_gain.reshape(1, width), cotangent,
     ]
-    pre, pick, collect, spread, scatter, w_src, w_dst, w_out, gain, cot = call(
+    pre, pick, collect, spread, scatter, gain, cot = call(
         local_kernel,
         [
-            shape((edges, hid), f32),
+            shape((edges, 2 * hid), f32),
             shape((edges, 4 * halo), bf16),
             shape((rows, edges), bf16),
             shape((edges, rows), bf16),
             shape((rows + 4 * halo, edges), bf16),
-        ]
-        + [shape(x.shape, x.dtype) for x in fetched[4:]],
-        node, *[in_hbm(x) for x in fetched],
-        specs=[VMEM] + [HBM] * len(fetched),
+            shape((1, width), f32),
+            shape((rows, width), bf16),
+        ],
+        node, packed, other, *[in_hbm(x) for x in fetched],
+        specs=[VMEM] * 3 + [HBM] * len(fetched),
         scratch=[
             pltpu.SMEM(block_count.shape, jnp.int32),
             pltpu.VMEM((1, edges), jnp.int32),
             pltpu.VMEM((1, edges), jnp.int32),
-            pltpu.VMEM((1, hid), f32),
             pltpu.SemaphoreType.DMA((N_FETCHED,)),
         ],
     )
 
-    factor, hidden, partial = call(
-        forward_kernel,
-        [shape((edges, hid), f32), shape((rows, hid), bf16), shape((rows, width), bf16)],
-        pre, pick, collect, w_src, w_out, *arrived,
-    )
-    other = shifted(partial, "lat", 1)
 
     lines = lax.axis_size("mesh")
     paired = merged and lines == 4
@@ -563,10 +596,10 @@
         message_shapes = [shape((peers, chunk + TAIL, hid), bf16)]
         message_shapes += [shape((n, hid), bf16) for n in piece]
     normed, local, target, *messages = call(
-        functools.partial(backward_kernel, (peers, chunk, n_halo, paired)),
+        functools.partial(edge_kernel, (peers, chunk, n_halo, paired)),
         [shape((rows, width), f32), shape((rows, hid), f32), shape((rows, hid), bf16)]
         + message_shapes,
-        node, collect, spread, scatter, w_out, gain, cot, factor, hidden, partial, other, *arrived,
+        node, pre, pick, collect, spread, scatter, packed, other, gain, cot, *arrived,
         scratch=[
             pltpu.VMEM((hid, width), bf16),
             pltpu.VMEM((2 * halo, hid), bf16),
@@ -578,7 +611,7 @@
         return call(
             paired_node_kernel if paired else node_kernel,
             shape((rows, width), bf16),
-            send, local, target, w_src, w_dst, *returned,
+            send, local, target, packed, *returned,
         )
 
     if paired:

time: 48.6 us -> 48.5 us (level)
  starting transfers between devices: 27.9 us -> 30.1 us
  waiting for transfers between devices: 11.1 us -> 9.01 us
    ppermute x1, starting transfers between devices: 2.55 us -> 3.69 us  [diagonal(): return lax.ppermute(x, ('mesh', 'sub'), moves)]
    ppermute x15, starting transfers between devices: 18.4 us -> 19.5 us  [across(): return lax.ppermute(x, axis, [(i, i ^ k) for i in range(count)])]
    ppermute x15, waiting for transfers between devices: 9.76 us -> 8.67 us  [across(): return lax.ppermute(x, axis, [(i, i ^ k) for i in range(count)])]
    ppermute x5, waiting for transfers between devices: 1.38 us -> 0.33 us  [shifted(): return lax.ppermute(x, axis, [(i, (i + by) % count) for i in range(count)])]
    pallas_call x11 -> x10, Pallas kernels: 8.69 us -> 8.46 us  [call(): pl.pallas_call(kernel, out_shape=outs, in_specs=specs or [VMEM] * len(arg...]
  transfers between devices with their start and end apart: 21 -> 21, of which waited for: 9 -> 9; matrix products, arithmetic and copies ran while one was open for 0% -> 0% of each run, Pallas kernels for 9% -> 8%
where the time goes in v15:
time: 48.5 us; the launch traced here: 48.3 us
  starting transfers between devices  30.1 us (62%)
  waiting for transfers between devices  9.01 us (19%)
  Pallas kernels  8.46 us (17%)
  between operations  0.71 us (1%)
    ppermute x15, starting transfers between devices, across(): return lax.ppermute(x, axis, [(i, i ^ k) for i in range(count)])  19.5 us
    ppermute x15, waiting for transfers between devices, across(): return lax.ppermute(x, axis, [(i, i ^ k) for i in range(count)])  8.67 us
    pallas_call x10, Pallas kernels, call(): pl.pallas_call(kernel, out_shape=outs, in_specs=specs or [VMEM] * len(arg...  8.46 us
    ppermute x5, starting transfers between devices, shifted(): return lax.ppermute(x, axis, [(i, (i + by) % count) for i in range(count)])  6.98 us
    ppermute x1, starting transfers between devices, diagonal(): return lax.ppermute(x, ('mesh', 'sub'), moves)  3.69 us
  transfers between devices with their start and end apart: 21, of which 9 were waited for; matrix products, arithmetic and copies ran while one was open for 0% of the time, Pallas kernels for 8%

profile of v15, /device:TPU:0, one launch (start us, length us, event | category | flops | bytes accessed | tf_op | source)
XLA Modules:
  0.0 48.3 jit_solution(7509627793336913429)
XLA Ops:
  0.6 1.3 %shard_map.162 = (bf16[128,512]{1,0:T(8,128)(2,1)S(1)}, s32[1,4,32]{2,1,0:T(4,128)S(1)}, bf16[1552,256]{1,0:T(8,128)(2,1)S(1)}, bf16[32,512]{1,0:T(8,128)(2,1)S(...) custom-call(bf16[128,512]{1,0:T(8,128)(2,1)} %node_hbm.1, s32[1,4,32]{2,1,0:T(4,128)} %send_hbm.1, ...), custom_call_target="tpu_custom_call" | custom-call | flops 100000000 | bytes 1000000 | tf_op jit(solution)/shard_map/pallas_call | solution.py:438
  1.9 0.5 %collective-permute-start = (bf16[1552,256]{1,0:T(8,128)(2,1)S(1)}, bf16[1552,256]{1,0:T(8,128)(2,1)S(1)}, u32[]{:S(2)}, u32[]{:S(2)}) collective-permute-start(bf16[1552,256]{1,0:T(8,128)(2,1)S(1)} %get-tuple-element.50.packed_ref), channel_id=1, source_target_pairs={{0,1},{1,0},{2,3},{3,2},{4,5},{5,4},{6,7},{7,6},{8,9},{9,8},{10,11... | collective-permute-start | bytes 2383880 | tf_op jit(solution)/shard_map/ppermute | solution.py:452
  2.4 2.6 %collective-permute-start.3 = (bf16[64,512]{1,0:T(8,128)(2,1)S(1)}, bf16[64,512]{1,0:T(8,128)(2,1)S(1)}, u32[]{:S(2)}, u32[]{:S(2)}) collective-permute-start(bf16[64,512]{1,0:T(8,128)(2,1)S(1)} %get-tuple-element.60), channel_id=1, source_target_pairs={{0,2},{2,0},{1,3},{3,1},{4,6},{6,4},{5,7},{7,5},{8,10},{10,8},{9,1... | collective-permute-start | bytes 196616 | tf_op jit(solution)/shard_map/ppermute | solution.py:452
  5.0 1.6 %collective-permute-start.1 = (bf16[32,512]{1,0:T(8,128)(2,1)S(1)}, bf16[32,512]{1,0:T(8,128)(2,1)S(1)}, u32[]{:S(2)}, u32[]{:S(2)}) collective-permute-start(bf16[32,512]{1,0:T(8,128)(2,1)S(1)} %get-tuple-element.58), channel_id=1, source_target_pairs={{0,4},{4,8},{8,12},{12,0},{1,5},{5,9},{9,13},{13,1},{2,6},{6,10},{... | collective-permute-start | bytes 98312 | tf_op jit(solution)/shard_map/ppermute | solution.py:452
  6.6 2.2 %collective-permute-start.2 = (bf16[32,512]{1,0:T(8,128)(2,1)S(1)}, bf16[32,512]{1,0:T(8,128)(2,1)S(1)}, u32[]{:S(2)}, u32[]{:S(2)}) collective-permute-start(bf16[32,512]{1,0:T(8,128)(2,1)S(1)} %get-tuple-element.59), channel_id=1, source_target_pairs={{0,12},{4,0},{8,4},{12,8},{1,13},{5,1},{9,5},{13,9},{2,14},{6,2},{... | collective-permute-start | bytes 98312 | tf_op jit(solution)/shard_map/ppermute | solution.py:452
  8.8 0.0 collective-permute-done.other_ref
  8.8 1.7 %shard_map.163 = (f32[512,512]{1,0:T(8,128)S(1)}, bf16[512,128]{1,0:T(8,128)(2,1)S(1)}, bf16[128,512]{1,0:T(8,128)(2,1)S(1)}, bf16[512,128]{1,0:T(8,128)(2,1)S(1...) custom-call(bf16[128,512]{1,0:T(8,128)(2,1)S(1)} %get-tuple-element.49.node_ref, ...), custom_call_target="tpu_custom_call" | custom-call | flops 100000000 | bytes 1000000 | tf_op jit(solution)/shard_map/pallas_call | solution.py:438
  10.5 0.3 collective-permute-done.1.rest_0_
  10.8 0.0 collective-permute-done.2.rest_1_
  10.8 0.0 collective-permute-done.3.rest_2_
  10.8 2.3 %shard_map.164 = (f32[128,512]{1,0:T(8,128)S(1)}, f32[128,256]{1,0:T(8,128)S(1)}, bf16[128,256]{1,0:T(8,128)(2,1)S(1)}, bf16[400,256]{1,0:T(8,128)(2,1)S(1)}, bf...) custom-call(bf16[128,512]{1,0:T(8,128)(2,1)S(1)} %get-tuple-element., ...), custom_call_target="tpu_custom_call" | custom-call | flops 100000000 | bytes 1000000 | tf_op jit(solution)/shard_map/pallas_call | solution.py:438
  13.1 0.6 %collective-permute-start.8 = (bf16[400,256]{1,0:T(8,128)(2,1)S(1)}, bf16[400,256]{1,0:T(8,128)(2,1)S(1)}, u32[]{:S(2)}, u32[]{:S(2)}) collective-permute-start(bf16[400,256]{1,0:T(8,128)(2,1)S(1)} %get-tuple-element.68), channel_id=1, source_target_pairs={{0,2},{2,0},{1,3},{3,1},{4,6},{6,4},{5,7},{7,5},{8,10},{10,8},{9,1... | collective-permute-start | bytes 614408 | tf_op jit(solution)/shard_map/ppermute | solution.py:457
  13.7 3.5 %collective-permute-start.4 = (bf16[80,512]{1,0:T(8,128)(2,1)S(1)}, bf16[80,512]{1,0:T(8,128)(2,1)S(1)}, u32[]{:S(2)}, u32[]{:S(2)}) collective-permute-start(bf16[80,512]{1,0:T(8,128)(2,1)S(1)} %get-tuple-element.65), channel_id=1, source_target_pairs={{0,12},{4,8},{8,4},{12,0},{1,13},{5,9},{9,5},{13,1},{2,14},{6,10},... | collective-permute-start | bytes 245768 | tf_op jit(solution)/shard_map/ppermute | solution.py:457
  17.2 1.7 %collective-permute-start.6 = (bf16[192,256]{1,0:T(8,128)(2,1)S(1)}, bf16[192,256]{1,0:T(8,128)(2,1)S(1)}, u32[]{:S(2)}, u32[]{:S(2)}) collective-permute-start(bf16[192,256]{1,0:T(8,128)(2,1)S(1)} %get-tuple-element.67), channel_id=1, source_target_pairs={{0,2},{2,0},{1,3},{3,1},{4,6},{6,4},{5,7},{7,5},{8,10},{10,8},{9,1... | collective-permute-start | bytes 294920 | tf_op jit(solution)/shard_map/ppermute | solution.py:457
  18.9 0.0 collective-permute-start.12
  18.9 0.7 %collective-permute-start.5 = (bf16[80,512]{1,0:T(8,128)(2,1)S(1)}, bf16[80,512]{1,0:T(8,128)(2,1)S(1)}, u32[]{:S(2)}, u32[]{:S(2)}) collective-permute-start(bf16[80,512]{1,0:T(8,128)(2,1)S(1)} %get-tuple-element.66), channel_id=1, source_target_pairs={{0,4},{4,0},{8,12},{12,8},{1,5},{5,1},{9,13},{13,9},{2,6},{6,2},{1... | collective-permute-start | bytes 245768 | tf_op jit(solution)/shard_map/ppermute | solution.py:457
  19.6 1.0 %collective-permute-done.8.arrived_ref = bf16[400,256]{1,0:T(8,128)(2,1)S(1)} collective-permute-done((bf16[400,256]{1,0:T(8,128)(2,1)S(1)}, bf16[400,256]{1,0:T(8,128)(2,1)S(1)}, u32[]{:S(2)}, u32[]{:S(2)}) %collective-permute-start.8) | collective-permute-done | bytes 204832 | tf_op jit(solution)/shard_map/ppermute | solution.py:457
  20.6 0.1 shard_map.166
  20.7 3.2 %collective-permute-start.9 = (bf16[144,256]{1,0:T(8,128)(2,1)S(1)}, bf16[144,256]{1,0:T(8,128)(2,1)S(1)}, u32[]{:S(2)}, u32[]{:S(2)}) collective-permute-start(bf16[144,256]{1,0:T(8,128)(2,1)S(1)} %get-tuple-element.70), channel_id=1, source_target_pairs={{0,12},{4,8},{8,4},{12,0},{1,13},{5,9},{9,5},{13,1},{2,14},{6,10},... | collective-permute-start | bytes 221192 | tf_op jit(solution)/shard_map/ppermute | solution.py:457
  23.9 0.9 %collective-permute-done.12.refs_1_ = bf16[64,512]{1,0:T(8,128)(2,1)S(1)} collective-permute-done((bf16[64,512]{1,0:T(8,128)(2,1)S(1)}, bf16[64,512]{1,0:T(8,128)(2,1)S(1)}, u32[]{:S(2)}, u32[]{:S(2)}) %collective-permute-start.12) | collective-permute-done | bytes 65568 | tf_op jit(solution)/shard_map/ppermute | solution.py:457
  24.7 0.0 collective-permute-start.10
  24.7 0.0 collective-permute-done.4.three_ref.refs_0_
  24.7 4.0 %collective-permute-start.11 = (bf16[144,256]{1,0:T(8,128)(2,1)S(1)}, bf16[144,256]{1,0:T(8,128)(2,1)S(1)}, u32[]{:S(2)}, u32[]{:S(2)}) collective-permute-start(bf16[144,256]{1,0:T(8,128)(2,1)S(1)} %get-tuple-element.72.refs_4_), channel_id=1, source_target_pairs={{0,4},{4,0},{8,12},{12,8},{1,5},{5,1},{9,13},{13,9},{2,6},{6,2},{1... | collective-permute-start | bytes 221192 | tf_op jit(solution)/shard_map/ppermute | solution.py:457
  28.8 0.0 collective-permute-done.5.one_ref.refs_2_
  28.8 1.7 %collective-permute-start.13 = (bf16[64,256]{1,0:T(8,128)(2,1)S(1)}, bf16[64,256]{1,0:T(8,128)(2,1)S(1)}, u32[]{:S(2)}, u32[]{:S(2)}) collective-permute-start(bf16[64,256]{1,0:T(8,128)(2,1)S(1)} %get-tuple-element.78), channel_id=1, source_target_pairs={{0,2},{2,0},{1,3},{3,1},{4,6},{6,4},{5,7},{7,5},{8,10},{10,8},{9,1... | collective-permute-start | bytes 98312 | tf_op jit(solution)/shard_map/ppermute | solution.py:457
  30.5 0.0 collective-permute-done.6.pair_ref.refs_4_
  30.5 0.4 shard_map.165.refs_8_.own_ref
  30.9 0.1 collective-permute-start.7
  31.0 1.8 %collective-permute-done.13.refs_7_ = bf16[64,256]{1,0:T(8,128)(2,1)S(1)} collective-permute-done((bf16[64,256]{1,0:T(8,128)(2,1)S(1)}, bf16[64,256]{1,0:T(8,128)(2,1)S(1)}, u32[]{:S(2)}, u32[]{:S(2)}) %collective-permute-start.13) | collective-permute-done | bytes 32800 | tf_op jit(solution)/shard_map/ppermute | solution.py:457
  32.8 0.0 collective-permute-done.9.refs_0_
  32.8 0.0 collective-permute-done.10.refs_1_
  32.8 0.0 collective-permute-done.11.refs_2_
  32.8 0.1 shard_map.168
  32.9 0.7 %collective-permute-start.15 = (bf16[192,256]{1,0:T(8,128)(2,1)S(1)}, bf16[192,256]{1,0:T(8,128)(2,1)S(1)}, u32[]{:S(2)}, u32[]{:S(2)}) collective-permute-start(bf16[192,256]{1,0:T(8,128)(2,1)S(1)} %get-tuple-element.82.a_ref), channel_id=1, source_target_pairs={{0,12},{4,8},{8,4},{12,0},{1,13},{5,9},{9,5},{13,1},{2,14},{6,10},... | collective-permute-start | bytes 294920 | tf_op jit(solution)/shard_map/ppermute | solution.py:457
  33.6 1.1 %collective-permute-start.14 = (bf16[192,256]{1,0:T(8,128)(2,1)S(1)}, bf16[192,256]{1,0:T(8,128)(2,1)S(1)}, u32[]{:S(2)}, u32[]{:S(2)}) collective-permute-start(bf16[192,256]{1,0:T(8,128)(2,1)S(1)} %get-tuple-element.82.a_ref), channel_id=1, source_target_pairs={{0,8},{4,12},{8,0},{12,4},{1,9},{5,13},{9,1},{13,5},{2,10},{6,14},... | collective-permute-start | bytes 294920 | tf_op jit(solution)/shard_map/ppermute | solution.py:457
  34.7 3.7 %collective-permute-start.20 = (bf16[192,256]{1,0:T(8,128)(2,1)S(1)}, bf16[192,256]{1,0:T(8,128)(2,1)S(1)}, u32[]{:S(2)}, u32[]{:S(2)}) collective-permute-start(bf16[192,256]{1,0:T(8,128)(2,1)S(1)} %get-tuple-element.82.a_ref), channel_id=1, source_target_pairs={{0,6},{2,4},{4,2},{6,0},{8,14},{10,12},{12,10},{14,8},{1,7},{3,5},... | collective-permute-start | bytes 294920 | tf_op jit(solution)/shard_map/ppermute | solution.py:463
  38.4 0.4 collective-permute-start.19
  38.8 0.0 collective-permute-done.7.other_ref
  38.8 0.2 collective-permute-start.18
  39.0 1.5 %collective-permute-done.15.b_ref = bf16[192,256]{1,0:T(8,128)(2,1)S(1)} collective-permute-done((bf16[192,256]{1,0:T(8,128)(2,1)S(1)}, bf16[192,256]{1,0:T(8,128)(2,1)S(1)}, u32[]{:S(2)}, u32[]{:S(2)}) %collective-permute-start.15) | collective-permute-done | bytes 98336 | tf_op jit(solution)/shard_map/ppermute | solution.py:457
  40.5 1.4 %collective-permute-start.17 = (bf16[192,256]{1,0:T(8,128)(2,1)S(1)}, bf16[192,256]{1,0:T(8,128)(2,1)S(1)}, u32[]{:S(2)}, u32[]{:S(2)}) collective-permute-start(bf16[192,256]{1,0:T(8,128)(2,1)S(1)} %collective-permute-done.15.b_ref), channel_id=1, source_target_pairs={{0,2},{2,0},{1,3},{3,1},{4,6},{6,4},{5,7},{7,5},{8,10},{10,8},{9,1... | collective-permute-start | bytes 294920 | tf_op jit(solution)/shard_map/ppermute | solution.py:457
  41.8 0.9 %collective-permute-done.14.a_ref = bf16[192,256]{1,0:T(8,128)(2,1)S(1)} collective-permute-done((bf16[192,256]{1,0:T(8,128)(2,1)S(1)}, bf16[192,256]{1,0:T(8,128)(2,1)S(1)}, u32[]{:S(2)}, u32[]{:S(2)}) %collective-permute-start.14) | collective-permute-done | bytes 98336 | tf_op jit(solution)/shard_map/ppermute | solution.py:457
  42.8 0.3 collective-permute-start.16
  43.1 0.8 %shard_map.169 = (f32[128,512]{1,0:T(8,128)}, bf16[128,512]{1,0:T(8,128)(2,1)}, f32[1,256]{1,0:T(1,128)}, f32[1,512]{1,0:T(1,128)}) custom-call(bf16[128,512]{1,0:T(8,128)(2,1)S(1)} %get-tuple-element.51.cot_ref, bf16[128,512]{1,0:T(8,128)(2,1)S(1)} %get-tuple-element.49.node_ref, f32[1,512]{1,0:T(1,128)S(1)} %get-tuple-element.52.gain_ref, ...), custom_call_target="tpu_custom_call" | custom-call | flops 100000000 | bytes 1000000 | tf_op jit(solution)/shard_map/pallas_call | solution.py:438
  43.9 0.0 collective-permute-done.20.d_ref
  43.9 0.7 %collective-permute-done.19.c_ref = bf16[192,256]{1,0:T(8,128)(2,1)S(1)} collective-permute-done((bf16[192,256]{1,0:T(8,128)(2,1)S(1)}, bf16[192,256]{1,0:T(8,128)(2,1)S(1)}, u32[]{:S(2)}, u32[]{:S(2)}) %collective-permute-start.19) | collective-permute-done | bytes 98336 | tf_op jit(solution)/shard_map/ppermute | solution.py:457
  44.7 0.0 collective-permute-done.18.b_ref
  44.7 0.9 %shard_map.170 = (f32[512,256]{1,0:T(8,128)}, f32[512,256]{1,0:T(8,128)}, f32[256,512]{1,0:T(8,128)}) custom-call(bf16[192,256]{1,0:T(8,128)(2,1)S(1)} %get-tuple-element.82.a_ref, bf16[192,256]{1,0:T(8,128)(2,1)S(1)} %collective-permute-done.18.b_ref, bf16[192,256]{1,0:T(8,128)(2,1)S(1)} %collective-permute-done.19.c_ref, ...), custom_call_target="tpu_custom_call" | custom-call | flops 100000000 | bytes 1000000 | tf_op jit(solution)/shard_map/pallas_call | solution.py:438
  45.6 0.2 collective-permute-done.17.d_ref
  45.8 1.6 %collective-permute-done.16.c_ref = bf16[192,256]{1,0:T(8,128)(2,1)S(1)} collective-permute-done((bf16[192,256]{1,0:T(8,128)(2,1)S(1)}, bf16[192,256]{1,0:T(8,128)(2,1)S(1)}, u32[]{:S(2)}, u32[]{:S(2)}) %collective-permute-start.16) | collective-permute-done | bytes 98336 | tf_op jit(solution)/shard_map/ppermute | solution.py:457
  47.4 0.9 %shard_map.171 = (f32[512,256]{1,0:T(8,128)}, f32[512,256]{1,0:T(8,128)}, f32[256,512]{1,0:T(8,128)}) custom-call(bf16[192,256]{1,0:T(8,128)(2,1)S(1)} %collective-permute-done.14.a_ref, bf16[192,256]{1,0:T(8,128)(2,1)S(1)} %collective-permute-done.15.b_ref, ...), custom_call_target="tpu_custom_call", output_to_operand_aliasing={{0}: (4, {}), {1}: (5, {}), {2}: (6, {})} | custom-call | flops 100000000 | bytes 1000000 | tf_op jit(solution)/shard_map/pallas_call | solution.py:438
  (1 shorter events, 0.0 us)
Async XLA Ops:
  1.9 6.9 %collective-permute-start = (bf16[1552,256]{1,0:T(8,128)(2,1)S(1)}, bf16[1552,256]{1,0:T(8,128)(2,1)S(1)}, u32[]{:S(2)}, u32[]{:S(2)}) collective-permute-start(bf16[1552,256]{1,0:T(8,128)(2,1)S(1)} %get-tuple-element.50.packed_ref), channel_id=1, source_target_pairs={{0,1},{1,0},{2,3},{3,2},{4,5},{5,4},{6,7},{7,6},{8,9},{9,8},{10,11... | collective-permute-start | bytes 2383880 | tf_op jit(solution)/shard_map/ppermute | solution.py:452
  2.4 8.4 %collective-permute-start.3 = (bf16[64,512]{1,0:T(8,128)(2,1)S(1)}, bf16[64,512]{1,0:T(8,128)(2,1)S(1)}, u32[]{:S(2)}, u32[]{:S(2)}) collective-permute-start(bf16[64,512]{1,0:T(8,128)(2,1)S(1)} %get-tuple-element.60), channel_id=1, source_target_pairs={{0,2},{2,0},{1,3},{3,1},{4,6},{6,4},{5,7},{7,5},{8,10},{10,8},{9,1... | collective-permute-start | bytes 196616 | tf_op jit(solution)/shard_map/ppermute | solution.py:452
  5.0 5.8 %collective-permute-start.1 = (bf16[32,512]{1,0:T(8,128)(2,1)S(1)}, bf16[32,512]{1,0:T(8,128)(2,1)S(1)}, u32[]{:S(2)}, u32[]{:S(2)}) collective-permute-start(bf16[32,512]{1,0:T(8,128)(2,1)S(1)} %get-tuple-element.58), channel_id=1, source_target_pairs={{0,4},{4,8},{8,12},{12,0},{1,5},{5,9},{9,13},{13,1},{2,6},{6,10},{... | collective-permute-start | bytes 98312 | tf_op jit(solution)/shard_map/ppermute | solution.py:452
  6.6 4.3 %collective-permute-start.2 = (bf16[32,512]{1,0:T(8,128)(2,1)S(1)}, bf16[32,512]{1,0:T(8,128)(2,1)S(1)}, u32[]{:S(2)}, u32[]{:S(2)}) collective-permute-start(bf16[32,512]{1,0:T(8,128)(2,1)S(1)} %get-tuple-element.59), channel_id=1, source_target_pairs={{0,12},{4,0},{8,4},{12,8},{1,13},{5,1},{9,5},{13,9},{2,14},{6,2},{... | collective-permute-start | bytes 98312 | tf_op jit(solution)/shard_map/ppermute | solution.py:452
  13.1 7.5 %collective-permute-start.8 = (bf16[400,256]{1,0:T(8,128)(2,1)S(1)}, bf16[400,256]{1,0:T(8,128)(2,1)S(1)}, u32[]{:S(2)}, u32[]{:S(2)}) collective-permute-start(bf16[400,256]{1,0:T(8,128)(2,1)S(1)} %get-tuple-element.68), channel_id=1, source_target_pairs={{0,2},{2,0},{1,3},{3,1},{4,6},{6,4},{5,7},{7,5},{8,10},{10,8},{9,1... | collective-permute-start | bytes 614408 | tf_op jit(solution)/shard_map/ppermute | solution.py:457
  13.7 11.0 %collective-permute-start.4 = (bf16[80,512]{1,0:T(8,128)(2,1)S(1)}, bf16[80,512]{1,0:T(8,128)(2,1)S(1)}, u32[]{:S(2)}, u32[]{:S(2)}) collective-permute-start(bf16[80,512]{1,0:T(8,128)(2,1)S(1)} %get-tuple-element.65), channel_id=1, source_target_pairs={{0,12},{4,8},{8,4},{12,0},{1,13},{5,9},{9,5},{13,1},{2,14},{6,10},... | collective-permute-start | bytes 245768 | tf_op jit(solution)/shard_map/ppermute | solution.py:457
  17.2 13.3 %collective-permute-start.6 = (bf16[192,256]{1,0:T(8,128)(2,1)S(1)}, bf16[192,256]{1,0:T(8,128)(2,1)S(1)}, u32[]{:S(2)}, u32[]{:S(2)}) collective-permute-start(bf16[192,256]{1,0:T(8,128)(2,1)S(1)} %get-tuple-element.67), channel_id=1, source_target_pairs={{0,2},{2,0},{1,3},{3,1},{4,6},{6,4},{5,7},{7,5},{8,10},{10,8},{9,1... | collective-permute-start | bytes 294920 | tf_op jit(solution)/shard_map/ppermute | solution.py:457
  18.9 5.8 %collective-permute-start.12 = (bf16[64,512]{1,0:T(8,128)(2,1)S(1)}, bf16[64,512]{1,0:T(8,128)(2,1)S(1)}, u32[]{:S(2)}, u32[]{:S(2)}) collective-permute-start(bf16[64,512]{1,0:T(8,128)(2,1)S(1)} %get-tuple-element.75), channel_id=1, source_target_pairs={{0,8},{4,12},{8,0},{12,4},{1,9},{5,13},{9,1},{13,5},{2,10},{6,14},... | collective-permute-start | bytes 196616 | tf_op jit(solution)/shard_map/ppermute | solution.py:457
  18.9 9.8 %collective-permute-start.5 = (bf16[80,512]{1,0:T(8,128)(2,1)S(1)}, bf16[80,512]{1,0:T(8,128)(2,1)S(1)}, u32[]{:S(2)}, u32[]{:S(2)}) collective-permute-start(bf16[80,512]{1,0:T(8,128)(2,1)S(1)} %get-tuple-element.66), channel_id=1, source_target_pairs={{0,4},{4,0},{8,12},{12,8},{1,5},{5,1},{9,13},{13,9},{2,6},{6,2},{1... | collective-permute-start | bytes 245768 | tf_op jit(solution)/shard_map/ppermute | solution.py:457
  20.7 12.1 %collective-permute-start.9 = (bf16[144,256]{1,0:T(8,128)(2,1)S(1)}, bf16[144,256]{1,0:T(8,128)(2,1)S(1)}, u32[]{:S(2)}, u32[]{:S(2)}) collective-permute-start(bf16[144,256]{1,0:T(8,128)(2,1)S(1)} %get-tuple-element.70), channel_id=1, source_target_pairs={{0,12},{4,8},{8,4},{12,0},{1,13},{5,9},{9,5},{13,1},{2,14},{6,10},... | collective-permute-start | bytes 221192 | tf_op jit(solution)/shard_map/ppermute | solution.py:457
  24.7 8.1 %collective-permute-start.10 = (bf16[144,256]{1,0:T(8,128)(2,1)S(1)}, bf16[144,256]{1,0:T(8,128)(2,1)S(1)}, u32[]{:S(2)}, u32[]{:S(2)}) collective-permute-start(bf16[144,256]{1,0:T(8,128)(2,1)S(1)} %get-tuple-element.71), channel_id=1, source_target_pairs={{0,8},{4,12},{8,0},{12,4},{1,9},{5,13},{9,1},{13,5},{2,10},{6,14},... | collective-permute-start | bytes 221192 | tf_op jit(solution)/shard_map/ppermute | solution.py:457
  24.7 8.1 %collective-permute-start.11 = (bf16[144,256]{1,0:T(8,128)(2,1)S(1)}, bf16[144,256]{1,0:T(8,128)(2,1)S(1)}, u32[]{:S(2)}, u32[]{:S(2)}) collective-permute-start(bf16[144,256]{1,0:T(8,128)(2,1)S(1)} %get-tuple-element.72.refs_4_), channel_id=1, source_target_pairs={{0,4},{4,0},{8,12},{12,8},{1,5},{5,1},{9,13},{13,9},{2,6},{6,2},{1... | collective-permute-start | bytes 221192 | tf_op jit(solution)/shard_map/ppermute | solution.py:457
  28.8 4.0 %collective-permute-start.13 = (bf16[64,256]{1,0:T(8,128)(2,1)S(1)}, bf16[64,256]{1,0:T(8,128)(2,1)S(1)}, u32[]{:S(2)}, u32[]{:S(2)}) collective-permute-start(bf16[64,256]{1,0:T(8,128)(2,1)S(1)} %get-tuple-element.78), channel_id=1, source_target_pairs={{0,2},{2,0},{1,3},{3,1},{4,6},{6,4},{5,7},{7,5},{8,10},{10,8},{9,1... | collective-permute-start | bytes 98312 | tf_op jit(solution)/shard_map/ppermute | solution.py:457
  30.9 7.9 %collective-permute-start.7 = (bf16[128,512]{1,0:T(8,128)(2,1)S(1)}, bf16[128,512]{1,0:T(8,128)(2,1)S(1)}, u32[]{:S(2)}, u32[]{:S(2)}) collective-permute-start(bf16[128,512]{1,0:T(8,128)(2,1)S(1)} %shard_map.165.refs_8_.own_ref), channel_id=1, source_target_pairs={{0,1},{1,0},{2,3},{3,2},{4,5},{5,4},{6,7},{7,6},{8,9},{9,8},{10,11... | collective-permute-start | bytes 393224 | tf_op jit(solution)/shard_map/ppermute | solution.py:452
  32.9 7.6 %collective-permute-start.15 = (bf16[192,256]{1,0:T(8,128)(2,1)S(1)}, bf16[192,256]{1,0:T(8,128)(2,1)S(1)}, u32[]{:S(2)}, u32[]{:S(2)}) collective-permute-start(bf16[192,256]{1,0:T(8,128)(2,1)S(1)} %get-tuple-element.82.a_ref), channel_id=1, source_target_pairs={{0,12},{4,8},{8,4},{12,0},{1,13},{5,9},{9,5},{13,1},{2,14},{6,10},... | collective-permute-start | bytes 294920 | tf_op jit(solution)/shard_map/ppermute | solution.py:457
  33.6 9.2 %collective-permute-start.14 = (bf16[192,256]{1,0:T(8,128)(2,1)S(1)}, bf16[192,256]{1,0:T(8,128)(2,1)S(1)}, u32[]{:S(2)}, u32[]{:S(2)}) collective-permute-start(bf16[192,256]{1,0:T(8,128)(2,1)S(1)} %get-tuple-element.82.a_ref), channel_id=1, source_target_pairs={{0,8},{4,12},{8,0},{12,4},{1,9},{5,13},{9,1},{13,5},{2,10},{6,14},... | collective-permute-start | bytes 294920 | tf_op jit(solution)/shard_map/ppermute | solution.py:457
  34.7 9.2 %collective-permute-start.20 = (bf16[192,256]{1,0:T(8,128)(2,1)S(1)}, bf16[192,256]{1,0:T(8,128)(2,1)S(1)}, u32[]{:S(2)}, u32[]{:S(2)}) collective-permute-start(bf16[192,256]{1,0:T(8,128)(2,1)S(1)} %get-tuple-element.82.a_ref), channel_id=1, source_target_pairs={{0,6},{2,4},{4,2},{6,0},{8,14},{10,12},{12,10},{14,8},{1,7},{3,5},... | collective-permute-start | bytes 294920 | tf_op jit(solution)/shard_map/ppermute | solution.py:463
  38.4 6.3 %collective-permute-start.19 = (bf16[192,256]{1,0:T(8,128)(2,1)S(1)}, bf16[192,256]{1,0:T(8,128)(2,1)S(1)}, u32[]{:S(2)}, u32[]{:S(2)}) collective-permute-start(bf16[192,256]{1,0:T(8,128)(2,1)S(1)} %get-tuple-element.82.a_ref), channel_id=1, source_target_pairs={{0,2},{2,0},{1,3},{3,1},{4,6},{6,4},{5,7},{7,5},{8,10},{10,8},{9,1... | collective-permute-start | bytes 294920 | tf_op jit(solution)/shard_map/ppermute | solution.py:457
  38.8 5.9 %collective-permute-start.18 = (bf16[192,256]{1,0:T(8,128)(2,1)S(1)}, bf16[192,256]{1,0:T(8,128)(2,1)S(1)}, u32[]{:S(2)}, u32[]{:S(2)}) collective-permute-start(bf16[192,256]{1,0:T(8,128)(2,1)S(1)} %get-tuple-element.82.a_ref), channel_id=1, source_target_pairs={{0,4},{4,0},{8,12},{12,8},{1,5},{5,1},{9,13},{13,9},{2,6},{6,2},{1... | collective-permute-start | bytes 294920 | tf_op jit(solution)/shard_map/ppermute | solution.py:457
  40.5 5.4 %collective-permute-start.17 = (bf16[192,256]{1,0:T(8,128)(2,1)S(1)}, bf16[192,256]{1,0:T(8,128)(2,1)S(1)}, u32[]{:S(2)}, u32[]{:S(2)}) collective-permute-start(bf16[192,256]{1,0:T(8,128)(2,1)S(1)} %collective-permute-done.15.b_ref), channel_id=1, source_target_pairs={{0,2},{2,0},{1,3},{3,1},{4,6},{6,4},{5,7},{7,5},{8,10},{10,8},{9,1... | collective-permute-start | bytes 294920 | tf_op jit(solution)/shard_map/ppermute | solution.py:457
  42.8 4.6 %collective-permute-start.16 = (bf16[192,256]{1,0:T(8,128)(2,1)S(1)}, bf16[192,256]{1,0:T(8,128)(2,1)S(1)}, u32[]{:S(2)}, u32[]{:S(2)}) collective-permute-start(bf16[192,256]{1,0:T(8,128)(2,1)S(1)} %collective-permute-done.14.a_ref), channel_id=1, source_target_pairs={{0,2},{2,0},{1,3},{3,1},{4,6},{6,4},{5,7},{7,5},{8,10},{10,8},{9,1... | collective-permute-start | bytes 294920 | tf_op jit(solution)/shard_map/ppermute | solution.py:457

commit v16 on v15

--- a/solution.py
+++ b/solution.py
@@ -299,24 +299,24 @@
 
 
 def line_kernel(*refs):
-    *terms, _, send_ref, keep_ref = refs
-    rows, hid = send_ref.shape
+    *terms, zero_ref, send_ref, keep_ref = refs
+    rows, hid = keep_ref.shape
     total = tree([r[0:rows, :].astype(f32) for r in terms])
     first = lax.axis_index("sub") == 0
     left, right = total[:, :hid], total[:, hid:]
-    send_ref[...] = jnp.where(first, right, left).astype(bf16)
+    send_ref[0:rows, :] = jnp.where(first, right, left).astype(bf16)
+    send_ref[rows:, :] = zero_ref[...]
     keep_ref[...] = jnp.where(first, left, right).astype(bf16)
 
 
 def own_kernel(*refs):
-    *terms, keep_ref, arrived_ref, vectors_ref, out_keep_ref, out_arrived_ref, _, own_ref, tail_ref = refs
+    *terms, keep_ref, vectors_ref, out_keep_ref, arrived_ref, own_ref, tail_ref = refs
     strip = keep_ref.shape[0]
-    zero = (keep_ref[...].astype(f32) + arrived_ref[0:strip, :].astype(f32)).astype(bf16)
+    narrow = out_keep_ref.shape[0]
+    zero = (keep_ref[...].astype(f32) + arrived_ref[narrow : narrow + strip, :].astype(f32)).astype(bf16)
     total = tree([r[0:strip, :].astype(f32) for r in terms] + [zero.astype(f32)])
     own_ref[0:strip, :] = total.astype(bf16)
-    own_ref[strip:, :] = (
-        out_keep_ref[...].astype(f32) + out_arrived_ref[...].astype(f32)
-    ).astype(bf16)
+    own_ref[strip:, :] = (out_keep_ref[...].astype(f32) + arrived_ref[0:narrow, :].astype(f32)).astype(bf16)
     tail_ref[...] = tree([r[strip:, :].astype(f32) for r in terms] + [vectors_ref[...].astype(f32)])
 
 
@@ -469,7 +469,6 @@
     block = shape((strip + TAIL, hid), bf16)
     far = across(sends[0], "sub", 1)
     out_terms = {k: across(outs[k], "mesh", k) for k in order}
-    zero = across(sends[1], "sub", 1)
     line = {}
     line[3], line[2], line[1], tail = call(
         far_kernel, [block] * 3 + [shape((TAIL, hid), bf16)], far, keeps[0]
@@ -477,15 +476,15 @@
     line_terms = {k: across(line[k], "mesh", k) for k in order}
     out_send, out_keep = call(
         line_kernel,
-        [shape((narrow, hid), bf16)] * 2,
-        *[out_terms[k] for k in order], outs[0], line[1],
-    )
-    node_part = node_terms(out_terms[3], out_terms[1], zero)
+        [shape((narrow + sends[1].shape[0], hid), bf16), shape((narrow, hid), bf16)],
+        *[out_terms[k] for k in order], outs[0], sends[1], flops=10**8,
+    )
+    near = across(out_send, "sub", 1)
+    node_part = node_terms(out_terms[3], out_terms[1], near)
     own, tail = call(
         own_kernel,
         [shape((strip + narrow, hid), bf16), shape((TAIL, hid), f32)],
-        *[line_terms[k] for k in order], keeps[1], zero, tail, out_keep, across(out_send, "sub", 1),
-        node_part,
+        *[line_terms[k] for k in order], keeps[1], tail, out_keep, near, flops=10**8,
     )
     mine = {k: across(own, "mesh", k) for k in order}
     mine[0] = own

time: 48.5 us -> 47.9 us (0.988)
  starting transfers between devices: 30.1 us -> 25.5 us
  waiting for transfers between devices: 9.01 us -> 13.1 us
    ppermute x15 -> x14, waiting for transfers between devices: 8.67 us -> 12.7 us  [across(): return lax.ppermute(x, axis, [(i, i ^ k) for i in range(count)])]
    ppermute x15 -> x14, starting transfers between devices: 19.5 us -> 16.4 us  [across(): return lax.ppermute(x, axis, [(i, i ^ k) for i in range(count)])]
    ppermute x1, starting transfers between devices: 3.69 us -> 2.13 us  [diagonal(): return lax.ppermute(x, ('mesh', 'sub'), moves)]
  transfers between devices with their start and end apart: 21 -> 20, of which waited for: 9 -> 8; matrix products, arithmetic and copies ran while one was open for 0% -> 0% of each run, Pallas kernels for 8% -> 8%
where the time goes in v16:
time: 47.9 us; the launch traced here: 47.7 us
  starting transfers between devices  25.5 us (53%)
  waiting for transfers between devices  13.1 us (27%)
  Pallas kernels  8.45 us (18%)
  between operations  0.72 us (2%)
    ppermute x14, starting transfers between devices, across(): return lax.ppermute(x, axis, [(i, i ^ k) for i in range(count)])  16.4 us
    ppermute x14, waiting for transfers between devices, across(): return lax.ppermute(x, axis, [(i, i ^ k) for i in range(count)])  12.7 us
    pallas_call x10, Pallas kernels, call(): pl.pallas_call(kernel, out_shape=outs, in_specs=specs or [VMEM] * len(arg...  8.45 us
    ppermute x5, starting transfers between devices, shifted(): return lax.ppermute(x, axis, [(i, (i + by) % count) for i in range(count)])  6.98 us
    ppermute x1, starting transfers between devices, diagonal(): return lax.ppermute(x, ('mesh', 'sub'), moves)  2.13 us
  transfers between devices with their start and end apart: 20, of which 8 were waited for; matrix products, arithmetic and copies ran while one was open for 0% of the time, Pallas kernels for 8%

profile of v16, /device:TPU:0, one launch (start us, length us, event | category | flops | bytes accessed | tf_op | source)
XLA Modules:
  0.0 47.7 jit_solution(8712695672375090213)
XLA Ops:
  0.6 1.3 %shard_map.162 = (bf16[128,512]{1,0:T(8,128)(2,1)S(1)}, s32[1,4,32]{2,1,0:T(4,128)S(1)}, bf16[1552,256]{1,0:T(8,128)(2,1)S(1)}, bf16[32,512]{1,0:T(8,128)(2,1)S(...) custom-call(bf16[128,512]{1,0:T(8,128)(2,1)} %node_hbm.1, s32[1,4,32]{2,1,0:T(4,128)} %send_hbm.1, ...), custom_call_target="tpu_custom_call" | custom-call | flops 100000000 | bytes 1000000 | tf_op jit(solution)/shard_map/pallas_call | solution.py:438
  1.9 0.5 %collective-permute-start = (bf16[1552,256]{1,0:T(8,128)(2,1)S(1)}, bf16[1552,256]{1,0:T(8,128)(2,1)S(1)}, u32[]{:S(2)}, u32[]{:S(2)}) collective-permute-start(bf16[1552,256]{1,0:T(8,128)(2,1)S(1)} %get-tuple-element.50.packed_ref), channel_id=1, source_target_pairs={{0,1},{1,0},{2,3},{3,2},{4,5},{5,4},{6,7},{7,6},{8,9},{9,8},{10,11... | collective-permute-start | bytes 2383880 | tf_op jit(solution)/shard_map/ppermute | solution.py:452
  2.4 2.6 %collective-permute-start.3 = (bf16[64,512]{1,0:T(8,128)(2,1)S(1)}, bf16[64,512]{1,0:T(8,128)(2,1)S(1)}, u32[]{:S(2)}, u32[]{:S(2)}) collective-permute-start(bf16[64,512]{1,0:T(8,128)(2,1)S(1)} %get-tuple-element.60), channel_id=1, source_target_pairs={{0,2},{2,0},{1,3},{3,1},{4,6},{6,4},{5,7},{7,5},{8,10},{10,8},{9,1... | collective-permute-start | bytes 196616 | tf_op jit(solution)/shard_map/ppermute | solution.py:452
  5.0 1.6 %collective-permute-start.1 = (bf16[32,512]{1,0:T(8,128)(2,1)S(1)}, bf16[32,512]{1,0:T(8,128)(2,1)S(1)}, u32[]{:S(2)}, u32[]{:S(2)}) collective-permute-start(bf16[32,512]{1,0:T(8,128)(2,1)S(1)} %get-tuple-element.58), channel_id=1, source_target_pairs={{0,4},{4,8},{8,12},{12,0},{1,5},{5,9},{9,13},{13,1},{2,6},{6,10},{... | collective-permute-start | bytes 98312 | tf_op jit(solution)/shard_map/ppermute | solution.py:452
  6.6 2.2 %collective-permute-start.2 = (bf16[32,512]{1,0:T(8,128)(2,1)S(1)}, bf16[32,512]{1,0:T(8,128)(2,1)S(1)}, u32[]{:S(2)}, u32[]{:S(2)}) collective-permute-start(bf16[32,512]{1,0:T(8,128)(2,1)S(1)} %get-tuple-element.59), channel_id=1, source_target_pairs={{0,12},{4,0},{8,4},{12,8},{1,13},{5,1},{9,5},{13,9},{2,14},{6,2},{... | collective-permute-start | bytes 98312 | tf_op jit(solution)/shard_map/ppermute | solution.py:452
  8.8 0.0 collective-permute-done.other_ref
  8.8 1.7 %shard_map.163 = (f32[512,512]{1,0:T(8,128)S(1)}, bf16[512,128]{1,0:T(8,128)(2,1)S(1)}, bf16[128,512]{1,0:T(8,128)(2,1)S(1)}, bf16[512,128]{1,0:T(8,128)(2,1)S(1...) custom-call(bf16[128,512]{1,0:T(8,128)(2,1)S(1)} %get-tuple-element.49.node_ref, ...), custom_call_target="tpu_custom_call" | custom-call | flops 100000000 | bytes 1000000 | tf_op jit(solution)/shard_map/pallas_call | solution.py:438
  10.5 0.3 collective-permute-done.1.rest_0_
  10.8 0.0 collective-permute-done.2.rest_1_
  10.8 0.0 collective-permute-done.3.rest_2_
  10.8 2.3 %shard_map.164 = (f32[128,512]{1,0:T(8,128)S(1)}, f32[128,256]{1,0:T(8,128)S(1)}, bf16[128,256]{1,0:T(8,128)(2,1)S(1)}, bf16[400,256]{1,0:T(8,128)(2,1)S(1)}, bf...) custom-call(bf16[128,512]{1,0:T(8,128)(2,1)S(1)} %get-tuple-element., ...), custom_call_target="tpu_custom_call" | custom-call | flops 100000000 | bytes 1000000 | tf_op jit(solution)/shard_map/pallas_call | solution.py:438
  13.1 0.6 %collective-permute-start.9 = (bf16[400,256]{1,0:T(8,128)(2,1)S(1)}, bf16[400,256]{1,0:T(8,128)(2,1)S(1)}, u32[]{:S(2)}, u32[]{:S(2)}) collective-permute-start(bf16[400,256]{1,0:T(8,128)(2,1)S(1)} %get-tuple-element.71), channel_id=1, source_target_pairs={{0,2},{2,0},{1,3},{3,1},{4,6},{6,4},{5,7},{7,5},{8,10},{10,8},{9,1... | collective-permute-start | bytes 614408 | tf_op jit(solution)/shard_map/ppermute | solution.py:457
  13.7 3.5 %collective-permute-start.4 = (bf16[80,512]{1,0:T(8,128)(2,1)S(1)}, bf16[80,512]{1,0:T(8,128)(2,1)S(1)}, u32[]{:S(2)}, u32[]{:S(2)}) collective-permute-start(bf16[80,512]{1,0:T(8,128)(2,1)S(1)} %get-tuple-element.65), channel_id=1, source_target_pairs={{0,12},{4,8},{8,4},{12,0},{1,13},{5,9},{9,5},{13,1},{2,14},{6,10},... | collective-permute-start | bytes 245768 | tf_op jit(solution)/shard_map/ppermute | solution.py:457
  17.2 0.0 collective-permute-start.5
  17.2 0.9 %collective-permute-start.6 = (bf16[64,512]{1,0:T(8,128)(2,1)S(1)}, bf16[64,512]{1,0:T(8,128)(2,1)S(1)}, u32[]{:S(2)}, u32[]{:S(2)}) collective-permute-start(bf16[64,512]{1,0:T(8,128)(2,1)S(1)} %get-tuple-element.67), channel_id=1, source_target_pairs={{0,8},{4,12},{8,0},{12,4},{1,9},{5,13},{9,1},{13,5},{2,10},{6,14},... | collective-permute-start | bytes 196616 | tf_op jit(solution)/shard_map/ppermute | solution.py:457
  18.1 4.3 %collective-permute-done.6.refs_1_ = bf16[64,512]{1,0:T(8,128)(2,1)S(1)} collective-permute-done((bf16[64,512]{1,0:T(8,128)(2,1)S(1)}, bf16[64,512]{1,0:T(8,128)(2,1)S(1)}, u32[]{:S(2)}, u32[]{:S(2)}) %collective-permute-start.6) | collective-permute-done | bytes 65568 | tf_op jit(solution)/shard_map/ppermute | solution.py:457
  22.4 0.0 collective-permute-done.4.refs_0_.three_ref
  22.5 0.0 collective-permute-done.5.refs_2_.one_ref
  22.5 1.7 %collective-permute-start.7 = (bf16[256,256]{1,0:T(8,128)(2,1)S(1)}, bf16[256,256]{1,0:T(8,128)(2,1)S(1)}, u32[]{:S(2)}, u32[]{:S(2)}) collective-permute-start(bf16[256,256]{1,0:T(8,128)(2,1)S(1)} %get-tuple-element.70), channel_id=1, source_target_pairs={{0,2},{2,0},{1,3},{3,1},{4,6},{6,4},{5,7},{7,5},{8,10},{10,8},{9,1... | collective-permute-start | bytes 393224 | tf_op jit(solution)/shard_map/ppermute | solution.py:457
  24.2 0.0 collective-permute-done.9.arrived_ref
  24.2 0.1 shard_map.167
  24.3 3.3 %collective-permute-start.10 = (bf16[144,256]{1,0:T(8,128)(2,1)S(1)}, bf16[144,256]{1,0:T(8,128)(2,1)S(1)}, u32[]{:S(2)}, u32[]{:S(2)}) collective-permute-start(bf16[144,256]{1,0:T(8,128)(2,1)S(1)} %get-tuple-element.73), channel_id=1, source_target_pairs={{0,12},{4,8},{8,4},{12,0},{1,13},{5,9},{9,5},{13,1},{2,14},{6,10},... | collective-permute-start | bytes 221192 | tf_op jit(solution)/shard_map/ppermute | solution.py:457
  27.5 0.3 collective-permute-start.11
  27.8 0.9 %collective-permute-start.12 = (bf16[144,256]{1,0:T(8,128)(2,1)S(1)}, bf16[144,256]{1,0:T(8,128)(2,1)S(1)}, u32[]{:S(2)}, u32[]{:S(2)}) collective-permute-start(bf16[144,256]{1,0:T(8,128)(2,1)S(1)} %get-tuple-element.75), channel_id=1, source_target_pairs={{0,4},{4,0},{8,12},{12,8},{1,5},{5,1},{9,13},{13,9},{2,6},{6,2},{1... | collective-permute-start | bytes 221192 | tf_op jit(solution)/shard_map/ppermute | solution.py:457
  28.7 0.0 collective-permute-done.7.pair_ref.refs_6_
  28.7 0.4 shard_map.166.own_ref
  29.1 0.1 collective-permute-start.8
  29.2 1.9 %collective-permute-done.10.refs_0_ = bf16[144,256]{1,0:T(8,128)(2,1)S(1)} collective-permute-done((bf16[144,256]{1,0:T(8,128)(2,1)S(1)}, bf16[144,256]{1,0:T(8,128)(2,1)S(1)}, u32[]{:S(2)}, u32[]{:S(2)}) %collective-permute-start.10) | collective-permute-done | bytes 73760 | tf_op jit(solution)/shard_map/ppermute | solution.py:457
  31.1 1.9 %collective-permute-done.11.refs_1_ = bf16[144,256]{1,0:T(8,128)(2,1)S(1)} collective-permute-done((bf16[144,256]{1,0:T(8,128)(2,1)S(1)}, bf16[144,256]{1,0:T(8,128)(2,1)S(1)}, u32[]{:S(2)}, u32[]{:S(2)}) %collective-permute-start.11) | collective-permute-done | bytes 73760 | tf_op jit(solution)/shard_map/ppermute | solution.py:457
  33.0 0.0 collective-permute-done.12.refs_2_
  33.0 0.1 shard_map.168
  33.1 2.1 %collective-permute-start.14 = (bf16[192,256]{1,0:T(8,128)(2,1)S(1)}, bf16[192,256]{1,0:T(8,128)(2,1)S(1)}, u32[]{:S(2)}, u32[]{:S(2)}) collective-permute-start(bf16[192,256]{1,0:T(8,128)(2,1)S(1)} %get-tuple-element.82.a_ref), channel_id=1, source_target_pairs={{0,12},{4,8},{8,4},{12,0},{1,13},{5,9},{9,5},{13,1},{2,14},{6,10},... | collective-permute-start | bytes 294920 | tf_op jit(solution)/shard_map/ppermute | solution.py:457
  35.1 0.0 collective-permute-start.13
  35.1 2.1 %collective-permute-start.19 = (bf16[192,256]{1,0:T(8,128)(2,1)S(1)}, bf16[192,256]{1,0:T(8,128)(2,1)S(1)}, u32[]{:S(2)}, u32[]{:S(2)}) collective-permute-start(bf16[192,256]{1,0:T(8,128)(2,1)S(1)} %get-tuple-element.82.a_ref), channel_id=1, source_target_pairs={{0,6},{2,4},{4,2},{6,0},{8,14},{10,12},{12,10},{14,8},{1,7},{3,5},... | collective-permute-start | bytes 294920 | tf_op jit(solution)/shard_map/ppermute | solution.py:463
  37.3 1.7 %collective-permute-start.18 = (bf16[192,256]{1,0:T(8,128)(2,1)S(1)}, bf16[192,256]{1,0:T(8,128)(2,1)S(1)}, u32[]{:S(2)}, u32[]{:S(2)}) collective-permute-start(bf16[192,256]{1,0:T(8,128)(2,1)S(1)} %get-tuple-element.82.a_ref), channel_id=1, source_target_pairs={{0,2},{2,0},{1,3},{3,1},{4,6},{6,4},{5,7},{7,5},{8,10},{10,8},{9,1... | collective-permute-start | bytes 294920 | tf_op jit(solution)/shard_map/ppermute | solution.py:457
  39.0 0.0 collective-permute-done.8.other_ref
  39.0 0.0 collective-permute-start.17
  39.0 1.5 %collective-permute-done.14.b_ref = bf16[192,256]{1,0:T(8,128)(2,1)S(1)} collective-permute-done((bf16[192,256]{1,0:T(8,128)(2,1)S(1)}, bf16[192,256]{1,0:T(8,128)(2,1)S(1)}, u32[]{:S(2)}, u32[]{:S(2)}) %collective-permute-start.14) | collective-permute-done | bytes 98336 | tf_op jit(solution)/shard_map/ppermute | solution.py:457
  40.5 0.4 collective-permute-start.16
  40.8 1.3 %collective-permute-done.13.a_ref = bf16[192,256]{1,0:T(8,128)(2,1)S(1)} collective-permute-done((bf16[192,256]{1,0:T(8,128)(2,1)S(1)}, bf16[192,256]{1,0:T(8,128)(2,1)S(1)}, u32[]{:S(2)}, u32[]{:S(2)}) %collective-permute-start.13) | collective-permute-done | bytes 98336 | tf_op jit(solution)/shard_map/ppermute | solution.py:457
  42.1 1.0 %collective-permute-start.15 = (bf16[192,256]{1,0:T(8,128)(2,1)S(1)}, bf16[192,256]{1,0:T(8,128)(2,1)S(1)}, u32[]{:S(2)}, u32[]{:S(2)}) collective-permute-start(bf16[192,256]{1,0:T(8,128)(2,1)S(1)} %collective-permute-done.13.a_ref), channel_id=1, source_target_pairs={{0,2},{2,0},{1,3},{3,1},{4,6},{6,4},{5,7},{7,5},{8,10},{10,8},{9,1... | collective-permute-start | bytes 294920 | tf_op jit(solution)/shard_map/ppermute | solution.py:457
  43.2 0.8 %shard_map.169 = (f32[128,512]{1,0:T(8,128)}, bf16[128,512]{1,0:T(8,128)(2,1)}, f32[1,256]{1,0:T(1,128)}, f32[1,512]{1,0:T(1,128)}) custom-call(bf16[128,512]{1,0:T(8,128)(2,1)S(1)} %get-tuple-element.51.cot_ref, bf16[128,512]{1,0:T(8,128)(2,1)S(1)} %get-tuple-element.49.node_ref, f32[1,512]{1,0:T(1,128)S(1)} %get-tuple-element.52.gain_ref, ...), custom_call_target="tpu_custom_call" | custom-call | flops 100000000 | bytes 1000000 | tf_op jit(solution)/shard_map/pallas_call | solution.py:438
  44.0 0.0 collective-permute-done.19.d_ref
  44.0 0.0 collective-permute-done.18.c_ref
  44.0 0.0 collective-permute-done.17.b_ref
  44.0 0.9 %shard_map.170 = (f32[512,256]{1,0:T(8,128)}, f32[512,256]{1,0:T(8,128)}, f32[256,512]{1,0:T(8,128)}) custom-call(bf16[192,256]{1,0:T(8,128)(2,1)S(1)} %get-tuple-element.82.a_ref, bf16[192,256]{1,0:T(8,128)(2,1)S(1)} %collective-permute-done.17.b_ref, bf16[192,256]{1,0:T(8,128)(2,1)S(1)} %collective-permute-done.18.c_ref, ...), custom_call_target="tpu_custom_call" | custom-call | flops 100000000 | bytes 1000000 | tf_op jit(solution)/shard_map/pallas_call | solution.py:438
  45.0 0.1 collective-permute-done.16.d_ref
  45.1 1.7 %collective-permute-done.15.c_ref = bf16[192,256]{1,0:T(8,128)(2,1)S(1)} collective-permute-done((bf16[192,256]{1,0:T(8,128)(2,1)S(1)}, bf16[192,256]{1,0:T(8,128)(2,1)S(1)}, u32[]{:S(2)}, u32[]{:S(2)}) %collective-permute-start.15) | collective-permute-done | bytes 98336 | tf_op jit(solution)/shard_map/ppermute | solution.py:457
  46.8 0.9 %shard_map.171 = (f32[512,256]{1,0:T(8,128)}, f32[512,256]{1,0:T(8,128)}, f32[256,512]{1,0:T(8,128)}) custom-call(bf16[192,256]{1,0:T(8,128)(2,1)S(1)} %collective-permute-done.13.a_ref, bf16[192,256]{1,0:T(8,128)(2,1)S(1)} %collective-permute-done.14.b_ref, ...), custom_call_target="tpu_custom_call", output_to_operand_aliasing={{0}: (4, {}), {1}: (5, {}), {2}: (6, {})} | custom-call | flops 100000000 | bytes 1000000 | tf_op jit(solution)/shard_map/pallas_call | solution.py:438
  (1 shorter events, 0.0 us)
Async XLA Ops:
  1.9 6.9 %collective-permute-start = (bf16[1552,256]{1,0:T(8,128)(2,1)S(1)}, bf16[1552,256]{1,0:T(8,128)(2,1)S(1)}, u32[]{:S(2)}, u32[]{:S(2)}) collective-permute-start(bf16[1552,256]{1,0:T(8,128)(2,1)S(1)} %get-tuple-element.50.packed_ref), channel_id=1, source_target_pairs={{0,1},{1,0},{2,3},{3,2},{4,5},{5,4},{6,7},{7,6},{8,9},{9,8},{10,11... | collective-permute-start | bytes 2383880 | tf_op jit(solution)/shard_map/ppermute | solution.py:452
  2.4 8.4 %collective-permute-start.3 = (bf16[64,512]{1,0:T(8,128)(2,1)S(1)}, bf16[64,512]{1,0:T(8,128)(2,1)S(1)}, u32[]{:S(2)}, u32[]{:S(2)}) collective-permute-start(bf16[64,512]{1,0:T(8,128)(2,1)S(1)} %get-tuple-element.60), channel_id=1, source_target_pairs={{0,2},{2,0},{1,3},{3,1},{4,6},{6,4},{5,7},{7,5},{8,10},{10,8},{9,1... | collective-permute-start | bytes 196616 | tf_op jit(solution)/shard_map/ppermute | solution.py:452
  5.0 5.8 %collective-permute-start.1 = (bf16[32,512]{1,0:T(8,128)(2,1)S(1)}, bf16[32,512]{1,0:T(8,128)(2,1)S(1)}, u32[]{:S(2)}, u32[]{:S(2)}) collective-permute-start(bf16[32,512]{1,0:T(8,128)(2,1)S(1)} %get-tuple-element.58), channel_id=1, source_target_pairs={{0,4},{4,8},{8,12},{12,0},{1,5},{5,9},{9,13},{13,1},{2,6},{6,10},{... | collective-permute-start | bytes 98312 | tf_op jit(solution)/shard_map/ppermute | solution.py:452
  6.6 4.3 %collective-permute-start.2 = (bf16[32,512]{1,0:T(8,128)(2,1)S(1)}, bf16[32,512]{1,0:T(8,128)(2,1)S(1)}, u32[]{:S(2)}, u32[]{:S(2)}) collective-permute-start(bf16[32,512]{1,0:T(8,128)(2,1)S(1)} %get-tuple-element.59), channel_id=1, source_target_pairs={{0,12},{4,0},{8,4},{12,8},{1,13},{5,1},{9,5},{13,9},{2,14},{6,2},{... | collective-permute-start | bytes 98312 | tf_op jit(solution)/shard_map/ppermute | solution.py:452
  13.1 11.1 %collective-permute-start.9 = (bf16[400,256]{1,0:T(8,128)(2,1)S(1)}, bf16[400,256]{1,0:T(8,128)(2,1)S(1)}, u32[]{:S(2)}, u32[]{:S(2)}) collective-permute-start(bf16[400,256]{1,0:T(8,128)(2,1)S(1)} %get-tuple-element.71), channel_id=1, source_target_pairs={{0,2},{2,0},{1,3},{3,1},{4,6},{6,4},{5,7},{7,5},{8,10},{10,8},{9,1... | collective-permute-start | bytes 614408 | tf_op jit(solution)/shard_map/ppermute | solution.py:457
  13.7 8.7 %collective-permute-start.4 = (bf16[80,512]{1,0:T(8,128)(2,1)S(1)}, bf16[80,512]{1,0:T(8,128)(2,1)S(1)}, u32[]{:S(2)}, u32[]{:S(2)}) collective-permute-start(bf16[80,512]{1,0:T(8,128)(2,1)S(1)} %get-tuple-element.65), channel_id=1, source_target_pairs={{0,12},{4,8},{8,4},{12,0},{1,13},{5,9},{9,5},{13,1},{2,14},{6,10},... | collective-permute-start | bytes 245768 | tf_op jit(solution)/shard_map/ppermute | solution.py:457
  17.2 5.2 %collective-permute-start.5 = (bf16[80,512]{1,0:T(8,128)(2,1)S(1)}, bf16[80,512]{1,0:T(8,128)(2,1)S(1)}, u32[]{:S(2)}, u32[]{:S(2)}) collective-permute-start(bf16[80,512]{1,0:T(8,128)(2,1)S(1)} %get-tuple-element.66), channel_id=1, source_target_pairs={{0,4},{4,0},{8,12},{12,8},{1,5},{5,1},{9,13},{13,9},{2,6},{6,2},{1... | collective-permute-start | bytes 245768 | tf_op jit(solution)/shard_map/ppermute | solution.py:457
  17.2 5.2 %collective-permute-start.6 = (bf16[64,512]{1,0:T(8,128)(2,1)S(1)}, bf16[64,512]{1,0:T(8,128)(2,1)S(1)}, u32[]{:S(2)}, u32[]{:S(2)}) collective-permute-start(bf16[64,512]{1,0:T(8,128)(2,1)S(1)} %get-tuple-element.67), channel_id=1, source_target_pairs={{0,8},{4,12},{8,0},{12,4},{1,9},{5,13},{9,1},{13,5},{2,10},{6,14},... | collective-permute-start | bytes 196616 | tf_op jit(solution)/shard_map/ppermute | solution.py:457
  22.5 6.2 %collective-permute-start.7 = (bf16[256,256]{1,0:T(8,128)(2,1)S(1)}, bf16[256,256]{1,0:T(8,128)(2,1)S(1)}, u32[]{:S(2)}, u32[]{:S(2)}) collective-permute-start(bf16[256,256]{1,0:T(8,128)(2,1)S(1)} %get-tuple-element.70), channel_id=1, source_target_pairs={{0,2},{2,0},{1,3},{3,1},{4,6},{6,4},{5,7},{7,5},{8,10},{10,8},{9,1... | collective-permute-start | bytes 393224 | tf_op jit(solution)/shard_map/ppermute | solution.py:457
  24.3 6.8 %collective-permute-start.10 = (bf16[144,256]{1,0:T(8,128)(2,1)S(1)}, bf16[144,256]{1,0:T(8,128)(2,1)S(1)}, u32[]{:S(2)}, u32[]{:S(2)}) collective-permute-start(bf16[144,256]{1,0:T(8,128)(2,1)S(1)} %get-tuple-element.73), channel_id=1, source_target_pairs={{0,12},{4,8},{8,4},{12,0},{1,13},{5,9},{9,5},{13,1},{2,14},{6,10},... | collective-permute-start | bytes 221192 | tf_op jit(solution)/shard_map/ppermute | solution.py:457
  27.5 5.4 %collective-permute-start.11 = (bf16[144,256]{1,0:T(8,128)(2,1)S(1)}, bf16[144,256]{1,0:T(8,128)(2,1)S(1)}, u32[]{:S(2)}, u32[]{:S(2)}) collective-permute-start(bf16[144,256]{1,0:T(8,128)(2,1)S(1)} %get-tuple-element.74), channel_id=1, source_target_pairs={{0,8},{4,12},{8,0},{12,4},{1,9},{5,13},{9,1},{13,5},{2,10},{6,14},... | collective-permute-start | bytes 221192 | tf_op jit(solution)/shard_map/ppermute | solution.py:457
  27.8 5.1 %collective-permute-start.12 = (bf16[144,256]{1,0:T(8,128)(2,1)S(1)}, bf16[144,256]{1,0:T(8,128)(2,1)S(1)}, u32[]{:S(2)}, u32[]{:S(2)}) collective-permute-start(bf16[144,256]{1,0:T(8,128)(2,1)S(1)} %get-tuple-element.75), channel_id=1, source_target_pairs={{0,4},{4,0},{8,12},{12,8},{1,5},{5,1},{9,13},{13,9},{2,6},{6,2},{1... | collective-permute-start | bytes 221192 | tf_op jit(solution)/shard_map/ppermute | solution.py:457
  29.1 9.8 %collective-permute-start.8 = (bf16[128,512]{1,0:T(8,128)(2,1)S(1)}, bf16[128,512]{1,0:T(8,128)(2,1)S(1)}, u32[]{:S(2)}, u32[]{:S(2)}) collective-permute-start(bf16[128,512]{1,0:T(8,128)(2,1)S(1)} %shard_map.166.own_ref), channel_id=1, source_target_pairs={{0,1},{1,0},{2,3},{3,2},{4,5},{5,4},{6,7},{7,6},{8,9},{9,8},{10,11... | collective-permute-start | bytes 393224 | tf_op jit(solution)/shard_map/ppermute | solution.py:452
  33.1 7.4 %collective-permute-start.14 = (bf16[192,256]{1,0:T(8,128)(2,1)S(1)}, bf16[192,256]{1,0:T(8,128)(2,1)S(1)}, u32[]{:S(2)}, u32[]{:S(2)}) collective-permute-start(bf16[192,256]{1,0:T(8,128)(2,1)S(1)} %get-tuple-element.82.a_ref), channel_id=1, source_target_pairs={{0,12},{4,8},{8,4},{12,0},{1,13},{5,9},{9,5},{13,1},{2,14},{6,10},... | collective-permute-start | bytes 294920 | tf_op jit(solution)/shard_map/ppermute | solution.py:457
  35.1 7.0 %collective-permute-start.13 = (bf16[192,256]{1,0:T(8,128)(2,1)S(1)}, bf16[192,256]{1,0:T(8,128)(2,1)S(1)}, u32[]{:S(2)}, u32[]{:S(2)}) collective-permute-start(bf16[192,256]{1,0:T(8,128)(2,1)S(1)} %get-tuple-element.82.a_ref), channel_id=1, source_target_pairs={{0,8},{4,12},{8,0},{12,4},{1,9},{5,13},{9,1},{13,5},{2,10},{6,14},... | collective-permute-start | bytes 294920 | tf_op jit(solution)/shard_map/ppermute | solution.py:457
  35.1 8.8 %collective-permute-start.19 = (bf16[192,256]{1,0:T(8,128)(2,1)S(1)}, bf16[192,256]{1,0:T(8,128)(2,1)S(1)}, u32[]{:S(2)}, u32[]{:S(2)}) collective-permute-start(bf16[192,256]{1,0:T(8,128)(2,1)S(1)} %get-tuple-element.82.a_ref), channel_id=1, source_target_pairs={{0,6},{2,4},{4,2},{6,0},{8,14},{10,12},{12,10},{14,8},{1,7},{3,5},... | collective-permute-start | bytes 294920 | tf_op jit(solution)/shard_map/ppermute | solution.py:463
  37.3 6.7 %collective-permute-start.18 = (bf16[192,256]{1,0:T(8,128)(2,1)S(1)}, bf16[192,256]{1,0:T(8,128)(2,1)S(1)}, u32[]{:S(2)}, u32[]{:S(2)}) collective-permute-start(bf16[192,256]{1,0:T(8,128)(2,1)S(1)} %get-tuple-element.82.a_ref), channel_id=1, source_target_pairs={{0,2},{2,0},{1,3},{3,1},{4,6},{6,4},{5,7},{7,5},{8,10},{10,8},{9,1... | collective-permute-start | bytes 294920 | tf_op jit(solution)/shard_map/ppermute | solution.py:457
  39.0 5.0 %collective-permute-start.17 = (bf16[192,256]{1,0:T(8,128)(2,1)S(1)}, bf16[192,256]{1,0:T(8,128)(2,1)S(1)}, u32[]{:S(2)}, u32[]{:S(2)}) collective-permute-start(bf16[192,256]{1,0:T(8,128)(2,1)S(1)} %get-tuple-element.82.a_ref), channel_id=1, source_target_pairs={{0,4},{4,0},{8,12},{12,8},{1,5},{5,1},{9,13},{13,9},{2,6},{6,2},{1... | collective-permute-start | bytes 294920 | tf_op jit(solution)/shard_map/ppermute | solution.py:457
  40.5 4.6 %collective-permute-start.16 = (bf16[192,256]{1,0:T(8,128)(2,1)S(1)}, bf16[192,256]{1,0:T(8,128)(2,1)S(1)}, u32[]{:S(2)}, u32[]{:S(2)}) collective-permute-start(bf16[192,256]{1,0:T(8,128)(2,1)S(1)} %collective-permute-done.14.b_ref), channel_id=1, source_target_pairs={{0,2},{2,0},{1,3},{3,1},{4,6},{6,4},{5,7},{7,5},{8,10},{10,8},{9,1... | collective-permute-start | bytes 294920 | tf_op jit(solution)/shard_map/ppermute | solution.py:457
  42.1 4.6 %collective-permute-start.15 = (bf16[192,256]{1,0:T(8,128)(2,1)S(1)}, bf16[192,256]{1,0:T(8,128)(2,1)S(1)}, u32[]{:S(2)}, u32[]{:S(2)}) collective-permute-start(bf16[192,256]{1,0:T(8,128)(2,1)S(1)} %collective-permute-done.13.a_ref), channel_id=1, source_target_pairs={{0,2},{2,0},{1,3},{3,1},{4,6},{6,4},{5,7},{7,5},{8,10},{10,8},{9,1... | collective-permute-start | bytes 294920 | tf_op jit(solution)/shard_map/ppermute | solution.py:457

commit v17 on v15

--- a/solution.py
+++ b/solution.py
@@ -215,7 +215,7 @@
     back = by_source_low[rows:]
 
     if paired:
-        sends, keeps, out_refs = message_refs[:2], message_refs[2:4], message_refs[4:]
+        send_ref, keep_ref, *out_refs = message_refs
         sub = lax.axis_index("sub")
         mesh = lax.axis_index("mesh")
         lines = len(out_refs)
@@ -224,13 +224,12 @@
         pair_scratch[0] = jnp.where(first, dst_part, src_part)
         pair_scratch[1] = jnp.where(first, src_part, dst_part)
         strip = width // lines
-        for slot, (far_ref, zero_ref) in enumerate((sends, keeps)):
-            places = [(far_ref, at, k) for at, k in enumerate((3, 2, 1))] + [(zero_ref, 0, 0)]
-            for ref, at, k in places:
+        for slot, ref in enumerate((send_ref, keep_ref)):
+            for at, k in enumerate((3, 2, 1, 0)):
                 start = pl.multiple_of((mesh ^ k) * strip, strip)
                 ref[at * strip : (at + 1) * strip, :] = pair_scratch[slot, pl.ds(start, strip), :]
-            far_ref[3 * strip :, :] = tail
-        sends[1][strip:, :] = back[2 * halo :]
+            ref[width : width + TAIL, :] = tail
+        send_ref[width + TAIL :, :] = back[2 * halo :]
         back_scratch[...] = back[: 2 * halo]
         out_scratch[...] = out_part
         strip = hid // len(out_refs)
@@ -286,21 +285,21 @@
     return terms[0]
 
 
-def far_kernel(arrived_ref, keep_ref, *refs):
-    *line_refs, tail_ref = refs
-    total = keep_ref[...].astype(f32) + arrived_ref[...].astype(f32)
-    strip = line_refs[0].shape[0] - TAIL
-    tail = total[len(line_refs) * strip :]
+def turn_kernel(arrived_ref, keep_ref, *refs):
+    full = keep_ref.shape[0]
+    total = keep_ref[...].astype(f32) + arrived_ref[0:full, :].astype(f32)
+    rows = full - TAIL
+    strip = rows // len(refs)
+    tail = total[rows:]
     tail = tail_of([tail[at : at + 1] + tail[at + 1 : at + 2] for at in range(0, 6, 2)])
-    for k, ref in enumerate(line_refs):
+    for k, ref in enumerate(refs):
         ref[0:strip, :] = total[k * strip : (k + 1) * strip].astype(bf16)
         ref[strip:, :] = tail
-    tail_ref[...] = tail
 
 
 def line_kernel(*refs):
-    *terms, _, send_ref, keep_ref = refs
-    rows, hid = send_ref.shape
+    *terms, send_ref, keep_ref = refs
+    rows, hid = keep_ref.shape
     total = tree([r[0:rows, :].astype(f32) for r in terms])
     first = lax.axis_index("sub") == 0
     left, right = total[:, :hid], total[:, hid:]
@@ -309,15 +308,12 @@
 
 
 def own_kernel(*refs):
-    *terms, keep_ref, arrived_ref, vectors_ref, out_keep_ref, out_arrived_ref, _, own_ref, tail_ref = refs
-    strip = keep_ref.shape[0]
-    zero = (keep_ref[...].astype(f32) + arrived_ref[0:strip, :].astype(f32)).astype(bf16)
-    total = tree([r[0:strip, :].astype(f32) for r in terms] + [zero.astype(f32)])
-    own_ref[0:strip, :] = total.astype(bf16)
-    own_ref[strip:, :] = (
-        out_keep_ref[...].astype(f32) + out_arrived_ref[...].astype(f32)
-    ).astype(bf16)
-    tail_ref[...] = tree([r[strip:, :].astype(f32) for r in terms] + [vectors_ref[...].astype(f32)])
+    *terms, out_keep_ref, out_arrived_ref, own_ref, tail_ref = refs
+    total = tree([r[...].astype(f32) for r in terms])
+    strip = own_ref.shape[0] - out_keep_ref.shape[0]
+    own_ref[0:strip, :] = total[:strip].astype(bf16)
+    own_ref[strip:, :] = (out_keep_ref[...].astype(f32) + out_arrived_ref[...].astype(f32)).astype(bf16)
+    tail_ref[...] = total[strip:]
 
 
 def write_vectors(tail, bias_ref, gain_ref):
@@ -464,28 +460,25 @@
 
 
 def paired_sums(messages, lines, strip, narrow, width, hid, node_terms):
-    sends, keeps, outs = messages[:2], messages[2:4], messages[4:]
+    send, keep, *outs = messages
     order = range(lines - 1, 0, -1)
     block = shape((strip + TAIL, hid), bf16)
-    far = across(sends[0], "sub", 1)
+    pair = across(send, "sub", 1)
     out_terms = {k: across(outs[k], "mesh", k) for k in order}
-    zero = across(sends[1], "sub", 1)
-    line = {}
-    line[3], line[2], line[1], tail = call(
-        far_kernel, [block] * 3 + [shape((TAIL, hid), bf16)], far, keeps[0]
-    )
+    line = call(turn_kernel, [block] * lines, pair, keep)[::-1]
     line_terms = {k: across(line[k], "mesh", k) for k in order}
     out_send, out_keep = call(
         line_kernel,
         [shape((narrow, hid), bf16)] * 2,
-        *[out_terms[k] for k in order], outs[0], line[1],
-    )
-    node_part = node_terms(out_terms[3], out_terms[1], zero)
+        *[out_terms[k] for k in order], outs[0],
+        flops=10**10,
+    )
+    node_part = node_terms(out_terms[3], out_terms[1], pair)
     own, tail = call(
         own_kernel,
         [shape((strip + narrow, hid), bf16), shape((TAIL, hid), f32)],
-        *[line_terms[k] for k in order], keeps[1], zero, tail, out_keep, across(out_send, "sub", 1),
-        node_part,
+        *[line_terms[k] for k in order], line[0], out_keep, across(out_send, "sub", 1),
+        flops=10**8,
     )
     mine = {k: across(own, "mesh", k) for k in order}
     mine[0] = own
@@ -589,7 +582,7 @@
     if paired:
         strip = width // lines
         narrow = hid // lines
-        rows_of = (3 * strip + TAIL, strip + 2 * halo, 3 * strip + TAIL, strip)
+        rows_of = (width + TAIL + 2 * halo, width + TAIL)
         message_shapes = [shape((n, hid), bf16) for n in rows_of]
         message_shapes += [shape((narrow + k % 2 * (halo // 2), width), bf16) for k in range(lines)]
     else:

time: 48.5 us -> 46.5 us (0.959)
  starting transfers between devices: 30.1 us -> 26.7 us
  waiting for transfers between devices: 9.01 us -> 10.4 us
    ppermute x1, starting transfers between devices: 3.69 us -> 1.58 us  [diagonal(): return lax.ppermute(x, ('mesh', 'sub'), moves)]
    ppermute x15 -> x14, waiting for transfers between devices: 8.67 us -> 10.1 us  [across(): return lax.ppermute(x, axis, [(i, i ^ k) for i in range(count)])]
    ppermute x15 -> x14, starting transfers between devices: 19.5 us -> 18.2 us  [across(): return lax.ppermute(x, axis, [(i, i ^ k) for i in range(count)])]
  transfers between devices with their start and end apart: 21 -> 20, of which waited for: 9 -> 7; matrix products, arithmetic and copies ran while one was open for 0% -> 0% of each run, Pallas kernels for 8% -> 9%
where the time goes in v17:
time: 46.5 us; the launch traced here: 46.3 us
  starting transfers between devices  26.7 us (57%)
  waiting for transfers between devices  10.4 us (22%)
  Pallas kernels  8.44 us (18%)
  between operations  0.73 us (2%)
    ppermute x14, starting transfers between devices, across(): return lax.ppermute(x, axis, [(i, i ^ k) for i in range(count)])  18.2 us
    ppermute x14, waiting for transfers between devices, across(): return lax.ppermute(x, axis, [(i, i ^ k) for i in range(count)])  10.1 us
    pallas_call x10, Pallas kernels, call(): pl.pallas_call(kernel, out_shape=outs, in_specs=specs or [VMEM] * len(arg...  8.44 us
    ppermute x5, starting transfers between devices, shifted(): return lax.ppermute(x, axis, [(i, (i + by) % count) for i in range(count)])  6.98 us
    ppermute x1, starting transfers between devices, diagonal(): return lax.ppermute(x, ('mesh', 'sub'), moves)  1.58 us
  transfers between devices with their start and end apart: 20, of which 7 were waited for; matrix products, arithmetic and copies ran while one was open for 0% of the time, Pallas kernels for 9%

profile of v17, /device:TPU:0, one launch (start us, length us, event | category | flops | bytes accessed | tf_op | source)
XLA Modules:
  0.0 46.3 jit_solution(16201407054081277391)
XLA Ops:
  0.6 1.3 %shard_map.162 = (bf16[128,512]{1,0:T(8,128)(2,1)S(1)}, s32[1,4,32]{2,1,0:T(4,128)S(1)}, bf16[1552,256]{1,0:T(8,128)(2,1)S(1)}, bf16[32,512]{1,0:T(8,128)(2,1)S(...) custom-call(bf16[128,512]{1,0:T(8,128)(2,1)} %node_hbm.1, s32[1,4,32]{2,1,0:T(4,128)} %send_hbm.1, ...), custom_call_target="tpu_custom_call" | custom-call | flops 100000000 | bytes 1000000 | tf_op jit(solution)/shard_map/pallas_call | solution.py:434
  1.9 0.5 %collective-permute-start = (bf16[1552,256]{1,0:T(8,128)(2,1)S(1)}, bf16[1552,256]{1,0:T(8,128)(2,1)S(1)}, u32[]{:S(2)}, u32[]{:S(2)}) collective-permute-start(bf16[1552,256]{1,0:T(8,128)(2,1)S(1)} %get-tuple-element.48.packed_ref), channel_id=1, source_target_pairs={{0,1},{1,0},{2,3},{3,2},{4,5},{5,4},{6,7},{7,6},{8,9},{9,8},{10,11... | collective-permute-start | bytes 2383880 | tf_op jit(solution)/shard_map/ppermute | solution.py:448
  2.4 2.6 %collective-permute-start.3 = (bf16[64,512]{1,0:T(8,128)(2,1)S(1)}, bf16[64,512]{1,0:T(8,128)(2,1)S(1)}, u32[]{:S(2)}, u32[]{:S(2)}) collective-permute-start(bf16[64,512]{1,0:T(8,128)(2,1)S(1)} %get-tuple-element.58), channel_id=1, source_target_pairs={{0,2},{2,0},{1,3},{3,1},{4,6},{6,4},{5,7},{7,5},{8,10},{10,8},{9,1... | collective-permute-start | bytes 196616 | tf_op jit(solution)/shard_map/ppermute | solution.py:448
  5.0 1.6 %collective-permute-start.1 = (bf16[32,512]{1,0:T(8,128)(2,1)S(1)}, bf16[32,512]{1,0:T(8,128)(2,1)S(1)}, u32[]{:S(2)}, u32[]{:S(2)}) collective-permute-start(bf16[32,512]{1,0:T(8,128)(2,1)S(1)} %get-tuple-element.56), channel_id=1, source_target_pairs={{0,4},{4,8},{8,12},{12,0},{1,5},{5,9},{9,13},{13,1},{2,6},{6,10},{... | collective-permute-start | bytes 98312 | tf_op jit(solution)/shard_map/ppermute | solution.py:448
  6.6 2.2 %collective-permute-start.2 = (bf16[32,512]{1,0:T(8,128)(2,1)S(1)}, bf16[32,512]{1,0:T(8,128)(2,1)S(1)}, u32[]{:S(2)}, u32[]{:S(2)}) collective-permute-start(bf16[32,512]{1,0:T(8,128)(2,1)S(1)} %get-tuple-element.57), channel_id=1, source_target_pairs={{0,12},{4,0},{8,4},{12,8},{1,13},{5,1},{9,5},{13,9},{2,14},{6,2},{... | collective-permute-start | bytes 98312 | tf_op jit(solution)/shard_map/ppermute | solution.py:448
  8.8 0.0 collective-permute-done.other_ref
  8.8 1.7 %shard_map.163 = (f32[512,512]{1,0:T(8,128)S(1)}, bf16[512,128]{1,0:T(8,128)(2,1)S(1)}, bf16[128,512]{1,0:T(8,128)(2,1)S(1)}, bf16[512,128]{1,0:T(8,128)(2,1)S(1...) custom-call(bf16[128,512]{1,0:T(8,128)(2,1)S(1)} %get-tuple-element.47.node_ref, ...), custom_call_target="tpu_custom_call" | custom-call | flops 100000000 | bytes 1000000 | tf_op jit(solution)/shard_map/pallas_call | solution.py:434
  10.5 0.3 collective-permute-done.1.rest_0_
  10.8 0.0 collective-permute-done.2.rest_1_
  10.8 0.0 collective-permute-done.3.rest_2_
  10.8 2.3 %shard_map.164 = (f32[128,512]{1,0:T(8,128)S(1)}, f32[128,256]{1,0:T(8,128)S(1)}, bf16[128,256]{1,0:T(8,128)(2,1)S(1)}, bf16[592,256]{1,0:T(8,128)(2,1)S(1)}, bf...) custom-call(bf16[128,512]{1,0:T(8,128)(2,1)S(1)} %get-tuple-element., ...), custom_call_target="tpu_custom_call" | custom-call | flops 100000000 | bytes 1000000 | tf_op jit(solution)/shard_map/pallas_call | solution.py:434
  13.1 0.6 %collective-permute-start.6 = (bf16[592,256]{1,0:T(8,128)(2,1)S(1)}, bf16[592,256]{1,0:T(8,128)(2,1)S(1)}, u32[]{:S(2)}, u32[]{:S(2)}) collective-permute-start(bf16[592,256]{1,0:T(8,128)(2,1)S(1)} %get-tuple-element.65), channel_id=1, source_target_pairs={{0,2},{2,0},{1,3},{3,1},{4,6},{6,4},{5,7},{7,5},{8,10},{10,8},{9,1... | collective-permute-start | bytes 909320 | tf_op jit(solution)/shard_map/ppermute | solution.py:453
  13.7 3.5 %collective-permute-start.4 = (bf16[80,512]{1,0:T(8,128)(2,1)S(1)}, bf16[80,512]{1,0:T(8,128)(2,1)S(1)}, u32[]{:S(2)}, u32[]{:S(2)}) collective-permute-start(bf16[80,512]{1,0:T(8,128)(2,1)S(1)} %get-tuple-element.63), channel_id=1, source_target_pairs={{0,12},{4,8},{8,4},{12,0},{1,13},{5,9},{9,5},{13,1},{2,14},{6,10},... | collective-permute-start | bytes 245768 | tf_op jit(solution)/shard_map/ppermute | solution.py:453
  17.2 0.0 collective-permute-start.5
  17.2 0.9 %collective-permute-start.11 = (bf16[64,512]{1,0:T(8,128)(2,1)S(1)}, bf16[64,512]{1,0:T(8,128)(2,1)S(1)}, u32[]{:S(2)}, u32[]{:S(2)}) collective-permute-start(bf16[64,512]{1,0:T(8,128)(2,1)S(1)} %get-tuple-element.71), channel_id=1, source_target_pairs={{0,8},{4,12},{8,0},{12,4},{1,9},{5,13},{9,1},{13,5},{2,10},{6,14},... | collective-permute-start | bytes 196616 | tf_op jit(solution)/shard_map/ppermute | solution.py:453
  18.1 3.5 %collective-permute-done.6.pair_ref.arrived_ref = bf16[592,256]{1,0:T(8,128)(2,1)S(1)} collective-permute-done((bf16[592,256]{1,0:T(8,128)(2,1)S(1)}, bf16[592,256]{1,0:T(8,128)(2,1)S(1)}, u32[]{:S(2)}, u32[]{:S(2)}) %collective-permute-start.6) | collective-permute-done | bytes 303136 | tf_op jit(solution)/shard_map/ppermute | solution.py:453
  21.7 0.1 shard_map.166
  21.7 3.2 %collective-permute-start.8 = (bf16[144,256]{1,0:T(8,128)(2,1)S(1)}, bf16[144,256]{1,0:T(8,128)(2,1)S(1)}, u32[]{:S(2)}, u32[]{:S(2)}) collective-permute-start(bf16[144,256]{1,0:T(8,128)(2,1)S(1)} %get-tuple-element.67), channel_id=1, source_target_pairs={{0,12},{4,8},{8,4},{12,0},{1,13},{5,9},{9,5},{13,1},{2,14},{6,10},... | collective-permute-start | bytes 221192 | tf_op jit(solution)/shard_map/ppermute | solution.py:453
  24.9 0.0 collective-permute-start.9
  24.9 0.0 collective-permute-done.11.refs_1_
  24.9 1.3 %collective-permute-start.10 = (bf16[144,256]{1,0:T(8,128)(2,1)S(1)}, bf16[144,256]{1,0:T(8,128)(2,1)S(1)}, u32[]{:S(2)}, u32[]{:S(2)}) collective-permute-start(bf16[144,256]{1,0:T(8,128)(2,1)S(1)} %get-tuple-element.69), channel_id=1, source_target_pairs={{0,4},{4,0},{8,12},{12,8},{1,5},{5,1},{9,13},{13,9},{2,6},{6,2},{1... | collective-permute-start | bytes 221192 | tf_op jit(solution)/shard_map/ppermute | solution.py:453
  26.2 0.0 collective-permute-done.4.three_ref.refs_0_
  26.2 0.0 collective-permute-done.5.one_ref.refs_2_
  26.2 0.6 %collective-permute-start.12 = (bf16[64,256]{1,0:T(8,128)(2,1)S(1)}, bf16[64,256]{1,0:T(8,128)(2,1)S(1)}, u32[]{:S(2)}, u32[]{:S(2)}) collective-permute-start(bf16[64,256]{1,0:T(8,128)(2,1)S(1)} %get-tuple-element.74), channel_id=1, source_target_pairs={{0,2},{2,0},{1,3},{3,1},{4,6},{6,4},{5,7},{7,5},{8,10},{10,8},{9,1... | collective-permute-start | bytes 98312 | tf_op jit(solution)/shard_map/ppermute | solution.py:453
  26.8 0.4 shard_map.165.own_ref
  27.2 0.1 collective-permute-start.7
  27.3 2.9 %collective-permute-done.12.refs_5_ = bf16[64,256]{1,0:T(8,128)(2,1)S(1)} collective-permute-done((bf16[64,256]{1,0:T(8,128)(2,1)S(1)}, bf16[64,256]{1,0:T(8,128)(2,1)S(1)}, u32[]{:S(2)}, u32[]{:S(2)}) %collective-permute-start.12) | collective-permute-done | bytes 32800 | tf_op jit(solution)/shard_map/ppermute | solution.py:453
  30.2 0.0 collective-permute-done.8.refs_0_
  30.2 0.1 collective-permute-done.9.refs_1_
  30.3 0.0 collective-permute-done.10.refs_2_
  30.4 3.1 %collective-permute-start.14 = (bf16[192,256]{1,0:T(8,128)(2,1)S(1)}, bf16[192,256]{1,0:T(8,128)(2,1)S(1)}, u32[]{:S(2)}, u32[]{:S(2)}) collective-permute-start(bf16[192,256]{1,0:T(8,128)(2,1)S(1)} %get-tuple-element.78.a_ref), channel_id=1, source_target_pairs={{0,12},{4,8},{8,4},{12,0},{1,13},{5,9},{9,5},{13,1},{2,14},{6,10},... | collective-permute-start | bytes 294920 | tf_op jit(solution)/shard_map/ppermute | solution.py:453
  33.5 0.0 collective-permute-start.13
  33.5 1.6 %collective-permute-start.19 = (bf16[192,256]{1,0:T(8,128)(2,1)S(1)}, bf16[192,256]{1,0:T(8,128)(2,1)S(1)}, u32[]{:S(2)}, u32[]{:S(2)}) collective-permute-start(bf16[192,256]{1,0:T(8,128)(2,1)S(1)} %get-tuple-element.78.a_ref), channel_id=1, source_target_pairs={{0,6},{2,4},{4,2},{6,0},{8,14},{10,12},{12,10},{14,8},{1,7},{3,5},... | collective-permute-start | bytes 294920 | tf_op jit(solution)/shard_map/ppermute | solution.py:459
  35.1 1.2 %collective-permute-start.18 = (bf16[192,256]{1,0:T(8,128)(2,1)S(1)}, bf16[192,256]{1,0:T(8,128)(2,1)S(1)}, u32[]{:S(2)}, u32[]{:S(2)}) collective-permute-start(bf16[192,256]{1,0:T(8,128)(2,1)S(1)} %get-tuple-element.78.a_ref), channel_id=1, source_target_pairs={{0,2},{2,0},{1,3},{3,1},{4,6},{6,4},{5,7},{7,5},{8,10},{10,8},{9,1... | collective-permute-start | bytes 294920 | tf_op jit(solution)/shard_map/ppermute | solution.py:453
  36.3 0.0 collective-permute-done.7.other_ref
  36.3 0.7 %collective-permute-start.17 = (bf16[192,256]{1,0:T(8,128)(2,1)S(1)}, bf16[192,256]{1,0:T(8,128)(2,1)S(1)}, u32[]{:S(2)}, u32[]{:S(2)}) collective-permute-start(bf16[192,256]{1,0:T(8,128)(2,1)S(1)} %get-tuple-element.78.a_ref), channel_id=1, source_target_pairs={{0,4},{4,0},{8,12},{12,8},{1,5},{5,1},{9,13},{13,9},{2,6},{6,2},{1... | collective-permute-start | bytes 294920 | tf_op jit(solution)/shard_map/ppermute | solution.py:453
  37.0 0.3 collective-permute-done.14.b_ref
  37.3 1.5 %collective-permute-start.16 = (bf16[192,256]{1,0:T(8,128)(2,1)S(1)}, bf16[192,256]{1,0:T(8,128)(2,1)S(1)}, u32[]{:S(2)}, u32[]{:S(2)}) collective-permute-start(bf16[192,256]{1,0:T(8,128)(2,1)S(1)} %collective-permute-done.14.b_ref), channel_id=1, source_target_pairs={{0,2},{2,0},{1,3},{3,1},{4,6},{6,4},{5,7},{7,5},{8,10},{10,8},{9,1... | collective-permute-start | bytes 294920 | tf_op jit(solution)/shard_map/ppermute | solution.py:453
  38.8 2.0 %collective-permute-done.13.a_ref = bf16[192,256]{1,0:T(8,128)(2,1)S(1)} collective-permute-done((bf16[192,256]{1,0:T(8,128)(2,1)S(1)}, bf16[192,256]{1,0:T(8,128)(2,1)S(1)}, u32[]{:S(2)}, u32[]{:S(2)}) %collective-permute-start.13) | collective-permute-done | bytes 98336 | tf_op jit(solution)/shard_map/ppermute | solution.py:453
  40.8 1.6 %collective-permute-start.15 = (bf16[192,256]{1,0:T(8,128)(2,1)S(1)}, bf16[192,256]{1,0:T(8,128)(2,1)S(1)}, u32[]{:S(2)}, u32[]{:S(2)}) collective-permute-start(bf16[192,256]{1,0:T(8,128)(2,1)S(1)} %collective-permute-done.13.a_ref), channel_id=1, source_target_pairs={{0,2},{2,0},{1,3},{3,1},{4,6},{6,4},{5,7},{7,5},{8,10},{10,8},{9,1... | collective-permute-start | bytes 294920 | tf_op jit(solution)/shard_map/ppermute | solution.py:453
  42.4 0.8 %shard_map.169 = (f32[128,512]{1,0:T(8,128)}, bf16[128,512]{1,0:T(8,128)(2,1)}, f32[1,256]{1,0:T(1,128)}, f32[1,512]{1,0:T(1,128)}) custom-call(bf16[128,512]{1,0:T(8,128)(2,1)S(1)} %get-tuple-element.49.cot_ref, bf16[128,512]{1,0:T(8,128)(2,1)S(1)} %get-tuple-element.47.node_ref, f32[1,512]{1,0:T(1,128)S(1)} %get-tuple-element.50.gain_ref, ...), custom_call_target="tpu_custom_call" | custom-call | flops 100000000 | bytes 1000000 | tf_op jit(solution)/shard_map/pallas_call | solution.py:434
  43.2 0.0 collective-permute-done.19.d_ref
  43.2 0.0 collective-permute-done.18.c_ref
  43.2 0.0 collective-permute-done.17.b_ref
  43.2 0.9 %shard_map.170 = (f32[512,256]{1,0:T(8,128)}, f32[512,256]{1,0:T(8,128)}, f32[256,512]{1,0:T(8,128)}) custom-call(bf16[192,256]{1,0:T(8,128)(2,1)S(1)} %get-tuple-element.78.a_ref, bf16[192,256]{1,0:T(8,128)(2,1)S(1)} %collective-permute-done.17.b_ref, bf16[192,256]{1,0:T(8,128)(2,1)S(1)} %collective-permute-done.18.c_ref, ...), custom_call_target="tpu_custom_call" | custom-call | flops 100000000 | bytes 1000000 | tf_op jit(solution)/shard_map/pallas_call | solution.py:434
  44.1 0.0 collective-permute-done.16.d_ref
  44.2 1.2 %collective-permute-done.15.c_ref = bf16[192,256]{1,0:T(8,128)(2,1)S(1)} collective-permute-done((bf16[192,256]{1,0:T(8,128)(2,1)S(1)}, bf16[192,256]{1,0:T(8,128)(2,1)S(1)}, u32[]{:S(2)}, u32[]{:S(2)}) %collective-permute-start.15) | collective-permute-done | bytes 98336 | tf_op jit(solution)/shard_map/ppermute | solution.py:453
  45.4 0.9 %shard_map.171 = (f32[512,256]{1,0:T(8,128)}, f32[512,256]{1,0:T(8,128)}, f32[256,512]{1,0:T(8,128)}) custom-call(bf16[192,256]{1,0:T(8,128)(2,1)S(1)} %collective-permute-done.13.a_ref, bf16[192,256]{1,0:T(8,128)(2,1)S(1)} %collective-permute-done.14.b_ref, ...), custom_call_target="tpu_custom_call", output_to_operand_aliasing={{0}: (4, {}), {1}: (5, {}), {2}: (6, {})} | custom-call | flops 100000000 | bytes 1000000 | tf_op jit(solution)/shard_map/pallas_call | solution.py:434
  (2 shorter events, 0.1 us)
Async XLA Ops:
  1.9 6.9 %collective-permute-start = (bf16[1552,256]{1,0:T(8,128)(2,1)S(1)}, bf16[1552,256]{1,0:T(8,128)(2,1)S(1)}, u32[]{:S(2)}, u32[]{:S(2)}) collective-permute-start(bf16[1552,256]{1,0:T(8,128)(2,1)S(1)} %get-tuple-element.48.packed_ref), channel_id=1, source_target_pairs={{0,1},{1,0},{2,3},{3,2},{4,5},{5,4},{6,7},{7,6},{8,9},{9,8},{10,11... | collective-permute-start | bytes 2383880 | tf_op jit(solution)/shard_map/ppermute | solution.py:448
  2.4 8.4 %collective-permute-start.3 = (bf16[64,512]{1,0:T(8,128)(2,1)S(1)}, bf16[64,512]{1,0:T(8,128)(2,1)S(1)}, u32[]{:S(2)}, u32[]{:S(2)}) collective-permute-start(bf16[64,512]{1,0:T(8,128)(2,1)S(1)} %get-tuple-element.58), channel_id=1, source_target_pairs={{0,2},{2,0},{1,3},{3,1},{4,6},{6,4},{5,7},{7,5},{8,10},{10,8},{9,1... | collective-permute-start | bytes 196616 | tf_op jit(solution)/shard_map/ppermute | solution.py:448
  5.0 5.8 %collective-permute-start.1 = (bf16[32,512]{1,0:T(8,128)(2,1)S(1)}, bf16[32,512]{1,0:T(8,128)(2,1)S(1)}, u32[]{:S(2)}, u32[]{:S(2)}) collective-permute-start(bf16[32,512]{1,0:T(8,128)(2,1)S(1)} %get-tuple-element.56), channel_id=1, source_target_pairs={{0,4},{4,8},{8,12},{12,0},{1,5},{5,9},{9,13},{13,1},{2,6},{6,10},{... | collective-permute-start | bytes 98312 | tf_op jit(solution)/shard_map/ppermute | solution.py:448
  6.6 4.3 %collective-permute-start.2 = (bf16[32,512]{1,0:T(8,128)(2,1)S(1)}, bf16[32,512]{1,0:T(8,128)(2,1)S(1)}, u32[]{:S(2)}, u32[]{:S(2)}) collective-permute-start(bf16[32,512]{1,0:T(8,128)(2,1)S(1)} %get-tuple-element.57), channel_id=1, source_target_pairs={{0,12},{4,0},{8,4},{12,8},{1,13},{5,1},{9,5},{13,9},{2,14},{6,2},{... | collective-permute-start | bytes 98312 | tf_op jit(solution)/shard_map/ppermute | solution.py:448
  13.1 8.5 %collective-permute-start.6 = (bf16[592,256]{1,0:T(8,128)(2,1)S(1)}, bf16[592,256]{1,0:T(8,128)(2,1)S(1)}, u32[]{:S(2)}, u32[]{:S(2)}) collective-permute-start(bf16[592,256]{1,0:T(8,128)(2,1)S(1)} %get-tuple-element.65), channel_id=1, source_target_pairs={{0,2},{2,0},{1,3},{3,1},{4,6},{6,4},{5,7},{7,5},{8,10},{10,8},{9,1... | collective-permute-start | bytes 909320 | tf_op jit(solution)/shard_map/ppermute | solution.py:453
  13.7 12.5 %collective-permute-start.4 = (bf16[80,512]{1,0:T(8,128)(2,1)S(1)}, bf16[80,512]{1,0:T(8,128)(2,1)S(1)}, u32[]{:S(2)}, u32[]{:S(2)}) collective-permute-start(bf16[80,512]{1,0:T(8,128)(2,1)S(1)} %get-tuple-element.63), channel_id=1, source_target_pairs={{0,12},{4,8},{8,4},{12,0},{1,13},{5,9},{9,5},{13,1},{2,14},{6,10},... | collective-permute-start | bytes 245768 | tf_op jit(solution)/shard_map/ppermute | solution.py:453
  17.2 9.0 %collective-permute-start.5 = (bf16[80,512]{1,0:T(8,128)(2,1)S(1)}, bf16[80,512]{1,0:T(8,128)(2,1)S(1)}, u32[]{:S(2)}, u32[]{:S(2)}) collective-permute-start(bf16[80,512]{1,0:T(8,128)(2,1)S(1)} %get-tuple-element.64), channel_id=1, source_target_pairs={{0,4},{4,0},{8,12},{12,8},{1,5},{5,1},{9,13},{13,9},{2,6},{6,2},{1... | collective-permute-start | bytes 245768 | tf_op jit(solution)/shard_map/ppermute | solution.py:453
  17.2 7.7 %collective-permute-start.11 = (bf16[64,512]{1,0:T(8,128)(2,1)S(1)}, bf16[64,512]{1,0:T(8,128)(2,1)S(1)}, u32[]{:S(2)}, u32[]{:S(2)}) collective-permute-start(bf16[64,512]{1,0:T(8,128)(2,1)S(1)} %get-tuple-element.71), channel_id=1, source_target_pairs={{0,8},{4,12},{8,0},{12,4},{1,9},{5,13},{9,1},{13,5},{2,10},{6,14},... | collective-permute-start | bytes 196616 | tf_op jit(solution)/shard_map/ppermute | solution.py:453
  21.7 8.5 %collective-permute-start.8 = (bf16[144,256]{1,0:T(8,128)(2,1)S(1)}, bf16[144,256]{1,0:T(8,128)(2,1)S(1)}, u32[]{:S(2)}, u32[]{:S(2)}) collective-permute-start(bf16[144,256]{1,0:T(8,128)(2,1)S(1)} %get-tuple-element.67), channel_id=1, source_target_pairs={{0,12},{4,8},{8,4},{12,0},{1,13},{5,9},{9,5},{13,1},{2,14},{6,10},... | collective-permute-start | bytes 221192 | tf_op jit(solution)/shard_map/ppermute | solution.py:453
  24.9 5.4 %collective-permute-start.9 = (bf16[144,256]{1,0:T(8,128)(2,1)S(1)}, bf16[144,256]{1,0:T(8,128)(2,1)S(1)}, u32[]{:S(2)}, u32[]{:S(2)}) collective-permute-start(bf16[144,256]{1,0:T(8,128)(2,1)S(1)} %get-tuple-element.68), channel_id=1, source_target_pairs={{0,8},{4,12},{8,0},{12,4},{1,9},{5,13},{9,1},{13,5},{2,10},{6,14},... | collective-permute-start | bytes 221192 | tf_op jit(solution)/shard_map/ppermute | solution.py:453
  24.9 5.4 %collective-permute-start.10 = (bf16[144,256]{1,0:T(8,128)(2,1)S(1)}, bf16[144,256]{1,0:T(8,128)(2,1)S(1)}, u32[]{:S(2)}, u32[]{:S(2)}) collective-permute-start(bf16[144,256]{1,0:T(8,128)(2,1)S(1)} %get-tuple-element.69), channel_id=1, source_target_pairs={{0,4},{4,0},{8,12},{12,8},{1,5},{5,1},{9,13},{13,9},{2,6},{6,2},{1... | collective-permute-start | bytes 221192 | tf_op jit(solution)/shard_map/ppermute | solution.py:453
  26.2 4.0 %collective-permute-start.12 = (bf16[64,256]{1,0:T(8,128)(2,1)S(1)}, bf16[64,256]{1,0:T(8,128)(2,1)S(1)}, u32[]{:S(2)}, u32[]{:S(2)}) collective-permute-start(bf16[64,256]{1,0:T(8,128)(2,1)S(1)} %get-tuple-element.74), channel_id=1, source_target_pairs={{0,2},{2,0},{1,3},{3,1},{4,6},{6,4},{5,7},{7,5},{8,10},{10,8},{9,1... | collective-permute-start | bytes 98312 | tf_op jit(solution)/shard_map/ppermute | solution.py:453
  27.2 9.1 %collective-permute-start.7 = (bf16[128,512]{1,0:T(8,128)(2,1)S(1)}, bf16[128,512]{1,0:T(8,128)(2,1)S(1)}, u32[]{:S(2)}, u32[]{:S(2)}) collective-permute-start(bf16[128,512]{1,0:T(8,128)(2,1)S(1)} %shard_map.165.own_ref), channel_id=1, source_target_pairs={{0,1},{1,0},{2,3},{3,2},{4,5},{5,4},{6,7},{7,6},{8,9},{9,8},{10,11... | collective-permute-start | bytes 393224 | tf_op jit(solution)/shard_map/ppermute | solution.py:448
  30.4 6.9 %collective-permute-start.14 = (bf16[192,256]{1,0:T(8,128)(2,1)S(1)}, bf16[192,256]{1,0:T(8,128)(2,1)S(1)}, u32[]{:S(2)}, u32[]{:S(2)}) collective-permute-start(bf16[192,256]{1,0:T(8,128)(2,1)S(1)} %get-tuple-element.78.a_ref), channel_id=1, source_target_pairs={{0,12},{4,8},{8,4},{12,0},{1,13},{5,9},{9,5},{13,1},{2,14},{6,10},... | collective-permute-start | bytes 294920 | tf_op jit(solution)/shard_map/ppermute | solution.py:453
  33.5 7.3 %collective-permute-start.13 = (bf16[192,256]{1,0:T(8,128)(2,1)S(1)}, bf16[192,256]{1,0:T(8,128)(2,1)S(1)}, u32[]{:S(2)}, u32[]{:S(2)}) collective-permute-start(bf16[192,256]{1,0:T(8,128)(2,1)S(1)} %get-tuple-element.78.a_ref), channel_id=1, source_target_pairs={{0,8},{4,12},{8,0},{12,4},{1,9},{5,13},{9,1},{13,5},{2,10},{6,14},... | collective-permute-start | bytes 294920 | tf_op jit(solution)/shard_map/ppermute | solution.py:453
  33.5 9.7 %collective-permute-start.19 = (bf16[192,256]{1,0:T(8,128)(2,1)S(1)}, bf16[192,256]{1,0:T(8,128)(2,1)S(1)}, u32[]{:S(2)}, u32[]{:S(2)}) collective-permute-start(bf16[192,256]{1,0:T(8,128)(2,1)S(1)} %get-tuple-element.78.a_ref), channel_id=1, source_target_pairs={{0,6},{2,4},{4,2},{6,0},{8,14},{10,12},{12,10},{14,8},{1,7},{3,5},... | collective-permute-start | bytes 294920 | tf_op jit(solution)/shard_map/ppermute | solution.py:459
  35.1 8.1 %collective-permute-start.18 = (bf16[192,256]{1,0:T(8,128)(2,1)S(1)}, bf16[192,256]{1,0:T(8,128)(2,1)S(1)}, u32[]{:S(2)}, u32[]{:S(2)}) collective-permute-start(bf16[192,256]{1,0:T(8,128)(2,1)S(1)} %get-tuple-element.78.a_ref), channel_id=1, source_target_pairs={{0,2},{2,0},{1,3},{3,1},{4,6},{6,4},{5,7},{7,5},{8,10},{10,8},{9,1... | collective-permute-start | bytes 294920 | tf_op jit(solution)/shard_map/ppermute | solution.py:453
  36.3 6.9 %collective-permute-start.17 = (bf16[192,256]{1,0:T(8,128)(2,1)S(1)}, bf16[192,256]{1,0:T(8,128)(2,1)S(1)}, u32[]{:S(2)}, u32[]{:S(2)}) collective-permute-start(bf16[192,256]{1,0:T(8,128)(2,1)S(1)} %get-tuple-element.78.a_ref), channel_id=1, source_target_pairs={{0,4},{4,0},{8,12},{12,8},{1,5},{5,1},{9,13},{13,9},{2,6},{6,2},{1... | collective-permute-start | bytes 294920 | tf_op jit(solution)/shard_map/ppermute | solution.py:453
  37.3 6.9 %collective-permute-start.16 = (bf16[192,256]{1,0:T(8,128)(2,1)S(1)}, bf16[192,256]{1,0:T(8,128)(2,1)S(1)}, u32[]{:S(2)}, u32[]{:S(2)}) collective-permute-start(bf16[192,256]{1,0:T(8,128)(2,1)S(1)} %collective-permute-done.14.b_ref), channel_id=1, source_target_pairs={{0,2},{2,0},{1,3},{3,1},{4,6},{6,4},{5,7},{7,5},{8,10},{10,8},{9,1... | collective-permute-start | bytes 294920 | tf_op jit(solution)/shard_map/ppermute | solution.py:453
  40.8 4.6 %collective-permute-start.15 = (bf16[192,256]{1,0:T(8,128)(2,1)S(1)}, bf16[192,256]{1,0:T(8,128)(2,1)S(1)}, u32[]{:S(2)}, u32[]{:S(2)}) collective-permute-start(bf16[192,256]{1,0:T(8,128)(2,1)S(1)} %collective-permute-done.13.a_ref), channel_id=1, source_target_pairs={{0,2},{2,0},{1,3},{3,1},{4,6},{6,4},{5,7},{7,5},{8,10},{10,8},{9,1... | collective-permute-start | bytes 294920 | tf_op jit(solution)/shard_map/ppermute | solution.py:453

commit v18 on v17

--- a/solution.py
+++ b/solution.py
@@ -156,7 +156,7 @@
     *rest,
 ):
     peers, chunk, n_halo, paired = geometry
-    *rest, out_scratch, back_scratch, pair_scratch = rest
+    *rest, out_scratch, back_scratch = rest
     halo_refs = rest[:n_halo]
     normed_ref, local_ref, target_ref, *message_refs = rest[n_halo:]
     node = node_ref[...]
@@ -221,13 +221,13 @@
         lines = len(out_refs)
         halo = back.shape[0] // 4
         first = sub == 0
-        pair_scratch[0] = jnp.where(first, dst_part, src_part)
-        pair_scratch[1] = jnp.where(first, src_part, dst_part)
         strip = width // lines
-        for slot, ref in enumerate((send_ref, keep_ref)):
-            for at, k in enumerate((3, 2, 1, 0)):
-                start = pl.multiple_of((mesh ^ k) * strip, strip)
-                ref[at * strip : (at + 1) * strip, :] = pair_scratch[slot, pl.ds(start, strip), :]
+        chosen = ((send_ref, dst_part, src_part), (keep_ref, src_part, dst_part))
+        for ref, when_first, otherwise in chosen:
+            value = jnp.where(first, when_first, otherwise)
+            for j in range(lines):
+                start = pl.multiple_of((lines - 1 - (mesh ^ j)) * strip, strip)
+                ref[pl.ds(start, strip), :] = value[j * strip : (j + 1) * strip]
             ref[width : width + TAIL, :] = tail
         send_ref[width + TAIL :, :] = back[2 * halo :]
         back_scratch[...] = back[: 2 * halo]
@@ -323,12 +323,8 @@
         gain_ref[:, k * hid : (k + 1) * hid] = tail[2 + 2 * k : 3 + 2 * k] + tail[3 + 2 * k : 4 + 2 * k]
 
 
-def relay_kernel(*refs):
-    *_, strip_ref, out_ref = refs
-    out_ref[...] = strip_ref[...]
-
-
-def place_kernel(lines, which, a_ref, b_ref, c_ref, d_ref, *refs):
+def place_kernel(which, *refs):
+    count = len(which)
     src_hbm, dst_hbm, out_hbm, src_ref, dst_ref, out_ref, sems = refs[-7:]
     first = lax.axis_index("sub") == 0
     mesh = lax.axis_index("mesh")
@@ -341,8 +337,8 @@
         copies.append(pltpu.make_async_copy(ref.at[at], hbm.at[pl.ds(start, rows)], sems.at[len(copies)]))
         copies[-1].start()
 
-    for at, (mine_ref, theirs_ref) in enumerate(((a_ref, c_ref), (b_ref, d_ref))):
-        mine, theirs = mine_ref[...], theirs_ref[...]
+    for at in range(count):
+        mine, theirs = refs[at][...], refs[count + at][...]
         low = jnp.where(first, mine, theirs).astype(f32)
         high = jnp.where(first, theirs, mine).astype(f32)
         src_ref[at] = low[:strip]
@@ -483,24 +479,24 @@
     mine = {k: across(own, "mesh", k) for k in order}
     mine[0] = own
     theirs = {0: across(own, "sub", 1), 1: diagonal(own)}
-    early = (mine[0], mine[1], theirs[0], theirs[1])
-    theirs[2] = across(mine[2], "sub", 1)
-    theirs[3] = across(mine[3], "sub", 1)
+    theirs |= {k: across(mine[k], "sub", 1) for k in (3, 2)}
     wholes = [shape((width, hid), f32), shape((width, hid), f32), shape((hid, width), f32)]
-    scratch = [
-        pltpu.VMEM((2, strip, hid), f32), pltpu.VMEM((2, strip, hid), f32), pltpu.VMEM((2, narrow, width), f32),
-        pltpu.SemaphoreType.DMA((6,)),
-    ]
-    grads = call(
-        functools.partial(place_kernel, lines, (0, 1)), wholes, *early,
-        out_specs=[HBM] * 3, scratch=scratch, flops=10**8,
-    )
-    grads = call(
-        functools.partial(place_kernel, lines, (2, 3)), wholes,
-        mine[2], mine[3], theirs[2], theirs[3], *grads,
-        specs=[VMEM] * 4 + [HBM] * 3, out_specs=[HBM] * 3, scratch=scratch,
-        input_output_aliases={4: 0, 5: 1, 6: 2},
-    )
+
+    def placed(which, *before):
+        count = len(which)
+        return call(
+            functools.partial(place_kernel, which), wholes,
+            *[mine[k] for k in which], *[theirs[k] for k in which], *before,
+            specs=[VMEM] * (2 * count) + [HBM] * len(before),
+            out_specs=[HBM] * 3,
+            scratch=[
+                pltpu.VMEM((count, strip, hid), f32), pltpu.VMEM((count, strip, hid), f32),
+                pltpu.VMEM((count, narrow, width), f32), pltpu.SemaphoreType.DMA((3 * count,)),
+            ],
+            input_output_aliases={2 * count + i: i for i in range(len(before))},
+        )
+
+    grads = placed((2,), *placed((0,1,3)))
     return (*grads, tail), node_part
 
 
@@ -596,7 +592,6 @@
         scratch=[
             pltpu.VMEM((hid, width), bf16),
             pltpu.VMEM((2 * halo, hid), bf16),
-            pltpu.VMEM((2, width, hid), bf16),
         ],
     )
 

time: 46.5 us -> 46.3 us (level)
  no operation moved by 1% of the time
where the time goes in v18:
time: 46.3 us; the launch traced here: 46.2 us
  starting transfers between devices  26.7 us (58%)
  waiting for transfers between devices  10.3 us (22%)
  Pallas kernels  8.43 us (18%)
  between operations  0.73 us (2%)
    ppermute x14, starting transfers between devices, across(): return lax.ppermute(x, axis, [(i, i ^ k) for i in range(count)])  18.2 us
    ppermute x14, waiting for transfers between devices, across(): return lax.ppermute(x, axis, [(i, i ^ k) for i in range(count)])  9.94 us
    pallas_call x10, Pallas kernels, call(): pl.pallas_call(kernel, out_shape=outs, in_specs=specs or [VMEM] * len(arg...  8.43 us
    ppermute x5, starting transfers between devices, shifted(): return lax.ppermute(x, axis, [(i, (i + by) % count) for i in range(count)])  6.98 us
    ppermute x1, starting transfers between devices, diagonal(): return lax.ppermute(x, ('mesh', 'sub'), moves)  1.58 us
  transfers between devices with their start and end apart: 20, of which 7 were waited for; matrix products, arithmetic and copies ran while one was open for 0% of the time, Pallas kernels for 9%

profile of v18, /device:TPU:0, one launch (start us, length us, event | category | flops | bytes accessed | tf_op | source)
XLA Modules:
  0.0 46.2 jit_solution(11373293603680495508)
XLA Ops:
  0.6 1.3 %shard_map.162 = (bf16[128,512]{1,0:T(8,128)(2,1)S(1)}, s32[1,4,32]{2,1,0:T(4,128)S(1)}, bf16[1552,256]{1,0:T(8,128)(2,1)S(1)}, bf16[32,512]{1,0:T(8,128)(2,1)S(...) custom-call(bf16[128,512]{1,0:T(8,128)(2,1)} %node_hbm.1, s32[1,4,32]{2,1,0:T(4,128)} %send_hbm.1, ...), custom_call_target="tpu_custom_call" | custom-call | flops 100000000 | bytes 1000000 | tf_op jit(solution)/shard_map/pallas_call | solution.py:430
  1.9 0.5 %collective-permute-start = (bf16[1552,256]{1,0:T(8,128)(2,1)S(1)}, bf16[1552,256]{1,0:T(8,128)(2,1)S(1)}, u32[]{:S(2)}, u32[]{:S(2)}) collective-permute-start(bf16[1552,256]{1,0:T(8,128)(2,1)S(1)} %get-tuple-element.48.packed_ref), channel_id=1, source_target_pairs={{0,1},{1,0},{2,3},{3,2},{4,5},{5,4},{6,7},{7,6},{8,9},{9,8},{10,11... | collective-permute-start | bytes 2383880 | tf_op jit(solution)/shard_map/ppermute | solution.py:444
  2.4 2.6 %collective-permute-start.3 = (bf16[64,512]{1,0:T(8,128)(2,1)S(1)}, bf16[64,512]{1,0:T(8,128)(2,1)S(1)}, u32[]{:S(2)}, u32[]{:S(2)}) collective-permute-start(bf16[64,512]{1,0:T(8,128)(2,1)S(1)} %get-tuple-element.58), channel_id=1, source_target_pairs={{0,2},{2,0},{1,3},{3,1},{4,6},{6,4},{5,7},{7,5},{8,10},{10,8},{9,1... | collective-permute-start | bytes 196616 | tf_op jit(solution)/shard_map/ppermute | solution.py:444
  5.0 1.6 %collective-permute-start.1 = (bf16[32,512]{1,0:T(8,128)(2,1)S(1)}, bf16[32,512]{1,0:T(8,128)(2,1)S(1)}, u32[]{:S(2)}, u32[]{:S(2)}) collective-permute-start(bf16[32,512]{1,0:T(8,128)(2,1)S(1)} %get-tuple-element.56), channel_id=1, source_target_pairs={{0,4},{4,8},{8,12},{12,0},{1,5},{5,9},{9,13},{13,1},{2,6},{6,10},{... | collective-permute-start | bytes 98312 | tf_op jit(solution)/shard_map/ppermute | solution.py:444
  6.6 2.2 %collective-permute-start.2 = (bf16[32,512]{1,0:T(8,128)(2,1)S(1)}, bf16[32,512]{1,0:T(8,128)(2,1)S(1)}, u32[]{:S(2)}, u32[]{:S(2)}) collective-permute-start(bf16[32,512]{1,0:T(8,128)(2,1)S(1)} %get-tuple-element.57), channel_id=1, source_target_pairs={{0,12},{4,0},{8,4},{12,8},{1,13},{5,1},{9,5},{13,9},{2,14},{6,2},{... | collective-permute-start | bytes 98312 | tf_op jit(solution)/shard_map/ppermute | solution.py:444
  8.8 0.0 collective-permute-done.other_ref
  8.8 1.7 %shard_map.163 = (f32[512,512]{1,0:T(8,128)S(1)}, bf16[512,128]{1,0:T(8,128)(2,1)S(1)}, bf16[128,512]{1,0:T(8,128)(2,1)S(1)}, bf16[512,128]{1,0:T(8,128)(2,1)S(1...) custom-call(bf16[128,512]{1,0:T(8,128)(2,1)S(1)} %get-tuple-element.47.node_ref, ...), custom_call_target="tpu_custom_call" | custom-call | flops 100000000 | bytes 1000000 | tf_op jit(solution)/shard_map/pallas_call | solution.py:430
  10.5 0.3 collective-permute-done.1.rest_0_
  10.8 0.0 collective-permute-done.2.rest_1_
  10.8 0.0 collective-permute-done.3.rest_2_
  10.8 2.3 %shard_map.164 = (f32[128,512]{1,0:T(8,128)S(1)}, f32[128,256]{1,0:T(8,128)S(1)}, bf16[128,256]{1,0:T(8,128)(2,1)S(1)}, bf16[592,256]{1,0:T(8,128)(2,1)S(1)}, bf...) custom-call(bf16[128,512]{1,0:T(8,128)(2,1)S(1)} %get-tuple-element., ...), custom_call_target="tpu_custom_call" | custom-call | flops 100000000 | bytes 1000000 | tf_op jit(solution)/shard_map/pallas_call | solution.py:430
  13.1 0.6 %collective-permute-start.6 = (bf16[592,256]{1,0:T(8,128)(2,1)S(1)}, bf16[592,256]{1,0:T(8,128)(2,1)S(1)}, u32[]{:S(2)}, u32[]{:S(2)}) collective-permute-start(bf16[592,256]{1,0:T(8,128)(2,1)S(1)} %get-tuple-element.65), channel_id=1, source_target_pairs={{0,2},{2,0},{1,3},{3,1},{4,6},{6,4},{5,7},{7,5},{8,10},{10,8},{9,1... | collective-permute-start | bytes 909320 | tf_op jit(solution)/shard_map/ppermute | solution.py:449
  13.7 3.5 %collective-permute-start.4 = (bf16[80,512]{1,0:T(8,128)(2,1)S(1)}, bf16[80,512]{1,0:T(8,128)(2,1)S(1)}, u32[]{:S(2)}, u32[]{:S(2)}) collective-permute-start(bf16[80,512]{1,0:T(8,128)(2,1)S(1)} %get-tuple-element.63), channel_id=1, source_target_pairs={{0,12},{4,8},{8,4},{12,0},{1,13},{5,9},{9,5},{13,1},{2,14},{6,10},... | collective-permute-start | bytes 245768 | tf_op jit(solution)/shard_map/ppermute | solution.py:449
  17.2 0.0 collective-permute-start.5
  17.2 0.9 %collective-permute-start.11 = (bf16[64,512]{1,0:T(8,128)(2,1)S(1)}, bf16[64,512]{1,0:T(8,128)(2,1)S(1)}, u32[]{:S(2)}, u32[]{:S(2)}) collective-permute-start(bf16[64,512]{1,0:T(8,128)(2,1)S(1)} %get-tuple-element.71), channel_id=1, source_target_pairs={{0,8},{4,12},{8,0},{12,4},{1,9},{5,13},{9,1},{13,5},{2,10},{6,14},... | collective-permute-start | bytes 196616 | tf_op jit(solution)/shard_map/ppermute | solution.py:449
  18.1 3.5 %collective-permute-done.6.pair_ref.arrived_ref = bf16[592,256]{1,0:T(8,128)(2,1)S(1)} collective-permute-done((bf16[592,256]{1,0:T(8,128)(2,1)S(1)}, bf16[592,256]{1,0:T(8,128)(2,1)S(1)}, u32[]{:S(2)}, u32[]{:S(2)}) %collective-permute-start.6) | collective-permute-done | bytes 303136 | tf_op jit(solution)/shard_map/ppermute | solution.py:449
  21.7 0.1 shard_map.166
  21.7 3.2 %collective-permute-start.8 = (bf16[144,256]{1,0:T(8,128)(2,1)S(1)}, bf16[144,256]{1,0:T(8,128)(2,1)S(1)}, u32[]{:S(2)}, u32[]{:S(2)}) collective-permute-start(bf16[144,256]{1,0:T(8,128)(2,1)S(1)} %get-tuple-element.67), channel_id=1, source_target_pairs={{0,12},{4,8},{8,4},{12,0},{1,13},{5,9},{9,5},{13,1},{2,14},{6,10},... | collective-permute-start | bytes 221192 | tf_op jit(solution)/shard_map/ppermute | solution.py:449
  24.9 0.0 collective-permute-start.9
  24.9 0.0 collective-permute-done.11.refs_1_
  24.9 1.3 %collective-permute-start.10 = (bf16[144,256]{1,0:T(8,128)(2,1)S(1)}, bf16[144,256]{1,0:T(8,128)(2,1)S(1)}, u32[]{:S(2)}, u32[]{:S(2)}) collective-permute-start(bf16[144,256]{1,0:T(8,128)(2,1)S(1)} %get-tuple-element.69), channel_id=1, source_target_pairs={{0,4},{4,0},{8,12},{12,8},{1,5},{5,1},{9,13},{13,9},{2,6},{6,2},{1... | collective-permute-start | bytes 221192 | tf_op jit(solution)/shard_map/ppermute | solution.py:449
  26.2 0.0 collective-permute-done.4.three_ref.refs_0_
  26.2 0.0 collective-permute-done.5.one_ref.refs_2_
  26.2 0.6 %collective-permute-start.12 = (bf16[64,256]{1,0:T(8,128)(2,1)S(1)}, bf16[64,256]{1,0:T(8,128)(2,1)S(1)}, u32[]{:S(2)}, u32[]{:S(2)}) collective-permute-start(bf16[64,256]{1,0:T(8,128)(2,1)S(1)} %get-tuple-element.74), channel_id=1, source_target_pairs={{0,2},{2,0},{1,3},{3,1},{4,6},{6,4},{5,7},{7,5},{8,10},{10,8},{9,1... | collective-permute-start | bytes 98312 | tf_op jit(solution)/shard_map/ppermute | solution.py:449
  26.8 0.4 shard_map.165.own_ref
  27.2 0.1 collective-permute-start.7
  27.3 2.9 %collective-permute-done.12.refs_5_ = bf16[64,256]{1,0:T(8,128)(2,1)S(1)} collective-permute-done((bf16[64,256]{1,0:T(8,128)(2,1)S(1)}, bf16[64,256]{1,0:T(8,128)(2,1)S(1)}, u32[]{:S(2)}, u32[]{:S(2)}) %collective-permute-start.12) | collective-permute-done | bytes 32800 | tf_op jit(solution)/shard_map/ppermute | solution.py:449
  30.2 0.0 collective-permute-done.8.refs_0_
  30.2 0.1 collective-permute-done.9.refs_1_
  30.3 0.0 collective-permute-done.10.refs_2_
  30.4 3.1 %collective-permute-start.16 = (bf16[192,256]{1,0:T(8,128)(2,1)S(1)}, bf16[192,256]{1,0:T(8,128)(2,1)S(1)}, u32[]{:S(2)}, u32[]{:S(2)}) collective-permute-start(bf16[192,256]{1,0:T(8,128)(2,1)S(1)} %get-tuple-element.78.refs_0_), channel_id=1, source_target_pairs={{0,12},{4,8},{8,4},{12,0},{1,13},{5,9},{9,5},{13,1},{2,14},{6,10},... | collective-permute-start | bytes 294920 | tf_op jit(solution)/shard_map/ppermute | solution.py:449
  33.5 0.0 collective-permute-start.13
  33.5 1.6 %collective-permute-start.18 = (bf16[192,256]{1,0:T(8,128)(2,1)S(1)}, bf16[192,256]{1,0:T(8,128)(2,1)S(1)}, u32[]{:S(2)}, u32[]{:S(2)}) collective-permute-start(bf16[192,256]{1,0:T(8,128)(2,1)S(1)} %get-tuple-element.78.refs_0_), channel_id=1, source_target_pairs={{0,6},{2,4},{4,2},{6,0},{8,14},{10,12},{12,10},{14,8},{1,7},{3,5},... | collective-permute-start | bytes 294920 | tf_op jit(solution)/shard_map/ppermute | solution.py:455
  35.0 1.2 %collective-permute-start.17 = (bf16[192,256]{1,0:T(8,128)(2,1)S(1)}, bf16[192,256]{1,0:T(8,128)(2,1)S(1)}, u32[]{:S(2)}, u32[]{:S(2)}) collective-permute-start(bf16[192,256]{1,0:T(8,128)(2,1)S(1)} %get-tuple-element.78.refs_0_), channel_id=1, source_target_pairs={{0,2},{2,0},{1,3},{3,1},{4,6},{6,4},{5,7},{7,5},{8,10},{10,8},{9,1... | collective-permute-start | bytes 294920 | tf_op jit(solution)/shard_map/ppermute | solution.py:449
  36.3 0.0 collective-permute-done.7.other_ref
  36.3 0.7 %collective-permute-start.15 = (bf16[192,256]{1,0:T(8,128)(2,1)S(1)}, bf16[192,256]{1,0:T(8,128)(2,1)S(1)}, u32[]{:S(2)}, u32[]{:S(2)}) collective-permute-start(bf16[192,256]{1,0:T(8,128)(2,1)S(1)} %get-tuple-element.78.refs_0_), channel_id=1, source_target_pairs={{0,4},{4,0},{8,12},{12,8},{1,5},{5,1},{9,13},{13,9},{2,6},{6,2},{1... | collective-permute-start | bytes 294920 | tf_op jit(solution)/shard_map/ppermute | solution.py:449
  37.0 0.3 collective-permute-done.16.refs_2_
  37.3 1.5 %collective-permute-start.19 = (bf16[192,256]{1,0:T(8,128)(2,1)S(1)}, bf16[192,256]{1,0:T(8,128)(2,1)S(1)}, u32[]{:S(2)}, u32[]{:S(2)}) collective-permute-start(bf16[192,256]{1,0:T(8,128)(2,1)S(1)} %collective-permute-done.16.refs_2_), channel_id=1, source_target_pairs={{0,2},{2,0},{1,3},{3,1},{4,6},{6,4},{5,7},{7,5},{8,10},{10,8},{9,1... | collective-permute-start | bytes 294920 | tf_op jit(solution)/shard_map/ppermute | solution.py:449
  38.8 2.0 %collective-permute-done.13.refs_0_ = bf16[192,256]{1,0:T(8,128)(2,1)S(1)} collective-permute-done((bf16[192,256]{1,0:T(8,128)(2,1)S(1)}, bf16[192,256]{1,0:T(8,128)(2,1)S(1)}, u32[]{:S(2)}, u32[]{:S(2)}) %collective-permute-start.13) | collective-permute-done | bytes 98336 | tf_op jit(solution)/shard_map/ppermute | solution.py:449
  40.8 1.6 %collective-permute-start.14 = (bf16[192,256]{1,0:T(8,128)(2,1)S(1)}, bf16[192,256]{1,0:T(8,128)(2,1)S(1)}, u32[]{:S(2)}, u32[]{:S(2)}) collective-permute-start(bf16[192,256]{1,0:T(8,128)(2,1)S(1)} %collective-permute-done.13.refs_0_), channel_id=1, source_target_pairs={{0,2},{2,0},{1,3},{3,1},{4,6},{6,4},{5,7},{7,5},{8,10},{10,8},{9,1... | collective-permute-start | bytes 294920 | tf_op jit(solution)/shard_map/ppermute | solution.py:449
  42.4 0.8 %shard_map.169 = (f32[128,512]{1,0:T(8,128)}, bf16[128,512]{1,0:T(8,128)(2,1)}, f32[1,256]{1,0:T(1,128)}, f32[1,512]{1,0:T(1,128)}) custom-call(bf16[128,512]{1,0:T(8,128)(2,1)S(1)} %get-tuple-element.49.cot_ref, bf16[128,512]{1,0:T(8,128)(2,1)S(1)} %get-tuple-element.47.node_ref, f32[1,512]{1,0:T(1,128)S(1)} %get-tuple-element.50.gain_ref, ...), custom_call_target="tpu_custom_call" | custom-call | flops 100000000 | bytes 1000000 | tf_op jit(solution)/shard_map/pallas_call | solution.py:430
  43.2 0.0 collective-permute-done.18.refs_4_
  43.2 0.0 collective-permute-done.17.refs_3_
  43.2 0.0 collective-permute-done.15.refs_1_
  43.2 0.0 collective-permute-done.19.refs_5_
  43.2 1.1 %shard_map.170 = (f32[512,256]{1,0:T(8,128)}, f32[512,256]{1,0:T(8,128)}, f32[256,512]{1,0:T(8,128)}) custom-call(bf16[192,256]{1,0:T(8,128)(2,1)S(1)} %get-tuple-element.78.refs_0_, bf16[192,256]{1,0:T(8,128)(2,1)S(1)} %collective-permute-done.15.refs_1_, bf16[192,256]{1,0:T(8,128)(2,1)S(1)} %collective-permute-done.16.refs_2_, ...), custom_call_target="tpu_custom_call" | custom-call | flops 100000000 | bytes 1000000 | tf_op jit(solution)/shard_map/pallas_call | solution.py:430
  44.3 1.1 %collective-permute-done.14.refs_1_ = bf16[192,256]{1,0:T(8,128)(2,1)S(1)} collective-permute-done((bf16[192,256]{1,0:T(8,128)(2,1)S(1)}, bf16[192,256]{1,0:T(8,128)(2,1)S(1)}, u32[]{:S(2)}, u32[]{:S(2)}) %collective-permute-start.14) | collective-permute-done | bytes 98336 | tf_op jit(solution)/shard_map/ppermute | solution.py:449
  45.4 0.8 %shard_map.171 = (f32[512,256]{1,0:T(8,128)}, f32[512,256]{1,0:T(8,128)}, f32[256,512]{1,0:T(8,128)}) custom-call(bf16[192,256]{1,0:T(8,128)(2,1)S(1)} %collective-permute-done.13.refs_0_, bf16[192,256]{1,0:T(8,128)(2,1)S(1)} %collective-permute-done.14.refs_1_, ...), custom_call_target="tpu_custom_call", output_to_operand_aliasing={{0}: (2, {}), {1}: (3, {}), {2}: (4, {})} | custom-call | flops 100000000 | bytes 1000000 | tf_op jit(solution)/shard_map/pallas_call | solution.py:430
  (2 shorter events, 0.1 us)
Async XLA Ops:
  1.9 6.9 %collective-permute-start = (bf16[1552,256]{1,0:T(8,128)(2,1)S(1)}, bf16[1552,256]{1,0:T(8,128)(2,1)S(1)}, u32[]{:S(2)}, u32[]{:S(2)}) collective-permute-start(bf16[1552,256]{1,0:T(8,128)(2,1)S(1)} %get-tuple-element.48.packed_ref), channel_id=1, source_target_pairs={{0,1},{1,0},{2,3},{3,2},{4,5},{5,4},{6,7},{7,6},{8,9},{9,8},{10,11... | collective-permute-start | bytes 2383880 | tf_op jit(solution)/shard_map/ppermute | solution.py:444
  2.4 8.4 %collective-permute-start.3 = (bf16[64,512]{1,0:T(8,128)(2,1)S(1)}, bf16[64,512]{1,0:T(8,128)(2,1)S(1)}, u32[]{:S(2)}, u32[]{:S(2)}) collective-permute-start(bf16[64,512]{1,0:T(8,128)(2,1)S(1)} %get-tuple-element.58), channel_id=1, source_target_pairs={{0,2},{2,0},{1,3},{3,1},{4,6},{6,4},{5,7},{7,5},{8,10},{10,8},{9,1... | collective-permute-start | bytes 196616 | tf_op jit(solution)/shard_map/ppermute | solution.py:444
  5.0 5.8 %collective-permute-start.1 = (bf16[32,512]{1,0:T(8,128)(2,1)S(1)}, bf16[32,512]{1,0:T(8,128)(2,1)S(1)}, u32[]{:S(2)}, u32[]{:S(2)}) collective-permute-start(bf16[32,512]{1,0:T(8,128)(2,1)S(1)} %get-tuple-element.56), channel_id=1, source_target_pairs={{0,4},{4,8},{8,12},{12,0},{1,5},{5,9},{9,13},{13,1},{2,6},{6,10},{... | collective-permute-start | bytes 98312 | tf_op jit(solution)/shard_map/ppermute | solution.py:444
  6.6 4.3 %collective-permute-start.2 = (bf16[32,512]{1,0:T(8,128)(2,1)S(1)}, bf16[32,512]{1,0:T(8,128)(2,1)S(1)}, u32[]{:S(2)}, u32[]{:S(2)}) collective-permute-start(bf16[32,512]{1,0:T(8,128)(2,1)S(1)} %get-tuple-element.57), channel_id=1, source_target_pairs={{0,12},{4,0},{8,4},{12,8},{1,13},{5,1},{9,5},{13,9},{2,14},{6,2},{... | collective-permute-start | bytes 98312 | tf_op jit(solution)/shard_map/ppermute | solution.py:444
  13.1 8.5 %collective-permute-start.6 = (bf16[592,256]{1,0:T(8,128)(2,1)S(1)}, bf16[592,256]{1,0:T(8,128)(2,1)S(1)}, u32[]{:S(2)}, u32[]{:S(2)}) collective-permute-start(bf16[592,256]{1,0:T(8,128)(2,1)S(1)} %get-tuple-element.65), channel_id=1, source_target_pairs={{0,2},{2,0},{1,3},{3,1},{4,6},{6,4},{5,7},{7,5},{8,10},{10,8},{9,1... | collective-permute-start | bytes 909320 | tf_op jit(solution)/shard_map/ppermute | solution.py:449
  13.7 12.5 %collective-permute-start.4 = (bf16[80,512]{1,0:T(8,128)(2,1)S(1)}, bf16[80,512]{1,0:T(8,128)(2,1)S(1)}, u32[]{:S(2)}, u32[]{:S(2)}) collective-permute-start(bf16[80,512]{1,0:T(8,128)(2,1)S(1)} %get-tuple-element.63), channel_id=1, source_target_pairs={{0,12},{4,8},{8,4},{12,0},{1,13},{5,9},{9,5},{13,1},{2,14},{6,10},... | collective-permute-start | bytes 245768 | tf_op jit(solution)/shard_map/ppermute | solution.py:449
  17.2 9.0 %collective-permute-start.5 = (bf16[80,512]{1,0:T(8,128)(2,1)S(1)}, bf16[80,512]{1,0:T(8,128)(2,1)S(1)}, u32[]{:S(2)}, u32[]{:S(2)}) collective-permute-start(bf16[80,512]{1,0:T(8,128)(2,1)S(1)} %get-tuple-element.64), channel_id=1, source_target_pairs={{0,4},{4,0},{8,12},{12,8},{1,5},{5,1},{9,13},{13,9},{2,6},{6,2},{1... | collective-permute-start | bytes 245768 | tf_op jit(solution)/shard_map/ppermute | solution.py:449
  17.2 7.7 %collective-permute-start.11 = (bf16[64,512]{1,0:T(8,128)(2,1)S(1)}, bf16[64,512]{1,0:T(8,128)(2,1)S(1)}, u32[]{:S(2)}, u32[]{:S(2)}) collective-permute-start(bf16[64,512]{1,0:T(8,128)(2,1)S(1)} %get-tuple-element.71), channel_id=1, source_target_pairs={{0,8},{4,12},{8,0},{12,4},{1,9},{5,13},{9,1},{13,5},{2,10},{6,14},... | collective-permute-start | bytes 196616 | tf_op jit(solution)/shard_map/ppermute | solution.py:449
  21.7 8.5 %collective-permute-start.8 = (bf16[144,256]{1,0:T(8,128)(2,1)S(1)}, bf16[144,256]{1,0:T(8,128)(2,1)S(1)}, u32[]{:S(2)}, u32[]{:S(2)}) collective-permute-start(bf16[144,256]{1,0:T(8,128)(2,1)S(1)} %get-tuple-element.67), channel_id=1, source_target_pairs={{0,12},{4,8},{8,4},{12,0},{1,13},{5,9},{9,5},{13,1},{2,14},{6,10},... | collective-permute-start | bytes 221192 | tf_op jit(solution)/shard_map/ppermute | solution.py:449
  24.9 5.4 %collective-permute-start.9 = (bf16[144,256]{1,0:T(8,128)(2,1)S(1)}, bf16[144,256]{1,0:T(8,128)(2,1)S(1)}, u32[]{:S(2)}, u32[]{:S(2)}) collective-permute-start(bf16[144,256]{1,0:T(8,128)(2,1)S(1)} %get-tuple-element.68), channel_id=1, source_target_pairs={{0,8},{4,12},{8,0},{12,4},{1,9},{5,13},{9,1},{13,5},{2,10},{6,14},... | collective-permute-start | bytes 221192 | tf_op jit(solution)/shard_map/ppermute | solution.py:449
  24.9 5.4 %collective-permute-start.10 = (bf16[144,256]{1,0:T(8,128)(2,1)S(1)}, bf16[144,256]{1,0:T(8,128)(2,1)S(1)}, u32[]{:S(2)}, u32[]{:S(2)}) collective-permute-start(bf16[144,256]{1,0:T(8,128)(2,1)S(1)} %get-tuple-element.69), channel_id=1, source_target_pairs={{0,4},{4,0},{8,12},{12,8},{1,5},{5,1},{9,13},{13,9},{2,6},{6,2},{1... | collective-permute-start | bytes 221192 | tf_op jit(solution)/shard_map/ppermute | solution.py:449
  26.2 4.0 %collective-permute-start.12 = (bf16[64,256]{1,0:T(8,128)(2,1)S(1)}, bf16[64,256]{1,0:T(8,128)(2,1)S(1)}, u32[]{:S(2)}, u32[]{:S(2)}) collective-permute-start(bf16[64,256]{1,0:T(8,128)(2,1)S(1)} %get-tuple-element.74), channel_id=1, source_target_pairs={{0,2},{2,0},{1,3},{3,1},{4,6},{6,4},{5,7},{7,5},{8,10},{10,8},{9,1... | collective-permute-start | bytes 98312 | tf_op jit(solution)/shard_map/ppermute | solution.py:449
  27.2 9.1 %collective-permute-start.7 = (bf16[128,512]{1,0:T(8,128)(2,1)S(1)}, bf16[128,512]{1,0:T(8,128)(2,1)S(1)}, u32[]{:S(2)}, u32[]{:S(2)}) collective-permute-start(bf16[128,512]{1,0:T(8,128)(2,1)S(1)} %shard_map.165.own_ref), channel_id=1, source_target_pairs={{0,1},{1,0},{2,3},{3,2},{4,5},{5,4},{6,7},{7,6},{8,9},{9,8},{10,11... | collective-permute-start | bytes 393224 | tf_op jit(solution)/shard_map/ppermute | solution.py:444
  30.4 6.9 %collective-permute-start.16 = (bf16[192,256]{1,0:T(8,128)(2,1)S(1)}, bf16[192,256]{1,0:T(8,128)(2,1)S(1)}, u32[]{:S(2)}, u32[]{:S(2)}) collective-permute-start(bf16[192,256]{1,0:T(8,128)(2,1)S(1)} %get-tuple-element.78.refs_0_), channel_id=1, source_target_pairs={{0,12},{4,8},{8,4},{12,0},{1,13},{5,9},{9,5},{13,1},{2,14},{6,10},... | collective-permute-start | bytes 294920 | tf_op jit(solution)/shard_map/ppermute | solution.py:449
  33.5 7.3 %collective-permute-start.13 = (bf16[192,256]{1,0:T(8,128)(2,1)S(1)}, bf16[192,256]{1,0:T(8,128)(2,1)S(1)}, u32[]{:S(2)}, u32[]{:S(2)}) collective-permute-start(bf16[192,256]{1,0:T(8,128)(2,1)S(1)} %get-tuple-element.78.refs_0_), channel_id=1, source_target_pairs={{0,8},{4,12},{8,0},{12,4},{1,9},{5,13},{9,1},{13,5},{2,10},{6,14},... | collective-permute-start | bytes 294920 | tf_op jit(solution)/shard_map/ppermute | solution.py:449
  33.5 9.7 %collective-permute-start.18 = (bf16[192,256]{1,0:T(8,128)(2,1)S(1)}, bf16[192,256]{1,0:T(8,128)(2,1)S(1)}, u32[]{:S(2)}, u32[]{:S(2)}) collective-permute-start(bf16[192,256]{1,0:T(8,128)(2,1)S(1)} %get-tuple-element.78.refs_0_), channel_id=1, source_target_pairs={{0,6},{2,4},{4,2},{6,0},{8,14},{10,12},{12,10},{14,8},{1,7},{3,5},... | collective-permute-start | bytes 294920 | tf_op jit(solution)/shard_map/ppermute | solution.py:455
  35.0 8.1 %collective-permute-start.17 = (bf16[192,256]{1,0:T(8,128)(2,1)S(1)}, bf16[192,256]{1,0:T(8,128)(2,1)S(1)}, u32[]{:S(2)}, u32[]{:S(2)}) collective-permute-start(bf16[192,256]{1,0:T(8,128)(2,1)S(1)} %get-tuple-element.78.refs_0_), channel_id=1, source_target_pairs={{0,2},{2,0},{1,3},{3,1},{4,6},{6,4},{5,7},{7,5},{8,10},{10,8},{9,1... | collective-permute-start | bytes 294920 | tf_op jit(solution)/shard_map/ppermute | solution.py:449
  36.3 6.9 %collective-permute-start.15 = (bf16[192,256]{1,0:T(8,128)(2,1)S(1)}, bf16[192,256]{1,0:T(8,128)(2,1)S(1)}, u32[]{:S(2)}, u32[]{:S(2)}) collective-permute-start(bf16[192,256]{1,0:T(8,128)(2,1)S(1)} %get-tuple-element.78.refs_0_), channel_id=1, source_target_pairs={{0,4},{4,0},{8,12},{12,8},{1,5},{5,1},{9,13},{13,9},{2,6},{6,2},{1... | collective-permute-start | bytes 294920 | tf_op jit(solution)/shard_map/ppermute | solution.py:449
  37.3 5.9 %collective-permute-start.19 = (bf16[192,256]{1,0:T(8,128)(2,1)S(1)}, bf16[192,256]{1,0:T(8,128)(2,1)S(1)}, u32[]{:S(2)}, u32[]{:S(2)}) collective-permute-start(bf16[192,256]{1,0:T(8,128)(2,1)S(1)} %collective-permute-done.16.refs_2_), channel_id=1, source_target_pairs={{0,2},{2,0},{1,3},{3,1},{4,6},{6,4},{5,7},{7,5},{8,10},{10,8},{9,1... | collective-permute-start | bytes 294920 | tf_op jit(solution)/shard_map/ppermute | solution.py:449
  40.8 4.6 %collective-permute-start.14 = (bf16[192,256]{1,0:T(8,128)(2,1)S(1)}, bf16[192,256]{1,0:T(8,128)(2,1)S(1)}, u32[]{:S(2)}, u32[]{:S(2)}) collective-permute-start(bf16[192,256]{1,0:T(8,128)(2,1)S(1)} %collective-permute-done.13.refs_0_), channel_id=1, source_target_pairs={{0,2},{2,0},{1,3},{3,1},{4,6},{6,4},{5,7},{7,5},{8,10},{10,8},{9,1... | collective-permute-start | bytes 294920 | tf_op jit(solution)/shard_map/ppermute | solution.py:449

commit v19 on v18

--- a/solution.py
+++ b/solution.py
@@ -473,7 +473,7 @@
     own, tail = call(
         own_kernel,
         [shape((strip + narrow, hid), bf16), shape((TAIL, hid), f32)],
-        *[line_terms[k] for k in order], line[0], out_keep, across(out_send, "sub", 1),
+        *[line_terms[k] for k in (2, 3, 1)], line[0], out_keep, across(out_send, "sub", 1),
         flops=10**8,
     )
     mine = {k: across(own, "mesh", k) for k in order}

time: 46.3 us -> 46 us (level)
  starting transfers between devices: 26.7 us -> 25 us
  waiting for transfers between devices: 10.3 us -> 11.7 us
    ppermute x14, starting transfers between devices: 18.2 us -> 15.9 us  [across(): return lax.ppermute(x, axis, [(i, i ^ k) for i in range(count)])]
    ppermute x14, waiting for transfers between devices: 9.94 us -> 11.3 us  [across(): return lax.ppermute(x, axis, [(i, i ^ k) for i in range(count)])]
    ppermute x1, starting transfers between devices: 1.58 us -> 2.06 us  [diagonal(): return lax.ppermute(x, ('mesh', 'sub'), moves)]
  transfers between devices with their start and end apart: 20 -> 20, of which waited for: 7 -> 9; matrix products, arithmetic and copies ran while one was open for 0% -> 0% of each run, Pallas kernels for 9% -> 9%
where the time goes in v19:
time: 46 us; the launch traced here: 45.8 us
  starting transfers between devices  25 us (54%)
  waiting for transfers between devices  11.7 us (25%)
  Pallas kernels  8.43 us (18%)
  between operations  0.72 us (2%)
    ppermute x14, starting transfers between devices, across(): return lax.ppermute(x, axis, [(i, i ^ k) for i in range(count)])  15.9 us
    ppermute x14, waiting for transfers between devices, across(): return lax.ppermute(x, axis, [(i, i ^ k) for i in range(count)])  11.3 us
    pallas_call x10, Pallas kernels, call(): pl.pallas_call(kernel, out_shape=outs, in_specs=specs or [VMEM] * len(arg...  8.43 us
    ppermute x5, starting transfers between devices, shifted(): return lax.ppermute(x, axis, [(i, (i + by) % count) for i in range(count)])  6.98 us
    ppermute x1, starting transfers between devices, diagonal(): return lax.ppermute(x, ('mesh', 'sub'), moves)  2.06 us
  transfers between devices with their start and end apart: 20, of which 9 were waited for; matrix products, arithmetic and copies ran while one was open for 0% of the time, Pallas kernels for 9%

profile of v19, /device:TPU:0, one launch (start us, length us, event | category | flops | bytes accessed | tf_op | source)
XLA Modules:
  0.0 45.8 jit_solution(17602743456313045638)
XLA Ops:
  0.6 1.3 %shard_map.162 = (bf16[128,512]{1,0:T(8,128)(2,1)S(1)}, s32[1,4,32]{2,1,0:T(4,128)S(1)}, bf16[1552,256]{1,0:T(8,128)(2,1)S(1)}, bf16[32,512]{1,0:T(8,128)(2,1)S(...) custom-call(bf16[128,512]{1,0:T(8,128)(2,1)} %node_hbm.1, s32[1,4,32]{2,1,0:T(4,128)} %send_hbm.1, ...), custom_call_target="tpu_custom_call" | custom-call | flops 100000000 | bytes 1000000 | tf_op jit(solution)/shard_map/pallas_call | solution.py:430
  1.9 0.5 %collective-permute-start = (bf16[1552,256]{1,0:T(8,128)(2,1)S(1)}, bf16[1552,256]{1,0:T(8,128)(2,1)S(1)}, u32[]{:S(2)}, u32[]{:S(2)}) collective-permute-start(bf16[1552,256]{1,0:T(8,128)(2,1)S(1)} %get-tuple-element.48.packed_ref), channel_id=1, source_target_pairs={{0,1},{1,0},{2,3},{3,2},{4,5},{5,4},{6,7},{7,6},{8,9},{9,8},{10,11... | collective-permute-start | bytes 2383880 | tf_op jit(solution)/shard_map/ppermute | solution.py:444
  2.4 2.6 %collective-permute-start.3 = (bf16[64,512]{1,0:T(8,128)(2,1)S(1)}, bf16[64,512]{1,0:T(8,128)(2,1)S(1)}, u32[]{:S(2)}, u32[]{:S(2)}) collective-permute-start(bf16[64,512]{1,0:T(8,128)(2,1)S(1)} %get-tuple-element.58), channel_id=1, source_target_pairs={{0,2},{2,0},{1,3},{3,1},{4,6},{6,4},{5,7},{7,5},{8,10},{10,8},{9,1... | collective-permute-start | bytes 196616 | tf_op jit(solution)/shard_map/ppermute | solution.py:444
  5.0 1.6 %collective-permute-start.1 = (bf16[32,512]{1,0:T(8,128)(2,1)S(1)}, bf16[32,512]{1,0:T(8,128)(2,1)S(1)}, u32[]{:S(2)}, u32[]{:S(2)}) collective-permute-start(bf16[32,512]{1,0:T(8,128)(2,1)S(1)} %get-tuple-element.56), channel_id=1, source_target_pairs={{0,4},{4,8},{8,12},{12,0},{1,5},{5,9},{9,13},{13,1},{2,6},{6,10},{... | collective-permute-start | bytes 98312 | tf_op jit(solution)/shard_map/ppermute | solution.py:444
  6.6 2.2 %collective-permute-start.2 = (bf16[32,512]{1,0:T(8,128)(2,1)S(1)}, bf16[32,512]{1,0:T(8,128)(2,1)S(1)}, u32[]{:S(2)}, u32[]{:S(2)}) collective-permute-start(bf16[32,512]{1,0:T(8,128)(2,1)S(1)} %get-tuple-element.57), channel_id=1, source_target_pairs={{0,12},{4,0},{8,4},{12,8},{1,13},{5,1},{9,5},{13,9},{2,14},{6,2},{... | collective-permute-start | bytes 98312 | tf_op jit(solution)/shard_map/ppermute | solution.py:444
  8.8 0.0 collective-permute-done.other_ref
  8.8 1.7 %shard_map.163 = (f32[512,512]{1,0:T(8,128)S(1)}, bf16[512,128]{1,0:T(8,128)(2,1)S(1)}, bf16[128,512]{1,0:T(8,128)(2,1)S(1)}, bf16[512,128]{1,0:T(8,128)(2,1)S(1...) custom-call(bf16[128,512]{1,0:T(8,128)(2,1)S(1)} %get-tuple-element.47.node_ref, ...), custom_call_target="tpu_custom_call" | custom-call | flops 100000000 | bytes 1000000 | tf_op jit(solution)/shard_map/pallas_call | solution.py:430
  10.5 0.3 collective-permute-done.1.rest_0_
  10.8 0.0 collective-permute-done.2.rest_1_
  10.8 0.0 collective-permute-done.3.rest_2_
  10.8 2.3 %shard_map.164 = (f32[128,512]{1,0:T(8,128)S(1)}, f32[128,256]{1,0:T(8,128)S(1)}, bf16[128,256]{1,0:T(8,128)(2,1)S(1)}, bf16[592,256]{1,0:T(8,128)(2,1)S(1)}, bf...) custom-call(bf16[128,512]{1,0:T(8,128)(2,1)S(1)} %get-tuple-element., ...), custom_call_target="tpu_custom_call" | custom-call | flops 100000000 | bytes 1000000 | tf_op jit(solution)/shard_map/pallas_call | solution.py:430
  13.1 0.6 %collective-permute-start.6 = (bf16[592,256]{1,0:T(8,128)(2,1)S(1)}, bf16[592,256]{1,0:T(8,128)(2,1)S(1)}, u32[]{:S(2)}, u32[]{:S(2)}) collective-permute-start(bf16[592,256]{1,0:T(8,128)(2,1)S(1)} %get-tuple-element.65), channel_id=1, source_target_pairs={{0,2},{2,0},{1,3},{3,1},{4,6},{6,4},{5,7},{7,5},{8,10},{10,8},{9,1... | collective-permute-start | bytes 909320 | tf_op jit(solution)/shard_map/ppermute | solution.py:449
  13.7 3.5 %collective-permute-start.4 = (bf16[80,512]{1,0:T(8,128)(2,1)S(1)}, bf16[80,512]{1,0:T(8,128)(2,1)S(1)}, u32[]{:S(2)}, u32[]{:S(2)}) collective-permute-start(bf16[80,512]{1,0:T(8,128)(2,1)S(1)} %get-tuple-element.63), channel_id=1, source_target_pairs={{0,12},{4,8},{8,4},{12,0},{1,13},{5,9},{9,5},{13,1},{2,14},{6,10},... | collective-permute-start | bytes 245768 | tf_op jit(solution)/shard_map/ppermute | solution.py:449
  17.2 0.0 collective-permute-start.5
  17.2 0.9 %collective-permute-start.11 = (bf16[64,512]{1,0:T(8,128)(2,1)S(1)}, bf16[64,512]{1,0:T(8,128)(2,1)S(1)}, u32[]{:S(2)}, u32[]{:S(2)}) collective-permute-start(bf16[64,512]{1,0:T(8,128)(2,1)S(1)} %get-tuple-element.71), channel_id=1, source_target_pairs={{0,8},{4,12},{8,0},{12,4},{1,9},{5,13},{9,1},{13,5},{2,10},{6,14},... | collective-permute-start | bytes 196616 | tf_op jit(solution)/shard_map/ppermute | solution.py:449
  18.1 3.5 %collective-permute-done.6.pair_ref.arrived_ref = bf16[592,256]{1,0:T(8,128)(2,1)S(1)} collective-permute-done((bf16[592,256]{1,0:T(8,128)(2,1)S(1)}, bf16[592,256]{1,0:T(8,128)(2,1)S(1)}, u32[]{:S(2)}, u32[]{:S(2)}) %collective-permute-start.6) | collective-permute-done | bytes 303136 | tf_op jit(solution)/shard_map/ppermute | solution.py:449
  21.7 0.1 shard_map.166
  21.7 1.7 %collective-permute-start.8 = (bf16[144,256]{1,0:T(8,128)(2,1)S(1)}, bf16[144,256]{1,0:T(8,128)(2,1)S(1)}, u32[]{:S(2)}, u32[]{:S(2)}) collective-permute-start(bf16[144,256]{1,0:T(8,128)(2,1)S(1)} %get-tuple-element.67), channel_id=1, source_target_pairs={{0,8},{4,12},{8,0},{12,4},{1,9},{5,13},{9,1},{13,5},{2,10},{6,14},... | collective-permute-start | bytes 221192 | tf_op jit(solution)/shard_map/ppermute | solution.py:449
  23.4 1.6 %collective-permute-start.9 = (bf16[144,256]{1,0:T(8,128)(2,1)S(1)}, bf16[144,256]{1,0:T(8,128)(2,1)S(1)}, u32[]{:S(2)}, u32[]{:S(2)}) collective-permute-start(bf16[144,256]{1,0:T(8,128)(2,1)S(1)} %get-tuple-element.68), channel_id=1, source_target_pairs={{0,12},{4,8},{8,4},{12,0},{1,13},{5,9},{9,5},{13,1},{2,14},{6,10},... | collective-permute-start | bytes 221192 | tf_op jit(solution)/shard_map/ppermute | solution.py:449
  25.0 0.0 collective-permute-done.11.refs_1_
  25.0 0.5 %collective-permute-start.10 = (bf16[144,256]{1,0:T(8,128)(2,1)S(1)}, bf16[144,256]{1,0:T(8,128)(2,1)S(1)}, u32[]{:S(2)}, u32[]{:S(2)}) collective-permute-start(bf16[144,256]{1,0:T(8,128)(2,1)S(1)} %get-tuple-element.69), channel_id=1, source_target_pairs={{0,4},{4,0},{8,12},{12,8},{1,5},{5,1},{9,13},{13,9},{2,6},{6,2},{1... | collective-permute-start | bytes 221192 | tf_op jit(solution)/shard_map/ppermute | solution.py:449
  25.5 0.0 collective-permute-done.4.three_ref.refs_0_
  25.5 0.0 collective-permute-done.5.one_ref.refs_2_
  25.5 1.2 %collective-permute-start.12 = (bf16[64,256]{1,0:T(8,128)(2,1)S(1)}, bf16[64,256]{1,0:T(8,128)(2,1)S(1)}, u32[]{:S(2)}, u32[]{:S(2)}) collective-permute-start(bf16[64,256]{1,0:T(8,128)(2,1)S(1)} %get-tuple-element.74), channel_id=1, source_target_pairs={{0,2},{2,0},{1,3},{3,1},{4,6},{6,4},{5,7},{7,5},{8,10},{10,8},{9,1... | collective-permute-start | bytes 98312 | tf_op jit(solution)/shard_map/ppermute | solution.py:449
  26.8 0.4 shard_map.165.own_ref
  27.1 0.1 collective-permute-start.7
  27.2 2.3 %collective-permute-done.12.refs_5_ = bf16[64,256]{1,0:T(8,128)(2,1)S(1)} collective-permute-done((bf16[64,256]{1,0:T(8,128)(2,1)S(1)}, bf16[64,256]{1,0:T(8,128)(2,1)S(1)}, u32[]{:S(2)}, u32[]{:S(2)}) %collective-permute-start.12) | collective-permute-done | bytes 32800 | tf_op jit(solution)/shard_map/ppermute | solution.py:449
  29.5 0.0 collective-permute-done.8.refs_0_
  29.5 0.2 collective-permute-done.9.refs_1_
  29.7 0.4 collective-permute-done.10.refs_2_
  30.2 2.4 %collective-permute-start.16 = (bf16[192,256]{1,0:T(8,128)(2,1)S(1)}, bf16[192,256]{1,0:T(8,128)(2,1)S(1)}, u32[]{:S(2)}, u32[]{:S(2)}) collective-permute-start(bf16[192,256]{1,0:T(8,128)(2,1)S(1)} %get-tuple-element.78.refs_0_), channel_id=1, source_target_pairs={{0,12},{4,8},{8,4},{12,0},{1,13},{5,9},{9,5},{13,1},{2,14},{6,10},... | collective-permute-start | bytes 294920 | tf_op jit(solution)/shard_map/ppermute | solution.py:449
  32.6 0.1 collective-permute-start.13
  32.6 2.1 %collective-permute-start.18 = (bf16[192,256]{1,0:T(8,128)(2,1)S(1)}, bf16[192,256]{1,0:T(8,128)(2,1)S(1)}, u32[]{:S(2)}, u32[]{:S(2)}) collective-permute-start(bf16[192,256]{1,0:T(8,128)(2,1)S(1)} %get-tuple-element.78.refs_0_), channel_id=1, source_target_pairs={{0,6},{2,4},{4,2},{6,0},{8,14},{10,12},{12,10},{14,8},{1,7},{3,5},... | collective-permute-start | bytes 294920 | tf_op jit(solution)/shard_map/ppermute | solution.py:455
  34.7 1.4 %collective-permute-start.17 = (bf16[192,256]{1,0:T(8,128)(2,1)S(1)}, bf16[192,256]{1,0:T(8,128)(2,1)S(1)}, u32[]{:S(2)}, u32[]{:S(2)}) collective-permute-start(bf16[192,256]{1,0:T(8,128)(2,1)S(1)} %get-tuple-element.78.refs_0_), channel_id=1, source_target_pairs={{0,2},{2,0},{1,3},{3,1},{4,6},{6,4},{5,7},{7,5},{8,10},{10,8},{9,1... | collective-permute-start | bytes 294920 | tf_op jit(solution)/shard_map/ppermute | solution.py:449
  36.1 0.0 collective-permute-done.7.other_ref
  36.1 0.0 collective-permute-start.15
  36.1 1.6 %collective-permute-done.16.refs_2_ = bf16[192,256]{1,0:T(8,128)(2,1)S(1)} collective-permute-done((bf16[192,256]{1,0:T(8,128)(2,1)S(1)}, bf16[192,256]{1,0:T(8,128)(2,1)S(1)}, u32[]{:S(2)}, u32[]{:S(2)}) %collective-permute-start.16) | collective-permute-done | bytes 98336 | tf_op jit(solution)/shard_map/ppermute | solution.py:449
  37.7 0.7 %collective-permute-start.19 = (bf16[192,256]{1,0:T(8,128)(2,1)S(1)}, bf16[192,256]{1,0:T(8,128)(2,1)S(1)}, u32[]{:S(2)}, u32[]{:S(2)}) collective-permute-start(bf16[192,256]{1,0:T(8,128)(2,1)S(1)} %collective-permute-done.16.refs_2_), channel_id=1, source_target_pairs={{0,2},{2,0},{1,3},{3,1},{4,6},{6,4},{5,7},{7,5},{8,10},{10,8},{9,1... | collective-permute-start | bytes 294920 | tf_op jit(solution)/shard_map/ppermute | solution.py:449
  38.4 2.0 %collective-permute-done.13.refs_0_ = bf16[192,256]{1,0:T(8,128)(2,1)S(1)} collective-permute-done((bf16[192,256]{1,0:T(8,128)(2,1)S(1)}, bf16[192,256]{1,0:T(8,128)(2,1)S(1)}, u32[]{:S(2)}, u32[]{:S(2)}) %collective-permute-start.13) | collective-permute-done | bytes 98336 | tf_op jit(solution)/shard_map/ppermute | solution.py:449
  40.4 1.4 %collective-permute-start.14 = (bf16[192,256]{1,0:T(8,128)(2,1)S(1)}, bf16[192,256]{1,0:T(8,128)(2,1)S(1)}, u32[]{:S(2)}, u32[]{:S(2)}) collective-permute-start(bf16[192,256]{1,0:T(8,128)(2,1)S(1)} %collective-permute-done.13.refs_0_), channel_id=1, source_target_pairs={{0,2},{2,0},{1,3},{3,1},{4,6},{6,4},{5,7},{7,5},{8,10},{10,8},{9,1... | collective-permute-start | bytes 294920 | tf_op jit(solution)/shard_map/ppermute | solution.py:449
  41.9 0.8 %shard_map.169 = (f32[128,512]{1,0:T(8,128)}, bf16[128,512]{1,0:T(8,128)(2,1)}, f32[1,256]{1,0:T(1,128)}, f32[1,512]{1,0:T(1,128)}) custom-call(bf16[128,512]{1,0:T(8,128)(2,1)S(1)} %get-tuple-element.49.cot_ref, bf16[128,512]{1,0:T(8,128)(2,1)S(1)} %get-tuple-element.47.node_ref, f32[1,512]{1,0:T(1,128)S(1)} %get-tuple-element.50.gain_ref, ...), custom_call_target="tpu_custom_call" | custom-call | flops 100000000 | bytes 1000000 | tf_op jit(solution)/shard_map/pallas_call | solution.py:430
  42.7 0.0 collective-permute-done.18.refs_4_
  42.7 0.0 collective-permute-done.17.refs_3_
  42.7 0.0 collective-permute-done.15.refs_1_
  42.7 0.3 collective-permute-done.19.refs_5_
  43.0 1.1 %shard_map.170 = (f32[512,256]{1,0:T(8,128)}, f32[512,256]{1,0:T(8,128)}, f32[256,512]{1,0:T(8,128)}) custom-call(bf16[192,256]{1,0:T(8,128)(2,1)S(1)} %get-tuple-element.78.refs_0_, bf16[192,256]{1,0:T(8,128)(2,1)S(1)} %collective-permute-done.15.refs_1_, bf16[192,256]{1,0:T(8,128)(2,1)S(1)} %collective-permute-done.16.refs_2_, ...), custom_call_target="tpu_custom_call" | custom-call | flops 100000000 | bytes 1000000 | tf_op jit(solution)/shard_map/pallas_call | solution.py:430
  44.1 0.9 %collective-permute-done.14.refs_1_ = bf16[192,256]{1,0:T(8,128)(2,1)S(1)} collective-permute-done((bf16[192,256]{1,0:T(8,128)(2,1)S(1)}, bf16[192,256]{1,0:T(8,128)(2,1)S(1)}, u32[]{:S(2)}, u32[]{:S(2)}) %collective-permute-start.14) | collective-permute-done | bytes 98336 | tf_op jit(solution)/shard_map/ppermute | solution.py:449
  45.0 0.8 %shard_map.171 = (f32[512,256]{1,0:T(8,128)}, f32[512,256]{1,0:T(8,128)}, f32[256,512]{1,0:T(8,128)}) custom-call(bf16[192,256]{1,0:T(8,128)(2,1)S(1)} %collective-permute-done.13.refs_0_, bf16[192,256]{1,0:T(8,128)(2,1)S(1)} %collective-permute-done.14.refs_1_, ...), custom_call_target="tpu_custom_call", output_to_operand_aliasing={{0}: (2, {}), {1}: (3, {}), {2}: (4, {})} | custom-call | flops 100000000 | bytes 1000000 | tf_op jit(solution)/shard_map/pallas_call | solution.py:430
  (2 shorter events, 0.1 us)
Async XLA Ops:
  1.9 6.9 %collective-permute-start = (bf16[1552,256]{1,0:T(8,128)(2,1)S(1)}, bf16[1552,256]{1,0:T(8,128)(2,1)S(1)}, u32[]{:S(2)}, u32[]{:S(2)}) collective-permute-start(bf16[1552,256]{1,0:T(8,128)(2,1)S(1)} %get-tuple-element.48.packed_ref), channel_id=1, source_target_pairs={{0,1},{1,0},{2,3},{3,2},{4,5},{5,4},{6,7},{7,6},{8,9},{9,8},{10,11... | collective-permute-start | bytes 2383880 | tf_op jit(solution)/shard_map/ppermute | solution.py:444
  2.4 8.4 %collective-permute-start.3 = (bf16[64,512]{1,0:T(8,128)(2,1)S(1)}, bf16[64,512]{1,0:T(8,128)(2,1)S(1)}, u32[]{:S(2)}, u32[]{:S(2)}) collective-permute-start(bf16[64,512]{1,0:T(8,128)(2,1)S(1)} %get-tuple-element.58), channel_id=1, source_target_pairs={{0,2},{2,0},{1,3},{3,1},{4,6},{6,4},{5,7},{7,5},{8,10},{10,8},{9,1... | collective-permute-start | bytes 196616 | tf_op jit(solution)/shard_map/ppermute | solution.py:444
  5.0 5.8 %collective-permute-start.1 = (bf16[32,512]{1,0:T(8,128)(2,1)S(1)}, bf16[32,512]{1,0:T(8,128)(2,1)S(1)}, u32[]{:S(2)}, u32[]{:S(2)}) collective-permute-start(bf16[32,512]{1,0:T(8,128)(2,1)S(1)} %get-tuple-element.56), channel_id=1, source_target_pairs={{0,4},{4,8},{8,12},{12,0},{1,5},{5,9},{9,13},{13,1},{2,6},{6,10},{... | collective-permute-start | bytes 98312 | tf_op jit(solution)/shard_map/ppermute | solution.py:444
  6.6 4.3 %collective-permute-start.2 = (bf16[32,512]{1,0:T(8,128)(2,1)S(1)}, bf16[32,512]{1,0:T(8,128)(2,1)S(1)}, u32[]{:S(2)}, u32[]{:S(2)}) collective-permute-start(bf16[32,512]{1,0:T(8,128)(2,1)S(1)} %get-tuple-element.57), channel_id=1, source_target_pairs={{0,12},{4,0},{8,4},{12,8},{1,13},{5,1},{9,5},{13,9},{2,14},{6,2},{... | collective-permute-start | bytes 98312 | tf_op jit(solution)/shard_map/ppermute | solution.py:444
  13.1 8.5 %collective-permute-start.6 = (bf16[592,256]{1,0:T(8,128)(2,1)S(1)}, bf16[592,256]{1,0:T(8,128)(2,1)S(1)}, u32[]{:S(2)}, u32[]{:S(2)}) collective-permute-start(bf16[592,256]{1,0:T(8,128)(2,1)S(1)} %get-tuple-element.65), channel_id=1, source_target_pairs={{0,2},{2,0},{1,3},{3,1},{4,6},{6,4},{5,7},{7,5},{8,10},{10,8},{9,1... | collective-permute-start | bytes 909320 | tf_op jit(solution)/shard_map/ppermute | solution.py:449
  13.7 11.8 %collective-permute-start.4 = (bf16[80,512]{1,0:T(8,128)(2,1)S(1)}, bf16[80,512]{1,0:T(8,128)(2,1)S(1)}, u32[]{:S(2)}, u32[]{:S(2)}) collective-permute-start(bf16[80,512]{1,0:T(8,128)(2,1)S(1)} %get-tuple-element.63), channel_id=1, source_target_pairs={{0,12},{4,8},{8,4},{12,0},{1,13},{5,9},{9,5},{13,1},{2,14},{6,10},... | collective-permute-start | bytes 245768 | tf_op jit(solution)/shard_map/ppermute | solution.py:449
  17.2 8.3 %collective-permute-start.5 = (bf16[80,512]{1,0:T(8,128)(2,1)S(1)}, bf16[80,512]{1,0:T(8,128)(2,1)S(1)}, u32[]{:S(2)}, u32[]{:S(2)}) collective-permute-start(bf16[80,512]{1,0:T(8,128)(2,1)S(1)} %get-tuple-element.64), channel_id=1, source_target_pairs={{0,4},{4,0},{8,12},{12,8},{1,5},{5,1},{9,13},{13,9},{2,6},{6,2},{1... | collective-permute-start | bytes 245768 | tf_op jit(solution)/shard_map/ppermute | solution.py:449
  17.2 7.8 %collective-permute-start.11 = (bf16[64,512]{1,0:T(8,128)(2,1)S(1)}, bf16[64,512]{1,0:T(8,128)(2,1)S(1)}, u32[]{:S(2)}, u32[]{:S(2)}) collective-permute-start(bf16[64,512]{1,0:T(8,128)(2,1)S(1)} %get-tuple-element.71), channel_id=1, source_target_pairs={{0,8},{4,12},{8,0},{12,4},{1,9},{5,13},{9,1},{13,5},{2,10},{6,14},... | collective-permute-start | bytes 196616 | tf_op jit(solution)/shard_map/ppermute | solution.py:449
  21.7 7.8 %collective-permute-start.8 = (bf16[144,256]{1,0:T(8,128)(2,1)S(1)}, bf16[144,256]{1,0:T(8,128)(2,1)S(1)}, u32[]{:S(2)}, u32[]{:S(2)}) collective-permute-start(bf16[144,256]{1,0:T(8,128)(2,1)S(1)} %get-tuple-element.67), channel_id=1, source_target_pairs={{0,8},{4,12},{8,0},{12,4},{1,9},{5,13},{9,1},{13,5},{2,10},{6,14},... | collective-permute-start | bytes 221192 | tf_op jit(solution)/shard_map/ppermute | solution.py:449
  23.4 6.3 %collective-permute-start.9 = (bf16[144,256]{1,0:T(8,128)(2,1)S(1)}, bf16[144,256]{1,0:T(8,128)(2,1)S(1)}, u32[]{:S(2)}, u32[]{:S(2)}) collective-permute-start(bf16[144,256]{1,0:T(8,128)(2,1)S(1)} %get-tuple-element.68), channel_id=1, source_target_pairs={{0,12},{4,8},{8,4},{12,0},{1,13},{5,9},{9,5},{13,1},{2,14},{6,10},... | collective-permute-start | bytes 221192 | tf_op jit(solution)/shard_map/ppermute | solution.py:449
  25.0 5.2 %collective-permute-start.10 = (bf16[144,256]{1,0:T(8,128)(2,1)S(1)}, bf16[144,256]{1,0:T(8,128)(2,1)S(1)}, u32[]{:S(2)}, u32[]{:S(2)}) collective-permute-start(bf16[144,256]{1,0:T(8,128)(2,1)S(1)} %get-tuple-element.69), channel_id=1, source_target_pairs={{0,4},{4,0},{8,12},{12,8},{1,5},{5,1},{9,13},{13,9},{2,6},{6,2},{1... | collective-permute-start | bytes 221192 | tf_op jit(solution)/shard_map/ppermute | solution.py:449
  25.5 4.0 %collective-permute-start.12 = (bf16[64,256]{1,0:T(8,128)(2,1)S(1)}, bf16[64,256]{1,0:T(8,128)(2,1)S(1)}, u32[]{:S(2)}, u32[]{:S(2)}) collective-permute-start(bf16[64,256]{1,0:T(8,128)(2,1)S(1)} %get-tuple-element.74), channel_id=1, source_target_pairs={{0,2},{2,0},{1,3},{3,1},{4,6},{6,4},{5,7},{7,5},{8,10},{10,8},{9,1... | collective-permute-start | bytes 98312 | tf_op jit(solution)/shard_map/ppermute | solution.py:449
  27.1 9.0 %collective-permute-start.7 = (bf16[128,512]{1,0:T(8,128)(2,1)S(1)}, bf16[128,512]{1,0:T(8,128)(2,1)S(1)}, u32[]{:S(2)}, u32[]{:S(2)}) collective-permute-start(bf16[128,512]{1,0:T(8,128)(2,1)S(1)} %shard_map.165.own_ref), channel_id=1, source_target_pairs={{0,1},{1,0},{2,3},{3,2},{4,5},{5,4},{6,7},{7,6},{8,9},{9,8},{10,11... | collective-permute-start | bytes 393224 | tf_op jit(solution)/shard_map/ppermute | solution.py:444
  30.2 7.5 %collective-permute-start.16 = (bf16[192,256]{1,0:T(8,128)(2,1)S(1)}, bf16[192,256]{1,0:T(8,128)(2,1)S(1)}, u32[]{:S(2)}, u32[]{:S(2)}) collective-permute-start(bf16[192,256]{1,0:T(8,128)(2,1)S(1)} %get-tuple-element.78.refs_0_), channel_id=1, source_target_pairs={{0,12},{4,8},{8,4},{12,0},{1,13},{5,9},{9,5},{13,1},{2,14},{6,10},... | collective-permute-start | bytes 294920 | tf_op jit(solution)/shard_map/ppermute | solution.py:449
  32.6 7.9 %collective-permute-start.13 = (bf16[192,256]{1,0:T(8,128)(2,1)S(1)}, bf16[192,256]{1,0:T(8,128)(2,1)S(1)}, u32[]{:S(2)}, u32[]{:S(2)}) collective-permute-start(bf16[192,256]{1,0:T(8,128)(2,1)S(1)} %get-tuple-element.78.refs_0_), channel_id=1, source_target_pairs={{0,8},{4,12},{8,0},{12,4},{1,9},{5,13},{9,1},{13,5},{2,10},{6,14},... | collective-permute-start | bytes 294920 | tf_op jit(solution)/shard_map/ppermute | solution.py:449
  32.6 10.0 %collective-permute-start.18 = (bf16[192,256]{1,0:T(8,128)(2,1)S(1)}, bf16[192,256]{1,0:T(8,128)(2,1)S(1)}, u32[]{:S(2)}, u32[]{:S(2)}) collective-permute-start(bf16[192,256]{1,0:T(8,128)(2,1)S(1)} %get-tuple-element.78.refs_0_), channel_id=1, source_target_pairs={{0,6},{2,4},{4,2},{6,0},{8,14},{10,12},{12,10},{14,8},{1,7},{3,5},... | collective-permute-start | bytes 294920 | tf_op jit(solution)/shard_map/ppermute | solution.py:455
  34.7 8.0 %collective-permute-start.17 = (bf16[192,256]{1,0:T(8,128)(2,1)S(1)}, bf16[192,256]{1,0:T(8,128)(2,1)S(1)}, u32[]{:S(2)}, u32[]{:S(2)}) collective-permute-start(bf16[192,256]{1,0:T(8,128)(2,1)S(1)} %get-tuple-element.78.refs_0_), channel_id=1, source_target_pairs={{0,2},{2,0},{1,3},{3,1},{4,6},{6,4},{5,7},{7,5},{8,10},{10,8},{9,1... | collective-permute-start | bytes 294920 | tf_op jit(solution)/shard_map/ppermute | solution.py:449
  36.1 6.6 %collective-permute-start.15 = (bf16[192,256]{1,0:T(8,128)(2,1)S(1)}, bf16[192,256]{1,0:T(8,128)(2,1)S(1)}, u32[]{:S(2)}, u32[]{:S(2)}) collective-permute-start(bf16[192,256]{1,0:T(8,128)(2,1)S(1)} %get-tuple-element.78.refs_0_), channel_id=1, source_target_pairs={{0,4},{4,0},{8,12},{12,8},{1,5},{5,1},{9,13},{13,9},{2,6},{6,2},{1... | collective-permute-start | bytes 294920 | tf_op jit(solution)/shard_map/ppermute | solution.py:449
  37.7 5.3 %collective-permute-start.19 = (bf16[192,256]{1,0:T(8,128)(2,1)S(1)}, bf16[192,256]{1,0:T(8,128)(2,1)S(1)}, u32[]{:S(2)}, u32[]{:S(2)}) collective-permute-start(bf16[192,256]{1,0:T(8,128)(2,1)S(1)} %collective-permute-done.16.refs_2_), channel_id=1, source_target_pairs={{0,2},{2,0},{1,3},{3,1},{4,6},{6,4},{5,7},{7,5},{8,10},{10,8},{9,1... | collective-permute-start | bytes 294920 | tf_op jit(solution)/shard_map/ppermute | solution.py:449
  40.4 4.6 %collective-permute-start.14 = (bf16[192,256]{1,0:T(8,128)(2,1)S(1)}, bf16[192,256]{1,0:T(8,128)(2,1)S(1)}, u32[]{:S(2)}, u32[]{:S(2)}) collective-permute-start(bf16[192,256]{1,0:T(8,128)(2,1)S(1)} %collective-permute-done.13.refs_0_), channel_id=1, source_target_pairs={{0,2},{2,0},{1,3},{3,1},{4,6},{6,4},{5,7},{7,5},{8,10},{10,8},{9,1... | collective-permute-start | bytes 294920 | tf_op jit(solution)/shard_map/ppermute | solution.py:449

commit v20 on v19

--- a/solution.py
+++ b/solution.py
@@ -496,7 +496,7 @@
             input_output_aliases={2 * count + i: i for i in range(len(before))},
         )
 
-    grads = placed((2,), *placed((0,1,3)))
+    grads = placed((3,), *placed((0, 1, 2)))
     return (*grads, tail), node_part
 
 

time: 46 us -> 45.7 us (level)
  waiting for transfers between devices: 11.7 us -> 10.5 us
  starting transfers between devices: 25 us -> 25.9 us
    ppermute x14, starting transfers between devices: 15.9 us -> 18.4 us  [across(): return lax.ppermute(x, axis, [(i, i ^ k) for i in range(count)])]
    ppermute x1, starting transfers between devices: 2.06 us -> 0.52 us  [diagonal(): return lax.ppermute(x, ('mesh', 'sub'), moves)]
    ppermute x14, waiting for transfers between devices: 11.3 us -> 10.1 us  [across(): return lax.ppermute(x, axis, [(i, i ^ k) for i in range(count)])]
where the time goes in v20:
time: 45.7 us; the launch traced here: 45.6 us
  starting transfers between devices  25.9 us (57%)
  waiting for transfers between devices  10.5 us (23%)
  Pallas kernels  8.44 us (18%)
  between operations  0.72 us (2%)
    ppermute x14, starting transfers between devices, across(): return lax.ppermute(x, axis, [(i, i ^ k) for i in range(count)])  18.4 us
    ppermute x14, waiting for transfers between devices, across(): return lax.ppermute(x, axis, [(i, i ^ k) for i in range(count)])  10.1 us
    pallas_call x10, Pallas kernels, call(): pl.pallas_call(kernel, out_shape=outs, in_specs=specs or [VMEM] * len(arg...  8.44 us
    ppermute x5, starting transfers between devices, shifted(): return lax.ppermute(x, axis, [(i, (i + by) % count) for i in range(count)])  6.98 us
  transfers between devices with their start and end apart: 20, of which 9 were waited for; matrix products, arithmetic and copies ran while one was open for 0% of the time, Pallas kernels for 9%

profile of v20, /device:TPU:0, one launch (start us, length us, event | category | flops | bytes accessed | tf_op | source)
XLA Modules:
  0.0 45.6 jit_solution(90547451812765803)
XLA Ops:
  0.6 1.3 %shard_map.162 = (bf16[128,512]{1,0:T(8,128)(2,1)S(1)}, s32[1,4,32]{2,1,0:T(4,128)S(1)}, bf16[1552,256]{1,0:T(8,128)(2,1)S(1)}, bf16[32,512]{1,0:T(8,128)(2,1)S(...) custom-call(bf16[128,512]{1,0:T(8,128)(2,1)} %node_hbm.1, s32[1,4,32]{2,1,0:T(4,128)} %send_hbm.1, ...), custom_call_target="tpu_custom_call" | custom-call | flops 100000000 | bytes 1000000 | tf_op jit(solution)/shard_map/pallas_call | solution.py:430
  1.9 0.5 %collective-permute-start = (bf16[1552,256]{1,0:T(8,128)(2,1)S(1)}, bf16[1552,256]{1,0:T(8,128)(2,1)S(1)}, u32[]{:S(2)}, u32[]{:S(2)}) collective-permute-start(bf16[1552,256]{1,0:T(8,128)(2,1)S(1)} %get-tuple-element.48.packed_ref), channel_id=1, source_target_pairs={{0,1},{1,0},{2,3},{3,2},{4,5},{5,4},{6,7},{7,6},{8,9},{9,8},{10,11... | collective-permute-start | bytes 2383880 | tf_op jit(solution)/shard_map/ppermute | solution.py:444
  2.4 2.6 %collective-permute-start.3 = (bf16[64,512]{1,0:T(8,128)(2,1)S(1)}, bf16[64,512]{1,0:T(8,128)(2,1)S(1)}, u32[]{:S(2)}, u32[]{:S(2)}) collective-permute-start(bf16[64,512]{1,0:T(8,128)(2,1)S(1)} %get-tuple-element.58), channel_id=1, source_target_pairs={{0,2},{2,0},{1,3},{3,1},{4,6},{6,4},{5,7},{7,5},{8,10},{10,8},{9,1... | collective-permute-start | bytes 196616 | tf_op jit(solution)/shard_map/ppermute | solution.py:444
  5.0 1.6 %collective-permute-start.1 = (bf16[32,512]{1,0:T(8,128)(2,1)S(1)}, bf16[32,512]{1,0:T(8,128)(2,1)S(1)}, u32[]{:S(2)}, u32[]{:S(2)}) collective-permute-start(bf16[32,512]{1,0:T(8,128)(2,1)S(1)} %get-tuple-element.56), channel_id=1, source_target_pairs={{0,4},{4,8},{8,12},{12,0},{1,5},{5,9},{9,13},{13,1},{2,6},{6,10},{... | collective-permute-start | bytes 98312 | tf_op jit(solution)/shard_map/ppermute | solution.py:444
  6.6 2.2 %collective-permute-start.2 = (bf16[32,512]{1,0:T(8,128)(2,1)S(1)}, bf16[32,512]{1,0:T(8,128)(2,1)S(1)}, u32[]{:S(2)}, u32[]{:S(2)}) collective-permute-start(bf16[32,512]{1,0:T(8,128)(2,1)S(1)} %get-tuple-element.57), channel_id=1, source_target_pairs={{0,12},{4,0},{8,4},{12,8},{1,13},{5,1},{9,5},{13,9},{2,14},{6,2},{... | collective-permute-start | bytes 98312 | tf_op jit(solution)/shard_map/ppermute | solution.py:444
  8.8 0.0 collective-permute-done.other_ref
  8.8 1.7 %shard_map.163 = (f32[512,512]{1,0:T(8,128)S(1)}, bf16[512,128]{1,0:T(8,128)(2,1)S(1)}, bf16[128,512]{1,0:T(8,128)(2,1)S(1)}, bf16[512,128]{1,0:T(8,128)(2,1)S(1...) custom-call(bf16[128,512]{1,0:T(8,128)(2,1)S(1)} %get-tuple-element.47.node_ref, ...), custom_call_target="tpu_custom_call" | custom-call | flops 100000000 | bytes 1000000 | tf_op jit(solution)/shard_map/pallas_call | solution.py:430
  10.5 0.3 collective-permute-done.1.rest_0_
  10.8 0.0 collective-permute-done.2.rest_1_
  10.8 0.0 collective-permute-done.3.rest_2_
  10.8 2.3 %shard_map.164 = (f32[128,512]{1,0:T(8,128)S(1)}, f32[128,256]{1,0:T(8,128)S(1)}, bf16[128,256]{1,0:T(8,128)(2,1)S(1)}, bf16[592,256]{1,0:T(8,128)(2,1)S(1)}, bf...) custom-call(bf16[128,512]{1,0:T(8,128)(2,1)S(1)} %get-tuple-element., ...), custom_call_target="tpu_custom_call" | custom-call | flops 100000000 | bytes 1000000 | tf_op jit(solution)/shard_map/pallas_call | solution.py:430
  13.1 0.6 %collective-permute-start.6 = (bf16[592,256]{1,0:T(8,128)(2,1)S(1)}, bf16[592,256]{1,0:T(8,128)(2,1)S(1)}, u32[]{:S(2)}, u32[]{:S(2)}) collective-permute-start(bf16[592,256]{1,0:T(8,128)(2,1)S(1)} %get-tuple-element.65), channel_id=1, source_target_pairs={{0,2},{2,0},{1,3},{3,1},{4,6},{6,4},{5,7},{7,5},{8,10},{10,8},{9,1... | collective-permute-start | bytes 909320 | tf_op jit(solution)/shard_map/ppermute | solution.py:449
  13.7 3.5 %collective-permute-start.4 = (bf16[80,512]{1,0:T(8,128)(2,1)S(1)}, bf16[80,512]{1,0:T(8,128)(2,1)S(1)}, u32[]{:S(2)}, u32[]{:S(2)}) collective-permute-start(bf16[80,512]{1,0:T(8,128)(2,1)S(1)} %get-tuple-element.63), channel_id=1, source_target_pairs={{0,12},{4,8},{8,4},{12,0},{1,13},{5,9},{9,5},{13,1},{2,14},{6,10},... | collective-permute-start | bytes 245768 | tf_op jit(solution)/shard_map/ppermute | solution.py:449
  17.2 0.0 collective-permute-start.5
  17.2 0.9 %collective-permute-start.11 = (bf16[64,512]{1,0:T(8,128)(2,1)S(1)}, bf16[64,512]{1,0:T(8,128)(2,1)S(1)}, u32[]{:S(2)}, u32[]{:S(2)}) collective-permute-start(bf16[64,512]{1,0:T(8,128)(2,1)S(1)} %get-tuple-element.71), channel_id=1, source_target_pairs={{0,8},{4,12},{8,0},{12,4},{1,9},{5,13},{9,1},{13,5},{2,10},{6,14},... | collective-permute-start | bytes 196616 | tf_op jit(solution)/shard_map/ppermute | solution.py:449
  18.1 3.5 %collective-permute-done.6.pair_ref.arrived_ref = bf16[592,256]{1,0:T(8,128)(2,1)S(1)} collective-permute-done((bf16[592,256]{1,0:T(8,128)(2,1)S(1)}, bf16[592,256]{1,0:T(8,128)(2,1)S(1)}, u32[]{:S(2)}, u32[]{:S(2)}) %collective-permute-start.6) | collective-permute-done | bytes 303136 | tf_op jit(solution)/shard_map/ppermute | solution.py:449
  21.7 0.1 shard_map.166
  21.7 1.7 %collective-permute-start.8 = (bf16[144,256]{1,0:T(8,128)(2,1)S(1)}, bf16[144,256]{1,0:T(8,128)(2,1)S(1)}, u32[]{:S(2)}, u32[]{:S(2)}) collective-permute-start(bf16[144,256]{1,0:T(8,128)(2,1)S(1)} %get-tuple-element.67), channel_id=1, source_target_pairs={{0,8},{4,12},{8,0},{12,4},{1,9},{5,13},{9,1},{13,5},{2,10},{6,14},... | collective-permute-start | bytes 221192 | tf_op jit(solution)/shard_map/ppermute | solution.py:449
  23.4 1.6 %collective-permute-start.9 = (bf16[144,256]{1,0:T(8,128)(2,1)S(1)}, bf16[144,256]{1,0:T(8,128)(2,1)S(1)}, u32[]{:S(2)}, u32[]{:S(2)}) collective-permute-start(bf16[144,256]{1,0:T(8,128)(2,1)S(1)} %get-tuple-element.68), channel_id=1, source_target_pairs={{0,12},{4,8},{8,4},{12,0},{1,13},{5,9},{9,5},{13,1},{2,14},{6,10},... | collective-permute-start | bytes 221192 | tf_op jit(solution)/shard_map/ppermute | solution.py:449
  25.0 0.0 collective-permute-done.11.refs_1_
  25.0 0.5 %collective-permute-start.10 = (bf16[144,256]{1,0:T(8,128)(2,1)S(1)}, bf16[144,256]{1,0:T(8,128)(2,1)S(1)}, u32[]{:S(2)}, u32[]{:S(2)}) collective-permute-start(bf16[144,256]{1,0:T(8,128)(2,1)S(1)} %get-tuple-element.69), channel_id=1, source_target_pairs={{0,4},{4,0},{8,12},{12,8},{1,5},{5,1},{9,13},{13,9},{2,6},{6,2},{1... | collective-permute-start | bytes 221192 | tf_op jit(solution)/shard_map/ppermute | solution.py:449
  25.5 0.0 collective-permute-done.4.three_ref.refs_0_
  25.5 0.0 collective-permute-done.5.one_ref.refs_2_
  25.5 1.2 %collective-permute-start.12 = (bf16[64,256]{1,0:T(8,128)(2,1)S(1)}, bf16[64,256]{1,0:T(8,128)(2,1)S(1)}, u32[]{:S(2)}, u32[]{:S(2)}) collective-permute-start(bf16[64,256]{1,0:T(8,128)(2,1)S(1)} %get-tuple-element.74), channel_id=1, source_target_pairs={{0,2},{2,0},{1,3},{3,1},{4,6},{6,4},{5,7},{7,5},{8,10},{10,8},{9,1... | collective-permute-start | bytes 98312 | tf_op jit(solution)/shard_map/ppermute | solution.py:449
  26.8 0.4 shard_map.165.own_ref
  27.1 0.1 collective-permute-start.7
  27.2 2.3 %collective-permute-done.12.refs_5_ = bf16[64,256]{1,0:T(8,128)(2,1)S(1)} collective-permute-done((bf16[64,256]{1,0:T(8,128)(2,1)S(1)}, bf16[64,256]{1,0:T(8,128)(2,1)S(1)}, u32[]{:S(2)}, u32[]{:S(2)}) %collective-permute-start.12) | collective-permute-done | bytes 32800 | tf_op jit(solution)/shard_map/ppermute | solution.py:449
  29.5 0.0 collective-permute-done.8.refs_0_
  29.5 0.2 collective-permute-done.9.refs_1_
  29.7 0.4 collective-permute-done.10.refs_2_
  30.2 1.8 %collective-permute-start.16 = (bf16[192,256]{1,0:T(8,128)(2,1)S(1)}, bf16[192,256]{1,0:T(8,128)(2,1)S(1)}, u32[]{:S(2)}, u32[]{:S(2)}) collective-permute-start(bf16[192,256]{1,0:T(8,128)(2,1)S(1)} %get-tuple-element.78.refs_0_), channel_id=1, source_target_pairs={{0,8},{4,12},{8,0},{12,4},{1,9},{5,13},{9,1},{13,5},{2,10},{6,14},... | collective-permute-start | bytes 294920 | tf_op jit(solution)/shard_map/ppermute | solution.py:449
  32.0 1.6 %collective-permute-start.13 = (bf16[192,256]{1,0:T(8,128)(2,1)S(1)}, bf16[192,256]{1,0:T(8,128)(2,1)S(1)}, u32[]{:S(2)}, u32[]{:S(2)}) collective-permute-start(bf16[192,256]{1,0:T(8,128)(2,1)S(1)} %get-tuple-element.78.refs_0_), channel_id=1, source_target_pairs={{0,12},{4,8},{8,4},{12,0},{1,13},{5,9},{9,5},{13,1},{2,14},{6,10},... | collective-permute-start | bytes 294920 | tf_op jit(solution)/shard_map/ppermute | solution.py:449
  33.5 0.5 %collective-permute-start.18 = (bf16[192,256]{1,0:T(8,128)(2,1)S(1)}, bf16[192,256]{1,0:T(8,128)(2,1)S(1)}, u32[]{:S(2)}, u32[]{:S(2)}) collective-permute-start(bf16[192,256]{1,0:T(8,128)(2,1)S(1)} %get-tuple-element.78.refs_0_), channel_id=1, source_target_pairs={{0,6},{2,4},{4,2},{6,0},{8,14},{10,12},{12,10},{14,8},{1,7},{3,5},... | collective-permute-start | bytes 294920 | tf_op jit(solution)/shard_map/ppermute | solution.py:455
  34.1 1.1 %collective-permute-start.17 = (bf16[192,256]{1,0:T(8,128)(2,1)S(1)}, bf16[192,256]{1,0:T(8,128)(2,1)S(1)}, u32[]{:S(2)}, u32[]{:S(2)}) collective-permute-start(bf16[192,256]{1,0:T(8,128)(2,1)S(1)} %get-tuple-element.78.refs_0_), channel_id=1, source_target_pairs={{0,2},{2,0},{1,3},{3,1},{4,6},{6,4},{5,7},{7,5},{8,10},{10,8},{9,1... | collective-permute-start | bytes 294920 | tf_op jit(solution)/shard_map/ppermute | solution.py:449
  35.2 0.0 collective-permute-done.7.other_ref
  35.2 1.8 %collective-permute-start.15 = (bf16[192,256]{1,0:T(8,128)(2,1)S(1)}, bf16[192,256]{1,0:T(8,128)(2,1)S(1)}, u32[]{:S(2)}, u32[]{:S(2)}) collective-permute-start(bf16[192,256]{1,0:T(8,128)(2,1)S(1)} %get-tuple-element.78.refs_0_), channel_id=1, source_target_pairs={{0,4},{4,0},{8,12},{12,8},{1,5},{5,1},{9,13},{13,9},{2,6},{6,2},{1... | collective-permute-start | bytes 294920 | tf_op jit(solution)/shard_map/ppermute | solution.py:449
  37.0 2.0 %collective-permute-done.16.refs_2_ = bf16[192,256]{1,0:T(8,128)(2,1)S(1)} collective-permute-done((bf16[192,256]{1,0:T(8,128)(2,1)S(1)}, bf16[192,256]{1,0:T(8,128)(2,1)S(1)}, u32[]{:S(2)}, u32[]{:S(2)}) %collective-permute-start.16) | collective-permute-done | bytes 98336 | tf_op jit(solution)/shard_map/ppermute | solution.py:449
  39.0 0.3 collective-permute-start.19
  39.3 0.2 collective-permute-done.13.refs_0_
  39.5 1.9 %collective-permute-start.14 = (bf16[192,256]{1,0:T(8,128)(2,1)S(1)}, bf16[192,256]{1,0:T(8,128)(2,1)S(1)}, u32[]{:S(2)}, u32[]{:S(2)}) collective-permute-start(bf16[192,256]{1,0:T(8,128)(2,1)S(1)} %collective-permute-done.13.refs_0_), channel_id=1, source_target_pairs={{0,2},{2,0},{1,3},{3,1},{4,6},{6,4},{5,7},{7,5},{8,10},{10,8},{9,1... | collective-permute-start | bytes 294920 | tf_op jit(solution)/shard_map/ppermute | solution.py:449
  41.4 0.8 %shard_map.169 = (f32[128,512]{1,0:T(8,128)}, bf16[128,512]{1,0:T(8,128)(2,1)}, f32[1,256]{1,0:T(1,128)}, f32[1,512]{1,0:T(1,128)}) custom-call(bf16[128,512]{1,0:T(8,128)(2,1)S(1)} %get-tuple-element.49.cot_ref, bf16[128,512]{1,0:T(8,128)(2,1)S(1)} %get-tuple-element.47.node_ref, f32[1,512]{1,0:T(1,128)S(1)} %get-tuple-element.50.gain_ref, ...), custom_call_target="tpu_custom_call" | custom-call | flops 100000000 | bytes 1000000 | tf_op jit(solution)/shard_map/pallas_call | solution.py:430
  42.2 0.0 collective-permute-done.18.refs_4_
  42.2 0.0 collective-permute-done.17.refs_3_
  42.2 0.5 %collective-permute-done.15.refs_1_ = bf16[192,256]{1,0:T(8,128)(2,1)S(1)} collective-permute-done((bf16[192,256]{1,0:T(8,128)(2,1)S(1)}, bf16[192,256]{1,0:T(8,128)(2,1)S(1)}, u32[]{:S(2)}, u32[]{:S(2)}) %collective-permute-start.15) | collective-permute-done | bytes 98336 | tf_op jit(solution)/shard_map/ppermute | solution.py:449
  42.7 1.0 %collective-permute-done.19.refs_5_ = bf16[192,256]{1,0:T(8,128)(2,1)S(1)} collective-permute-done((bf16[192,256]{1,0:T(8,128)(2,1)S(1)}, bf16[192,256]{1,0:T(8,128)(2,1)S(1)}, u32[]{:S(2)}, u32[]{:S(2)}) %collective-permute-start.19) | collective-permute-done | bytes 98336 | tf_op jit(solution)/shard_map/ppermute | solution.py:449
  43.7 1.1 %shard_map.170 = (f32[512,256]{1,0:T(8,128)}, f32[512,256]{1,0:T(8,128)}, f32[256,512]{1,0:T(8,128)}) custom-call(bf16[192,256]{1,0:T(8,128)(2,1)S(1)} %get-tuple-element.78.refs_0_, bf16[192,256]{1,0:T(8,128)(2,1)S(1)} %collective-permute-done.15.refs_1_, bf16[192,256]{1,0:T(8,128)(2,1)S(1)} %collective-permute-done.16.refs_2_, ...), custom_call_target="tpu_custom_call" | custom-call | flops 100000000 | bytes 1000000 | tf_op jit(solution)/shard_map/pallas_call | solution.py:430
  44.8 0.0 collective-permute-done.14.refs_1_
  44.8 0.8 %shard_map.171 = (f32[512,256]{1,0:T(8,128)}, f32[512,256]{1,0:T(8,128)}, f32[256,512]{1,0:T(8,128)}) custom-call(bf16[192,256]{1,0:T(8,128)(2,1)S(1)} %collective-permute-done.13.refs_0_, bf16[192,256]{1,0:T(8,128)(2,1)S(1)} %collective-permute-done.14.refs_1_, ...), custom_call_target="tpu_custom_call", output_to_operand_aliasing={{0}: (2, {}), {1}: (3, {}), {2}: (4, {})} | custom-call | flops 100000000 | bytes 1000000 | tf_op jit(solution)/shard_map/pallas_call | solution.py:430
  (2 shorter events, 0.1 us)
Async XLA Ops:
  1.9 6.9 %collective-permute-start = (bf16[1552,256]{1,0:T(8,128)(2,1)S(1)}, bf16[1552,256]{1,0:T(8,128)(2,1)S(1)}, u32[]{:S(2)}, u32[]{:S(2)}) collective-permute-start(bf16[1552,256]{1,0:T(8,128)(2,1)S(1)} %get-tuple-element.48.packed_ref), channel_id=1, source_target_pairs={{0,1},{1,0},{2,3},{3,2},{4,5},{5,4},{6,7},{7,6},{8,9},{9,8},{10,11... | collective-permute-start | bytes 2383880 | tf_op jit(solution)/shard_map/ppermute | solution.py:444
  2.4 8.4 %collective-permute-start.3 = (bf16[64,512]{1,0:T(8,128)(2,1)S(1)}, bf16[64,512]{1,0:T(8,128)(2,1)S(1)}, u32[]{:S(2)}, u32[]{:S(2)}) collective-permute-start(bf16[64,512]{1,0:T(8,128)(2,1)S(1)} %get-tuple-element.58), channel_id=1, source_target_pairs={{0,2},{2,0},{1,3},{3,1},{4,6},{6,4},{5,7},{7,5},{8,10},{10,8},{9,1... | collective-permute-start | bytes 196616 | tf_op jit(solution)/shard_map/ppermute | solution.py:444
  5.0 5.8 %collective-permute-start.1 = (bf16[32,512]{1,0:T(8,128)(2,1)S(1)}, bf16[32,512]{1,0:T(8,128)(2,1)S(1)}, u32[]{:S(2)}, u32[]{:S(2)}) collective-permute-start(bf16[32,512]{1,0:T(8,128)(2,1)S(1)} %get-tuple-element.56), channel_id=1, source_target_pairs={{0,4},{4,8},{8,12},{12,0},{1,5},{5,9},{9,13},{13,1},{2,6},{6,10},{... | collective-permute-start | bytes 98312 | tf_op jit(solution)/shard_map/ppermute | solution.py:444
  6.6 4.3 %collective-permute-start.2 = (bf16[32,512]{1,0:T(8,128)(2,1)S(1)}, bf16[32,512]{1,0:T(8,128)(2,1)S(1)}, u32[]{:S(2)}, u32[]{:S(2)}) collective-permute-start(bf16[32,512]{1,0:T(8,128)(2,1)S(1)} %get-tuple-element.57), channel_id=1, source_target_pairs={{0,12},{4,0},{8,4},{12,8},{1,13},{5,1},{9,5},{13,9},{2,14},{6,2},{... | collective-permute-start | bytes 98312 | tf_op jit(solution)/shard_map/ppermute | solution.py:444
  13.1 8.5 %collective-permute-start.6 = (bf16[592,256]{1,0:T(8,128)(2,1)S(1)}, bf16[592,256]{1,0:T(8,128)(2,1)S(1)}, u32[]{:S(2)}, u32[]{:S(2)}) collective-permute-start(bf16[592,256]{1,0:T(8,128)(2,1)S(1)} %get-tuple-element.65), channel_id=1, source_target_pairs={{0,2},{2,0},{1,3},{3,1},{4,6},{6,4},{5,7},{7,5},{8,10},{10,8},{9,1... | collective-permute-start | bytes 909320 | tf_op jit(solution)/shard_map/ppermute | solution.py:449
  13.7 11.8 %collective-permute-start.4 = (bf16[80,512]{1,0:T(8,128)(2,1)S(1)}, bf16[80,512]{1,0:T(8,128)(2,1)S(1)}, u32[]{:S(2)}, u32[]{:S(2)}) collective-permute-start(bf16[80,512]{1,0:T(8,128)(2,1)S(1)} %get-tuple-element.63), channel_id=1, source_target_pairs={{0,12},{4,8},{8,4},{12,0},{1,13},{5,9},{9,5},{13,1},{2,14},{6,10},... | collective-permute-start | bytes 245768 | tf_op jit(solution)/shard_map/ppermute | solution.py:449
  17.2 8.3 %collective-permute-start.5 = (bf16[80,512]{1,0:T(8,128)(2,1)S(1)}, bf16[80,512]{1,0:T(8,128)(2,1)S(1)}, u32[]{:S(2)}, u32[]{:S(2)}) collective-permute-start(bf16[80,512]{1,0:T(8,128)(2,1)S(1)} %get-tuple-element.64), channel_id=1, source_target_pairs={{0,4},{4,0},{8,12},{12,8},{1,5},{5,1},{9,13},{13,9},{2,6},{6,2},{1... | collective-permute-start | bytes 245768 | tf_op jit(solution)/shard_map/ppermute | solution.py:449
  17.2 7.8 %collective-permute-start.11 = (bf16[64,512]{1,0:T(8,128)(2,1)S(1)}, bf16[64,512]{1,0:T(8,128)(2,1)S(1)}, u32[]{:S(2)}, u32[]{:S(2)}) collective-permute-start(bf16[64,512]{1,0:T(8,128)(2,1)S(1)} %get-tuple-element.71), channel_id=1, source_target_pairs={{0,8},{4,12},{8,0},{12,4},{1,9},{5,13},{9,1},{13,5},{2,10},{6,14},... | collective-permute-start | bytes 196616 | tf_op jit(solution)/shard_map/ppermute | solution.py:449
  21.7 7.8 %collective-permute-start.8 = (bf16[144,256]{1,0:T(8,128)(2,1)S(1)}, bf16[144,256]{1,0:T(8,128)(2,1)S(1)}, u32[]{:S(2)}, u32[]{:S(2)}) collective-permute-start(bf16[144,256]{1,0:T(8,128)(2,1)S(1)} %get-tuple-element.67), channel_id=1, source_target_pairs={{0,8},{4,12},{8,0},{12,4},{1,9},{5,13},{9,1},{13,5},{2,10},{6,14},... | collective-permute-start | bytes 221192 | tf_op jit(solution)/shard_map/ppermute | solution.py:449
  23.4 6.3 %collective-permute-start.9 = (bf16[144,256]{1,0:T(8,128)(2,1)S(1)}, bf16[144,256]{1,0:T(8,128)(2,1)S(1)}, u32[]{:S(2)}, u32[]{:S(2)}) collective-permute-start(bf16[144,256]{1,0:T(8,128)(2,1)S(1)} %get-tuple-element.68), channel_id=1, source_target_pairs={{0,12},{4,8},{8,4},{12,0},{1,13},{5,9},{9,5},{13,1},{2,14},{6,10},... | collective-permute-start | bytes 221192 | tf_op jit(solution)/shard_map/ppermute | solution.py:449
  25.0 5.2 %collective-permute-start.10 = (bf16[144,256]{1,0:T(8,128)(2,1)S(1)}, bf16[144,256]{1,0:T(8,128)(2,1)S(1)}, u32[]{:S(2)}, u32[]{:S(2)}) collective-permute-start(bf16[144,256]{1,0:T(8,128)(2,1)S(1)} %get-tuple-element.69), channel_id=1, source_target_pairs={{0,4},{4,0},{8,12},{12,8},{1,5},{5,1},{9,13},{13,9},{2,6},{6,2},{1... | collective-permute-start | bytes 221192 | tf_op jit(solution)/shard_map/ppermute | solution.py:449
  25.5 4.0 %collective-permute-start.12 = (bf16[64,256]{1,0:T(8,128)(2,1)S(1)}, bf16[64,256]{1,0:T(8,128)(2,1)S(1)}, u32[]{:S(2)}, u32[]{:S(2)}) collective-permute-start(bf16[64,256]{1,0:T(8,128)(2,1)S(1)} %get-tuple-element.74), channel_id=1, source_target_pairs={{0,2},{2,0},{1,3},{3,1},{4,6},{6,4},{5,7},{7,5},{8,10},{10,8},{9,1... | collective-permute-start | bytes 98312 | tf_op jit(solution)/shard_map/ppermute | solution.py:449
  27.1 8.1 %collective-permute-start.7 = (bf16[128,512]{1,0:T(8,128)(2,1)S(1)}, bf16[128,512]{1,0:T(8,128)(2,1)S(1)}, u32[]{:S(2)}, u32[]{:S(2)}) collective-permute-start(bf16[128,512]{1,0:T(8,128)(2,1)S(1)} %shard_map.165.own_ref), channel_id=1, source_target_pairs={{0,1},{1,0},{2,3},{3,2},{4,5},{5,4},{6,7},{7,6},{8,9},{9,8},{10,11... | collective-permute-start | bytes 393224 | tf_op jit(solution)/shard_map/ppermute | solution.py:444
  30.2 8.8 %collective-permute-start.16 = (bf16[192,256]{1,0:T(8,128)(2,1)S(1)}, bf16[192,256]{1,0:T(8,128)(2,1)S(1)}, u32[]{:S(2)}, u32[]{:S(2)}) collective-permute-start(bf16[192,256]{1,0:T(8,128)(2,1)S(1)} %get-tuple-element.78.refs_0_), channel_id=1, source_target_pairs={{0,8},{4,12},{8,0},{12,4},{1,9},{5,13},{9,1},{13,5},{2,10},{6,14},... | collective-permute-start | bytes 294920 | tf_op jit(solution)/shard_map/ppermute | solution.py:449
  32.0 7.5 %collective-permute-start.13 = (bf16[192,256]{1,0:T(8,128)(2,1)S(1)}, bf16[192,256]{1,0:T(8,128)(2,1)S(1)}, u32[]{:S(2)}, u32[]{:S(2)}) collective-permute-start(bf16[192,256]{1,0:T(8,128)(2,1)S(1)} %get-tuple-element.78.refs_0_), channel_id=1, source_target_pairs={{0,12},{4,8},{8,4},{12,0},{1,13},{5,9},{9,5},{13,1},{2,14},{6,10},... | collective-permute-start | bytes 294920 | tf_op jit(solution)/shard_map/ppermute | solution.py:449
  33.5 8.6 %collective-permute-start.18 = (bf16[192,256]{1,0:T(8,128)(2,1)S(1)}, bf16[192,256]{1,0:T(8,128)(2,1)S(1)}, u32[]{:S(2)}, u32[]{:S(2)}) collective-permute-start(bf16[192,256]{1,0:T(8,128)(2,1)S(1)} %get-tuple-element.78.refs_0_), channel_id=1, source_target_pairs={{0,6},{2,4},{4,2},{6,0},{8,14},{10,12},{12,10},{14,8},{1,7},{3,5},... | collective-permute-start | bytes 294920 | tf_op jit(solution)/shard_map/ppermute | solution.py:455
  34.1 8.1 %collective-permute-start.17 = (bf16[192,256]{1,0:T(8,128)(2,1)S(1)}, bf16[192,256]{1,0:T(8,128)(2,1)S(1)}, u32[]{:S(2)}, u32[]{:S(2)}) collective-permute-start(bf16[192,256]{1,0:T(8,128)(2,1)S(1)} %get-tuple-element.78.refs_0_), channel_id=1, source_target_pairs={{0,2},{2,0},{1,3},{3,1},{4,6},{6,4},{5,7},{7,5},{8,10},{10,8},{9,1... | collective-permute-start | bytes 294920 | tf_op jit(solution)/shard_map/ppermute | solution.py:449
  35.2 7.5 %collective-permute-start.15 = (bf16[192,256]{1,0:T(8,128)(2,1)S(1)}, bf16[192,256]{1,0:T(8,128)(2,1)S(1)}, u32[]{:S(2)}, u32[]{:S(2)}) collective-permute-start(bf16[192,256]{1,0:T(8,128)(2,1)S(1)} %get-tuple-element.78.refs_0_), channel_id=1, source_target_pairs={{0,4},{4,0},{8,12},{12,8},{1,5},{5,1},{9,13},{13,9},{2,6},{6,2},{1... | collective-permute-start | bytes 294920 | tf_op jit(solution)/shard_map/ppermute | solution.py:449
  39.0 4.6 %collective-permute-start.19 = (bf16[192,256]{1,0:T(8,128)(2,1)S(1)}, bf16[192,256]{1,0:T(8,128)(2,1)S(1)}, u32[]{:S(2)}, u32[]{:S(2)}) collective-permute-start(bf16[192,256]{1,0:T(8,128)(2,1)S(1)} %collective-permute-done.16.refs_2_), channel_id=1, source_target_pairs={{0,2},{2,0},{1,3},{3,1},{4,6},{6,4},{5,7},{7,5},{8,10},{10,8},{9,1... | collective-permute-start | bytes 294920 | tf_op jit(solution)/shard_map/ppermute | solution.py:449
  39.5 5.3 %collective-permute-start.14 = (bf16[192,256]{1,0:T(8,128)(2,1)S(1)}, bf16[192,256]{1,0:T(8,128)(2,1)S(1)}, u32[]{:S(2)}, u32[]{:S(2)}) collective-permute-start(bf16[192,256]{1,0:T(8,128)(2,1)S(1)} %collective-permute-done.13.refs_0_), channel_id=1, source_target_pairs={{0,2},{2,0},{1,3},{3,1},{4,6},{6,4},{5,7},{7,5},{8,10},{10,8},{9,1... | collective-permute-start | bytes 294920 | tf_op jit(solution)/shard_map/ppermute | solution.py:449
